TPU v7x, 32 devices: a whole 2x2x4 slice. The times are simulated.
32 devices in a mesh: ctx: 4 (over y, x), tp: 8 (over z, core).
Axes of the slice: x: 2, y: 2, z: 4, core: 2. Of those that a mesh axis runs over, the one named last changes fastest.
Arguments:
- tokens: bfloat16 [512, 4096], P('ctx'), may hold values from -6 to 6
- new_token_states: bfloat16 [4, 4096], replicated, may hold values from -6.0625 to 6.0625
- w_query: bfloat16 [4096, 2048], P('ctx', 'tp'), may hold values from -0.12162204 to 0.12162204
- key_matrix: bfloat16 [4096, 1024], P('ctx', 'tp'), may hold values from -0.12162204 to 0.12162204
- value_matrix: bfloat16 [4096, 1024], P('ctx', 'tp'), may hold values from -0.09375 to 0.09375
- w_out: bfloat16 [2048, 4096], P('tp', 'ctx'), may hold values from -0.125 to 0.125
- lengths: int32 [4], replicated, may hold values from 1 to 256, 512 in all
- block_map: int32 [8], replicated, may hold values from 0 to 7, each once
Outputs:
- prefill_out: bfloat16 [512, 4096], P('ctx', 'tp')
- decode_out: bfloat16 [4, 4096], P(None, 'tp')
Inputs may be any that keep to these rules, and one draw needn't show every extreme that they name: The lengths sum to 512, and some request has exactly 256 tokens. `block_map`: each of the 8 initial blocks is held exactly once.
All inputs are finite; a program needn't handle non-finite values.
Results may differ from a plain program's by a relative error of at most 0.015.
Values may be sent and summed in bfloat16 or wider, within the bound.
No kernel may reach another device: no remote copies, remote signals or barrier semaphores. Data moves between devices by JAX's collectives and lax.ppermute only.
A program may use at most 64 MiB of HBM per device.

v0:
```python
import math

import jax
import jax.numpy as jnp
from jax import lax
from jax.sharding import PartitionSpec as P

HEAD_SIZE = 128


floor_value = -1e30


def initial_positions(block_map, first_row, row_count, block_rows):
    row_ids = first_row + jnp.arange(row_count, dtype=jnp.int32)
    block_ids = row_ids // block_rows
    table_ids = jnp.arange(block_map.shape[0], dtype=jnp.int32)
    mapped = jnp.sum(
        jnp.where(block_ids[:, None] == table_ids[None, :], block_map[None, :], 0), axis=1
    )
    return mapped * block_rows + row_ids % block_rows


def request_index(positions, request_ends):
    return jnp.sum((positions[:, None] >= request_ends[None, :]).astype(jnp.int32), axis=1)


def round_weights(weights):
    rounded = weights.astype(jnp.bfloat16)
    rounded = lax.optimization_barrier(rounded)
    return rounded.astype(jnp.float32)


def softmax_parts(
    dec_heads, projected_key_rows, projected_value_rows, owned, kv_heads, head_dim, score_scale
):
    row_count = projected_key_rows.shape[0]
    scores = (
        jnp.einsum(
            "rgjd,tgd->rgjt",
            dec_heads,
            projected_key_rows.reshape(row_count, kv_heads, head_dim),
            preferred_element_type=jnp.float32,
        )
        * score_scale
    )
    scores = jnp.where(owned, scores, floor_value)
    part_peak = jnp.max(scores, axis=3)
    weights = jnp.where(owned, jnp.exp(scores - part_peak[..., None]), 0.0)
    part_total = jnp.sum(weights, axis=3)
    part_mixed = jnp.einsum(
        "rgjt,tgd->rgjd",
        weights.astype(jnp.bfloat16),
        projected_value_rows.reshape(row_count, kv_heads, head_dim),
        preferred_element_type=jnp.float32,
    )
    return (part_peak, part_total, part_mixed)


def on_device(
    tokens, new_token_states, w_query, key_matrix, value_matrix, w_out, lengths, block_map
):
    local_rows = tokens.shape[0]
    block_rows = local_rows // 2
    request_count = new_token_states.shape[0]
    head_dim = HEAD_SIZE
    query_width = w_query.shape[1]
    kv_width = key_matrix.shape[1]
    kv_heads = kv_width // head_dim
    query_group_count = query_width // kv_width
    score_scale = 1.0 / math.sqrt(head_dim)
    device = lax.axis_index("ctx")
    request_ends = jnp.cumsum(lengths)
    inputs = jnp.concatenate([tokens, new_token_states], axis=0)
    shard_pieces = (
        lax.all_gather(w_query, "ctx", axis=0, tiled=True),
        lax.all_gather(key_matrix, "ctx", axis=0, tiled=True),
        lax.all_gather(value_matrix, "ctx", axis=0, tiled=True),
    )
    query_all, key_all, value_all = tuple(
        (jnp.dot(inputs, weight, preferred_element_type=jnp.float32) for weight in shard_pieces)
    )
    query_all = query_all.astype(jnp.bfloat16)
    key_all = key_all.astype(jnp.bfloat16)
    value_all = value_all.astype(jnp.bfloat16)
    local_query = query_all[:local_rows]
    local_keys = key_all[:local_rows]
    local_values = value_all[:local_rows]
    dec_query = query_all[local_rows:]
    decode_key_rows = key_all[local_rows:]
    decode_value_rows = value_all[local_rows:]
    token_pos = initial_positions(block_map, device * local_rows, local_rows, block_rows)
    token_request = request_index(token_pos, request_ends)
    query_heads = local_query.reshape(local_rows, kv_heads, query_group_count, head_dim)

    def attend(running, shard_pieces, first_row):
        peak_run, total_run, mixed_run = running
        key_piece, value_piece = shard_pieces
        row_count = key_piece.shape[0]
        key_pos = initial_positions(block_map, first_row, row_count, block_rows)
        key_request = request_index(key_pos, request_ends)
        allowed = (key_request[None, :] == token_request[:, None]) & (
            key_pos[None, :] <= token_pos[:, None]
        )
        scores = (
            jnp.einsum(
                "tgjd,kgd->gjtk",
                query_heads,
                key_piece.reshape(row_count, kv_heads, head_dim),
                preferred_element_type=jnp.float32,
            )
            * score_scale
        )
        scores = jnp.where(allowed, scores, floor_value)
        peak_new = jnp.maximum(peak_run, jnp.max(scores, axis=3))
        weights = jnp.where(allowed, jnp.exp(scores - peak_new[..., None]), 0.0)
        rescale = jnp.exp(peak_run - peak_new)
        total_new = total_run * rescale + jnp.sum(weights, axis=3)
        mixed_new = mixed_run * rescale[..., None] + jnp.einsum(
            "gjtk,kgd->gjtd",
            weights.astype(jnp.bfloat16),
            value_piece.reshape(row_count, kv_heads, head_dim),
            preferred_element_type=jnp.float32,
        )
        return (peak_new, total_new, mixed_new)

    start_state = (
        jnp.full((kv_heads, query_group_count, local_rows), floor_value, jnp.float32),
        jnp.zeros((kv_heads, query_group_count, local_rows), jnp.float32),
        jnp.zeros((kv_heads, query_group_count, local_rows, head_dim), jnp.float32),
    )
    dec_heads = dec_query.reshape(request_count, kv_heads, query_group_count, head_dim)
    request_ids = jnp.arange(request_count, dtype=jnp.int32)
    cache_keys, cache_values = (
        lax.all_gather(local_keys, "ctx", axis=0, tiled=True),
        lax.all_gather(local_values, "ctx", axis=0, tiled=True),
    )
    total_rows = cache_keys.shape[0]
    shard_count = total_rows // local_rows
    limit = max(1, 1024 // local_rows)
    step_rows = local_rows * math.gcd(shard_count, 1 << limit.bit_length() - 1)

    def key_step(running, step_index):
        first_row = step_index * step_rows
        pieces = (
            lax.dynamic_slice_in_dim(cache_keys, first_row, step_rows, 0),
            lax.dynamic_slice_in_dim(cache_values, first_row, step_rows, 0),
        )
        return (attend(running, pieces, first_row), None)

    final_state, unused = lax.scan(
        key_step, start_state, jnp.arange(total_rows // step_rows, dtype=jnp.int32)
    )
    peak_run, total_run, mixed_run = final_state
    cache_pos = (
        block_map[:, None] * block_rows + jnp.arange(block_rows, dtype=jnp.int32)[None, :]
    ).reshape(total_rows)
    cache_request = request_index(cache_pos, request_ends)
    owned = (cache_request[None, :] == request_ids[:, None])[:, None, None, :]
    cache_peak, cache_total, cache_mixed = softmax_parts(
        dec_heads, cache_keys, cache_values, owned, kv_heads, head_dim, score_scale
    )
    attended = (
        (mixed_run / total_run[..., None]).transpose(2, 0, 1, 3).reshape(local_rows, query_width)
    )
    attended = attended.astype(jnp.bfloat16)
    own_keys = decode_key_rows.reshape(request_count, kv_heads, 1, head_dim).astype(jnp.float32)
    own_values = decode_value_rows.reshape(request_count, kv_heads, 1, head_dim).astype(jnp.float32)
    self_scores = jnp.sum(dec_heads.astype(jnp.float32) * own_keys, axis=3) * score_scale
    peak_all = jnp.maximum(cache_peak, self_scores)
    rescale = jnp.exp(cache_peak - peak_all)
    self_weights = jnp.exp(self_scores - peak_all)
    dec_total = cache_total * rescale + self_weights
    dec_mixed = (
        cache_mixed * rescale[..., None] + round_weights(self_weights)[..., None] * own_values
    )
    dec_attn = (
        (dec_mixed / dec_total[..., None]).reshape(request_count, query_width).astype(jnp.bfloat16)
    )
    attended_all = jnp.concatenate([attended, dec_attn], axis=0)
    head_block = lax.all_gather(w_out, "ctx", axis=1, tiled=True)
    column_block = lax.all_to_all(head_block, "tp", split_axis=1, concat_axis=0, tiled=True)
    summed_rows = jnp.dot(
        lax.all_gather(attended_all, "tp", axis=1, tiled=True),
        column_block,
        preferred_element_type=jnp.float32,
    )
    summed_rows = summed_rows.astype(jnp.bfloat16)
    return (summed_rows[:local_rows], summed_rows[local_rows:])


def solution(mesh):
    return jax.shard_map(
        on_device,
        mesh=mesh,
        in_specs=(
            P("ctx", None),
            P(),
            P("ctx", "tp"),
            P("ctx", "tp"),
            P("ctx", "tp"),
            P("tp", "ctx"),
            P(),
            P(),
        ),
        out_specs=(P("ctx", "tp"), P(None, "tp")),
        check_vma=False,
    )
```

profile of v0, /device:TPU:0, one launch (start us, length us, event | category | flops | bytes accessed | tf_op | source)
XLA Modules:
  0.0 183.1 jit_solution(9726246331177293041)
XLA Ops:
  7.2 0.7 all-gather.5.cloned.1.call-update
  7.9 0.7 all-gather.9.cloned.1.call-update
  8.7 2.1 %copy.52 = bf16[256,1024]{0,1:T(8,128)(2,1)} copy(bf16[256,1024]{1,0:T(8,128)(2,1)} %param.13) | data formatting | bytes 1048576 | tf_op args[5]
  10.9 0.5 all-gather.7.cloned.1.call-update
  11.8 0.2 reduce-window.8
  12.1 0.1 convert_reduce_fusion.1
  12.2 0.2 compare_and_fusion
  12.4 0.1 constant_dynamic-update-slice_fusion.1
  12.6 26.6 %all-gather.5.cloned.1.call-done = bf16[4096,128]{1,0:T(8,128)(2,1)} async-done(((bf16[1024,128]{1,0:T(8,128)(2,1)}), bf16[4096,128]{1,0:T(8,128)(2,1)}) %all-gather.5.cloned.1.call-update) | async-done | bytes 1048592 | tf_op jit(solution)/shard_map/all_gather | solution.py:77
  39.2 1.7 convolution_convert_fusion.3
  40.9 26.8 %all-gather.9.cloned.1.call-done = bf16[4096,128]{1,0:T(8,128)(2,1)} async-done(((bf16[1024,128]{1,0:T(8,128)(2,1)}), bf16[4096,128]{1,0:T(8,128)(2,1)}) %all-gather.9.cloned.1.call-update) | async-done | bytes 1048592 | tf_op jit(solution)/shard_map/all_gather | solution.py:78
  67.7 1.7 convolution_convert_fusion.2
  69.4 8.4 %all_gather.22 = bf16[512,128]{1,0:T(8,128)(2,1)S(1)} all-gather(bf16[128,128]{1,0:T(8,128)(2,1)S(1)} %slice.32), channel_id=1, replica_groups=mesh['ctx'=4,'tp'=8] {'ctx'}, dimensions={0}, use_global_device_ids=true | all-gather | bytes 163840 | tf_op jit(solution)/shard_map/all_gather | solution.py:135
  77.8 27.1 %all-gather.11.cloned.1.call-done = bf16[256,4096]{0,1:T(8,128)(2,1)} async-done(((bf16[256,1024]{0,1:T(8,128)(2,1)}), bf16[256,4096]{0,1:T(8,128)(2,1)}) %all-gather.11.cloned.1.call-update) | async-done | bytes 2097168 | tf_op jit(solution)/shard_map/all_gather | solution.py:181
  104.9 4.6 %all-to-all-start = ((bf16[256,8,512]{0,2,1:T(8,128)(2,1)}), bf16[256,8,512]{0,2,1:T(8,128)(2,1)S(1)}, u32[]{:S(2)}, u32[]{:S(2)}) async-start(bf16[256,8,512]{0,2,1:T(8,128)(2,1)} %bitcast.100), calls=%async_computation | async-start | bytes 4194304 | tf_op jit(solution)/shard_map/all_to_all | solution.py:182
  109.5 9.5 %all_gather.25 = bf16[512,128]{1,0:T(8,128)(2,1)} all-gather(bf16[128,128]{1,0:T(8,128)(2,1)S(1)} %slice.34), channel_id=1, replica_groups=mesh['ctx'=4,'tp'=8] {'ctx'}, dimensions={0}, use_global_device_ids=true | all-gather | bytes 163840 | tf_op jit(solution)/shard_map/all_gather | solution.py:136
  119.0 23.6 %all-gather.7.cloned.1.call-done = bf16[4096,256]{1,0:T(8,128)(2,1)} async-done(((bf16[1024,256]{1,0:T(8,128)(2,1)}), bf16[4096,256]{1,0:T(8,128)(2,1)}) %all-gather.7.cloned.1.call-update) | async-done | bytes 2097168 | tf_op jit(solution)/shard_map/all_gather | solution.py:76
  142.6 2.1 %convolution_convert_fusion.1 = bf16[132,256]{1,0:T(8,128)(2,1)S(1)} fusion(bf16[132,4096]{1,0:T(8,128)(2,1)S(1)} %constant_dynamic-update-slice_fusion, bf16[4096,256]{1,0:T(8,128)(2,1)} %all-gather.7.cloned.1.call-done), kind=kOutput, calls=%fused_computation.6 | convolution fusion | flops 276857856 | bytes 3246080 | tf_op jit(solution)/shard_map/dot_general | solution.py:81
  144.7 0.6 copy-done.2
  145.4 0.1 copy.50
  145.5 0.9 fusion.51
  146.4 0.2 fusion.25
  146.6 0.2 fusion.11
  146.8 0.1 copy.51
  147.0 1.1 fusion.52
  148.1 0.1 fusion.12
  148.2 0.3 fusion.3
  148.5 22.3 %all_gather.26 = bf16[132,2048]{0,1:T(8,128)(2,1)S(1)} all-gather(bf16[132,256]{0,1:T(8,128)(2,1)S(1)} %pad_maximum_fusion), channel_id=1, replica_groups=mesh['ctx'=4,'tp'=8] {'tp'}, dimensions={1}, use_global_device_ids=true | all-gather | bytes 608256 | tf_op jit(solution)/shard_map/all_gather | solution.py:184
  170.9 2.4 %copy.53 = bf16[8,256,512]{2,1,0:T(8,128)(2,1)} copy(bf16[8,256,512]{1,2,0:T(8,128)(2,1)S(1)} %bitcast.98) | data formatting | bytes 4194304 | tf_op jit(solution)/shard_map/all_to_all | solution.py:182
  173.2 2.1 %convolution_convert_fusion = bf16[132,512]{1,0:T(8,128)(2,1)S(1)} fusion(bf16[132,2048]{0,1:T(8,128)(2,1)S(1)} %all_gather.26, bf16[2048,512]{1,0:T(8,128)(2,1)} %bitcast.99), kind=kOutput, calls=%fused_computation.3 | convolution fusion | flops 276891648 | bytes 2772992 | tf_op jit(solution)/shard_map/dot_general | solution.py:183
  175.3 0.7 slice.38
  176.0 0.6 slice.39
  (42 shorter events, 0.9 us)
Async XLA Ops:
  7.2 32.0 %all-gather.5.cloned.1.call-start = ((), (), s32[]{:S(2)}) async-start(), calls=%async_computation.1 | async-start | bytes 1310720 | tf_op jit(solution)/shard_map/all_gather | solution.py:77
  7.9 59.8 %all-gather.9.cloned.1.call-start = ((), (), s32[]{:S(2)}) async-start(), calls=%async_computation.3 | async-start | bytes 1310720 | tf_op jit(solution)/shard_map/all_gather | solution.py:78
  8.6 2.9 %copy-start.4 = (s32[8]{0:T(128)S(1)}, s32[8]{0:T(128)}, u32[]{:S(2)}) copy-start(s32[8]{0:T(128)} %param.15) | copy-start | bytes 100
  8.7 3.1 %copy-start.5 = (s32[4]{0:T(128)S(1)}, s32[4]{0:T(128)}, u32[]{:S(2)}) copy-start(s32[4]{0:T(128)} %param.14) | copy-start | bytes 52
  8.7 3.8 %copy-start = (bf16[128,4096]{1,0:T(8,128)(2,1)S(1)}, bf16[128,4096]{1,0:T(8,128)(2,1)}, u32[]{:S(2)}) copy-start(bf16[128,4096]{1,0:T(8,128)(2,1)} %param.8) | copy-start | bytes 3145732
  8.7 96.2 %all-gather.11.cloned.1.call-start = ((), (), s32[]{:S(2)}) async-start(), calls=%async_computation.4 | async-start | bytes 2621440 | tf_op jit(solution)/shard_map/all_gather | solution.py:181
  10.9 131.7 %all-gather.7.cloned.1.call-start = ((), (), s32[]{:S(2)}) async-start(), calls=%async_computation.2 | async-start | bytes 2621440 | tf_op jit(solution)/shard_map/all_gather | solution.py:76
  11.5 1.1 copy-start.3
  104.9 66.0 %all-to-all-start = ((bf16[256,8,512]{0,2,1:T(8,128)(2,1)}), bf16[256,8,512]{0,2,1:T(8,128)(2,1)S(1)}, u32[]{:S(2)}, u32[]{:S(2)}) async-start(bf16[256,8,512]{0,2,1:T(8,128)(2,1)} %bitcast.100), calls=%async_computation | async-start | bytes 4194304 | tf_op jit(solution)/shard_map/all_to_all | solution.py:182
  119.0 27.6 %copy-start.1 = (bf16[512,128]{1,0:T(8,128)(2,1)S(1)}, bf16[512,128]{1,0:T(8,128)(2,1)}, u32[]{:S(2)}) copy-start(bf16[512,128]{1,0:T(8,128)(2,1)} %all_gather.25) | copy-start | bytes 393220
  144.7 0.6 copy-start.2
Sparse Core Ops, SparseCore 0:
  9.8 29.3 all-gather.4
  41.0 26.6 all-gather.8
  69.6 35.2 all-gather.10
  106.6 35.9 all-gather.6
where the time goes:
time: 184 us; the launch traced here: 183 us
  waiting for transfers between devices  106 us (58%)
  blocking collectives  40.2 us (22%)
  between operations  14 us (8%)
  matrix products  9.96 us (5%)
  local copies, waits for them, and re-layouts  6.9 us (4%)
  starting transfers between devices  4.76 us (3%)
    all_gather x1, waiting for transfers between devices, on_device(): head_block = lax.all_gather(w_out, 'ctx', axis=1, tiled=True)  27.1 us
    all_gather x1, waiting for transfers between devices, on_device(): lax.all_gather(value_matrix, 'ctx', axis=0, tiled=True)  26.8 us
    all_gather x1, waiting for transfers between devices, on_device(): lax.all_gather(key_matrix, 'ctx', axis=0, tiled=True)  26.6 us
    all_gather x1, waiting for transfers between devices, on_device(): lax.all_gather(w_query, 'ctx', axis=0, tiled=True)  23.6 us
    all_gather x1, blocking collectives, on_device(): lax.all_gather(attended_all, 'tp', axis=1, tiled=True)  22.3 us
    all_gather x1, blocking collectives, on_device(): lax.all_gather(local_values, 'ctx', axis=0, tiled=True)  9.49 us
    all_gather x1, blocking collectives, on_device(): lax.all_gather(local_keys, 'ctx', axis=0, tiled=True)  8.41 us
    dot_general x3, matrix products, on_device(): jnp.dot(inputs, weight, preferred_element_type=jnp.float32)  5.41 us
  transfers between devices with their start and end apart: 5, of which 4 were waited for; matrix products, arithmetic and copies ran while one was open for 6% of the time, Pallas kernels for 0%

commit v1 on v0

--- a/solution.py
+++ b/solution.py
@@ -1,11 +1,321 @@
+import functools
 import math
 
 import jax
 import jax.numpy as jnp
 from jax import lax
+from jax.experimental import pallas as pl
+from jax.experimental.pallas import tpu as pltpu
 from jax.sharding import PartitionSpec as P
 
 HEAD_SIZE = 128
+FLOOR = -1e30
+LAST = 1 << 30
+ROW_TILE = 8
+VMEM_BYTES = 48 * 1024 * 1024
+
+
+def vmem():
+    return pl.BlockSpec(memory_space=pltpu.VMEM)
+
+
+def smem():
+    return pl.BlockSpec(memory_space=pltpu.SMEM)
+
+
+def hbm():
+    return pl.BlockSpec(memory_space=pl.ANY)
+
+
+def params():
+    return pltpu.CompilerParams(vmem_limit_bytes=VMEM_BYTES)
+
+
+def slice_kernel(place, tokens, *rest):
+    outs, sem = rest[:-1], rest[-1]
+    rows, width = outs[0].shape
+    first = pl.multiple_of(place[2] * rows, rows)
+    copies = []
+    for step, out in enumerate(outs, 1):
+        column = pl.multiple_of((place[0] ^ step) * width, width)
+        copies.append(
+            pltpu.make_async_copy(
+                tokens.at[pl.ds(first, rows), pl.ds(column, width)], out, sem.at[step - 1]
+            )
+        )
+    for copy in copies:
+        copy.start()
+    for copy in copies:
+        copy.wait()
+
+
+def project_kernel(steps, place, own, *rest):
+    blocks, rest = (own,) + rest[: steps - 1], rest[steps - 1 :]
+    new, wq, wq2, wk, wk2, wv, wv2 = rest[:7]
+    outs, inputs = rest[7 : 7 + steps], rest[7 + steps]
+    rows = own.shape[0]
+    count = new.shape[0]
+    tail = steps * rows
+    for step, block in enumerate(blocks):
+        inputs[step * rows : (step + 1) * rows, :] = block[...]
+    inputs[tail:, :] = jnp.zeros_like(inputs[tail:, :])
+    inputs[tail : tail + count, :] = new[...]
+    x = inputs[...]
+    column = 0
+    pad = outs[0].shape[0] - rows
+    for first, second in ((wq, wq2), (wk, wk2), (wv, wv2)):
+        weight = jnp.concatenate([first[...], second[...]], axis=1)
+        part = jnp.dot(x, weight, preferred_element_type=jnp.float32)
+        to = slice(column, column + weight.shape[1])
+        for step, out in enumerate(outs):
+            out[:rows, to] = part[step * rows : (step + 1) * rows].astype(out.dtype)
+            out[rows:, to] = part[tail : tail + pad].astype(out.dtype)
+        column += weight.shape[1]
+
+
+def add_kernel(steps, *refs):
+    parts, (query, keyval, new) = refs[:steps], refs[steps:]
+    rows = query.shape[0]
+    total = parts[0][...]
+    for part in parts[1:]:
+        total = total + part[...].astype(jnp.float32)
+    total = total.astype(jnp.bfloat16)
+    half = query.shape[1]
+    query[...] = total[:rows, :half]
+    keyval[...] = total[:rows, half:]
+    new[...] = total[rows:]
+
+
+def request_of(position, ends):
+    found = jnp.zeros_like(position)
+    for end in ends:
+        found = found + jnp.where(position >= end, 1, 0)
+    return found
+
+
+def attend_kernel(steps, count, scale, place, block_map, lengths, *refs):
+    queries, refs = refs[:steps], refs[steps:]
+    mine, refs = refs[:steps], refs[steps:]
+    theirs, refs = refs[:steps], refs[steps:]
+    new, w_own, w_other = refs[:3]
+    outs, (q_all, key_all, value_all, attended, result) = refs[3 : 3 + 2 * steps], refs[3 + 2 * steps :]
+    rows, q_width = queries[0].shape
+    kv_width = q_width // 2
+    head = HEAD_SIZE
+    groups = kv_width // head
+    per_group = q_width // kv_width
+    pad = new.shape[0]
+    tail = steps * rows
+    q_rows = q_all.shape[0]
+    k_rows = key_all.shape[0]
+    k_tail = 2 * tail
+    c, z, k = place[0], place[1], place[2]
+
+    q_all[tail:, :] = jnp.zeros_like(q_all[tail:, :])
+    key_all[k_tail:, :] = jnp.zeros_like(key_all[k_tail:, :])
+    value_all[k_tail:, :] = jnp.zeros_like(value_all[k_tail:, :])
+    for step in range(steps):
+        at = slice(step * rows, (step + 1) * rows)
+        q_all[at, :] = queries[step][...]
+        key_all[at, :] = mine[step][:, :kv_width]
+        value_all[at, :] = mine[step][:, kv_width:]
+        at = slice(tail + step * rows, tail + (step + 1) * rows)
+        half = kv_width // 2
+        key_all[at, :half] = theirs[step][:, half:kv_width]
+        key_all[at, half:] = theirs[step][:, :half]
+        value_all[at, :half] = theirs[step][:, kv_width + half :]
+        value_all[at, half:] = theirs[step][:, kv_width : kv_width + half]
+    q_all[tail : tail + pad, :] = new[:, :q_width]
+    key_all[k_tail : k_tail + pad, :] = new[:, q_width : q_width + kv_width]
+    value_all[k_tail : k_tail + pad, :] = new[:, q_width + kv_width :]
+
+    ends, total = [], 0
+    for request in range(count):
+        total = total + lengths[request]
+        ends.append(total)
+
+    def labels(shape, axis, halves):
+        index = lax.broadcasted_iota(jnp.int32, shape, axis)
+        position = jnp.zeros(shape, jnp.int32)
+        for number in range(halves * steps):
+            held = 2 * (c ^ (number % steps)) + (k ^ (number // steps))
+            inside = (index >= number * rows) & (index < (number + 1) * rows)
+            position = jnp.where(inside, block_map[held] * rows + index - number * rows, position)
+        last = halves * tail
+        is_new = index >= last
+        request = jnp.where(is_new, index - last, request_of(position, ends))
+        return jnp.where(is_new, LAST, position), request
+
+    q_position, q_request = labels((q_rows, 1), 0, 1)
+    k_position, k_request = labels((1, k_rows), 1, 2)
+    allowed = (q_request == k_request) & (k_position <= q_position)
+
+    for group in range(groups):
+        keys = key_all[:, group * head : (group + 1) * head]
+        values = value_all[:, group * head : (group + 1) * head]
+        for member in range(per_group):
+            at = (group * per_group + member) * head
+            scores = lax.dot_general(
+                q_all[:, at : at + head],
+                keys,
+                (((1,), (1,)), ((), ())),
+                preferred_element_type=jnp.float32,
+            )
+            scores = jnp.where(allowed, scores * scale, FLOOR)
+            weights = jnp.exp(scores - jnp.max(scores, axis=1, keepdims=True))
+            denom = jnp.sum(weights, axis=1, keepdims=True)
+            mixed = jnp.dot(
+                weights.astype(jnp.bfloat16), values, preferred_element_type=jnp.float32
+            )
+            attended[:, at : at + head] = (mixed / denom).astype(jnp.bfloat16)
+
+    rows_own = w_own.shape[0]
+    result[...] = (
+        jnp.dot(attended[:, :rows_own], w_own[...], preferred_element_type=jnp.float32)
+        + jnp.dot(attended[:, rows_own:], w_other[...], preferred_element_type=jnp.float32)
+    ).astype(jnp.bfloat16)
+    width = outs[0].shape[1]
+    for step in range(steps):
+        first = pl.multiple_of((c ^ z ^ step) * rows, rows)
+        for other in range(2):
+            column = pl.multiple_of((k ^ other) * width, width)
+            out = outs[2 * step + other]
+            out[:rows, :] = result[pl.ds(first, rows), pl.ds(column, width)]
+            out[rows:, :] = result[tail : tail + pad, pl.ds(column, width)]
+
+
+def finish_kernel(steps, place, *refs):
+    parts, (prefill, decode) = refs[: 2 * steps], refs[2 * steps :]
+    rows = prefill.shape[0] // 2
+    count = decode.shape[0]
+
+    def tree(terms):
+        while len(terms) > 1:
+            terms = [a + b for a, b in zip(terms[::2], terms[1::2])]
+        return terms[0]
+
+    for other in range(2):
+        total = tree([parts[2 * step + other][...].astype(jnp.float32) for step in range(steps)])
+        total = total.astype(jnp.bfloat16)
+        prefill[pl.ds(pl.multiple_of((place[2] ^ other) * rows, rows), rows), :] = total[:rows]
+        if other == 0:
+            decode[...] = total[rows : rows + count]
+
+
+def on_device_small(
+    steps, tp, tokens, new_token_states, w_query, key_matrix, value_matrix, w_out, lengths, block_map
+):
+    bf16, f32 = jnp.bfloat16, jnp.float32
+    rows = tokens.shape[0] // 2
+    depth = w_query.shape[0]
+    count = new_token_states.shape[0]
+    pad = -(-count // ROW_TILE) * ROW_TILE
+    q_width = 2 * w_query.shape[1]
+    kv_width = 2 * key_matrix.shape[1]
+    features = q_width + 2 * kv_width
+    width = w_out.shape[1] // 2
+    c, t = lax.axis_index("ctx"), lax.axis_index("tp")
+    place = jnp.stack([c, t // 2, t % 2]).astype(jnp.int32)
+
+    def to_core(value):
+        return lax.ppermute(value, "tp", [(i, i ^ 1) for i in range(tp)])
+
+    def to_ctx(value, step):
+        return lax.ppermute(value, "ctx", [(i, i ^ step) for i in range(steps)])
+
+    sent = pl.pallas_call(
+        slice_kernel,
+        out_shape=[jax.ShapeDtypeStruct((rows, depth), bf16)] * (steps - 1),
+        in_specs=[smem(), hbm()],
+        out_specs=[hbm()] * (steps - 1),
+        scratch_shapes=[pltpu.SemaphoreType.DMA((steps - 1,))],
+        name="slice_tokens",
+    )(place, tokens)
+    got = [to_ctx(value, step) for step, value in enumerate(sent, 1)]
+    wq2, wk2, wv2, wo2 = (to_core(w) for w in (w_query, key_matrix, value_matrix, w_out))
+
+    def whole(shape):
+        return pl.BlockSpec(shape, lambda i, at: (0,) * len(shape))
+
+    part_shape = (rows + pad, features)
+    x_rows = -(-(steps * rows + pad) // 16) * 16
+    weights = (w_query, wq2, key_matrix, wk2, value_matrix, wv2)
+    parts = pl.pallas_call(
+        functools.partial(project_kernel, steps),
+        out_shape=[jax.ShapeDtypeStruct(part_shape, f32)]
+        + [jax.ShapeDtypeStruct(part_shape, bf16)] * (steps - 1),
+        grid_spec=pltpu.PrefetchScalarGridSpec(
+            num_scalar_prefetch=1,
+            grid=(1,),
+            in_specs=[pl.BlockSpec((rows, depth), lambda i, at: (at[2], at[0]))]
+            + [whole((rows, depth))] * (steps - 1)
+            + [pl.BlockSpec((count, depth), lambda i, at: (0, at[0]))]
+            + [whole(w.shape) for w in weights],
+            out_specs=[whole(part_shape)] * steps,
+            scratch_shapes=[pltpu.VMEM((x_rows, depth), bf16)],
+        ),
+        compiler_params=params(),
+        name="project",
+    )(place, tokens, *got, new_token_states, *weights)
+
+    parts = [parts[0]] + [to_ctx(part, step) for step, part in enumerate(parts[1:], 1)]
+    query, keyval, new = pl.pallas_call(
+        functools.partial(add_kernel, steps),
+        out_shape=[
+            jax.ShapeDtypeStruct((rows, q_width), bf16),
+            jax.ShapeDtypeStruct((rows, 2 * kv_width), bf16),
+            jax.ShapeDtypeStruct((pad, features), bf16),
+        ],
+        in_specs=[vmem()] * steps,
+        out_specs=[vmem()] * 3,
+        compiler_params=params(),
+        name="add_parts",
+    )(*parts)
+
+    mine = [keyval] + [to_ctx(keyval, step) for step in range(1, steps)]
+    queries = [query] + [to_ctx(query, step) for step in range(1, steps)]
+    theirs = [to_core(value) for value in mine]
+
+    k_rows = -(-(2 * steps * rows + pad) // 128) * 128
+    out_shape = (rows + pad, width)
+    outs = pl.pallas_call(
+        functools.partial(attend_kernel, steps, count, 1.0 / math.sqrt(HEAD_SIZE)),
+        out_shape=[jax.ShapeDtypeStruct(out_shape, bf16)] * (2 * steps),
+        in_specs=[smem()] * 3 + [vmem()] * (3 * steps + 3),
+        out_specs=[vmem()] * (2 * steps),
+        scratch_shapes=[
+            pltpu.VMEM((x_rows, q_width), bf16),
+            pltpu.VMEM((k_rows, kv_width), bf16),
+            pltpu.VMEM((k_rows, kv_width), bf16),
+            pltpu.VMEM((x_rows, q_width), bf16),
+            pltpu.VMEM((x_rows, 2 * width), bf16),
+        ],
+        compiler_params=params(),
+        name="attend",
+    )(place, block_map, lengths, *queries, *mine, *theirs, new, w_out, wo2)
+
+    def to_owner(value, step, other):
+        pairs = []
+        for source in range(steps * tp):
+            at, rest = divmod(source, tp)
+            z, core = divmod(rest, 2)
+            pairs.append((source, (z ^ step) * tp + 2 * at + (core ^ other)))
+        return lax.ppermute(value, ("ctx", "tp"), pairs)
+
+    arrived = [to_owner(value, i // 2, i % 2) for i, value in enumerate(outs)]
+    return tuple(
+        pl.pallas_call(
+            functools.partial(finish_kernel, steps),
+            out_shape=[
+                jax.ShapeDtypeStruct((2 * rows, width), bf16),
+                jax.ShapeDtypeStruct((count, width), bf16),
+            ],
+            in_specs=[smem()] + [vmem()] * (2 * steps),
+            out_specs=[vmem()] * 2,
+            compiler_params=params(),
+            name="finish",
+        )(place, *arrived)
+    )
 
 
 floor_value = -1e30
@@ -57,7 +367,7 @@
     return (part_peak, part_total, part_mixed)
 
 
-def on_device(
+def on_device_large(
     tokens, new_token_states, w_query, key_matrix, value_matrix, w_out, lengths, block_map
 ):
     local_rows = tokens.shape[0]
@@ -188,8 +498,15 @@
     summed_rows = summed_rows.astype(jnp.bfloat16)
     return (summed_rows[:local_rows], summed_rows[local_rows:])
 
-
 def solution(mesh):
+    steps, tp = mesh.shape["ctx"], mesh.shape["tp"]
+
+    def on_device(tokens, *rest):
+        small = tp == 2 * steps and steps & (steps - 1) == 0 and tokens.shape[0] * steps <= 1024
+        if small:
+            return on_device_small(steps, tp, tokens, *rest)
+        return on_device_large(tokens, *rest)
+
     return jax.shard_map(
         on_device,
         mesh=mesh,

time: 184 us -> 101 us (0.55)
  the two profiles are of different devices: /device:TPU:0 before, /device:TPU:5 now
where the time goes in v1:
time: 101 us; the launch traced here: 100 us
  starting transfers between devices  48.4 us (48%)
  waiting for transfers between devices  28.2 us (28%)
  Pallas kernels  19.3 us (19%)
  local copies, waits for them, and re-layouts  2.96 us (3%)
    ppermute x8, starting transfers between devices, to_owner(): return lax.ppermute(value, ('ctx', 'tp'), pairs)  29.9 us
    ppermute x12, waiting for transfers between devices, to_ctx(): return lax.ppermute(value, 'ctx', [(i, i ^ step) for i in range(steps)])  14.1 us
    pallas_call x1, Pallas kernels, on_device_small(): pl.pallas_call(slice_kernel, out_shape=[jax.ShapeDtypeStruct((rows, depth...  13.8 us
    ppermute x8, waiting for transfers between devices, to_owner(): return lax.ppermute(value, ('ctx', 'tp'), pairs)  13.2 us
    ppermute x12, starting transfers between devices, to_ctx(): return lax.ppermute(value, 'ctx', [(i, i ^ step) for i in range(steps)])  9.93 us
    ppermute x8, starting transfers between devices, to_core(): return lax.ppermute(value, 'tp', [(i, i ^ 1) for i in range(tp)])  8.63 us
    unnamed x18, local copies, waits for them, and re-layouts  2.96 us
    pallas_call x1, Pallas kernels, on_device_small(): pl.pallas_call(functools.partial(attend_kernel, steps, count, 1.0 / math....  2.84 us
  transfers between devices with their start and end apart: 28, of which 10 were waited for; matrix products, arithmetic and copies ran while one was open for 1% of the time, Pallas kernels for 15%

profile of v1, /device:TPU:5, one launch (start us, length us, event | category | flops | bytes accessed | tf_op | source)
XLA Modules:
  0.0 100.3 jit_solution(14185636735513768437)
XLA Ops:
  0.6 0.7 collective-permute-start.3
  2.0 13.8 %slice_tokens.1 = (bf16[64,1024]{1,0:T(8,128)(2,1)}, bf16[64,1024]{1,0:T(8,128)(2,1)}, bf16[64,1024]{1,0:T(8,128)(2,1)}) custom-call(s32[3]{0:T(128)} %pad_add_fusion.place, bf16[128,4096]{1,0:T(8,128)(2,1)} %own.1), custom_call_target="tpu_custom_call" | custom-call | tf_op jit(solution)/shard_map/slice_tokens/pallas_call | solution.py:226
  15.9 1.3 %collective-permute-start = (bf16[64,1024]{1,0:T(8,128)(2,1)}, bf16[64,1024]{1,0:T(8,128)(2,1)S(1)}, u32[]{:S(2)}, u32[]{:S(2)}) collective-permute-start(bf16[64,1024]{1,0:T(8,128)(2,1)} %get-tuple-element.20), channel_id=1, source_target_pairs={{0,8},{8,0},{16,24},{24,16},{1,9},{9,1},{17,25},{25,17},{2,10},{10... | collective-permute-start | bytes 393224 | tf_op jit(solution)/shard_map/ppermute | solution.py:224
  18.2 3.1 %collective-permute-done.rest_0_ = bf16[64,1024]{1,0:T(8,128)(2,1)S(1)} collective-permute-done((bf16[64,1024]{1,0:T(8,128)(2,1)}, bf16[64,1024]{1,0:T(8,128)(2,1)S(1)}, u32[]{:S(2)}, u32[]{:S(2)}) %collective-permute-start) | collective-permute-done | bytes 131104 | tf_op jit(solution)/shard_map/ppermute | solution.py:224
  21.2 0.8 collective-permute-start.5
  23.2 4.3 %collective-permute-done.2.rest_2_ = bf16[64,1024]{1,0:T(8,128)(2,1)S(1)} collective-permute-done((bf16[64,1024]{1,0:T(8,128)(2,1)}, bf16[64,1024]{1,0:T(8,128)(2,1)S(1)}, u32[]{:S(2)}, u32[]{:S(2)}) %collective-permute-start.2) | collective-permute-done | bytes 131104 | tf_op jit(solution)/shard_map/ppermute | solution.py:224
  27.6 1.0 %copy-done.2 = bf16[1024,256]{1,0:T(8,128)(2,1)S(1)} copy-done((bf16[1024,256]{1,0:T(8,128)(2,1)S(1)}, bf16[1024,256]{1,0:T(8,128)(2,1)}, u32[]{:S(2)}) %copy-start.2) | copy-done | bytes 524312
  28.6 0.9 copy-done.3
  29.6 0.9 copy-done.4
  30.5 1.3 %project.1 = (f32[72,1024]{1,0:T(8,128)S(1)}, bf16[72,1024]{1,0:T(8,128)(2,1)S(1)}, bf16[72,1024]{1,0:T(8,128)(2,1)S(1)}, bf16[72,1024]{1,0:T(8,128)(2,1)S(1)}) custom-call(s32[3]{0:T(128)S(1)} %copy-done.6, bf16[128,4096]{1,0:T(8,128)(2,1)S(1)} %copy-done, bf16[64,1024]{1,0:T(8,128)(2,1)S(1)} %collective-permute-done.rest_0_, ...), custom_call_target="tpu_custom_call" | custom-call | tf_op jit(solution)/shard_map/project/pallas_call | solution.py:243
  31.8 1.4 %collective-permute-start.6 = (bf16[72,1024]{1,0:T(8,128)(2,1)S(1)}, bf16[72,1024]{1,0:T(8,128)(2,1)S(1)}, u32[]{:S(2)}, u32[]{:S(2)}) collective-permute-start(bf16[72,1024]{1,0:T(8,128)(2,1)S(1)} %get-tuple-element.24), channel_id=1, source_target_pairs={{0,8},{8,0},{16,24},{24,16},{1,9},{9,1},{17,25},{25,17},{2,10},{10... | collective-permute-start | bytes 442376 | tf_op jit(solution)/shard_map/ppermute | solution.py:224
  33.7 0.8 collective-permute-start.8
  34.5 1.3 %collective-permute-done.6.refs_1_ = bf16[72,1024]{1,0:T(8,128)(2,1)S(1)} collective-permute-done((bf16[72,1024]{1,0:T(8,128)(2,1)S(1)}, bf16[72,1024]{1,0:T(8,128)(2,1)S(1)}, u32[]{:S(2)}, u32[]{:S(2)}) %collective-permute-start.6) | collective-permute-done | bytes 147488 | tf_op jit(solution)/shard_map/ppermute | solution.py:224
  35.9 1.9 %collective-permute-done.7.refs_2_ = bf16[72,1024]{1,0:T(8,128)(2,1)S(1)} collective-permute-done((bf16[72,1024]{1,0:T(8,128)(2,1)S(1)}, bf16[72,1024]{1,0:T(8,128)(2,1)S(1)}, u32[]{:S(2)}, u32[]{:S(2)}) %collective-permute-start.7) | collective-permute-done | bytes 147488 | tf_op jit(solution)/shard_map/ppermute | solution.py:224
  37.7 2.7 %collective-permute-done.8.refs_3_ = bf16[72,1024]{1,0:T(8,128)(2,1)S(1)} collective-permute-done((bf16[72,1024]{1,0:T(8,128)(2,1)S(1)}, bf16[72,1024]{1,0:T(8,128)(2,1)S(1)}, u32[]{:S(2)}, u32[]{:S(2)}) %collective-permute-start.8) | collective-permute-done | bytes 147488 | tf_op jit(solution)/shard_map/ppermute | solution.py:224
  41.1 0.7 collective-permute-start.10
  41.8 1.8 %collective-permute-start.14 = (bf16[64,512]{1,0:T(8,128)(2,1)S(1)}, bf16[64,512]{1,0:T(8,128)(2,1)S(1)}, u32[]{:S(2)}, u32[]{:S(2)}) collective-permute-start(bf16[64,512]{1,0:T(8,128)(2,1)S(1)} %get-tuple-element.28.refs_4_), channel_id=1, source_target_pairs={{0,24},{8,16},{16,8},{24,0},{1,25},{9,17},{17,9},{25,1},{2,26},{10... | collective-permute-start | bytes 196616 | tf_op jit(solution)/shard_map/ppermute | solution.py:224
  43.6 0.8 collective-permute-start.13
  44.8 1.2 %collective-permute-start.9 = (bf16[64,512]{1,0:T(8,128)(2,1)S(1)}, bf16[64,512]{1,0:T(8,128)(2,1)S(1)}, u32[]{:S(2)}, u32[]{:S(2)}) collective-permute-start(bf16[64,512]{1,0:T(8,128)(2,1)S(1)} %get-tuple-element.27.refs_0_), channel_id=1, source_target_pairs={{0,8},{8,0},{16,24},{24,16},{1,9},{9,1},{17,25},{25,17},{2,10},{10... | collective-permute-start | bytes 196616 | tf_op jit(solution)/shard_map/ppermute | solution.py:224
  46.0 4.1 %collective-permute-start.15 = (bf16[64,512]{1,0:T(8,128)(2,1)S(1)}, bf16[64,512]{1,0:T(8,128)(2,1)S(1)}, u32[]{:S(2)}, u32[]{:S(2)}) collective-permute-start(bf16[64,512]{1,0:T(8,128)(2,1)S(1)} %get-tuple-element.28.refs_4_), channel_id=1, source_target_pairs={{0,1},{1,0},{2,3},{3,2},{4,5},{5,4},{6,7},{7,6},{8,9},{9,8},{10,11... | collective-permute-start | bytes 196616 | tf_op jit(solution)/shard_map/ppermute | solution.py:221
  51.2 1.1 %collective-permute-start.16 = (bf16[64,512]{1,0:T(8,128)(2,1)S(1)}, bf16[64,512]{1,0:T(8,128)(2,1)S(1)}, u32[]{:S(2)}, u32[]{:S(2)}) collective-permute-start(bf16[64,512]{1,0:T(8,128)(2,1)S(1)} %collective-permute-done.12.refs_5_), channel_id=1, source_target_pairs={{0,1},{1,0},{2,3},{3,2},{4,5},{5,4},{6,7},{7,6},{8,9},{9,8},{10,11... | collective-permute-start | bytes 196616 | tf_op jit(solution)/shard_map/ppermute | solution.py:221
  52.3 0.9 collective-permute-done.16.refs_9_
  53.2 2.8 %attend.1 = (bf16[72,512]{1,0:T(8,128)(2,1)S(1)}, bf16[72,512]{1,0:T(8,128)(2,1)S(1)}, bf16[72,512]{1,0:T(8,128)(2,1)S(1)}, bf16[72,512]{1,0:T(8,128)(2,1)S(1)},...) custom-call(s32[3]{0:T(128)S(1)} %copy-done.6, ...), custom_call_target="tpu_custom_call" | custom-call | tf_op jit(solution)/shard_map/attend/pallas_call | solution.py:281
  56.0 4.5 %collective-permute-start.20 = (bf16[72,512]{1,0:T(8,128)(2,1)S(1)}, bf16[72,512]{1,0:T(8,128)(2,1)S(1)}, u32[]{:S(2)}, u32[]{:S(2)}) collective-permute-start(bf16[72,512]{1,0:T(8,128)(2,1)S(1)} %get-tuple-element.30), channel_id=1, source_target_pairs={{0,0},{1,1},{2,8},{3,9},{4,16},{5,17},{6,24},{7,25},{8,2},{9,3},{1... | collective-permute-start | bytes 221192 | tf_op jit(solution)/shard_map/ppermute | solution.py:303
  60.5 1.3 %collective-permute-start.21 = (bf16[72,512]{1,0:T(8,128)(2,1)S(1)}, bf16[72,512]{1,0:T(8,128)(2,1)S(1)}, u32[]{:S(2)}, u32[]{:S(2)}) collective-permute-start(bf16[72,512]{1,0:T(8,128)(2,1)S(1)} %get-tuple-element.31), channel_id=1, source_target_pairs={{0,1},{1,0},{2,9},{3,8},{4,17},{5,16},{6,25},{7,24},{8,3},{9,2},{1... | collective-permute-start | bytes 221192 | tf_op jit(solution)/shard_map/ppermute | solution.py:303
  61.8 2.9 %collective-permute-start.22 = (bf16[72,512]{1,0:T(8,128)(2,1)S(1)}, bf16[72,512]{1,0:T(8,128)(2,1)S(1)}, u32[]{:S(2)}, u32[]{:S(2)}) collective-permute-start(bf16[72,512]{1,0:T(8,128)(2,1)S(1)} %get-tuple-element.32), channel_id=1, source_target_pairs={{0,8},{1,9},{2,0},{3,1},{4,24},{5,25},{6,16},{7,17},{8,10},{9,11},... | collective-permute-start | bytes 221192 | tf_op jit(solution)/shard_map/ppermute | solution.py:303
  65.2 4.6 %collective-permute-start.25 = (bf16[72,512]{1,0:T(8,128)(2,1)S(1)}, bf16[72,512]{1,0:T(8,128)(2,1)S(1)}, u32[]{:S(2)}, u32[]{:S(2)}) collective-permute-start(bf16[72,512]{1,0:T(8,128)(2,1)S(1)} %get-tuple-element.35), channel_id=1, source_target_pairs={{0,17},{1,16},{2,25},{3,24},{4,1},{5,0},{6,9},{7,8},{8,19},{9,18},... | collective-permute-start | bytes 221192 | tf_op jit(solution)/shard_map/ppermute | solution.py:303
  69.8 12.8 %collective-permute-start.26 = (bf16[72,512]{1,0:T(8,128)(2,1)S(1)}, bf16[72,512]{1,0:T(8,128)(2,1)S(1)}, u32[]{:S(2)}, u32[]{:S(2)}) collective-permute-start(bf16[72,512]{1,0:T(8,128)(2,1)S(1)} %get-tuple-element.36), channel_id=1, source_target_pairs={{0,24},{1,25},{2,16},{3,17},{4,8},{5,9},{6,0},{7,1},{8,26},{9,27},... | collective-permute-start | bytes 221192 | tf_op jit(solution)/shard_map/ppermute | solution.py:303
  82.6 3.3 %collective-permute-start.27 = (bf16[72,512]{1,0:T(8,128)(2,1)S(1)}, bf16[72,512]{1,0:T(8,128)(2,1)S(1)}, u32[]{:S(2)}, u32[]{:S(2)}) collective-permute-start(bf16[72,512]{1,0:T(8,128)(2,1)S(1)} %get-tuple-element.37), channel_id=1, source_target_pairs={{0,25},{1,24},{2,17},{3,16},{4,9},{5,8},{6,1},{7,0},{8,27},{9,26},... | collective-permute-start | bytes 221192 | tf_op jit(solution)/shard_map/ppermute | solution.py:303
  85.9 11.6 %collective-permute-done.26.refs_6_ = bf16[72,512]{1,0:T(8,128)(2,1)S(1)} collective-permute-done((bf16[72,512]{1,0:T(8,128)(2,1)S(1)}, bf16[72,512]{1,0:T(8,128)(2,1)S(1)}, u32[]{:S(2)}, u32[]{:S(2)}) %collective-permute-start.26) | collective-permute-done | bytes 73760 | tf_op jit(solution)/shard_map/ppermute | solution.py:303
  97.5 1.6 %collective-permute-done.27.refs_7_ = bf16[72,512]{1,0:T(8,128)(2,1)S(1)} collective-permute-done((bf16[72,512]{1,0:T(8,128)(2,1)S(1)}, bf16[72,512]{1,0:T(8,128)(2,1)S(1)}, u32[]{:S(2)}, u32[]{:S(2)}) %collective-permute-start.27) | collective-permute-done | bytes 73760 | tf_op jit(solution)/shard_map/ppermute | solution.py:303
  99.0 1.3 %finish.1 = (bf16[128,512]{1,0:T(8,128)(2,1)}, bf16[4,512]{1,0:T(4,128)(2,1)}) custom-call(s32[3]{0:T(128)S(1)} %copy-done.6, bf16[72,512]{1,0:T(8,128)(2,1)S(1)} %collective-permute-done.20.refs_0_, bf16[72,512]{1,0:T(8,128)(2,1)S(1)} %collective-permute-done.21.refs_1_, bf16[72,512]{1,0:T(8,128)(2,1)S(1)} %collective-permute-done.22.refs_2_, ...), custom_call_target="tpu_custom_call" | custom-call | tf_op jit(solution)/shard_map/finish/pallas_call | solution.py:307
  (48 shorter events, 6.0 us)
Async XLA Ops:
  0.6 26.9 %copy-start = (bf16[128,4096]{1,0:T(8,128)(2,1)S(1)}, bf16[128,4096]{1,0:T(8,128)(2,1)}, u32[]{:S(2)}) copy-start(bf16[128,4096]{1,0:T(8,128)(2,1)} %own.1) | copy-start | bytes 3145732
  0.6 26.9 %collective-permute-start.3 = (bf16[1024,256]{1,0:T(8,128)(2,1)}, bf16[1024,256]{1,0:T(8,128)(2,1)S(1)}, u32[]{:S(2)}, u32[]{:S(2)}) collective-permute-start(bf16[1024,256]{1,0:T(8,128)(2,1)} %rest_4_.1), channel_id=1, source_target_pairs={{0,1},{1,0},{2,3},{3,2},{4,5},{5,4},{6,7},{7,6},{8,9},{9,8},{10,11... | collective-permute-start | bytes 1572872 | tf_op jit(solution)/shard_map/ppermute | solution.py:221
  2.0 25.5 %copy-start.5 = (bf16[4,4096]{1,0:T(4,128)(2,1)S(1)}, bf16[4,4096]{1,0:T(4,128)(2,1)}, u32[]{:S(2)}) copy-start(bf16[4,4096]{1,0:T(4,128)(2,1)} %rest_3_.1) | copy-start | bytes 98308
  15.9 5.4 %collective-permute-start = (bf16[64,1024]{1,0:T(8,128)(2,1)}, bf16[64,1024]{1,0:T(8,128)(2,1)S(1)}, u32[]{:S(2)}, u32[]{:S(2)}) collective-permute-start(bf16[64,1024]{1,0:T(8,128)(2,1)} %get-tuple-element.20), channel_id=1, source_target_pairs={{0,8},{8,0},{16,24},{24,16},{1,9},{9,1},{17,25},{25,17},{2,10},{10... | collective-permute-start | bytes 393224 | tf_op jit(solution)/shard_map/ppermute | solution.py:224
  17.2 27.3 %collective-permute-start.19 = (bf16[256,1024]{1,0:T(8,128)(2,1)}, bf16[256,1024]{1,0:T(8,128)(2,1)S(1)}, u32[]{:S(2)}, u32[]{:S(2)}) collective-permute-start(bf16[256,1024]{1,0:T(8,128)(2,1)} %refs_13_.1), channel_id=1, source_target_pairs={{0,1},{1,0},{2,3},{3,2},{4,5},{5,4},{6,7},{7,6},{8,9},{9,8},{10,11... | collective-permute-start | bytes 1572872 | tf_op jit(solution)/shard_map/ppermute | solution.py:221
  17.5 5.1 %collective-permute-start.1 = (bf16[64,1024]{1,0:T(8,128)(2,1)}, bf16[64,1024]{1,0:T(8,128)(2,1)S(1)}, u32[]{:S(2)}, u32[]{:S(2)}) collective-permute-start(bf16[64,1024]{1,0:T(8,128)(2,1)} %get-tuple-element.21), channel_id=1, source_target_pairs={{0,16},{8,24},{16,0},{24,8},{1,17},{9,25},{17,1},{25,9},{2,18},{10... | collective-permute-start | bytes 393224 | tf_op jit(solution)/shard_map/ppermute | solution.py:224
  17.7 9.8 %collective-permute-start.4 = (bf16[1024,128]{1,0:T(8,128)(2,1)}, bf16[1024,128]{1,0:T(8,128)(2,1)S(1)}, u32[]{:S(2)}, u32[]{:S(2)}) collective-permute-start(bf16[1024,128]{1,0:T(8,128)(2,1)} %rest_6_.1), channel_id=1, source_target_pairs={{0,1},{1,0},{2,3},{3,2},{4,5},{5,4},{6,7},{7,6},{8,9},{9,8},{10,11... | collective-permute-start | bytes 786440 | tf_op jit(solution)/shard_map/ppermute | solution.py:221
  21.2 6.3 %collective-permute-start.5 = (bf16[1024,128]{1,0:T(8,128)(2,1)}, bf16[1024,128]{1,0:T(8,128)(2,1)S(1)}, u32[]{:S(2)}, u32[]{:S(2)}) collective-permute-start(bf16[1024,128]{1,0:T(8,128)(2,1)} %rest_8_.1), channel_id=1, source_target_pairs={{0,1},{1,0},{2,3},{3,2},{4,5},{5,4},{6,7},{7,6},{8,9},{9,8},{10,11... | collective-permute-start | bytes 786440 | tf_op jit(solution)/shard_map/ppermute | solution.py:221
  22.6 4.9 %collective-permute-start.2 = (bf16[64,1024]{1,0:T(8,128)(2,1)}, bf16[64,1024]{1,0:T(8,128)(2,1)S(1)}, u32[]{:S(2)}, u32[]{:S(2)}) collective-permute-start(bf16[64,1024]{1,0:T(8,128)(2,1)} %get-tuple-element.22), channel_id=1, source_target_pairs={{0,24},{8,16},{16,8},{24,0},{1,25},{9,17},{17,9},{25,1},{2,26},{10... | collective-permute-start | bytes 393224 | tf_op jit(solution)/shard_map/ppermute | solution.py:224
  31.8 21.3 %copy-start.1 = (bf16[256,1024]{1,0:T(8,128)(2,1)S(1)}, bf16[256,1024]{1,0:T(8,128)(2,1)}, u32[]{:S(2)}) copy-start(bf16[256,1024]{1,0:T(8,128)(2,1)} %refs_13_.1) | copy-start | bytes 1572868
  31.8 4.1 %collective-permute-start.6 = (bf16[72,1024]{1,0:T(8,128)(2,1)S(1)}, bf16[72,1024]{1,0:T(8,128)(2,1)S(1)}, u32[]{:S(2)}, u32[]{:S(2)}) collective-permute-start(bf16[72,1024]{1,0:T(8,128)(2,1)S(1)} %get-tuple-element.24), channel_id=1, source_target_pairs={{0,8},{8,0},{16,24},{24,16},{1,9},{9,1},{17,25},{25,17},{2,10},{10... | collective-permute-start | bytes 442376 | tf_op jit(solution)/shard_map/ppermute | solution.py:224
  33.3 4.5 %collective-permute-start.7 = (bf16[72,1024]{1,0:T(8,128)(2,1)S(1)}, bf16[72,1024]{1,0:T(8,128)(2,1)S(1)}, u32[]{:S(2)}, u32[]{:S(2)}) collective-permute-start(bf16[72,1024]{1,0:T(8,128)(2,1)S(1)} %get-tuple-element.25), channel_id=1, source_target_pairs={{0,16},{8,24},{16,0},{24,8},{1,17},{9,25},{17,1},{25,9},{2,18},{10... | collective-permute-start | bytes 442376 | tf_op jit(solution)/shard_map/ppermute | solution.py:224
  33.7 6.8 %collective-permute-start.8 = (bf16[72,1024]{1,0:T(8,128)(2,1)S(1)}, bf16[72,1024]{1,0:T(8,128)(2,1)S(1)}, u32[]{:S(2)}, u32[]{:S(2)}) collective-permute-start(bf16[72,1024]{1,0:T(8,128)(2,1)S(1)} %get-tuple-element.26), channel_id=1, source_target_pairs={{0,24},{8,16},{16,8},{24,0},{1,25},{9,17},{17,9},{25,1},{2,26},{10... | collective-permute-start | bytes 442376 | tf_op jit(solution)/shard_map/ppermute | solution.py:224
  40.6 4.2 %collective-permute-start.11 = (bf16[64,512]{1,0:T(8,128)(2,1)S(1)}, bf16[64,512]{1,0:T(8,128)(2,1)S(1)}, u32[]{:S(2)}, u32[]{:S(2)}) collective-permute-start(bf16[64,512]{1,0:T(8,128)(2,1)S(1)} %get-tuple-element.27.refs_0_), channel_id=1, source_target_pairs={{0,24},{8,16},{16,8},{24,0},{1,25},{9,17},{17,9},{25,1},{2,26},{10... | collective-permute-start | bytes 196616 | tf_op jit(solution)/shard_map/ppermute | solution.py:224
  41.1 4.9 %collective-permute-start.10 = (bf16[64,512]{1,0:T(8,128)(2,1)S(1)}, bf16[64,512]{1,0:T(8,128)(2,1)S(1)}, u32[]{:S(2)}, u32[]{:S(2)}) collective-permute-start(bf16[64,512]{1,0:T(8,128)(2,1)S(1)} %get-tuple-element.27.refs_0_), channel_id=1, source_target_pairs={{0,16},{8,24},{16,0},{24,8},{1,17},{9,25},{17,1},{25,9},{2,18},{10... | collective-permute-start | bytes 196616 | tf_op jit(solution)/shard_map/ppermute | solution.py:224
  41.8 11.3 %copy-start.8 = (s32[4]{0:T(128)S(1)}, s32[4]{0:T(128)}, u32[]{:S(2)}) copy-start(s32[4]{0:T(128)} %lengths.1) | copy-start | bytes 52
  41.8 8.2 %collective-permute-start.14 = (bf16[64,512]{1,0:T(8,128)(2,1)S(1)}, bf16[64,512]{1,0:T(8,128)(2,1)S(1)}, u32[]{:S(2)}, u32[]{:S(2)}) collective-permute-start(bf16[64,512]{1,0:T(8,128)(2,1)S(1)} %get-tuple-element.28.refs_4_), channel_id=1, source_target_pairs={{0,24},{8,16},{16,8},{24,0},{1,25},{9,17},{17,9},{25,1},{2,26},{10... | collective-permute-start | bytes 196616 | tf_op jit(solution)/shard_map/ppermute | solution.py:224
  43.6 6.8 %collective-permute-start.13 = (bf16[64,512]{1,0:T(8,128)(2,1)S(1)}, bf16[64,512]{1,0:T(8,128)(2,1)S(1)}, u32[]{:S(2)}, u32[]{:S(2)}) collective-permute-start(bf16[64,512]{1,0:T(8,128)(2,1)S(1)} %get-tuple-element.28.refs_4_), channel_id=1, source_target_pairs={{0,16},{8,24},{16,0},{24,8},{1,17},{9,25},{17,1},{25,9},{2,18},{10... | collective-permute-start | bytes 196616 | tf_op jit(solution)/shard_map/ppermute | solution.py:224
  44.5 6.7 %collective-permute-start.12 = (bf16[64,512]{1,0:T(8,128)(2,1)S(1)}, bf16[64,512]{1,0:T(8,128)(2,1)S(1)}, u32[]{:S(2)}, u32[]{:S(2)}) collective-permute-start(bf16[64,512]{1,0:T(8,128)(2,1)S(1)} %get-tuple-element.28.refs_4_), channel_id=1, source_target_pairs={{0,8},{8,0},{16,24},{24,16},{1,9},{9,1},{17,25},{25,17},{2,10},{10... | collective-permute-start | bytes 196616 | tf_op jit(solution)/shard_map/ppermute | solution.py:224
  44.8 7.5 %collective-permute-start.9 = (bf16[64,512]{1,0:T(8,128)(2,1)S(1)}, bf16[64,512]{1,0:T(8,128)(2,1)S(1)}, u32[]{:S(2)}, u32[]{:S(2)}) collective-permute-start(bf16[64,512]{1,0:T(8,128)(2,1)S(1)} %get-tuple-element.27.refs_0_), channel_id=1, source_target_pairs={{0,8},{8,0},{16,24},{24,16},{1,9},{9,1},{17,25},{25,17},{2,10},{10... | collective-permute-start | bytes 196616 | tf_op jit(solution)/shard_map/ppermute | solution.py:224
  46.0 6.3 %collective-permute-start.15 = (bf16[64,512]{1,0:T(8,128)(2,1)S(1)}, bf16[64,512]{1,0:T(8,128)(2,1)S(1)}, u32[]{:S(2)}, u32[]{:S(2)}) collective-permute-start(bf16[64,512]{1,0:T(8,128)(2,1)S(1)} %get-tuple-element.28.refs_4_), channel_id=1, source_target_pairs={{0,1},{1,0},{2,3},{3,2},{4,5},{5,4},{6,7},{7,6},{8,9},{9,8},{10,11... | collective-permute-start | bytes 196616 | tf_op jit(solution)/shard_map/ppermute | solution.py:221
  50.0 2.2 %collective-permute-start.18 = (bf16[64,512]{1,0:T(8,128)(2,1)S(1)}, bf16[64,512]{1,0:T(8,128)(2,1)S(1)}, u32[]{:S(2)}, u32[]{:S(2)}) collective-permute-start(bf16[64,512]{1,0:T(8,128)(2,1)S(1)} %collective-permute-done.14.refs_7_), channel_id=1, source_target_pairs={{0,1},{1,0},{2,3},{3,2},{4,5},{5,4},{6,7},{7,6},{8,9},{9,8},{10,11... | collective-permute-start | bytes 196616 | tf_op jit(solution)/shard_map/ppermute | solution.py:221
  50.5 1.8 %collective-permute-start.17 = (bf16[64,512]{1,0:T(8,128)(2,1)S(1)}, bf16[64,512]{1,0:T(8,128)(2,1)S(1)}, u32[]{:S(2)}, u32[]{:S(2)}) collective-permute-start(bf16[64,512]{1,0:T(8,128)(2,1)S(1)} %collective-permute-done.13.refs_6_), channel_id=1, source_target_pairs={{0,1},{1,0},{2,3},{3,2},{4,5},{5,4},{6,7},{7,6},{8,9},{9,8},{10,11... | collective-permute-start | bytes 196616 | tf_op jit(solution)/shard_map/ppermute | solution.py:221
  51.2 2.0 %collective-permute-start.16 = (bf16[64,512]{1,0:T(8,128)(2,1)S(1)}, bf16[64,512]{1,0:T(8,128)(2,1)S(1)}, u32[]{:S(2)}, u32[]{:S(2)}) collective-permute-start(bf16[64,512]{1,0:T(8,128)(2,1)S(1)} %collective-permute-done.12.refs_5_), channel_id=1, source_target_pairs={{0,1},{1,0},{2,3},{3,2},{4,5},{5,4},{6,7},{7,6},{8,9},{9,8},{10,11... | collective-permute-start | bytes 196616 | tf_op jit(solution)/shard_map/ppermute | solution.py:221
  56.0 9.2 %collective-permute-start.20 = (bf16[72,512]{1,0:T(8,128)(2,1)S(1)}, bf16[72,512]{1,0:T(8,128)(2,1)S(1)}, u32[]{:S(2)}, u32[]{:S(2)}) collective-permute-start(bf16[72,512]{1,0:T(8,128)(2,1)S(1)} %get-tuple-element.30), channel_id=1, source_target_pairs={{0,0},{1,1},{2,8},{3,9},{4,16},{5,17},{6,24},{7,25},{8,2},{9,3},{1... | collective-permute-start | bytes 221192 | tf_op jit(solution)/shard_map/ppermute | solution.py:303
  60.5 9.2 %collective-permute-start.21 = (bf16[72,512]{1,0:T(8,128)(2,1)S(1)}, bf16[72,512]{1,0:T(8,128)(2,1)S(1)}, u32[]{:S(2)}, u32[]{:S(2)}) collective-permute-start(bf16[72,512]{1,0:T(8,128)(2,1)S(1)} %get-tuple-element.31), channel_id=1, source_target_pairs={{0,1},{1,0},{2,9},{3,8},{4,17},{5,16},{6,25},{7,24},{8,3},{9,2},{1... | collective-permute-start | bytes 221192 | tf_op jit(solution)/shard_map/ppermute | solution.py:303
  61.8 20.8 %collective-permute-start.22 = (bf16[72,512]{1,0:T(8,128)(2,1)S(1)}, bf16[72,512]{1,0:T(8,128)(2,1)S(1)}, u32[]{:S(2)}, u32[]{:S(2)}) collective-permute-start(bf16[72,512]{1,0:T(8,128)(2,1)S(1)} %get-tuple-element.32), channel_id=1, source_target_pairs={{0,8},{1,9},{2,0},{3,1},{4,24},{5,25},{6,16},{7,17},{8,10},{9,11},... | collective-permute-start | bytes 221192 | tf_op jit(solution)/shard_map/ppermute | solution.py:303
  64.7 21.2 %collective-permute-start.23 = (bf16[72,512]{1,0:T(8,128)(2,1)S(1)}, bf16[72,512]{1,0:T(8,128)(2,1)S(1)}, u32[]{:S(2)}, u32[]{:S(2)}) collective-permute-start(bf16[72,512]{1,0:T(8,128)(2,1)S(1)} %get-tuple-element.33), channel_id=1, source_target_pairs={{0,9},{1,8},{2,1},{3,0},{4,25},{5,24},{6,17},{7,16},{8,11},{9,10},... | collective-permute-start | bytes 221192 | tf_op jit(solution)/shard_map/ppermute | solution.py:303
  65.2 20.7 %collective-permute-start.24 = (bf16[72,512]{1,0:T(8,128)(2,1)S(1)}, bf16[72,512]{1,0:T(8,128)(2,1)S(1)}, u32[]{:S(2)}, u32[]{:S(2)}) collective-permute-start(bf16[72,512]{1,0:T(8,128)(2,1)S(1)} %get-tuple-element.34), channel_id=1, source_target_pairs={{0,16},{1,17},{2,24},{3,25},{4,0},{5,1},{6,8},{7,9},{8,18},{9,19},... | collective-permute-start | bytes 221192 | tf_op jit(solution)/shard_map/ppermute | solution.py:303
  65.2 20.7 %collective-permute-start.25 = (bf16[72,512]{1,0:T(8,128)(2,1)S(1)}, bf16[72,512]{1,0:T(8,128)(2,1)S(1)}, u32[]{:S(2)}, u32[]{:S(2)}) collective-permute-start(bf16[72,512]{1,0:T(8,128)(2,1)S(1)} %get-tuple-element.35), channel_id=1, source_target_pairs={{0,17},{1,16},{2,25},{3,24},{4,1},{5,0},{6,9},{7,8},{8,19},{9,18},... | collective-permute-start | bytes 221192 | tf_op jit(solution)/shard_map/ppermute | solution.py:303
  69.8 27.7 %collective-permute-start.26 = (bf16[72,512]{1,0:T(8,128)(2,1)S(1)}, bf16[72,512]{1,0:T(8,128)(2,1)S(1)}, u32[]{:S(2)}, u32[]{:S(2)}) collective-permute-start(bf16[72,512]{1,0:T(8,128)(2,1)S(1)} %get-tuple-element.36), channel_id=1, source_target_pairs={{0,24},{1,25},{2,16},{3,17},{4,8},{5,9},{6,0},{7,1},{8,26},{9,27},... | collective-permute-start | bytes 221192 | tf_op jit(solution)/shard_map/ppermute | solution.py:303
  82.6 16.4 %collective-permute-start.27 = (bf16[72,512]{1,0:T(8,128)(2,1)S(1)}, bf16[72,512]{1,0:T(8,128)(2,1)S(1)}, u32[]{:S(2)}, u32[]{:S(2)}) collective-permute-start(bf16[72,512]{1,0:T(8,128)(2,1)S(1)} %get-tuple-element.37), channel_id=1, source_target_pairs={{0,25},{1,24},{2,17},{3,16},{4,9},{5,8},{6,1},{7,0},{8,27},{9,26},... | collective-permute-start | bytes 221192 | tf_op jit(solution)/shard_map/ppermute | solution.py:303
  (5 other events, 24.4 us)

commit v2 on v1

--- a/solution.py
+++ b/solution.py
@@ -31,29 +31,40 @@
     return pltpu.CompilerParams(vmem_limit_bytes=VMEM_BYTES)
 
 
-def slice_kernel(place, tokens, *rest):
-    outs, sem = rest[:-1], rest[-1]
+def place():
+    t = lax.axis_index("tp")
+    return lax.axis_index("ctx"), t // 2, t % 2
+
+
+def slice_kernel(steps, tokens, new, *rest):
+    outs, new_out, sem = rest[:steps], rest[steps], rest[steps + 1]
+    c, _, k = place()
     rows, width = outs[0].shape
-    first = pl.multiple_of(place[2] * rows, rows)
+    first = pl.multiple_of(k * rows, rows)
     copies = []
-    for step, out in enumerate(outs, 1):
-        column = pl.multiple_of((place[0] ^ step) * width, width)
+    for step, out in enumerate(outs):
+        column = pl.multiple_of((c ^ step) * width, width)
         copies.append(
             pltpu.make_async_copy(
-                tokens.at[pl.ds(first, rows), pl.ds(column, width)], out, sem.at[step - 1]
+                tokens.at[pl.ds(first, rows), pl.ds(column, width)], out, sem.at[step]
             )
         )
     for copy in copies:
         copy.start()
+    new_out[...] = new[:, pl.ds(pl.multiple_of(c * width, width), width)]
     for copy in copies:
         copy.wait()
 
 
-def project_kernel(steps, place, own, *rest):
-    blocks, rest = (own,) + rest[: steps - 1], rest[steps - 1 :]
-    new, wq, wq2, wk, wk2, wv, wv2 = rest[:7]
-    outs, inputs = rest[7 : 7 + steps], rest[7 + steps]
-    rows = own.shape[0]
+def pack_kernel(*refs):
+    out = refs[-1]
+    out[...] = jnp.concatenate([ref[...] for ref in refs[:-1]], axis=1)
+
+
+def project_kernel(steps, parts_of, *refs):
+    blocks, (new, own, other), refs = refs[:steps], refs[steps : steps + 3], refs[steps + 3 :]
+    outs, inputs = refs[:steps], refs[steps]
+    rows = blocks[0].shape[0]
     count = new.shape[0]
     tail = steps * rows
     for step, block in enumerate(blocks):
@@ -61,10 +72,10 @@
     inputs[tail:, :] = jnp.zeros_like(inputs[tail:, :])
     inputs[tail : tail + count, :] = new[...]
     x = inputs[...]
+    pad = outs[0].shape[0] - rows
     column = 0
-    pad = outs[0].shape[0] - rows
-    for first, second in ((wq, wq2), (wk, wk2), (wv, wv2)):
-        weight = jnp.concatenate([first[...], second[...]], axis=1)
+    for start, stop in parts_of:
+        weight = jnp.concatenate([own[:, start:stop], other[:, start:stop]], axis=1)
         part = jnp.dot(x, weight, preferred_element_type=jnp.float32)
         to = slice(column, column + weight.shape[1])
         for step, out in enumerate(outs):
@@ -74,15 +85,13 @@
 
 
 def add_kernel(steps, *refs):
-    parts, (query, keyval, new) = refs[:steps], refs[steps:]
-    rows = query.shape[0]
+    parts, (held, new) = refs[:steps], refs[steps:]
+    rows = held.shape[0]
     total = parts[0][...]
     for part in parts[1:]:
         total = total + part[...].astype(jnp.float32)
     total = total.astype(jnp.bfloat16)
-    half = query.shape[1]
-    query[...] = total[:rows, :half]
-    keyval[...] = total[:rows, half:]
+    held[...] = total[:rows]
     new[...] = total[rows:]
 
 
@@ -93,14 +102,13 @@
     return found
 
 
-def attend_kernel(steps, count, scale, place, block_map, lengths, *refs):
-    queries, refs = refs[:steps], refs[steps:]
+def attend_kernel(steps, count, scale, block_map, lengths, *refs):
     mine, refs = refs[:steps], refs[steps:]
     theirs, refs = refs[:steps], refs[steps:]
     new, w_own, w_other = refs[:3]
-    outs, (q_all, key_all, value_all, attended, result) = refs[3 : 3 + 2 * steps], refs[3 + 2 * steps :]
-    rows, q_width = queries[0].shape
-    kv_width = q_width // 2
+    outs, (q_all, key_all, value_all, attended) = refs[3 : 3 + steps], refs[3 + steps :]
+    rows = mine[0].shape[0]
+    q_width, kv_width = q_all.shape[1], key_all.shape[1]
     head = HEAD_SIZE
     groups = kv_width // head
     per_group = q_width // kv_width
@@ -109,25 +117,26 @@
     q_rows = q_all.shape[0]
     k_rows = key_all.shape[0]
     k_tail = 2 * tail
-    c, z, k = place[0], place[1], place[2]
+    half = kv_width // 2
+    k_at, v_at = q_width, q_width + kv_width
+    c, _, k = place()
 
     q_all[tail:, :] = jnp.zeros_like(q_all[tail:, :])
     key_all[k_tail:, :] = jnp.zeros_like(key_all[k_tail:, :])
     value_all[k_tail:, :] = jnp.zeros_like(value_all[k_tail:, :])
     for step in range(steps):
         at = slice(step * rows, (step + 1) * rows)
-        q_all[at, :] = queries[step][...]
-        key_all[at, :] = mine[step][:, :kv_width]
-        value_all[at, :] = mine[step][:, kv_width:]
+        q_all[at, :] = mine[step][:, :q_width]
+        key_all[at, :] = mine[step][:, k_at:v_at]
+        value_all[at, :] = mine[step][:, v_at:]
         at = slice(tail + step * rows, tail + (step + 1) * rows)
-        half = kv_width // 2
-        key_all[at, :half] = theirs[step][:, half:kv_width]
-        key_all[at, half:] = theirs[step][:, :half]
-        value_all[at, :half] = theirs[step][:, kv_width + half :]
-        value_all[at, half:] = theirs[step][:, kv_width : kv_width + half]
+        key_all[at, :half] = theirs[step][:, k_at + half : v_at]
+        key_all[at, half:] = theirs[step][:, k_at : k_at + half]
+        value_all[at, :half] = theirs[step][:, v_at + half :]
+        value_all[at, half:] = theirs[step][:, v_at : v_at + half]
     q_all[tail : tail + pad, :] = new[:, :q_width]
-    key_all[k_tail : k_tail + pad, :] = new[:, q_width : q_width + kv_width]
-    value_all[k_tail : k_tail + pad, :] = new[:, q_width + kv_width :]
+    key_all[k_tail : k_tail + pad, :] = new[:, k_at:v_at]
+    value_all[k_tail : k_tail + pad, :] = new[:, v_at:]
 
     ends, total = [], 0
     for request in range(count):
@@ -170,36 +179,45 @@
             attended[:, at : at + head] = (mixed / denom).astype(jnp.bfloat16)
 
     rows_own = w_own.shape[0]
-    result[...] = (
+    result = (
         jnp.dot(attended[:, :rows_own], w_own[...], preferred_element_type=jnp.float32)
         + jnp.dot(attended[:, rows_own:], w_other[...], preferred_element_type=jnp.float32)
     ).astype(jnp.bfloat16)
-    width = outs[0].shape[1]
-    for step in range(steps):
-        first = pl.multiple_of((c ^ z ^ step) * rows, rows)
-        for other in range(2):
-            column = pl.multiple_of((k ^ other) * width, width)
-            out = outs[2 * step + other]
-            out[:rows, :] = result[pl.ds(first, rows), pl.ds(column, width)]
-            out[rows:, :] = result[tail : tail + pad, pl.ds(column, width)]
-
-
-def finish_kernel(steps, place, *refs):
-    parts, (prefill, decode) = refs[: 2 * steps], refs[2 * steps :]
-    rows = prefill.shape[0] // 2
-    count = decode.shape[0]
-
-    def tree(terms):
+    for step, out in enumerate(outs):
+        out[:rows, :] = result[step * rows : (step + 1) * rows]
+        out[rows:, :] = result[tail : tail + pad]
+
+
+def relay_kernel(steps, *refs):
+    blocks, outs = refs[:steps], refs[steps:]
+    c, z, _ = place()
+    for slot, out in enumerate(outs):
+        for step, block in enumerate(blocks):
+
+            @pl.when((c ^ z ^ slot) == step)
+            def _(out=out, block=block):
+                out[...] = block[...]
+
+
+def sum_kernel(steps, *refs):
+    parts, (keep, send) = refs[:steps], refs[steps:]
+    width = keep.shape[1]
+    rows = send.shape[0]
+    _, _, k = place()
+    for out, core in ((keep, k), (send, 1 - k)):
+        column = pl.ds(pl.multiple_of(core * width, width), width)
+        terms = [part[:, column].astype(jnp.float32) for part in parts]
         while len(terms) > 1:
             terms = [a + b for a, b in zip(terms[::2], terms[1::2])]
-        return terms[0]
-
-    for other in range(2):
-        total = tree([parts[2 * step + other][...].astype(jnp.float32) for step in range(steps)])
-        total = total.astype(jnp.bfloat16)
-        prefill[pl.ds(pl.multiple_of((place[2] ^ other) * rows, rows), rows), :] = total[:rows]
-        if other == 0:
-            decode[...] = total[rows : rows + count]
+        out[...] = terms[0][: out.shape[0]].astype(out.dtype)
+
+
+def finish_kernel(keep, other, prefill, decode):
+    _, _, k = place()
+    rows = other.shape[0]
+    prefill[pl.ds(pl.multiple_of(k * rows, rows), rows), :] = keep[:rows]
+    prefill[pl.ds(pl.multiple_of((1 - k) * rows, rows), rows), :] = other[...]
+    decode[...] = keep[rows : rows + decode.shape[0]]
 
 
 def on_device_small(
@@ -213,9 +231,7 @@
     q_width = 2 * w_query.shape[1]
     kv_width = 2 * key_matrix.shape[1]
     features = q_width + 2 * kv_width
-    width = w_out.shape[1] // 2
-    c, t = lax.axis_index("ctx"), lax.axis_index("tp")
-    place = jnp.stack([c, t // 2, t % 2]).astype(jnp.int32)
+    out_width = w_out.shape[1]
 
     def to_core(value):
         return lax.ppermute(value, "tp", [(i, i ^ 1) for i in range(tp)])
@@ -223,98 +239,95 @@
     def to_ctx(value, step):
         return lax.ppermute(value, "ctx", [(i, i ^ step) for i in range(steps)])
 
-    sent = pl.pallas_call(
-        slice_kernel,
-        out_shape=[jax.ShapeDtypeStruct((rows, depth), bf16)] * (steps - 1),
-        in_specs=[smem(), hbm()],
-        out_specs=[hbm()] * (steps - 1),
-        scratch_shapes=[pltpu.SemaphoreType.DMA((steps - 1,))],
-        name="slice_tokens",
-    )(place, tokens)
-    got = [to_ctx(value, step) for step, value in enumerate(sent, 1)]
-    wq2, wk2, wv2, wo2 = (to_core(w) for w in (w_query, key_matrix, value_matrix, w_out))
-
-    def whole(shape):
-        return pl.BlockSpec(shape, lambda i, at: (0,) * len(shape))
+    def to_chip(value, step):
+        return lax.ppermute(value, "tp", [(i, i ^ (2 * step)) for i in range(tp)])
+
+    def call(kernel, name, inputs, shapes, scratch=(), spaces=None):
+        return pl.pallas_call(
+            kernel,
+            out_shape=[jax.ShapeDtypeStruct(shape, kind) for shape, kind in shapes],
+            in_specs=spaces or [vmem()] * len(inputs),
+            out_specs=[vmem()] * len(shapes),
+            scratch_shapes=list(scratch),
+            compiler_params=params(),
+            name=name,
+        )(*inputs)
+
+    *sent, new_columns = call(
+        functools.partial(slice_kernel, steps),
+        "slice_tokens",
+        (tokens, new_token_states),
+        [((rows, depth), bf16)] * steps + [((count, depth), bf16)],
+        [pltpu.SemaphoreType.DMA((steps,))],
+        [hbm(), vmem()],
+    )
+    blocks = [sent[0]] + [to_ctx(value, step) for step, value in enumerate(sent[1:], 1)]
+    weights = (w_query, key_matrix, value_matrix)
+    (own,) = call(
+        pack_kernel, "pack_weights", weights, [((depth, features // 2), bf16)]
+    )
+    other = to_core(own)
+    w_out_late, _ = lax.optimization_barrier((w_out, blocks[1]))
+    w_other = to_core(w_out_late)
 
     part_shape = (rows + pad, features)
     x_rows = -(-(steps * rows + pad) // 16) * 16
-    weights = (w_query, wq2, key_matrix, wk2, value_matrix, wv2)
-    parts = pl.pallas_call(
-        functools.partial(project_kernel, steps),
-        out_shape=[jax.ShapeDtypeStruct(part_shape, f32)]
-        + [jax.ShapeDtypeStruct(part_shape, bf16)] * (steps - 1),
-        grid_spec=pltpu.PrefetchScalarGridSpec(
-            num_scalar_prefetch=1,
-            grid=(1,),
-            in_specs=[pl.BlockSpec((rows, depth), lambda i, at: (at[2], at[0]))]
-            + [whole((rows, depth))] * (steps - 1)
-            + [pl.BlockSpec((count, depth), lambda i, at: (0, at[0]))]
-            + [whole(w.shape) for w in weights],
-            out_specs=[whole(part_shape)] * steps,
-            scratch_shapes=[pltpu.VMEM((x_rows, depth), bf16)],
-        ),
-        compiler_params=params(),
-        name="project",
-    )(place, tokens, *got, new_token_states, *weights)
+    edges = [0, q_width // 2, (q_width + kv_width) // 2, features // 2]
+    parts = call(
+        functools.partial(project_kernel, steps, list(zip(edges, edges[1:]))),
+        "project",
+        (*blocks, new_columns, own, other),
+        [(part_shape, f32)] + [(part_shape, bf16)] * (steps - 1),
+        [pltpu.VMEM((x_rows, depth), bf16)],
+    )
 
     parts = [parts[0]] + [to_ctx(part, step) for step, part in enumerate(parts[1:], 1)]
-    query, keyval, new = pl.pallas_call(
+    held, new = call(
         functools.partial(add_kernel, steps),
-        out_shape=[
-            jax.ShapeDtypeStruct((rows, q_width), bf16),
-            jax.ShapeDtypeStruct((rows, 2 * kv_width), bf16),
-            jax.ShapeDtypeStruct((pad, features), bf16),
-        ],
-        in_specs=[vmem()] * steps,
-        out_specs=[vmem()] * 3,
-        compiler_params=params(),
-        name="add_parts",
-    )(*parts)
-
-    mine = [keyval] + [to_ctx(keyval, step) for step in range(1, steps)]
-    queries = [query] + [to_ctx(query, step) for step in range(1, steps)]
+        "add_parts",
+        parts,
+        [((rows, features), bf16), ((pad, features), bf16)],
+    )
+
+    mine = [held] + [to_ctx(held, step) for step in range(1, steps)]
     theirs = [to_core(value) for value in mine]
 
     k_rows = -(-(2 * steps * rows + pad) // 128) * 128
-    out_shape = (rows + pad, width)
-    outs = pl.pallas_call(
+    outs = call(
         functools.partial(attend_kernel, steps, count, 1.0 / math.sqrt(HEAD_SIZE)),
-        out_shape=[jax.ShapeDtypeStruct(out_shape, bf16)] * (2 * steps),
-        in_specs=[smem()] * 3 + [vmem()] * (3 * steps + 3),
-        out_specs=[vmem()] * (2 * steps),
-        scratch_shapes=[
+        "attend",
+        (block_map, lengths, *mine, *theirs, new, w_out, w_other),
+        [((rows + pad, out_width), bf16)] * steps,
+        [
             pltpu.VMEM((x_rows, q_width), bf16),
             pltpu.VMEM((k_rows, kv_width), bf16),
             pltpu.VMEM((k_rows, kv_width), bf16),
             pltpu.VMEM((x_rows, q_width), bf16),
-            pltpu.VMEM((x_rows, 2 * width), bf16),
         ],
-        compiler_params=params(),
-        name="attend",
-    )(place, block_map, lengths, *queries, *mine, *theirs, new, w_out, wo2)
-
-    def to_owner(value, step, other):
-        pairs = []
-        for source in range(steps * tp):
-            at, rest = divmod(source, tp)
-            z, core = divmod(rest, 2)
-            pairs.append((source, (z ^ step) * tp + 2 * at + (core ^ other)))
-        return lax.ppermute(value, ("ctx", "tp"), pairs)
-
-    arrived = [to_owner(value, i // 2, i % 2) for i, value in enumerate(outs)]
+        [smem()] * 2 + [vmem()] * (2 * steps + 3),
+    )
+
+    arrived = [outs[0]] + [to_ctx(out, step) for step, out in enumerate(outs[1:], 1)]
+    slots = call(
+        functools.partial(relay_kernel, steps),
+        "relay",
+        arrived,
+        [((rows + pad, out_width), bf16)] * steps,
+    )
+    slots = [slots[0]] + [to_chip(slot, step) for step, slot in enumerate(slots[1:], 1)]
+    keep, send = call(
+        functools.partial(sum_kernel, steps),
+        "sum_heads",
+        slots,
+        [((rows + pad, out_width // 2), bf16), ((rows, out_width // 2), bf16)],
+    )
     return tuple(
-        pl.pallas_call(
-            functools.partial(finish_kernel, steps),
-            out_shape=[
-                jax.ShapeDtypeStruct((2 * rows, width), bf16),
-                jax.ShapeDtypeStruct((count, width), bf16),
-            ],
-            in_specs=[smem()] + [vmem()] * (2 * steps),
-            out_specs=[vmem()] * 2,
-            compiler_params=params(),
-            name="finish",
-        )(place, *arrived)
+        call(
+            finish_kernel,
+            "finish",
+            (keep, to_core(send)),
+            [((2 * rows, out_width // 2), bf16), ((count, out_width // 2), bf16)],
+        )
     )
 
 

time: 101 us -> 64.3 us (0.64)
  the two profiles are of different devices: /device:TPU:5 before, /device:TPU:0 now
where the time goes in v2:
time: 64.3 us; the launch traced here: 64.1 us
  waiting for transfers between devices  35.1 us (55%)
  starting transfers between devices  20.4 us (32%)
  Pallas kernels  4.66 us (7%)
  local copies, waits for them, and re-layouts  3.16 us (5%)
  between operations  0.77 us (1%)
    ppermute x12, waiting for transfers between devices, to_ctx(): return lax.ppermute(value, 'ctx', [(i, i ^ step) for i in range(steps)])  22.6 us
    ppermute x12, starting transfers between devices, to_ctx(): return lax.ppermute(value, 'ctx', [(i, i ^ step) for i in range(steps)])  15.2 us
    ppermute x3, waiting for transfers between devices, to_chip(): return lax.ppermute(value, 'tp', [(i, i ^ 2 * step) for i in range(tp)])  9.93 us
    pallas_call x8, Pallas kernels, call(): pl.pallas_call(kernel, out_shape=[jax.ShapeDtypeStruct(shape, kind) for s...  4.66 us
    ppermute x3, starting transfers between devices, to_chip(): return lax.ppermute(value, 'tp', [(i, i ^ 2 * step) for i in range(tp)])  4.45 us
    unnamed x16, local copies, waits for them, and re-layouts  3.16 us
    ppermute x7, waiting for transfers between devices, to_core(): return lax.ppermute(value, 'tp', [(i, i ^ 1) for i in range(tp)])  2.57 us
  transfers between devices with their start and end apart: 22, of which 13 were waited for; matrix products, arithmetic and copies ran while one was open for 0% of the time, Pallas kernels for 1%

profile of v2, /device:TPU:0, one launch (start us, length us, event | category | flops | bytes accessed | tf_op | source)
XLA Modules:
  0.0 64.1 jit_solution(15128454437905932182)
XLA Ops:
  0.7 1.1 %copy-done.1 = bf16[1024,256]{1,0:T(8,128)(2,1)S(1)} copy-done((bf16[1024,256]{1,0:T(8,128)(2,1)S(1)}, bf16[1024,256]{1,0:T(8,128)(2,1)}, u32[]{:S(2)}) %copy-start.1) | copy-done | bytes 524312
  1.8 0.9 %copy-done.3 = bf16[1024,128]{1,0:T(8,128)(2,1)S(1)} copy-done((bf16[1024,128]{1,0:T(8,128)(2,1)S(1)}, bf16[1024,128]{1,0:T(8,128)(2,1)}, u32[]{:S(2)}) %copy-start.3) | copy-done | bytes 262168
  2.7 0.9 %copy-done.4 = bf16[1024,128]{1,0:T(8,128)(2,1)S(1)} copy-done((bf16[1024,128]{1,0:T(8,128)(2,1)S(1)}, bf16[1024,128]{1,0:T(8,128)(2,1)}, u32[]{:S(2)}) %copy-start.4) | copy-done | bytes 262168
  3.8 0.5 collective-permute-start.3
  4.6 3.0 %collective-permute-start = (bf16[64,1024]{1,0:T(8,128)(2,1)S(1)}, bf16[64,1024]{1,0:T(8,128)(2,1)S(1)}, u32[]{:S(2)}, u32[]{:S(2)}) collective-permute-start(bf16[64,1024]{1,0:T(8,128)(2,1)S(1)} %get-tuple-element.25), channel_id=1, source_target_pairs={{0,8},{8,0},{16,24},{24,16},{1,9},{9,1},{17,25},{25,17},{2,10},{10... | collective-permute-start | bytes 393224 | tf_op jit(solution)/shard_map/ppermute | solution.py:240
  7.6 1.5 %collective-permute-start.1 = (bf16[64,1024]{1,0:T(8,128)(2,1)S(1)}, bf16[64,1024]{1,0:T(8,128)(2,1)S(1)}, u32[]{:S(2)}, u32[]{:S(2)}) collective-permute-start(bf16[64,1024]{1,0:T(8,128)(2,1)S(1)} %get-tuple-element.26), channel_id=1, source_target_pairs={{0,16},{8,24},{16,0},{24,8},{1,17},{9,25},{17,1},{25,9},{2,18},{10... | collective-permute-start | bytes 393224 | tf_op jit(solution)/shard_map/ppermute | solution.py:240
  9.1 2.3 %collective-permute-done.refs_1_ = bf16[64,1024]{1,0:T(8,128)(2,1)S(1)} collective-permute-done((bf16[64,1024]{1,0:T(8,128)(2,1)S(1)}, bf16[64,1024]{1,0:T(8,128)(2,1)S(1)}, u32[]{:S(2)}, u32[]{:S(2)}) %collective-permute-start) | collective-permute-done | bytes 131104 | tf_op jit(solution)/shard_map/ppermute | solution.py:240
  11.5 4.0 %collective-permute-done.1.refs_2_ = bf16[64,1024]{1,0:T(8,128)(2,1)S(1)} collective-permute-done((bf16[64,1024]{1,0:T(8,128)(2,1)S(1)}, bf16[64,1024]{1,0:T(8,128)(2,1)S(1)}, u32[]{:S(2)}, u32[]{:S(2)}) %collective-permute-start.1) | collective-permute-done | bytes 131104 | tf_op jit(solution)/shard_map/ppermute | solution.py:240
  15.5 0.7 %project.1 = (f32[72,1024]{1,0:T(8,128)S(1)}, bf16[72,1024]{1,0:T(8,128)(2,1)S(1)}, bf16[72,1024]{1,0:T(8,128)(2,1)S(1)}, bf16[72,1024]{1,0:T(8,128)(2,1)S(1)}) custom-call(bf16[64,1024]{1,0:T(8,128)(2,1)S(1)} %get-tuple-element.24.refs_0_, bf16[64,1024]{1,0:T(8,128)(2,1)S(1)} %collective-permute-done.refs_1_, ...), custom_call_target="tpu_custom_call" | custom-call | tf_op jit(solution)/shard_map/project/pallas_call | solution.py:246
  16.2 1.3 %collective-permute-start.4 = (bf16[72,1024]{1,0:T(8,128)(2,1)S(1)}, bf16[72,1024]{1,0:T(8,128)(2,1)S(1)}, u32[]{:S(2)}, u32[]{:S(2)}) collective-permute-start(bf16[72,1024]{1,0:T(8,128)(2,1)S(1)} %get-tuple-element.30), channel_id=1, source_target_pairs={{0,8},{8,0},{16,24},{24,16},{1,9},{9,1},{17,25},{25,17},{2,10},{10... | collective-permute-start | bytes 442376 | tf_op jit(solution)/shard_map/ppermute | solution.py:240
  17.5 0.8 %collective-permute-start.5 = (bf16[72,1024]{1,0:T(8,128)(2,1)S(1)}, bf16[72,1024]{1,0:T(8,128)(2,1)S(1)}, u32[]{:S(2)}, u32[]{:S(2)}) collective-permute-start(bf16[72,1024]{1,0:T(8,128)(2,1)S(1)} %get-tuple-element.31), channel_id=1, source_target_pairs={{0,16},{8,24},{16,0},{24,8},{1,17},{9,25},{17,1},{25,9},{2,18},{10... | collective-permute-start | bytes 442376 | tf_op jit(solution)/shard_map/ppermute | solution.py:240
  18.3 1.4 %collective-permute-start.6 = (bf16[72,1024]{1,0:T(8,128)(2,1)S(1)}, bf16[72,1024]{1,0:T(8,128)(2,1)S(1)}, u32[]{:S(2)}, u32[]{:S(2)}) collective-permute-start(bf16[72,1024]{1,0:T(8,128)(2,1)S(1)} %get-tuple-element.32), channel_id=1, source_target_pairs={{0,24},{8,16},{16,8},{24,0},{1,25},{9,17},{17,9},{25,1},{2,26},{10... | collective-permute-start | bytes 442376 | tf_op jit(solution)/shard_map/ppermute | solution.py:240
  19.8 3.0 %collective-permute-done.4.refs_1_ = bf16[72,1024]{1,0:T(8,128)(2,1)S(1)} collective-permute-done((bf16[72,1024]{1,0:T(8,128)(2,1)S(1)}, bf16[72,1024]{1,0:T(8,128)(2,1)S(1)}, u32[]{:S(2)}, u32[]{:S(2)}) %collective-permute-start.4) | collective-permute-done | bytes 147488 | tf_op jit(solution)/shard_map/ppermute | solution.py:240
  22.7 2.5 %collective-permute-done.5.refs_2_ = bf16[72,1024]{1,0:T(8,128)(2,1)S(1)} collective-permute-done((bf16[72,1024]{1,0:T(8,128)(2,1)S(1)}, bf16[72,1024]{1,0:T(8,128)(2,1)S(1)}, u32[]{:S(2)}, u32[]{:S(2)}) %collective-permute-start.5) | collective-permute-done | bytes 147488 | tf_op jit(solution)/shard_map/ppermute | solution.py:240
  25.3 1.3 %collective-permute-start.7 = (bf16[64,1024]{1,0:T(8,128)(2,1)S(1)}, bf16[64,1024]{1,0:T(8,128)(2,1)S(1)}, u32[]{:S(2)}, u32[]{:S(2)}) collective-permute-start(bf16[64,1024]{1,0:T(8,128)(2,1)S(1)} %get-tuple-element.33.refs_0_), channel_id=1, source_target_pairs={{0,8},{8,0},{16,24},{24,16},{1,9},{9,1},{17,25},{25,17},{2,10},{10... | collective-permute-start | bytes 393224 | tf_op jit(solution)/shard_map/ppermute | solution.py:240
  26.6 0.9 %collective-permute-start.8 = (bf16[64,1024]{1,0:T(8,128)(2,1)S(1)}, bf16[64,1024]{1,0:T(8,128)(2,1)S(1)}, u32[]{:S(2)}, u32[]{:S(2)}) collective-permute-start(bf16[64,1024]{1,0:T(8,128)(2,1)S(1)} %get-tuple-element.33.refs_0_), channel_id=1, source_target_pairs={{0,16},{8,24},{16,0},{24,8},{1,17},{9,25},{17,1},{25,9},{2,18},{10... | collective-permute-start | bytes 393224 | tf_op jit(solution)/shard_map/ppermute | solution.py:240
  27.5 1.4 %collective-permute-start.9 = (bf16[64,1024]{1,0:T(8,128)(2,1)S(1)}, bf16[64,1024]{1,0:T(8,128)(2,1)S(1)}, u32[]{:S(2)}, u32[]{:S(2)}) collective-permute-start(bf16[64,1024]{1,0:T(8,128)(2,1)S(1)} %get-tuple-element.33.refs_0_), channel_id=1, source_target_pairs={{0,24},{8,16},{16,8},{24,0},{1,25},{9,17},{17,9},{25,1},{2,26},{10... | collective-permute-start | bytes 393224 | tf_op jit(solution)/shard_map/ppermute | solution.py:240
  28.9 2.3 %collective-permute-done.7.refs_1_ = bf16[64,1024]{1,0:T(8,128)(2,1)S(1)} collective-permute-done((bf16[64,1024]{1,0:T(8,128)(2,1)S(1)}, bf16[64,1024]{1,0:T(8,128)(2,1)S(1)}, u32[]{:S(2)}, u32[]{:S(2)}) %collective-permute-start.7) | collective-permute-done | bytes 131104 | tf_op jit(solution)/shard_map/ppermute | solution.py:240
  31.7 1.7 %collective-permute-done.9.refs_3_ = bf16[64,1024]{1,0:T(8,128)(2,1)S(1)} collective-permute-done((bf16[64,1024]{1,0:T(8,128)(2,1)S(1)}, bf16[64,1024]{1,0:T(8,128)(2,1)S(1)}, u32[]{:S(2)}, u32[]{:S(2)}) %collective-permute-start.9) | collective-permute-done | bytes 131104 | tf_op jit(solution)/shard_map/ppermute | solution.py:240
  33.4 1.3 %collective-permute-done.13.refs_7_ = bf16[64,1024]{1,0:T(8,128)(2,1)S(1)} collective-permute-done((bf16[64,1024]{1,0:T(8,128)(2,1)S(1)}, bf16[64,1024]{1,0:T(8,128)(2,1)S(1)}, u32[]{:S(2)}, u32[]{:S(2)}) %collective-permute-start.13) | collective-permute-done | bytes 131104 | tf_op jit(solution)/shard_map/ppermute | solution.py:237
  34.7 2.8 %attend.1 = (bf16[72,1024]{1,0:T(8,128)(2,1)S(1)}, bf16[72,1024]{1,0:T(8,128)(2,1)S(1)}, bf16[72,1024]{1,0:T(8,128)(2,1)S(1)}, bf16[72,1024]{1,0:T(8,128)(2,1)S(1)}) custom-call(s32[8]{0:T(128)S(1)} %copy-done.6, s32[4]{0:T(128)S(1)} %copy-done.7, bf16[64,1024]{1,0:T(8,128)(2,1)S(1)} %get-tuple-element.33.refs_0_, ...), custom_call_target="tpu_custom_call" | custom-call | tf_op jit(solution)/shard_map/attend/pallas_call | solution.py:246
  37.5 1.2 %collective-permute-start.15 = (bf16[72,1024]{1,0:T(8,128)(2,1)S(1)}, bf16[72,1024]{1,0:T(8,128)(2,1)S(1)}, u32[]{:S(2)}, u32[]{:S(2)}) collective-permute-start(bf16[72,1024]{1,0:T(8,128)(2,1)S(1)} %get-tuple-element.37), channel_id=1, source_target_pairs={{0,8},{8,0},{16,24},{24,16},{1,9},{9,1},{17,25},{25,17},{2,10},{10... | collective-permute-start | bytes 442376 | tf_op jit(solution)/shard_map/ppermute | solution.py:240
  38.7 0.8 %collective-permute-start.16 = (bf16[72,1024]{1,0:T(8,128)(2,1)S(1)}, bf16[72,1024]{1,0:T(8,128)(2,1)S(1)}, u32[]{:S(2)}, u32[]{:S(2)}) collective-permute-start(bf16[72,1024]{1,0:T(8,128)(2,1)S(1)} %get-tuple-element.38), channel_id=1, source_target_pairs={{0,16},{8,24},{16,0},{24,8},{1,17},{9,25},{17,1},{25,9},{2,18},{10... | collective-permute-start | bytes 442376 | tf_op jit(solution)/shard_map/ppermute | solution.py:240
  39.5 1.6 %collective-permute-start.17 = (bf16[72,1024]{1,0:T(8,128)(2,1)S(1)}, bf16[72,1024]{1,0:T(8,128)(2,1)S(1)}, u32[]{:S(2)}, u32[]{:S(2)}) collective-permute-start(bf16[72,1024]{1,0:T(8,128)(2,1)S(1)} %get-tuple-element.39), channel_id=1, source_target_pairs={{0,24},{8,16},{16,8},{24,0},{1,25},{9,17},{17,9},{25,1},{2,26},{10... | collective-permute-start | bytes 442376 | tf_op jit(solution)/shard_map/ppermute | solution.py:240
  41.1 3.2 %collective-permute-done.15.refs_1_ = bf16[72,1024]{1,0:T(8,128)(2,1)S(1)} collective-permute-done((bf16[72,1024]{1,0:T(8,128)(2,1)S(1)}, bf16[72,1024]{1,0:T(8,128)(2,1)S(1)}, u32[]{:S(2)}, u32[]{:S(2)}) %collective-permute-start.15) | collective-permute-done | bytes 147488 | tf_op jit(solution)/shard_map/ppermute | solution.py:240
  44.3 3.2 %collective-permute-done.16.refs_2_ = bf16[72,1024]{1,0:T(8,128)(2,1)S(1)} collective-permute-done((bf16[72,1024]{1,0:T(8,128)(2,1)S(1)}, bf16[72,1024]{1,0:T(8,128)(2,1)S(1)}, u32[]{:S(2)}, u32[]{:S(2)}) %collective-permute-start.16) | collective-permute-done | bytes 147488 | tf_op jit(solution)/shard_map/ppermute | solution.py:240
  47.6 1.6 %collective-permute-start.18 = (bf16[72,1024]{1,0:T(8,128)(2,1)S(1)}, bf16[72,1024]{1,0:T(8,128)(2,1)S(1)}, u32[]{:S(2)}, u32[]{:S(2)}) collective-permute-start(bf16[72,1024]{1,0:T(8,128)(2,1)S(1)} %get-tuple-element.41), channel_id=1, source_target_pairs={{0,2},{1,3},{2,0},{3,1},{4,6},{5,7},{6,4},{7,5},{8,10},{9,11},{10,... | collective-permute-start | bytes 442376 | tf_op jit(solution)/shard_map/ppermute | solution.py:243
  49.2 2.6 %collective-permute-start.19 = (bf16[72,1024]{1,0:T(8,128)(2,1)S(1)}, bf16[72,1024]{1,0:T(8,128)(2,1)S(1)}, u32[]{:S(2)}, u32[]{:S(2)}) collective-permute-start(bf16[72,1024]{1,0:T(8,128)(2,1)S(1)} %get-tuple-element.42), channel_id=1, source_target_pairs={{0,4},{1,5},{2,6},{3,7},{4,0},{5,1},{6,2},{7,3},{8,12},{9,13},{10,... | collective-permute-start | bytes 442376 | tf_op jit(solution)/shard_map/ppermute | solution.py:243
  52.1 2.1 %collective-permute-done.18.refs_1_ = bf16[72,1024]{1,0:T(8,128)(2,1)S(1)} collective-permute-done((bf16[72,1024]{1,0:T(8,128)(2,1)S(1)}, bf16[72,1024]{1,0:T(8,128)(2,1)S(1)}, u32[]{:S(2)}, u32[]{:S(2)}) %collective-permute-start.18) | collective-permute-done | bytes 147488 | tf_op jit(solution)/shard_map/ppermute | solution.py:243
  54.2 7.8 %collective-permute-done.19.refs_2_ = bf16[72,1024]{1,0:T(8,128)(2,1)S(1)} collective-permute-done((bf16[72,1024]{1,0:T(8,128)(2,1)S(1)}, bf16[72,1024]{1,0:T(8,128)(2,1)S(1)}, u32[]{:S(2)}, u32[]{:S(2)}) %collective-permute-start.19) | collective-permute-done | bytes 147488 | tf_op jit(solution)/shard_map/ppermute | solution.py:243
  62.2 1.2 %collective-permute-done.21.other = bf16[64,512]{1,0:T(8,128)(2,1)S(1)} collective-permute-done((bf16[64,512]{1,0:T(8,128)(2,1)S(1)}, bf16[64,512]{1,0:T(8,128)(2,1)S(1)}, u32[]{:S(2)}, u32[]{:S(2)}) %collective-permute-start.21) | collective-permute-done | bytes 65568 | tf_op jit(solution)/shard_map/ppermute | solution.py:237
  63.4 0.7 %finish.1 = (bf16[128,512]{1,0:T(8,128)(2,1)}, bf16[4,512]{1,0:T(4,128)(2,1)}) custom-call(bf16[72,512]{1,0:T(8,128)(2,1)S(1)} %get-tuple-element.44.keep, bf16[64,512]{1,0:T(8,128)(2,1)S(1)} %collective-permute-done.21.other), custom_call_target="tpu_custom_call" | custom-call | tf_op jit(solution)/shard_map/finish/pallas_call | solution.py:246
  (36 shorter events, 1.5 us)
Async XLA Ops:
  0.6 3.7 %copy-start = (bf16[128,4096]{1,0:T(8,128)(2,1)S(1)}, bf16[128,4096]{1,0:T(8,128)(2,1)}, u32[]{:S(2)}) copy-start(bf16[128,4096]{1,0:T(8,128)(2,1)} %tokens.1) | copy-start | bytes 3145732
  0.6 1.1 %copy-start.1 = (bf16[1024,256]{1,0:T(8,128)(2,1)S(1)}, bf16[1024,256]{1,0:T(8,128)(2,1)}, u32[]{:S(2)}) copy-start(bf16[1024,256]{1,0:T(8,128)(2,1)} %refs_0_.1) | copy-start | bytes 1572868
  1.8 0.9 %copy-start.3 = (bf16[1024,128]{1,0:T(8,128)(2,1)S(1)}, bf16[1024,128]{1,0:T(8,128)(2,1)}, u32[]{:S(2)}) copy-start(bf16[1024,128]{1,0:T(8,128)(2,1)} %refs_1_.1) | copy-start | bytes 786436
  2.7 0.9 %copy-start.4 = (bf16[1024,128]{1,0:T(8,128)(2,1)S(1)}, bf16[1024,128]{1,0:T(8,128)(2,1)}, u32[]{:S(2)}) copy-start(bf16[1024,128]{1,0:T(8,128)(2,1)} %refs_2_.1) | copy-start | bytes 786436
  3.7 0.8 %copy-start.5 = (bf16[4,4096]{1,0:T(4,128)(2,1)S(1)}, bf16[4,4096]{1,0:T(4,128)(2,1)}, u32[]{:S(2)}) copy-start(bf16[4,4096]{1,0:T(4,128)(2,1)} %new.1) | copy-start | bytes 98308
  3.8 7.7 %copy-start.2 = (bf16[256,1024]{1,0:T(8,128)(2,1)S(1)}, bf16[256,1024]{1,0:T(8,128)(2,1)}, u32[]{:S(2)}) copy-start(bf16[256,1024]{1,0:T(8,128)(2,1)} %refs_9_.1) | copy-start | bytes 1572868
  3.8 11.7 %collective-permute-start.3 = (bf16[1024,512]{1,0:T(8,128)(2,1)S(1)}, bf16[1024,512]{1,0:T(8,128)(2,1)S(1)}, u32[]{:S(2)}, u32[]{:S(2)}) collective-permute-start(bf16[1024,512]{1,0:T(8,128)(2,1)S(1)} %pack_weights.1.refs_5_), channel_id=1, source_target_pairs={{0,1},{1,0},{2,3},{3,2},{4,5},{5,4},{6,7},{7,6},{8,9},{9,8},{10,11... | collective-permute-start | bytes 3145736 | tf_op jit(solution)/shard_map/ppermute | solution.py:237
  4.6 6.9 %collective-permute-start = (bf16[64,1024]{1,0:T(8,128)(2,1)S(1)}, bf16[64,1024]{1,0:T(8,128)(2,1)S(1)}, u32[]{:S(2)}, u32[]{:S(2)}) collective-permute-start(bf16[64,1024]{1,0:T(8,128)(2,1)S(1)} %get-tuple-element.25), channel_id=1, source_target_pairs={{0,8},{8,0},{16,24},{24,16},{1,9},{9,1},{17,25},{25,17},{2,10},{10... | collective-permute-start | bytes 393224 | tf_op jit(solution)/shard_map/ppermute | solution.py:240
  7.6 7.9 %collective-permute-start.1 = (bf16[64,1024]{1,0:T(8,128)(2,1)S(1)}, bf16[64,1024]{1,0:T(8,128)(2,1)S(1)}, u32[]{:S(2)}, u32[]{:S(2)}) collective-permute-start(bf16[64,1024]{1,0:T(8,128)(2,1)S(1)} %get-tuple-element.26), channel_id=1, source_target_pairs={{0,16},{8,24},{16,0},{24,8},{1,17},{9,25},{17,1},{25,9},{2,18},{10... | collective-permute-start | bytes 393224 | tf_op jit(solution)/shard_map/ppermute | solution.py:240
  9.1 6.4 %collective-permute-start.2 = (bf16[64,1024]{1,0:T(8,128)(2,1)S(1)}, bf16[64,1024]{1,0:T(8,128)(2,1)S(1)}, u32[]{:S(2)}, u32[]{:S(2)}) collective-permute-start(bf16[64,1024]{1,0:T(8,128)(2,1)S(1)} %get-tuple-element.27), channel_id=1, source_target_pairs={{0,24},{8,16},{16,8},{24,0},{1,25},{9,17},{17,9},{25,1},{2,26},{10... | collective-permute-start | bytes 393224 | tf_op jit(solution)/shard_map/ppermute | solution.py:240
  11.5 21.9 %collective-permute-start.14 = (bf16[256,1024]{1,0:T(8,128)(2,1)S(1)}, bf16[256,1024]{1,0:T(8,128)(2,1)S(1)}, u32[]{:S(2)}, u32[]{:S(2)}) collective-permute-start(bf16[256,1024]{1,0:T(8,128)(2,1)S(1)} %copy-done.2), channel_id=1, source_target_pairs={{0,1},{1,0},{2,3},{3,2},{4,5},{5,4},{6,7},{7,6},{8,9},{9,8},{10,11... | collective-permute-start | bytes 1572872 | tf_op jit(solution)/shard_map/ppermute | solution.py:237
  16.2 6.5 %collective-permute-start.4 = (bf16[72,1024]{1,0:T(8,128)(2,1)S(1)}, bf16[72,1024]{1,0:T(8,128)(2,1)S(1)}, u32[]{:S(2)}, u32[]{:S(2)}) collective-permute-start(bf16[72,1024]{1,0:T(8,128)(2,1)S(1)} %get-tuple-element.30), channel_id=1, source_target_pairs={{0,8},{8,0},{16,24},{24,16},{1,9},{9,1},{17,25},{25,17},{2,10},{10... | collective-permute-start | bytes 442376 | tf_op jit(solution)/shard_map/ppermute | solution.py:240
  17.5 7.7 %collective-permute-start.5 = (bf16[72,1024]{1,0:T(8,128)(2,1)S(1)}, bf16[72,1024]{1,0:T(8,128)(2,1)S(1)}, u32[]{:S(2)}, u32[]{:S(2)}) collective-permute-start(bf16[72,1024]{1,0:T(8,128)(2,1)S(1)} %get-tuple-element.31), channel_id=1, source_target_pairs={{0,16},{8,24},{16,0},{24,8},{1,17},{9,25},{17,1},{25,9},{2,18},{10... | collective-permute-start | bytes 442376 | tf_op jit(solution)/shard_map/ppermute | solution.py:240
  18.3 6.9 %collective-permute-start.6 = (bf16[72,1024]{1,0:T(8,128)(2,1)S(1)}, bf16[72,1024]{1,0:T(8,128)(2,1)S(1)}, u32[]{:S(2)}, u32[]{:S(2)}) collective-permute-start(bf16[72,1024]{1,0:T(8,128)(2,1)S(1)} %get-tuple-element.32), channel_id=1, source_target_pairs={{0,24},{8,16},{16,8},{24,0},{1,25},{9,17},{17,9},{25,1},{2,26},{10... | collective-permute-start | bytes 442376 | tf_op jit(solution)/shard_map/ppermute | solution.py:240
  25.3 9.4 %copy-start.6 = (s32[8]{0:T(128)S(1)}, s32[8]{0:T(128)}, u32[]{:S(2)}) copy-start(s32[8]{0:T(128)} %block_map.1) | copy-start | bytes 100
  25.3 9.4 %copy-start.7 = (s32[4]{0:T(128)S(1)}, s32[4]{0:T(128)}, u32[]{:S(2)}) copy-start(s32[4]{0:T(128)} %lengths.1) | copy-start | bytes 52
  25.3 5.9 %collective-permute-start.7 = (bf16[64,1024]{1,0:T(8,128)(2,1)S(1)}, bf16[64,1024]{1,0:T(8,128)(2,1)S(1)}, u32[]{:S(2)}, u32[]{:S(2)}) collective-permute-start(bf16[64,1024]{1,0:T(8,128)(2,1)S(1)} %get-tuple-element.33.refs_0_), channel_id=1, source_target_pairs={{0,8},{8,0},{16,24},{24,16},{1,9},{9,1},{17,25},{25,17},{2,10},{10... | collective-permute-start | bytes 393224 | tf_op jit(solution)/shard_map/ppermute | solution.py:240
  26.6 5.0 %collective-permute-start.8 = (bf16[64,1024]{1,0:T(8,128)(2,1)S(1)}, bf16[64,1024]{1,0:T(8,128)(2,1)S(1)}, u32[]{:S(2)}, u32[]{:S(2)}) collective-permute-start(bf16[64,1024]{1,0:T(8,128)(2,1)S(1)} %get-tuple-element.33.refs_0_), channel_id=1, source_target_pairs={{0,16},{8,24},{16,0},{24,8},{1,17},{9,25},{17,1},{25,9},{2,18},{10... | collective-permute-start | bytes 393224 | tf_op jit(solution)/shard_map/ppermute | solution.py:240
  27.5 5.9 %collective-permute-start.9 = (bf16[64,1024]{1,0:T(8,128)(2,1)S(1)}, bf16[64,1024]{1,0:T(8,128)(2,1)S(1)}, u32[]{:S(2)}, u32[]{:S(2)}) collective-permute-start(bf16[64,1024]{1,0:T(8,128)(2,1)S(1)} %get-tuple-element.33.refs_0_), channel_id=1, source_target_pairs={{0,24},{8,16},{16,8},{24,0},{1,25},{9,17},{17,9},{25,1},{2,26},{10... | collective-permute-start | bytes 393224 | tf_op jit(solution)/shard_map/ppermute | solution.py:240
  28.9 4.5 %collective-permute-start.10 = (bf16[64,1024]{1,0:T(8,128)(2,1)S(1)}, bf16[64,1024]{1,0:T(8,128)(2,1)S(1)}, u32[]{:S(2)}, u32[]{:S(2)}) collective-permute-start(bf16[64,1024]{1,0:T(8,128)(2,1)S(1)} %get-tuple-element.33.refs_0_), channel_id=1, source_target_pairs={{0,1},{1,0},{2,3},{3,2},{4,5},{5,4},{6,7},{7,6},{8,9},{9,8},{10,11... | collective-permute-start | bytes 393224 | tf_op jit(solution)/shard_map/ppermute | solution.py:237
  31.2 2.2 %collective-permute-start.11 = (bf16[64,1024]{1,0:T(8,128)(2,1)S(1)}, bf16[64,1024]{1,0:T(8,128)(2,1)S(1)}, u32[]{:S(2)}, u32[]{:S(2)}) collective-permute-start(bf16[64,1024]{1,0:T(8,128)(2,1)S(1)} %collective-permute-done.7.refs_1_), channel_id=1, source_target_pairs={{0,1},{1,0},{2,3},{3,2},{4,5},{5,4},{6,7},{7,6},{8,9},{9,8},{10,11... | collective-permute-start | bytes 393224 | tf_op jit(solution)/shard_map/ppermute | solution.py:237
  31.6 1.8 %collective-permute-start.12 = (bf16[64,1024]{1,0:T(8,128)(2,1)S(1)}, bf16[64,1024]{1,0:T(8,128)(2,1)S(1)}, u32[]{:S(2)}, u32[]{:S(2)}) collective-permute-start(bf16[64,1024]{1,0:T(8,128)(2,1)S(1)} %collective-permute-done.8.refs_2_), channel_id=1, source_target_pairs={{0,1},{1,0},{2,3},{3,2},{4,5},{5,4},{6,7},{7,6},{8,9},{9,8},{10,11... | collective-permute-start | bytes 393224 | tf_op jit(solution)/shard_map/ppermute | solution.py:237
  33.4 1.3 %collective-permute-start.13 = (bf16[64,1024]{1,0:T(8,128)(2,1)S(1)}, bf16[64,1024]{1,0:T(8,128)(2,1)S(1)}, u32[]{:S(2)}, u32[]{:S(2)}) collective-permute-start(bf16[64,1024]{1,0:T(8,128)(2,1)S(1)} %collective-permute-done.9.refs_3_), channel_id=1, source_target_pairs={{0,1},{1,0},{2,3},{3,2},{4,5},{5,4},{6,7},{7,6},{8,9},{9,8},{10,11... | collective-permute-start | bytes 393224 | tf_op jit(solution)/shard_map/ppermute | solution.py:237
  37.5 6.8 %collective-permute-start.15 = (bf16[72,1024]{1,0:T(8,128)(2,1)S(1)}, bf16[72,1024]{1,0:T(8,128)(2,1)S(1)}, u32[]{:S(2)}, u32[]{:S(2)}) collective-permute-start(bf16[72,1024]{1,0:T(8,128)(2,1)S(1)} %get-tuple-element.37), channel_id=1, source_target_pairs={{0,8},{8,0},{16,24},{24,16},{1,9},{9,1},{17,25},{25,17},{2,10},{10... | collective-permute-start | bytes 442376 | tf_op jit(solution)/shard_map/ppermute | solution.py:240
  38.7 8.8 %collective-permute-start.16 = (bf16[72,1024]{1,0:T(8,128)(2,1)S(1)}, bf16[72,1024]{1,0:T(8,128)(2,1)S(1)}, u32[]{:S(2)}, u32[]{:S(2)}) collective-permute-start(bf16[72,1024]{1,0:T(8,128)(2,1)S(1)} %get-tuple-element.38), channel_id=1, source_target_pairs={{0,16},{8,24},{16,0},{24,8},{1,17},{9,25},{17,1},{25,9},{2,18},{10... | collective-permute-start | bytes 442376 | tf_op jit(solution)/shard_map/ppermute | solution.py:240
  39.5 8.0 %collective-permute-start.17 = (bf16[72,1024]{1,0:T(8,128)(2,1)S(1)}, bf16[72,1024]{1,0:T(8,128)(2,1)S(1)}, u32[]{:S(2)}, u32[]{:S(2)}) collective-permute-start(bf16[72,1024]{1,0:T(8,128)(2,1)S(1)} %get-tuple-element.39), channel_id=1, source_target_pairs={{0,24},{8,16},{16,8},{24,0},{1,25},{9,17},{17,9},{25,1},{2,26},{10... | collective-permute-start | bytes 442376 | tf_op jit(solution)/shard_map/ppermute | solution.py:240
  47.6 6.6 %collective-permute-start.18 = (bf16[72,1024]{1,0:T(8,128)(2,1)S(1)}, bf16[72,1024]{1,0:T(8,128)(2,1)S(1)}, u32[]{:S(2)}, u32[]{:S(2)}) collective-permute-start(bf16[72,1024]{1,0:T(8,128)(2,1)S(1)} %get-tuple-element.41), channel_id=1, source_target_pairs={{0,2},{1,3},{2,0},{3,1},{4,6},{5,7},{6,4},{7,5},{8,10},{9,11},{10,... | collective-permute-start | bytes 442376 | tf_op jit(solution)/shard_map/ppermute | solution.py:243
  49.2 12.7 %collective-permute-start.19 = (bf16[72,1024]{1,0:T(8,128)(2,1)S(1)}, bf16[72,1024]{1,0:T(8,128)(2,1)S(1)}, u32[]{:S(2)}, u32[]{:S(2)}) collective-permute-start(bf16[72,1024]{1,0:T(8,128)(2,1)S(1)} %get-tuple-element.42), channel_id=1, source_target_pairs={{0,4},{1,5},{2,6},{3,7},{4,0},{5,1},{6,2},{7,3},{8,12},{9,13},{10,... | collective-permute-start | bytes 442376 | tf_op jit(solution)/shard_map/ppermute | solution.py:243
  51.8 10.2 %collective-permute-start.20 = (bf16[72,1024]{1,0:T(8,128)(2,1)S(1)}, bf16[72,1024]{1,0:T(8,128)(2,1)S(1)}, u32[]{:S(2)}, u32[]{:S(2)}) collective-permute-start(bf16[72,1024]{1,0:T(8,128)(2,1)S(1)} %get-tuple-element.43), channel_id=1, source_target_pairs={{0,6},{1,7},{2,4},{3,5},{4,2},{5,3},{6,0},{7,1},{8,14},{9,15},{10,... | collective-permute-start | bytes 442376 | tf_op jit(solution)/shard_map/ppermute | solution.py:243
  62.1 1.3 %collective-permute-start.21 = (bf16[64,512]{1,0:T(8,128)(2,1)S(1)}, bf16[64,512]{1,0:T(8,128)(2,1)S(1)}, u32[]{:S(2)}, u32[]{:S(2)}) collective-permute-start(bf16[64,512]{1,0:T(8,128)(2,1)S(1)} %get-tuple-element.45), channel_id=1, source_target_pairs={{0,1},{1,0},{2,3},{3,2},{4,5},{5,4},{6,7},{7,6},{8,9},{9,8},{10,11... | collective-permute-start | bytes 196616 | tf_op jit(solution)/shard_map/ppermute | solution.py:237

commit v3 on v2

--- a/solution.py
+++ b/solution.py
@@ -13,6 +13,7 @@
 LAST = 1 << 30
 ROW_TILE = 8
 VMEM_BYTES = 48 * 1024 * 1024
+LOAD_VMEM_BYTES = 62 * 1024 * 1024
 
 
 def vmem():
@@ -24,11 +25,7 @@
 
 
 def hbm():
-    return pl.BlockSpec(memory_space=pl.ANY)
-
-
-def params():
-    return pltpu.CompilerParams(vmem_limit_bytes=VMEM_BYTES)
+    return pl.BlockSpec(memory_space=pltpu.HBM)
 
 
 def place():
@@ -36,19 +33,21 @@
     return lax.axis_index("ctx"), t // 2, t % 2
 
 
-def slice_kernel(steps, tokens, new, *rest):
-    outs, new_out, sem = rest[:steps], rest[steps], rest[steps + 1]
+def load_kernel(steps, *refs):
+    (tokens, new, *weights), refs = refs[:5], refs[5:]
+    outs, (new_out, packed, sem) = refs[:steps], refs[steps:]
     c, _, k = place()
     rows, width = outs[0].shape
     first = pl.multiple_of(k * rows, rows)
-    copies = []
+    pairs = []
     for step, out in enumerate(outs):
         column = pl.multiple_of((c ^ step) * width, width)
-        copies.append(
-            pltpu.make_async_copy(
-                tokens.at[pl.ds(first, rows), pl.ds(column, width)], out, sem.at[step]
-            )
-        )
+        pairs.append((tokens.at[pl.ds(first, rows), pl.ds(column, width)], out))
+    column = 0
+    for weight in weights:
+        pairs.append((weight, packed.at[:, pl.ds(column, weight.shape[1])]))
+        column += weight.shape[1]
+    copies = [pltpu.make_async_copy(*pair, sem.at[i]) for i, pair in enumerate(pairs)]
     for copy in copies:
         copy.start()
     new_out[...] = new[:, pl.ds(pl.multiple_of(c * width, width), width)]
@@ -56,36 +55,41 @@
         copy.wait()
 
 
-def pack_kernel(*refs):
-    out = refs[-1]
-    out[...] = jnp.concatenate([ref[...] for ref in refs[:-1]], axis=1)
-
-
-def project_kernel(steps, parts_of, *refs):
-    blocks, (new, own, other), refs = refs[:steps], refs[steps : steps + 3], refs[steps + 3 :]
-    outs, inputs = refs[:steps], refs[steps]
-    rows = blocks[0].shape[0]
-    count = new.shape[0]
-    tail = steps * rows
-    for step, block in enumerate(blocks):
-        inputs[step * rows : (step + 1) * rows, :] = block[...]
-    inputs[tail:, :] = jnp.zeros_like(inputs[tail:, :])
-    inputs[tail : tail + count, :] = new[...]
-    x = inputs[...]
-    pad = outs[0].shape[0] - rows
-    column = 0
+def project(x, own, other, parts_of):
+    results = []
     for start, stop in parts_of:
         weight = jnp.concatenate([own[:, start:stop], other[:, start:stop]], axis=1)
-        part = jnp.dot(x, weight, preferred_element_type=jnp.float32)
-        to = slice(column, column + weight.shape[1])
-        for step, out in enumerate(outs):
-            out[:rows, to] = part[step * rows : (step + 1) * rows].astype(out.dtype)
-            out[rows:, to] = part[tail : tail + pad].astype(out.dtype)
-        column += weight.shape[1]
-
-
-def add_kernel(steps, *refs):
-    parts, (held, new) = refs[:steps], refs[steps:]
+        results.append(jnp.dot(x, weight, preferred_element_type=jnp.float32))
+    return jnp.concatenate(results, axis=1)
+
+
+def project_own_kernel(parts_of, block, new, own, other, out, new_out, inputs):
+    rows, count = block.shape[0], new.shape[0]
+    inputs[:rows, :] = block[...]
+    inputs[rows:, :] = jnp.zeros_like(inputs[rows:, :])
+    inputs[rows : rows + count, :] = new[...]
+    part = project(inputs[...], own, other, parts_of)
+    out[...] = part[: out.shape[0]]
+    new_out[...] = part[rows : out.shape[0]].astype(new_out.dtype)
+
+
+def project_kernel(number, parts_of, *refs):
+    blocks, (new, own, other), refs = refs[:number], refs[number : number + 3], refs[number + 3 :]
+    outs = refs[:number]
+    rows = blocks[0].shape[0]
+    x = jnp.concatenate([block[...] for block in blocks], axis=0)
+    part = project(x, own, other, parts_of)
+    for step, out in enumerate(outs):
+        out[:rows, :] = part[step * rows : (step + 1) * rows].astype(out.dtype)
+        out[rows:, :] = new[...]
+
+
+def add_kernel(first, second, out):
+    out[...] = first[...] + second[...].astype(jnp.float32)
+
+
+def add_last_kernel(*refs):
+    parts, (held, new) = refs[:-2], refs[-2:]
     rows = held.shape[0]
     total = parts[0][...]
     for part in parts[1:]:
@@ -102,11 +106,13 @@
     return found
 
 
-def attend_kernel(steps, count, scale, block_map, lengths, *refs):
+def attend_kernel(steps, step, count, scale, block_map, lengths, *refs):
     mine, refs = refs[:steps], refs[steps:]
     theirs, refs = refs[:steps], refs[steps:]
     new, w_own, w_other = refs[:3]
-    outs, (q_all, key_all, value_all, attended) = refs[3 : 3 + steps], refs[3 + steps :]
+    if step is not None:
+        new_out, refs = refs[3], refs[1:]
+    out, q_all, key_all, value_all, attended = refs[3:]
     rows = mine[0].shape[0]
     q_width, kv_width = q_all.shape[1], key_all.shape[1]
     head = HEAD_SIZE
@@ -121,71 +127,75 @@
     k_at, v_at = q_width, q_width + kv_width
     c, _, k = place()
 
-    q_all[tail:, :] = jnp.zeros_like(q_all[tail:, :])
     key_all[k_tail:, :] = jnp.zeros_like(key_all[k_tail:, :])
     value_all[k_tail:, :] = jnp.zeros_like(value_all[k_tail:, :])
-    for step in range(steps):
-        at = slice(step * rows, (step + 1) * rows)
-        q_all[at, :] = mine[step][:, :q_width]
-        key_all[at, :] = mine[step][:, k_at:v_at]
-        value_all[at, :] = mine[step][:, v_at:]
-        at = slice(tail + step * rows, tail + (step + 1) * rows)
-        key_all[at, :half] = theirs[step][:, k_at + half : v_at]
-        key_all[at, half:] = theirs[step][:, k_at : k_at + half]
-        value_all[at, :half] = theirs[step][:, v_at + half :]
-        value_all[at, half:] = theirs[step][:, v_at : v_at + half]
-    q_all[tail : tail + pad, :] = new[:, :q_width]
+    for number in range(steps):
+        at = slice(number * rows, (number + 1) * rows)
+        key_all[at, :] = mine[number][:, k_at:v_at]
+        value_all[at, :] = mine[number][:, v_at:]
+        at = slice(tail + number * rows, tail + (number + 1) * rows)
+        key_all[at, :half] = theirs[number][:, k_at + half : v_at]
+        key_all[at, half:] = theirs[number][:, k_at : k_at + half]
+        value_all[at, :half] = theirs[number][:, v_at + half :]
+        value_all[at, half:] = theirs[number][:, v_at : v_at + half]
     key_all[k_tail : k_tail + pad, :] = new[:, k_at:v_at]
     value_all[k_tail : k_tail + pad, :] = new[:, v_at:]
+    if step is None:
+        q_all[...] = jnp.zeros_like(q_all)
+        q_all[:pad, :] = new[:, :q_width]
+    else:
+        q_all[...] = mine[step][:, :q_width]
 
     ends, total = [], 0
     for request in range(count):
         total = total + lengths[request]
         ends.append(total)
 
-    def labels(shape, axis, halves):
+    def labels(shape, axis, held, last):
         index = lax.broadcasted_iota(jnp.int32, shape, axis)
         position = jnp.zeros(shape, jnp.int32)
-        for number in range(halves * steps):
-            held = 2 * (c ^ (number % steps)) + (k ^ (number // steps))
+        for number, block in enumerate(held):
             inside = (index >= number * rows) & (index < (number + 1) * rows)
-            position = jnp.where(inside, block_map[held] * rows + index - number * rows, position)
-        last = halves * tail
+            position = jnp.where(inside, block_map[block] * rows + index - number * rows, position)
         is_new = index >= last
         request = jnp.where(is_new, index - last, request_of(position, ends))
         return jnp.where(is_new, LAST, position), request
 
-    q_position, q_request = labels((q_rows, 1), 0, 1)
-    k_position, k_request = labels((1, k_rows), 1, 2)
+    if step is None:
+        q_position, q_request = labels((q_rows, 1), 0, [], 0)
+    else:
+        q_position, q_request = labels((q_rows, 1), 0, [2 * (c ^ step) + k], rows)
+    held = [2 * (c ^ number) + (k ^ other) for other in range(2) for number in range(steps)]
+    k_position, k_request = labels((1, k_rows), 1, held, k_tail)
     allowed = (q_request == k_request) & (k_position <= q_position)
+    allowed = jnp.concatenate([allowed] * per_group, axis=0)
 
     for group in range(groups):
         keys = key_all[:, group * head : (group + 1) * head]
         values = value_all[:, group * head : (group + 1) * head]
-        for member in range(per_group):
-            at = (group * per_group + member) * head
-            scores = lax.dot_general(
-                q_all[:, at : at + head],
-                keys,
-                (((1,), (1,)), ((), ())),
-                preferred_element_type=jnp.float32,
-            )
-            scores = jnp.where(allowed, scores * scale, FLOOR)
-            weights = jnp.exp(scores - jnp.max(scores, axis=1, keepdims=True))
-            denom = jnp.sum(weights, axis=1, keepdims=True)
-            mixed = jnp.dot(
-                weights.astype(jnp.bfloat16), values, preferred_element_type=jnp.float32
-            )
-            attended[:, at : at + head] = (mixed / denom).astype(jnp.bfloat16)
+        places = [(group * per_group + member) * head for member in range(per_group)]
+        query = jnp.concatenate([q_all[:, at : at + head] for at in places], axis=0)
+        scores = lax.dot_general(
+            query, keys, (((1,), (1,)), ((), ())), preferred_element_type=jnp.float32
+        )
+        scores = jnp.where(allowed, scores * scale, FLOOR)
+        weights = jnp.exp(scores - jnp.max(scores, axis=1, keepdims=True))
+        denom = jnp.sum(weights, axis=1, keepdims=True)
+        mixed = jnp.dot(weights.astype(jnp.bfloat16), values, preferred_element_type=jnp.float32)
+        mixed = (mixed / denom).astype(jnp.bfloat16)
+        for member, at in enumerate(places):
+            attended[:, at : at + head] = mixed[member * q_rows : (member + 1) * q_rows]
 
     rows_own = w_own.shape[0]
     result = (
         jnp.dot(attended[:, :rows_own], w_own[...], preferred_element_type=jnp.float32)
         + jnp.dot(attended[:, rows_own:], w_other[...], preferred_element_type=jnp.float32)
     ).astype(jnp.bfloat16)
-    for step, out in enumerate(outs):
-        out[:rows, :] = result[step * rows : (step + 1) * rows]
-        out[rows:, :] = result[tail : tail + pad]
+    if step is None:
+        out[...] = result[:pad]
+    else:
+        out[:rows, :] = result
+        out[rows:, :] = new_out[...]
 
 
 def relay_kernel(steps, *refs):
@@ -242,50 +252,63 @@
     def to_chip(value, step):
         return lax.ppermute(value, "tp", [(i, i ^ (2 * step)) for i in range(tp)])
 
-    def call(kernel, name, inputs, shapes, scratch=(), spaces=None):
+    def call(kernel, name, inputs, shapes, scratch=(), spaces=None, limit=VMEM_BYTES, flops=0):
+        moved = sum(2 * math.prod(shape) for shape, _ in shapes) + sum(2 * x.size for x in inputs)
         return pl.pallas_call(
             kernel,
             out_shape=[jax.ShapeDtypeStruct(shape, kind) for shape, kind in shapes],
             in_specs=spaces or [vmem()] * len(inputs),
             out_specs=[vmem()] * len(shapes),
             scratch_shapes=list(scratch),
-            compiler_params=params(),
+            compiler_params=pltpu.CompilerParams(vmem_limit_bytes=limit),
+            cost_estimate=pl.CostEstimate(flops=flops, bytes_accessed=moved, transcendentals=0),
             name=name,
         )(*inputs)
 
-    *sent, new_columns = call(
-        functools.partial(slice_kernel, steps),
-        "slice_tokens",
-        (tokens, new_token_states),
-        [((rows, depth), bf16)] * steps + [((count, depth), bf16)],
-        [pltpu.SemaphoreType.DMA((steps,))],
-        [hbm(), vmem()],
+    weights = (w_query, key_matrix, value_matrix)
+    *sent, new_columns, own = call(
+        functools.partial(load_kernel, steps),
+        "load",
+        (tokens, new_token_states, *weights),
+        [((rows, depth), bf16)] * steps + [((count, depth), bf16), ((depth, features // 2), bf16)],
+        [pltpu.SemaphoreType.DMA((steps + len(weights),))],
+        [hbm(), vmem()] + [hbm()] * len(weights),
+        LOAD_VMEM_BYTES,
     )
     blocks = [sent[0]] + [to_ctx(value, step) for step, value in enumerate(sent[1:], 1)]
-    weights = (w_query, key_matrix, value_matrix)
-    (own,) = call(
-        pack_kernel, "pack_weights", weights, [((depth, features // 2), bf16)]
-    )
     other = to_core(own)
     w_out_late, _ = lax.optimization_barrier((w_out, blocks[1]))
     w_other = to_core(w_out_late)
 
     part_shape = (rows + pad, features)
-    x_rows = -(-(steps * rows + pad) // 16) * 16
+    x_rows = -(-(rows + pad) // 16) * 16
     edges = [0, q_width // 2, (q_width + kv_width) // 2, features // 2]
-    parts = call(
-        functools.partial(project_kernel, steps, list(zip(edges, edges[1:]))),
-        "project",
-        (*blocks, new_columns, own, other),
-        [(part_shape, f32)] + [(part_shape, bf16)] * (steps - 1),
+    edges = list(zip(edges, edges[1:]))
+    flops = 2 * rows * depth * features
+    own_part, new_part = call(
+        functools.partial(project_own_kernel, edges),
+        "project_own",
+        (blocks[0], new_columns, own, other),
+        [(part_shape, f32), ((pad, features), bf16)],
         [pltpu.VMEM((x_rows, depth), bf16)],
-    )
+        flops=flops,
+    )
+    parts = [own_part]
+    for group in (blocks[1:2], blocks[2:]):
+        parts += call(
+            functools.partial(project_kernel, len(group), edges),
+            "project",
+            (*group, new_part, own, other),
+            [(part_shape, bf16)] * len(group),
+            flops=flops * len(group),
+        )
 
     parts = [parts[0]] + [to_ctx(part, step) for step, part in enumerate(parts[1:], 1)]
+    (total,) = call(add_kernel, "add_first", parts[:2], [(part_shape, f32)])
     held, new = call(
-        functools.partial(add_kernel, steps),
+        add_last_kernel,
         "add_parts",
-        parts,
+        (total, *parts[2:]),
         [((rows, features), bf16), ((pad, features), bf16)],
     )
 
@@ -293,19 +316,26 @@
     theirs = [to_core(value) for value in mine]
 
     k_rows = -(-(2 * steps * rows + pad) // 128) * 128
-    outs = call(
-        functools.partial(attend_kernel, steps, count, 1.0 / math.sqrt(HEAD_SIZE)),
-        "attend",
-        (block_map, lengths, *mine, *theirs, new, w_out, w_other),
-        [((rows + pad, out_width), bf16)] * steps,
-        [
-            pltpu.VMEM((x_rows, q_width), bf16),
-            pltpu.VMEM((k_rows, kv_width), bf16),
-            pltpu.VMEM((k_rows, kv_width), bf16),
-            pltpu.VMEM((x_rows, q_width), bf16),
-        ],
-        [smem()] * 2 + [vmem()] * (2 * steps + 3),
-    )
+    def attend(step, *extra):
+        q_rows = 2 * ROW_TILE if step is None else rows
+        (out,) = call(
+            functools.partial(attend_kernel, steps, step, count, 1.0 / math.sqrt(HEAD_SIZE)),
+            "attend",
+            (block_map, lengths, *mine, *theirs, new, w_out, w_other, *extra),
+            [((pad if step is None else rows + pad, out_width), bf16)],
+            [
+                pltpu.VMEM((q_rows, q_width), bf16),
+                pltpu.VMEM((k_rows, kv_width), bf16),
+                pltpu.VMEM((k_rows, kv_width), bf16),
+                pltpu.VMEM((q_rows, q_width), bf16),
+            ],
+            [smem()] * 2 + [vmem()] * (2 * steps + 3 + len(extra)),
+            flops=2 * q_rows * q_width * (2 * k_rows + out_width),
+        )
+        return out
+
+    new_out = attend(None)
+    outs = [attend(step, new_out) for step in range(steps)]
 
     arrived = [outs[0]] + [to_ctx(out, step) for step, out in enumerate(outs[1:], 1)]
     slots = call(

time: 64.3 us -> 69.7 us (1.084)
  Pallas kernels: 4.66 us -> 13.8 us
  waiting for transfers between devices: 35.1 us -> 31.7 us
    pallas_call x8 -> x14, Pallas kernels: 4.66 us -> 13.8 us  [call(): pl.pallas_call(kernel, out_shape=[jax.ShapeDtypeStruct(shape, kind) for s...]
    ppermute x12, waiting for transfers between devices: 22.6 us -> 18.7 us  [to_ctx(): return lax.ppermute(value, 'ctx', [(i, i ^ step) for i in range(steps)])]
    unnamed x16 -> x14, local copies, waits for them, and re-layouts: 3.16 us -> 2.88 us
  transfers between devices with their start and end apart: 22 -> 22, of which waited for: 13 -> 12; matrix products, arithmetic and copies ran while one was open for 0% -> 0% of each run, Pallas kernels for 1% -> 9%
where the time goes in v3:
time: 69.7 us; the launch traced here: 69.4 us
  waiting for transfers between devices  31.7 us (45%)
  starting transfers between devices  20.2 us (29%)
  Pallas kernels  13.8 us (20%)
  local copies, waits for them, and re-layouts  2.88 us (4%)
  between operations  0.81 us (1%)
    ppermute x12, waiting for transfers between devices, to_ctx(): return lax.ppermute(value, 'ctx', [(i, i ^ step) for i in range(steps)])  18.7 us
    ppermute x12, starting transfers between devices, to_ctx(): return lax.ppermute(value, 'ctx', [(i, i ^ step) for i in range(steps)])  15.1 us
    pallas_call x14, Pallas kernels, call(): pl.pallas_call(kernel, out_shape=[jax.ShapeDtypeStruct(shape, kind) for s...  13.8 us
    ppermute x3, waiting for transfers between devices, to_chip(): return lax.ppermute(value, 'tp', [(i, i ^ 2 * step) for i in range(tp)])  10.4 us
    ppermute x3, starting transfers between devices, to_chip(): return lax.ppermute(value, 'tp', [(i, i ^ 2 * step) for i in range(tp)])  4.45 us
    unnamed x14, local copies, waits for them, and re-layouts  2.88 us
    ppermute x7, waiting for transfers between devices, to_core(): return lax.ppermute(value, 'tp', [(i, i ^ 1) for i in range(tp)])  2.57 us
  transfers between devices with their start and end apart: 22, of which 12 were waited for; matrix products, arithmetic and copies ran while one was open for 0% of the time, Pallas kernels for 9%

profile of v3, /device:TPU:0, one launch (start us, length us, event | category | flops | bytes accessed | tf_op | source)
XLA Modules:
  0.0 69.4 jit_solution(14046908058364241104)
XLA Ops:
  0.6 3.5 %load.1 = (bf16[64,1024]{1,0:T(8,128)(2,1)}, bf16[64,1024]{1,0:T(8,128)(2,1)}, bf16[64,1024]{1,0:T(8,128)(2,1)}, bf16[64,1024]{1,0:T(8,128)(2,1)}, bf16[4,1024]{1,0:T(4,128)(2,1)}, /*index=5*/bf16[1024,512]{1,0:T(8,128)(2,1)}) custom-call(bf16[128,4096]{1,0:T(8,128)(2,1)} %refs_0_.1, bf16[4,4096]{1,0:T(4,128)(2,1)} %refs_1_.1, bf16[1024,256]{1,0:T(8,128)(2,1)} %refs_2_.1, ...), custom_call_target="tpu_custom_call" | custom-call | bytes 3710976 | tf_op jit(solution)/shard_map/load/pallas_call | solution.py:257
  4.7 2.6 %collective-permute-start.1 = (bf16[64,1024]{1,0:T(8,128)(2,1)}, bf16[64,1024]{1,0:T(8,128)(2,1)S(1)}, u32[]{:S(2)}, u32[]{:S(2)}) collective-permute-start(bf16[64,1024]{1,0:T(8,128)(2,1)} %get-tuple-element.25), channel_id=1, source_target_pairs={{0,8},{8,0},{16,24},{24,16},{1,9},{9,1},{17,25},{25,17},{2,10},{10... | collective-permute-start | bytes 393224 | tf_op jit(solution)/shard_map/ppermute | solution.py:250
  7.2 1.5 %collective-permute-start.3 = (bf16[64,1024]{1,0:T(8,128)(2,1)}, bf16[64,1024]{1,0:T(8,128)(2,1)S(1)}, u32[]{:S(2)}, u32[]{:S(2)}) collective-permute-start(bf16[64,1024]{1,0:T(8,128)(2,1)} %get-tuple-element.27), channel_id=1, source_target_pairs={{0,16},{8,24},{16,0},{24,8},{1,17},{9,25},{17,1},{25,9},{2,18},{10... | collective-permute-start | bytes 393224 | tf_op jit(solution)/shard_map/ppermute | solution.py:250
  8.8 2.8 %collective-permute-done.1.refs_0_ = bf16[64,1024]{1,0:T(8,128)(2,1)S(1)} collective-permute-done((bf16[64,1024]{1,0:T(8,128)(2,1)}, bf16[64,1024]{1,0:T(8,128)(2,1)S(1)}, u32[]{:S(2)}, u32[]{:S(2)}) %collective-permute-start.1) | collective-permute-done | bytes 131104 | tf_op jit(solution)/shard_map/ppermute | solution.py:250
  11.6 1.2 %copy-done.1 = bf16[1024,512]{1,0:T(8,128)(2,1)S(1)} copy-done((bf16[1024,512]{1,0:T(8,128)(2,1)S(1)}, bf16[1024,512]{1,0:T(8,128)(2,1)}, u32[]{:S(2)}) %copy-start.1) | copy-done | bytes 1048600
  12.9 0.9 %copy-done.3 = bf16[64,1024]{1,0:T(8,128)(2,1)S(1)} copy-done((bf16[64,1024]{1,0:T(8,128)(2,1)S(1)}, bf16[64,1024]{1,0:T(8,128)(2,1)}, u32[]{:S(2)}) %copy-start.3) | copy-done | bytes 131096
  14.2 0.7 %copy-done.2 = bf16[1024,512]{1,0:T(8,128)(2,1)S(1)} copy-done((bf16[1024,512]{1,0:T(8,128)(2,1)S(1)}, bf16[1024,512]{1,0:T(8,128)(2,1)}, u32[]{:S(2)}) %copy-start.2) | copy-done | bytes 1048600
  15.5 2.2 %collective-permute-start.2 = (bf16[72,1024]{1,0:T(8,128)(2,1)S(1)}, bf16[72,1024]{1,0:T(8,128)(2,1)S(1)}, u32[]{:S(2)}, u32[]{:S(2)}) collective-permute-start(bf16[72,1024]{1,0:T(8,128)(2,1)S(1)} %project.2), channel_id=1, source_target_pairs={{0,8},{8,0},{16,24},{24,16},{1,9},{9,1},{17,25},{25,17},{2,10},{10... | collective-permute-start | bytes 442376 | tf_op jit(solution)/shard_map/ppermute | solution.py:250
  18.1 1.6 %collective-permute-start.5 = (bf16[72,1024]{1,0:T(8,128)(2,1)S(1)}, bf16[72,1024]{1,0:T(8,128)(2,1)S(1)}, u32[]{:S(2)}, u32[]{:S(2)}) collective-permute-start(bf16[72,1024]{1,0:T(8,128)(2,1)S(1)} %get-tuple-element.29), channel_id=1, source_target_pairs={{0,16},{8,24},{16,0},{24,8},{1,17},{9,25},{17,1},{25,9},{2,18},{10... | collective-permute-start | bytes 442376 | tf_op jit(solution)/shard_map/ppermute | solution.py:250
  19.7 2.5 %collective-permute-done.2.second = bf16[72,1024]{1,0:T(8,128)(2,1)S(1)} collective-permute-done((bf16[72,1024]{1,0:T(8,128)(2,1)S(1)}, bf16[72,1024]{1,0:T(8,128)(2,1)S(1)}, u32[]{:S(2)}, u32[]{:S(2)}) %collective-permute-start.2) | collective-permute-done | bytes 147488 | tf_op jit(solution)/shard_map/ppermute | solution.py:250
  22.2 5.1 %collective-permute-done.5.refs_1_ = bf16[72,1024]{1,0:T(8,128)(2,1)S(1)} collective-permute-done((bf16[72,1024]{1,0:T(8,128)(2,1)S(1)}, bf16[72,1024]{1,0:T(8,128)(2,1)S(1)}, u32[]{:S(2)}, u32[]{:S(2)}) %collective-permute-start.5) | collective-permute-done | bytes 147488 | tf_op jit(solution)/shard_map/ppermute | solution.py:250
  27.4 0.8 %collective-permute-start.7 = (bf16[64,1024]{1,0:T(8,128)(2,1)S(1)}, bf16[64,1024]{1,0:T(8,128)(2,1)S(1)}, u32[]{:S(2)}, u32[]{:S(2)}) collective-permute-start(bf16[64,1024]{1,0:T(8,128)(2,1)S(1)} %get-tuple-element.31.refs_0_), channel_id=1, source_target_pairs={{0,8},{8,0},{16,24},{24,16},{1,9},{9,1},{17,25},{25,17},{2,10},{10... | collective-permute-start | bytes 393224 | tf_op jit(solution)/shard_map/ppermute | solution.py:250
  28.2 1.2 %collective-permute-start.8 = (bf16[64,1024]{1,0:T(8,128)(2,1)S(1)}, bf16[64,1024]{1,0:T(8,128)(2,1)S(1)}, u32[]{:S(2)}, u32[]{:S(2)}) collective-permute-start(bf16[64,1024]{1,0:T(8,128)(2,1)S(1)} %get-tuple-element.31.refs_0_), channel_id=1, source_target_pairs={{0,16},{8,24},{16,0},{24,8},{1,17},{9,25},{17,1},{25,9},{2,18},{10... | collective-permute-start | bytes 393224 | tf_op jit(solution)/shard_map/ppermute | solution.py:250
  29.4 1.5 %collective-permute-start.9 = (bf16[64,1024]{1,0:T(8,128)(2,1)S(1)}, bf16[64,1024]{1,0:T(8,128)(2,1)S(1)}, u32[]{:S(2)}, u32[]{:S(2)}) collective-permute-start(bf16[64,1024]{1,0:T(8,128)(2,1)S(1)} %get-tuple-element.31.refs_0_), channel_id=1, source_target_pairs={{0,24},{8,16},{16,8},{24,0},{1,25},{9,17},{17,9},{25,1},{2,26},{10... | collective-permute-start | bytes 393224 | tf_op jit(solution)/shard_map/ppermute | solution.py:250
  31.0 2.6 %collective-permute-done.7.refs_1_ = bf16[64,1024]{1,0:T(8,128)(2,1)S(1)} collective-permute-done((bf16[64,1024]{1,0:T(8,128)(2,1)S(1)}, bf16[64,1024]{1,0:T(8,128)(2,1)S(1)}, u32[]{:S(2)}, u32[]{:S(2)}) %collective-permute-start.7) | collective-permute-done | bytes 131104 | tf_op jit(solution)/shard_map/ppermute | solution.py:250
  33.6 1.1 %collective-permute-done.8.refs_2_ = bf16[64,1024]{1,0:T(8,128)(2,1)S(1)} collective-permute-done((bf16[64,1024]{1,0:T(8,128)(2,1)S(1)}, bf16[64,1024]{1,0:T(8,128)(2,1)S(1)}, u32[]{:S(2)}, u32[]{:S(2)}) %collective-permute-start.8) | collective-permute-done | bytes 131104 | tf_op jit(solution)/shard_map/ppermute | solution.py:250
  34.6 1.4 %collective-permute-done.9.refs_3_ = bf16[64,1024]{1,0:T(8,128)(2,1)S(1)} collective-permute-done((bf16[64,1024]{1,0:T(8,128)(2,1)S(1)}, bf16[64,1024]{1,0:T(8,128)(2,1)S(1)}, u32[]{:S(2)}, u32[]{:S(2)}) %collective-permute-start.9) | collective-permute-done | bytes 131104 | tf_op jit(solution)/shard_map/ppermute | solution.py:250
  36.1 1.3 %collective-permute-done.13.refs_7_ = bf16[64,1024]{1,0:T(8,128)(2,1)S(1)} collective-permute-done((bf16[64,1024]{1,0:T(8,128)(2,1)S(1)}, bf16[64,1024]{1,0:T(8,128)(2,1)S(1)}, u32[]{:S(2)}, u32[]{:S(2)}) %collective-permute-start.13) | collective-permute-done | bytes 131104 | tf_op jit(solution)/shard_map/ppermute | solution.py:247
  37.4 1.5 %attend.5.refs_11_ = bf16[8,1024]{1,0:T(8,128)(2,1)S(1)} custom-call(s32[8]{0:T(128)S(1)} %copy-done.4, s32[4]{0:T(128)S(1)} %copy-done.5, bf16[64,1024]{1,0:T(8,128)(2,1)S(1)} %get-tuple-element.31.refs_0_, bf16[64,1024]{1,0:T(8,128)(2,1)S(1)} %collective-permute-done.7.refs_1_, bf16[64,1024]{1,0:T(8,128)(2,1)S(1)} %collective-permute-done.8.refs_2_, ...), custom_call_target="tpu_custom_call" | custom-call | flops 37748736 | bytes 2129944 | tf_op jit(solution)/shard_map/attend/pallas_call | solution.py:257
  38.9 1.6 %attend.9 = bf16[72,1024]{1,0:T(8,128)(2,1)S(1)} custom-call(s32[8]{0:T(128)S(1)} %copy-done.4, s32[4]{0:T(128)S(1)} %copy-done.5, bf16[64,1024]{1,0:T(8,128)(2,1)S(1)} %get-tuple-element.31.refs_0_, bf16[64,1024]{1,0:T(8,128)(2,1)S(1)} %collective-permute-done.7.refs_1_, bf16[64,1024]{1,0:T(8,128)(2,1)S(1)} %collective-permute-done.8.refs_2_, ...), custom_call_target="tpu_custom_call" | custom-call | flops 150994944 | bytes 2277400 | tf_op jit(solution)/shard_map/attend/pallas_call | solution.py:257
  40.5 2.1 %collective-permute-start.17 = (bf16[72,1024]{1,0:T(8,128)(2,1)S(1)}, bf16[72,1024]{1,0:T(8,128)(2,1)S(1)}, u32[]{:S(2)}, u32[]{:S(2)}) collective-permute-start(bf16[72,1024]{1,0:T(8,128)(2,1)S(1)} %attend.9), channel_id=1, source_target_pairs={{0,24},{8,16},{16,8},{24,0},{1,25},{9,17},{17,9},{25,1},{2,26},{10... | collective-permute-start | bytes 442376 | tf_op jit(solution)/shard_map/ppermute | solution.py:250
  42.6 1.6 %attend.8 = bf16[72,1024]{1,0:T(8,128)(2,1)S(1)} custom-call(s32[8]{0:T(128)S(1)} %copy-done.4, s32[4]{0:T(128)S(1)} %copy-done.5, bf16[64,1024]{1,0:T(8,128)(2,1)S(1)} %get-tuple-element.31.refs_0_, bf16[64,1024]{1,0:T(8,128)(2,1)S(1)} %collective-permute-done.7.refs_1_, bf16[64,1024]{1,0:T(8,128)(2,1)S(1)} %collective-permute-done.8.refs_2_, ...), custom_call_target="tpu_custom_call" | custom-call | flops 150994944 | bytes 2277400 | tf_op jit(solution)/shard_map/attend/pallas_call | solution.py:257
  44.2 1.0 %collective-permute-start.16 = (bf16[72,1024]{1,0:T(8,128)(2,1)S(1)}, bf16[72,1024]{1,0:T(8,128)(2,1)S(1)}, u32[]{:S(2)}, u32[]{:S(2)}) collective-permute-start(bf16[72,1024]{1,0:T(8,128)(2,1)S(1)} %attend.8), channel_id=1, source_target_pairs={{0,16},{8,24},{16,0},{24,8},{1,17},{9,25},{17,1},{25,9},{2,18},{10... | collective-permute-start | bytes 442376 | tf_op jit(solution)/shard_map/ppermute | solution.py:250
  45.2 1.6 %attend.7 = bf16[72,1024]{1,0:T(8,128)(2,1)S(1)} custom-call(s32[8]{0:T(128)S(1)} %copy-done.4, s32[4]{0:T(128)S(1)} %copy-done.5, bf16[64,1024]{1,0:T(8,128)(2,1)S(1)} %get-tuple-element.31.refs_0_, bf16[64,1024]{1,0:T(8,128)(2,1)S(1)} %collective-permute-done.7.refs_1_, bf16[64,1024]{1,0:T(8,128)(2,1)S(1)} %collective-permute-done.8.refs_2_, ...), custom_call_target="tpu_custom_call" | custom-call | flops 150994944 | bytes 2277400 | tf_op jit(solution)/shard_map/attend/pallas_call | solution.py:257
  47.5 1.6 %attend.6.refs_0_ = bf16[72,1024]{1,0:T(8,128)(2,1)S(1)} custom-call(s32[8]{0:T(128)S(1)} %copy-done.4, s32[4]{0:T(128)S(1)} %copy-done.5, bf16[64,1024]{1,0:T(8,128)(2,1)S(1)} %get-tuple-element.31.refs_0_, bf16[64,1024]{1,0:T(8,128)(2,1)S(1)} %collective-permute-done.7.refs_1_, bf16[64,1024]{1,0:T(8,128)(2,1)S(1)} %collective-permute-done.8.refs_2_, ...), custom_call_target="tpu_custom_call" | custom-call | flops 150994944 | bytes 2277400 | tf_op jit(solution)/shard_map/attend/pallas_call | solution.py:257
  49.1 1.5 %collective-permute-done.16.refs_2_ = bf16[72,1024]{1,0:T(8,128)(2,1)S(1)} collective-permute-done((bf16[72,1024]{1,0:T(8,128)(2,1)S(1)}, bf16[72,1024]{1,0:T(8,128)(2,1)S(1)}, u32[]{:S(2)}, u32[]{:S(2)}) %collective-permute-start.16) | collective-permute-done | bytes 147488 | tf_op jit(solution)/shard_map/ppermute | solution.py:250
  50.6 1.8 %collective-permute-done.15.refs_1_ = bf16[72,1024]{1,0:T(8,128)(2,1)S(1)} collective-permute-done((bf16[72,1024]{1,0:T(8,128)(2,1)S(1)}, bf16[72,1024]{1,0:T(8,128)(2,1)S(1)}, u32[]{:S(2)}, u32[]{:S(2)}) %collective-permute-start.15) | collective-permute-done | bytes 147488 | tf_op jit(solution)/shard_map/ppermute | solution.py:250
  52.5 1.6 %collective-permute-start.18 = (bf16[72,1024]{1,0:T(8,128)(2,1)S(1)}, bf16[72,1024]{1,0:T(8,128)(2,1)S(1)}, u32[]{:S(2)}, u32[]{:S(2)}) collective-permute-start(bf16[72,1024]{1,0:T(8,128)(2,1)S(1)} %get-tuple-element.35), channel_id=1, source_target_pairs={{0,2},{1,3},{2,0},{3,1},{4,6},{5,7},{6,4},{7,5},{8,10},{9,11},{10,... | collective-permute-start | bytes 442376 | tf_op jit(solution)/shard_map/ppermute | solution.py:253
  54.1 2.6 %collective-permute-start.19 = (bf16[72,1024]{1,0:T(8,128)(2,1)S(1)}, bf16[72,1024]{1,0:T(8,128)(2,1)S(1)}, u32[]{:S(2)}, u32[]{:S(2)}) collective-permute-start(bf16[72,1024]{1,0:T(8,128)(2,1)S(1)} %get-tuple-element.36), channel_id=1, source_target_pairs={{0,4},{1,5},{2,6},{3,7},{4,0},{5,1},{6,2},{7,3},{8,12},{9,13},{10,... | collective-permute-start | bytes 442376 | tf_op jit(solution)/shard_map/ppermute | solution.py:253
  56.9 2.5 %collective-permute-done.18.refs_1_ = bf16[72,1024]{1,0:T(8,128)(2,1)S(1)} collective-permute-done((bf16[72,1024]{1,0:T(8,128)(2,1)S(1)}, bf16[72,1024]{1,0:T(8,128)(2,1)S(1)}, u32[]{:S(2)}, u32[]{:S(2)}) %collective-permute-start.18) | collective-permute-done | bytes 147488 | tf_op jit(solution)/shard_map/ppermute | solution.py:253
  59.5 7.9 %collective-permute-done.19.refs_2_ = bf16[72,1024]{1,0:T(8,128)(2,1)S(1)} collective-permute-done((bf16[72,1024]{1,0:T(8,128)(2,1)S(1)}, bf16[72,1024]{1,0:T(8,128)(2,1)S(1)}, u32[]{:S(2)}, u32[]{:S(2)}) %collective-permute-start.19) | collective-permute-done | bytes 147488 | tf_op jit(solution)/shard_map/ppermute | solution.py:253
  67.5 1.2 %collective-permute-done.21.other = bf16[64,512]{1,0:T(8,128)(2,1)S(1)} collective-permute-done((bf16[64,512]{1,0:T(8,128)(2,1)S(1)}, bf16[64,512]{1,0:T(8,128)(2,1)S(1)}, u32[]{:S(2)}, u32[]{:S(2)}) %collective-permute-start.21) | collective-permute-done | bytes 65568 | tf_op jit(solution)/shard_map/ppermute | solution.py:247
  (40 shorter events, 3.9 us)
Async XLA Ops:
  0.6 11.0 %copy-start = (bf16[256,1024]{1,0:T(8,128)(2,1)S(1)}, bf16[256,1024]{1,0:T(8,128)(2,1)}, u32[]{:S(2)}) copy-start(bf16[256,1024]{1,0:T(8,128)(2,1)} %refs_9_.9) | copy-start | bytes 1572868
  4.1 7.5 %copy-start.6 = (bf16[4,1024]{1,0:T(4,128)(2,1)S(1)}, bf16[4,1024]{1,0:T(4,128)(2,1)}, u32[]{:S(2)}) copy-start(bf16[4,1024]{1,0:T(4,128)(2,1)} %get-tuple-element.22.new) | copy-start | bytes 24580
  4.1 7.5 %collective-permute-start = (bf16[1024,512]{1,0:T(8,128)(2,1)}, bf16[1024,512]{1,0:T(8,128)(2,1)S(1)}, u32[]{:S(2)}, u32[]{:S(2)}) collective-permute-start(bf16[1024,512]{1,0:T(8,128)(2,1)} %get-tuple-element.23.own.refs_2_.refs_3_), channel_id=1, source_target_pairs={{0,1},{1,0},{2,3},{3,2},{4,5},{5,4},{6,7},{7,6},{8,9},{9,8},{10,11... | collective-permute-start | bytes 3145736 | tf_op jit(solution)/shard_map/ppermute | solution.py:247
  4.7 6.9 %collective-permute-start.1 = (bf16[64,1024]{1,0:T(8,128)(2,1)}, bf16[64,1024]{1,0:T(8,128)(2,1)S(1)}, u32[]{:S(2)}, u32[]{:S(2)}) collective-permute-start(bf16[64,1024]{1,0:T(8,128)(2,1)} %get-tuple-element.25), channel_id=1, source_target_pairs={{0,8},{8,0},{16,24},{24,16},{1,9},{9,1},{17,25},{25,17},{2,10},{10... | collective-permute-start | bytes 393224 | tf_op jit(solution)/shard_map/ppermute | solution.py:250
  7.2 10.4 %collective-permute-start.3 = (bf16[64,1024]{1,0:T(8,128)(2,1)}, bf16[64,1024]{1,0:T(8,128)(2,1)S(1)}, u32[]{:S(2)}, u32[]{:S(2)}) collective-permute-start(bf16[64,1024]{1,0:T(8,128)(2,1)} %get-tuple-element.27), channel_id=1, source_target_pairs={{0,16},{8,24},{16,0},{24,8},{1,17},{9,25},{17,1},{25,9},{2,18},{10... | collective-permute-start | bytes 393224 | tf_op jit(solution)/shard_map/ppermute | solution.py:250
  8.8 8.9 %collective-permute-start.4 = (bf16[64,1024]{1,0:T(8,128)(2,1)}, bf16[64,1024]{1,0:T(8,128)(2,1)S(1)}, u32[]{:S(2)}, u32[]{:S(2)}) collective-permute-start(bf16[64,1024]{1,0:T(8,128)(2,1)} %get-tuple-element.28), channel_id=1, source_target_pairs={{0,24},{8,16},{16,8},{24,0},{1,25},{9,17},{17,9},{25,1},{2,26},{10... | collective-permute-start | bytes 393224 | tf_op jit(solution)/shard_map/ppermute | solution.py:250
  11.6 24.4 %collective-permute-start.14 = (bf16[256,1024]{1,0:T(8,128)(2,1)S(1)}, bf16[256,1024]{1,0:T(8,128)(2,1)S(1)}, u32[]{:S(2)}, u32[]{:S(2)}) collective-permute-start(bf16[256,1024]{1,0:T(8,128)(2,1)S(1)} %copy-done), channel_id=1, source_target_pairs={{0,1},{1,0},{2,3},{3,2},{4,5},{5,4},{6,7},{7,6},{8,9},{9,8},{10,11... | collective-permute-start | bytes 1572872 | tf_op jit(solution)/shard_map/ppermute | solution.py:247
  11.6 1.2 %copy-start.1 = (bf16[1024,512]{1,0:T(8,128)(2,1)S(1)}, bf16[1024,512]{1,0:T(8,128)(2,1)}, u32[]{:S(2)}) copy-start(bf16[1024,512]{1,0:T(8,128)(2,1)} %get-tuple-element.23.own.refs_2_.refs_3_) | copy-start | bytes 3145732
  12.9 0.9 %copy-start.3 = (bf16[64,1024]{1,0:T(8,128)(2,1)S(1)}, bf16[64,1024]{1,0:T(8,128)(2,1)}, u32[]{:S(2)}) copy-start(bf16[64,1024]{1,0:T(8,128)(2,1)} %get-tuple-element.21.block) | copy-start | bytes 393220
  13.8 1.2 %copy-start.2 = (bf16[1024,512]{1,0:T(8,128)(2,1)S(1)}, bf16[1024,512]{1,0:T(8,128)(2,1)}, u32[]{:S(2)}) copy-start(bf16[1024,512]{1,0:T(8,128)(2,1)} %get-tuple-element.23.own.refs_2_.refs_3_) | copy-start | bytes 3145732
  15.5 6.7 %collective-permute-start.2 = (bf16[72,1024]{1,0:T(8,128)(2,1)S(1)}, bf16[72,1024]{1,0:T(8,128)(2,1)S(1)}, u32[]{:S(2)}, u32[]{:S(2)}) collective-permute-start(bf16[72,1024]{1,0:T(8,128)(2,1)S(1)} %project.2), channel_id=1, source_target_pairs={{0,8},{8,0},{16,24},{24,16},{1,9},{9,1},{17,25},{25,17},{2,10},{10... | collective-permute-start | bytes 442376 | tf_op jit(solution)/shard_map/ppermute | solution.py:250
  18.1 9.2 %collective-permute-start.5 = (bf16[72,1024]{1,0:T(8,128)(2,1)S(1)}, bf16[72,1024]{1,0:T(8,128)(2,1)S(1)}, u32[]{:S(2)}, u32[]{:S(2)}) collective-permute-start(bf16[72,1024]{1,0:T(8,128)(2,1)S(1)} %get-tuple-element.29), channel_id=1, source_target_pairs={{0,16},{8,24},{16,0},{24,8},{1,17},{9,25},{17,1},{25,9},{2,18},{10... | collective-permute-start | bytes 442376 | tf_op jit(solution)/shard_map/ppermute | solution.py:250
  19.7 7.6 %collective-permute-start.6 = (bf16[72,1024]{1,0:T(8,128)(2,1)S(1)}, bf16[72,1024]{1,0:T(8,128)(2,1)S(1)}, u32[]{:S(2)}, u32[]{:S(2)}) collective-permute-start(bf16[72,1024]{1,0:T(8,128)(2,1)S(1)} %get-tuple-element.30), channel_id=1, source_target_pairs={{0,24},{8,16},{16,8},{24,0},{1,25},{9,17},{17,9},{25,1},{2,26},{10... | collective-permute-start | bytes 442376 | tf_op jit(solution)/shard_map/ppermute | solution.py:250
  27.4 10.0 %copy-start.4 = (s32[8]{0:T(128)S(1)}, s32[8]{0:T(128)}, u32[]{:S(2)}) copy-start(s32[8]{0:T(128)} %block_map.9) | copy-start | bytes 100
  27.4 10.0 %copy-start.5 = (s32[4]{0:T(128)S(1)}, s32[4]{0:T(128)}, u32[]{:S(2)}) copy-start(s32[4]{0:T(128)} %lengths.9) | copy-start | bytes 52
  27.4 6.2 %collective-permute-start.7 = (bf16[64,1024]{1,0:T(8,128)(2,1)S(1)}, bf16[64,1024]{1,0:T(8,128)(2,1)S(1)}, u32[]{:S(2)}, u32[]{:S(2)}) collective-permute-start(bf16[64,1024]{1,0:T(8,128)(2,1)S(1)} %get-tuple-element.31.refs_0_), channel_id=1, source_target_pairs={{0,8},{8,0},{16,24},{24,16},{1,9},{9,1},{17,25},{25,17},{2,10},{10... | collective-permute-start | bytes 393224 | tf_op jit(solution)/shard_map/ppermute | solution.py:250
  28.2 6.5 %collective-permute-start.8 = (bf16[64,1024]{1,0:T(8,128)(2,1)S(1)}, bf16[64,1024]{1,0:T(8,128)(2,1)S(1)}, u32[]{:S(2)}, u32[]{:S(2)}) collective-permute-start(bf16[64,1024]{1,0:T(8,128)(2,1)S(1)} %get-tuple-element.31.refs_0_), channel_id=1, source_target_pairs={{0,16},{8,24},{16,0},{24,8},{1,17},{9,25},{17,1},{25,9},{2,18},{10... | collective-permute-start | bytes 393224 | tf_op jit(solution)/shard_map/ppermute | solution.py:250
  29.4 6.6 %collective-permute-start.9 = (bf16[64,1024]{1,0:T(8,128)(2,1)S(1)}, bf16[64,1024]{1,0:T(8,128)(2,1)S(1)}, u32[]{:S(2)}, u32[]{:S(2)}) collective-permute-start(bf16[64,1024]{1,0:T(8,128)(2,1)S(1)} %get-tuple-element.31.refs_0_), channel_id=1, source_target_pairs={{0,24},{8,16},{16,8},{24,0},{1,25},{9,17},{17,9},{25,1},{2,26},{10... | collective-permute-start | bytes 393224 | tf_op jit(solution)/shard_map/ppermute | solution.py:250
  31.0 5.1 %collective-permute-start.10 = (bf16[64,1024]{1,0:T(8,128)(2,1)S(1)}, bf16[64,1024]{1,0:T(8,128)(2,1)S(1)}, u32[]{:S(2)}, u32[]{:S(2)}) collective-permute-start(bf16[64,1024]{1,0:T(8,128)(2,1)S(1)} %get-tuple-element.31.refs_0_), channel_id=1, source_target_pairs={{0,1},{1,0},{2,3},{3,2},{4,5},{5,4},{6,7},{7,6},{8,9},{9,8},{10,11... | collective-permute-start | bytes 393224 | tf_op jit(solution)/shard_map/ppermute | solution.py:247
  33.6 2.5 %collective-permute-start.11 = (bf16[64,1024]{1,0:T(8,128)(2,1)S(1)}, bf16[64,1024]{1,0:T(8,128)(2,1)S(1)}, u32[]{:S(2)}, u32[]{:S(2)}) collective-permute-start(bf16[64,1024]{1,0:T(8,128)(2,1)S(1)} %collective-permute-done.7.refs_1_), channel_id=1, source_target_pairs={{0,1},{1,0},{2,3},{3,2},{4,5},{5,4},{6,7},{7,6},{8,9},{9,8},{10,11... | collective-permute-start | bytes 393224 | tf_op jit(solution)/shard_map/ppermute | solution.py:247
  34.6 1.4 %collective-permute-start.12 = (bf16[64,1024]{1,0:T(8,128)(2,1)S(1)}, bf16[64,1024]{1,0:T(8,128)(2,1)S(1)}, u32[]{:S(2)}, u32[]{:S(2)}) collective-permute-start(bf16[64,1024]{1,0:T(8,128)(2,1)S(1)} %collective-permute-done.8.refs_2_), channel_id=1, source_target_pairs={{0,1},{1,0},{2,3},{3,2},{4,5},{5,4},{6,7},{7,6},{8,9},{9,8},{10,11... | collective-permute-start | bytes 393224 | tf_op jit(solution)/shard_map/ppermute | solution.py:247
  36.0 1.3 %collective-permute-start.13 = (bf16[64,1024]{1,0:T(8,128)(2,1)S(1)}, bf16[64,1024]{1,0:T(8,128)(2,1)S(1)}, u32[]{:S(2)}, u32[]{:S(2)}) collective-permute-start(bf16[64,1024]{1,0:T(8,128)(2,1)S(1)} %collective-permute-done.9.refs_3_), channel_id=1, source_target_pairs={{0,1},{1,0},{2,3},{3,2},{4,5},{5,4},{6,7},{7,6},{8,9},{9,8},{10,11... | collective-permute-start | bytes 393224 | tf_op jit(solution)/shard_map/ppermute | solution.py:247
  40.5 8.6 %collective-permute-start.17 = (bf16[72,1024]{1,0:T(8,128)(2,1)S(1)}, bf16[72,1024]{1,0:T(8,128)(2,1)S(1)}, u32[]{:S(2)}, u32[]{:S(2)}) collective-permute-start(bf16[72,1024]{1,0:T(8,128)(2,1)S(1)} %attend.9), channel_id=1, source_target_pairs={{0,24},{8,16},{16,8},{24,0},{1,25},{9,17},{17,9},{25,1},{2,26},{10... | collective-permute-start | bytes 442376 | tf_op jit(solution)/shard_map/ppermute | solution.py:250
  44.2 6.3 %collective-permute-start.16 = (bf16[72,1024]{1,0:T(8,128)(2,1)S(1)}, bf16[72,1024]{1,0:T(8,128)(2,1)S(1)}, u32[]{:S(2)}, u32[]{:S(2)}) collective-permute-start(bf16[72,1024]{1,0:T(8,128)(2,1)S(1)} %attend.8), channel_id=1, source_target_pairs={{0,16},{8,24},{16,0},{24,8},{1,17},{9,25},{17,1},{25,9},{2,18},{10... | collective-permute-start | bytes 442376 | tf_op jit(solution)/shard_map/ppermute | solution.py:250
  46.8 5.6 %collective-permute-start.15 = (bf16[72,1024]{1,0:T(8,128)(2,1)S(1)}, bf16[72,1024]{1,0:T(8,128)(2,1)S(1)}, u32[]{:S(2)}, u32[]{:S(2)}) collective-permute-start(bf16[72,1024]{1,0:T(8,128)(2,1)S(1)} %attend.7), channel_id=1, source_target_pairs={{0,8},{8,0},{16,24},{24,16},{1,9},{9,1},{17,25},{25,17},{2,10},{10... | collective-permute-start | bytes 442376 | tf_op jit(solution)/shard_map/ppermute | solution.py:250
  52.5 7.0 %collective-permute-start.18 = (bf16[72,1024]{1,0:T(8,128)(2,1)S(1)}, bf16[72,1024]{1,0:T(8,128)(2,1)S(1)}, u32[]{:S(2)}, u32[]{:S(2)}) collective-permute-start(bf16[72,1024]{1,0:T(8,128)(2,1)S(1)} %get-tuple-element.35), channel_id=1, source_target_pairs={{0,2},{1,3},{2,0},{3,1},{4,6},{5,7},{6,4},{7,5},{8,10},{9,11},{10,... | collective-permute-start | bytes 442376 | tf_op jit(solution)/shard_map/ppermute | solution.py:253
  54.1 13.2 %collective-permute-start.19 = (bf16[72,1024]{1,0:T(8,128)(2,1)S(1)}, bf16[72,1024]{1,0:T(8,128)(2,1)S(1)}, u32[]{:S(2)}, u32[]{:S(2)}) collective-permute-start(bf16[72,1024]{1,0:T(8,128)(2,1)S(1)} %get-tuple-element.36), channel_id=1, source_target_pairs={{0,4},{1,5},{2,6},{3,7},{4,0},{5,1},{6,2},{7,3},{8,12},{9,13},{10,... | collective-permute-start | bytes 442376 | tf_op jit(solution)/shard_map/ppermute | solution.py:253
  56.7 10.6 %collective-permute-start.20 = (bf16[72,1024]{1,0:T(8,128)(2,1)S(1)}, bf16[72,1024]{1,0:T(8,128)(2,1)S(1)}, u32[]{:S(2)}, u32[]{:S(2)}) collective-permute-start(bf16[72,1024]{1,0:T(8,128)(2,1)S(1)} %get-tuple-element.37), channel_id=1, source_target_pairs={{0,6},{1,7},{2,4},{3,5},{4,2},{5,3},{6,0},{7,1},{8,14},{9,15},{10,... | collective-permute-start | bytes 442376 | tf_op jit(solution)/shard_map/ppermute | solution.py:253
  67.4 1.3 %collective-permute-start.21 = (bf16[64,512]{1,0:T(8,128)(2,1)S(1)}, bf16[64,512]{1,0:T(8,128)(2,1)S(1)}, u32[]{:S(2)}, u32[]{:S(2)}) collective-permute-start(bf16[64,512]{1,0:T(8,128)(2,1)S(1)} %get-tuple-element.39), channel_id=1, source_target_pairs={{0,1},{1,0},{2,3},{3,2},{4,5},{5,4},{6,7},{7,6},{8,9},{9,8},{10,11... | collective-permute-start | bytes 196616 | tf_op jit(solution)/shard_map/ppermute | solution.py:247

commit v4 on v2

--- a/solution.py
+++ b/solution.py
@@ -23,37 +23,13 @@
     return pl.BlockSpec(memory_space=pltpu.SMEM)
 
 
-def hbm():
-    return pl.BlockSpec(memory_space=pl.ANY)
-
-
-def params():
-    return pltpu.CompilerParams(vmem_limit_bytes=VMEM_BYTES)
+def way(steps):
+    return [0] + list(range(steps - 1, 0, -1))
 
 
 def place():
     t = lax.axis_index("tp")
     return lax.axis_index("ctx"), t // 2, t % 2
-
-
-def slice_kernel(steps, tokens, new, *rest):
-    outs, new_out, sem = rest[:steps], rest[steps], rest[steps + 1]
-    c, _, k = place()
-    rows, width = outs[0].shape
-    first = pl.multiple_of(k * rows, rows)
-    copies = []
-    for step, out in enumerate(outs):
-        column = pl.multiple_of((c ^ step) * width, width)
-        copies.append(
-            pltpu.make_async_copy(
-                tokens.at[pl.ds(first, rows), pl.ds(column, width)], out, sem.at[step]
-            )
-        )
-    for copy in copies:
-        copy.start()
-    new_out[...] = new[:, pl.ds(pl.multiple_of(c * width, width), width)]
-    for copy in copies:
-        copy.wait()
 
 
 def pack_kernel(*refs):
@@ -147,7 +123,7 @@
         index = lax.broadcasted_iota(jnp.int32, shape, axis)
         position = jnp.zeros(shape, jnp.int32)
         for number in range(halves * steps):
-            held = 2 * (c ^ (number % steps)) + (k ^ (number // steps))
+            held = 2 * (c ^ way(steps)[number % steps]) + (k ^ (number // steps))
             inside = (index >= number * rows) & (index < (number + 1) * rows)
             position = jnp.where(inside, block_map[held] * rows + index - number * rows, position)
         last = halves * tail
@@ -191,8 +167,8 @@
 def relay_kernel(steps, *refs):
     blocks, outs = refs[:steps], refs[steps:]
     c, z, _ = place()
-    for slot, out in enumerate(outs):
-        for step, block in enumerate(blocks):
+    for slot, out in zip(way(steps), outs):
+        for step, block in zip(way(steps), blocks):
 
             @pl.when((c ^ z ^ slot) == step)
             def _(out=out, block=block):
@@ -207,6 +183,7 @@
     for out, core in ((keep, k), (send, 1 - k)):
         column = pl.ds(pl.multiple_of(core * width, width), width)
         terms = [part[:, column].astype(jnp.float32) for part in parts]
+        terms = [terms[way(steps).index(m)] for m in range(steps)]
         while len(terms) > 1:
             terms = [a + b for a, b in zip(terms[::2], terms[1::2])]
         out[...] = terms[0][: out.shape[0]].astype(out.dtype)
@@ -242,6 +219,14 @@
     def to_chip(value, step):
         return lax.ppermute(value, "tp", [(i, i ^ (2 * step)) for i in range(tp)])
 
+    def all_to_ctx(values):
+        values = list(values)
+        return values[:1] + [to_ctx(value, m) for value, m in zip(values[1:], way(steps)[1:])]
+
+    def all_to_chip(values):
+        values = list(values)
+        return values[:1] + [to_chip(value, m) for value, m in zip(values[1:], way(steps)[1:])]
+
     def call(kernel, name, inputs, shapes, scratch=(), spaces=None):
         return pl.pallas_call(
             kernel,
@@ -249,26 +234,19 @@
             in_specs=spaces or [vmem()] * len(inputs),
             out_specs=[vmem()] * len(shapes),
             scratch_shapes=list(scratch),
-            compiler_params=params(),
+            compiler_params=pltpu.CompilerParams(vmem_limit_bytes=VMEM_BYTES),
             name=name,
         )(*inputs)
 
-    *sent, new_columns = call(
-        functools.partial(slice_kernel, steps),
-        "slice_tokens",
-        (tokens, new_token_states),
-        [((rows, depth), bf16)] * steps + [((count, depth), bf16)],
-        [pltpu.SemaphoreType.DMA((steps,))],
-        [hbm(), vmem()],
-    )
-    blocks = [sent[0]] + [to_ctx(value, step) for step, value in enumerate(sent[1:], 1)]
-    weights = (w_query, key_matrix, value_matrix)
-    (own,) = call(
-        pack_kernel, "pack_weights", weights, [((depth, features // 2), bf16)]
-    )
+    c, _, k = place()
+    sent = [
+        lax.dynamic_slice(tokens, (k * rows, (c ^ m) * depth), (rows, depth)) for m in way(steps)
+    ]
+    new_columns = lax.dynamic_slice_in_dim(new_token_states, c * depth, depth, 1)
+    blocks = all_to_ctx(sent)
+    *weights, _ = lax.optimization_barrier((w_query, key_matrix, value_matrix, sent[1]))
+    (own,) = call(pack_kernel, "pack_weights", weights, [((depth, features // 2), bf16)])
     other = to_core(own)
-    w_out_late, _ = lax.optimization_barrier((w_out, blocks[1]))
-    w_other = to_core(w_out_late)
 
     part_shape = (rows + pad, features)
     x_rows = -(-(steps * rows + pad) // 16) * 16
@@ -281,7 +259,9 @@
         [pltpu.VMEM((x_rows, depth), bf16)],
     )
 
-    parts = [parts[0]] + [to_ctx(part, step) for step, part in enumerate(parts[1:], 1)]
+    w_out_late, _ = lax.optimization_barrier((w_out, parts[0]))
+    parts = all_to_ctx(parts)
+    w_other = to_core(w_out_late)
     held, new = call(
         functools.partial(add_kernel, steps),
         "add_parts",
@@ -289,7 +269,7 @@
         [((rows, features), bf16), ((pad, features), bf16)],
     )
 
-    mine = [held] + [to_ctx(held, step) for step in range(1, steps)]
+    mine = all_to_ctx([held] * steps)
     theirs = [to_core(value) for value in mine]
 
     k_rows = -(-(2 * steps * rows + pad) // 128) * 128
@@ -307,14 +287,14 @@
         [smem()] * 2 + [vmem()] * (2 * steps + 3),
     )
 
-    arrived = [outs[0]] + [to_ctx(out, step) for step, out in enumerate(outs[1:], 1)]
+    arrived = all_to_ctx(outs)
     slots = call(
         functools.partial(relay_kernel, steps),
         "relay",
         arrived,
         [((rows + pad, out_width), bf16)] * steps,
     )
-    slots = [slots[0]] + [to_chip(slot, step) for step, slot in enumerate(slots[1:], 1)]
+    slots = all_to_chip(slots)
     keep, send = call(
         functools.partial(sum_kernel, steps),
         "sum_heads",

time: 64.3 us -> 67.3 us (1.047)
  waiting for transfers between devices: 35.1 us -> 40.3 us
  local copies, waits for them, and re-layouts: 3.16 us -> 1.73 us
    ppermute x12, waiting for transfers between devices: 22.6 us -> 25.8 us  [to_ctx(): return lax.ppermute(value, 'ctx', [(i, i ^ step) for i in range(steps)])]
    unnamed x16 -> x14, local copies, waits for them, and re-layouts: 3.16 us -> 0.5 us
    ppermute x3, waiting for transfers between devices: 9.93 us -> 11.9 us  [to_chip(): return lax.ppermute(value, 'tp', [(i, i ^ 2 * step) for i in range(tp)])]
    dynamic_slice x0 -> x2, local copies, waits for them, and re-layouts: none -> 1.23 us  [the longest x1 1.22 us: on_device_small(): lax.dynamic_slice(tokens, (k * rows, (c ^ m) * depth), (rows, depth))]
    pallas_call x8 -> x7, Pallas kernels: 4.66 us -> 4.54 us  [call(): pl.pallas_call(kernel, out_shape=[jax.ShapeDtypeStruct(shape, kind) for s...]
  transfers between devices with their start and end apart: 22 -> 22, of which waited for: 13 -> 14; matrix products, arithmetic and copies ran while one was open for 0% -> 0% of each run, Pallas kernels for 1% -> 0%
where the time goes in v4:
time: 67.3 us; the launch traced here: 67.1 us
  waiting for transfers between devices  40.3 us (60%)
  starting transfers between devices  19.8 us (29%)
  Pallas kernels  4.54 us (7%)
  local copies, waits for them, and re-layouts  1.73 us (3%)
  between operations  0.8 us (1%)
    ppermute x12, waiting for transfers between devices, to_ctx(): return lax.ppermute(value, 'ctx', [(i, i ^ step) for i in range(steps)])  25.8 us
    ppermute x12, starting transfers between devices, to_ctx(): return lax.ppermute(value, 'ctx', [(i, i ^ step) for i in range(steps)])  14.7 us
    ppermute x3, waiting for transfers between devices, to_chip(): return lax.ppermute(value, 'tp', [(i, i ^ 2 * step) for i in range(tp)])  11.9 us
    pallas_call x7, Pallas kernels, call(): pl.pallas_call(kernel, out_shape=[jax.ShapeDtypeStruct(shape, kind) for s...  4.54 us
    ppermute x3, starting transfers between devices, to_chip(): return lax.ppermute(value, 'tp', [(i, i ^ 2 * step) for i in range(tp)])  4.45 us
    ppermute x7, waiting for transfers between devices, to_core(): return lax.ppermute(value, 'tp', [(i, i ^ 1) for i in range(tp)])  2.58 us
  transfers between devices with their start and end apart: 22, of which 14 were waited for; matrix products, arithmetic and copies ran while one was open for 0% of the time, Pallas kernels for 0%

profile of v4, /device:TPU:0, one launch (start us, length us, event | category | flops | bytes accessed | tf_op | source)
XLA Modules:
  0.0 67.1 jit_solution(13461911215746287070)
XLA Ops:
  0.7 1.2 %fusion = (bf16[64,1024]{1,0:T(8,128)(2,1)S(1)}, bf16[64,1024]{1,0:T(8,128)(2,1)S(1)}, bf16[64,1024]{1,0:T(8,128)(2,1)S(1)}, bf16[64,1024]{1,0:T(8,128)(2,1)S(1)}) fusion(bf16[128,4096]{1,0:T(8,128)(2,1)} %param.8, s32[]{:T(128)S(6)} %select_n.27, s32[]{:T(128)S(6)} %select_n.31, s32[]{:T(128)S(6)} %select_n.29, s32[]{:T(128)S(6)} %select_n.28, s32[]{:T(128)S(6)} %select_n.30), kind=kLoop, calls=%fused_computation.1 | loop fusion | bytes 1048596 | tf_op jit(solution)/shard_map/dynamic_slice | solution.py:243
  2.2 0.5 collective-permute-start.3
  2.7 2.6 %collective-permute-start.2 = (bf16[64,1024]{1,0:T(8,128)(2,1)S(1)}, bf16[64,1024]{1,0:T(8,128)(2,1)S(1)}, u32[]{:S(2)}, u32[]{:S(2)}) collective-permute-start(bf16[64,1024]{1,0:T(8,128)(2,1)S(1)} %get-tuple-element.42), channel_id=1, source_target_pairs={{0,8},{8,0},{16,24},{24,16},{1,9},{9,1},{17,25},{25,17},{2,10},{10... | collective-permute-start | bytes 393224 | tf_op jit(solution)/shard_map/ppermute | solution.py:217
  5.3 1.5 %collective-permute-start.1 = (bf16[64,1024]{1,0:T(8,128)(2,1)S(1)}, bf16[64,1024]{1,0:T(8,128)(2,1)S(1)}, u32[]{:S(2)}, u32[]{:S(2)}) collective-permute-start(bf16[64,1024]{1,0:T(8,128)(2,1)S(1)} %get-tuple-element.45), channel_id=1, source_target_pairs={{0,16},{8,24},{16,0},{24,8},{1,17},{9,25},{17,1},{25,9},{2,18},{10... | collective-permute-start | bytes 393224 | tf_op jit(solution)/shard_map/ppermute | solution.py:217
  6.8 2.6 %collective-permute-done.2.refs_3_ = bf16[64,1024]{1,0:T(8,128)(2,1)S(1)} collective-permute-done((bf16[64,1024]{1,0:T(8,128)(2,1)S(1)}, bf16[64,1024]{1,0:T(8,128)(2,1)S(1)}, u32[]{:S(2)}, u32[]{:S(2)}) %collective-permute-start.2) | collective-permute-done | bytes 131104 | tf_op jit(solution)/shard_map/ppermute | solution.py:217
  9.5 4.2 %collective-permute-done.1.refs_2_ = bf16[64,1024]{1,0:T(8,128)(2,1)S(1)} collective-permute-done((bf16[64,1024]{1,0:T(8,128)(2,1)S(1)}, bf16[64,1024]{1,0:T(8,128)(2,1)S(1)}, u32[]{:S(2)}, u32[]{:S(2)}) %collective-permute-start.1) | collective-permute-done | bytes 131104 | tf_op jit(solution)/shard_map/ppermute | solution.py:217
  13.7 0.7 %project.1 = (f32[72,1024]{1,0:T(8,128)S(1)}, bf16[72,1024]{1,0:T(8,128)(2,1)S(1)}, bf16[72,1024]{1,0:T(8,128)(2,1)S(1)}, bf16[72,1024]{1,0:T(8,128)(2,1)S(1)}) custom-call(bf16[64,1024]{1,0:T(8,128)(2,1)S(1)} %get-tuple-element.44.refs_0_, bf16[64,1024]{1,0:T(8,128)(2,1)S(1)} %collective-permute-done.refs_1_, ...), custom_call_target="tpu_custom_call" | custom-call | tf_op jit(solution)/shard_map/project/pallas_call | solution.py:231
  14.4 0.3 copy-done.2
  14.7 1.5 %collective-permute-start.4 = (bf16[72,1024]{1,0:T(8,128)(2,1)S(1)}, bf16[72,1024]{1,0:T(8,128)(2,1)S(1)}, u32[]{:S(2)}, u32[]{:S(2)}) collective-permute-start(bf16[72,1024]{1,0:T(8,128)(2,1)S(1)} %get-tuple-element.26), channel_id=1, source_target_pairs={{0,24},{8,16},{16,8},{24,0},{1,25},{9,17},{17,9},{25,1},{2,26},{10... | collective-permute-start | bytes 442376 | tf_op jit(solution)/shard_map/ppermute | solution.py:217
  16.2 1.2 %collective-permute-start.5 = (bf16[72,1024]{1,0:T(8,128)(2,1)S(1)}, bf16[72,1024]{1,0:T(8,128)(2,1)S(1)}, u32[]{:S(2)}, u32[]{:S(2)}) collective-permute-start(bf16[72,1024]{1,0:T(8,128)(2,1)S(1)} %get-tuple-element.27), channel_id=1, source_target_pairs={{0,16},{8,24},{16,0},{24,8},{1,17},{9,25},{17,1},{25,9},{2,18},{10... | collective-permute-start | bytes 442376 | tf_op jit(solution)/shard_map/ppermute | solution.py:217
  17.4 0.8 %collective-permute-start.6 = (bf16[72,1024]{1,0:T(8,128)(2,1)S(1)}, bf16[72,1024]{1,0:T(8,128)(2,1)S(1)}, u32[]{:S(2)}, u32[]{:S(2)}) collective-permute-start(bf16[72,1024]{1,0:T(8,128)(2,1)S(1)} %get-tuple-element.28), channel_id=1, source_target_pairs={{0,8},{8,0},{16,24},{24,16},{1,9},{9,1},{17,25},{25,17},{2,10},{10... | collective-permute-start | bytes 442376 | tf_op jit(solution)/shard_map/ppermute | solution.py:217
  18.2 4.1 %collective-permute-done.4.refs_1_ = bf16[72,1024]{1,0:T(8,128)(2,1)S(1)} collective-permute-done((bf16[72,1024]{1,0:T(8,128)(2,1)S(1)}, bf16[72,1024]{1,0:T(8,128)(2,1)S(1)}, u32[]{:S(2)}, u32[]{:S(2)}) %collective-permute-start.4) | collective-permute-done | bytes 147488 | tf_op jit(solution)/shard_map/ppermute | solution.py:217
  22.3 2.7 %collective-permute-done.5.refs_2_ = bf16[72,1024]{1,0:T(8,128)(2,1)S(1)} collective-permute-done((bf16[72,1024]{1,0:T(8,128)(2,1)S(1)}, bf16[72,1024]{1,0:T(8,128)(2,1)S(1)}, u32[]{:S(2)}, u32[]{:S(2)}) %collective-permute-start.5) | collective-permute-done | bytes 147488 | tf_op jit(solution)/shard_map/ppermute | solution.py:217
  25.2 1.2 %collective-permute-start.9 = (bf16[64,1024]{1,0:T(8,128)(2,1)S(1)}, bf16[64,1024]{1,0:T(8,128)(2,1)S(1)}, u32[]{:S(2)}, u32[]{:S(2)}) collective-permute-start(bf16[64,1024]{1,0:T(8,128)(2,1)S(1)} %get-tuple-element.29.refs_0_), channel_id=1, source_target_pairs={{0,8},{8,0},{16,24},{24,16},{1,9},{9,1},{17,25},{25,17},{2,10},{10... | collective-permute-start | bytes 393224 | tf_op jit(solution)/shard_map/ppermute | solution.py:217
  26.4 0.8 %collective-permute-start.8 = (bf16[64,1024]{1,0:T(8,128)(2,1)S(1)}, bf16[64,1024]{1,0:T(8,128)(2,1)S(1)}, u32[]{:S(2)}, u32[]{:S(2)}) collective-permute-start(bf16[64,1024]{1,0:T(8,128)(2,1)S(1)} %get-tuple-element.29.refs_0_), channel_id=1, source_target_pairs={{0,16},{8,24},{16,0},{24,8},{1,17},{9,25},{17,1},{25,9},{2,18},{10... | collective-permute-start | bytes 393224 | tf_op jit(solution)/shard_map/ppermute | solution.py:217
  27.3 1.5 %collective-permute-start.7 = (bf16[64,1024]{1,0:T(8,128)(2,1)S(1)}, bf16[64,1024]{1,0:T(8,128)(2,1)S(1)}, u32[]{:S(2)}, u32[]{:S(2)}) collective-permute-start(bf16[64,1024]{1,0:T(8,128)(2,1)S(1)} %get-tuple-element.29.refs_0_), channel_id=1, source_target_pairs={{0,24},{8,16},{16,8},{24,0},{1,25},{9,17},{17,9},{25,1},{2,26},{10... | collective-permute-start | bytes 393224 | tf_op jit(solution)/shard_map/ppermute | solution.py:217
  28.8 2.5 %collective-permute-done.9.refs_3_ = bf16[64,1024]{1,0:T(8,128)(2,1)S(1)} collective-permute-done((bf16[64,1024]{1,0:T(8,128)(2,1)S(1)}, bf16[64,1024]{1,0:T(8,128)(2,1)S(1)}, u32[]{:S(2)}, u32[]{:S(2)}) %collective-permute-start.9) | collective-permute-done | bytes 131104 | tf_op jit(solution)/shard_map/ppermute | solution.py:217
  31.3 1.5 %collective-permute-done.8.refs_2_ = bf16[64,1024]{1,0:T(8,128)(2,1)S(1)} collective-permute-done((bf16[64,1024]{1,0:T(8,128)(2,1)S(1)}, bf16[64,1024]{1,0:T(8,128)(2,1)S(1)}, u32[]{:S(2)}, u32[]{:S(2)}) %collective-permute-start.8) | collective-permute-done | bytes 131104 | tf_op jit(solution)/shard_map/ppermute | solution.py:217
  32.8 1.6 %collective-permute-done.7.refs_1_ = bf16[64,1024]{1,0:T(8,128)(2,1)S(1)} collective-permute-done((bf16[64,1024]{1,0:T(8,128)(2,1)S(1)}, bf16[64,1024]{1,0:T(8,128)(2,1)S(1)}, u32[]{:S(2)}, u32[]{:S(2)}) %collective-permute-start.7) | collective-permute-done | bytes 131104 | tf_op jit(solution)/shard_map/ppermute | solution.py:217
  34.4 1.3 %collective-permute-done.11.refs_5_ = bf16[64,1024]{1,0:T(8,128)(2,1)S(1)} collective-permute-done((bf16[64,1024]{1,0:T(8,128)(2,1)S(1)}, bf16[64,1024]{1,0:T(8,128)(2,1)S(1)}, u32[]{:S(2)}, u32[]{:S(2)}) %collective-permute-start.11) | collective-permute-done | bytes 131104 | tf_op jit(solution)/shard_map/ppermute | solution.py:214
  35.8 2.8 %attend.1 = (bf16[72,1024]{1,0:T(8,128)(2,1)S(1)}, bf16[72,1024]{1,0:T(8,128)(2,1)S(1)}, bf16[72,1024]{1,0:T(8,128)(2,1)S(1)}, bf16[72,1024]{1,0:T(8,128)(2,1)S(1)}) custom-call(s32[8]{0:T(128)S(1)} %copy-done.5, s32[4]{0:T(128)S(1)} %copy-done.6, bf16[64,1024]{1,0:T(8,128)(2,1)S(1)} %get-tuple-element.29.refs_0_, ...), custom_call_target="tpu_custom_call" | custom-call | tf_op jit(solution)/shard_map/attend/pallas_call | solution.py:231
  38.6 2.0 %collective-permute-start.15 = (bf16[72,1024]{1,0:T(8,128)(2,1)S(1)}, bf16[72,1024]{1,0:T(8,128)(2,1)S(1)}, u32[]{:S(2)}, u32[]{:S(2)}) collective-permute-start(bf16[72,1024]{1,0:T(8,128)(2,1)S(1)} %get-tuple-element.33), channel_id=1, source_target_pairs={{0,24},{8,16},{16,8},{24,0},{1,25},{9,17},{17,9},{25,1},{2,26},{10... | collective-permute-start | bytes 442376 | tf_op jit(solution)/shard_map/ppermute | solution.py:217
  40.5 0.5 collective-permute-start.16
  41.1 1.0 %collective-permute-start.17 = (bf16[72,1024]{1,0:T(8,128)(2,1)S(1)}, bf16[72,1024]{1,0:T(8,128)(2,1)S(1)}, u32[]{:S(2)}, u32[]{:S(2)}) collective-permute-start(bf16[72,1024]{1,0:T(8,128)(2,1)S(1)} %get-tuple-element.35), channel_id=1, source_target_pairs={{0,8},{8,0},{16,24},{24,16},{1,9},{9,1},{17,25},{25,17},{2,10},{10... | collective-permute-start | bytes 442376 | tf_op jit(solution)/shard_map/ppermute | solution.py:217
  42.1 4.1 %collective-permute-done.15.refs_1_ = bf16[72,1024]{1,0:T(8,128)(2,1)S(1)} collective-permute-done((bf16[72,1024]{1,0:T(8,128)(2,1)S(1)}, bf16[72,1024]{1,0:T(8,128)(2,1)S(1)}, u32[]{:S(2)}, u32[]{:S(2)}) %collective-permute-start.15) | collective-permute-done | bytes 147488 | tf_op jit(solution)/shard_map/ppermute | solution.py:217
  46.2 2.4 %collective-permute-done.16.refs_2_ = bf16[72,1024]{1,0:T(8,128)(2,1)S(1)} collective-permute-done((bf16[72,1024]{1,0:T(8,128)(2,1)S(1)}, bf16[72,1024]{1,0:T(8,128)(2,1)S(1)}, u32[]{:S(2)}, u32[]{:S(2)}) %collective-permute-start.16) | collective-permute-done | bytes 147488 | tf_op jit(solution)/shard_map/ppermute | solution.py:217
  48.7 3.7 %collective-permute-start.18 = (bf16[72,1024]{1,0:T(8,128)(2,1)S(1)}, bf16[72,1024]{1,0:T(8,128)(2,1)S(1)}, u32[]{:S(2)}, u32[]{:S(2)}) collective-permute-start(bf16[72,1024]{1,0:T(8,128)(2,1)S(1)} %get-tuple-element.37), channel_id=1, source_target_pairs={{0,6},{1,7},{2,4},{3,5},{4,2},{5,3},{6,0},{7,1},{8,14},{9,15},{10,... | collective-permute-start | bytes 442376 | tf_op jit(solution)/shard_map/ppermute | solution.py:220
  52.4 0.8 %collective-permute-start.20 = (bf16[72,1024]{1,0:T(8,128)(2,1)S(1)}, bf16[72,1024]{1,0:T(8,128)(2,1)S(1)}, u32[]{:S(2)}, u32[]{:S(2)}) collective-permute-start(bf16[72,1024]{1,0:T(8,128)(2,1)S(1)} %get-tuple-element.39), channel_id=1, source_target_pairs={{0,2},{1,3},{2,0},{3,1},{4,6},{5,7},{6,4},{7,5},{8,10},{9,11},{10,... | collective-permute-start | bytes 442376 | tf_op jit(solution)/shard_map/ppermute | solution.py:220
  53.2 4.2 %collective-permute-done.18.refs_1_ = bf16[72,1024]{1,0:T(8,128)(2,1)S(1)} collective-permute-done((bf16[72,1024]{1,0:T(8,128)(2,1)S(1)}, bf16[72,1024]{1,0:T(8,128)(2,1)S(1)}, u32[]{:S(2)}, u32[]{:S(2)}) %collective-permute-start.18) | collective-permute-done | bytes 147488 | tf_op jit(solution)/shard_map/ppermute | solution.py:220
  57.4 7.7 %collective-permute-done.19.refs_2_ = bf16[72,1024]{1,0:T(8,128)(2,1)S(1)} collective-permute-done((bf16[72,1024]{1,0:T(8,128)(2,1)S(1)}, bf16[72,1024]{1,0:T(8,128)(2,1)S(1)}, u32[]{:S(2)}, u32[]{:S(2)}) %collective-permute-start.19) | collective-permute-done | bytes 147488 | tf_op jit(solution)/shard_map/ppermute | solution.py:220
  65.2 1.2 %collective-permute-done.21.other = bf16[64,512]{1,0:T(8,128)(2,1)S(1)} collective-permute-done((bf16[64,512]{1,0:T(8,128)(2,1)S(1)}, bf16[64,512]{1,0:T(8,128)(2,1)S(1)}, u32[]{:S(2)}, u32[]{:S(2)}) %collective-permute-start.21) | collective-permute-done | bytes 65568 | tf_op jit(solution)/shard_map/ppermute | solution.py:214
  66.4 0.7 %finish.1 = (bf16[128,512]{1,0:T(8,128)(2,1)}, bf16[4,512]{1,0:T(4,128)(2,1)}) custom-call(bf16[72,512]{1,0:T(8,128)(2,1)S(1)} %get-tuple-element.40.keep, bf16[64,512]{1,0:T(8,128)(2,1)S(1)} %collective-permute-done.21.other), custom_call_target="tpu_custom_call" | custom-call | tf_op jit(solution)/shard_map/finish/pallas_call | solution.py:231
  (35 shorter events, 0.8 us)
Async XLA Ops:
  0.6 6.2 %copy-start = (bf16[4,4096]{1,0:T(4,128)(2,1)S(1)}, bf16[4,4096]{1,0:T(4,128)(2,1)}, u32[]{:S(2)}) copy-start(bf16[4,4096]{1,0:T(4,128)(2,1)} %param.9) | copy-start | bytes 98308
  0.7 1.3 %copy-start.1 = (bf16[1024,256]{1,0:T(8,128)(2,1)S(1)}, bf16[1024,256]{1,0:T(8,128)(2,1)}, u32[]{:S(2)}) copy-start(bf16[1024,256]{1,0:T(8,128)(2,1)} %refs_0_) | copy-start | bytes 1572868
  0.7 1.4 %copy-start.3 = (bf16[1024,128]{1,0:T(8,128)(2,1)S(1)}, bf16[1024,128]{1,0:T(8,128)(2,1)}, u32[]{:S(2)}) copy-start(bf16[1024,128]{1,0:T(8,128)(2,1)} %refs_1_) | copy-start | bytes 786436
  0.7 1.4 %copy-start.4 = (bf16[1024,128]{1,0:T(8,128)(2,1)S(1)}, bf16[1024,128]{1,0:T(8,128)(2,1)}, u32[]{:S(2)}) copy-start(bf16[1024,128]{1,0:T(8,128)(2,1)} %refs_2_) | copy-start | bytes 786436
  2.2 11.5 %collective-permute-start.3 = (bf16[1024,512]{1,0:T(8,128)(2,1)S(1)}, bf16[1024,512]{1,0:T(8,128)(2,1)S(1)}, u32[]{:S(2)}, u32[]{:S(2)}) collective-permute-start(bf16[1024,512]{1,0:T(8,128)(2,1)S(1)} %pack_weights.1.refs_5_), channel_id=1, source_target_pairs={{0,1},{1,0},{2,3},{3,2},{4,5},{5,4},{6,7},{7,6},{8,9},{9,8},{10,11... | collective-permute-start | bytes 3145736 | tf_op jit(solution)/shard_map/ppermute | solution.py:214
  2.7 6.7 %collective-permute-start.2 = (bf16[64,1024]{1,0:T(8,128)(2,1)S(1)}, bf16[64,1024]{1,0:T(8,128)(2,1)S(1)}, u32[]{:S(2)}, u32[]{:S(2)}) collective-permute-start(bf16[64,1024]{1,0:T(8,128)(2,1)S(1)} %get-tuple-element.42), channel_id=1, source_target_pairs={{0,8},{8,0},{16,24},{24,16},{1,9},{9,1},{17,25},{25,17},{2,10},{10... | collective-permute-start | bytes 393224 | tf_op jit(solution)/shard_map/ppermute | solution.py:217
  5.3 8.4 %collective-permute-start.1 = (bf16[64,1024]{1,0:T(8,128)(2,1)S(1)}, bf16[64,1024]{1,0:T(8,128)(2,1)S(1)}, u32[]{:S(2)}, u32[]{:S(2)}) collective-permute-start(bf16[64,1024]{1,0:T(8,128)(2,1)S(1)} %get-tuple-element.45), channel_id=1, source_target_pairs={{0,16},{8,24},{16,0},{24,8},{1,17},{9,25},{17,1},{25,9},{2,18},{10... | collective-permute-start | bytes 393224 | tf_op jit(solution)/shard_map/ppermute | solution.py:217
  6.8 6.9 %collective-permute-start = (bf16[64,1024]{1,0:T(8,128)(2,1)S(1)}, bf16[64,1024]{1,0:T(8,128)(2,1)S(1)}, u32[]{:S(2)}, u32[]{:S(2)}) collective-permute-start(bf16[64,1024]{1,0:T(8,128)(2,1)S(1)} %get-tuple-element.43), channel_id=1, source_target_pairs={{0,24},{8,16},{16,8},{24,0},{1,25},{9,17},{17,9},{25,1},{2,26},{10... | collective-permute-start | bytes 393224 | tf_op jit(solution)/shard_map/ppermute | solution.py:217
  13.7 1.0 %copy-start.2 = (bf16[256,1024]{1,0:T(8,128)(2,1)S(1)}, bf16[256,1024]{1,0:T(8,128)(2,1)}, u32[]{:S(2)}) copy-start(bf16[256,1024]{1,0:T(8,128)(2,1)} %refs_9_.1) | copy-start | bytes 1572868
  14.7 21.1 %collective-permute-start.14 = (bf16[256,1024]{1,0:T(8,128)(2,1)S(1)}, bf16[256,1024]{1,0:T(8,128)(2,1)S(1)}, u32[]{:S(2)}, u32[]{:S(2)}) collective-permute-start(bf16[256,1024]{1,0:T(8,128)(2,1)S(1)} %copy-done.2), channel_id=1, source_target_pairs={{0,1},{1,0},{2,3},{3,2},{4,5},{5,4},{6,7},{7,6},{8,9},{9,8},{10,11... | collective-permute-start | bytes 1572872 | tf_op jit(solution)/shard_map/ppermute | solution.py:214
  14.7 7.6 %collective-permute-start.4 = (bf16[72,1024]{1,0:T(8,128)(2,1)S(1)}, bf16[72,1024]{1,0:T(8,128)(2,1)S(1)}, u32[]{:S(2)}, u32[]{:S(2)}) collective-permute-start(bf16[72,1024]{1,0:T(8,128)(2,1)S(1)} %get-tuple-element.26), channel_id=1, source_target_pairs={{0,24},{8,16},{16,8},{24,0},{1,25},{9,17},{17,9},{25,1},{2,26},{10... | collective-permute-start | bytes 442376 | tf_op jit(solution)/shard_map/ppermute | solution.py:217
  16.2 8.8 %collective-permute-start.5 = (bf16[72,1024]{1,0:T(8,128)(2,1)S(1)}, bf16[72,1024]{1,0:T(8,128)(2,1)S(1)}, u32[]{:S(2)}, u32[]{:S(2)}) collective-permute-start(bf16[72,1024]{1,0:T(8,128)(2,1)S(1)} %get-tuple-element.27), channel_id=1, source_target_pairs={{0,16},{8,24},{16,0},{24,8},{1,17},{9,25},{17,1},{25,9},{2,18},{10... | collective-permute-start | bytes 442376 | tf_op jit(solution)/shard_map/ppermute | solution.py:217
  17.4 7.7 %collective-permute-start.6 = (bf16[72,1024]{1,0:T(8,128)(2,1)S(1)}, bf16[72,1024]{1,0:T(8,128)(2,1)S(1)}, u32[]{:S(2)}, u32[]{:S(2)}) collective-permute-start(bf16[72,1024]{1,0:T(8,128)(2,1)S(1)} %get-tuple-element.28), channel_id=1, source_target_pairs={{0,8},{8,0},{16,24},{24,16},{1,9},{9,1},{17,25},{25,17},{2,10},{10... | collective-permute-start | bytes 442376 | tf_op jit(solution)/shard_map/ppermute | solution.py:217
  25.2 10.6 %copy-start.5 = (s32[8]{0:T(128)S(1)}, s32[8]{0:T(128)}, u32[]{:S(2)}) copy-start(s32[8]{0:T(128)} %block_map.1) | copy-start | bytes 100
  25.2 10.5 %copy-start.6 = (s32[4]{0:T(128)S(1)}, s32[4]{0:T(128)}, u32[]{:S(2)}) copy-start(s32[4]{0:T(128)} %lengths.1) | copy-start | bytes 52
  25.2 6.1 %collective-permute-start.9 = (bf16[64,1024]{1,0:T(8,128)(2,1)S(1)}, bf16[64,1024]{1,0:T(8,128)(2,1)S(1)}, u32[]{:S(2)}, u32[]{:S(2)}) collective-permute-start(bf16[64,1024]{1,0:T(8,128)(2,1)S(1)} %get-tuple-element.29.refs_0_), channel_id=1, source_target_pairs={{0,8},{8,0},{16,24},{24,16},{1,9},{9,1},{17,25},{25,17},{2,10},{10... | collective-permute-start | bytes 393224 | tf_op jit(solution)/shard_map/ppermute | solution.py:217
  26.4 6.3 %collective-permute-start.8 = (bf16[64,1024]{1,0:T(8,128)(2,1)S(1)}, bf16[64,1024]{1,0:T(8,128)(2,1)S(1)}, u32[]{:S(2)}, u32[]{:S(2)}) collective-permute-start(bf16[64,1024]{1,0:T(8,128)(2,1)S(1)} %get-tuple-element.29.refs_0_), channel_id=1, source_target_pairs={{0,16},{8,24},{16,0},{24,8},{1,17},{9,25},{17,1},{25,9},{2,18},{10... | collective-permute-start | bytes 393224 | tf_op jit(solution)/shard_map/ppermute | solution.py:217
  27.3 7.2 %collective-permute-start.7 = (bf16[64,1024]{1,0:T(8,128)(2,1)S(1)}, bf16[64,1024]{1,0:T(8,128)(2,1)S(1)}, u32[]{:S(2)}, u32[]{:S(2)}) collective-permute-start(bf16[64,1024]{1,0:T(8,128)(2,1)S(1)} %get-tuple-element.29.refs_0_), channel_id=1, source_target_pairs={{0,24},{8,16},{16,8},{24,0},{1,25},{9,17},{17,9},{25,1},{2,26},{10... | collective-permute-start | bytes 393224 | tf_op jit(solution)/shard_map/ppermute | solution.py:217
  28.8 5.6 %collective-permute-start.10 = (bf16[64,1024]{1,0:T(8,128)(2,1)S(1)}, bf16[64,1024]{1,0:T(8,128)(2,1)S(1)}, u32[]{:S(2)}, u32[]{:S(2)}) collective-permute-start(bf16[64,1024]{1,0:T(8,128)(2,1)S(1)} %get-tuple-element.29.refs_0_), channel_id=1, source_target_pairs={{0,1},{1,0},{2,3},{3,2},{4,5},{5,4},{6,7},{7,6},{8,9},{9,8},{10,11... | collective-permute-start | bytes 393224 | tf_op jit(solution)/shard_map/ppermute | solution.py:214
  31.3 3.1 %collective-permute-start.13 = (bf16[64,1024]{1,0:T(8,128)(2,1)S(1)}, bf16[64,1024]{1,0:T(8,128)(2,1)S(1)}, u32[]{:S(2)}, u32[]{:S(2)}) collective-permute-start(bf16[64,1024]{1,0:T(8,128)(2,1)S(1)} %collective-permute-done.9.refs_3_), channel_id=1, source_target_pairs={{0,1},{1,0},{2,3},{3,2},{4,5},{5,4},{6,7},{7,6},{8,9},{9,8},{10,11... | collective-permute-start | bytes 393224 | tf_op jit(solution)/shard_map/ppermute | solution.py:214
  32.8 1.6 %collective-permute-start.12 = (bf16[64,1024]{1,0:T(8,128)(2,1)S(1)}, bf16[64,1024]{1,0:T(8,128)(2,1)S(1)}, u32[]{:S(2)}, u32[]{:S(2)}) collective-permute-start(bf16[64,1024]{1,0:T(8,128)(2,1)S(1)} %collective-permute-done.8.refs_2_), channel_id=1, source_target_pairs={{0,1},{1,0},{2,3},{3,2},{4,5},{5,4},{6,7},{7,6},{8,9},{9,8},{10,11... | collective-permute-start | bytes 393224 | tf_op jit(solution)/shard_map/ppermute | solution.py:214
  34.4 1.3 %collective-permute-start.11 = (bf16[64,1024]{1,0:T(8,128)(2,1)S(1)}, bf16[64,1024]{1,0:T(8,128)(2,1)S(1)}, u32[]{:S(2)}, u32[]{:S(2)}) collective-permute-start(bf16[64,1024]{1,0:T(8,128)(2,1)S(1)} %collective-permute-done.7.refs_1_), channel_id=1, source_target_pairs={{0,1},{1,0},{2,3},{3,2},{4,5},{5,4},{6,7},{7,6},{8,9},{9,8},{10,11... | collective-permute-start | bytes 393224 | tf_op jit(solution)/shard_map/ppermute | solution.py:214
  38.6 7.7 %collective-permute-start.15 = (bf16[72,1024]{1,0:T(8,128)(2,1)S(1)}, bf16[72,1024]{1,0:T(8,128)(2,1)S(1)}, u32[]{:S(2)}, u32[]{:S(2)}) collective-permute-start(bf16[72,1024]{1,0:T(8,128)(2,1)S(1)} %get-tuple-element.33), channel_id=1, source_target_pairs={{0,24},{8,16},{16,8},{24,0},{1,25},{9,17},{17,9},{25,1},{2,26},{10... | collective-permute-start | bytes 442376 | tf_op jit(solution)/shard_map/ppermute | solution.py:217
  40.5 8.1 %collective-permute-start.16 = (bf16[72,1024]{1,0:T(8,128)(2,1)S(1)}, bf16[72,1024]{1,0:T(8,128)(2,1)S(1)}, u32[]{:S(2)}, u32[]{:S(2)}) collective-permute-start(bf16[72,1024]{1,0:T(8,128)(2,1)S(1)} %get-tuple-element.34), channel_id=1, source_target_pairs={{0,16},{8,24},{16,0},{24,8},{1,17},{9,25},{17,1},{25,9},{2,18},{10... | collective-permute-start | bytes 442376 | tf_op jit(solution)/shard_map/ppermute | solution.py:217
  41.1 7.5 %collective-permute-start.17 = (bf16[72,1024]{1,0:T(8,128)(2,1)S(1)}, bf16[72,1024]{1,0:T(8,128)(2,1)S(1)}, u32[]{:S(2)}, u32[]{:S(2)}) collective-permute-start(bf16[72,1024]{1,0:T(8,128)(2,1)S(1)} %get-tuple-element.35), channel_id=1, source_target_pairs={{0,8},{8,0},{16,24},{24,16},{1,9},{9,1},{17,25},{25,17},{2,10},{10... | collective-permute-start | bytes 442376 | tf_op jit(solution)/shard_map/ppermute | solution.py:217
  48.7 8.7 %collective-permute-start.18 = (bf16[72,1024]{1,0:T(8,128)(2,1)S(1)}, bf16[72,1024]{1,0:T(8,128)(2,1)S(1)}, u32[]{:S(2)}, u32[]{:S(2)}) collective-permute-start(bf16[72,1024]{1,0:T(8,128)(2,1)S(1)} %get-tuple-element.37), channel_id=1, source_target_pairs={{0,6},{1,7},{2,4},{3,5},{4,2},{5,3},{6,0},{7,1},{8,14},{9,15},{10,... | collective-permute-start | bytes 442376 | tf_op jit(solution)/shard_map/ppermute | solution.py:220
  52.4 12.7 %collective-permute-start.19 = (bf16[72,1024]{1,0:T(8,128)(2,1)S(1)}, bf16[72,1024]{1,0:T(8,128)(2,1)S(1)}, u32[]{:S(2)}, u32[]{:S(2)}) collective-permute-start(bf16[72,1024]{1,0:T(8,128)(2,1)S(1)} %get-tuple-element.38), channel_id=1, source_target_pairs={{0,4},{1,5},{2,6},{3,7},{4,0},{5,1},{6,2},{7,3},{8,12},{9,13},{10,... | collective-permute-start | bytes 442376 | tf_op jit(solution)/shard_map/ppermute | solution.py:220
  52.4 12.7 %collective-permute-start.20 = (bf16[72,1024]{1,0:T(8,128)(2,1)S(1)}, bf16[72,1024]{1,0:T(8,128)(2,1)S(1)}, u32[]{:S(2)}, u32[]{:S(2)}) collective-permute-start(bf16[72,1024]{1,0:T(8,128)(2,1)S(1)} %get-tuple-element.39), channel_id=1, source_target_pairs={{0,2},{1,3},{2,0},{3,1},{4,6},{5,7},{6,4},{7,5},{8,10},{9,11},{10,... | collective-permute-start | bytes 442376 | tf_op jit(solution)/shard_map/ppermute | solution.py:220
  65.1 1.3 %collective-permute-start.21 = (bf16[64,512]{1,0:T(8,128)(2,1)S(1)}, bf16[64,512]{1,0:T(8,128)(2,1)S(1)}, u32[]{:S(2)}, u32[]{:S(2)}) collective-permute-start(bf16[64,512]{1,0:T(8,128)(2,1)S(1)} %get-tuple-element.41), channel_id=1, source_target_pairs={{0,1},{1,0},{2,3},{3,2},{4,5},{5,4},{6,7},{7,6},{8,9},{9,8},{10,11... | collective-permute-start | bytes 196616 | tf_op jit(solution)/shard_map/ppermute | solution.py:214

commit v5 on v4

--- a/solution.py
+++ b/solution.py
@@ -23,8 +23,8 @@
     return pl.BlockSpec(memory_space=pltpu.SMEM)
 
 
-def way(steps):
-    return [0] + list(range(steps - 1, 0, -1))
+def partners(core):
+    return [0, 2 - core, 1 + core, 3]
 
 
 def place():
@@ -37,38 +37,44 @@
     out[...] = jnp.concatenate([ref[...] for ref in refs[:-1]], axis=1)
 
 
-def project_kernel(steps, parts_of, *refs):
-    blocks, (new, own, other), refs = refs[:steps], refs[steps : steps + 3], refs[steps + 3 :]
-    outs, inputs = refs[:steps], refs[steps]
-    rows = blocks[0].shape[0]
+def project_kernel(parts_of, *refs):
+    blocks, (new, own, other), refs = refs[:4], refs[4:7], refs[7:]
+    (held, new_held), outs, inputs = refs[:2], refs[2:5], refs[5]
+    rows = held.shape[0]
     count = new.shape[0]
-    tail = steps * rows
+    pad = new_held.shape[0]
+    tail = len(blocks) * rows
     for step, block in enumerate(blocks):
         inputs[step * rows : (step + 1) * rows, :] = block[...]
     inputs[tail:, :] = jnp.zeros_like(inputs[tail:, :])
     inputs[tail : tail + count, :] = new[...]
     x = inputs[...]
-    pad = outs[0].shape[0] - rows
     column = 0
     for start, stop in parts_of:
         weight = jnp.concatenate([own[:, start:stop], other[:, start:stop]], axis=1)
         part = jnp.dot(x, weight, preferred_element_type=jnp.float32)
         to = slice(column, column + weight.shape[1])
-        for step, out in enumerate(outs):
+        held[:, to] = part[:rows]
+        news = part[tail : tail + pad].astype(new_held.dtype)
+        new_held[:, to] = news
+        for step, out in enumerate(outs, 1):
             out[:rows, to] = part[step * rows : (step + 1) * rows].astype(out.dtype)
-            out[rows:, to] = part[tail : tail + pad].astype(out.dtype)
+            out[rows:, to] = news
         column += weight.shape[1]
 
 
-def add_kernel(steps, *refs):
-    parts, (held, new) = refs[:steps], refs[steps:]
+def add_kernel(own, new_own, first, second, both, held, keyval, new):
     rows = held.shape[0]
-    total = parts[0][...]
-    for part in parts[1:]:
-        total = total + part[...].astype(jnp.float32)
-    total = total.astype(jnp.bfloat16)
-    held[...] = total[:rows]
-    new[...] = total[rows:]
+
+    def total(own, at):
+        parts = [own[...].astype(jnp.float32)]
+        parts += [ref[at, :].astype(jnp.float32) for ref in (first, second, both)]
+        return ((parts[0] + parts[1]) + (parts[2] + parts[3])).astype(held.dtype)
+
+    sums = total(own, slice(0, rows))
+    held[...] = sums
+    keyval[...] = sums[:, held.shape[1] - keyval.shape[1] :]
+    new[...] = total(new_own, slice(rows, None))
 
 
 def request_of(position, ends):
@@ -78,61 +84,64 @@
     return found
 
 
-def attend_kernel(steps, count, scale, block_map, lengths, *refs):
-    mine, refs = refs[:steps], refs[steps:]
-    theirs, refs = refs[:steps], refs[steps:]
-    new, w_own, w_other = refs[:3]
-    outs, (q_all, key_all, value_all, attended) = refs[3 : 3 + steps], refs[3 + steps :]
-    rows = mine[0].shape[0]
+def attend_kernel(count, scale, block_map, lengths, *refs):
+    mine, theirs, refs = refs[:4], refs[4:8], refs[8:]
+    new, columns, refs = refs[0], (refs[1:3], refs[3:5]), refs[5:]
+    keep, send, q_all, key_all, value_all, attended = refs
+    steps = len(mine)
+    rows, features = mine[0].shape
     q_width, kv_width = q_all.shape[1], key_all.shape[1]
     head = HEAD_SIZE
     groups = kv_width // head
     per_group = q_width // kv_width
     pad = new.shape[0]
-    tail = steps * rows
+    tail = 2 * rows
     q_rows = q_all.shape[0]
     k_rows = key_all.shape[0]
-    k_tail = 2 * tail
+    k_tail = 2 * steps * rows
     half = kv_width // 2
-    k_at, v_at = q_width, q_width + kv_width
     c, _, k = place()
 
-    q_all[tail:, :] = jnp.zeros_like(q_all[tail:, :])
     key_all[k_tail:, :] = jnp.zeros_like(key_all[k_tail:, :])
     value_all[k_tail:, :] = jnp.zeros_like(value_all[k_tail:, :])
-    for step in range(steps):
-        at = slice(step * rows, (step + 1) * rows)
-        q_all[at, :] = mine[step][:, :q_width]
-        key_all[at, :] = mine[step][:, k_at:v_at]
-        value_all[at, :] = mine[step][:, v_at:]
-        at = slice(tail + step * rows, tail + (step + 1) * rows)
-        key_all[at, :half] = theirs[step][:, k_at + half : v_at]
-        key_all[at, half:] = theirs[step][:, k_at : k_at + half]
-        value_all[at, :half] = theirs[step][:, v_at + half :]
-        value_all[at, half:] = theirs[step][:, v_at : v_at + half]
+    for number in range(steps):
+        at = slice(number * rows, (number + 1) * rows)
+        v_at = mine[number].shape[1] - kv_width
+        key_all[at, :] = mine[number][:, v_at - kv_width : v_at]
+        value_all[at, :] = mine[number][:, v_at:]
+        at = slice((steps + number) * rows, (steps + number + 1) * rows)
+        v_at = theirs[number].shape[1] - kv_width
+        k_at = v_at - kv_width
+        key_all[at, :half] = theirs[number][:, k_at + half : v_at]
+        key_all[at, half:] = theirs[number][:, k_at : k_at + half]
+        value_all[at, :half] = theirs[number][:, v_at + half :]
+        value_all[at, half:] = theirs[number][:, v_at : v_at + half]
+    key_all[k_tail : k_tail + pad, :] = new[:, q_width : q_width + kv_width]
+    value_all[k_tail : k_tail + pad, :] = new[:, q_width + kv_width :]
+    q_all[tail:, :] = jnp.zeros_like(q_all[tail:, :])
+    for number in range(2):
+        q_all[number * rows : (number + 1) * rows, :] = mine[number][:, :q_width]
     q_all[tail : tail + pad, :] = new[:, :q_width]
-    key_all[k_tail : k_tail + pad, :] = new[:, k_at:v_at]
-    value_all[k_tail : k_tail + pad, :] = new[:, v_at:]
 
     ends, total = [], 0
     for request in range(count):
         total = total + lengths[request]
         ends.append(total)
 
-    def labels(shape, axis, halves):
+    def labels(shape, axis, held):
         index = lax.broadcasted_iota(jnp.int32, shape, axis)
         position = jnp.zeros(shape, jnp.int32)
-        for number in range(halves * steps):
-            held = 2 * (c ^ way(steps)[number % steps]) + (k ^ (number // steps))
+        for number, block in enumerate(held):
             inside = (index >= number * rows) & (index < (number + 1) * rows)
-            position = jnp.where(inside, block_map[held] * rows + index - number * rows, position)
-        last = halves * tail
+            position = jnp.where(inside, block_map[block] * rows + index - number * rows, position)
+        last = len(held) * rows
         is_new = index >= last
         request = jnp.where(is_new, index - last, request_of(position, ends))
         return jnp.where(is_new, LAST, position), request
 
-    q_position, q_request = labels((q_rows, 1), 0, 1)
-    k_position, k_request = labels((1, k_rows), 1, 2)
+    held = [2 * (c ^ mask) + core for core in (k, 1 - k) for mask in partners(core)]
+    q_position, q_request = labels((q_rows, 1), 0, held[:2])
+    k_position, k_request = labels((1, k_rows), 1, held)
     allowed = (q_request == k_request) & (k_position <= q_position)
 
     for group in range(groups):
@@ -154,36 +163,39 @@
             )
             attended[:, at : at + head] = (mixed / denom).astype(jnp.bfloat16)
 
-    rows_own = w_own.shape[0]
-    result = (
-        jnp.dot(attended[:, :rows_own], w_own[...], preferred_element_type=jnp.float32)
-        + jnp.dot(attended[:, rows_own:], w_other[...], preferred_element_type=jnp.float32)
-    ).astype(jnp.bfloat16)
-    for step, out in enumerate(outs):
-        out[:rows, :] = result[step * rows : (step + 1) * rows]
-        out[rows:, :] = result[tail : tail + pad]
-
-
-def relay_kernel(steps, *refs):
-    blocks, outs = refs[:steps], refs[steps:]
-    c, z, _ = place()
-    for slot, out in zip(way(steps), outs):
-        for step, block in zip(way(steps), blocks):
-
-            @pl.when((c ^ z ^ slot) == step)
-            def _(out=out, block=block):
-                out[...] = block[...]
-
-
-def sum_kernel(steps, *refs):
-    parts, (keep, send) = refs[:steps], refs[steps:]
+    for number, (w_own, w_other) in enumerate(columns):
+        rows_own = w_own.shape[0]
+        result = (
+            jnp.dot(attended[:, :rows_own], w_own[...], preferred_element_type=jnp.float32)
+            + jnp.dot(attended[:, rows_own:], w_other[...], preferred_element_type=jnp.float32)
+        ).astype(jnp.bfloat16)
+        for out, block in ((keep, 0), (send, 1)):
+            at = number * (rows + pad)
+            out[at : at + rows, :] = result[block * rows : (block + 1) * rows]
+            out[at + rows : at + rows + pad, :] = result[tail : tail + pad]
+
+
+def relay_kernel(keep, got, *outs):
+    c, z, k = place()
+    rows = outs[0].shape[0]
+    blocks = [(ref, number) for ref in (keep, got) for number in range(2)]
+    masks = [partners(k)[i] for i in (0, 2, 1, 3)]
+    for slot, out in enumerate(outs):
+        for mask, (ref, number) in zip(masks, blocks):
+
+            @pl.when((c ^ z ^ slot) == mask)
+            def _(out=out, ref=ref, number=number):
+                out[...] = ref[number * rows : (number + 1) * rows, :]
+
+
+def sum_kernel(*refs):
+    parts, (keep, send) = refs[:-2], refs[-2:]
     width = keep.shape[1]
     rows = send.shape[0]
     _, _, k = place()
     for out, core in ((keep, k), (send, 1 - k)):
         column = pl.ds(pl.multiple_of(core * width, width), width)
         terms = [part[:, column].astype(jnp.float32) for part in parts]
-        terms = [terms[way(steps).index(m)] for m in range(steps)]
         while len(terms) > 1:
             terms = [a + b for a, b in zip(terms[::2], terms[1::2])]
         out[...] = terms[0][: out.shape[0]].astype(out.dtype)
@@ -209,23 +221,23 @@
     kv_width = 2 * key_matrix.shape[1]
     features = q_width + 2 * kv_width
     out_width = w_out.shape[1]
+    devices = [divmod(source, tp) for source in range(steps * tp)]
 
     def to_core(value):
         return lax.ppermute(value, "tp", [(i, i ^ 1) for i in range(tp)])
 
-    def to_ctx(value, step):
-        return lax.ppermute(value, "ctx", [(i, i ^ step) for i in range(steps)])
-
     def to_chip(value, step):
         return lax.ppermute(value, "tp", [(i, i ^ (2 * step)) for i in range(tp)])
 
-    def all_to_ctx(values):
-        values = list(values)
-        return values[:1] + [to_ctx(value, m) for value, m in zip(values[1:], way(steps)[1:])]
-
-    def all_to_chip(values):
-        values = list(values)
-        return values[:1] + [to_chip(value, m) for value, m in zip(values[1:], way(steps)[1:])]
+    def to_partner(value, number, swap=0):
+        pairs = [
+            (c * tp + t, (c ^ partners((t ^ swap) % 2)[number]) * tp + (t ^ swap))
+            for c, t in devices
+        ]
+        return lax.ppermute(value, ("ctx", "tp"), pairs)
+
+    def to_partners(values):
+        return [to_partner(value, number) for number, value in enumerate(values, 1)]
 
     def call(kernel, name, inputs, shapes, scratch=(), spaces=None):
         return pl.pallas_call(
@@ -240,10 +252,11 @@
 
     c, _, k = place()
     sent = [
-        lax.dynamic_slice(tokens, (k * rows, (c ^ m) * depth), (rows, depth)) for m in way(steps)
+        lax.dynamic_slice(tokens, (k * rows, (c ^ mask) * depth), (rows, depth))
+        for mask in partners(k)
     ]
     new_columns = lax.dynamic_slice_in_dim(new_token_states, c * depth, depth, 1)
-    blocks = all_to_ctx(sent)
+    blocks = [sent[0]] + to_partners(sent[1:])
     *weights, _ = lax.optimization_barrier((w_query, key_matrix, value_matrix, sent[1]))
     (own,) = call(pack_kernel, "pack_weights", weights, [((depth, features // 2), bf16)])
     other = to_core(own)
@@ -251,52 +264,52 @@
     part_shape = (rows + pad, features)
     x_rows = -(-(steps * rows + pad) // 16) * 16
     edges = [0, q_width // 2, (q_width + kv_width) // 2, features // 2]
-    parts = call(
-        functools.partial(project_kernel, steps, list(zip(edges, edges[1:]))),
+    own_part, new_part, *parts = call(
+        functools.partial(project_kernel, list(zip(edges, edges[1:]))),
         "project",
         (*blocks, new_columns, own, other),
-        [(part_shape, f32)] + [(part_shape, bf16)] * (steps - 1),
+        [((rows, features), f32), ((pad, features), bf16)] + [(part_shape, bf16)] * (steps - 1),
         [pltpu.VMEM((x_rows, depth), bf16)],
     )
 
-    w_out_late, _ = lax.optimization_barrier((w_out, parts[0]))
-    parts = all_to_ctx(parts)
-    w_other = to_core(w_out_late)
-    held, new = call(
-        functools.partial(add_kernel, steps),
+    w_second = to_partner(w_out, 2)
+    w_out_later, _ = lax.optimization_barrier((w_out, new_part))
+    w_second_other = to_partner(w_out_later, 2, 1)
+
+    held, keyval, new = call(
+        add_kernel,
         "add_parts",
-        parts,
-        [((rows, features), bf16), ((pad, features), bf16)],
-    )
-
-    mine = all_to_ctx([held] * steps)
-    theirs = [to_core(value) for value in mine]
-
+        (own_part, new_part, *to_partners(parts)),
+        [((rows, features), bf16), ((rows, 2 * kv_width), bf16), ((pad, features), bf16)],
+    )
+    w_out_last, _, w_second = lax.optimization_barrier((w_out, new, w_second))
+    w_other = to_core(w_out_last)
+
+    mine = [held] + to_partners([held, keyval, keyval])
+    theirs = [to_core(value) for value in [keyval] + mine[1:]]
+
+    q_rows = -(-(2 * rows + pad) // 16) * 16
     k_rows = -(-(2 * steps * rows + pad) // 128) * 128
-    outs = call(
-        functools.partial(attend_kernel, steps, count, 1.0 / math.sqrt(HEAD_SIZE)),
+    block = (rows + pad, out_width)
+    keep, send = call(
+        functools.partial(attend_kernel, count, 1.0 / math.sqrt(HEAD_SIZE)),
         "attend",
-        (block_map, lengths, *mine, *theirs, new, w_out, w_other),
-        [((rows + pad, out_width), bf16)] * steps,
+        (block_map, lengths, *mine, *theirs, new, w_out, w_other, w_second, w_second_other),
+        [((2 * block[0], out_width), bf16)] * 2,
         [
-            pltpu.VMEM((x_rows, q_width), bf16),
+            pltpu.VMEM((q_rows, q_width), bf16),
             pltpu.VMEM((k_rows, kv_width), bf16),
             pltpu.VMEM((k_rows, kv_width), bf16),
-            pltpu.VMEM((x_rows, q_width), bf16),
+            pltpu.VMEM((q_rows, q_width), bf16),
         ],
-        [smem()] * 2 + [vmem()] * (2 * steps + 3),
-    )
-
-    arrived = all_to_ctx(outs)
-    slots = call(
-        functools.partial(relay_kernel, steps),
-        "relay",
-        arrived,
-        [((rows + pad, out_width), bf16)] * steps,
-    )
-    slots = all_to_chip(slots)
+        [smem()] * 2 + [vmem()] * (2 * steps + 5),
+    )
+
+    got = to_partner(send, 1)
+    slots = call(relay_kernel, "relay", (keep, got), [(block, bf16)] * steps)
+    slots = [slots[0]] + [to_chip(slot, step) for step, slot in enumerate(slots[1:], 1)]
     keep, send = call(
-        functools.partial(sum_kernel, steps),
+        sum_kernel,
         "sum_heads",
         slots,
         [((rows + pad, out_width // 2), bf16), ((rows, out_width // 2), bf16)],
@@ -495,7 +508,7 @@
     steps, tp = mesh.shape["ctx"], mesh.shape["tp"]
 
     def on_device(tokens, *rest):
-        small = tp == 2 * steps and steps & (steps - 1) == 0 and tokens.shape[0] * steps <= 1024
+        small = steps == 4 and tp == 8 and tokens.shape[0] * steps <= 1024
         if small:
             return on_device_small(steps, tp, tokens, *rest)
         return on_device_large(tokens, *rest)

time: 67.3 us -> 66.9 us (level)
  waiting for transfers between devices: 40.3 us -> 39.5 us
    ppermute x7, starting transfers between devices: 0.6 us -> 1.68 us  [to_core(): return lax.ppermute(value, 'tp', [(i, i ^ 1) for i in range(tp)])]
    ppermute x3, waiting for transfers between devices: 11.9 us -> 11 us  [to_chip(): return lax.ppermute(value, 'tp', [(i, i ^ 2 * step) for i in range(tp)])]
  transfers between devices with their start and end apart: 22 -> 22, of which waited for: 14 -> 13; matrix products, arithmetic and copies ran while one was open for 0% -> 0% of each run, Pallas kernels for 0% -> 1%
where the time goes in v5:
time: 66.9 us; the launch traced here: 66.7 us
  waiting for transfers between devices  39.5 us (59%)
  starting transfers between devices  20.3 us (30%)
  Pallas kernels  4.24 us (6%)
  local copies, waits for them, and re-layouts  1.87 us (3%)
  between operations  0.82 us (1%)
    ppermute x12, waiting for transfers between devices, to_partner(): return lax.ppermute(value, ('ctx', 'tp'), pairs)  26.3 us
    ppermute x12, starting transfers between devices, to_partner(): return lax.ppermute(value, ('ctx', 'tp'), pairs)  14.2 us
    ppermute x3, waiting for transfers between devices, to_chip(): return lax.ppermute(value, 'tp', [(i, i ^ 2 * step) for i in range(tp)])  11 us
    ppermute x3, starting transfers between devices, to_chip(): return lax.ppermute(value, 'tp', [(i, i ^ 2 * step) for i in range(tp)])  4.45 us
    pallas_call x7, Pallas kernels, call(): pl.pallas_call(kernel, out_shape=[jax.ShapeDtypeStruct(shape, kind) for s...  4.24 us
    ppermute x7, waiting for transfers between devices, to_core(): return lax.ppermute(value, 'tp', [(i, i ^ 1) for i in range(tp)])  2.15 us
    ppermute x7, starting transfers between devices, to_core(): return lax.ppermute(value, 'tp', [(i, i ^ 1) for i in range(tp)])  1.68 us
  transfers between devices with their start and end apart: 22, of which 13 were waited for; matrix products, arithmetic and copies ran while one was open for 0% of the time, Pallas kernels for 1%

profile of v5, /device:TPU:0, one launch (start us, length us, event | category | flops | bytes accessed | tf_op | source)
XLA Modules:
  0.0 66.7 jit_solution(7477666337088358662)
XLA Ops:
  0.7 1.2 %fusion = (bf16[64,1024]{1,0:T(8,128)(2,1)S(1)}, bf16[64,1024]{1,0:T(8,128)(2,1)S(1)}, bf16[64,1024]{1,0:T(8,128)(2,1)S(1)}, bf16[64,1024]{1,0:T(8,128)(2,1)S(1)}) fusion(bf16[128,4096]{1,0:T(8,128)(2,1)} %param.8, s32[]{:T(128)S(6)} %select_n.27, s32[]{:T(128)S(6)} %select_n.31, s32[]{:T(128)S(6)} %select_n.29, s32[]{:T(128)S(6)} %select_n.28, s32[]{:T(128)S(6)} %select_n.30), kind=kLoop, calls=%fused_computation.1 | loop fusion | bytes 1048596 | tf_op jit(solution)/shard_map/dynamic_slice | solution.py:255
  2.2 0.5 collective-permute-start.3
  2.7 0.4 copy-done.1
  3.2 2.9 %collective-permute-start.14 = (bf16[256,1024]{1,0:T(8,128)(2,1)S(1)}, bf16[256,1024]{1,0:T(8,128)(2,1)S(1)}, u32[]{:S(2)}, u32[]{:S(2)}) collective-permute-start(bf16[256,1024]{1,0:T(8,128)(2,1)S(1)} %copy-done.1), channel_id=1, source_target_pairs={{0,8},{1,17},{2,10},{3,19},{4,12},{5,21},{6,14},{7,23},{8,0},{9,25... | collective-permute-start | bytes 1572872 | tf_op jit(solution)/shard_map/ppermute | solution.py:237
  6.1 1.5 %collective-permute-start = (bf16[64,1024]{1,0:T(8,128)(2,1)S(1)}, bf16[64,1024]{1,0:T(8,128)(2,1)S(1)}, u32[]{:S(2)}, u32[]{:S(2)}) collective-permute-start(bf16[64,1024]{1,0:T(8,128)(2,1)S(1)} %get-tuple-element.47), channel_id=1, source_target_pairs={{0,16},{1,9},{2,18},{3,11},{4,20},{5,13},{6,22},{7,15},{8,24},{9,1... | collective-permute-start | bytes 393224 | tf_op jit(solution)/shard_map/ppermute | solution.py:237
  7.6 0.5 collective-permute-start.1
  8.2 1.4 %collective-permute-start.2 = (bf16[64,1024]{1,0:T(8,128)(2,1)S(1)}, bf16[64,1024]{1,0:T(8,128)(2,1)S(1)}, u32[]{:S(2)}, u32[]{:S(2)}) collective-permute-start(bf16[64,1024]{1,0:T(8,128)(2,1)S(1)} %get-tuple-element.46), channel_id=1, source_target_pairs={{0,24},{1,25},{2,26},{3,27},{4,28},{5,29},{6,30},{7,31},{8,16},{9,... | collective-permute-start | bytes 393224 | tf_op jit(solution)/shard_map/ppermute | solution.py:237
  9.6 4.3 %collective-permute-done.refs_1_ = bf16[64,1024]{1,0:T(8,128)(2,1)S(1)} collective-permute-done((bf16[64,1024]{1,0:T(8,128)(2,1)S(1)}, bf16[64,1024]{1,0:T(8,128)(2,1)S(1)}, u32[]{:S(2)}, u32[]{:S(2)}) %collective-permute-start) | collective-permute-done | bytes 131104 | tf_op jit(solution)/shard_map/ppermute | solution.py:237
  13.9 3.5 %collective-permute-done.1.refs_2_ = bf16[64,1024]{1,0:T(8,128)(2,1)S(1)} collective-permute-done((bf16[64,1024]{1,0:T(8,128)(2,1)S(1)}, bf16[64,1024]{1,0:T(8,128)(2,1)S(1)}, u32[]{:S(2)}, u32[]{:S(2)}) %collective-permute-start.1) | collective-permute-done | bytes 131104 | tf_op jit(solution)/shard_map/ppermute | solution.py:237
  17.5 1.8 %collective-permute-done.2.refs_3_ = bf16[64,1024]{1,0:T(8,128)(2,1)S(1)} collective-permute-done((bf16[64,1024]{1,0:T(8,128)(2,1)S(1)}, bf16[64,1024]{1,0:T(8,128)(2,1)S(1)}, u32[]{:S(2)}, u32[]{:S(2)}) %collective-permute-start.2) | collective-permute-done | bytes 131104 | tf_op jit(solution)/shard_map/ppermute | solution.py:237
  19.2 0.7 %project.1 = (f32[64,1024]{1,0:T(8,128)S(1)}, bf16[8,1024]{1,0:T(8,128)(2,1)S(1)}, bf16[72,1024]{1,0:T(8,128)(2,1)S(1)}, bf16[72,1024]{1,0:T(8,128)(2,1)S(1)}, bf16[72,1024]{1,0:T(8,128)(2,1)S(1)}) custom-call(bf16[64,1024]{1,0:T(8,128)(2,1)S(1)} %get-tuple-element.48.refs_0_, bf16[64,1024]{1,0:T(8,128)(2,1)S(1)} %collective-permute-done.refs_1_, ...), custom_call_target="tpu_custom_call" | custom-call | tf_op jit(solution)/shard_map/project/pallas_call | solution.py:243
  20.0 1.2 %collective-permute-start.4 = (bf16[72,1024]{1,0:T(8,128)(2,1)S(1)}, bf16[72,1024]{1,0:T(8,128)(2,1)S(1)}, u32[]{:S(2)}, u32[]{:S(2)}) collective-permute-start(bf16[72,1024]{1,0:T(8,128)(2,1)S(1)} %get-tuple-element.29), channel_id=1, source_target_pairs={{0,16},{1,9},{2,18},{3,11},{4,20},{5,13},{6,22},{7,15},{8,24},{9,1... | collective-permute-start | bytes 442376 | tf_op jit(solution)/shard_map/ppermute | solution.py:237
  21.2 2.0 %collective-permute-start.5 = (bf16[72,1024]{1,0:T(8,128)(2,1)S(1)}, bf16[72,1024]{1,0:T(8,128)(2,1)S(1)}, u32[]{:S(2)}, u32[]{:S(2)}) collective-permute-start(bf16[72,1024]{1,0:T(8,128)(2,1)S(1)} %get-tuple-element.30), channel_id=1, source_target_pairs={{0,8},{1,17},{2,10},{3,19},{4,12},{5,21},{6,14},{7,23},{8,0},{9,25... | collective-permute-start | bytes 442376 | tf_op jit(solution)/shard_map/ppermute | solution.py:237
  23.5 3.2 %collective-permute-done.4.first = bf16[72,1024]{1,0:T(8,128)(2,1)S(1)} collective-permute-done((bf16[72,1024]{1,0:T(8,128)(2,1)S(1)}, bf16[72,1024]{1,0:T(8,128)(2,1)S(1)}, u32[]{:S(2)}, u32[]{:S(2)}) %collective-permute-start.4) | collective-permute-done | bytes 147488 | tf_op jit(solution)/shard_map/ppermute | solution.py:237
  26.8 4.0 %collective-permute-done.6.both = bf16[72,1024]{1,0:T(8,128)(2,1)S(1)} collective-permute-done((bf16[72,1024]{1,0:T(8,128)(2,1)S(1)}, bf16[72,1024]{1,0:T(8,128)(2,1)S(1)}, u32[]{:S(2)}, u32[]{:S(2)}) %collective-permute-start.6) | collective-permute-done | bytes 147488 | tf_op jit(solution)/shard_map/ppermute | solution.py:237
  30.9 0.7 %collective-permute-start.7 = (bf16[64,1024]{1,0:T(8,128)(2,1)S(1)}, bf16[64,1024]{1,0:T(8,128)(2,1)S(1)}, u32[]{:S(2)}, u32[]{:S(2)}) collective-permute-start(bf16[64,1024]{1,0:T(8,128)(2,1)S(1)} %get-tuple-element.32.refs_0_), channel_id=1, source_target_pairs={{0,16},{1,9},{2,18},{3,11},{4,20},{5,13},{6,22},{7,15},{8,24},{9,1... | collective-permute-start | bytes 393224 | tf_op jit(solution)/shard_map/ppermute | solution.py:237
  31.7 1.5 %collective-permute-start.8 = (bf16[64,512]{1,0:T(8,128)(2,1)S(1)}, bf16[64,512]{1,0:T(8,128)(2,1)S(1)}, u32[]{:S(2)}, u32[]{:S(2)}) collective-permute-start(bf16[64,512]{1,0:T(8,128)(2,1)S(1)} %get-tuple-element.33), channel_id=1, source_target_pairs={{0,8},{1,17},{2,10},{3,19},{4,12},{5,21},{6,14},{7,23},{8,0},{9,25... | collective-permute-start | bytes 196616 | tf_op jit(solution)/shard_map/ppermute | solution.py:237
  33.2 1.3 %collective-permute-start.9 = (bf16[64,512]{1,0:T(8,128)(2,1)S(1)}, bf16[64,512]{1,0:T(8,128)(2,1)S(1)}, u32[]{:S(2)}, u32[]{:S(2)}) collective-permute-start(bf16[64,512]{1,0:T(8,128)(2,1)S(1)} %get-tuple-element.33), channel_id=1, source_target_pairs={{0,24},{1,25},{2,26},{3,27},{4,28},{5,29},{6,30},{7,31},{8,16},{9,... | collective-permute-start | bytes 196616 | tf_op jit(solution)/shard_map/ppermute | solution.py:237
  34.5 2.2 %collective-permute-done.8.refs_2_ = bf16[64,512]{1,0:T(8,128)(2,1)S(1)} collective-permute-done((bf16[64,512]{1,0:T(8,128)(2,1)S(1)}, bf16[64,512]{1,0:T(8,128)(2,1)S(1)}, u32[]{:S(2)}, u32[]{:S(2)}) %collective-permute-start.8) | collective-permute-done | bytes 65568 | tf_op jit(solution)/shard_map/ppermute | solution.py:237
  36.7 0.5 collective-permute-start.11
  37.2 1.2 %collective-permute-done.9.refs_3_ = bf16[64,512]{1,0:T(8,128)(2,1)S(1)} collective-permute-done((bf16[64,512]{1,0:T(8,128)(2,1)S(1)}, bf16[64,512]{1,0:T(8,128)(2,1)S(1)}, u32[]{:S(2)}, u32[]{:S(2)}) %collective-permute-start.9) | collective-permute-done | bytes 65568 | tf_op jit(solution)/shard_map/ppermute | solution.py:237
  38.4 0.5 collective-permute-start.13
  38.9 0.7 %collective-permute-done.12.refs_6_ = bf16[64,512]{1,0:T(8,128)(2,1)S(1)} collective-permute-done((bf16[64,512]{1,0:T(8,128)(2,1)S(1)}, bf16[64,512]{1,0:T(8,128)(2,1)S(1)}, u32[]{:S(2)}, u32[]{:S(2)}) %collective-permute-start.12) | collective-permute-done | bytes 65568 | tf_op jit(solution)/shard_map/ppermute | solution.py:227
  39.8 2.5 %attend.1 = (bf16[144,1024]{1,0:T(8,128)(2,1)S(1)}, bf16[144,1024]{1,0:T(8,128)(2,1)S(1)}) custom-call(s32[8]{0:T(128)S(1)} %copy-done.5, s32[4]{0:T(128)S(1)} %copy-done.6, bf16[64,1024]{1,0:T(8,128)(2,1)S(1)} %get-tuple-element.32.refs_0_, bf16[64,1024]{1,0:T(8,128)(2,1)S(1)} %collective-permute-done.7.refs_1_, ...), custom_call_target="tpu_custom_call" | custom-call | tf_op jit(solution)/shard_map/attend/pallas_call | solution.py:243
  42.3 0.7 collective-permute-start.17
  43.0 6.1 %collective-permute-done.17.got = bf16[144,1024]{1,0:T(8,128)(2,1)S(1)} collective-permute-done((bf16[144,1024]{1,0:T(8,128)(2,1)S(1)}, bf16[144,1024]{1,0:T(8,128)(2,1)S(1)}, u32[]{:S(2)}, u32[]{:S(2)}) %collective-permute-start.17) | collective-permute-done | bytes 294944 | tf_op jit(solution)/shard_map/ppermute | solution.py:237
  49.2 1.6 %collective-permute-start.18 = (bf16[72,1024]{1,0:T(8,128)(2,1)S(1)}, bf16[72,1024]{1,0:T(8,128)(2,1)S(1)}, u32[]{:S(2)}, u32[]{:S(2)}) collective-permute-start(bf16[72,1024]{1,0:T(8,128)(2,1)S(1)} %get-tuple-element.41), channel_id=1, source_target_pairs={{0,2},{1,3},{2,0},{3,1},{4,6},{5,7},{6,4},{7,5},{8,10},{9,11},{10,... | collective-permute-start | bytes 442376 | tf_op jit(solution)/shard_map/ppermute | solution.py:230
  50.9 2.6 %collective-permute-start.19 = (bf16[72,1024]{1,0:T(8,128)(2,1)S(1)}, bf16[72,1024]{1,0:T(8,128)(2,1)S(1)}, u32[]{:S(2)}, u32[]{:S(2)}) collective-permute-start(bf16[72,1024]{1,0:T(8,128)(2,1)S(1)} %get-tuple-element.42), channel_id=1, source_target_pairs={{0,4},{1,5},{2,6},{3,7},{4,0},{5,1},{6,2},{7,3},{8,12},{9,13},{10,... | collective-permute-start | bytes 442376 | tf_op jit(solution)/shard_map/ppermute | solution.py:230
  53.7 2.7 %collective-permute-done.18.refs_1_ = bf16[72,1024]{1,0:T(8,128)(2,1)S(1)} collective-permute-done((bf16[72,1024]{1,0:T(8,128)(2,1)S(1)}, bf16[72,1024]{1,0:T(8,128)(2,1)S(1)}, u32[]{:S(2)}, u32[]{:S(2)}) %collective-permute-start.18) | collective-permute-done | bytes 147488 | tf_op jit(solution)/shard_map/ppermute | solution.py:230
  56.3 8.3 %collective-permute-done.19.refs_2_ = bf16[72,1024]{1,0:T(8,128)(2,1)S(1)} collective-permute-done((bf16[72,1024]{1,0:T(8,128)(2,1)S(1)}, bf16[72,1024]{1,0:T(8,128)(2,1)S(1)}, u32[]{:S(2)}, u32[]{:S(2)}) %collective-permute-start.19) | collective-permute-done | bytes 147488 | tf_op jit(solution)/shard_map/ppermute | solution.py:230
  64.8 1.2 %collective-permute-done.21.other = bf16[64,512]{1,0:T(8,128)(2,1)S(1)} collective-permute-done((bf16[64,512]{1,0:T(8,128)(2,1)S(1)}, bf16[64,512]{1,0:T(8,128)(2,1)S(1)}, u32[]{:S(2)}, u32[]{:S(2)}) %collective-permute-start.21) | collective-permute-done | bytes 65568 | tf_op jit(solution)/shard_map/ppermute | solution.py:227
  66.1 0.7 %finish.1 = (bf16[128,512]{1,0:T(8,128)(2,1)}, bf16[4,512]{1,0:T(4,128)(2,1)}) custom-call(bf16[72,512]{1,0:T(8,128)(2,1)S(1)} %get-tuple-element.44.keep, bf16[64,512]{1,0:T(8,128)(2,1)S(1)} %collective-permute-done.21.other), custom_call_target="tpu_custom_call" | custom-call | tf_op jit(solution)/shard_map/finish/pallas_call | solution.py:243
  (35 shorter events, 1.5 us)
Async XLA Ops:
  0.6 9.0 %copy-start = (bf16[4,4096]{1,0:T(4,128)(2,1)S(1)}, bf16[4,4096]{1,0:T(4,128)(2,1)}, u32[]{:S(2)}) copy-start(bf16[4,4096]{1,0:T(4,128)(2,1)} %param.9) | copy-start | bytes 98308
  0.7 1.3 %copy-start.2 = (bf16[1024,256]{1,0:T(8,128)(2,1)S(1)}, bf16[1024,256]{1,0:T(8,128)(2,1)}, u32[]{:S(2)}) copy-start(bf16[1024,256]{1,0:T(8,128)(2,1)} %refs_0_) | copy-start | bytes 1572868
  0.7 1.4 %copy-start.3 = (bf16[1024,128]{1,0:T(8,128)(2,1)S(1)}, bf16[1024,128]{1,0:T(8,128)(2,1)}, u32[]{:S(2)}) copy-start(bf16[1024,128]{1,0:T(8,128)(2,1)} %refs_1_) | copy-start | bytes 786436
  0.7 1.4 %copy-start.4 = (bf16[1024,128]{1,0:T(8,128)(2,1)S(1)}, bf16[1024,128]{1,0:T(8,128)(2,1)}, u32[]{:S(2)}) copy-start(bf16[1024,128]{1,0:T(8,128)(2,1)} %refs_2_) | copy-start | bytes 786436
  2.1 1.0 %copy-start.1 = (bf16[256,1024]{1,0:T(8,128)(2,1)S(1)}, bf16[256,1024]{1,0:T(8,128)(2,1)}, u32[]{:S(2)}) copy-start(bf16[256,1024]{1,0:T(8,128)(2,1)} %refs_9_.1) | copy-start | bytes 1572868
  2.2 17.0 %collective-permute-start.3 = (bf16[1024,512]{1,0:T(8,128)(2,1)S(1)}, bf16[1024,512]{1,0:T(8,128)(2,1)S(1)}, u32[]{:S(2)}, u32[]{:S(2)}) collective-permute-start(bf16[1024,512]{1,0:T(8,128)(2,1)S(1)} %pack_weights.1.refs_5_), channel_id=1, source_target_pairs={{0,1},{1,0},{2,3},{3,2},{4,5},{5,4},{6,7},{7,6},{8,9},{9,8},{10,11... | collective-permute-start | bytes 3145736 | tf_op jit(solution)/shard_map/ppermute | solution.py:227
  3.2 27.7 %collective-permute-start.14 = (bf16[256,1024]{1,0:T(8,128)(2,1)S(1)}, bf16[256,1024]{1,0:T(8,128)(2,1)S(1)}, u32[]{:S(2)}, u32[]{:S(2)}) collective-permute-start(bf16[256,1024]{1,0:T(8,128)(2,1)S(1)} %copy-done.1), channel_id=1, source_target_pairs={{0,8},{1,17},{2,10},{3,19},{4,12},{5,21},{6,14},{7,23},{8,0},{9,25... | collective-permute-start | bytes 1572872 | tf_op jit(solution)/shard_map/ppermute | solution.py:237
  6.1 7.8 %collective-permute-start = (bf16[64,1024]{1,0:T(8,128)(2,1)S(1)}, bf16[64,1024]{1,0:T(8,128)(2,1)S(1)}, u32[]{:S(2)}, u32[]{:S(2)}) collective-permute-start(bf16[64,1024]{1,0:T(8,128)(2,1)S(1)} %get-tuple-element.47), channel_id=1, source_target_pairs={{0,16},{1,9},{2,18},{3,11},{4,20},{5,13},{6,22},{7,15},{8,24},{9,1... | collective-permute-start | bytes 393224 | tf_op jit(solution)/shard_map/ppermute | solution.py:237
  7.6 9.9 %collective-permute-start.1 = (bf16[64,1024]{1,0:T(8,128)(2,1)S(1)}, bf16[64,1024]{1,0:T(8,128)(2,1)S(1)}, u32[]{:S(2)}, u32[]{:S(2)}) collective-permute-start(bf16[64,1024]{1,0:T(8,128)(2,1)S(1)} %get-tuple-element.49), channel_id=1, source_target_pairs={{0,8},{1,17},{2,10},{3,19},{4,12},{5,21},{6,14},{7,23},{8,0},{9,25... | collective-permute-start | bytes 393224 | tf_op jit(solution)/shard_map/ppermute | solution.py:237
  8.2 11.1 %collective-permute-start.2 = (bf16[64,1024]{1,0:T(8,128)(2,1)S(1)}, bf16[64,1024]{1,0:T(8,128)(2,1)S(1)}, u32[]{:S(2)}, u32[]{:S(2)}) collective-permute-start(bf16[64,1024]{1,0:T(8,128)(2,1)S(1)} %get-tuple-element.46), channel_id=1, source_target_pairs={{0,24},{1,25},{2,26},{3,27},{4,28},{5,29},{6,30},{7,31},{8,16},{9,... | collective-permute-start | bytes 393224 | tf_op jit(solution)/shard_map/ppermute | solution.py:237
  20.0 6.8 %collective-permute-start.4 = (bf16[72,1024]{1,0:T(8,128)(2,1)S(1)}, bf16[72,1024]{1,0:T(8,128)(2,1)S(1)}, u32[]{:S(2)}, u32[]{:S(2)}) collective-permute-start(bf16[72,1024]{1,0:T(8,128)(2,1)S(1)} %get-tuple-element.29), channel_id=1, source_target_pairs={{0,16},{1,9},{2,18},{3,11},{4,20},{5,13},{6,22},{7,15},{8,24},{9,1... | collective-permute-start | bytes 442376 | tf_op jit(solution)/shard_map/ppermute | solution.py:237
  21.2 5.6 %collective-permute-start.5 = (bf16[72,1024]{1,0:T(8,128)(2,1)S(1)}, bf16[72,1024]{1,0:T(8,128)(2,1)S(1)}, u32[]{:S(2)}, u32[]{:S(2)}) collective-permute-start(bf16[72,1024]{1,0:T(8,128)(2,1)S(1)} %get-tuple-element.30), channel_id=1, source_target_pairs={{0,8},{1,17},{2,10},{3,19},{4,12},{5,21},{6,14},{7,23},{8,0},{9,25... | collective-permute-start | bytes 442376 | tf_op jit(solution)/shard_map/ppermute | solution.py:237
  23.2 7.6 %collective-permute-start.6 = (bf16[72,1024]{1,0:T(8,128)(2,1)S(1)}, bf16[72,1024]{1,0:T(8,128)(2,1)S(1)}, u32[]{:S(2)}, u32[]{:S(2)}) collective-permute-start(bf16[72,1024]{1,0:T(8,128)(2,1)S(1)} %get-tuple-element.31), channel_id=1, source_target_pairs={{0,24},{1,25},{2,26},{3,27},{4,28},{5,29},{6,30},{7,31},{8,16},{9,... | collective-permute-start | bytes 442376 | tf_op jit(solution)/shard_map/ppermute | solution.py:237
  23.5 16.3 %collective-permute-start.16 = (bf16[256,1024]{1,0:T(8,128)(2,1)S(1)}, bf16[256,1024]{1,0:T(8,128)(2,1)S(1)}, u32[]{:S(2)}, u32[]{:S(2)}) collective-permute-start(bf16[256,1024]{1,0:T(8,128)(2,1)S(1)} %copy-done.1), channel_id=1, source_target_pairs={{0,17},{1,8},{2,19},{3,10},{4,21},{5,12},{6,23},{7,14},{8,25},{9,0... | collective-permute-start | bytes 1572872 | tf_op jit(solution)/shard_map/ppermute | solution.py:237
  30.8 9.0 %collective-permute-start.15 = (bf16[256,1024]{1,0:T(8,128)(2,1)S(1)}, bf16[256,1024]{1,0:T(8,128)(2,1)S(1)}, u32[]{:S(2)}, u32[]{:S(2)}) collective-permute-start(bf16[256,1024]{1,0:T(8,128)(2,1)S(1)} %copy-done.1), channel_id=1, source_target_pairs={{0,1},{1,0},{2,3},{3,2},{4,5},{5,4},{6,7},{7,6},{8,9},{9,8},{10,11... | collective-permute-start | bytes 1572872 | tf_op jit(solution)/shard_map/ppermute | solution.py:227
  30.9 8.9 %copy-start.5 = (s32[8]{0:T(128)S(1)}, s32[8]{0:T(128)}, u32[]{:S(2)}) copy-start(s32[8]{0:T(128)} %block_map.1) | copy-start | bytes 100
  30.9 8.9 %copy-start.6 = (s32[4]{0:T(128)S(1)}, s32[4]{0:T(128)}, u32[]{:S(2)}) copy-start(s32[4]{0:T(128)} %lengths.1) | copy-start | bytes 52
  30.9 5.7 %collective-permute-start.7 = (bf16[64,1024]{1,0:T(8,128)(2,1)S(1)}, bf16[64,1024]{1,0:T(8,128)(2,1)S(1)}, u32[]{:S(2)}, u32[]{:S(2)}) collective-permute-start(bf16[64,1024]{1,0:T(8,128)(2,1)S(1)} %get-tuple-element.32.refs_0_), channel_id=1, source_target_pairs={{0,16},{1,9},{2,18},{3,11},{4,20},{5,13},{6,22},{7,15},{8,24},{9,1... | collective-permute-start | bytes 393224 | tf_op jit(solution)/shard_map/ppermute | solution.py:237
  31.7 5.0 %collective-permute-start.8 = (bf16[64,512]{1,0:T(8,128)(2,1)S(1)}, bf16[64,512]{1,0:T(8,128)(2,1)S(1)}, u32[]{:S(2)}, u32[]{:S(2)}) collective-permute-start(bf16[64,512]{1,0:T(8,128)(2,1)S(1)} %get-tuple-element.33), channel_id=1, source_target_pairs={{0,8},{1,17},{2,10},{3,19},{4,12},{5,21},{6,14},{7,23},{8,0},{9,25... | collective-permute-start | bytes 196616 | tf_op jit(solution)/shard_map/ppermute | solution.py:237
  33.2 5.2 %collective-permute-start.9 = (bf16[64,512]{1,0:T(8,128)(2,1)S(1)}, bf16[64,512]{1,0:T(8,128)(2,1)S(1)}, u32[]{:S(2)}, u32[]{:S(2)}) collective-permute-start(bf16[64,512]{1,0:T(8,128)(2,1)S(1)} %get-tuple-element.33), channel_id=1, source_target_pairs={{0,24},{1,25},{2,26},{3,27},{4,28},{5,29},{6,30},{7,31},{8,16},{9,... | collective-permute-start | bytes 196616 | tf_op jit(solution)/shard_map/ppermute | solution.py:237
  36.7 1.7 %collective-permute-start.10 = (bf16[64,512]{1,0:T(8,128)(2,1)S(1)}, bf16[64,512]{1,0:T(8,128)(2,1)S(1)}, u32[]{:S(2)}, u32[]{:S(2)}) collective-permute-start(bf16[64,512]{1,0:T(8,128)(2,1)S(1)} %get-tuple-element.33), channel_id=1, source_target_pairs={{0,1},{1,0},{2,3},{3,2},{4,5},{5,4},{6,7},{7,6},{8,9},{9,8},{10,11... | collective-permute-start | bytes 196616 | tf_op jit(solution)/shard_map/ppermute | solution.py:227
  36.7 3.1 %collective-permute-start.11 = (bf16[64,1024]{1,0:T(8,128)(2,1)S(1)}, bf16[64,1024]{1,0:T(8,128)(2,1)S(1)}, u32[]{:S(2)}, u32[]{:S(2)}) collective-permute-start(bf16[64,1024]{1,0:T(8,128)(2,1)S(1)} %collective-permute-done.7.refs_1_), channel_id=1, source_target_pairs={{0,1},{1,0},{2,3},{3,2},{4,5},{5,4},{6,7},{7,6},{8,9},{9,8},{10,11... | collective-permute-start | bytes 393224 | tf_op jit(solution)/shard_map/ppermute | solution.py:227
  38.4 1.3 %collective-permute-start.12 = (bf16[64,512]{1,0:T(8,128)(2,1)S(1)}, bf16[64,512]{1,0:T(8,128)(2,1)S(1)}, u32[]{:S(2)}, u32[]{:S(2)}) collective-permute-start(bf16[64,512]{1,0:T(8,128)(2,1)S(1)} %collective-permute-done.8.refs_2_), channel_id=1, source_target_pairs={{0,1},{1,0},{2,3},{3,2},{4,5},{5,4},{6,7},{7,6},{8,9},{9,8},{10,11... | collective-permute-start | bytes 196616 | tf_op jit(solution)/shard_map/ppermute | solution.py:227
  38.4 1.4 %collective-permute-start.13 = (bf16[64,512]{1,0:T(8,128)(2,1)S(1)}, bf16[64,512]{1,0:T(8,128)(2,1)S(1)}, u32[]{:S(2)}, u32[]{:S(2)}) collective-permute-start(bf16[64,512]{1,0:T(8,128)(2,1)S(1)} %collective-permute-done.9.refs_3_), channel_id=1, source_target_pairs={{0,1},{1,0},{2,3},{3,2},{4,5},{5,4},{6,7},{7,6},{8,9},{9,8},{10,11... | collective-permute-start | bytes 196616 | tf_op jit(solution)/shard_map/ppermute | solution.py:227
  42.3 6.8 %collective-permute-start.17 = (bf16[144,1024]{1,0:T(8,128)(2,1)S(1)}, bf16[144,1024]{1,0:T(8,128)(2,1)S(1)}, u32[]{:S(2)}, u32[]{:S(2)}) collective-permute-start(bf16[144,1024]{1,0:T(8,128)(2,1)S(1)} %get-tuple-element.39), channel_id=1, source_target_pairs={{0,16},{1,9},{2,18},{3,11},{4,20},{5,13},{6,22},{7,15},{8,24},{9,1... | collective-permute-start | bytes 884744 | tf_op jit(solution)/shard_map/ppermute | solution.py:237
  49.2 7.1 %collective-permute-start.18 = (bf16[72,1024]{1,0:T(8,128)(2,1)S(1)}, bf16[72,1024]{1,0:T(8,128)(2,1)S(1)}, u32[]{:S(2)}, u32[]{:S(2)}) collective-permute-start(bf16[72,1024]{1,0:T(8,128)(2,1)S(1)} %get-tuple-element.41), channel_id=1, source_target_pairs={{0,2},{1,3},{2,0},{3,1},{4,6},{5,7},{6,4},{7,5},{8,10},{9,11},{10,... | collective-permute-start | bytes 442376 | tf_op jit(solution)/shard_map/ppermute | solution.py:230
  50.9 13.8 %collective-permute-start.19 = (bf16[72,1024]{1,0:T(8,128)(2,1)S(1)}, bf16[72,1024]{1,0:T(8,128)(2,1)S(1)}, u32[]{:S(2)}, u32[]{:S(2)}) collective-permute-start(bf16[72,1024]{1,0:T(8,128)(2,1)S(1)} %get-tuple-element.42), channel_id=1, source_target_pairs={{0,4},{1,5},{2,6},{3,7},{4,0},{5,1},{6,2},{7,3},{8,12},{9,13},{10,... | collective-permute-start | bytes 442376 | tf_op jit(solution)/shard_map/ppermute | solution.py:230
  53.4 11.2 %collective-permute-start.20 = (bf16[72,1024]{1,0:T(8,128)(2,1)S(1)}, bf16[72,1024]{1,0:T(8,128)(2,1)S(1)}, u32[]{:S(2)}, u32[]{:S(2)}) collective-permute-start(bf16[72,1024]{1,0:T(8,128)(2,1)S(1)} %get-tuple-element.43), channel_id=1, source_target_pairs={{0,6},{1,7},{2,4},{3,5},{4,2},{5,3},{6,0},{7,1},{8,14},{9,15},{10,... | collective-permute-start | bytes 442376 | tf_op jit(solution)/shard_map/ppermute | solution.py:230
  64.8 1.3 %collective-permute-start.21 = (bf16[64,512]{1,0:T(8,128)(2,1)S(1)}, bf16[64,512]{1,0:T(8,128)(2,1)S(1)}, u32[]{:S(2)}, u32[]{:S(2)}) collective-permute-start(bf16[64,512]{1,0:T(8,128)(2,1)S(1)} %get-tuple-element.45), channel_id=1, source_target_pairs={{0,1},{1,0},{2,3},{3,2},{4,5},{5,4},{6,7},{7,6},{8,9},{9,8},{10,11... | collective-permute-start | bytes 196616 | tf_op jit(solution)/shard_map/ppermute | solution.py:227

commit v6 on v5

--- a/solution.py
+++ b/solution.py
@@ -27,6 +27,10 @@
     return [0, 2 - core, 1 + core, 3]
 
 
+def turned(values):
+    return [values[0], *values[:0:-1]]
+
+
 def place():
     t = lax.axis_index("tp")
     return lax.axis_index("ctx"), t // 2, t % 2
@@ -38,7 +42,7 @@
 
 
 def project_kernel(parts_of, *refs):
-    blocks, (new, own, other), refs = refs[:4], refs[4:7], refs[7:]
+    blocks, (new, own, other), refs = turned(refs[:4]), refs[4:7], refs[7:]
     (held, new_held), outs, inputs = refs[:2], refs[2:5], refs[5]
     rows = held.shape[0]
     count = new.shape[0]
@@ -63,7 +67,7 @@
         column += weight.shape[1]
 
 
-def add_kernel(own, new_own, first, second, both, held, keyval, new):
+def add_kernel(own, new_own, first, second, both, held, new):
     rows = held.shape[0]
 
     def total(own, at):
@@ -71,9 +75,7 @@
         parts += [ref[at, :].astype(jnp.float32) for ref in (first, second, both)]
         return ((parts[0] + parts[1]) + (parts[2] + parts[3])).astype(held.dtype)
 
-    sums = total(own, slice(0, rows))
-    held[...] = sums
-    keyval[...] = sums[:, held.shape[1] - keyval.shape[1] :]
+    held[...] = total(own, slice(0, rows))
     new[...] = total(new_own, slice(rows, None))
 
 
@@ -85,9 +87,9 @@
 
 
 def attend_kernel(count, scale, block_map, lengths, *refs):
-    mine, theirs, refs = refs[:4], refs[4:8], refs[8:]
-    new, columns, refs = refs[0], (refs[1:3], refs[3:5]), refs[5:]
-    keep, send, q_all, key_all, value_all, attended = refs
+    mine, theirs, refs = turned(refs[:4]), turned(refs[4:8]), refs[8:]
+    (new, w_own, w_other), outs, refs = refs[:3], (refs[3:7], refs[7:11]), refs[11:]
+    q_all, key_all, value_all, attended, result = refs
     steps = len(mine)
     rows, features = mine[0].shape
     q_width, kv_width = q_all.shape[1], key_all.shape[1]
@@ -95,7 +97,7 @@
     groups = kv_width // head
     per_group = q_width // kv_width
     pad = new.shape[0]
-    tail = 2 * rows
+    tail = steps * rows
     q_rows = q_all.shape[0]
     k_rows = key_all.shape[0]
     k_tail = 2 * steps * rows
@@ -119,7 +121,7 @@
     key_all[k_tail : k_tail + pad, :] = new[:, q_width : q_width + kv_width]
     value_all[k_tail : k_tail + pad, :] = new[:, q_width + kv_width :]
     q_all[tail:, :] = jnp.zeros_like(q_all[tail:, :])
-    for number in range(2):
+    for number in range(steps):
         q_all[number * rows : (number + 1) * rows, :] = mine[number][:, :q_width]
     q_all[tail : tail + pad, :] = new[:, :q_width]
 
@@ -140,7 +142,7 @@
         return jnp.where(is_new, LAST, position), request
 
     held = [2 * (c ^ mask) + core for core in (k, 1 - k) for mask in partners(core)]
-    q_position, q_request = labels((q_rows, 1), 0, held[:2])
+    q_position, q_request = labels((q_rows, 1), 0, held[:steps])
     k_position, k_request = labels((1, k_rows), 1, held)
     allowed = (q_request == k_request) & (k_position <= q_position)
 
@@ -163,50 +165,48 @@
             )
             attended[:, at : at + head] = (mixed / denom).astype(jnp.bfloat16)
 
-    for number, (w_own, w_other) in enumerate(columns):
-        rows_own = w_own.shape[0]
-        result = (
-            jnp.dot(attended[:, :rows_own], w_own[...], preferred_element_type=jnp.float32)
-            + jnp.dot(attended[:, rows_own:], w_other[...], preferred_element_type=jnp.float32)
-        ).astype(jnp.bfloat16)
-        for out, block in ((keep, 0), (send, 1)):
-            at = number * (rows + pad)
-            out[at : at + rows, :] = result[block * rows : (block + 1) * rows]
-            out[at + rows : at + rows + pad, :] = result[tail : tail + pad]
-
-
-def relay_kernel(keep, got, *outs):
+    rows_own = w_own.shape[0]
+    result[...] = (
+        jnp.dot(attended[:, :rows_own], w_own[...], preferred_element_type=jnp.float32)
+        + jnp.dot(attended[:, rows_own:], w_other[...], preferred_element_type=jnp.float32)
+    ).astype(jnp.bfloat16)
+    for core, half_outs in zip((1 - k, k), outs):
+        width = half_outs[0].shape[1]
+        column = pl.ds(pl.multiple_of(core * width, width), width)
+        for number, out in enumerate(half_outs):
+            out[:rows, :] = result[number * rows : (number + 1) * rows, column]
+            out[rows:, :] = result[tail : tail + pad, column]
+
+
+def relay_kernel(*refs):
+    blocks, outs = refs[:4], refs[4:]
     c, z, k = place()
-    rows = outs[0].shape[0]
-    blocks = [(ref, number) for ref in (keep, got) for number in range(2)]
-    masks = [partners(k)[i] for i in (0, 2, 1, 3)]
     for slot, out in enumerate(outs):
-        for mask, (ref, number) in zip(masks, blocks):
+        for mask, block in zip(partners(k), blocks):
 
             @pl.when((c ^ z ^ slot) == mask)
-            def _(out=out, ref=ref, number=number):
-                out[...] = ref[number * rows : (number + 1) * rows, :]
+            def _(out=out, block=block):
+                out[...] = block[...]
+
+
+def sum_heads(parts):
+    terms = [part[...].astype(jnp.float32) for part in parts]
+    return ((terms[0] + terms[1]) + (terms[2] + terms[3])).astype(jnp.bfloat16)
 
 
 def sum_kernel(*refs):
-    parts, (keep, send) = refs[:-2], refs[-2:]
-    width = keep.shape[1]
-    rows = send.shape[0]
-    _, _, k = place()
-    for out, core in ((keep, k), (send, 1 - k)):
-        column = pl.ds(pl.multiple_of(core * width, width), width)
-        terms = [part[:, column].astype(jnp.float32) for part in parts]
-        while len(terms) > 1:
-            terms = [a + b for a, b in zip(terms[::2], terms[1::2])]
-        out[...] = terms[0][: out.shape[0]].astype(out.dtype)
-
-
-def finish_kernel(keep, other, prefill, decode):
+    send = refs[-1]
+    send[...] = sum_heads(refs[:-1])[: send.shape[0]]
+
+
+def finish_kernel(*refs):
+    parts, (other, prefill, decode) = refs[:4], refs[4:]
     _, _, k = place()
     rows = other.shape[0]
-    prefill[pl.ds(pl.multiple_of(k * rows, rows), rows), :] = keep[:rows]
+    total = sum_heads(parts)
+    prefill[pl.ds(pl.multiple_of(k * rows, rows), rows), :] = total[:rows]
     prefill[pl.ds(pl.multiple_of((1 - k) * rows, rows), rows), :] = other[...]
-    decode[...] = keep[rows : rows + decode.shape[0]]
+    decode[...] = total[rows : rows + decode.shape[0]]
 
 
 def on_device_small(
@@ -229,11 +229,8 @@
     def to_chip(value, step):
         return lax.ppermute(value, "tp", [(i, i ^ (2 * step)) for i in range(tp)])
 
-    def to_partner(value, number, swap=0):
-        pairs = [
-            (c * tp + t, (c ^ partners((t ^ swap) % 2)[number]) * tp + (t ^ swap))
-            for c, t in devices
-        ]
+    def to_partner(value, number):
+        pairs = [(c * tp + t, (c ^ partners(t % 2)[number]) * tp + t) for c, t in devices]
         return lax.ppermute(value, ("ctx", "tp"), pairs)
 
     def to_partners(values):
@@ -267,58 +264,54 @@
     own_part, new_part, *parts = call(
         functools.partial(project_kernel, list(zip(edges, edges[1:]))),
         "project",
-        (*blocks, new_columns, own, other),
+        (*turned(blocks), new_columns, own, other),
         [((rows, features), f32), ((pad, features), bf16)] + [(part_shape, bf16)] * (steps - 1),
         [pltpu.VMEM((x_rows, depth), bf16)],
     )
 
-    w_second = to_partner(w_out, 2)
     w_out_later, _ = lax.optimization_barrier((w_out, new_part))
-    w_second_other = to_partner(w_out_later, 2, 1)
-
-    held, keyval, new = call(
+    w_other = to_core(w_out_later)
+
+    held, new = call(
         add_kernel,
         "add_parts",
         (own_part, new_part, *to_partners(parts)),
-        [((rows, features), bf16), ((rows, 2 * kv_width), bf16), ((pad, features), bf16)],
-    )
-    w_out_last, _, w_second = lax.optimization_barrier((w_out, new, w_second))
-    w_other = to_core(w_out_last)
-
-    mine = [held] + to_partners([held, keyval, keyval])
-    theirs = [to_core(value) for value in [keyval] + mine[1:]]
-
-    q_rows = -(-(2 * rows + pad) // 16) * 16
+        [((rows, features), bf16), ((pad, features), bf16)],
+    )
+    mine = [held] + to_partners([held] * (steps - 1))
+    theirs = [to_core(value) for value in mine]
+
     k_rows = -(-(2 * steps * rows + pad) // 128) * 128
-    block = (rows + pad, out_width)
-    keep, send = call(
+    block = (rows + pad, out_width // 2)
+    outs = call(
         functools.partial(attend_kernel, count, 1.0 / math.sqrt(HEAD_SIZE)),
         "attend",
-        (block_map, lengths, *mine, *theirs, new, w_out, w_other, w_second, w_second_other),
-        [((2 * block[0], out_width), bf16)] * 2,
+        (block_map, lengths, *turned(mine), *turned(theirs), new, w_out, w_other),
+        [(block, bf16)] * (2 * steps),
         [
-            pltpu.VMEM((q_rows, q_width), bf16),
+            pltpu.VMEM((x_rows, q_width), bf16),
             pltpu.VMEM((k_rows, kv_width), bf16),
             pltpu.VMEM((k_rows, kv_width), bf16),
-            pltpu.VMEM((q_rows, q_width), bf16),
+            pltpu.VMEM((x_rows, q_width), bf16),
+            pltpu.VMEM((x_rows, out_width), bf16),
         ],
-        [smem()] * 2 + [vmem()] * (2 * steps + 5),
-    )
-
-    got = to_partner(send, 1)
-    slots = call(relay_kernel, "relay", (keep, got), [(block, bf16)] * steps)
-    slots = [slots[0]] + [to_chip(slot, step) for step, slot in enumerate(slots[1:], 1)]
-    keep, send = call(
-        sum_kernel,
-        "sum_heads",
-        slots,
-        [((rows + pad, out_width // 2), bf16), ((rows, out_width // 2), bf16)],
-    )
+        [smem()] * 2 + [vmem()] * (2 * steps + 3),
+    )
+
+    halves = []
+    for half in (outs[:steps], outs[steps:]):
+        got = [half[0]] + to_partners(half[1:])
+        slots = call(relay_kernel, "relay", got, [(block, bf16)] * steps)
+        halves.append(
+            [slots[0]] + [to_chip(slot, step) for step, slot in enumerate(slots[1:], 1)]
+        )
+    shape = (rows, out_width // 2)
+    (send,) = call(sum_kernel, "sum_heads", halves[0], [(shape, bf16)])
     return tuple(
         call(
             finish_kernel,
             "finish",
-            (keep, to_core(send)),
+            (*halves[1], to_core(send)),
             [((2 * rows, out_width // 2), bf16), ((count, out_width // 2), bf16)],
         )
     )

time: 66.9 us -> 63 us (0.942)
  waiting for transfers between devices: 39.5 us -> 26 us
  starting transfers between devices: 20.3 us -> 29.6 us
    ppermute x12 -> x15, waiting for transfers between devices: 26.3 us -> 19 us  [to_partner(): return lax.ppermute(value, ('ctx', 'tp'), pairs)]
    ppermute x3 -> x6, starting transfers between devices: 4.45 us -> 10.2 us  [to_chip(): return lax.ppermute(value, 'tp', [(i, i ^ 2 * step) for i in range(tp)])]
    ppermute x3 -> x6, waiting for transfers between devices: 11 us -> 5.64 us  [to_chip(): return lax.ppermute(value, 'tp', [(i, i ^ 2 * step) for i in range(tp)])]
    ppermute x12 -> x15, starting transfers between devices: 14.2 us -> 18.2 us  [to_partner(): return lax.ppermute(value, ('ctx', 'tp'), pairs)]
    ppermute x7, waiting for transfers between devices: 2.15 us -> 1.34 us  [to_core(): return lax.ppermute(value, 'tp', [(i, i ^ 1) for i in range(tp)])]
    pallas_call x7 -> x8, Pallas kernels: 4.24 us -> 4.64 us  [call(): pl.pallas_call(kernel, out_shape=[jax.ShapeDtypeStruct(shape, kind) for s...]
  transfers between devices with their start and end apart: 22 -> 28, of which waited for: 13 -> 11; matrix products, arithmetic and copies ran while one was open for 0% -> 0% of each run, Pallas kernels for 1% -> 0%
where the time goes in v6:
time: 63 us; the launch traced here: 62.8 us
  starting transfers between devices  29.6 us (47%)
  waiting for transfers between devices  26 us (41%)
  Pallas kernels  4.64 us (7%)
  local copies, waits for them, and re-layouts  1.73 us (3%)
  between operations  0.82 us (1%)
    ppermute x15, waiting for transfers between devices, to_partner(): return lax.ppermute(value, ('ctx', 'tp'), pairs)  19 us
    ppermute x15, starting transfers between devices, to_partner(): return lax.ppermute(value, ('ctx', 'tp'), pairs)  18.2 us
    ppermute x6, starting transfers between devices, to_chip(): return lax.ppermute(value, 'tp', [(i, i ^ 2 * step) for i in range(tp)])  10.2 us
    ppermute x6, waiting for transfers between devices, to_chip(): return lax.ppermute(value, 'tp', [(i, i ^ 2 * step) for i in range(tp)])  5.64 us
    pallas_call x8, Pallas kernels, call(): pl.pallas_call(kernel, out_shape=[jax.ShapeDtypeStruct(shape, kind) for s...  4.64 us
    ppermute x7, waiting for transfers between devices, to_core(): return lax.ppermute(value, 'tp', [(i, i ^ 1) for i in range(tp)])  1.34 us
  transfers between devices with their start and end apart: 28, of which 11 were waited for; matrix products, arithmetic and copies ran while one was open for 0% of the time, Pallas kernels for 0%

profile of v6, /device:TPU:0, one launch (start us, length us, event | category | flops | bytes accessed | tf_op | source)
XLA Modules:
  0.0 62.8 jit_solution(15233655727236981376)
XLA Ops:
  0.7 1.2 %fusion = (bf16[64,1024]{1,0:T(8,128)(2,1)S(1)}, bf16[64,1024]{1,0:T(8,128)(2,1)S(1)}, bf16[64,1024]{1,0:T(8,128)(2,1)S(1)}, bf16[64,1024]{1,0:T(8,128)(2,1)S(1)}) fusion(bf16[128,4096]{1,0:T(8,128)(2,1)} %param.8, s32[]{:T(128)S(6)} %select_n.27, s32[]{:T(128)S(6)} %select_n.31, s32[]{:T(128)S(6)} %select_n.29, s32[]{:T(128)S(6)} %select_n.28, s32[]{:T(128)S(6)} %select_n.30), kind=kLoop, calls=%fused_computation.1 | loop fusion | bytes 1048596 | tf_op jit(solution)/shard_map/dynamic_slice | solution.py:252
  2.7 3.5 %collective-permute-start = (bf16[64,1024]{1,0:T(8,128)(2,1)S(1)}, bf16[64,1024]{1,0:T(8,128)(2,1)S(1)}, u32[]{:S(2)}, u32[]{:S(2)}) collective-permute-start(bf16[64,1024]{1,0:T(8,128)(2,1)S(1)} %get-tuple-element.57), channel_id=1, source_target_pairs={{0,24},{1,25},{2,26},{3,27},{4,28},{5,29},{6,30},{7,31},{8,16},{9,... | collective-permute-start | bytes 393224 | tf_op jit(solution)/shard_map/ppermute | solution.py:234
  6.9 3.5 %collective-permute-done.refs_1_ = bf16[64,1024]{1,0:T(8,128)(2,1)S(1)} collective-permute-done((bf16[64,1024]{1,0:T(8,128)(2,1)S(1)}, bf16[64,1024]{1,0:T(8,128)(2,1)S(1)}, u32[]{:S(2)}, u32[]{:S(2)}) %collective-permute-start) | collective-permute-done | bytes 131104 | tf_op jit(solution)/shard_map/ppermute | solution.py:234
  10.4 3.0 %collective-permute-done.1.refs_2_ = bf16[64,1024]{1,0:T(8,128)(2,1)S(1)} collective-permute-done((bf16[64,1024]{1,0:T(8,128)(2,1)S(1)}, bf16[64,1024]{1,0:T(8,128)(2,1)S(1)}, u32[]{:S(2)}, u32[]{:S(2)}) %collective-permute-start.1) | collective-permute-done | bytes 131104 | tf_op jit(solution)/shard_map/ppermute | solution.py:234
  13.5 0.7 %project.1 = (f32[64,1024]{1,0:T(8,128)S(1)}, bf16[8,1024]{1,0:T(8,128)(2,1)S(1)}, bf16[72,1024]{1,0:T(8,128)(2,1)S(1)}, bf16[72,1024]{1,0:T(8,128)(2,1)S(1)}, bf16[72,1024]{1,0:T(8,128)(2,1)S(1)}) custom-call(bf16[64,1024]{1,0:T(8,128)(2,1)S(1)} %get-tuple-element.58.refs_0_, bf16[64,1024]{1,0:T(8,128)(2,1)S(1)} %collective-permute-done.refs_1_, ...), custom_call_target="tpu_custom_call" | custom-call | tf_op jit(solution)/shard_map/project/pallas_call | solution.py:240
  14.5 1.4 %collective-permute-start.4 = (bf16[72,1024]{1,0:T(8,128)(2,1)S(1)}, bf16[72,1024]{1,0:T(8,128)(2,1)S(1)}, u32[]{:S(2)}, u32[]{:S(2)}) collective-permute-start(bf16[72,1024]{1,0:T(8,128)(2,1)S(1)} %get-tuple-element.34), channel_id=1, source_target_pairs={{0,16},{1,9},{2,18},{3,11},{4,20},{5,13},{6,22},{7,15},{8,24},{9,1... | collective-permute-start | bytes 442376 | tf_op jit(solution)/shard_map/ppermute | solution.py:234
  16.0 0.6 collective-permute-start.5
  16.5 1.5 %collective-permute-start.6 = (bf16[72,1024]{1,0:T(8,128)(2,1)S(1)}, bf16[72,1024]{1,0:T(8,128)(2,1)S(1)}, u32[]{:S(2)}, u32[]{:S(2)}) collective-permute-start(bf16[72,1024]{1,0:T(8,128)(2,1)S(1)} %get-tuple-element.36), channel_id=1, source_target_pairs={{0,24},{1,25},{2,26},{3,27},{4,28},{5,29},{6,30},{7,31},{8,16},{9,... | collective-permute-start | bytes 442376 | tf_op jit(solution)/shard_map/ppermute | solution.py:234
  18.0 3.0 %collective-permute-done.4.first = bf16[72,1024]{1,0:T(8,128)(2,1)S(1)} collective-permute-done((bf16[72,1024]{1,0:T(8,128)(2,1)S(1)}, bf16[72,1024]{1,0:T(8,128)(2,1)S(1)}, u32[]{:S(2)}, u32[]{:S(2)}) %collective-permute-start.4) | collective-permute-done | bytes 147488 | tf_op jit(solution)/shard_map/ppermute | solution.py:234
  21.0 1.3 %collective-permute-done.5.second = bf16[72,1024]{1,0:T(8,128)(2,1)S(1)} collective-permute-done((bf16[72,1024]{1,0:T(8,128)(2,1)S(1)}, bf16[72,1024]{1,0:T(8,128)(2,1)S(1)}, u32[]{:S(2)}, u32[]{:S(2)}) %collective-permute-start.5) | collective-permute-done | bytes 147488 | tf_op jit(solution)/shard_map/ppermute | solution.py:234
  22.3 2.5 %collective-permute-done.6.both = bf16[72,1024]{1,0:T(8,128)(2,1)S(1)} collective-permute-done((bf16[72,1024]{1,0:T(8,128)(2,1)S(1)}, bf16[72,1024]{1,0:T(8,128)(2,1)S(1)}, u32[]{:S(2)}, u32[]{:S(2)}) %collective-permute-start.6) | collective-permute-done | bytes 147488 | tf_op jit(solution)/shard_map/ppermute | solution.py:234
  24.9 1.0 %collective-permute-start.9 = (bf16[64,1024]{1,0:T(8,128)(2,1)S(1)}, bf16[64,1024]{1,0:T(8,128)(2,1)S(1)}, u32[]{:S(2)}, u32[]{:S(2)}) collective-permute-start(bf16[64,1024]{1,0:T(8,128)(2,1)S(1)} %get-tuple-element.37.refs_0_), channel_id=1, source_target_pairs={{0,16},{1,9},{2,18},{3,11},{4,20},{5,13},{6,22},{7,15},{8,24},{9,1... | collective-permute-start | bytes 393224 | tf_op jit(solution)/shard_map/ppermute | solution.py:234
  25.9 1.2 %collective-permute-start.8 = (bf16[64,1024]{1,0:T(8,128)(2,1)S(1)}, bf16[64,1024]{1,0:T(8,128)(2,1)S(1)}, u32[]{:S(2)}, u32[]{:S(2)}) collective-permute-start(bf16[64,1024]{1,0:T(8,128)(2,1)S(1)} %get-tuple-element.37.refs_0_), channel_id=1, source_target_pairs={{0,8},{1,17},{2,10},{3,19},{4,12},{5,21},{6,14},{7,23},{8,0},{9,25... | collective-permute-start | bytes 393224 | tf_op jit(solution)/shard_map/ppermute | solution.py:234
  27.1 1.4 %collective-permute-start.7 = (bf16[64,1024]{1,0:T(8,128)(2,1)S(1)}, bf16[64,1024]{1,0:T(8,128)(2,1)S(1)}, u32[]{:S(2)}, u32[]{:S(2)}) collective-permute-start(bf16[64,1024]{1,0:T(8,128)(2,1)S(1)} %get-tuple-element.37.refs_0_), channel_id=1, source_target_pairs={{0,24},{1,25},{2,26},{3,27},{4,28},{5,29},{6,30},{7,31},{8,16},{9,... | collective-permute-start | bytes 393224 | tf_op jit(solution)/shard_map/ppermute | solution.py:234
  28.4 2.9 %collective-permute-done.9.refs_3_ = bf16[64,1024]{1,0:T(8,128)(2,1)S(1)} collective-permute-done((bf16[64,1024]{1,0:T(8,128)(2,1)S(1)}, bf16[64,1024]{1,0:T(8,128)(2,1)S(1)}, u32[]{:S(2)}, u32[]{:S(2)}) %collective-permute-start.9) | collective-permute-done | bytes 131104 | tf_op jit(solution)/shard_map/ppermute | solution.py:234
  31.8 1.5 %collective-permute-done.7.refs_1_ = bf16[64,1024]{1,0:T(8,128)(2,1)S(1)} collective-permute-done((bf16[64,1024]{1,0:T(8,128)(2,1)S(1)}, bf16[64,1024]{1,0:T(8,128)(2,1)S(1)}, u32[]{:S(2)}, u32[]{:S(2)}) %collective-permute-start.7) | collective-permute-done | bytes 131104 | tf_op jit(solution)/shard_map/ppermute | solution.py:234
  33.4 1.3 %collective-permute-done.11.refs_5_ = bf16[64,1024]{1,0:T(8,128)(2,1)S(1)} collective-permute-done((bf16[64,1024]{1,0:T(8,128)(2,1)S(1)}, bf16[64,1024]{1,0:T(8,128)(2,1)S(1)}, u32[]{:S(2)}, u32[]{:S(2)}) %collective-permute-start.11) | collective-permute-done | bytes 131104 | tf_op jit(solution)/shard_map/ppermute | solution.py:227
  34.7 2.9 %attend.1 = (bf16[72,512]{1,0:T(8,128)(2,1)S(1)}, bf16[72,512]{1,0:T(8,128)(2,1)S(1)}, bf16[72,512]{1,0:T(8,128)(2,1)S(1)}, bf16[72,512]{1,0:T(8,128)(2,1)S(1)},...) custom-call(s32[8]{0:T(128)S(1)} %copy-done.5, ...), custom_call_target="tpu_custom_call" | custom-call | tf_op jit(solution)/shard_map/attend/pallas_call | solution.py:240
  37.6 1.4 %collective-permute-start.21 = (bf16[72,512]{1,0:T(8,128)(2,1)S(1)}, bf16[72,512]{1,0:T(8,128)(2,1)S(1)}, u32[]{:S(2)}, u32[]{:S(2)}) collective-permute-start(bf16[72,512]{1,0:T(8,128)(2,1)S(1)} %get-tuple-element.49), channel_id=1, source_target_pairs={{0,16},{1,9},{2,18},{3,11},{4,20},{5,13},{6,22},{7,15},{8,24},{9,1... | collective-permute-start | bytes 221192 | tf_op jit(solution)/shard_map/ppermute | solution.py:234
  39.0 0.6 collective-permute-start.22
  39.5 1.6 %collective-permute-start.23 = (bf16[72,512]{1,0:T(8,128)(2,1)S(1)}, bf16[72,512]{1,0:T(8,128)(2,1)S(1)}, u32[]{:S(2)}, u32[]{:S(2)}) collective-permute-start(bf16[72,512]{1,0:T(8,128)(2,1)S(1)} %get-tuple-element.51), channel_id=1, source_target_pairs={{0,24},{1,25},{2,26},{3,27},{4,28},{5,29},{6,30},{7,31},{8,16},{9,... | collective-permute-start | bytes 221192 | tf_op jit(solution)/shard_map/ppermute | solution.py:234
  41.1 1.3 %collective-permute-start.15 = (bf16[72,512]{1,0:T(8,128)(2,1)S(1)}, bf16[72,512]{1,0:T(8,128)(2,1)S(1)}, u32[]{:S(2)}, u32[]{:S(2)}) collective-permute-start(bf16[72,512]{1,0:T(8,128)(2,1)S(1)} %get-tuple-element.41), channel_id=1, source_target_pairs={{0,16},{1,9},{2,18},{3,11},{4,20},{5,13},{6,22},{7,15},{8,24},{9,1... | collective-permute-start | bytes 221192 | tf_op jit(solution)/shard_map/ppermute | solution.py:234
  42.4 0.6 collective-permute-start.16
  43.0 1.6 %collective-permute-start.17 = (bf16[72,512]{1,0:T(8,128)(2,1)S(1)}, bf16[72,512]{1,0:T(8,128)(2,1)S(1)}, u32[]{:S(2)}, u32[]{:S(2)}) collective-permute-start(bf16[72,512]{1,0:T(8,128)(2,1)S(1)} %get-tuple-element.43), channel_id=1, source_target_pairs={{0,24},{1,25},{2,26},{3,27},{4,28},{5,29},{6,30},{7,31},{8,16},{9,... | collective-permute-start | bytes 221192 | tf_op jit(solution)/shard_map/ppermute | solution.py:234
  44.6 1.3 %collective-permute-done.23.refs_3_ = bf16[72,512]{1,0:T(8,128)(2,1)S(1)} collective-permute-done((bf16[72,512]{1,0:T(8,128)(2,1)S(1)}, bf16[72,512]{1,0:T(8,128)(2,1)S(1)}, u32[]{:S(2)}, u32[]{:S(2)}) %collective-permute-start.23) | collective-permute-done | bytes 73760 | tf_op jit(solution)/shard_map/ppermute | solution.py:234
  46.0 2.1 %collective-permute-start.24 = (bf16[72,512]{1,0:T(8,128)(2,1)S(1)}, bf16[72,512]{1,0:T(8,128)(2,1)S(1)}, u32[]{:S(2)}, u32[]{:S(2)}) collective-permute-start(bf16[72,512]{1,0:T(8,128)(2,1)S(1)} %get-tuple-element.53), channel_id=1, source_target_pairs={{0,2},{1,3},{2,0},{3,1},{4,6},{5,7},{6,4},{7,5},{8,10},{9,11},{10,... | collective-permute-start | bytes 221192 | tf_op jit(solution)/shard_map/ppermute | solution.py:230
  48.1 2.6 %collective-permute-start.25 = (bf16[72,512]{1,0:T(8,128)(2,1)S(1)}, bf16[72,512]{1,0:T(8,128)(2,1)S(1)}, u32[]{:S(2)}, u32[]{:S(2)}) collective-permute-start(bf16[72,512]{1,0:T(8,128)(2,1)S(1)} %get-tuple-element.54), channel_id=1, source_target_pairs={{0,4},{1,5},{2,6},{3,7},{4,0},{5,1},{6,2},{7,3},{8,12},{9,13},{10,... | collective-permute-start | bytes 221192 | tf_op jit(solution)/shard_map/ppermute | solution.py:230
  51.8 3.5 %collective-permute-start.19 = (bf16[72,512]{1,0:T(8,128)(2,1)S(1)}, bf16[72,512]{1,0:T(8,128)(2,1)S(1)}, u32[]{:S(2)}, u32[]{:S(2)}) collective-permute-start(bf16[72,512]{1,0:T(8,128)(2,1)S(1)} %get-tuple-element.46), channel_id=1, source_target_pairs={{0,4},{1,5},{2,6},{3,7},{4,0},{5,1},{6,2},{7,3},{8,12},{9,13},{10,... | collective-permute-start | bytes 221192 | tf_op jit(solution)/shard_map/ppermute | solution.py:230
  55.3 1.1 %collective-permute-start.20 = (bf16[72,512]{1,0:T(8,128)(2,1)S(1)}, bf16[72,512]{1,0:T(8,128)(2,1)S(1)}, u32[]{:S(2)}, u32[]{:S(2)}) collective-permute-start(bf16[72,512]{1,0:T(8,128)(2,1)S(1)} %get-tuple-element.47), channel_id=1, source_target_pairs={{0,6},{1,7},{2,4},{3,5},{4,2},{5,3},{6,0},{7,1},{8,14},{9,15},{10,... | collective-permute-start | bytes 221192 | tf_op jit(solution)/shard_map/ppermute | solution.py:230
  56.3 1.4 %collective-permute-done.25.refs_2_ = bf16[72,512]{1,0:T(8,128)(2,1)S(1)} collective-permute-done((bf16[72,512]{1,0:T(8,128)(2,1)S(1)}, bf16[72,512]{1,0:T(8,128)(2,1)S(1)}, u32[]{:S(2)}, u32[]{:S(2)}) %collective-permute-start.25) | collective-permute-done | bytes 73760 | tf_op jit(solution)/shard_map/ppermute | solution.py:230
  57.8 4.3 %collective-permute-done.19.refs_2_ = bf16[72,512]{1,0:T(8,128)(2,1)S(1)} collective-permute-done((bf16[72,512]{1,0:T(8,128)(2,1)S(1)}, bf16[72,512]{1,0:T(8,128)(2,1)S(1)}, u32[]{:S(2)}, u32[]{:S(2)}) %collective-permute-start.19) | collective-permute-done | bytes 73760 | tf_op jit(solution)/shard_map/ppermute | solution.py:230
  62.1 0.7 %finish.1 = (bf16[128,512]{1,0:T(8,128)(2,1)}, bf16[4,512]{1,0:T(4,128)(2,1)}) custom-call(bf16[72,512]{1,0:T(8,128)(2,1)S(1)} %get-tuple-element.44.refs_0_, bf16[72,512]{1,0:T(8,128)(2,1)S(1)} %collective-permute-done.18.refs_1_, bf16[72,512]{1,0:T(8,128)(2,1)S(1)} %collective-permute-done.19.refs_2_, bf16[72,512]{1,0:T(8,128)(2,1)S(1)} %collective-permute-done.20.refs_3_, ...), custom_call_target="tpu_custom_call" | custom-call | tf_op jit(solution)/shard_map/finish/pallas_call | solution.py:240
  (48 shorter events, 3.6 us)
Async XLA Ops:
  0.6 6.3 %copy-start = (bf16[4,4096]{1,0:T(4,128)(2,1)S(1)}, bf16[4,4096]{1,0:T(4,128)(2,1)}, u32[]{:S(2)}) copy-start(bf16[4,4096]{1,0:T(4,128)(2,1)} %param.9) | copy-start | bytes 98308
  0.7 1.4 %copy-start.4 = (bf16[1024,128]{1,0:T(8,128)(2,1)S(1)}, bf16[1024,128]{1,0:T(8,128)(2,1)}, u32[]{:S(2)}) copy-start(bf16[1024,128]{1,0:T(8,128)(2,1)} %refs_2_) | copy-start | bytes 786436
  2.2 11.3 %collective-permute-start.3 = (bf16[1024,512]{1,0:T(8,128)(2,1)S(1)}, bf16[1024,512]{1,0:T(8,128)(2,1)S(1)}, u32[]{:S(2)}, u32[]{:S(2)}) collective-permute-start(bf16[1024,512]{1,0:T(8,128)(2,1)S(1)} %pack_weights.1.refs_5_), channel_id=1, source_target_pairs={{0,1},{1,0},{2,3},{3,2},{4,5},{5,4},{6,7},{7,6},{8,9},{9,8},{10,11... | collective-permute-start | bytes 3145736 | tf_op jit(solution)/shard_map/ppermute | solution.py:227
  2.7 7.7 %collective-permute-start = (bf16[64,1024]{1,0:T(8,128)(2,1)S(1)}, bf16[64,1024]{1,0:T(8,128)(2,1)S(1)}, u32[]{:S(2)}, u32[]{:S(2)}) collective-permute-start(bf16[64,1024]{1,0:T(8,128)(2,1)S(1)} %get-tuple-element.57), channel_id=1, source_target_pairs={{0,24},{1,25},{2,26},{3,27},{4,28},{5,29},{6,30},{7,31},{8,16},{9,... | collective-permute-start | bytes 393224 | tf_op jit(solution)/shard_map/ppermute | solution.py:234
  6.3 7.2 %collective-permute-start.1 = (bf16[64,1024]{1,0:T(8,128)(2,1)S(1)}, bf16[64,1024]{1,0:T(8,128)(2,1)S(1)}, u32[]{:S(2)}, u32[]{:S(2)}) collective-permute-start(bf16[64,1024]{1,0:T(8,128)(2,1)S(1)} %get-tuple-element.59), channel_id=1, source_target_pairs={{0,8},{1,17},{2,10},{3,19},{4,12},{5,21},{6,14},{7,23},{8,0},{9,25... | collective-permute-start | bytes 393224 | tf_op jit(solution)/shard_map/ppermute | solution.py:234
  6.8 6.7 %collective-permute-start.2 = (bf16[64,1024]{1,0:T(8,128)(2,1)S(1)}, bf16[64,1024]{1,0:T(8,128)(2,1)S(1)}, u32[]{:S(2)}, u32[]{:S(2)}) collective-permute-start(bf16[64,1024]{1,0:T(8,128)(2,1)S(1)} %get-tuple-element.56), channel_id=1, source_target_pairs={{0,16},{1,9},{2,18},{3,11},{4,20},{5,13},{6,22},{7,15},{8,24},{9,1... | collective-permute-start | bytes 393224 | tf_op jit(solution)/shard_map/ppermute | solution.py:234
  14.5 20.2 %collective-permute-start.14 = (bf16[256,1024]{1,0:T(8,128)(2,1)S(1)}, bf16[256,1024]{1,0:T(8,128)(2,1)S(1)}, u32[]{:S(2)}, u32[]{:S(2)}) collective-permute-start(bf16[256,1024]{1,0:T(8,128)(2,1)S(1)} %copy-done.2), channel_id=1, source_target_pairs={{0,1},{1,0},{2,3},{3,2},{4,5},{5,4},{6,7},{7,6},{8,9},{9,8},{10,11... | collective-permute-start | bytes 1572872 | tf_op jit(solution)/shard_map/ppermute | solution.py:227
  14.5 6.4 %collective-permute-start.4 = (bf16[72,1024]{1,0:T(8,128)(2,1)S(1)}, bf16[72,1024]{1,0:T(8,128)(2,1)S(1)}, u32[]{:S(2)}, u32[]{:S(2)}) collective-permute-start(bf16[72,1024]{1,0:T(8,128)(2,1)S(1)} %get-tuple-element.34), channel_id=1, source_target_pairs={{0,16},{1,9},{2,18},{3,11},{4,20},{5,13},{6,22},{7,15},{8,24},{9,1... | collective-permute-start | bytes 442376 | tf_op jit(solution)/shard_map/ppermute | solution.py:234
  16.0 6.3 %collective-permute-start.5 = (bf16[72,1024]{1,0:T(8,128)(2,1)S(1)}, bf16[72,1024]{1,0:T(8,128)(2,1)S(1)}, u32[]{:S(2)}, u32[]{:S(2)}) collective-permute-start(bf16[72,1024]{1,0:T(8,128)(2,1)S(1)} %get-tuple-element.35), channel_id=1, source_target_pairs={{0,8},{1,17},{2,10},{3,19},{4,12},{5,21},{6,14},{7,23},{8,0},{9,25... | collective-permute-start | bytes 442376 | tf_op jit(solution)/shard_map/ppermute | solution.py:234
  16.5 8.3 %collective-permute-start.6 = (bf16[72,1024]{1,0:T(8,128)(2,1)S(1)}, bf16[72,1024]{1,0:T(8,128)(2,1)S(1)}, u32[]{:S(2)}, u32[]{:S(2)}) collective-permute-start(bf16[72,1024]{1,0:T(8,128)(2,1)S(1)} %get-tuple-element.36), channel_id=1, source_target_pairs={{0,24},{1,25},{2,26},{3,27},{4,28},{5,29},{6,30},{7,31},{8,16},{9,... | collective-permute-start | bytes 442376 | tf_op jit(solution)/shard_map/ppermute | solution.py:234
  24.9 9.8 %copy-start.5 = (s32[8]{0:T(128)S(1)}, s32[8]{0:T(128)}, u32[]{:S(2)}) copy-start(s32[8]{0:T(128)} %block_map.1) | copy-start | bytes 100
  24.9 9.8 %copy-start.6 = (s32[4]{0:T(128)S(1)}, s32[4]{0:T(128)}, u32[]{:S(2)}) copy-start(s32[4]{0:T(128)} %lengths.1) | copy-start | bytes 52
  24.9 6.4 %collective-permute-start.9 = (bf16[64,1024]{1,0:T(8,128)(2,1)S(1)}, bf16[64,1024]{1,0:T(8,128)(2,1)S(1)}, u32[]{:S(2)}, u32[]{:S(2)}) collective-permute-start(bf16[64,1024]{1,0:T(8,128)(2,1)S(1)} %get-tuple-element.37.refs_0_), channel_id=1, source_target_pairs={{0,16},{1,9},{2,18},{3,11},{4,20},{5,13},{6,22},{7,15},{8,24},{9,1... | collective-permute-start | bytes 393224 | tf_op jit(solution)/shard_map/ppermute | solution.py:234
  25.9 5.4 %collective-permute-start.8 = (bf16[64,1024]{1,0:T(8,128)(2,1)S(1)}, bf16[64,1024]{1,0:T(8,128)(2,1)S(1)}, u32[]{:S(2)}, u32[]{:S(2)}) collective-permute-start(bf16[64,1024]{1,0:T(8,128)(2,1)S(1)} %get-tuple-element.37.refs_0_), channel_id=1, source_target_pairs={{0,8},{1,17},{2,10},{3,19},{4,12},{5,21},{6,14},{7,23},{8,0},{9,25... | collective-permute-start | bytes 393224 | tf_op jit(solution)/shard_map/ppermute | solution.py:234
  27.1 6.3 %collective-permute-start.7 = (bf16[64,1024]{1,0:T(8,128)(2,1)S(1)}, bf16[64,1024]{1,0:T(8,128)(2,1)S(1)}, u32[]{:S(2)}, u32[]{:S(2)}) collective-permute-start(bf16[64,1024]{1,0:T(8,128)(2,1)S(1)} %get-tuple-element.37.refs_0_), channel_id=1, source_target_pairs={{0,24},{1,25},{2,26},{3,27},{4,28},{5,29},{6,30},{7,31},{8,16},{9,... | collective-permute-start | bytes 393224 | tf_op jit(solution)/shard_map/ppermute | solution.py:234
  28.4 4.9 %collective-permute-start.10 = (bf16[64,1024]{1,0:T(8,128)(2,1)S(1)}, bf16[64,1024]{1,0:T(8,128)(2,1)S(1)}, u32[]{:S(2)}, u32[]{:S(2)}) collective-permute-start(bf16[64,1024]{1,0:T(8,128)(2,1)S(1)} %get-tuple-element.37.refs_0_), channel_id=1, source_target_pairs={{0,1},{1,0},{2,3},{3,2},{4,5},{5,4},{6,7},{7,6},{8,9},{9,8},{10,11... | collective-permute-start | bytes 393224 | tf_op jit(solution)/shard_map/ppermute | solution.py:227
  31.3 2.0 %collective-permute-start.13 = (bf16[64,1024]{1,0:T(8,128)(2,1)S(1)}, bf16[64,1024]{1,0:T(8,128)(2,1)S(1)}, u32[]{:S(2)}, u32[]{:S(2)}) collective-permute-start(bf16[64,1024]{1,0:T(8,128)(2,1)S(1)} %collective-permute-done.9.refs_3_), channel_id=1, source_target_pairs={{0,1},{1,0},{2,3},{3,2},{4,5},{5,4},{6,7},{7,6},{8,9},{9,8},{10,11... | collective-permute-start | bytes 393224 | tf_op jit(solution)/shard_map/ppermute | solution.py:227
  31.3 2.0 %collective-permute-start.12 = (bf16[64,1024]{1,0:T(8,128)(2,1)S(1)}, bf16[64,1024]{1,0:T(8,128)(2,1)S(1)}, u32[]{:S(2)}, u32[]{:S(2)}) collective-permute-start(bf16[64,1024]{1,0:T(8,128)(2,1)S(1)} %collective-permute-done.8.refs_2_), channel_id=1, source_target_pairs={{0,1},{1,0},{2,3},{3,2},{4,5},{5,4},{6,7},{7,6},{8,9},{9,8},{10,11... | collective-permute-start | bytes 393224 | tf_op jit(solution)/shard_map/ppermute | solution.py:227
  33.4 1.3 %collective-permute-start.11 = (bf16[64,1024]{1,0:T(8,128)(2,1)S(1)}, bf16[64,1024]{1,0:T(8,128)(2,1)S(1)}, u32[]{:S(2)}, u32[]{:S(2)}) collective-permute-start(bf16[64,1024]{1,0:T(8,128)(2,1)S(1)} %collective-permute-done.7.refs_1_), channel_id=1, source_target_pairs={{0,1},{1,0},{2,3},{3,2},{4,5},{5,4},{6,7},{7,6},{8,9},{9,8},{10,11... | collective-permute-start | bytes 393224 | tf_op jit(solution)/shard_map/ppermute | solution.py:227
  37.6 5.4 %collective-permute-start.21 = (bf16[72,512]{1,0:T(8,128)(2,1)S(1)}, bf16[72,512]{1,0:T(8,128)(2,1)S(1)}, u32[]{:S(2)}, u32[]{:S(2)}) collective-permute-start(bf16[72,512]{1,0:T(8,128)(2,1)S(1)} %get-tuple-element.49), channel_id=1, source_target_pairs={{0,16},{1,9},{2,18},{3,11},{4,20},{5,13},{6,22},{7,15},{8,24},{9,1... | collective-permute-start | bytes 221192 | tf_op jit(solution)/shard_map/ppermute | solution.py:234
  39.0 5.7 %collective-permute-start.22 = (bf16[72,512]{1,0:T(8,128)(2,1)S(1)}, bf16[72,512]{1,0:T(8,128)(2,1)S(1)}, u32[]{:S(2)}, u32[]{:S(2)}) collective-permute-start(bf16[72,512]{1,0:T(8,128)(2,1)S(1)} %get-tuple-element.50), channel_id=1, source_target_pairs={{0,8},{1,17},{2,10},{3,19},{4,12},{5,21},{6,14},{7,23},{8,0},{9,25... | collective-permute-start | bytes 221192 | tf_op jit(solution)/shard_map/ppermute | solution.py:234
  39.5 6.4 %collective-permute-start.23 = (bf16[72,512]{1,0:T(8,128)(2,1)S(1)}, bf16[72,512]{1,0:T(8,128)(2,1)S(1)}, u32[]{:S(2)}, u32[]{:S(2)}) collective-permute-start(bf16[72,512]{1,0:T(8,128)(2,1)S(1)} %get-tuple-element.51), channel_id=1, source_target_pairs={{0,24},{1,25},{2,26},{3,27},{4,28},{5,29},{6,30},{7,31},{8,16},{9,... | collective-permute-start | bytes 221192 | tf_op jit(solution)/shard_map/ppermute | solution.py:234
  41.1 9.6 %collective-permute-start.15 = (bf16[72,512]{1,0:T(8,128)(2,1)S(1)}, bf16[72,512]{1,0:T(8,128)(2,1)S(1)}, u32[]{:S(2)}, u32[]{:S(2)}) collective-permute-start(bf16[72,512]{1,0:T(8,128)(2,1)S(1)} %get-tuple-element.41), channel_id=1, source_target_pairs={{0,16},{1,9},{2,18},{3,11},{4,20},{5,13},{6,22},{7,15},{8,24},{9,1... | collective-permute-start | bytes 221192 | tf_op jit(solution)/shard_map/ppermute | solution.py:234
  42.4 8.8 %collective-permute-start.16 = (bf16[72,512]{1,0:T(8,128)(2,1)S(1)}, bf16[72,512]{1,0:T(8,128)(2,1)S(1)}, u32[]{:S(2)}, u32[]{:S(2)}) collective-permute-start(bf16[72,512]{1,0:T(8,128)(2,1)S(1)} %get-tuple-element.42), channel_id=1, source_target_pairs={{0,8},{1,17},{2,10},{3,19},{4,12},{5,21},{6,14},{7,23},{8,0},{9,25... | collective-permute-start | bytes 221192 | tf_op jit(solution)/shard_map/ppermute | solution.py:234
  43.0 8.2 %collective-permute-start.17 = (bf16[72,512]{1,0:T(8,128)(2,1)S(1)}, bf16[72,512]{1,0:T(8,128)(2,1)S(1)}, u32[]{:S(2)}, u32[]{:S(2)}) collective-permute-start(bf16[72,512]{1,0:T(8,128)(2,1)S(1)} %get-tuple-element.43), channel_id=1, source_target_pairs={{0,24},{1,25},{2,26},{3,27},{4,28},{5,29},{6,30},{7,31},{8,16},{9,... | collective-permute-start | bytes 221192 | tf_op jit(solution)/shard_map/ppermute | solution.py:234
  46.0 9.3 %collective-permute-start.24 = (bf16[72,512]{1,0:T(8,128)(2,1)S(1)}, bf16[72,512]{1,0:T(8,128)(2,1)S(1)}, u32[]{:S(2)}, u32[]{:S(2)}) collective-permute-start(bf16[72,512]{1,0:T(8,128)(2,1)S(1)} %get-tuple-element.53), channel_id=1, source_target_pairs={{0,2},{1,3},{2,0},{3,1},{4,6},{5,7},{6,4},{7,5},{8,10},{9,11},{10,... | collective-permute-start | bytes 221192 | tf_op jit(solution)/shard_map/ppermute | solution.py:230
  48.1 9.5 %collective-permute-start.25 = (bf16[72,512]{1,0:T(8,128)(2,1)S(1)}, bf16[72,512]{1,0:T(8,128)(2,1)S(1)}, u32[]{:S(2)}, u32[]{:S(2)}) collective-permute-start(bf16[72,512]{1,0:T(8,128)(2,1)S(1)} %get-tuple-element.54), channel_id=1, source_target_pairs={{0,4},{1,5},{2,6},{3,7},{4,0},{5,1},{6,2},{7,3},{8,12},{9,13},{10,... | collective-permute-start | bytes 221192 | tf_op jit(solution)/shard_map/ppermute | solution.py:230
  50.7 7.0 %collective-permute-start.26 = (bf16[72,512]{1,0:T(8,128)(2,1)S(1)}, bf16[72,512]{1,0:T(8,128)(2,1)S(1)}, u32[]{:S(2)}, u32[]{:S(2)}) collective-permute-start(bf16[72,512]{1,0:T(8,128)(2,1)S(1)} %get-tuple-element.55), channel_id=1, source_target_pairs={{0,6},{1,7},{2,4},{3,5},{4,2},{5,3},{6,0},{7,1},{8,14},{9,15},{10,... | collective-permute-start | bytes 221192 | tf_op jit(solution)/shard_map/ppermute | solution.py:230
  51.3 6.5 %collective-permute-start.18 = (bf16[72,512]{1,0:T(8,128)(2,1)S(1)}, bf16[72,512]{1,0:T(8,128)(2,1)S(1)}, u32[]{:S(2)}, u32[]{:S(2)}) collective-permute-start(bf16[72,512]{1,0:T(8,128)(2,1)S(1)} %get-tuple-element.45), channel_id=1, source_target_pairs={{0,2},{1,3},{2,0},{3,1},{4,6},{5,7},{6,4},{7,5},{8,10},{9,11},{10,... | collective-permute-start | bytes 221192 | tf_op jit(solution)/shard_map/ppermute | solution.py:230
  51.8 10.3 %collective-permute-start.19 = (bf16[72,512]{1,0:T(8,128)(2,1)S(1)}, bf16[72,512]{1,0:T(8,128)(2,1)S(1)}, u32[]{:S(2)}, u32[]{:S(2)}) collective-permute-start(bf16[72,512]{1,0:T(8,128)(2,1)S(1)} %get-tuple-element.46), channel_id=1, source_target_pairs={{0,4},{1,5},{2,6},{3,7},{4,0},{5,1},{6,2},{7,3},{8,12},{9,13},{10,... | collective-permute-start | bytes 221192 | tf_op jit(solution)/shard_map/ppermute | solution.py:230
  55.3 6.8 %collective-permute-start.20 = (bf16[72,512]{1,0:T(8,128)(2,1)S(1)}, bf16[72,512]{1,0:T(8,128)(2,1)S(1)}, u32[]{:S(2)}, u32[]{:S(2)}) collective-permute-start(bf16[72,512]{1,0:T(8,128)(2,1)S(1)} %get-tuple-element.47), channel_id=1, source_target_pairs={{0,6},{1,7},{2,4},{3,5},{4,2},{5,3},{6,0},{7,1},{8,14},{9,15},{10,... | collective-permute-start | bytes 221192 | tf_op jit(solution)/shard_map/ppermute | solution.py:230
  57.7 4.4 %collective-permute-start.27 = (bf16[64,512]{1,0:T(8,128)(2,1)S(1)}, bf16[64,512]{1,0:T(8,128)(2,1)S(1)}, u32[]{:S(2)}, u32[]{:S(2)}) collective-permute-start(bf16[64,512]{1,0:T(8,128)(2,1)S(1)} %sum_heads.1), channel_id=1, source_target_pairs={{0,1},{1,0},{2,3},{3,2},{4,5},{5,4},{6,7},{7,6},{8,9},{9,8},{10,11... | collective-permute-start | bytes 196616 | tf_op jit(solution)/shard_map/ppermute | solution.py:227
  (3 other events, 3.7 us)

commit v7 on v6

--- a/solution.py
+++ b/solution.py
@@ -43,7 +43,7 @@
 
 def project_kernel(parts_of, *refs):
     blocks, (new, own, other), refs = turned(refs[:4]), refs[4:7], refs[7:]
-    (held, new_held), outs, inputs = refs[:2], refs[2:5], refs[5]
+    held, held_second, new_held, send, inputs = refs
     rows = held.shape[0]
     count = new.shape[0]
     pad = new_held.shape[0]
@@ -58,25 +58,32 @@
         weight = jnp.concatenate([own[:, start:stop], other[:, start:stop]], axis=1)
         part = jnp.dot(x, weight, preferred_element_type=jnp.float32)
         to = slice(column, column + weight.shape[1])
-        held[:, to] = part[:rows]
+        own_rows, first, second, both = (part[i * rows : (i + 1) * rows] for i in range(4))
+        held[:, to] = own_rows
+        held_second[:, to] = second
         news = part[tail : tail + pad].astype(new_held.dtype)
         new_held[:, to] = news
-        for step, out in enumerate(outs, 1):
-            out[:rows, to] = part[step * rows : (step + 1) * rows].astype(out.dtype)
-            out[rows:, to] = news
+        send[:rows, to] = first.astype(send.dtype)
+        send[rows : 2 * rows, to] = both.astype(send.dtype)
+        send[2 * rows :, to] = news
         column += weight.shape[1]
 
 
-def add_kernel(own, new_own, first, second, both, held, new):
+def add_pair_kernel(held, held_second, new_held, got, out, new_out, send):
     rows = held.shape[0]
-
-    def total(own, at):
-        parts = [own[...].astype(jnp.float32)]
-        parts += [ref[at, :].astype(jnp.float32) for ref in (first, second, both)]
-        return ((parts[0] + parts[1]) + (parts[2] + parts[3])).astype(held.dtype)
-
-    held[...] = total(own, slice(0, rows))
-    new[...] = total(new_own, slice(rows, None))
+    out[...] = held[...] + got[:rows].astype(jnp.float32)
+    second = held_second[...] + got[rows : 2 * rows].astype(jnp.float32)
+    send[:rows, :] = second.astype(send.dtype)
+    news = new_held[...].astype(jnp.float32) + got[2 * rows :].astype(jnp.float32)
+    new_out[...] = news.astype(new_out.dtype)
+    send[rows:, :] = news.astype(send.dtype)
+
+
+def add_last_kernel(part, new_part, got, held, new):
+    rows = held.shape[0]
+    held[...] = (part[...] + got[:rows].astype(jnp.float32)).astype(held.dtype)
+    news = new_part[...].astype(jnp.float32) + got[rows:].astype(jnp.float32)
+    new[...] = news.astype(new.dtype)
 
 
 def request_of(position, ends):
@@ -179,9 +186,11 @@
 
 
 def relay_kernel(*refs):
-    blocks, outs = refs[:4], refs[4:]
+    blocks, (held, held_second, send) = refs[:4], refs[4:]
     c, z, k = place()
-    for slot, out in enumerate(outs):
+    rows = held.shape[0]
+    slots = (held, send.at[:rows], held_second, send.at[rows:])
+    for slot, out in enumerate(slots):
         for mask, block in zip(partners(k), blocks):
 
             @pl.when((c ^ z ^ slot) == mask)
@@ -189,21 +198,21 @@
                 out[...] = block[...]
 
 
-def sum_heads(parts):
-    terms = [part[...].astype(jnp.float32) for part in parts]
-    return ((terms[0] + terms[1]) + (terms[2] + terms[3])).astype(jnp.bfloat16)
-
-
-def sum_kernel(*refs):
-    send = refs[-1]
-    send[...] = sum_heads(refs[:-1])[: send.shape[0]]
-
-
-def finish_kernel(*refs):
-    parts, (other, prefill, decode) = refs[:4], refs[4:]
+def add_heads_kernel(held, held_second, got, out, send):
+    rows = held.shape[0]
+    out[...] = held[...].astype(jnp.float32) + got[:rows].astype(jnp.float32)
+    second = held_second[...].astype(jnp.float32) + got[rows:].astype(jnp.float32)
+    send[...] = second.astype(send.dtype)
+
+
+def sum_kernel(held, got, send):
+    send[...] = (held[...] + got[...].astype(jnp.float32))[: send.shape[0]].astype(send.dtype)
+
+
+def finish_kernel(held, got, other, prefill, decode):
     _, _, k = place()
     rows = other.shape[0]
-    total = sum_heads(parts)
+    total = (held[...] + got[...].astype(jnp.float32)).astype(prefill.dtype)
     prefill[pl.ds(pl.multiple_of(k * rows, rows), rows), :] = total[:rows]
     prefill[pl.ds(pl.multiple_of((1 - k) * rows, rows), rows), :] = other[...]
     decode[...] = total[rows : rows + decode.shape[0]]
@@ -258,27 +267,34 @@
     (own,) = call(pack_kernel, "pack_weights", weights, [((depth, features // 2), bf16)])
     other = to_core(own)
 
-    part_shape = (rows + pad, features)
     x_rows = -(-(steps * rows + pad) // 16) * 16
     edges = [0, q_width // 2, (q_width + kv_width) // 2, features // 2]
-    own_part, new_part, *parts = call(
+    own_part, second_part, new_part, send = call(
         functools.partial(project_kernel, list(zip(edges, edges[1:]))),
         "project",
         (*turned(blocks), new_columns, own, other),
-        [((rows, features), f32), ((pad, features), bf16)] + [(part_shape, bf16)] * (steps - 1),
+        [((rows, features), f32)] * 2
+        + [((pad, features), bf16), ((2 * rows + pad, features), bf16)],
         [pltpu.VMEM((x_rows, depth), bf16)],
     )
-
     w_out_later, _ = lax.optimization_barrier((w_out, new_part))
     w_other = to_core(w_out_later)
 
+    own_part, new_part, send = call(
+        add_pair_kernel,
+        "add_pair",
+        (own_part, second_part, new_part, to_partner(send, 1)),
+        [((rows, features), f32), ((pad, features), bf16), ((rows + pad, features), bf16)],
+    )
     held, new = call(
-        add_kernel,
-        "add_parts",
-        (own_part, new_part, *to_partners(parts)),
+        add_last_kernel,
+        "add_last",
+        (own_part, new_part, to_partner(send, 2)),
         [((rows, features), bf16), ((pad, features), bf16)],
     )
-    mine = [held] + to_partners([held] * (steps - 1))
+
+    first = to_partner(held, 1)
+    mine = [held, first, to_partner(held, 2), to_partner(first, 2)]
     theirs = [to_core(value) for value in mine]
 
     k_rows = -(-(2 * steps * rows + pad) // 128) * 128
@@ -300,19 +316,26 @@
 
     halves = []
     for half in (outs[:steps], outs[steps:]):
-        got = [half[0]] + to_partners(half[1:])
-        slots = call(relay_kernel, "relay", got, [(block, bf16)] * steps)
-        halves.append(
-            [slots[0]] + [to_chip(slot, step) for step, slot in enumerate(slots[1:], 1)]
-        )
-    shape = (rows, out_width // 2)
-    (send,) = call(sum_kernel, "sum_heads", halves[0], [(shape, bf16)])
+        held, second, send = call(
+            relay_kernel,
+            "relay",
+            [half[0]] + to_partners(half[1:]),
+            [(block, bf16)] * 2 + [((2 * block[0], block[1]), bf16)],
+        )
+        held, send = call(
+            add_heads_kernel,
+            "add_heads",
+            (held, second, to_chip(send, 1)),
+            [(block, f32), (block, bf16)],
+        )
+        halves.append((held, to_chip(send, 2)))
+    (send,) = call(sum_kernel, "sum_heads", halves[0], [((rows, block[1]), bf16)])
     return tuple(
         call(
             finish_kernel,
             "finish",
             (*halves[1], to_core(send)),
-            [((2 * rows, out_width // 2), bf16), ((count, out_width // 2), bf16)],
+            [((2 * rows, block[1]), bf16), ((count, block[1]), bf16)],
         )
     )
 

time: 63 us -> 66.5 us (1.056)
  waiting for transfers between devices: 26 us -> 32.8 us
  starting transfers between devices: 29.6 us -> 26.6 us
    ppermute x15 -> x14, waiting for transfers between devices: 19 us -> 24.5 us  [to_partner(): return lax.ppermute(value, ('ctx', 'tp'), pairs)]
    ppermute x6 -> x4, starting transfers between devices: 10.2 us -> 7.9 us  [to_chip(): return lax.ppermute(value, 'tp', [(i, i ^ 2 * step) for i in range(tp)])]
    ppermute x6 -> x4, waiting for transfers between devices: 5.64 us -> 6.42 us  [to_chip(): return lax.ppermute(value, 'tp', [(i, i ^ 2 * step) for i in range(tp)])]
    ppermute x15 -> x14, starting transfers between devices: 18.2 us -> 17.6 us  [to_partner(): return lax.ppermute(value, ('ctx', 'tp'), pairs)]
    pallas_call x8 -> x11, Pallas kernels: 4.64 us -> 4.67 us  [call(): pl.pallas_call(kernel, out_shape=[jax.ShapeDtypeStruct(shape, kind) for s...]
  transfers between devices with their start and end apart: 28 -> 25, of which waited for: 11 -> 13; matrix products, arithmetic and copies ran while one was open for 0% -> 0% of each run, Pallas kernels for 0% -> 0%
where the time goes in v7:
time: 66.5 us; the launch traced here: 66.4 us
  waiting for transfers between devices  32.8 us (49%)
  starting transfers between devices  26.6 us (40%)
  Pallas kernels  4.67 us (7%)
  local copies, waits for them, and re-layouts  1.45 us (2%)
  between operations  0.83 us (1%)
    ppermute x14, waiting for transfers between devices, to_partner(): return lax.ppermute(value, ('ctx', 'tp'), pairs)  24.5 us
    ppermute x14, starting transfers between devices, to_partner(): return lax.ppermute(value, ('ctx', 'tp'), pairs)  17.6 us
    ppermute x4, starting transfers between devices, to_chip(): return lax.ppermute(value, 'tp', [(i, i ^ 2 * step) for i in range(tp)])  7.9 us
    ppermute x4, waiting for transfers between devices, to_chip(): return lax.ppermute(value, 'tp', [(i, i ^ 2 * step) for i in range(tp)])  6.42 us
    pallas_call x11, Pallas kernels, call(): pl.pallas_call(kernel, out_shape=[jax.ShapeDtypeStruct(shape, kind) for s...  4.67 us
    ppermute x7, waiting for transfers between devices, to_core(): return lax.ppermute(value, 'tp', [(i, i ^ 1) for i in range(tp)])  1.87 us
  transfers between devices with their start and end apart: 25, of which 13 were waited for; matrix products, arithmetic and copies ran while one was open for 0% of the time, Pallas kernels for 0%

profile of v7, /device:TPU:0, one launch (start us, length us, event | category | flops | bytes accessed | tf_op | source)
XLA Modules:
  0.0 66.4 jit_solution(8457346332614610969)
XLA Ops:
  0.7 1.2 %fusion = (bf16[64,1024]{1,0:T(8,128)(2,1)S(1)}, bf16[64,1024]{1,0:T(8,128)(2,1)S(1)}, bf16[64,1024]{1,0:T(8,128)(2,1)S(1)}, bf16[64,1024]{1,0:T(8,128)(2,1)S(1)}) fusion(bf16[128,4096]{1,0:T(8,128)(2,1)} %param.8, s32[]{:T(128)S(6)} %select_n.27, s32[]{:T(128)S(6)} %select_n.31, s32[]{:T(128)S(6)} %select_n.29, s32[]{:T(128)S(6)} %select_n.28, s32[]{:T(128)S(6)} %select_n.30), kind=kLoop, calls=%fused_computation.1 | loop fusion | bytes 1048596 | tf_op jit(solution)/shard_map/dynamic_slice | solution.py:261
  2.7 3.5 %collective-permute-start = (bf16[64,1024]{1,0:T(8,128)(2,1)S(1)}, bf16[64,1024]{1,0:T(8,128)(2,1)S(1)}, u32[]{:S(2)}, u32[]{:S(2)}) collective-permute-start(bf16[64,1024]{1,0:T(8,128)(2,1)S(1)} %get-tuple-element.65), channel_id=1, source_target_pairs={{0,24},{1,25},{2,26},{3,27},{4,28},{5,29},{6,30},{7,31},{8,16},{9,... | collective-permute-start | bytes 393224 | tf_op jit(solution)/shard_map/ppermute | solution.py:243
  6.9 3.5 %collective-permute-done.refs_1_ = bf16[64,1024]{1,0:T(8,128)(2,1)S(1)} collective-permute-done((bf16[64,1024]{1,0:T(8,128)(2,1)S(1)}, bf16[64,1024]{1,0:T(8,128)(2,1)S(1)}, u32[]{:S(2)}, u32[]{:S(2)}) %collective-permute-start) | collective-permute-done | bytes 131104 | tf_op jit(solution)/shard_map/ppermute | solution.py:243
  10.4 3.0 %collective-permute-done.1.refs_2_ = bf16[64,1024]{1,0:T(8,128)(2,1)S(1)} collective-permute-done((bf16[64,1024]{1,0:T(8,128)(2,1)S(1)}, bf16[64,1024]{1,0:T(8,128)(2,1)S(1)}, u32[]{:S(2)}, u32[]{:S(2)}) %collective-permute-start.1) | collective-permute-done | bytes 131104 | tf_op jit(solution)/shard_map/ppermute | solution.py:243
  13.5 0.7 %project.1 = (f32[64,1024]{1,0:T(8,128)S(1)}, f32[64,1024]{1,0:T(8,128)S(1)}, bf16[8,1024]{1,0:T(8,128)(2,1)S(1)}, bf16[136,1024]{1,0:T(8,128)(2,1)S(1)}) custom-call(bf16[64,1024]{1,0:T(8,128)(2,1)S(1)} %get-tuple-element.66.refs_0_, bf16[64,1024]{1,0:T(8,128)(2,1)S(1)} %collective-permute-done.refs_1_, ...), custom_call_target="tpu_custom_call" | custom-call | tf_op jit(solution)/shard_map/project/pallas_call | solution.py:249
  14.2 1.5 %collective-permute-start.4 = (bf16[136,1024]{1,0:T(8,128)(2,1)S(1)}, bf16[136,1024]{1,0:T(8,128)(2,1)S(1)}, u32[]{:S(2)}, u32[]{:S(2)}) collective-permute-start(bf16[136,1024]{1,0:T(8,128)(2,1)S(1)} %get-tuple-element.39), channel_id=1, source_target_pairs={{0,16},{1,9},{2,18},{3,11},{4,20},{5,13},{6,22},{7,15},{8,24},{9,1... | collective-permute-start | bytes 835592 | tf_op jit(solution)/shard_map/ppermute | solution.py:243
  15.7 5.1 %collective-permute-done.4.got = bf16[136,1024]{1,0:T(8,128)(2,1)S(1)} collective-permute-done((bf16[136,1024]{1,0:T(8,128)(2,1)S(1)}, bf16[136,1024]{1,0:T(8,128)(2,1)S(1)}, u32[]{:S(2)}, u32[]{:S(2)}) %collective-permute-start.4) | collective-permute-done | bytes 278560 | tf_op jit(solution)/shard_map/ppermute | solution.py:243
  20.9 1.6 %collective-permute-start.5 = (bf16[72,1024]{1,0:T(8,128)(2,1)S(1)}, bf16[72,1024]{1,0:T(8,128)(2,1)S(1)}, u32[]{:S(2)}, u32[]{:S(2)}) collective-permute-start(bf16[72,1024]{1,0:T(8,128)(2,1)S(1)} %get-tuple-element.42), channel_id=1, source_target_pairs={{0,8},{1,17},{2,10},{3,19},{4,12},{5,21},{6,14},{7,23},{8,0},{9,25... | collective-permute-start | bytes 442376 | tf_op jit(solution)/shard_map/ppermute | solution.py:243
  22.5 3.6 %collective-permute-done.5.got = bf16[72,1024]{1,0:T(8,128)(2,1)S(1)} collective-permute-done((bf16[72,1024]{1,0:T(8,128)(2,1)S(1)}, bf16[72,1024]{1,0:T(8,128)(2,1)S(1)}, u32[]{:S(2)}, u32[]{:S(2)}) %collective-permute-start.5) | collective-permute-done | bytes 147488 | tf_op jit(solution)/shard_map/ppermute | solution.py:243
  26.2 1.5 %collective-permute-start.6 = (bf16[64,1024]{1,0:T(8,128)(2,1)S(1)}, bf16[64,1024]{1,0:T(8,128)(2,1)S(1)}, u32[]{:S(2)}, u32[]{:S(2)}) collective-permute-start(bf16[64,1024]{1,0:T(8,128)(2,1)S(1)} %get-tuple-element.43.refs_0_), channel_id=1, source_target_pairs={{0,16},{1,9},{2,18},{3,11},{4,20},{5,13},{6,22},{7,15},{8,24},{9,1... | collective-permute-start | bytes 393224 | tf_op jit(solution)/shard_map/ppermute | solution.py:243
  27.7 0.6 collective-permute-start.8
  28.2 3.9 %collective-permute-done.6.refs_3_ = bf16[64,1024]{1,0:T(8,128)(2,1)S(1)} collective-permute-done((bf16[64,1024]{1,0:T(8,128)(2,1)S(1)}, bf16[64,1024]{1,0:T(8,128)(2,1)S(1)}, u32[]{:S(2)}, u32[]{:S(2)}) %collective-permute-start.6) | collective-permute-done | bytes 131104 | tf_op jit(solution)/shard_map/ppermute | solution.py:243
  32.1 1.3 %collective-permute-start.7 = (bf16[64,1024]{1,0:T(8,128)(2,1)S(1)}, bf16[64,1024]{1,0:T(8,128)(2,1)S(1)}, u32[]{:S(2)}, u32[]{:S(2)}) collective-permute-start(bf16[64,1024]{1,0:T(8,128)(2,1)S(1)} %collective-permute-done.6.refs_3_), channel_id=1, source_target_pairs={{0,8},{1,17},{2,10},{3,19},{4,12},{5,21},{6,14},{7,23},{8,0},{9,25... | collective-permute-start | bytes 393224 | tf_op jit(solution)/shard_map/ppermute | solution.py:243
  34.0 3.1 %collective-permute-done.7.refs_1_ = bf16[64,1024]{1,0:T(8,128)(2,1)S(1)} collective-permute-done((bf16[64,1024]{1,0:T(8,128)(2,1)S(1)}, bf16[64,1024]{1,0:T(8,128)(2,1)S(1)}, u32[]{:S(2)}, u32[]{:S(2)}) %collective-permute-start.7) | collective-permute-done | bytes 131104 | tf_op jit(solution)/shard_map/ppermute | solution.py:243
  37.1 1.3 %collective-permute-done.10.refs_5_ = bf16[64,1024]{1,0:T(8,128)(2,1)S(1)} collective-permute-done((bf16[64,1024]{1,0:T(8,128)(2,1)S(1)}, bf16[64,1024]{1,0:T(8,128)(2,1)S(1)}, u32[]{:S(2)}, u32[]{:S(2)}) %collective-permute-start.10) | collective-permute-done | bytes 131104 | tf_op jit(solution)/shard_map/ppermute | solution.py:236
  38.5 2.9 %attend.1 = (bf16[72,512]{1,0:T(8,128)(2,1)S(1)}, bf16[72,512]{1,0:T(8,128)(2,1)S(1)}, bf16[72,512]{1,0:T(8,128)(2,1)S(1)}, bf16[72,512]{1,0:T(8,128)(2,1)S(1)},...) custom-call(s32[8]{0:T(128)S(1)} %copy-done.5, ...), custom_call_target="tpu_custom_call" | custom-call | tf_op jit(solution)/shard_map/attend/pallas_call | solution.py:249
  41.3 1.1 %collective-permute-start.19 = (bf16[72,512]{1,0:T(8,128)(2,1)S(1)}, bf16[72,512]{1,0:T(8,128)(2,1)S(1)}, u32[]{:S(2)}, u32[]{:S(2)}) collective-permute-start(bf16[72,512]{1,0:T(8,128)(2,1)S(1)} %get-tuple-element.56), channel_id=1, source_target_pairs={{0,16},{1,9},{2,18},{3,11},{4,20},{5,13},{6,22},{7,15},{8,24},{9,1... | collective-permute-start | bytes 221192 | tf_op jit(solution)/shard_map/ppermute | solution.py:243
  42.4 0.9 %collective-permute-start.20 = (bf16[72,512]{1,0:T(8,128)(2,1)S(1)}, bf16[72,512]{1,0:T(8,128)(2,1)S(1)}, u32[]{:S(2)}, u32[]{:S(2)}) collective-permute-start(bf16[72,512]{1,0:T(8,128)(2,1)S(1)} %get-tuple-element.57), channel_id=1, source_target_pairs={{0,8},{1,17},{2,10},{3,19},{4,12},{5,21},{6,14},{7,23},{8,0},{9,25... | collective-permute-start | bytes 221192 | tf_op jit(solution)/shard_map/ppermute | solution.py:243
  43.3 1.5 %collective-permute-start.21 = (bf16[72,512]{1,0:T(8,128)(2,1)S(1)}, bf16[72,512]{1,0:T(8,128)(2,1)S(1)}, u32[]{:S(2)}, u32[]{:S(2)}) collective-permute-start(bf16[72,512]{1,0:T(8,128)(2,1)S(1)} %get-tuple-element.58), channel_id=1, source_target_pairs={{0,24},{1,25},{2,26},{3,27},{4,28},{5,29},{6,30},{7,31},{8,16},{9,... | collective-permute-start | bytes 221192 | tf_op jit(solution)/shard_map/ppermute | solution.py:243
  44.9 1.0 %collective-permute-start.14 = (bf16[72,512]{1,0:T(8,128)(2,1)S(1)}, bf16[72,512]{1,0:T(8,128)(2,1)S(1)}, u32[]{:S(2)}, u32[]{:S(2)}) collective-permute-start(bf16[72,512]{1,0:T(8,128)(2,1)S(1)} %get-tuple-element.47), channel_id=1, source_target_pairs={{0,16},{1,9},{2,18},{3,11},{4,20},{5,13},{6,22},{7,15},{8,24},{9,1... | collective-permute-start | bytes 221192 | tf_op jit(solution)/shard_map/ppermute | solution.py:243
  45.9 0.9 %collective-permute-start.15 = (bf16[72,512]{1,0:T(8,128)(2,1)S(1)}, bf16[72,512]{1,0:T(8,128)(2,1)S(1)}, u32[]{:S(2)}, u32[]{:S(2)}) collective-permute-start(bf16[72,512]{1,0:T(8,128)(2,1)S(1)} %get-tuple-element.48), channel_id=1, source_target_pairs={{0,8},{1,17},{2,10},{3,19},{4,12},{5,21},{6,14},{7,23},{8,0},{9,25... | collective-permute-start | bytes 221192 | tf_op jit(solution)/shard_map/ppermute | solution.py:243
  46.8 1.5 %collective-permute-start.16 = (bf16[72,512]{1,0:T(8,128)(2,1)S(1)}, bf16[72,512]{1,0:T(8,128)(2,1)S(1)}, u32[]{:S(2)}, u32[]{:S(2)}) collective-permute-start(bf16[72,512]{1,0:T(8,128)(2,1)S(1)} %get-tuple-element.49), channel_id=1, source_target_pairs={{0,24},{1,25},{2,26},{3,27},{4,28},{5,29},{6,30},{7,31},{8,16},{9,... | collective-permute-start | bytes 221192 | tf_op jit(solution)/shard_map/ppermute | solution.py:243
  48.4 1.2 %collective-permute-done.21.refs_3_ = bf16[72,512]{1,0:T(8,128)(2,1)S(1)} collective-permute-done((bf16[72,512]{1,0:T(8,128)(2,1)S(1)}, bf16[72,512]{1,0:T(8,128)(2,1)S(1)}, u32[]{:S(2)}, u32[]{:S(2)}) %collective-permute-start.21) | collective-permute-done | bytes 73760 | tf_op jit(solution)/shard_map/ppermute | solution.py:243
  49.6 1.5 %collective-permute-start.22 = (bf16[144,512]{1,0:T(8,128)(2,1)S(1)}, bf16[144,512]{1,0:T(8,128)(2,1)S(1)}, u32[]{:S(2)}, u32[]{:S(2)}) collective-permute-start(bf16[144,512]{1,0:T(8,128)(2,1)S(1)} %get-tuple-element.61), channel_id=1, source_target_pairs={{0,2},{1,3},{2,0},{3,1},{4,6},{5,7},{6,4},{7,5},{8,10},{9,11},{10,... | collective-permute-start | bytes 442376 | tf_op jit(solution)/shard_map/ppermute | solution.py:239
  51.2 0.9 %collective-permute-done.16.refs_3_ = bf16[72,512]{1,0:T(8,128)(2,1)S(1)} collective-permute-done((bf16[72,512]{1,0:T(8,128)(2,1)S(1)}, bf16[72,512]{1,0:T(8,128)(2,1)S(1)}, u32[]{:S(2)}, u32[]{:S(2)}) %collective-permute-start.16) | collective-permute-done | bytes 73760 | tf_op jit(solution)/shard_map/ppermute | solution.py:243
  52.2 2.1 %collective-permute-start.17 = (bf16[144,512]{1,0:T(8,128)(2,1)S(1)}, bf16[144,512]{1,0:T(8,128)(2,1)S(1)}, u32[]{:S(2)}, u32[]{:S(2)}) collective-permute-start(bf16[144,512]{1,0:T(8,128)(2,1)S(1)} %get-tuple-element.52), channel_id=1, source_target_pairs={{0,2},{1,3},{2,0},{3,1},{4,6},{5,7},{6,4},{7,5},{8,10},{9,11},{10,... | collective-permute-start | bytes 442376 | tf_op jit(solution)/shard_map/ppermute | solution.py:239
  54.3 2.7 %collective-permute-done.22.got = bf16[144,512]{1,0:T(8,128)(2,1)S(1)} collective-permute-done((bf16[144,512]{1,0:T(8,128)(2,1)S(1)}, bf16[144,512]{1,0:T(8,128)(2,1)S(1)}, u32[]{:S(2)}, u32[]{:S(2)}) %collective-permute-start.22) | collective-permute-done | bytes 147488 | tf_op jit(solution)/shard_map/ppermute | solution.py:239
  57.0 1.8 %collective-permute-start.23 = (bf16[72,512]{1,0:T(8,128)(2,1)S(1)}, bf16[72,512]{1,0:T(8,128)(2,1)S(1)}, u32[]{:S(2)}, u32[]{:S(2)}) collective-permute-start(bf16[72,512]{1,0:T(8,128)(2,1)S(1)} %get-tuple-element.63), channel_id=1, source_target_pairs={{0,4},{1,5},{2,6},{3,7},{4,0},{5,1},{6,2},{7,3},{8,12},{9,13},{10,... | collective-permute-start | bytes 221192 | tf_op jit(solution)/shard_map/ppermute | solution.py:239
  58.8 2.5 %collective-permute-start.18 = (bf16[72,512]{1,0:T(8,128)(2,1)S(1)}, bf16[72,512]{1,0:T(8,128)(2,1)S(1)}, u32[]{:S(2)}, u32[]{:S(2)}) collective-permute-start(bf16[72,512]{1,0:T(8,128)(2,1)S(1)} %get-tuple-element.54), channel_id=1, source_target_pairs={{0,4},{1,5},{2,6},{3,7},{4,0},{5,1},{6,2},{7,3},{8,12},{9,13},{10,... | collective-permute-start | bytes 221192 | tf_op jit(solution)/shard_map/ppermute | solution.py:239
  61.3 3.0 %collective-permute-done.23.got = bf16[72,512]{1,0:T(8,128)(2,1)S(1)} collective-permute-done((bf16[72,512]{1,0:T(8,128)(2,1)S(1)}, bf16[72,512]{1,0:T(8,128)(2,1)S(1)}, u32[]{:S(2)}, u32[]{:S(2)}) %collective-permute-start.23) | collective-permute-done | bytes 73760 | tf_op jit(solution)/shard_map/ppermute | solution.py:239
  64.4 0.7 %collective-permute-done.18.got = bf16[72,512]{1,0:T(8,128)(2,1)S(1)} collective-permute-done((bf16[72,512]{1,0:T(8,128)(2,1)S(1)}, bf16[72,512]{1,0:T(8,128)(2,1)S(1)}, u32[]{:S(2)}, u32[]{:S(2)}) %collective-permute-start.18) | collective-permute-done | bytes 73760 | tf_op jit(solution)/shard_map/ppermute | solution.py:239
  65.7 0.7 %finish.1 = (bf16[128,512]{1,0:T(8,128)(2,1)}, bf16[4,512]{1,0:T(4,128)(2,1)}) custom-call(f32[72,512]{1,0:T(8,128)S(1)} %get-tuple-element.53.held, bf16[72,512]{1,0:T(8,128)(2,1)S(1)} %collective-permute-done.18.got, bf16[64,512]{1,0:T(8,128)(2,1)S(1)} %collective-permute-done.24.other), custom_call_target="tpu_custom_call" | custom-call | tf_op jit(solution)/shard_map/finish/pallas_call | solution.py:249
  (45 shorter events, 3.0 us)
Async XLA Ops:
  0.6 6.3 %copy-start = (bf16[4,4096]{1,0:T(4,128)(2,1)S(1)}, bf16[4,4096]{1,0:T(4,128)(2,1)}, u32[]{:S(2)}) copy-start(bf16[4,4096]{1,0:T(4,128)(2,1)} %param.9) | copy-start | bytes 98308
  0.7 1.3 %copy-start.1 = (bf16[1024,256]{1,0:T(8,128)(2,1)S(1)}, bf16[1024,256]{1,0:T(8,128)(2,1)}, u32[]{:S(2)}) copy-start(bf16[1024,256]{1,0:T(8,128)(2,1)} %refs_0_) | copy-start | bytes 1572868
  0.7 1.4 %copy-start.3 = (bf16[1024,128]{1,0:T(8,128)(2,1)S(1)}, bf16[1024,128]{1,0:T(8,128)(2,1)}, u32[]{:S(2)}) copy-start(bf16[1024,128]{1,0:T(8,128)(2,1)} %refs_1_) | copy-start | bytes 786436
  0.7 1.4 %copy-start.4 = (bf16[1024,128]{1,0:T(8,128)(2,1)S(1)}, bf16[1024,128]{1,0:T(8,128)(2,1)}, u32[]{:S(2)}) copy-start(bf16[1024,128]{1,0:T(8,128)(2,1)} %refs_2_) | copy-start | bytes 786436
  2.2 11.3 %collective-permute-start.3 = (bf16[1024,512]{1,0:T(8,128)(2,1)S(1)}, bf16[1024,512]{1,0:T(8,128)(2,1)S(1)}, u32[]{:S(2)}, u32[]{:S(2)}) collective-permute-start(bf16[1024,512]{1,0:T(8,128)(2,1)S(1)} %pack_weights.1.refs_5_), channel_id=1, source_target_pairs={{0,1},{1,0},{2,3},{3,2},{4,5},{5,4},{6,7},{7,6},{8,9},{9,8},{10,11... | collective-permute-start | bytes 3145736 | tf_op jit(solution)/shard_map/ppermute | solution.py:236
  2.7 7.7 %collective-permute-start = (bf16[64,1024]{1,0:T(8,128)(2,1)S(1)}, bf16[64,1024]{1,0:T(8,128)(2,1)S(1)}, u32[]{:S(2)}, u32[]{:S(2)}) collective-permute-start(bf16[64,1024]{1,0:T(8,128)(2,1)S(1)} %get-tuple-element.65), channel_id=1, source_target_pairs={{0,24},{1,25},{2,26},{3,27},{4,28},{5,29},{6,30},{7,31},{8,16},{9,... | collective-permute-start | bytes 393224 | tf_op jit(solution)/shard_map/ppermute | solution.py:243
  6.2 7.2 %collective-permute-start.1 = (bf16[64,1024]{1,0:T(8,128)(2,1)S(1)}, bf16[64,1024]{1,0:T(8,128)(2,1)S(1)}, u32[]{:S(2)}, u32[]{:S(2)}) collective-permute-start(bf16[64,1024]{1,0:T(8,128)(2,1)S(1)} %get-tuple-element.67), channel_id=1, source_target_pairs={{0,8},{1,17},{2,10},{3,19},{4,12},{5,21},{6,14},{7,23},{8,0},{9,25... | collective-permute-start | bytes 393224 | tf_op jit(solution)/shard_map/ppermute | solution.py:243
  6.8 6.7 %collective-permute-start.2 = (bf16[64,1024]{1,0:T(8,128)(2,1)S(1)}, bf16[64,1024]{1,0:T(8,128)(2,1)S(1)}, u32[]{:S(2)}, u32[]{:S(2)}) collective-permute-start(bf16[64,1024]{1,0:T(8,128)(2,1)S(1)} %get-tuple-element.64), channel_id=1, source_target_pairs={{0,16},{1,9},{2,18},{3,11},{4,20},{5,13},{6,22},{7,15},{8,24},{9,1... | collective-permute-start | bytes 393224 | tf_op jit(solution)/shard_map/ppermute | solution.py:243
  14.2 8.3 %copy-start.2 = (bf16[256,1024]{1,0:T(8,128)(2,1)S(1)}, bf16[256,1024]{1,0:T(8,128)(2,1)}, u32[]{:S(2)}) copy-start(bf16[256,1024]{1,0:T(8,128)(2,1)} %refs_9_.1) | copy-start | bytes 1572868
  14.2 6.6 %collective-permute-start.4 = (bf16[136,1024]{1,0:T(8,128)(2,1)S(1)}, bf16[136,1024]{1,0:T(8,128)(2,1)S(1)}, u32[]{:S(2)}, u32[]{:S(2)}) collective-permute-start(bf16[136,1024]{1,0:T(8,128)(2,1)S(1)} %get-tuple-element.39), channel_id=1, source_target_pairs={{0,16},{1,9},{2,18},{3,11},{4,20},{5,13},{6,22},{7,15},{8,24},{9,1... | collective-permute-start | bytes 835592 | tf_op jit(solution)/shard_map/ppermute | solution.py:243
  20.9 5.2 %collective-permute-start.5 = (bf16[72,1024]{1,0:T(8,128)(2,1)S(1)}, bf16[72,1024]{1,0:T(8,128)(2,1)S(1)}, u32[]{:S(2)}, u32[]{:S(2)}) collective-permute-start(bf16[72,1024]{1,0:T(8,128)(2,1)S(1)} %get-tuple-element.42), channel_id=1, source_target_pairs={{0,8},{1,17},{2,10},{3,19},{4,12},{5,21},{6,14},{7,23},{8,0},{9,25... | collective-permute-start | bytes 442376 | tf_op jit(solution)/shard_map/ppermute | solution.py:243
  22.5 14.6 %collective-permute-start.13 = (bf16[256,1024]{1,0:T(8,128)(2,1)S(1)}, bf16[256,1024]{1,0:T(8,128)(2,1)S(1)}, u32[]{:S(2)}, u32[]{:S(2)}) collective-permute-start(bf16[256,1024]{1,0:T(8,128)(2,1)S(1)} %copy-done.2), channel_id=1, source_target_pairs={{0,1},{1,0},{2,3},{3,2},{4,5},{5,4},{6,7},{7,6},{8,9},{9,8},{10,11... | collective-permute-start | bytes 1572872 | tf_op jit(solution)/shard_map/ppermute | solution.py:236
  26.2 12.3 %copy-start.5 = (s32[8]{0:T(128)S(1)}, s32[8]{0:T(128)}, u32[]{:S(2)}) copy-start(s32[8]{0:T(128)} %block_map.1) | copy-start | bytes 100
  26.2 12.3 %copy-start.6 = (s32[4]{0:T(128)S(1)}, s32[4]{0:T(128)}, u32[]{:S(2)}) copy-start(s32[4]{0:T(128)} %lengths.1) | copy-start | bytes 52
  26.2 5.9 %collective-permute-start.6 = (bf16[64,1024]{1,0:T(8,128)(2,1)S(1)}, bf16[64,1024]{1,0:T(8,128)(2,1)S(1)}, u32[]{:S(2)}, u32[]{:S(2)}) collective-permute-start(bf16[64,1024]{1,0:T(8,128)(2,1)S(1)} %get-tuple-element.43.refs_0_), channel_id=1, source_target_pairs={{0,16},{1,9},{2,18},{3,11},{4,20},{5,13},{6,22},{7,15},{8,24},{9,1... | collective-permute-start | bytes 393224 | tf_op jit(solution)/shard_map/ppermute | solution.py:243
  27.7 6.3 %collective-permute-start.8 = (bf16[64,1024]{1,0:T(8,128)(2,1)S(1)}, bf16[64,1024]{1,0:T(8,128)(2,1)S(1)}, u32[]{:S(2)}, u32[]{:S(2)}) collective-permute-start(bf16[64,1024]{1,0:T(8,128)(2,1)S(1)} %get-tuple-element.43.refs_0_), channel_id=1, source_target_pairs={{0,8},{1,17},{2,10},{3,19},{4,12},{5,21},{6,14},{7,23},{8,0},{9,25... | collective-permute-start | bytes 393224 | tf_op jit(solution)/shard_map/ppermute | solution.py:243
  32.1 5.0 %collective-permute-start.7 = (bf16[64,1024]{1,0:T(8,128)(2,1)S(1)}, bf16[64,1024]{1,0:T(8,128)(2,1)S(1)}, u32[]{:S(2)}, u32[]{:S(2)}) collective-permute-start(bf16[64,1024]{1,0:T(8,128)(2,1)S(1)} %collective-permute-done.6.refs_3_), channel_id=1, source_target_pairs={{0,8},{1,17},{2,10},{3,19},{4,12},{5,21},{6,14},{7,23},{8,0},{9,25... | collective-permute-start | bytes 393224 | tf_op jit(solution)/shard_map/ppermute | solution.py:243
  33.5 3.7 %collective-permute-start.9 = (bf16[64,1024]{1,0:T(8,128)(2,1)S(1)}, bf16[64,1024]{1,0:T(8,128)(2,1)S(1)}, u32[]{:S(2)}, u32[]{:S(2)}) collective-permute-start(bf16[64,1024]{1,0:T(8,128)(2,1)S(1)} %get-tuple-element.43.refs_0_), channel_id=1, source_target_pairs={{0,1},{1,0},{2,3},{3,2},{4,5},{5,4},{6,7},{7,6},{8,9},{9,8},{10,11... | collective-permute-start | bytes 393224 | tf_op jit(solution)/shard_map/ppermute | solution.py:236
  33.5 3.7 %collective-permute-start.12 = (bf16[64,1024]{1,0:T(8,128)(2,1)S(1)}, bf16[64,1024]{1,0:T(8,128)(2,1)S(1)}, u32[]{:S(2)}, u32[]{:S(2)}) collective-permute-start(bf16[64,1024]{1,0:T(8,128)(2,1)S(1)} %collective-permute-done.6.refs_3_), channel_id=1, source_target_pairs={{0,1},{1,0},{2,3},{3,2},{4,5},{5,4},{6,7},{7,6},{8,9},{9,8},{10,11... | collective-permute-start | bytes 393224 | tf_op jit(solution)/shard_map/ppermute | solution.py:236
  34.0 3.1 %collective-permute-start.11 = (bf16[64,1024]{1,0:T(8,128)(2,1)S(1)}, bf16[64,1024]{1,0:T(8,128)(2,1)S(1)}, u32[]{:S(2)}, u32[]{:S(2)}) collective-permute-start(bf16[64,1024]{1,0:T(8,128)(2,1)S(1)} %collective-permute-done.8.refs_2_), channel_id=1, source_target_pairs={{0,1},{1,0},{2,3},{3,2},{4,5},{5,4},{6,7},{7,6},{8,9},{9,8},{10,11... | collective-permute-start | bytes 393224 | tf_op jit(solution)/shard_map/ppermute | solution.py:236
  37.1 1.3 %collective-permute-start.10 = (bf16[64,1024]{1,0:T(8,128)(2,1)S(1)}, bf16[64,1024]{1,0:T(8,128)(2,1)S(1)}, u32[]{:S(2)}, u32[]{:S(2)}) collective-permute-start(bf16[64,1024]{1,0:T(8,128)(2,1)S(1)} %collective-permute-done.7.refs_1_), channel_id=1, source_target_pairs={{0,1},{1,0},{2,3},{3,2},{4,5},{5,4},{6,7},{7,6},{8,9},{9,8},{10,11... | collective-permute-start | bytes 393224 | tf_op jit(solution)/shard_map/ppermute | solution.py:236
  41.3 5.5 %collective-permute-start.19 = (bf16[72,512]{1,0:T(8,128)(2,1)S(1)}, bf16[72,512]{1,0:T(8,128)(2,1)S(1)}, u32[]{:S(2)}, u32[]{:S(2)}) collective-permute-start(bf16[72,512]{1,0:T(8,128)(2,1)S(1)} %get-tuple-element.56), channel_id=1, source_target_pairs={{0,16},{1,9},{2,18},{3,11},{4,20},{5,13},{6,22},{7,15},{8,24},{9,1... | collective-permute-start | bytes 221192 | tf_op jit(solution)/shard_map/ppermute | solution.py:243
  42.4 5.9 %collective-permute-start.20 = (bf16[72,512]{1,0:T(8,128)(2,1)S(1)}, bf16[72,512]{1,0:T(8,128)(2,1)S(1)}, u32[]{:S(2)}, u32[]{:S(2)}) collective-permute-start(bf16[72,512]{1,0:T(8,128)(2,1)S(1)} %get-tuple-element.57), channel_id=1, source_target_pairs={{0,8},{1,17},{2,10},{3,19},{4,12},{5,21},{6,14},{7,23},{8,0},{9,25... | collective-permute-start | bytes 221192 | tf_op jit(solution)/shard_map/ppermute | solution.py:243
  43.3 6.2 %collective-permute-start.21 = (bf16[72,512]{1,0:T(8,128)(2,1)S(1)}, bf16[72,512]{1,0:T(8,128)(2,1)S(1)}, u32[]{:S(2)}, u32[]{:S(2)}) collective-permute-start(bf16[72,512]{1,0:T(8,128)(2,1)S(1)} %get-tuple-element.58), channel_id=1, source_target_pairs={{0,24},{1,25},{2,26},{3,27},{4,28},{5,29},{6,30},{7,31},{8,16},{9,... | collective-permute-start | bytes 221192 | tf_op jit(solution)/shard_map/ppermute | solution.py:243
  44.9 6.3 %collective-permute-start.14 = (bf16[72,512]{1,0:T(8,128)(2,1)S(1)}, bf16[72,512]{1,0:T(8,128)(2,1)S(1)}, u32[]{:S(2)}, u32[]{:S(2)}) collective-permute-start(bf16[72,512]{1,0:T(8,128)(2,1)S(1)} %get-tuple-element.47), channel_id=1, source_target_pairs={{0,16},{1,9},{2,18},{3,11},{4,20},{5,13},{6,22},{7,15},{8,24},{9,1... | collective-permute-start | bytes 221192 | tf_op jit(solution)/shard_map/ppermute | solution.py:243
  45.9 5.2 %collective-permute-start.15 = (bf16[72,512]{1,0:T(8,128)(2,1)S(1)}, bf16[72,512]{1,0:T(8,128)(2,1)S(1)}, u32[]{:S(2)}, u32[]{:S(2)}) collective-permute-start(bf16[72,512]{1,0:T(8,128)(2,1)S(1)} %get-tuple-element.48), channel_id=1, source_target_pairs={{0,8},{1,17},{2,10},{3,19},{4,12},{5,21},{6,14},{7,23},{8,0},{9,25... | collective-permute-start | bytes 221192 | tf_op jit(solution)/shard_map/ppermute | solution.py:243
  46.8 5.3 %collective-permute-start.16 = (bf16[72,512]{1,0:T(8,128)(2,1)S(1)}, bf16[72,512]{1,0:T(8,128)(2,1)S(1)}, u32[]{:S(2)}, u32[]{:S(2)}) collective-permute-start(bf16[72,512]{1,0:T(8,128)(2,1)S(1)} %get-tuple-element.49), channel_id=1, source_target_pairs={{0,24},{1,25},{2,26},{3,27},{4,28},{5,29},{6,30},{7,31},{8,16},{9,... | collective-permute-start | bytes 221192 | tf_op jit(solution)/shard_map/ppermute | solution.py:243
  49.6 7.3 %collective-permute-start.22 = (bf16[144,512]{1,0:T(8,128)(2,1)S(1)}, bf16[144,512]{1,0:T(8,128)(2,1)S(1)}, u32[]{:S(2)}, u32[]{:S(2)}) collective-permute-start(bf16[144,512]{1,0:T(8,128)(2,1)S(1)} %get-tuple-element.61), channel_id=1, source_target_pairs={{0,2},{1,3},{2,0},{3,1},{4,6},{5,7},{6,4},{7,5},{8,10},{9,11},{10,... | collective-permute-start | bytes 442376 | tf_op jit(solution)/shard_map/ppermute | solution.py:239
  52.2 6.6 %collective-permute-start.17 = (bf16[144,512]{1,0:T(8,128)(2,1)S(1)}, bf16[144,512]{1,0:T(8,128)(2,1)S(1)}, u32[]{:S(2)}, u32[]{:S(2)}) collective-permute-start(bf16[144,512]{1,0:T(8,128)(2,1)S(1)} %get-tuple-element.52), channel_id=1, source_target_pairs={{0,2},{1,3},{2,0},{3,1},{4,6},{5,7},{6,4},{7,5},{8,10},{9,11},{10,... | collective-permute-start | bytes 442376 | tf_op jit(solution)/shard_map/ppermute | solution.py:239
  57.0 7.4 %collective-permute-start.23 = (bf16[72,512]{1,0:T(8,128)(2,1)S(1)}, bf16[72,512]{1,0:T(8,128)(2,1)S(1)}, u32[]{:S(2)}, u32[]{:S(2)}) collective-permute-start(bf16[72,512]{1,0:T(8,128)(2,1)S(1)} %get-tuple-element.63), channel_id=1, source_target_pairs={{0,4},{1,5},{2,6},{3,7},{4,0},{5,1},{6,2},{7,3},{8,12},{9,13},{10,... | collective-permute-start | bytes 221192 | tf_op jit(solution)/shard_map/ppermute | solution.py:239
  58.8 6.3 %collective-permute-start.18 = (bf16[72,512]{1,0:T(8,128)(2,1)S(1)}, bf16[72,512]{1,0:T(8,128)(2,1)S(1)}, u32[]{:S(2)}, u32[]{:S(2)}) collective-permute-start(bf16[72,512]{1,0:T(8,128)(2,1)S(1)} %get-tuple-element.54), channel_id=1, source_target_pairs={{0,4},{1,5},{2,6},{3,7},{4,0},{5,1},{6,2},{7,3},{8,12},{9,13},{10,... | collective-permute-start | bytes 221192 | tf_op jit(solution)/shard_map/ppermute | solution.py:239
  64.4 1.3 %collective-permute-start.24 = (bf16[64,512]{1,0:T(8,128)(2,1)S(1)}, bf16[64,512]{1,0:T(8,128)(2,1)S(1)}, u32[]{:S(2)}, u32[]{:S(2)}) collective-permute-start(bf16[64,512]{1,0:T(8,128)(2,1)S(1)} %sum_heads.1), channel_id=1, source_target_pairs={{0,1},{1,0},{2,3},{3,2},{4,5},{5,4},{6,7},{7,6},{8,9},{9,8},{10,11... | collective-permute-start | bytes 196616 | tf_op jit(solution)/shard_map/ppermute | solution.py:236

commit v8 on v6

--- a/solution.py
+++ b/solution.py
@@ -23,14 +23,6 @@
     return pl.BlockSpec(memory_space=pltpu.SMEM)
 
 
-def partners(core):
-    return [0, 2 - core, 1 + core, 3]
-
-
-def turned(values):
-    return [values[0], *values[:0:-1]]
-
-
 def place():
     t = lax.axis_index("tp")
     return lax.axis_index("ctx"), t // 2, t % 2
@@ -42,7 +34,7 @@
 
 
 def project_kernel(parts_of, *refs):
-    blocks, (new, own, other), refs = turned(refs[:4]), refs[4:7], refs[7:]
+    blocks, (new, own, other), refs = refs[:4], refs[4:7], refs[7:]
     (held, new_held), outs, inputs = refs[:2], refs[2:5], refs[5]
     rows = held.shape[0]
     count = new.shape[0]
@@ -86,23 +78,24 @@
     return found
 
 
-def attend_kernel(count, scale, block_map, lengths, *refs):
-    mine, theirs, refs = turned(refs[:4]), turned(refs[4:8]), refs[8:]
-    (new, w_own, w_other), outs, refs = refs[:3], (refs[3:7], refs[7:11]), refs[11:]
-    q_all, key_all, value_all, attended, result = refs
+def attend_kernel(sent, count, scale, block_map, lengths, *refs):
+    mine, theirs, refs = refs[:4], refs[4:8], refs[8:]
+    new, attended, q_all, key_all, value_all = refs
     steps = len(mine)
     rows, features = mine[0].shape
+    part = rows // 2
     q_width, kv_width = q_all.shape[1], key_all.shape[1]
     head = HEAD_SIZE
     groups = kv_width // head
     per_group = q_width // kv_width
     pad = new.shape[0]
-    tail = steps * rows
+    tail = steps * part
     q_rows = q_all.shape[0]
     k_rows = key_all.shape[0]
     k_tail = 2 * steps * rows
     half = kv_width // 2
-    c, _, k = place()
+    c, z, k = place()
+    first = part * (1 - z % 2 if sent else z % 2)
 
     key_all[k_tail:, :] = jnp.zeros_like(key_all[k_tail:, :])
     value_all[k_tail:, :] = jnp.zeros_like(value_all[k_tail:, :])
@@ -120,30 +113,33 @@
         value_all[at, half:] = theirs[number][:, v_at : v_at + half]
     key_all[k_tail : k_tail + pad, :] = new[:, q_width : q_width + kv_width]
     value_all[k_tail : k_tail + pad, :] = new[:, q_width + kv_width :]
-    q_all[tail:, :] = jnp.zeros_like(q_all[tail:, :])
     for number in range(steps):
-        q_all[number * rows : (number + 1) * rows, :] = mine[number][:, :q_width]
-    q_all[tail : tail + pad, :] = new[:, :q_width]
+        at = pl.ds(pl.multiple_of(first, part), part)
+        q_all[number * part : (number + 1) * part, :] = mine[number][at, :q_width]
+    if sent:
+        q_all[tail:, :] = jnp.zeros_like(q_all[tail:, :])
+        q_all[tail : tail + pad, :] = new[:, :q_width]
 
     ends, total = [], 0
     for request in range(count):
         total = total + lengths[request]
         ends.append(total)
 
-    def labels(shape, axis, held):
+    def labels(shape, axis, held, taken, first):
         index = lax.broadcasted_iota(jnp.int32, shape, axis)
         position = jnp.zeros(shape, jnp.int32)
         for number, block in enumerate(held):
-            inside = (index >= number * rows) & (index < (number + 1) * rows)
-            position = jnp.where(inside, block_map[block] * rows + index - number * rows, position)
-        last = len(held) * rows
+            start = number * taken
+            inside = (index >= start) & (index < start + taken)
+            position = jnp.where(inside, block_map[block] * rows + first + index - start, position)
+        last = len(held) * taken
         is_new = index >= last
         request = jnp.where(is_new, index - last, request_of(position, ends))
         return jnp.where(is_new, LAST, position), request
 
-    held = [2 * (c ^ mask) + core for core in (k, 1 - k) for mask in partners(core)]
-    q_position, q_request = labels((q_rows, 1), 0, held[:steps])
-    k_position, k_request = labels((1, k_rows), 1, held)
+    held = [2 * (c ^ mask) + core for core in (k, 1 - k) for mask in range(steps)]
+    q_position, q_request = labels((q_rows, 1), 0, held[:steps], part, first)
+    k_position, k_request = labels((1, k_rows), 1, held, rows, 0)
     allowed = (q_request == k_request) & (k_position <= q_position)
 
     for group in range(groups):
@@ -165,48 +161,60 @@
             )
             attended[:, at : at + head] = (mixed / denom).astype(jnp.bfloat16)
 
-    rows_own = w_own.shape[0]
-    result[...] = (
-        jnp.dot(attended[:, :rows_own], w_own[...], preferred_element_type=jnp.float32)
-        + jnp.dot(attended[:, rows_own:], w_other[...], preferred_element_type=jnp.float32)
-    ).astype(jnp.bfloat16)
-    for core, half_outs in zip((1 - k, k), outs):
-        width = half_outs[0].shape[1]
-        column = pl.ds(pl.multiple_of(core * width, width), width)
-        for number, out in enumerate(half_outs):
-            out[:rows, :] = result[number * rows : (number + 1) * rows, column]
-            out[rows:, :] = result[tail : tail + pad, column]
+
+def output_kernel(own, sent, got, *refs):
+    weights, outs = refs[:4], refs[4:]
+    part = own.shape[0] // len(outs)
+    tail = own.shape[0]
+    pad = outs[0].shape[0] - part
+    at, total = 0, None
+    for mine, theirs in zip(weights[:2], weights[2:]):
+        to = slice(at, at + mine.shape[0])
+        at += mine.shape[0]
+        x = jnp.concatenate([own[:, to], sent[tail:, to]], axis=0)
+        term = jnp.dot(x, mine[...], preferred_element_type=jnp.float32)
+        term += jnp.dot(got[:, to], theirs[...], preferred_element_type=jnp.float32)
+        total = term if total is None else total + term
+    total = total.astype(outs[0].dtype)
+    for number, out in enumerate(outs):
+        out[:part, :] = total[number * part : (number + 1) * part]
+        out[part:, :] = total[tail : tail + pad]
 
 
 def relay_kernel(*refs):
     blocks, outs = refs[:4], refs[4:]
-    c, z, k = place()
+    c, z, _ = place()
     for slot, out in enumerate(outs):
-        for mask, block in zip(partners(k), blocks):
+        for mask, block in enumerate(blocks):
 
             @pl.when((c ^ z ^ slot) == mask)
             def _(out=out, block=block):
-                out[...] = block[...]
-
-
-def sum_heads(parts):
-    terms = [part[...].astype(jnp.float32) for part in parts]
-    return ((terms[0] + terms[1]) + (terms[2] + terms[3])).astype(jnp.bfloat16)
+                out[...] = block[: out.shape[0], :]
 
 
 def sum_kernel(*refs):
-    send = refs[-1]
-    send[...] = sum_heads(refs[:-1])[: send.shape[0]]
-
-
-def finish_kernel(*refs):
-    parts, (other, prefill, decode) = refs[:4], refs[4:]
+    parts, (keep, news, send) = refs[:4], refs[4:]
+    width = keep.shape[1]
+    part = keep.shape[0] // 2
+    count = news.shape[0]
+    _, z, k = place()
+    for out, core in ((keep, k), (send, 1 - k)):
+        column = pl.ds(pl.multiple_of(core * width, width), width)
+        for odd in range(2):
+            total = sum(parts[i][:, column].astype(jnp.float32) for i in (odd, odd + 2))
+            total = total.astype(out.dtype)
+            first = part * (z % 2 if odd == 0 else 1 - z % 2)
+            out[pl.ds(pl.multiple_of(first, part), part), :] = total[:part]
+            if odd == 0 and out is keep:
+                news[...] = total[part : part + count]
+
+
+def finish_kernel(keep, news, other, prefill, decode):
     _, _, k = place()
     rows = other.shape[0]
-    total = sum_heads(parts)
-    prefill[pl.ds(pl.multiple_of(k * rows, rows), rows), :] = total[:rows]
+    prefill[pl.ds(pl.multiple_of(k * rows, rows), rows), :] = keep[...]
     prefill[pl.ds(pl.multiple_of((1 - k) * rows, rows), rows), :] = other[...]
-    decode[...] = total[rows : rows + decode.shape[0]]
+    decode[...] = news[...]
 
 
 def on_device_small(
@@ -221,7 +229,6 @@
     kv_width = 2 * key_matrix.shape[1]
     features = q_width + 2 * kv_width
     out_width = w_out.shape[1]
-    devices = [divmod(source, tp) for source in range(steps * tp)]
 
     def to_core(value):
         return lax.ppermute(value, "tp", [(i, i ^ 1) for i in range(tp)])
@@ -229,12 +236,11 @@
     def to_chip(value, step):
         return lax.ppermute(value, "tp", [(i, i ^ (2 * step)) for i in range(tp)])
 
-    def to_partner(value, number):
-        pairs = [(c * tp + t, (c ^ partners(t % 2)[number]) * tp + t) for c, t in devices]
-        return lax.ppermute(value, ("ctx", "tp"), pairs)
-
     def to_partners(values):
-        return [to_partner(value, number) for number, value in enumerate(values, 1)]
+        return [
+            lax.ppermute(value, "ctx", [(i, i ^ mask) for i in range(steps)])
+            for mask, value in enumerate(values, 1)
+        ]
 
     def call(kernel, name, inputs, shapes, scratch=(), spaces=None):
         return pl.pallas_call(
@@ -250,7 +256,7 @@
     c, _, k = place()
     sent = [
         lax.dynamic_slice(tokens, (k * rows, (c ^ mask) * depth), (rows, depth))
-        for mask in partners(k)
+        for mask in range(steps)
     ]
     new_columns = lax.dynamic_slice_in_dim(new_token_states, c * depth, depth, 1)
     blocks = [sent[0]] + to_partners(sent[1:])
@@ -264,13 +270,18 @@
     own_part, new_part, *parts = call(
         functools.partial(project_kernel, list(zip(edges, edges[1:]))),
         "project",
-        (*turned(blocks), new_columns, own, other),
+        (*blocks, new_columns, own, other),
         [((rows, features), f32), ((pad, features), bf16)] + [(part_shape, bf16)] * (steps - 1),
         [pltpu.VMEM((x_rows, depth), bf16)],
     )
 
+
+    w_next = to_chip(w_out, 1)
     w_out_later, _ = lax.optimization_barrier((w_out, new_part))
     w_other = to_core(w_out_later)
+    new_part, w_other = lax.optimization_barrier((new_part, w_other))
+    w_out_last, w_next, _ = lax.optimization_barrier((w_out, w_next, own_part))
+    w_next_other = lax.ppermute(w_out_last, "tp", [(i, i ^ 3) for i in range(tp)])
 
     held, new = call(
         add_kernel,
@@ -281,38 +292,57 @@
     mine = [held] + to_partners([held] * (steps - 1))
     theirs = [to_core(value) for value in mine]
 
+    part = rows // 2
     k_rows = -(-(2 * steps * rows + pad) // 128) * 128
-    block = (rows + pad, out_width // 2)
+
+    def attend(sent):
+        q_rows = steps * part + (-(-pad // 16) * 16 if sent else 0)
+        (attended,) = call(
+            functools.partial(attend_kernel, sent, count, 1.0 / math.sqrt(HEAD_SIZE)),
+            "attend_sent" if sent else "attend_kept",
+            (block_map, lengths, *mine, *theirs, new),
+            [((q_rows, q_width), bf16)],
+            [
+                pltpu.VMEM((q_rows, q_width), bf16),
+                pltpu.VMEM((k_rows, kv_width), bf16),
+                pltpu.VMEM((k_rows, kv_width), bf16),
+            ],
+            [smem()] * 2 + [vmem()] * (2 * steps + 1),
+        )
+        return attended
+
+    sent = attend(True)
+    got = to_chip(sent, 1)
+    kept = attend(False)
+
+    block = (part + pad, out_width)
     outs = call(
-        functools.partial(attend_kernel, count, 1.0 / math.sqrt(HEAD_SIZE)),
-        "attend",
-        (block_map, lengths, *turned(mine), *turned(theirs), new, w_out, w_other),
-        [(block, bf16)] * (2 * steps),
-        [
-            pltpu.VMEM((x_rows, q_width), bf16),
-            pltpu.VMEM((k_rows, kv_width), bf16),
-            pltpu.VMEM((k_rows, kv_width), bf16),
-            pltpu.VMEM((x_rows, q_width), bf16),
-            pltpu.VMEM((x_rows, out_width), bf16),
-        ],
-        [smem()] * 2 + [vmem()] * (2 * steps + 3),
-    )
-
-    halves = []
-    for half in (outs[:steps], outs[steps:]):
-        got = [half[0]] + to_partners(half[1:])
-        slots = call(relay_kernel, "relay", got, [(block, bf16)] * steps)
-        halves.append(
-            [slots[0]] + [to_chip(slot, step) for step, slot in enumerate(slots[1:], 1)]
-        )
-    shape = (rows, out_width // 2)
-    (send,) = call(sum_kernel, "sum_heads", halves[0], [(shape, bf16)])
+        output_kernel,
+        "project_out",
+        (kept, sent, got, w_out, w_other, w_next, w_next_other),
+        [(block, bf16)] * steps,
+    )
+
+    slots = call(
+        relay_kernel,
+        "relay",
+        [outs[0]] + to_partners(outs[1:]),
+        [(block if i % 2 == 0 else (part, out_width), bf16) for i in range(steps)],
+    )
+    slots = [slots[0]] + [to_chip(slot, step) for step, slot in enumerate(slots[1:], 1)]
+    width = out_width // 2
+    keep, news, send = call(
+        sum_kernel,
+        "sum_heads",
+        slots,
+        [((rows, width), bf16), ((count, width), bf16), ((rows, width), bf16)],
+    )
     return tuple(
         call(
             finish_kernel,
             "finish",
-            (*halves[1], to_core(send)),
-            [((2 * rows, out_width // 2), bf16), ((count, out_width // 2), bf16)],
+            (keep, news, to_core(send)),
+            [((2 * rows, width), bf16), ((count, width), bf16)],
         )
     )
 

time: 63 us -> 63.8 us (1.013)
  starting transfers between devices: 29.6 us -> 24.1 us
  waiting for transfers between devices: 26 us -> 31.2 us
  Pallas kernels: 4.64 us -> 6.15 us
    ppermute x6 -> x5, waiting for transfers between devices: 5.64 us -> 10.9 us  [to_chip(): return lax.ppermute(value, 'tp', [(i, i ^ 2 * step) for i in range(tp)])]
    ppermute x15 -> x13, starting transfers between devices: 18.2 us -> 14.8 us  [the longest x12 14.8 us: to_partners(): lax.ppermute(value, 'ctx', [(i, i ^ mask) for i in range(steps)])]
    ppermute x6 -> x5, starting transfers between devices: 10.2 us -> 8.13 us  [to_chip(): return lax.ppermute(value, 'tp', [(i, i ^ 2 * step) for i in range(tp)])]
    pallas_call x8 -> x9, Pallas kernels: 4.64 us -> 6.15 us  [call(): pl.pallas_call(kernel, out_shape=[jax.ShapeDtypeStruct(shape, kind) for s...]
    ppermute x15 -> x13, waiting for transfers between devices: 19 us -> 18 us  [the longest x12 18 us: to_partners(): lax.ppermute(value, 'ctx', [(i, i ^ mask) for i in range(steps)])]
    ppermute x7, waiting for transfers between devices: 1.34 us -> 2.27 us  [to_core(): return lax.ppermute(value, 'tp', [(i, i ^ 1) for i in range(tp)])]
  transfers between devices with their start and end apart: 28 -> 25, of which waited for: 11 -> 17; matrix products, arithmetic and copies ran while one was open for 0% -> 0% of each run, Pallas kernels for 0% -> 8%
where the time goes in v8:
time: 63.8 us; the launch traced here: 63.7 us
  waiting for transfers between devices  31.2 us (49%)
  starting transfers between devices  24.1 us (38%)
  Pallas kernels  6.15 us (10%)
  local copies, waits for them, and re-layouts  1.44 us (2%)
  between operations  0.81 us (1%)
    ppermute x12, waiting for transfers between devices, to_partners(): lax.ppermute(value, 'ctx', [(i, i ^ mask) for i in range(steps)])  18 us
    ppermute x12, starting transfers between devices, to_partners(): lax.ppermute(value, 'ctx', [(i, i ^ mask) for i in range(steps)])  14.8 us
    ppermute x5, waiting for transfers between devices, to_chip(): return lax.ppermute(value, 'tp', [(i, i ^ 2 * step) for i in range(tp)])  10.9 us
    ppermute x5, starting transfers between devices, to_chip(): return lax.ppermute(value, 'tp', [(i, i ^ 2 * step) for i in range(tp)])  8.13 us
    pallas_call x9, Pallas kernels, call(): pl.pallas_call(kernel, out_shape=[jax.ShapeDtypeStruct(shape, kind) for s...  6.15 us
    ppermute x7, waiting for transfers between devices, to_core(): return lax.ppermute(value, 'tp', [(i, i ^ 1) for i in range(tp)])  2.27 us
  transfers between devices with their start and end apart: 25, of which 17 were waited for; matrix products, arithmetic and copies ran while one was open for 0% of the time, Pallas kernels for 8%

profile of v8, /device:TPU:0, one launch (start us, length us, event | category | flops | bytes accessed | tf_op | source)
XLA Modules:
  0.0 63.7 jit_solution(4542596076834680075)
XLA Ops:
  0.7 1.2 %fusion = (bf16[64,1024]{1,0:T(8,128)(2,1)S(1)}, bf16[64,1024]{1,0:T(8,128)(2,1)S(1)}, bf16[64,1024]{1,0:T(8,128)(2,1)S(1)}, bf16[64,1024]{1,0:T(8,128)(2,1)S(1)}) fusion(bf16[128,4096]{1,0:T(8,128)(2,1)} %param.8, s32[]{:T(128)S(6)} %select_n.27, s32[]{:T(128)S(6)} %select_n.31, s32[]{:T(128)S(6)} %select_n.29, s32[]{:T(128)S(6)} %select_n.28, s32[]{:T(128)S(6)} %select_n.30), kind=kLoop, calls=%fused_computation.1 | loop fusion | bytes 1048596 | tf_op jit(solution)/shard_map/dynamic_slice | solution.py:258
  2.7 2.6 %collective-permute-start = (bf16[64,1024]{1,0:T(8,128)(2,1)S(1)}, bf16[64,1024]{1,0:T(8,128)(2,1)S(1)}, u32[]{:S(2)}, u32[]{:S(2)}) collective-permute-start(bf16[64,1024]{1,0:T(8,128)(2,1)S(1)} %get-tuple-element.55), channel_id=1, source_target_pairs={{0,8},{8,0},{16,24},{24,16},{1,9},{9,1},{17,25},{25,17},{2,10},{10... | collective-permute-start | bytes 393224 | tf_op jit(solution)/shard_map/ppermute | solution.py:241
  5.3 1.5 %collective-permute-start.1 = (bf16[64,1024]{1,0:T(8,128)(2,1)S(1)}, bf16[64,1024]{1,0:T(8,128)(2,1)S(1)}, u32[]{:S(2)}, u32[]{:S(2)}) collective-permute-start(bf16[64,1024]{1,0:T(8,128)(2,1)S(1)} %get-tuple-element.57), channel_id=1, source_target_pairs={{0,16},{8,24},{16,0},{24,8},{1,17},{9,25},{17,1},{25,9},{2,18},{10... | collective-permute-start | bytes 393224 | tf_op jit(solution)/shard_map/ppermute | solution.py:241
  6.8 2.0 %collective-permute-start.16 = (bf16[256,1024]{1,0:T(8,128)(2,1)S(1)}, bf16[256,1024]{1,0:T(8,128)(2,1)S(1)}, u32[]{:S(2)}, u32[]{:S(2)}) collective-permute-start(bf16[256,1024]{1,0:T(8,128)(2,1)S(1)} %copy-done.1), channel_id=1, source_target_pairs={{0,2},{1,3},{2,0},{3,1},{4,6},{5,7},{6,4},{7,5},{8,10},{9,11},{10,... | collective-permute-start | bytes 1572872 | tf_op jit(solution)/shard_map/ppermute | solution.py:237
  9.5 4.2 %collective-permute-done.1.refs_2_ = bf16[64,1024]{1,0:T(8,128)(2,1)S(1)} collective-permute-done((bf16[64,1024]{1,0:T(8,128)(2,1)S(1)}, bf16[64,1024]{1,0:T(8,128)(2,1)S(1)}, u32[]{:S(2)}, u32[]{:S(2)}) %collective-permute-start.1) | collective-permute-done | bytes 131104 | tf_op jit(solution)/shard_map/ppermute | solution.py:241
  14.5 1.3 %collective-permute-start.5 = (bf16[72,1024]{1,0:T(8,128)(2,1)S(1)}, bf16[72,1024]{1,0:T(8,128)(2,1)S(1)}, u32[]{:S(2)}, u32[]{:S(2)}) collective-permute-start(bf16[72,1024]{1,0:T(8,128)(2,1)S(1)} %get-tuple-element.35), channel_id=1, source_target_pairs={{0,8},{8,0},{16,24},{24,16},{1,9},{9,1},{17,25},{25,17},{2,10},{10... | collective-permute-start | bytes 442376 | tf_op jit(solution)/shard_map/ppermute | solution.py:241
  15.8 0.8 %collective-permute-start.6 = (bf16[72,1024]{1,0:T(8,128)(2,1)S(1)}, bf16[72,1024]{1,0:T(8,128)(2,1)S(1)}, u32[]{:S(2)}, u32[]{:S(2)}) collective-permute-start(bf16[72,1024]{1,0:T(8,128)(2,1)S(1)} %get-tuple-element.36), channel_id=1, source_target_pairs={{0,16},{8,24},{16,0},{24,8},{1,17},{9,25},{17,1},{25,9},{2,18},{10... | collective-permute-start | bytes 442376 | tf_op jit(solution)/shard_map/ppermute | solution.py:241
  16.6 1.4 %collective-permute-start.7 = (bf16[72,1024]{1,0:T(8,128)(2,1)S(1)}, bf16[72,1024]{1,0:T(8,128)(2,1)S(1)}, u32[]{:S(2)}, u32[]{:S(2)}) collective-permute-start(bf16[72,1024]{1,0:T(8,128)(2,1)S(1)} %get-tuple-element.37), channel_id=1, source_target_pairs={{0,24},{8,16},{16,8},{24,0},{1,25},{9,17},{17,9},{25,1},{2,26},{10... | collective-permute-start | bytes 442376 | tf_op jit(solution)/shard_map/ppermute | solution.py:241
  18.1 2.5 %collective-permute-done.16.refs_2_ = bf16[256,1024]{1,0:T(8,128)(2,1)S(1)} collective-permute-done((bf16[256,1024]{1,0:T(8,128)(2,1)S(1)}, bf16[256,1024]{1,0:T(8,128)(2,1)S(1)}, u32[]{:S(2)}, u32[]{:S(2)}) %collective-permute-start.16) | collective-permute-done | bytes 524320 | tf_op jit(solution)/shard_map/ppermute | solution.py:237
  21.2 2.0 %collective-permute-done.6.second = bf16[72,1024]{1,0:T(8,128)(2,1)S(1)} collective-permute-done((bf16[72,1024]{1,0:T(8,128)(2,1)S(1)}, bf16[72,1024]{1,0:T(8,128)(2,1)S(1)}, u32[]{:S(2)}, u32[]{:S(2)}) %collective-permute-start.6) | collective-permute-done | bytes 147488 | tf_op jit(solution)/shard_map/ppermute | solution.py:241
  23.3 1.6 %collective-permute-done.7.both = bf16[72,1024]{1,0:T(8,128)(2,1)S(1)} collective-permute-done((bf16[72,1024]{1,0:T(8,128)(2,1)S(1)}, bf16[72,1024]{1,0:T(8,128)(2,1)S(1)}, u32[]{:S(2)}, u32[]{:S(2)}) %collective-permute-start.7) | collective-permute-done | bytes 147488 | tf_op jit(solution)/shard_map/ppermute | solution.py:241
  25.0 0.9 %collective-permute-start.8 = (bf16[64,1024]{1,0:T(8,128)(2,1)S(1)}, bf16[64,1024]{1,0:T(8,128)(2,1)S(1)}, u32[]{:S(2)}, u32[]{:S(2)}) collective-permute-start(bf16[64,1024]{1,0:T(8,128)(2,1)S(1)} %get-tuple-element.38.refs_0_), channel_id=1, source_target_pairs={{0,8},{8,0},{16,24},{24,16},{1,9},{9,1},{17,25},{25,17},{2,10},{10... | collective-permute-start | bytes 393224 | tf_op jit(solution)/shard_map/ppermute | solution.py:241
  25.8 1.5 %collective-permute-start.9 = (bf16[64,1024]{1,0:T(8,128)(2,1)S(1)}, bf16[64,1024]{1,0:T(8,128)(2,1)S(1)}, u32[]{:S(2)}, u32[]{:S(2)}) collective-permute-start(bf16[64,1024]{1,0:T(8,128)(2,1)S(1)} %get-tuple-element.38.refs_0_), channel_id=1, source_target_pairs={{0,16},{8,24},{16,0},{24,8},{1,17},{9,25},{17,1},{25,9},{2,18},{10... | collective-permute-start | bytes 393224 | tf_op jit(solution)/shard_map/ppermute | solution.py:241
  27.4 1.2 %collective-permute-start.10 = (bf16[64,1024]{1,0:T(8,128)(2,1)S(1)}, bf16[64,1024]{1,0:T(8,128)(2,1)S(1)}, u32[]{:S(2)}, u32[]{:S(2)}) collective-permute-start(bf16[64,1024]{1,0:T(8,128)(2,1)S(1)} %get-tuple-element.38.refs_0_), channel_id=1, source_target_pairs={{0,24},{8,16},{16,8},{24,0},{1,25},{9,17},{17,9},{25,1},{2,26},{10... | collective-permute-start | bytes 393224 | tf_op jit(solution)/shard_map/ppermute | solution.py:241
  28.5 2.9 %collective-permute-done.8.refs_1_ = bf16[64,1024]{1,0:T(8,128)(2,1)S(1)} collective-permute-done((bf16[64,1024]{1,0:T(8,128)(2,1)S(1)}, bf16[64,1024]{1,0:T(8,128)(2,1)S(1)}, u32[]{:S(2)}, u32[]{:S(2)}) %collective-permute-start.8) | collective-permute-done | bytes 131104 | tf_op jit(solution)/shard_map/ppermute | solution.py:241
  31.4 2.2 %collective-permute-done.9.refs_2_ = bf16[64,1024]{1,0:T(8,128)(2,1)S(1)} collective-permute-done((bf16[64,1024]{1,0:T(8,128)(2,1)S(1)}, bf16[64,1024]{1,0:T(8,128)(2,1)S(1)}, u32[]{:S(2)}, u32[]{:S(2)}) %collective-permute-start.9) | collective-permute-done | bytes 131104 | tf_op jit(solution)/shard_map/ppermute | solution.py:241
  34.1 0.8 %collective-permute-done.13.refs_6_ = bf16[64,1024]{1,0:T(8,128)(2,1)S(1)} collective-permute-done((bf16[64,1024]{1,0:T(8,128)(2,1)S(1)}, bf16[64,1024]{1,0:T(8,128)(2,1)S(1)}, u32[]{:S(2)}, u32[]{:S(2)}) %collective-permute-start.13) | collective-permute-done | bytes 131104 | tf_op jit(solution)/shard_map/ppermute | solution.py:234
  35.2 2.0 %attend_sent.1.sent = bf16[144,512]{1,0:T(8,128)(2,1)S(1)} custom-call(s32[8]{0:T(128)S(1)} %copy-done.5, s32[4]{0:T(128)S(1)} %copy-done.6, bf16[64,1024]{1,0:T(8,128)(2,1)S(1)} %get-tuple-element.38.refs_0_, bf16[64,1024]{1,0:T(8,128)(2,1)S(1)} %collective-permute-done.8.refs_1_, bf16[64,1024]{1,0:T(8,128)(2,1)S(1)} %collective-permute-done.9.refs_2_, ...), custom_call_target="tpu_custom_call" | custom-call | tf_op jit(solution)/shard_map/attend_sent/pallas_call | solution.py:246
  37.2 1.6 %collective-permute-start.15 = (bf16[144,512]{1,0:T(8,128)(2,1)S(1)}, bf16[144,512]{1,0:T(8,128)(2,1)S(1)}, u32[]{:S(2)}, u32[]{:S(2)}) collective-permute-start(bf16[144,512]{1,0:T(8,128)(2,1)S(1)} %attend_sent.1.sent), channel_id=1, source_target_pairs={{0,2},{1,3},{2,0},{3,1},{4,6},{5,7},{6,4},{7,5},{8,10},{9,11},{10,... | collective-permute-start | bytes 442376 | tf_op jit(solution)/shard_map/ppermute | solution.py:237
  38.8 2.0 %attend_kept.1.own = bf16[128,512]{1,0:T(8,128)(2,1)S(1)} custom-call(s32[8]{0:T(128)S(1)} %copy-done.5, s32[4]{0:T(128)S(1)} %copy-done.6, bf16[64,1024]{1,0:T(8,128)(2,1)S(1)} %get-tuple-element.38.refs_0_, bf16[64,1024]{1,0:T(8,128)(2,1)S(1)} %collective-permute-done.8.refs_1_, bf16[64,1024]{1,0:T(8,128)(2,1)S(1)} %collective-permute-done.9.refs_2_, ...), custom_call_target="tpu_custom_call" | custom-call | tf_op jit(solution)/shard_map/attend_kept/pallas_call | solution.py:246
  40.8 2.5 %collective-permute-done.15.got = bf16[144,512]{1,0:T(8,128)(2,1)S(1)} collective-permute-done((bf16[144,512]{1,0:T(8,128)(2,1)S(1)}, bf16[144,512]{1,0:T(8,128)(2,1)S(1)}, u32[]{:S(2)}, u32[]{:S(2)}) %collective-permute-start.15) | collective-permute-done | bytes 147488 | tf_op jit(solution)/shard_map/ppermute | solution.py:237
  43.8 1.1 %collective-permute-start.18 = (bf16[40,1024]{1,0:T(8,128)(2,1)S(1)}, bf16[40,1024]{1,0:T(8,128)(2,1)S(1)}, u32[]{:S(2)}, u32[]{:S(2)}) collective-permute-start(bf16[40,1024]{1,0:T(8,128)(2,1)S(1)} %get-tuple-element.44), channel_id=1, source_target_pairs={{0,8},{8,0},{16,24},{24,16},{1,9},{9,1},{17,25},{25,17},{2,10},{10... | collective-permute-start | bytes 245768 | tf_op jit(solution)/shard_map/ppermute | solution.py:241
  45.0 1.0 %collective-permute-start.19 = (bf16[40,1024]{1,0:T(8,128)(2,1)S(1)}, bf16[40,1024]{1,0:T(8,128)(2,1)S(1)}, u32[]{:S(2)}, u32[]{:S(2)}) collective-permute-start(bf16[40,1024]{1,0:T(8,128)(2,1)S(1)} %get-tuple-element.45), channel_id=1, source_target_pairs={{0,16},{8,24},{16,0},{24,8},{1,17},{9,25},{17,1},{25,9},{2,18},{10... | collective-permute-start | bytes 245768 | tf_op jit(solution)/shard_map/ppermute | solution.py:241
  46.0 1.4 %collective-permute-start.20 = (bf16[40,1024]{1,0:T(8,128)(2,1)S(1)}, bf16[40,1024]{1,0:T(8,128)(2,1)S(1)}, u32[]{:S(2)}, u32[]{:S(2)}) collective-permute-start(bf16[40,1024]{1,0:T(8,128)(2,1)S(1)} %get-tuple-element.46), channel_id=1, source_target_pairs={{0,24},{8,16},{16,8},{24,0},{1,25},{9,17},{17,9},{25,1},{2,26},{10... | collective-permute-start | bytes 245768 | tf_op jit(solution)/shard_map/ppermute | solution.py:241
  47.4 1.4 %collective-permute-done.18.refs_1_ = bf16[40,1024]{1,0:T(8,128)(2,1)S(1)} collective-permute-done((bf16[40,1024]{1,0:T(8,128)(2,1)S(1)}, bf16[40,1024]{1,0:T(8,128)(2,1)S(1)}, u32[]{:S(2)}, u32[]{:S(2)}) %collective-permute-start.18) | collective-permute-done | bytes 81952 | tf_op jit(solution)/shard_map/ppermute | solution.py:241
  48.8 1.4 %collective-permute-done.19.refs_2_ = bf16[40,1024]{1,0:T(8,128)(2,1)S(1)} collective-permute-done((bf16[40,1024]{1,0:T(8,128)(2,1)S(1)}, bf16[40,1024]{1,0:T(8,128)(2,1)S(1)}, u32[]{:S(2)}, u32[]{:S(2)}) %collective-permute-start.19) | collective-permute-done | bytes 81952 | tf_op jit(solution)/shard_map/ppermute | solution.py:241
  50.2 1.1 %collective-permute-done.20.refs_3_ = bf16[40,1024]{1,0:T(8,128)(2,1)S(1)} collective-permute-done((bf16[40,1024]{1,0:T(8,128)(2,1)S(1)}, bf16[40,1024]{1,0:T(8,128)(2,1)S(1)}, u32[]{:S(2)}, u32[]{:S(2)}) %collective-permute-start.20) | collective-permute-done | bytes 81952 | tf_op jit(solution)/shard_map/ppermute | solution.py:241
  51.4 2.6 %collective-permute-start.22 = (bf16[40,1024]{1,0:T(8,128)(2,1)S(1)}, bf16[40,1024]{1,0:T(8,128)(2,1)S(1)}, u32[]{:S(2)}, u32[]{:S(2)}) collective-permute-start(bf16[40,1024]{1,0:T(8,128)(2,1)S(1)} %get-tuple-element.49), channel_id=1, source_target_pairs={{0,4},{1,5},{2,6},{3,7},{4,0},{5,1},{6,2},{7,3},{8,12},{9,13},{10,... | collective-permute-start | bytes 245768 | tf_op jit(solution)/shard_map/ppermute | solution.py:237
  54.0 1.6 %collective-permute-start.21 = (bf16[32,1024]{1,0:T(8,128)(2,1)S(1)}, bf16[32,1024]{1,0:T(8,128)(2,1)S(1)}, u32[]{:S(2)}, u32[]{:S(2)}) collective-permute-start(bf16[32,1024]{1,0:T(8,128)(2,1)S(1)} %get-tuple-element.48), channel_id=1, source_target_pairs={{0,2},{1,3},{2,0},{3,1},{4,6},{5,7},{6,4},{7,5},{8,10},{9,11},{10,... | collective-permute-start | bytes 196616 | tf_op jit(solution)/shard_map/ppermute | solution.py:237
  55.8 3.4 %collective-permute-done.21.refs_1_ = bf16[32,1024]{1,0:T(8,128)(2,1)S(1)} collective-permute-done((bf16[32,1024]{1,0:T(8,128)(2,1)S(1)}, bf16[32,1024]{1,0:T(8,128)(2,1)S(1)}, u32[]{:S(2)}, u32[]{:S(2)}) %collective-permute-start.21) | collective-permute-done | bytes 65568 | tf_op jit(solution)/shard_map/ppermute | solution.py:237
  59.3 2.4 %collective-permute-done.23.refs_3_ = bf16[32,1024]{1,0:T(8,128)(2,1)S(1)} collective-permute-done((bf16[32,1024]{1,0:T(8,128)(2,1)S(1)}, bf16[32,1024]{1,0:T(8,128)(2,1)S(1)}, u32[]{:S(2)}, u32[]{:S(2)}) %collective-permute-start.23) | collective-permute-done | bytes 65568 | tf_op jit(solution)/shard_map/ppermute | solution.py:237
  61.8 1.2 %collective-permute-done.24.other = bf16[64,512]{1,0:T(8,128)(2,1)S(1)} collective-permute-done((bf16[64,512]{1,0:T(8,128)(2,1)S(1)}, bf16[64,512]{1,0:T(8,128)(2,1)S(1)}, u32[]{:S(2)}, u32[]{:S(2)}) %collective-permute-start.24) | collective-permute-done | bytes 65568 | tf_op jit(solution)/shard_map/ppermute | solution.py:234
  (43 shorter events, 5.2 us)
Async XLA Ops:
  0.6 8.2 %copy-start = (bf16[4,4096]{1,0:T(4,128)(2,1)S(1)}, bf16[4,4096]{1,0:T(4,128)(2,1)}, u32[]{:S(2)}) copy-start(bf16[4,4096]{1,0:T(4,128)(2,1)} %param.9) | copy-start | bytes 98308
  0.7 1.3 %copy-start.2 = (bf16[1024,256]{1,0:T(8,128)(2,1)S(1)}, bf16[1024,256]{1,0:T(8,128)(2,1)}, u32[]{:S(2)}) copy-start(bf16[1024,256]{1,0:T(8,128)(2,1)} %refs_0_.1) | copy-start | bytes 1572868
  0.7 1.4 %copy-start.3 = (bf16[1024,128]{1,0:T(8,128)(2,1)S(1)}, bf16[1024,128]{1,0:T(8,128)(2,1)}, u32[]{:S(2)}) copy-start(bf16[1024,128]{1,0:T(8,128)(2,1)} %refs_1_) | copy-start | bytes 786436
  0.7 1.4 %copy-start.4 = (bf16[1024,128]{1,0:T(8,128)(2,1)S(1)}, bf16[1024,128]{1,0:T(8,128)(2,1)}, u32[]{:S(2)}) copy-start(bf16[1024,128]{1,0:T(8,128)(2,1)} %refs_2_) | copy-start | bytes 786436
  2.1 4.7 %copy-start.1 = (bf16[256,1024]{1,0:T(8,128)(2,1)S(1)}, bf16[256,1024]{1,0:T(8,128)(2,1)}, u32[]{:S(2)}) copy-start(bf16[256,1024]{1,0:T(8,128)(2,1)} %refs_0_.2) | copy-start | bytes 1572868
  2.2 11.5 %collective-permute-start.3 = (bf16[1024,512]{1,0:T(8,128)(2,1)S(1)}, bf16[1024,512]{1,0:T(8,128)(2,1)S(1)}, u32[]{:S(2)}, u32[]{:S(2)}) collective-permute-start(bf16[1024,512]{1,0:T(8,128)(2,1)S(1)} %pack_weights.1.refs_5_), channel_id=1, source_target_pairs={{0,1},{1,0},{2,3},{3,2},{4,5},{5,4},{6,7},{7,6},{8,9},{9,8},{10,11... | collective-permute-start | bytes 3145736 | tf_op jit(solution)/shard_map/ppermute | solution.py:234
  2.7 6.7 %collective-permute-start = (bf16[64,1024]{1,0:T(8,128)(2,1)S(1)}, bf16[64,1024]{1,0:T(8,128)(2,1)S(1)}, u32[]{:S(2)}, u32[]{:S(2)}) collective-permute-start(bf16[64,1024]{1,0:T(8,128)(2,1)S(1)} %get-tuple-element.55), channel_id=1, source_target_pairs={{0,8},{8,0},{16,24},{24,16},{1,9},{9,1},{17,25},{25,17},{2,10},{10... | collective-permute-start | bytes 393224 | tf_op jit(solution)/shard_map/ppermute | solution.py:241
  5.3 8.4 %collective-permute-start.1 = (bf16[64,1024]{1,0:T(8,128)(2,1)S(1)}, bf16[64,1024]{1,0:T(8,128)(2,1)S(1)}, u32[]{:S(2)}, u32[]{:S(2)}) collective-permute-start(bf16[64,1024]{1,0:T(8,128)(2,1)S(1)} %get-tuple-element.57), channel_id=1, source_target_pairs={{0,16},{8,24},{16,0},{24,8},{1,17},{9,25},{17,1},{25,9},{2,18},{10... | collective-permute-start | bytes 393224 | tf_op jit(solution)/shard_map/ppermute | solution.py:241
  6.8 6.9 %collective-permute-start.2 = (bf16[64,1024]{1,0:T(8,128)(2,1)S(1)}, bf16[64,1024]{1,0:T(8,128)(2,1)S(1)}, u32[]{:S(2)}, u32[]{:S(2)}) collective-permute-start(bf16[64,1024]{1,0:T(8,128)(2,1)S(1)} %get-tuple-element.54), channel_id=1, source_target_pairs={{0,24},{8,16},{16,8},{24,0},{1,25},{9,17},{17,9},{25,1},{2,26},{10... | collective-permute-start | bytes 393224 | tf_op jit(solution)/shard_map/ppermute | solution.py:241
  6.8 13.7 %collective-permute-start.16 = (bf16[256,1024]{1,0:T(8,128)(2,1)S(1)}, bf16[256,1024]{1,0:T(8,128)(2,1)S(1)}, u32[]{:S(2)}, u32[]{:S(2)}) collective-permute-start(bf16[256,1024]{1,0:T(8,128)(2,1)S(1)} %copy-done.1), channel_id=1, source_target_pairs={{0,2},{1,3},{2,0},{3,1},{4,6},{5,7},{6,4},{7,5},{8,10},{9,11},{10,... | collective-permute-start | bytes 1572872 | tf_op jit(solution)/shard_map/ppermute | solution.py:237
  14.4 6.2 %collective-permute-start.4 = (bf16[256,1024]{1,0:T(8,128)(2,1)S(1)}, bf16[256,1024]{1,0:T(8,128)(2,1)S(1)}, u32[]{:S(2)}, u32[]{:S(2)}) collective-permute-start(bf16[256,1024]{1,0:T(8,128)(2,1)S(1)} %copy-done.1), channel_id=1, source_target_pairs={{0,1},{1,0},{2,3},{3,2},{4,5},{5,4},{6,7},{7,6},{8,9},{9,8},{10,11... | collective-permute-start | bytes 1572872 | tf_op jit(solution)/shard_map/ppermute | solution.py:234
  14.5 6.7 %collective-permute-start.5 = (bf16[72,1024]{1,0:T(8,128)(2,1)S(1)}, bf16[72,1024]{1,0:T(8,128)(2,1)S(1)}, u32[]{:S(2)}, u32[]{:S(2)}) collective-permute-start(bf16[72,1024]{1,0:T(8,128)(2,1)S(1)} %get-tuple-element.35), channel_id=1, source_target_pairs={{0,8},{8,0},{16,24},{24,16},{1,9},{9,1},{17,25},{25,17},{2,10},{10... | collective-permute-start | bytes 442376 | tf_op jit(solution)/shard_map/ppermute | solution.py:241
  15.8 7.5 %collective-permute-start.6 = (bf16[72,1024]{1,0:T(8,128)(2,1)S(1)}, bf16[72,1024]{1,0:T(8,128)(2,1)S(1)}, u32[]{:S(2)}, u32[]{:S(2)}) collective-permute-start(bf16[72,1024]{1,0:T(8,128)(2,1)S(1)} %get-tuple-element.36), channel_id=1, source_target_pairs={{0,16},{8,24},{16,0},{24,8},{1,17},{9,25},{17,1},{25,9},{2,18},{10... | collective-permute-start | bytes 442376 | tf_op jit(solution)/shard_map/ppermute | solution.py:241
  16.6 8.3 %collective-permute-start.7 = (bf16[72,1024]{1,0:T(8,128)(2,1)S(1)}, bf16[72,1024]{1,0:T(8,128)(2,1)S(1)}, u32[]{:S(2)}, u32[]{:S(2)}) collective-permute-start(bf16[72,1024]{1,0:T(8,128)(2,1)S(1)} %get-tuple-element.37), channel_id=1, source_target_pairs={{0,24},{8,16},{16,8},{24,0},{1,25},{9,17},{17,9},{25,1},{2,26},{10... | collective-permute-start | bytes 442376 | tf_op jit(solution)/shard_map/ppermute | solution.py:241
  20.6 20.3 %collective-permute-start.17 = (bf16[256,1024]{1,0:T(8,128)(2,1)S(1)}, bf16[256,1024]{1,0:T(8,128)(2,1)S(1)}, u32[]{:S(2)}, u32[]{:S(2)}) collective-permute-start(bf16[256,1024]{1,0:T(8,128)(2,1)S(1)} %copy-done.1), channel_id=1, source_target_pairs={{0,3},{1,2},{2,1},{3,0},{4,7},{5,6},{6,5},{7,4},{8,11},{9,10},{10,... | collective-permute-start | bytes 1572872 | tf_op jit(solution)/shard_map/ppermute | solution.py:284
  25.0 10.2 %copy-start.5 = (s32[8]{0:T(128)S(1)}, s32[8]{0:T(128)}, u32[]{:S(2)}) copy-start(s32[8]{0:T(128)} %block_map.3) | copy-start | bytes 100
  25.0 10.2 %copy-start.6 = (s32[4]{0:T(128)S(1)}, s32[4]{0:T(128)}, u32[]{:S(2)}) copy-start(s32[4]{0:T(128)} %lengths.3) | copy-start | bytes 52
  25.0 6.4 %collective-permute-start.8 = (bf16[64,1024]{1,0:T(8,128)(2,1)S(1)}, bf16[64,1024]{1,0:T(8,128)(2,1)S(1)}, u32[]{:S(2)}, u32[]{:S(2)}) collective-permute-start(bf16[64,1024]{1,0:T(8,128)(2,1)S(1)} %get-tuple-element.38.refs_0_), channel_id=1, source_target_pairs={{0,8},{8,0},{16,24},{24,16},{1,9},{9,1},{17,25},{25,17},{2,10},{10... | collective-permute-start | bytes 393224 | tf_op jit(solution)/shard_map/ppermute | solution.py:241
  25.8 7.8 %collective-permute-start.9 = (bf16[64,1024]{1,0:T(8,128)(2,1)S(1)}, bf16[64,1024]{1,0:T(8,128)(2,1)S(1)}, u32[]{:S(2)}, u32[]{:S(2)}) collective-permute-start(bf16[64,1024]{1,0:T(8,128)(2,1)S(1)} %get-tuple-element.38.refs_0_), channel_id=1, source_target_pairs={{0,16},{8,24},{16,0},{24,8},{1,17},{9,25},{17,1},{25,9},{2,18},{10... | collective-permute-start | bytes 393224 | tf_op jit(solution)/shard_map/ppermute | solution.py:241
  27.4 6.3 %collective-permute-start.10 = (bf16[64,1024]{1,0:T(8,128)(2,1)S(1)}, bf16[64,1024]{1,0:T(8,128)(2,1)S(1)}, u32[]{:S(2)}, u32[]{:S(2)}) collective-permute-start(bf16[64,1024]{1,0:T(8,128)(2,1)S(1)} %get-tuple-element.38.refs_0_), channel_id=1, source_target_pairs={{0,24},{8,16},{16,8},{24,0},{1,25},{9,17},{17,9},{25,1},{2,26},{10... | collective-permute-start | bytes 393224 | tf_op jit(solution)/shard_map/ppermute | solution.py:241
  28.5 5.6 %collective-permute-start.11 = (bf16[64,1024]{1,0:T(8,128)(2,1)S(1)}, bf16[64,1024]{1,0:T(8,128)(2,1)S(1)}, u32[]{:S(2)}, u32[]{:S(2)}) collective-permute-start(bf16[64,1024]{1,0:T(8,128)(2,1)S(1)} %get-tuple-element.38.refs_0_), channel_id=1, source_target_pairs={{0,1},{1,0},{2,3},{3,2},{4,5},{5,4},{6,7},{7,6},{8,9},{9,8},{10,11... | collective-permute-start | bytes 393224 | tf_op jit(solution)/shard_map/ppermute | solution.py:234
  31.4 2.7 %collective-permute-start.12 = (bf16[64,1024]{1,0:T(8,128)(2,1)S(1)}, bf16[64,1024]{1,0:T(8,128)(2,1)S(1)}, u32[]{:S(2)}, u32[]{:S(2)}) collective-permute-start(bf16[64,1024]{1,0:T(8,128)(2,1)S(1)} %collective-permute-done.8.refs_1_), channel_id=1, source_target_pairs={{0,1},{1,0},{2,3},{3,2},{4,5},{5,4},{6,7},{7,6},{8,9},{9,8},{10,11... | collective-permute-start | bytes 393224 | tf_op jit(solution)/shard_map/ppermute | solution.py:234
  33.6 1.3 %collective-permute-start.13 = (bf16[64,1024]{1,0:T(8,128)(2,1)S(1)}, bf16[64,1024]{1,0:T(8,128)(2,1)S(1)}, u32[]{:S(2)}, u32[]{:S(2)}) collective-permute-start(bf16[64,1024]{1,0:T(8,128)(2,1)S(1)} %collective-permute-done.9.refs_2_), channel_id=1, source_target_pairs={{0,1},{1,0},{2,3},{3,2},{4,5},{5,4},{6,7},{7,6},{8,9},{9,8},{10,11... | collective-permute-start | bytes 393224 | tf_op jit(solution)/shard_map/ppermute | solution.py:234
  33.6 1.5 %collective-permute-start.14 = (bf16[64,1024]{1,0:T(8,128)(2,1)S(1)}, bf16[64,1024]{1,0:T(8,128)(2,1)S(1)}, u32[]{:S(2)}, u32[]{:S(2)}) collective-permute-start(bf16[64,1024]{1,0:T(8,128)(2,1)S(1)} %collective-permute-done.10.refs_3_), channel_id=1, source_target_pairs={{0,1},{1,0},{2,3},{3,2},{4,5},{5,4},{6,7},{7,6},{8,9},{9,8},{10,11... | collective-permute-start | bytes 393224 | tf_op jit(solution)/shard_map/ppermute | solution.py:234
  37.2 6.2 %collective-permute-start.15 = (bf16[144,512]{1,0:T(8,128)(2,1)S(1)}, bf16[144,512]{1,0:T(8,128)(2,1)S(1)}, u32[]{:S(2)}, u32[]{:S(2)}) collective-permute-start(bf16[144,512]{1,0:T(8,128)(2,1)S(1)} %attend_sent.1.sent), channel_id=1, source_target_pairs={{0,2},{1,3},{2,0},{3,1},{4,6},{5,7},{6,4},{7,5},{8,10},{9,11},{10,... | collective-permute-start | bytes 442376 | tf_op jit(solution)/shard_map/ppermute | solution.py:237
  43.8 5.0 %collective-permute-start.18 = (bf16[40,1024]{1,0:T(8,128)(2,1)S(1)}, bf16[40,1024]{1,0:T(8,128)(2,1)S(1)}, u32[]{:S(2)}, u32[]{:S(2)}) collective-permute-start(bf16[40,1024]{1,0:T(8,128)(2,1)S(1)} %get-tuple-element.44), channel_id=1, source_target_pairs={{0,8},{8,0},{16,24},{24,16},{1,9},{9,1},{17,25},{25,17},{2,10},{10... | collective-permute-start | bytes 245768 | tf_op jit(solution)/shard_map/ppermute | solution.py:241
  45.0 5.3 %collective-permute-start.19 = (bf16[40,1024]{1,0:T(8,128)(2,1)S(1)}, bf16[40,1024]{1,0:T(8,128)(2,1)S(1)}, u32[]{:S(2)}, u32[]{:S(2)}) collective-permute-start(bf16[40,1024]{1,0:T(8,128)(2,1)S(1)} %get-tuple-element.45), channel_id=1, source_target_pairs={{0,16},{8,24},{16,0},{24,8},{1,17},{9,25},{17,1},{25,9},{2,18},{10... | collective-permute-start | bytes 245768 | tf_op jit(solution)/shard_map/ppermute | solution.py:241
  46.0 5.3 %collective-permute-start.20 = (bf16[40,1024]{1,0:T(8,128)(2,1)S(1)}, bf16[40,1024]{1,0:T(8,128)(2,1)S(1)}, u32[]{:S(2)}, u32[]{:S(2)}) collective-permute-start(bf16[40,1024]{1,0:T(8,128)(2,1)S(1)} %get-tuple-element.46), channel_id=1, source_target_pairs={{0,24},{8,16},{16,8},{24,0},{1,25},{9,17},{17,9},{25,1},{2,26},{10... | collective-permute-start | bytes 245768 | tf_op jit(solution)/shard_map/ppermute | solution.py:241
  51.4 10.3 %collective-permute-start.22 = (bf16[40,1024]{1,0:T(8,128)(2,1)S(1)}, bf16[40,1024]{1,0:T(8,128)(2,1)S(1)}, u32[]{:S(2)}, u32[]{:S(2)}) collective-permute-start(bf16[40,1024]{1,0:T(8,128)(2,1)S(1)} %get-tuple-element.49), channel_id=1, source_target_pairs={{0,4},{1,5},{2,6},{3,7},{4,0},{5,1},{6,2},{7,3},{8,12},{9,13},{10,... | collective-permute-start | bytes 245768 | tf_op jit(solution)/shard_map/ppermute | solution.py:237
  54.0 5.2 %collective-permute-start.21 = (bf16[32,1024]{1,0:T(8,128)(2,1)S(1)}, bf16[32,1024]{1,0:T(8,128)(2,1)S(1)}, u32[]{:S(2)}, u32[]{:S(2)}) collective-permute-start(bf16[32,1024]{1,0:T(8,128)(2,1)S(1)} %get-tuple-element.48), channel_id=1, source_target_pairs={{0,2},{1,3},{2,0},{3,1},{4,6},{5,7},{6,4},{7,5},{8,10},{9,11},{10,... | collective-permute-start | bytes 196616 | tf_op jit(solution)/shard_map/ppermute | solution.py:237
  55.6 6.1 %collective-permute-start.23 = (bf16[32,1024]{1,0:T(8,128)(2,1)S(1)}, bf16[32,1024]{1,0:T(8,128)(2,1)S(1)}, u32[]{:S(2)}, u32[]{:S(2)}) collective-permute-start(bf16[32,1024]{1,0:T(8,128)(2,1)S(1)} %get-tuple-element.50), channel_id=1, source_target_pairs={{0,6},{1,7},{2,4},{3,5},{4,2},{5,3},{6,0},{7,1},{8,14},{9,15},{10,... | collective-permute-start | bytes 196616 | tf_op jit(solution)/shard_map/ppermute | solution.py:237
  61.7 1.3 %collective-permute-start.24 = (bf16[64,512]{1,0:T(8,128)(2,1)S(1)}, bf16[64,512]{1,0:T(8,128)(2,1)S(1)}, u32[]{:S(2)}, u32[]{:S(2)}) collective-permute-start(bf16[64,512]{1,0:T(8,128)(2,1)S(1)} %get-tuple-element.53), channel_id=1, source_target_pairs={{0,1},{1,0},{2,3},{3,2},{4,5},{5,4},{6,7},{7,6},{8,9},{9,8},{10,11... | collective-permute-start | bytes 196616 | tf_op jit(solution)/shard_map/ppermute | solution.py:234

commit v9 on v0

--- a/solution.py
+++ b/solution.py
@@ -1,11 +1,292 @@
+import functools
 import math
 
 import jax
 import jax.numpy as jnp
 from jax import lax
+from jax.experimental import pallas as pl
+from jax.experimental.pallas import tpu as pltpu
 from jax.sharding import PartitionSpec as P
 
 HEAD_SIZE = 128
+FLOOR = -1e30
+LAST = 1 << 30
+ROW_TILE = 8
+VMEM_BYTES = 48 * 1024 * 1024
+
+
+def vmem():
+    return pl.BlockSpec(memory_space=pltpu.VMEM)
+
+
+def smem():
+    return pl.BlockSpec(memory_space=pltpu.SMEM)
+
+
+def turned(values):
+    return [values[0], *values[:0:-1]]
+
+
+def place():
+    t = lax.axis_index("tp")
+    return lax.axis_index("ctx"), t // 2, t % 2
+
+
+def pack_kernel(*refs):
+    out = refs[-1]
+    out[...] = jnp.concatenate([ref[...] for ref in refs[:-1]], axis=1)
+
+
+def project_kernel(parts_of, *refs):
+    blocks, (new, own, other), refs = turned(refs[:4]), refs[4:7], refs[7:]
+    outs, (inputs, result) = refs[:4], refs[4:]
+    rows = blocks[0].shape[0]
+    count = new.shape[0]
+    tail = len(blocks) * rows
+    c, _, k = place()
+    for mask, block in enumerate(blocks):
+        inputs[pl.ds(pl.multiple_of((c ^ mask) * rows, rows), rows), :] = block[...]
+    inputs[tail:, :] = jnp.zeros_like(inputs[tail:, :])
+    inputs[tail : tail + count, :] = new[...]
+    x = inputs[...]
+    starts = []
+    for start, stop in parts_of:
+        weight = jnp.concatenate([own[:, start:stop], other[:, start:stop]], axis=1)
+        starts.append(2 * start)
+        result[:, 2 * start : 2 * stop] = jnp.dot(x, weight, preferred_element_type=jnp.float32)
+    head = HEAD_SIZE
+    for mask, out in enumerate(outs):
+        query, keyval = head_places(c ^ mask, k)
+        for number, (start, at) in enumerate(zip(starts, (query, keyval, keyval))):
+            column = pl.ds(pl.multiple_of(start + at * head, head), head)
+            values = result[: out.shape[0], column]
+            out[:, number * head : (number + 1) * head] = values.astype(out.dtype)
+
+
+def head_places(number, core):
+    keyval = (number // 2) ^ core
+    return 2 * keyval + number % 2, keyval
+
+
+def add_kernel(own, first, second, both, query, keyval):
+    head = query.shape[1]
+    total = own[...]
+    for part in (first, second, both):
+        total = total + part[...].astype(jnp.float32)
+    total = total.astype(query.dtype)
+    query[...] = total[:, :head]
+    keyval[...] = total[:, head:]
+
+
+def request_of(position, ends):
+    found = jnp.zeros_like(position)
+    for end in ends:
+        found = found + jnp.where(position >= end, 1, 0)
+    return found
+
+
+def attend_kernel(steps, count, scale, block_map, lengths, query, mine, theirs, *refs):
+    attended, key_all, value_all = refs
+    q_rows, head = query.shape
+    pad = -(-count // ROW_TILE) * ROW_TILE
+    tail = q_rows - pad
+    rows = tail // steps
+    k_rows = key_all.shape[0]
+    _, _, k = place()
+    for ref, at in ((key_all, 0), (value_all, head)):
+        ref[:tail, :] = mine[:tail, at : at + head]
+        ref[tail : 2 * tail, :] = theirs[:tail, at : at + head]
+        ref[2 * tail :, :] = jnp.zeros_like(ref[2 * tail :, :])
+        ref[2 * tail : 2 * tail + pad, :] = mine[tail:, at : at + head]
+
+    ends, total = [], 0
+    for request in range(count):
+        total = total + lengths[request]
+        ends.append(total)
+
+    def labels(shape, axis, held):
+        index = lax.broadcasted_iota(jnp.int32, shape, axis)
+        position = jnp.zeros(shape, jnp.int32)
+        for number, block in enumerate(held):
+            inside = (index >= number * rows) & (index < (number + 1) * rows)
+            position = jnp.where(inside, block_map[block] * rows + index - number * rows, position)
+        last = len(held) * rows
+        is_new = index >= last
+        request = jnp.where(is_new, index - last, request_of(position, ends))
+        return jnp.where(is_new, LAST, position), request
+
+    held = [2 * number + core for core in (k, 1 - k) for number in range(steps)]
+    q_position, q_request = labels((q_rows, 1), 0, held[:steps])
+    k_position, k_request = labels((1, k_rows), 1, held)
+    allowed = (q_request == k_request) & (k_position <= q_position)
+    scores = lax.dot_general(
+        query[...],
+        key_all[...],
+        (((1,), (1,)), ((), ())),
+        preferred_element_type=jnp.float32,
+    )
+    scores = jnp.where(allowed, scores * scale, FLOOR)
+    weights = jnp.exp(scores - jnp.max(scores, axis=1, keepdims=True))
+    denom = jnp.sum(weights, axis=1, keepdims=True)
+    mixed = jnp.dot(
+        weights.astype(jnp.bfloat16), value_all[...], preferred_element_type=jnp.float32
+    )
+    attended[...] = (mixed / denom).astype(jnp.bfloat16)
+
+
+def output_kernel(rows, *refs):
+    heads, (w_own, w_other), refs = turned(refs[:4]), refs[4:6], refs[6:]
+    outs, (attended, result) = refs[:4], refs[4:]
+    c, _, k = place()
+    head = heads[0].shape[1]
+    for mask, ref in enumerate(heads):
+        at, _ = head_places(c ^ mask, k)
+        attended[:, pl.ds(pl.multiple_of(at * head, head), head)] = ref[...]
+    rows_own = w_own.shape[0]
+    total = jnp.dot(attended[:, :rows_own], w_own[...], preferred_element_type=jnp.float32)
+    total += jnp.dot(attended[:, rows_own:], w_other[...], preferred_element_type=jnp.float32)
+    result[...] = total.astype(result.dtype)
+    tail = 4 * rows
+    for mask, out in enumerate(outs):
+        out[:rows, :] = result[pl.ds(pl.multiple_of((c ^ mask) * rows, rows), rows), :]
+        out[rows:, :] = result[tail:, :]
+
+
+def relay_kernel(*refs):
+    blocks, outs = refs[:4], refs[4:]
+    c, z, _ = place()
+    for slot, out in enumerate(outs):
+        for mask, block in enumerate(blocks):
+
+            @pl.when((c ^ z ^ slot) == mask)
+            def _(out=out, block=block):
+                out[...] = block[: out.shape[0], :]
+
+
+def sum_kernel(*refs):
+    parts, (keep, send) = refs[:4], refs[4:]
+    width = keep.shape[1]
+    _, _, k = place()
+    for out, core in ((keep, k), (send, 1 - k)):
+        column = pl.ds(pl.multiple_of(core * width, width), width)
+        terms = [part[:, column].astype(jnp.float32) for part in parts]
+        total = (terms[0] + terms[1]) + (terms[2] + terms[3])
+        out[...] = total[: out.shape[0]].astype(out.dtype)
+
+
+def finish_kernel(keep, other, prefill, decode):
+    _, _, k = place()
+    rows = other.shape[0]
+    prefill[pl.ds(pl.multiple_of(k * rows, rows), rows), :] = keep[:rows]
+    prefill[pl.ds(pl.multiple_of((1 - k) * rows, rows), rows), :] = other[...]
+    decode[...] = keep[rows : rows + decode.shape[0]]
+
+
+def on_device_small(
+    steps, tp, tokens, new_token_states, w_query, key_matrix, value_matrix, w_out, lengths, block_map
+):
+    bf16, f32 = jnp.bfloat16, jnp.float32
+    rows = tokens.shape[0] // 2
+    depth = w_query.shape[0]
+    count = new_token_states.shape[0]
+    pad = -(-count // ROW_TILE) * ROW_TILE
+    q_width = 2 * w_query.shape[1]
+    kv_width = 2 * key_matrix.shape[1]
+    features = q_width + 2 * kv_width
+    out_width = w_out.shape[1]
+
+    def to_core(value):
+        return lax.ppermute(value, "tp", [(i, i ^ 1) for i in range(tp)])
+
+    def to_chip(value, step):
+        return lax.ppermute(value, "tp", [(i, i ^ (2 * step)) for i in range(tp)])
+
+    def to_partners(values):
+        return [
+            lax.ppermute(value, "ctx", [(i, i ^ mask) for i in range(steps)])
+            for mask, value in enumerate(values, 1)
+        ]
+
+    def call(kernel, name, inputs, shapes, scratch=(), spaces=None):
+        return pl.pallas_call(
+            kernel,
+            out_shape=[jax.ShapeDtypeStruct(shape, kind) for shape, kind in shapes],
+            in_specs=spaces or [vmem()] * len(inputs),
+            out_specs=[vmem()] * len(shapes),
+            scratch_shapes=list(scratch),
+            compiler_params=pltpu.CompilerParams(vmem_limit_bytes=VMEM_BYTES),
+            name=name,
+        )(*inputs)
+
+    c, _, k = place()
+    sent = [
+        lax.dynamic_slice(tokens, (k * rows, (c ^ mask) * depth), (rows, depth))
+        for mask in range(steps)
+    ]
+    new_columns = lax.dynamic_slice_in_dim(new_token_states, c * depth, depth, 1)
+    blocks = [sent[0]] + to_partners(sent[1:])
+    *weights, _ = lax.optimization_barrier((w_query, key_matrix, value_matrix, sent[1]))
+    (own,) = call(pack_kernel, "pack_weights", weights, [((depth, features // 2), bf16)])
+    other = to_core(own)
+
+    all_rows = steps * rows + pad
+    x_rows = -(-all_rows // 16) * 16
+    part = (all_rows, 3 * HEAD_SIZE)
+    edges = [0, q_width // 2, (q_width + kv_width) // 2, features // 2]
+    parts = call(
+        functools.partial(project_kernel, list(zip(edges, edges[1:]))),
+        "project",
+        (*turned(blocks), new_columns, own, other),
+        [(part, f32)] + [(part, bf16)] * (steps - 1),
+        [pltpu.VMEM((x_rows, depth), bf16), pltpu.VMEM((x_rows, features), f32)],
+    )
+    w_out_later, _ = lax.optimization_barrier((w_out, parts[0]))
+    w_other = to_core(w_out_later)
+
+    query, keyval = call(
+        add_kernel,
+        "add_parts",
+        (parts[0], *to_partners(parts[1:])),
+        [((all_rows, HEAD_SIZE), bf16), ((all_rows, 2 * HEAD_SIZE), bf16)],
+    )
+    k_rows = -(-(2 * steps * rows + pad) // 128) * 128
+    (attended,) = call(
+        functools.partial(attend_kernel, steps, count, 1.0 / math.sqrt(HEAD_SIZE)),
+        "attend",
+        (block_map, lengths, query, keyval, to_core(keyval)),
+        [((all_rows, HEAD_SIZE), bf16)],
+        [pltpu.VMEM((k_rows, HEAD_SIZE), bf16)] * 2,
+        [smem()] * 2 + [vmem()] * 3,
+    )
+
+    block = (rows + pad, out_width)
+    outs = call(
+        functools.partial(output_kernel, rows),
+        "project_out",
+        (*turned([attended, *to_partners([attended] * (steps - 1))]), w_out, w_other),
+        [(block, bf16)] * steps,
+        [pltpu.VMEM((all_rows, q_width), bf16), pltpu.VMEM((all_rows, out_width), bf16)],
+    )
+
+    slots = call(
+        relay_kernel,
+        "relay",
+        [outs[0]] + to_partners(outs[1:]),
+        [(block, bf16)] * steps,
+    )
+    slots = [slots[0]] + [to_chip(slot, step) for step, slot in enumerate(slots[1:], 1)]
+    width = out_width // 2
+    keep, send = call(
+        sum_kernel, "sum_heads", slots, [((rows + pad, width), bf16), ((rows, width), bf16)]
+    )
+    return tuple(
+        call(
+            finish_kernel,
+            "finish",
+            (keep, to_core(send)),
+            [((2 * rows, width), bf16), ((count, width), bf16)],
+        )
+    )
 
 
 floor_value = -1e30
@@ -57,7 +338,7 @@
     return (part_peak, part_total, part_mixed)
 
 
-def on_device(
+def on_device_large(
     tokens, new_token_states, w_query, key_matrix, value_matrix, w_out, lengths, block_map
 ):
     local_rows = tokens.shape[0]
@@ -188,8 +469,16 @@
     summed_rows = summed_rows.astype(jnp.bfloat16)
     return (summed_rows[:local_rows], summed_rows[local_rows:])
 
-
 def solution(mesh):
+    steps, tp = mesh.shape["ctx"], mesh.shape["tp"]
+
+    def on_device(tokens, *rest):
+        chip_heads = 2 * rest[1].shape[1] // HEAD_SIZE
+        small = steps == 4 and tp == 8 and chip_heads == 4 and tokens.shape[0] * steps <= 1024
+        if small:
+            return on_device_small(steps, tp, tokens, *rest)
+        return on_device_large(tokens, *rest)
+
     return jax.shard_map(
         on_device,
         mesh=mesh,

time: 184 us -> 62.9 us (0.34)
  waiting for transfers between devices: 106 us -> 36.6 us
  blocking collectives: 40.2 us -> 0 us
  starting transfers between devices: 4.76 us -> 20 us
  between operations: 14 us -> 0.81 us
  matrix products: 9.96 us -> 0 us
  local copies, waits for them, and re-layouts: 6.9 us -> 1.5 us
  Pallas kernels: 0 us -> 3.91 us
    all_gather x4 -> x0, waiting for transfers between devices: 104 us -> none  [the longest x1 27.1 us: on_device(): head_block = lax.all_gather(w_out, 'ctx', axis=1, tiled=True)]
    all_gather x3 -> x0, blocking collectives: 40.2 us -> none  [the longest x1 22.3 us: on_device(): lax.all_gather(attended_all, 'tp', axis=1, tiled=True)]
    ppermute x0 -> x19, waiting for transfers between devices: none -> 36.6 us  [the longest x12 24.7 us: to_partners(): lax.ppermute(value, 'ctx', [(i, i ^ mask) for i in range(steps)])]
    ppermute x0 -> x19, starting transfers between devices: none -> 20 us  [the longest x12 14.8 us: to_partners(): lax.ppermute(value, 'ctx', [(i, i ^ mask) for i in range(steps)])]
    dot_general x8 -> x0, matrix products: 9.96 us -> none  [the longest x3 5.41 us: on_device(): jnp.dot(inputs, weight, preferred_element_type=jnp.float32)]
    all_to_all x1 -> x0, starting transfers between devices: 4.61 us -> none  [on_device(): lax.all_to_all(head_block, 'tp', split_axis=1, concat_axis=0, tiled=True)]
    pallas_call x0 -> x8, Pallas kernels: none -> 3.91 us  [call(): pl.pallas_call(kernel, out_shape=[jax.ShapeDtypeStruct(shape, kind) for s...]
    unnamed x14, local copies, waits for them, and re-layouts: 2.88 us -> 0.27 us
  transfers between devices with their start and end apart: 5 -> 19, of which waited for: 4 -> 14; matrix products, arithmetic and copies ran while one was open for 6% -> 0% of each run, Pallas kernels for 0% -> 2%
where the time goes in v9:
time: 62.9 us; the launch traced here: 62.7 us
  waiting for transfers between devices  36.6 us (58%)
  starting transfers between devices  20 us (32%)
  Pallas kernels  3.91 us (6%)
  local copies, waits for them, and re-layouts  1.5 us (2%)
  between operations  0.81 us (1%)
    ppermute x12, waiting for transfers between devices, to_partners(): lax.ppermute(value, 'ctx', [(i, i ^ mask) for i in range(steps)])  24.7 us
    ppermute x12, starting transfers between devices, to_partners(): lax.ppermute(value, 'ctx', [(i, i ^ mask) for i in range(steps)])  14.8 us
    ppermute x3, waiting for transfers between devices, to_chip(): return lax.ppermute(value, 'tp', [(i, i ^ 2 * step) for i in range(tp)])  9.28 us
    ppermute x3, starting transfers between devices, to_chip(): return lax.ppermute(value, 'tp', [(i, i ^ 2 * step) for i in range(tp)])  4.45 us
    pallas_call x8, Pallas kernels, call(): pl.pallas_call(kernel, out_shape=[jax.ShapeDtypeStruct(shape, kind) for s...  3.91 us
    ppermute x4, waiting for transfers between devices, to_core(): return lax.ppermute(value, 'tp', [(i, i ^ 1) for i in range(tp)])  2.59 us
  transfers between devices with their start and end apart: 19, of which 14 were waited for; matrix products, arithmetic and copies ran while one was open for 0% of the time, Pallas kernels for 2%

profile of v9, /device:TPU:0, one launch (start us, length us, event | category | flops | bytes accessed | tf_op | source)
XLA Modules:
  0.0 62.7 jit_solution(6809462500886043147)
XLA Ops:
  0.7 1.2 %fusion = (bf16[64,1024]{1,0:T(8,128)(2,1)S(1)}, bf16[64,1024]{1,0:T(8,128)(2,1)S(1)}, bf16[64,1024]{1,0:T(8,128)(2,1)S(1)}, bf16[64,1024]{1,0:T(8,128)(2,1)S(1)}) fusion(bf16[128,4096]{1,0:T(8,128)(2,1)} %param.8, s32[]{:T(128)S(6)} %select_n.27, s32[]{:T(128)S(6)} %select_n.31, s32[]{:T(128)S(6)} %select_n.29, s32[]{:T(128)S(6)} %select_n.28, s32[]{:T(128)S(6)} %select_n.30), kind=kLoop, calls=%fused_computation.1 | loop fusion | bytes 1048596 | tf_op jit(solution)/shard_map/dynamic_slice | solution.py:223
  2.2 0.5 collective-permute-start.3
  2.7 3.5 %collective-permute-start = (bf16[64,1024]{1,0:T(8,128)(2,1)S(1)}, bf16[64,1024]{1,0:T(8,128)(2,1)S(1)}, u32[]{:S(2)}, u32[]{:S(2)}) collective-permute-start(bf16[64,1024]{1,0:T(8,128)(2,1)S(1)} %get-tuple-element.43), channel_id=1, source_target_pairs={{0,24},{8,16},{16,8},{24,0},{1,25},{9,17},{17,9},{25,1},{2,26},{10... | collective-permute-start | bytes 393224 | tf_op jit(solution)/shard_map/ppermute | solution.py:206
  6.2 0.5 collective-permute-start.1
  6.9 3.5 %collective-permute-done.refs_1_ = bf16[64,1024]{1,0:T(8,128)(2,1)S(1)} collective-permute-done((bf16[64,1024]{1,0:T(8,128)(2,1)S(1)}, bf16[64,1024]{1,0:T(8,128)(2,1)S(1)}, u32[]{:S(2)}, u32[]{:S(2)}) %collective-permute-start) | collective-permute-done | bytes 131104 | tf_op jit(solution)/shard_map/ppermute | solution.py:206
  10.4 2.7 %collective-permute-done.1.refs_2_ = bf16[64,1024]{1,0:T(8,128)(2,1)S(1)} collective-permute-done((bf16[64,1024]{1,0:T(8,128)(2,1)S(1)}, bf16[64,1024]{1,0:T(8,128)(2,1)S(1)}, u32[]{:S(2)}, u32[]{:S(2)}) %collective-permute-start.1) | collective-permute-done | bytes 131104 | tf_op jit(solution)/shard_map/ppermute | solution.py:206
  13.5 1.0 %project.1 = (f32[264,384]{1,0:T(8,128)S(1)}, bf16[264,384]{1,0:T(8,128)(2,1)S(1)}, bf16[264,384]{1,0:T(8,128)(2,1)S(1)}, bf16[264,384]{1,0:T(8,128)(2,1)S(1)}) custom-call(bf16[64,1024]{1,0:T(8,128)(2,1)S(1)} %get-tuple-element.44.refs_0_, bf16[64,1024]{1,0:T(8,128)(2,1)S(1)} %collective-permute-done.refs_1_, ...), custom_call_target="tpu_custom_call" | custom-call | tf_op jit(solution)/shard_map/project/pallas_call | solution.py:211
  14.5 1.6 %collective-permute-start.4 = (bf16[264,384]{1,0:T(8,128)(2,1)S(1)}, bf16[264,384]{1,0:T(8,128)(2,1)S(1)}, u32[]{:S(2)}, u32[]{:S(2)}) collective-permute-start(bf16[264,384]{1,0:T(8,128)(2,1)S(1)} %get-tuple-element.26), channel_id=1, source_target_pairs={{0,8},{8,0},{16,24},{24,16},{1,9},{9,1},{17,25},{25,17},{2,10},{10... | collective-permute-start | bytes 608264 | tf_op jit(solution)/shard_map/ppermute | solution.py:206
  16.1 0.5 collective-permute-start.5
  16.6 1.5 %collective-permute-start.6 = (bf16[264,384]{1,0:T(8,128)(2,1)S(1)}, bf16[264,384]{1,0:T(8,128)(2,1)S(1)}, u32[]{:S(2)}, u32[]{:S(2)}) collective-permute-start(bf16[264,384]{1,0:T(8,128)(2,1)S(1)} %get-tuple-element.28), channel_id=1, source_target_pairs={{0,24},{8,16},{16,8},{24,0},{1,25},{9,17},{17,9},{25,1},{2,26},{10... | collective-permute-start | bytes 608264 | tf_op jit(solution)/shard_map/ppermute | solution.py:206
  18.1 4.3 %collective-permute-done.4.first = bf16[264,384]{1,0:T(8,128)(2,1)S(1)} collective-permute-done((bf16[264,384]{1,0:T(8,128)(2,1)S(1)}, bf16[264,384]{1,0:T(8,128)(2,1)S(1)}, u32[]{:S(2)}, u32[]{:S(2)}) %collective-permute-start.4) | collective-permute-done | bytes 202784 | tf_op jit(solution)/shard_map/ppermute | solution.py:206
  22.4 5.1 %collective-permute-done.5.second = bf16[264,384]{1,0:T(8,128)(2,1)S(1)} collective-permute-done((bf16[264,384]{1,0:T(8,128)(2,1)S(1)}, bf16[264,384]{1,0:T(8,128)(2,1)S(1)}, u32[]{:S(2)}, u32[]{:S(2)}) %collective-permute-start.5) | collective-permute-done | bytes 202784 | tf_op jit(solution)/shard_map/ppermute | solution.py:206
  27.8 1.3 %collective-permute-done.7.theirs = bf16[264,256]{1,0:T(8,128)(2,1)S(1)} collective-permute-done((bf16[264,256]{1,0:T(8,128)(2,1)S(1)}, bf16[264,256]{1,0:T(8,128)(2,1)S(1)}, u32[]{:S(2)}, u32[]{:S(2)}) %collective-permute-start.7) | collective-permute-done | bytes 135200 | tf_op jit(solution)/shard_map/ppermute | solution.py:199
  29.1 1.3 %attend.1.refs_0_ = bf16[264,128]{1,0:T(8,128)(2,1)S(1)} custom-call(s32[8]{0:T(128)S(1)} %copy-done.5, s32[4]{0:T(128)S(1)} %copy-done.6, bf16[264,128]{1,0:T(8,128)(2,1)S(1)} %get-tuple-element.29.query, bf16[264,256]{1,0:T(8,128)(2,1)S(1)} %get-tuple-element.30.mine, bf16[264,256]{1,0:T(8,128)(2,1)S(1)} %collective-permute-done.7.theirs), custom_call_target="tpu_custom_call" | custom-call | tf_op jit(solution)/shard_map/attend/pallas_call | solution.py:211
  30.5 0.6 collective-permute-start.10
  31.1 1.4 %collective-permute-start.9 = (bf16[264,128]{1,0:T(8,128)(2,1)S(1)}, bf16[264,128]{1,0:T(8,128)(2,1)S(1)}, u32[]{:S(2)}, u32[]{:S(2)}) collective-permute-start(bf16[264,128]{1,0:T(8,128)(2,1)S(1)} %attend.1.refs_0_), channel_id=1, source_target_pairs={{0,16},{8,24},{16,0},{24,8},{1,17},{9,25},{17,1},{25,9},{2,18},{10... | collective-permute-start | bytes 202760 | tf_op jit(solution)/shard_map/ppermute | solution.py:206
  32.5 1.5 %collective-permute-start.8 = (bf16[264,128]{1,0:T(8,128)(2,1)S(1)}, bf16[264,128]{1,0:T(8,128)(2,1)S(1)}, u32[]{:S(2)}, u32[]{:S(2)}) collective-permute-start(bf16[264,128]{1,0:T(8,128)(2,1)S(1)} %attend.1.refs_0_), channel_id=1, source_target_pairs={{0,24},{8,16},{16,8},{24,0},{1,25},{9,17},{17,9},{25,1},{2,26},{10... | collective-permute-start | bytes 202760 | tf_op jit(solution)/shard_map/ppermute | solution.py:206
  34.0 1.0 %collective-permute-done.10.refs_3_ = bf16[264,128]{1,0:T(8,128)(2,1)S(1)} collective-permute-done((bf16[264,128]{1,0:T(8,128)(2,1)S(1)}, bf16[264,128]{1,0:T(8,128)(2,1)S(1)}, u32[]{:S(2)}, u32[]{:S(2)}) %collective-permute-start.10) | collective-permute-done | bytes 67616 | tf_op jit(solution)/shard_map/ppermute | solution.py:206
  35.0 0.4 collective-permute-done.9.refs_2_
  35.4 2.3 %collective-permute-done.8.refs_1_ = bf16[264,128]{1,0:T(8,128)(2,1)S(1)} collective-permute-done((bf16[264,128]{1,0:T(8,128)(2,1)S(1)}, bf16[264,128]{1,0:T(8,128)(2,1)S(1)}, u32[]{:S(2)}, u32[]{:S(2)}) %collective-permute-start.8) | collective-permute-done | bytes 67616 | tf_op jit(solution)/shard_map/ppermute | solution.py:206
  37.7 0.5 project_out.1
  38.2 0.7 %collective-permute-start.12 = (bf16[72,1024]{1,0:T(8,128)(2,1)S(1)}, bf16[72,1024]{1,0:T(8,128)(2,1)S(1)}, u32[]{:S(2)}, u32[]{:S(2)}) collective-permute-start(bf16[72,1024]{1,0:T(8,128)(2,1)S(1)} %get-tuple-element.33), channel_id=1, source_target_pairs={{0,8},{8,0},{16,24},{24,16},{1,9},{9,1},{17,25},{25,17},{2,10},{10... | collective-permute-start | bytes 442376 | tf_op jit(solution)/shard_map/ppermute | solution.py:206
  38.9 1.5 %collective-permute-start.13 = (bf16[72,1024]{1,0:T(8,128)(2,1)S(1)}, bf16[72,1024]{1,0:T(8,128)(2,1)S(1)}, u32[]{:S(2)}, u32[]{:S(2)}) collective-permute-start(bf16[72,1024]{1,0:T(8,128)(2,1)S(1)} %get-tuple-element.34), channel_id=1, source_target_pairs={{0,16},{8,24},{16,0},{24,8},{1,17},{9,25},{17,1},{25,9},{2,18},{10... | collective-permute-start | bytes 442376 | tf_op jit(solution)/shard_map/ppermute | solution.py:206
  40.4 1.4 %collective-permute-start.14 = (bf16[72,1024]{1,0:T(8,128)(2,1)S(1)}, bf16[72,1024]{1,0:T(8,128)(2,1)S(1)}, u32[]{:S(2)}, u32[]{:S(2)}) collective-permute-start(bf16[72,1024]{1,0:T(8,128)(2,1)S(1)} %get-tuple-element.35), channel_id=1, source_target_pairs={{0,24},{8,16},{16,8},{24,0},{1,25},{9,17},{17,9},{25,1},{2,26},{10... | collective-permute-start | bytes 442376 | tf_op jit(solution)/shard_map/ppermute | solution.py:206
  41.8 2.3 %collective-permute-done.12.refs_1_ = bf16[72,1024]{1,0:T(8,128)(2,1)S(1)} collective-permute-done((bf16[72,1024]{1,0:T(8,128)(2,1)S(1)}, bf16[72,1024]{1,0:T(8,128)(2,1)S(1)}, u32[]{:S(2)}, u32[]{:S(2)}) %collective-permute-start.12) | collective-permute-done | bytes 147488 | tf_op jit(solution)/shard_map/ppermute | solution.py:206
  44.1 2.7 %collective-permute-done.13.refs_2_ = bf16[72,1024]{1,0:T(8,128)(2,1)S(1)} collective-permute-done((bf16[72,1024]{1,0:T(8,128)(2,1)S(1)}, bf16[72,1024]{1,0:T(8,128)(2,1)S(1)}, u32[]{:S(2)}, u32[]{:S(2)}) %collective-permute-start.13) | collective-permute-done | bytes 147488 | tf_op jit(solution)/shard_map/ppermute | solution.py:206
  46.9 1.7 %collective-permute-start.15 = (bf16[72,1024]{1,0:T(8,128)(2,1)S(1)}, bf16[72,1024]{1,0:T(8,128)(2,1)S(1)}, u32[]{:S(2)}, u32[]{:S(2)}) collective-permute-start(bf16[72,1024]{1,0:T(8,128)(2,1)S(1)} %get-tuple-element.37), channel_id=1, source_target_pairs={{0,2},{1,3},{2,0},{3,1},{4,6},{5,7},{6,4},{7,5},{8,10},{9,11},{10,... | collective-permute-start | bytes 442376 | tf_op jit(solution)/shard_map/ppermute | solution.py:202
  48.6 2.6 %collective-permute-start.16 = (bf16[72,1024]{1,0:T(8,128)(2,1)S(1)}, bf16[72,1024]{1,0:T(8,128)(2,1)S(1)}, u32[]{:S(2)}, u32[]{:S(2)}) collective-permute-start(bf16[72,1024]{1,0:T(8,128)(2,1)S(1)} %get-tuple-element.38), channel_id=1, source_target_pairs={{0,4},{1,5},{2,6},{3,7},{4,0},{5,1},{6,2},{7,3},{8,12},{9,13},{10,... | collective-permute-start | bytes 442376 | tf_op jit(solution)/shard_map/ppermute | solution.py:202
  51.4 1.5 %collective-permute-done.15.refs_1_ = bf16[72,1024]{1,0:T(8,128)(2,1)S(1)} collective-permute-done((bf16[72,1024]{1,0:T(8,128)(2,1)S(1)}, bf16[72,1024]{1,0:T(8,128)(2,1)S(1)}, u32[]{:S(2)}, u32[]{:S(2)}) %collective-permute-start.15) | collective-permute-done | bytes 147488 | tf_op jit(solution)/shard_map/ppermute | solution.py:202
  52.9 7.8 %collective-permute-done.16.refs_2_ = bf16[72,1024]{1,0:T(8,128)(2,1)S(1)} collective-permute-done((bf16[72,1024]{1,0:T(8,128)(2,1)S(1)}, bf16[72,1024]{1,0:T(8,128)(2,1)S(1)}, u32[]{:S(2)}, u32[]{:S(2)}) %collective-permute-start.16) | collective-permute-done | bytes 147488 | tf_op jit(solution)/shard_map/ppermute | solution.py:202
  60.8 1.2 %collective-permute-done.18.other = bf16[64,512]{1,0:T(8,128)(2,1)S(1)} collective-permute-done((bf16[64,512]{1,0:T(8,128)(2,1)S(1)}, bf16[64,512]{1,0:T(8,128)(2,1)S(1)}, u32[]{:S(2)}, u32[]{:S(2)}) %collective-permute-start.18) | collective-permute-done | bytes 65568 | tf_op jit(solution)/shard_map/ppermute | solution.py:199
  62.1 0.7 %finish.1 = (bf16[128,512]{1,0:T(8,128)(2,1)}, bf16[4,512]{1,0:T(4,128)(2,1)}) custom-call(bf16[72,512]{1,0:T(8,128)(2,1)S(1)} %get-tuple-element.40.keep, bf16[64,512]{1,0:T(8,128)(2,1)S(1)} %collective-permute-done.18.other), custom_call_target="tpu_custom_call" | custom-call | tf_op jit(solution)/shard_map/finish/pallas_call | solution.py:211
  (30 shorter events, 1.4 us)
Async XLA Ops:
  0.6 6.3 %copy-start = (bf16[4,4096]{1,0:T(4,128)(2,1)S(1)}, bf16[4,4096]{1,0:T(4,128)(2,1)}, u32[]{:S(2)}) copy-start(bf16[4,4096]{1,0:T(4,128)(2,1)} %param.9) | copy-start | bytes 98308
  0.7 1.3 %copy-start.2 = (bf16[1024,256]{1,0:T(8,128)(2,1)S(1)}, bf16[1024,256]{1,0:T(8,128)(2,1)}, u32[]{:S(2)}) copy-start(bf16[1024,256]{1,0:T(8,128)(2,1)} %refs_0_) | copy-start | bytes 1572868
  0.7 1.4 %copy-start.3 = (bf16[1024,128]{1,0:T(8,128)(2,1)S(1)}, bf16[1024,128]{1,0:T(8,128)(2,1)}, u32[]{:S(2)}) copy-start(bf16[1024,128]{1,0:T(8,128)(2,1)} %refs_1_) | copy-start | bytes 786436
  0.7 1.4 %copy-start.4 = (bf16[1024,128]{1,0:T(8,128)(2,1)S(1)}, bf16[1024,128]{1,0:T(8,128)(2,1)}, u32[]{:S(2)}) copy-start(bf16[1024,128]{1,0:T(8,128)(2,1)} %refs_2_) | copy-start | bytes 786436
  2.2 11.3 %collective-permute-start.3 = (bf16[1024,512]{1,0:T(8,128)(2,1)S(1)}, bf16[1024,512]{1,0:T(8,128)(2,1)S(1)}, u32[]{:S(2)}, u32[]{:S(2)}) collective-permute-start(bf16[1024,512]{1,0:T(8,128)(2,1)S(1)} %pack_weights.1.refs_5_), channel_id=1, source_target_pairs={{0,1},{1,0},{2,3},{3,2},{4,5},{5,4},{6,7},{7,6},{8,9},{9,8},{10,11... | collective-permute-start | bytes 3145736 | tf_op jit(solution)/shard_map/ppermute | solution.py:199
  2.7 7.7 %collective-permute-start = (bf16[64,1024]{1,0:T(8,128)(2,1)S(1)}, bf16[64,1024]{1,0:T(8,128)(2,1)S(1)}, u32[]{:S(2)}, u32[]{:S(2)}) collective-permute-start(bf16[64,1024]{1,0:T(8,128)(2,1)S(1)} %get-tuple-element.43), channel_id=1, source_target_pairs={{0,24},{8,16},{16,8},{24,0},{1,25},{9,17},{17,9},{25,1},{2,26},{10... | collective-permute-start | bytes 393224 | tf_op jit(solution)/shard_map/ppermute | solution.py:206
  6.2 6.9 %collective-permute-start.1 = (bf16[64,1024]{1,0:T(8,128)(2,1)S(1)}, bf16[64,1024]{1,0:T(8,128)(2,1)S(1)}, u32[]{:S(2)}, u32[]{:S(2)}) collective-permute-start(bf16[64,1024]{1,0:T(8,128)(2,1)S(1)} %get-tuple-element.45), channel_id=1, source_target_pairs={{0,16},{8,24},{16,0},{24,8},{1,17},{9,25},{17,1},{25,9},{2,18},{10... | collective-permute-start | bytes 393224 | tf_op jit(solution)/shard_map/ppermute | solution.py:206
  6.8 6.7 %collective-permute-start.2 = (bf16[64,1024]{1,0:T(8,128)(2,1)S(1)}, bf16[64,1024]{1,0:T(8,128)(2,1)S(1)}, u32[]{:S(2)}, u32[]{:S(2)}) collective-permute-start(bf16[64,1024]{1,0:T(8,128)(2,1)S(1)} %get-tuple-element.42), channel_id=1, source_target_pairs={{0,8},{8,0},{16,24},{24,16},{1,9},{9,1},{17,25},{25,17},{2,10},{10... | collective-permute-start | bytes 393224 | tf_op jit(solution)/shard_map/ppermute | solution.py:206
  13.5 1.0 %copy-start.1 = (bf16[256,1024]{1,0:T(8,128)(2,1)S(1)}, bf16[256,1024]{1,0:T(8,128)(2,1)}, u32[]{:S(2)}) copy-start(bf16[256,1024]{1,0:T(8,128)(2,1)} %refs_4_.1) | copy-start | bytes 1572868
  14.5 23.2 %collective-permute-start.11 = (bf16[256,1024]{1,0:T(8,128)(2,1)S(1)}, bf16[256,1024]{1,0:T(8,128)(2,1)S(1)}, u32[]{:S(2)}, u32[]{:S(2)}) collective-permute-start(bf16[256,1024]{1,0:T(8,128)(2,1)S(1)} %copy-done.1), channel_id=1, source_target_pairs={{0,1},{1,0},{2,3},{3,2},{4,5},{5,4},{6,7},{7,6},{8,9},{9,8},{10,11... | collective-permute-start | bytes 1572872 | tf_op jit(solution)/shard_map/ppermute | solution.py:199
  14.5 7.9 %collective-permute-start.4 = (bf16[264,384]{1,0:T(8,128)(2,1)S(1)}, bf16[264,384]{1,0:T(8,128)(2,1)S(1)}, u32[]{:S(2)}, u32[]{:S(2)}) collective-permute-start(bf16[264,384]{1,0:T(8,128)(2,1)S(1)} %get-tuple-element.26), channel_id=1, source_target_pairs={{0,8},{8,0},{16,24},{24,16},{1,9},{9,1},{17,25},{25,17},{2,10},{10... | collective-permute-start | bytes 608264 | tf_op jit(solution)/shard_map/ppermute | solution.py:206
  16.1 11.4 %collective-permute-start.5 = (bf16[264,384]{1,0:T(8,128)(2,1)S(1)}, bf16[264,384]{1,0:T(8,128)(2,1)S(1)}, u32[]{:S(2)}, u32[]{:S(2)}) collective-permute-start(bf16[264,384]{1,0:T(8,128)(2,1)S(1)} %get-tuple-element.27), channel_id=1, source_target_pairs={{0,16},{8,24},{16,0},{24,8},{1,17},{9,25},{17,1},{25,9},{2,18},{10... | collective-permute-start | bytes 608264 | tf_op jit(solution)/shard_map/ppermute | solution.py:206
  16.6 10.9 %collective-permute-start.6 = (bf16[264,384]{1,0:T(8,128)(2,1)S(1)}, bf16[264,384]{1,0:T(8,128)(2,1)S(1)}, u32[]{:S(2)}, u32[]{:S(2)}) collective-permute-start(bf16[264,384]{1,0:T(8,128)(2,1)S(1)} %get-tuple-element.28), channel_id=1, source_target_pairs={{0,24},{8,16},{16,8},{24,0},{1,25},{9,17},{17,9},{25,1},{2,26},{10... | collective-permute-start | bytes 608264 | tf_op jit(solution)/shard_map/ppermute | solution.py:206
  27.7 1.4 %copy-start.5 = (s32[8]{0:T(128)S(1)}, s32[8]{0:T(128)}, u32[]{:S(2)}) copy-start(s32[8]{0:T(128)} %block_map.1) | copy-start | bytes 100
  27.7 1.4 %copy-start.6 = (s32[4]{0:T(128)S(1)}, s32[4]{0:T(128)}, u32[]{:S(2)}) copy-start(s32[4]{0:T(128)} %lengths.1) | copy-start | bytes 52
  27.7 1.4 %collective-permute-start.7 = (bf16[264,256]{1,0:T(8,128)(2,1)S(1)}, bf16[264,256]{1,0:T(8,128)(2,1)S(1)}, u32[]{:S(2)}, u32[]{:S(2)}) collective-permute-start(bf16[264,256]{1,0:T(8,128)(2,1)S(1)} %get-tuple-element.30.mine), channel_id=1, source_target_pairs={{0,1},{1,0},{2,3},{3,2},{4,5},{5,4},{6,7},{7,6},{8,9},{9,8},{10,11... | collective-permute-start | bytes 405512 | tf_op jit(solution)/shard_map/ppermute | solution.py:199
  30.5 4.5 %collective-permute-start.10 = (bf16[264,128]{1,0:T(8,128)(2,1)S(1)}, bf16[264,128]{1,0:T(8,128)(2,1)S(1)}, u32[]{:S(2)}, u32[]{:S(2)}) collective-permute-start(bf16[264,128]{1,0:T(8,128)(2,1)S(1)} %attend.1.refs_0_), channel_id=1, source_target_pairs={{0,8},{8,0},{16,24},{24,16},{1,9},{9,1},{17,25},{25,17},{2,10},{10... | collective-permute-start | bytes 202760 | tf_op jit(solution)/shard_map/ppermute | solution.py:206
  31.1 4.3 %collective-permute-start.9 = (bf16[264,128]{1,0:T(8,128)(2,1)S(1)}, bf16[264,128]{1,0:T(8,128)(2,1)S(1)}, u32[]{:S(2)}, u32[]{:S(2)}) collective-permute-start(bf16[264,128]{1,0:T(8,128)(2,1)S(1)} %attend.1.refs_0_), channel_id=1, source_target_pairs={{0,16},{8,24},{16,0},{24,8},{1,17},{9,25},{17,1},{25,9},{2,18},{10... | collective-permute-start | bytes 202760 | tf_op jit(solution)/shard_map/ppermute | solution.py:206
  32.5 5.2 %collective-permute-start.8 = (bf16[264,128]{1,0:T(8,128)(2,1)S(1)}, bf16[264,128]{1,0:T(8,128)(2,1)S(1)}, u32[]{:S(2)}, u32[]{:S(2)}) collective-permute-start(bf16[264,128]{1,0:T(8,128)(2,1)S(1)} %attend.1.refs_0_), channel_id=1, source_target_pairs={{0,24},{8,16},{16,8},{24,0},{1,25},{9,17},{17,9},{25,1},{2,26},{10... | collective-permute-start | bytes 202760 | tf_op jit(solution)/shard_map/ppermute | solution.py:206
  38.2 5.9 %collective-permute-start.12 = (bf16[72,1024]{1,0:T(8,128)(2,1)S(1)}, bf16[72,1024]{1,0:T(8,128)(2,1)S(1)}, u32[]{:S(2)}, u32[]{:S(2)}) collective-permute-start(bf16[72,1024]{1,0:T(8,128)(2,1)S(1)} %get-tuple-element.33), channel_id=1, source_target_pairs={{0,8},{8,0},{16,24},{24,16},{1,9},{9,1},{17,25},{25,17},{2,10},{10... | collective-permute-start | bytes 442376 | tf_op jit(solution)/shard_map/ppermute | solution.py:206
  38.9 7.9 %collective-permute-start.13 = (bf16[72,1024]{1,0:T(8,128)(2,1)S(1)}, bf16[72,1024]{1,0:T(8,128)(2,1)S(1)}, u32[]{:S(2)}, u32[]{:S(2)}) collective-permute-start(bf16[72,1024]{1,0:T(8,128)(2,1)S(1)} %get-tuple-element.34), channel_id=1, source_target_pairs={{0,16},{8,24},{16,0},{24,8},{1,17},{9,25},{17,1},{25,9},{2,18},{10... | collective-permute-start | bytes 442376 | tf_op jit(solution)/shard_map/ppermute | solution.py:206
  40.4 6.4 %collective-permute-start.14 = (bf16[72,1024]{1,0:T(8,128)(2,1)S(1)}, bf16[72,1024]{1,0:T(8,128)(2,1)S(1)}, u32[]{:S(2)}, u32[]{:S(2)}) collective-permute-start(bf16[72,1024]{1,0:T(8,128)(2,1)S(1)} %get-tuple-element.35), channel_id=1, source_target_pairs={{0,24},{8,16},{16,8},{24,0},{1,25},{9,17},{17,9},{25,1},{2,26},{10... | collective-permute-start | bytes 442376 | tf_op jit(solution)/shard_map/ppermute | solution.py:206
  46.9 6.0 %collective-permute-start.15 = (bf16[72,1024]{1,0:T(8,128)(2,1)S(1)}, bf16[72,1024]{1,0:T(8,128)(2,1)S(1)}, u32[]{:S(2)}, u32[]{:S(2)}) collective-permute-start(bf16[72,1024]{1,0:T(8,128)(2,1)S(1)} %get-tuple-element.37), channel_id=1, source_target_pairs={{0,2},{1,3},{2,0},{3,1},{4,6},{5,7},{6,4},{7,5},{8,10},{9,11},{10,... | collective-permute-start | bytes 442376 | tf_op jit(solution)/shard_map/ppermute | solution.py:202
  48.6 12.0 %collective-permute-start.16 = (bf16[72,1024]{1,0:T(8,128)(2,1)S(1)}, bf16[72,1024]{1,0:T(8,128)(2,1)S(1)}, u32[]{:S(2)}, u32[]{:S(2)}) collective-permute-start(bf16[72,1024]{1,0:T(8,128)(2,1)S(1)} %get-tuple-element.38), channel_id=1, source_target_pairs={{0,4},{1,5},{2,6},{3,7},{4,0},{5,1},{6,2},{7,3},{8,12},{9,13},{10,... | collective-permute-start | bytes 442376 | tf_op jit(solution)/shard_map/ppermute | solution.py:202
  51.2 9.4 %collective-permute-start.17 = (bf16[72,1024]{1,0:T(8,128)(2,1)S(1)}, bf16[72,1024]{1,0:T(8,128)(2,1)S(1)}, u32[]{:S(2)}, u32[]{:S(2)}) collective-permute-start(bf16[72,1024]{1,0:T(8,128)(2,1)S(1)} %get-tuple-element.39), channel_id=1, source_target_pairs={{0,6},{1,7},{2,4},{3,5},{4,2},{5,3},{6,0},{7,1},{8,14},{9,15},{10,... | collective-permute-start | bytes 442376 | tf_op jit(solution)/shard_map/ppermute | solution.py:202
  60.7 1.3 %collective-permute-start.18 = (bf16[64,512]{1,0:T(8,128)(2,1)S(1)}, bf16[64,512]{1,0:T(8,128)(2,1)S(1)}, u32[]{:S(2)}, u32[]{:S(2)}) collective-permute-start(bf16[64,512]{1,0:T(8,128)(2,1)S(1)} %get-tuple-element.41), channel_id=1, source_target_pairs={{0,1},{1,0},{2,3},{3,2},{4,5},{5,4},{6,7},{7,6},{8,9},{9,8},{10,11... | collective-permute-start | bytes 196616 | tf_op jit(solution)/shard_map/ppermute | solution.py:199

commit v10 on v0

--- a/solution.py
+++ b/solution.py
@@ -1,11 +1,276 @@
+import functools
 import math
 
 import jax
 import jax.numpy as jnp
 from jax import lax
+from jax.experimental import pallas as pl
+from jax.experimental.pallas import tpu as pltpu
 from jax.sharding import PartitionSpec as P
 
 HEAD_SIZE = 128
+FLOOR = -1e30
+LAST = 1 << 30
+ROW_TILE = 8
+VMEM_BYTES = 48 * 1024 * 1024
+
+
+def vmem():
+    return pl.BlockSpec(memory_space=pltpu.VMEM)
+
+
+def smem():
+    return pl.BlockSpec(memory_space=pltpu.SMEM)
+
+
+def place():
+    t = lax.axis_index("tp")
+    return lax.axis_index("ctx"), t // 2, t % 2
+
+
+def project_kernel(rows, own, *refs):
+    (mine, theirs), refs = ([refs[2], *refs[:2]], [refs[5], *refs[3:5]]), refs[6:]
+    (new, *weights), refs = refs[:4], refs[4:]
+    held, new_held, *outs, inputs = refs
+    count = new.shape[0]
+    pad = new_held.shape[0]
+    tail = 4 * rows
+    _, _, k = place()
+    inputs[:rows, :] = own[...]
+    for number, pair in enumerate(zip(mine, theirs), 1):
+        for core, block in zip((k, 1 - k), pair):
+            first = number * rows + core * block.shape[0]
+            inputs[pl.ds(pl.multiple_of(first, block.shape[0]), block.shape[0]), :] = block[...]
+    inputs[tail:, :] = jnp.zeros_like(inputs[tail:, :])
+    inputs[tail : tail + count, :] = new[...]
+    x = inputs[...]
+    column = 0
+    for weight in (weights[0][...], jnp.concatenate([weights[1][...], weights[2][...]], axis=1)):
+        part = jnp.dot(x, weight, preferred_element_type=jnp.float32)
+        to = slice(column, column + weight.shape[1])
+        held[:, to] = part[:rows]
+        news = part[tail : tail + pad].astype(new_held.dtype)
+        new_held[:, to] = news
+        for step, out in enumerate(outs, 1):
+            out[:rows, to] = part[step * rows : (step + 1) * rows].astype(out.dtype)
+            out[rows:, to] = news
+        column += weight.shape[1]
+
+
+def add_kernel(own, new_own, first, second, both, held, new):
+    rows = held.shape[0]
+
+    def total(own, at):
+        parts = [own[...].astype(jnp.float32)]
+        parts += [ref[at, :].astype(jnp.float32) for ref in (first, second, both)]
+        return ((parts[0] + parts[1]) + (parts[2] + parts[3])).astype(held.dtype)
+
+    held[...] = total(own, slice(0, rows))
+    new[...] = total(new_own, slice(rows, None))
+
+
+def request_of(position, ends):
+    found = jnp.zeros_like(position)
+    for end in ends:
+        found = found + jnp.where(position >= end, 1, 0)
+    return found
+
+
+def attend_kernel(block_rows, count, scale, block_map, lengths, *refs):
+    blocks, new, attended = (refs[0], *refs[3:0:-1]), refs[4], refs[5]
+    rows, features = blocks[0].shape
+    head = HEAD_SIZE
+    q_width = features - 2 * head
+    pad = new.shape[0]
+    tail = len(blocks) * rows
+    c, _, _ = place()
+
+    def column(number):
+        at = slice(number * head, (number + 1) * head)
+        news = jnp.concatenate([new[:, at], jnp.zeros((head - pad, head), new.dtype)], axis=0)
+        return jnp.concatenate([block[:, at] for block in blocks], axis=0), news
+
+    keys, new_keys = column(q_width // head)
+    values, new_values = column(q_width // head + 1)
+
+    ends, total = [], 0
+    for request in range(count):
+        total = total + lengths[request]
+        ends.append(total)
+
+    def labels(shape, axis):
+        index = lax.broadcasted_iota(jnp.int32, shape, axis)
+        position = jnp.zeros(shape, jnp.int32)
+        per_device = rows // block_rows
+        for number in range(len(blocks) * per_device):
+            held = per_device * (c ^ (number // per_device)) + number % per_device
+            start = number * block_rows
+            inside = (index >= start) & (index < start + block_rows)
+            position = jnp.where(inside, block_map[held] * block_rows + index - start, position)
+        return position, request_of(position, ends)
+
+    q_position, q_request = labels((tail, 1), 0)
+    k_position, k_request = labels((1, tail), 1)
+    allowed = (q_request == k_request) & (k_position <= q_position)
+    new_rows = 2 * ROW_TILE
+    new_request = lax.broadcasted_iota(jnp.int32, (new_rows, 1), 0)
+    new_allowed = new_request == k_request
+    own_allowed = new_request == lax.broadcasted_iota(jnp.int32, (1, head), 1)
+
+    def scores_of(query, keys, allowed):
+        scores = lax.dot_general(
+            query, keys, (((1,), (1,)), ((), ())), preferred_element_type=jnp.float32
+        )
+        return jnp.where(allowed, scores * scale, FLOOR)
+
+    def mix(weights, values):
+        return jnp.dot(weights.astype(jnp.bfloat16), values, preferred_element_type=jnp.float32)
+
+    for number in range(q_width // head):
+        at = slice(number * head, (number + 1) * head)
+        query, new_query = column(number)
+        scores = scores_of(query, keys, allowed)
+        weights = jnp.exp(scores - jnp.max(scores, axis=1, keepdims=True))
+        denom = jnp.sum(weights, axis=1, keepdims=True)
+        attended[:tail, at] = (mix(weights, values) / denom).astype(jnp.bfloat16)
+        new_query = new_query[:new_rows]
+        scores = scores_of(new_query, keys, new_allowed)
+        own_scores = scores_of(new_query, new_keys, own_allowed)
+        peak = jnp.maximum(
+            jnp.max(scores, axis=1, keepdims=True), jnp.max(own_scores, axis=1, keepdims=True)
+        )
+        weights, own_weights = jnp.exp(scores - peak), jnp.exp(own_scores - peak)
+        denom = jnp.sum(weights, axis=1, keepdims=True)
+        denom += jnp.sum(own_weights, axis=1, keepdims=True)
+        mixed = (mix(weights, values) + mix(own_weights, new_values)) / denom
+        attended[tail:, at] = mixed[:pad].astype(jnp.bfloat16)
+
+
+def output_kernel(rows, mine, theirs, w_own, w_other, *outs):
+    _, _, k = place()
+    width = w_other.shape[1]
+    w_mine = w_own[:, pl.ds(pl.multiple_of(k * width, width), width)]
+    total = jnp.dot(mine[...], w_mine, preferred_element_type=jnp.float32)
+    total += jnp.dot(theirs[...], w_other[...], preferred_element_type=jnp.float32)
+    total = total.astype(outs[0].dtype)
+    for number, out in enumerate(outs):
+        out[:rows, :] = total[number * rows : (number + 1) * rows]
+        out[rows:, :] = total[len(outs) * rows :]
+
+
+def relay_kernel(*refs):
+    blocks, outs = refs[:4], refs[4:]
+    c, z, _ = place()
+    for slot, out in enumerate(outs):
+        for mask, block in enumerate(blocks):
+
+            @pl.when((c ^ z ^ slot) == mask)
+            def _(out=out, block=block):
+                out[...] = block[: out.shape[0], :]
+
+
+def finish_kernel(*refs):
+    parts, (prefill, decode) = refs[:4], refs[4:]
+    terms = [part[...].astype(jnp.float32) for part in parts]
+    total = ((terms[0] + terms[1]) + (terms[2] + terms[3])).astype(prefill.dtype)
+    rows = prefill.shape[0]
+    prefill[...] = total[:rows]
+    decode[...] = total[rows : rows + decode.shape[0]]
+
+
+def on_device_small(
+    steps, tp, tokens, new_token_states, w_query, key_matrix, value_matrix, w_out, lengths, block_map
+):
+    bf16, f32 = jnp.bfloat16, jnp.float32
+    rows = tokens.shape[0]
+    half = rows // 2
+    depth = w_query.shape[0]
+    count = new_token_states.shape[0]
+    pad = -(-count // ROW_TILE) * ROW_TILE
+    q_width = w_query.shape[1]
+    features = q_width + 2 * key_matrix.shape[1]
+    width = w_out.shape[1] // 2
+    all_rows = steps * rows + pad
+
+    def to_core(value):
+        return lax.ppermute(value, "tp", [(i, i ^ 1) for i in range(tp)])
+
+    def to_chip(value, step):
+        return lax.ppermute(value, "tp", [(i, i ^ (2 * step)) for i in range(tp)])
+
+    def to_partners(values):
+        return [
+            lax.ppermute(value, "ctx", [(i, i ^ mask) for i in range(steps)])
+            for mask, value in enumerate(values, 1)
+        ]
+
+    def call(kernel, name, inputs, shapes, scratch=(), spaces=None):
+        return pl.pallas_call(
+            kernel,
+            out_shape=[jax.ShapeDtypeStruct(shape, kind) for shape, kind in shapes],
+            in_specs=spaces or [vmem()] * len(inputs),
+            out_specs=[vmem()] * len(shapes),
+            scratch_shapes=list(scratch),
+            compiler_params=pltpu.CompilerParams(vmem_limit_bytes=VMEM_BYTES),
+            name=name,
+        )(*inputs)
+
+    c, _, k = place()
+    sent = [
+        lax.dynamic_slice(tokens, (k * half, (c ^ mask) * depth), (half, depth))
+        for mask in range(1, steps)
+    ]
+    own = lax.dynamic_slice_in_dim(tokens, c * depth, depth, 1)
+    new_columns = lax.dynamic_slice_in_dim(new_token_states, c * depth, depth, 1)
+    mine = to_partners(sent)
+    theirs = [to_core(value) for value in mine]
+
+    part = (rows + pad, features)
+    own_part, new_part, *parts = call(
+        functools.partial(project_kernel, rows),
+        "project",
+        (own, *mine[1:], mine[0], *theirs[1:], theirs[0], new_columns, w_query, key_matrix, value_matrix),
+        [((rows, features), f32), ((pad, features), bf16)] + [(part, bf16)] * (steps - 1),
+        [pltpu.VMEM((-(-all_rows // 16) * 16, depth), bf16)],
+    )
+
+    w_sent = lax.dynamic_slice_in_dim(w_out, (1 - k) * width, width, 1)
+    w_sent, _ = lax.optimization_barrier((w_sent, new_part))
+    w_other = to_core(w_sent)
+    new_part, w_other = lax.optimization_barrier((new_part, w_other))
+
+    held, new = call(
+        add_kernel,
+        "add_parts",
+        (own_part, new_part, *to_partners(parts)),
+        [((rows, features), bf16), ((pad, features), bf16)],
+    )
+
+    (attended,) = call(
+        functools.partial(
+            attend_kernel, steps * rows // block_map.shape[0], count, 1.0 / math.sqrt(HEAD_SIZE)
+        ),
+        "attend",
+        (block_map, lengths, held, *to_partners([held] * (steps - 1))[::-1], new),
+        [((all_rows, q_width), bf16)],
+        spaces=[smem()] * 2 + [vmem()] * (steps + 1),
+    )
+
+    block = (rows + pad, width)
+    outs = call(
+        functools.partial(output_kernel, rows),
+        "project_out",
+        (attended, to_core(attended), w_out, w_other),
+        [(block, bf16)] * steps,
+    )
+
+    slots = call(
+        relay_kernel, "relay", [outs[0]] + to_partners(outs[1:]), [(block, bf16)] * steps
+    )
+    slots = [slots[0]] + [to_chip(slot, step) for step, slot in enumerate(slots[1:], 1)]
+    return tuple(
+        call(finish_kernel, "finish", slots, [((rows, width), bf16), ((count, width), bf16)])
+    )
 
 
 floor_value = -1e30
@@ -57,7 +322,7 @@
     return (part_peak, part_total, part_mixed)
 
 
-def on_device(
+def on_device_large(
     tokens, new_token_states, w_query, key_matrix, value_matrix, w_out, lengths, block_map
 ):
     local_rows = tokens.shape[0]
@@ -188,8 +453,16 @@
     summed_rows = summed_rows.astype(jnp.bfloat16)
     return (summed_rows[:local_rows], summed_rows[local_rows:])
 
-
 def solution(mesh):
+    steps, tp = mesh.shape["ctx"], mesh.shape["tp"]
+
+    def on_device(tokens, *rest):
+        one_head = rest[2].shape[1] == HEAD_SIZE
+        small = steps == 4 and tp == 8 and one_head and tokens.shape[0] * steps <= 1024
+        if small:
+            return on_device_small(steps, tp, tokens, *rest)
+        return on_device_large(tokens, *rest)
+
     return jax.shard_map(
         on_device,
         mesh=mesh,

time: 184 us -> 63 us (0.34)
  waiting for transfers between devices: 106 us -> 35.5 us
  blocking collectives: 40.2 us -> 0 us
  starting transfers between devices: 4.76 us -> 20.2 us
  between operations: 14 us -> 0.82 us
  matrix products: 9.96 us -> 0 us
  local copies, waits for them, and re-layouts: 6.9 us -> 2.22 us
  Pallas kernels: 0 us -> 4.1 us
    all_gather x4 -> x0, waiting for transfers between devices: 104 us -> none  [the longest x1 27.1 us: on_device(): head_block = lax.all_gather(w_out, 'ctx', axis=1, tiled=True)]
    all_gather x3 -> x0, blocking collectives: 40.2 us -> none  [the longest x1 22.3 us: on_device(): lax.all_gather(attended_all, 'tp', axis=1, tiled=True)]
    ppermute x0 -> x20, waiting for transfers between devices: none -> 35.5 us  [the longest x12 23 us: to_partners(): lax.ppermute(value, 'ctx', [(i, i ^ mask) for i in range(steps)])]
    ppermute x0 -> x20, starting transfers between devices: none -> 20.2 us  [the longest x12 15.2 us: to_partners(): lax.ppermute(value, 'ctx', [(i, i ^ mask) for i in range(steps)])]
    dot_general x8 -> x0, matrix products: 9.96 us -> none  [the longest x3 5.41 us: on_device(): jnp.dot(inputs, weight, preferred_element_type=jnp.float32)]
    all_to_all x1 -> x0, starting transfers between devices: 4.61 us -> none  [on_device(): lax.all_to_all(head_block, 'tp', split_axis=1, concat_axis=0, tiled=True)]
    pallas_call x0 -> x6, Pallas kernels: none -> 4.1 us  [call(): pl.pallas_call(kernel, out_shape=[jax.ShapeDtypeStruct(shape, kind) for s...]
    unnamed x14, local copies, waits for them, and re-layouts: 2.88 us -> 0.04 us
  transfers between devices with their start and end apart: 5 -> 20, of which waited for: 4 -> 15; matrix products, arithmetic and copies ran while one was open for 6% -> 2% of each run, Pallas kernels for 0% -> 0%
where the time goes in v10:
time: 63 us; the launch traced here: 62.8 us
  waiting for transfers between devices  35.5 us (56%)
  starting transfers between devices  20.2 us (32%)
  Pallas kernels  4.1 us (7%)
  local copies, waits for them, and re-layouts  2.22 us (4%)
  between operations  0.82 us (1%)
    ppermute x12, waiting for transfers between devices, to_partners(): lax.ppermute(value, 'ctx', [(i, i ^ mask) for i in range(steps)])  23 us
    ppermute x12, starting transfers between devices, to_partners(): lax.ppermute(value, 'ctx', [(i, i ^ mask) for i in range(steps)])  15.2 us
    ppermute x3, waiting for transfers between devices, to_chip(): return lax.ppermute(value, 'tp', [(i, i ^ 2 * step) for i in range(tp)])  9.93 us
    ppermute x3, starting transfers between devices, to_chip(): return lax.ppermute(value, 'tp', [(i, i ^ 2 * step) for i in range(tp)])  4.45 us
    pallas_call x6, Pallas kernels, call(): pl.pallas_call(kernel, out_shape=[jax.ShapeDtypeStruct(shape, kind) for s...  4.1 us
    ppermute x5, waiting for transfers between devices, to_core(): return lax.ppermute(value, 'tp', [(i, i ^ 1) for i in range(tp)])  2.57 us
  transfers between devices with their start and end apart: 20, of which 15 were waited for; matrix products, arithmetic and copies ran while one was open for 2% of the time, Pallas kernels for 0%

profile of v10, /device:TPU:0, one launch (start us, length us, event | category | flops | bytes accessed | tf_op | source)
XLA Modules:
  0.0 62.8 jit_solution(6290774347551646492)
XLA Ops:
  0.7 1.1 %fusion = (bf16[64,1024]{1,0:T(8,128)(2,1)S(1)}, bf16[64,1024]{1,0:T(8,128)(2,1)S(1)}, bf16[64,1024]{1,0:T(8,128)(2,1)S(1)}) fusion(bf16[128,4096]{1,0:T(8,128)(2,1)} %param.8, s32[]{:T(128)S(6)} %select_n.30, s32[]{:T(128)S(6)} %select_n.33, s32[]{:T(128)S(6)} %select_n.31, s32[]{:T(128)S(6)} %select_n.32), kind=kLoop, calls=%fused_computation.3 | loop fusion | bytes 786448 | tf_op jit(solution)/shard_map/dynamic_slice | solution.py:220
  1.8 3.0 %collective-permute-start = (bf16[64,1024]{1,0:T(8,128)(2,1)S(1)}, bf16[64,1024]{1,0:T(8,128)(2,1)S(1)}, u32[]{:S(2)}, u32[]{:S(2)}) collective-permute-start(bf16[64,1024]{1,0:T(8,128)(2,1)S(1)} %get-tuple-element.39), channel_id=1, source_target_pairs={{0,16},{8,24},{16,0},{24,8},{1,17},{9,25},{17,1},{25,9},{2,18},{10... | collective-permute-start | bytes 393224 | tf_op jit(solution)/shard_map/ppermute | solution.py:203
  4.8 1.4 %collective-permute-start.1 = (bf16[64,1024]{1,0:T(8,128)(2,1)S(1)}, bf16[64,1024]{1,0:T(8,128)(2,1)S(1)}, u32[]{:S(2)}, u32[]{:S(2)}) collective-permute-start(bf16[64,1024]{1,0:T(8,128)(2,1)S(1)} %get-tuple-element.40), channel_id=1, source_target_pairs={{0,24},{8,16},{16,8},{24,0},{1,25},{9,17},{17,9},{25,1},{2,26},{10... | collective-permute-start | bytes 393224 | tf_op jit(solution)/shard_map/ppermute | solution.py:203
  6.4 1.0 %constant_dynamic-slice_fusion.2.own = bf16[128,1024]{1,0:T(8,128)(2,1)S(1)} fusion(bf16[128,4096]{1,0:T(8,128)(2,1)} %param.8, s32[]{:T(128)S(6)} %select_n.28), kind=kLoop, calls=%fused_computation.2 | loop fusion | bytes 524292 | tf_op jit(solution)/shard_map/dynamic_slice | solution.py:223
  7.4 3.0 %collective-permute-done.refs_0_ = bf16[64,1024]{1,0:T(8,128)(2,1)S(1)} collective-permute-done((bf16[64,1024]{1,0:T(8,128)(2,1)S(1)}, bf16[64,1024]{1,0:T(8,128)(2,1)S(1)}, u32[]{:S(2)}, u32[]{:S(2)}) %collective-permute-start) | collective-permute-done | bytes 131104 | tf_op jit(solution)/shard_map/ppermute | solution.py:203
  10.4 1.7 %collective-permute-done.1.refs_1_ = bf16[64,1024]{1,0:T(8,128)(2,1)S(1)} collective-permute-done((bf16[64,1024]{1,0:T(8,128)(2,1)S(1)}, bf16[64,1024]{1,0:T(8,128)(2,1)S(1)}, u32[]{:S(2)}, u32[]{:S(2)}) %collective-permute-start.1) | collective-permute-done | bytes 131104 | tf_op jit(solution)/shard_map/ppermute | solution.py:203
  12.8 0.7 %collective-permute-done.4.refs_4_ = bf16[64,1024]{1,0:T(8,128)(2,1)S(1)} collective-permute-done((bf16[64,1024]{1,0:T(8,128)(2,1)S(1)}, bf16[64,1024]{1,0:T(8,128)(2,1)S(1)}, u32[]{:S(2)}, u32[]{:S(2)}) %collective-permute-start.4) | collective-permute-done | bytes 131104 | tf_op jit(solution)/shard_map/ppermute | solution.py:196
  13.5 0.3 collective-permute-done.5.refs_5_
  13.8 0.7 %project.1 = (f32[128,512]{1,0:T(8,128)S(1)}, bf16[8,512]{1,0:T(8,128)(2,1)S(1)}, bf16[136,512]{1,0:T(8,128)(2,1)S(1)}, bf16[136,512]{1,0:T(8,128)(2,1)S(1)}, bf16[136,512]{1,0:T(8,128)(2,1)S(1)}) custom-call(bf16[128,1024]{1,0:T(8,128)(2,1)S(1)} %constant_dynamic-slice_fusion.2.own, bf16[64,1024]{1,0:T(8,128)(2,1)S(1)} %collective-permute-done.refs_0_, ...), custom_call_target="tpu_custom_call" | custom-call | tf_op jit(solution)/shard_map/project/pallas_call | solution.py:208
  14.8 1.6 %collective-permute-start.7 = (bf16[136,512]{1,0:T(8,128)(2,1)S(1)}, bf16[136,512]{1,0:T(8,128)(2,1)S(1)}, u32[]{:S(2)}, u32[]{:S(2)}) collective-permute-start(bf16[136,512]{1,0:T(8,128)(2,1)S(1)} %get-tuple-element.24), channel_id=1, source_target_pairs={{0,8},{8,0},{16,24},{24,16},{1,9},{9,1},{17,25},{25,17},{2,10},{10... | collective-permute-start | bytes 417800 | tf_op jit(solution)/shard_map/ppermute | solution.py:203
  16.5 1.5 %collective-permute-start.8 = (bf16[136,512]{1,0:T(8,128)(2,1)S(1)}, bf16[136,512]{1,0:T(8,128)(2,1)S(1)}, u32[]{:S(2)}, u32[]{:S(2)}) collective-permute-start(bf16[136,512]{1,0:T(8,128)(2,1)S(1)} %get-tuple-element.25), channel_id=1, source_target_pairs={{0,16},{8,24},{16,0},{24,8},{1,17},{9,25},{17,1},{25,9},{2,18},{10... | collective-permute-start | bytes 417800 | tf_op jit(solution)/shard_map/ppermute | solution.py:203
  18.0 0.3 collective-permute-start.9
  18.3 2.7 %collective-permute-done.7.first = bf16[136,512]{1,0:T(8,128)(2,1)S(1)} collective-permute-done((bf16[136,512]{1,0:T(8,128)(2,1)S(1)}, bf16[136,512]{1,0:T(8,128)(2,1)S(1)}, u32[]{:S(2)}, u32[]{:S(2)}) %collective-permute-start.7) | collective-permute-done | bytes 139296 | tf_op jit(solution)/shard_map/ppermute | solution.py:203
  21.1 4.0 %collective-permute-done.8.second = bf16[136,512]{1,0:T(8,128)(2,1)S(1)} collective-permute-done((bf16[136,512]{1,0:T(8,128)(2,1)S(1)}, bf16[136,512]{1,0:T(8,128)(2,1)S(1)}, u32[]{:S(2)}, u32[]{:S(2)}) %collective-permute-start.8) | collective-permute-done | bytes 139296 | tf_op jit(solution)/shard_map/ppermute | solution.py:203
  25.2 1.6 %collective-permute-start.10 = (bf16[128,512]{1,0:T(8,128)(2,1)S(1)}, bf16[128,512]{1,0:T(8,128)(2,1)S(1)}, u32[]{:S(2)}, u32[]{:S(2)}) collective-permute-start(bf16[128,512]{1,0:T(8,128)(2,1)S(1)} %get-tuple-element.27.refs_0_), channel_id=1, source_target_pairs={{0,24},{8,16},{16,8},{24,0},{1,25},{9,17},{17,9},{25,1},{2,26},{10... | collective-permute-start | bytes 393224 | tf_op jit(solution)/shard_map/ppermute | solution.py:203
  26.7 1.2 %collective-permute-start.11 = (bf16[128,512]{1,0:T(8,128)(2,1)S(1)}, bf16[128,512]{1,0:T(8,128)(2,1)S(1)}, u32[]{:S(2)}, u32[]{:S(2)}) collective-permute-start(bf16[128,512]{1,0:T(8,128)(2,1)S(1)} %get-tuple-element.27.refs_0_), channel_id=1, source_target_pairs={{0,16},{8,24},{16,0},{24,8},{1,17},{9,25},{17,1},{25,9},{2,18},{10... | collective-permute-start | bytes 393224 | tf_op jit(solution)/shard_map/ppermute | solution.py:203
  27.9 0.8 %collective-permute-start.12 = (bf16[128,512]{1,0:T(8,128)(2,1)S(1)}, bf16[128,512]{1,0:T(8,128)(2,1)S(1)}, u32[]{:S(2)}, u32[]{:S(2)}) collective-permute-start(bf16[128,512]{1,0:T(8,128)(2,1)S(1)} %get-tuple-element.27.refs_0_), channel_id=1, source_target_pairs={{0,8},{8,0},{16,24},{24,16},{1,9},{9,1},{17,25},{25,17},{2,10},{10... | collective-permute-start | bytes 393224 | tf_op jit(solution)/shard_map/ppermute | solution.py:203
  28.7 3.6 %collective-permute-done.10.refs_1_ = bf16[128,512]{1,0:T(8,128)(2,1)S(1)} collective-permute-done((bf16[128,512]{1,0:T(8,128)(2,1)S(1)}, bf16[128,512]{1,0:T(8,128)(2,1)S(1)}, u32[]{:S(2)}, u32[]{:S(2)}) %collective-permute-start.10) | collective-permute-done | bytes 131104 | tf_op jit(solution)/shard_map/ppermute | solution.py:203
  32.3 1.3 %collective-permute-done.11.refs_2_ = bf16[128,512]{1,0:T(8,128)(2,1)S(1)} collective-permute-done((bf16[128,512]{1,0:T(8,128)(2,1)S(1)}, bf16[128,512]{1,0:T(8,128)(2,1)S(1)}, u32[]{:S(2)}, u32[]{:S(2)}) %collective-permute-start.11) | collective-permute-done | bytes 131104 | tf_op jit(solution)/shard_map/ppermute | solution.py:203
  33.7 2.0 %attend.1.mine = bf16[520,256]{1,0:T(8,128)(2,1)S(1)} custom-call(s32[8]{0:T(128)S(1)} %copy-done.5, s32[4]{0:T(128)S(1)} %copy-done.6, bf16[128,512]{1,0:T(8,128)(2,1)S(1)} %get-tuple-element.27.refs_0_, bf16[128,512]{1,0:T(8,128)(2,1)S(1)} %collective-permute-done.10.refs_1_, bf16[128,512]{1,0:T(8,128)(2,1)S(1)} %collective-permute-done.11.refs_2_, ...), custom_call_target="tpu_custom_call" | custom-call | tf_op jit(solution)/shard_map/attend/pallas_call | solution.py:208
  35.8 1.5 %collective-permute-done.13.theirs = bf16[520,256]{1,0:T(8,128)(2,1)S(1)} collective-permute-done((bf16[520,256]{1,0:T(8,128)(2,1)S(1)}, bf16[520,256]{1,0:T(8,128)(2,1)S(1)}, u32[]{:S(2)}, u32[]{:S(2)}) %collective-permute-start.13) | collective-permute-done | bytes 266272 | tf_op jit(solution)/shard_map/ppermute | solution.py:196
  37.3 0.4 project_out.1
  37.7 1.5 %collective-permute-start.14 = (bf16[136,512]{1,0:T(8,128)(2,1)S(1)}, bf16[136,512]{1,0:T(8,128)(2,1)S(1)}, u32[]{:S(2)}, u32[]{:S(2)}) collective-permute-start(bf16[136,512]{1,0:T(8,128)(2,1)S(1)} %get-tuple-element.31), channel_id=1, source_target_pairs={{0,8},{8,0},{16,24},{24,16},{1,9},{9,1},{17,25},{25,17},{2,10},{10... | collective-permute-start | bytes 417800 | tf_op jit(solution)/shard_map/ppermute | solution.py:203
  39.2 0.6 collective-permute-start.15
  39.8 1.5 %collective-permute-start.16 = (bf16[136,512]{1,0:T(8,128)(2,1)S(1)}, bf16[136,512]{1,0:T(8,128)(2,1)S(1)}, u32[]{:S(2)}, u32[]{:S(2)}) collective-permute-start(bf16[136,512]{1,0:T(8,128)(2,1)S(1)} %get-tuple-element.33), channel_id=1, source_target_pairs={{0,24},{8,16},{16,8},{24,0},{1,25},{9,17},{17,9},{25,1},{2,26},{10... | collective-permute-start | bytes 417800 | tf_op jit(solution)/shard_map/ppermute | solution.py:203
  41.3 2.8 %collective-permute-done.14.refs_1_ = bf16[136,512]{1,0:T(8,128)(2,1)S(1)} collective-permute-done((bf16[136,512]{1,0:T(8,128)(2,1)S(1)}, bf16[136,512]{1,0:T(8,128)(2,1)S(1)}, u32[]{:S(2)}, u32[]{:S(2)}) %collective-permute-start.14) | collective-permute-done | bytes 139296 | tf_op jit(solution)/shard_map/ppermute | solution.py:203
  44.1 3.5 %collective-permute-done.15.refs_2_ = bf16[136,512]{1,0:T(8,128)(2,1)S(1)} collective-permute-done((bf16[136,512]{1,0:T(8,128)(2,1)S(1)}, bf16[136,512]{1,0:T(8,128)(2,1)S(1)}, u32[]{:S(2)}, u32[]{:S(2)}) %collective-permute-start.15) | collective-permute-done | bytes 139296 | tf_op jit(solution)/shard_map/ppermute | solution.py:203
  47.7 1.7 %collective-permute-start.17 = (bf16[136,512]{1,0:T(8,128)(2,1)S(1)}, bf16[136,512]{1,0:T(8,128)(2,1)S(1)}, u32[]{:S(2)}, u32[]{:S(2)}) collective-permute-start(bf16[136,512]{1,0:T(8,128)(2,1)S(1)} %get-tuple-element.35), channel_id=1, source_target_pairs={{0,2},{1,3},{2,0},{3,1},{4,6},{5,7},{6,4},{7,5},{8,10},{9,11},{10,... | collective-permute-start | bytes 417800 | tf_op jit(solution)/shard_map/ppermute | solution.py:199
  49.4 2.6 %collective-permute-start.18 = (bf16[136,512]{1,0:T(8,128)(2,1)S(1)}, bf16[136,512]{1,0:T(8,128)(2,1)S(1)}, u32[]{:S(2)}, u32[]{:S(2)}) collective-permute-start(bf16[136,512]{1,0:T(8,128)(2,1)S(1)} %get-tuple-element.36), channel_id=1, source_target_pairs={{0,4},{1,5},{2,6},{3,7},{4,0},{5,1},{6,2},{7,3},{8,12},{9,13},{10,... | collective-permute-start | bytes 417800 | tf_op jit(solution)/shard_map/ppermute | solution.py:199
  52.2 2.3 %collective-permute-done.17.refs_1_ = bf16[136,512]{1,0:T(8,128)(2,1)S(1)} collective-permute-done((bf16[136,512]{1,0:T(8,128)(2,1)S(1)}, bf16[136,512]{1,0:T(8,128)(2,1)S(1)}, u32[]{:S(2)}, u32[]{:S(2)}) %collective-permute-start.17) | collective-permute-done | bytes 139296 | tf_op jit(solution)/shard_map/ppermute | solution.py:199
  54.5 7.6 %collective-permute-done.18.refs_2_ = bf16[136,512]{1,0:T(8,128)(2,1)S(1)} collective-permute-done((bf16[136,512]{1,0:T(8,128)(2,1)S(1)}, bf16[136,512]{1,0:T(8,128)(2,1)S(1)}, u32[]{:S(2)}, u32[]{:S(2)}) %collective-permute-start.18) | collective-permute-done | bytes 139296 | tf_op jit(solution)/shard_map/ppermute | solution.py:199
  62.1 0.7 %finish.1 = (bf16[128,512]{1,0:T(8,128)(2,1)}, bf16[4,512]{1,0:T(4,128)(2,1)}) custom-call(bf16[136,512]{1,0:T(8,128)(2,1)S(1)} %get-tuple-element.34.refs_0_, bf16[136,512]{1,0:T(8,128)(2,1)S(1)} %collective-permute-done.17.refs_1_, bf16[136,512]{1,0:T(8,128)(2,1)S(1)} %collective-permute-done.18.refs_2_, bf16[136,512]{1,0:T(8,128)(2,1)S(1)} %collective-permute-done.19.refs_3_), custom_call_target="tpu_custom_call" | custom-call | tf_op jit(solution)/shard_map/finish/pallas_call | solution.py:208
  (32 shorter events, 1.5 us)
Async XLA Ops:
  0.6 12.0 %copy-start = (bf16[4,4096]{1,0:T(4,128)(2,1)S(1)}, bf16[4,4096]{1,0:T(4,128)(2,1)}, u32[]{:S(2)}) copy-start(bf16[4,4096]{1,0:T(4,128)(2,1)} %param.9) | copy-start | bytes 98308
  0.7 12.0 %copy-start.1 = (bf16[256,1024]{1,0:T(8,128)(2,1)S(1)}, bf16[256,1024]{1,0:T(8,128)(2,1)}, u32[]{:S(2)}) copy-start(bf16[256,1024]{1,0:T(8,128)(2,1)} %w_own.1) | copy-start | bytes 1572868
  1.8 8.6 %collective-permute-start = (bf16[64,1024]{1,0:T(8,128)(2,1)S(1)}, bf16[64,1024]{1,0:T(8,128)(2,1)S(1)}, u32[]{:S(2)}, u32[]{:S(2)}) collective-permute-start(bf16[64,1024]{1,0:T(8,128)(2,1)S(1)} %get-tuple-element.39), channel_id=1, source_target_pairs={{0,16},{8,24},{16,0},{24,8},{1,17},{9,25},{17,1},{25,9},{2,18},{10... | collective-permute-start | bytes 393224 | tf_op jit(solution)/shard_map/ppermute | solution.py:203
  4.8 7.3 %collective-permute-start.1 = (bf16[64,1024]{1,0:T(8,128)(2,1)S(1)}, bf16[64,1024]{1,0:T(8,128)(2,1)S(1)}, u32[]{:S(2)}, u32[]{:S(2)}) collective-permute-start(bf16[64,1024]{1,0:T(8,128)(2,1)S(1)} %get-tuple-element.40), channel_id=1, source_target_pairs={{0,24},{8,16},{16,8},{24,0},{1,25},{9,17},{17,9},{25,1},{2,26},{10... | collective-permute-start | bytes 393224 | tf_op jit(solution)/shard_map/ppermute | solution.py:203
  6.3 6.2 %collective-permute-start.2 = (bf16[64,1024]{1,0:T(8,128)(2,1)S(1)}, bf16[64,1024]{1,0:T(8,128)(2,1)S(1)}, u32[]{:S(2)}, u32[]{:S(2)}) collective-permute-start(bf16[64,1024]{1,0:T(8,128)(2,1)S(1)} %get-tuple-element.38), channel_id=1, source_target_pairs={{0,8},{8,0},{16,24},{24,16},{1,9},{9,1},{17,25},{25,17},{2,10},{10... | collective-permute-start | bytes 393224 | tf_op jit(solution)/shard_map/ppermute | solution.py:203
  6.4 7.4 %copy-start.2 = (bf16[1024,256]{1,0:T(8,128)(2,1)S(1)}, bf16[1024,256]{1,0:T(8,128)(2,1)}, u32[]{:S(2)}) copy-start(bf16[1024,256]{1,0:T(8,128)(2,1)} %refs_7_.1) | copy-start | bytes 1572868
  10.4 2.3 %collective-permute-start.3 = (bf16[64,1024]{1,0:T(8,128)(2,1)S(1)}, bf16[64,1024]{1,0:T(8,128)(2,1)S(1)}, u32[]{:S(2)}, u32[]{:S(2)}) collective-permute-start(bf16[64,1024]{1,0:T(8,128)(2,1)S(1)} %collective-permute-done.refs_0_), channel_id=1, source_target_pairs={{0,1},{1,0},{2,3},{3,2},{4,5},{5,4},{6,7},{7,6},{8,9},{9,8},{10,11... | collective-permute-start | bytes 393224 | tf_op jit(solution)/shard_map/ppermute | solution.py:196
  12.2 1.3 %collective-permute-start.4 = (bf16[64,1024]{1,0:T(8,128)(2,1)S(1)}, bf16[64,1024]{1,0:T(8,128)(2,1)S(1)}, u32[]{:S(2)}, u32[]{:S(2)}) collective-permute-start(bf16[64,1024]{1,0:T(8,128)(2,1)S(1)} %collective-permute-done.1.refs_1_), channel_id=1, source_target_pairs={{0,1},{1,0},{2,3},{3,2},{4,5},{5,4},{6,7},{7,6},{8,9},{9,8},{10,11... | collective-permute-start | bytes 393224 | tf_op jit(solution)/shard_map/ppermute | solution.py:196
  12.5 1.3 %collective-permute-start.5 = (bf16[64,1024]{1,0:T(8,128)(2,1)S(1)}, bf16[64,1024]{1,0:T(8,128)(2,1)S(1)}, u32[]{:S(2)}, u32[]{:S(2)}) collective-permute-start(bf16[64,1024]{1,0:T(8,128)(2,1)S(1)} %collective-permute-done.2.refs_2_), channel_id=1, source_target_pairs={{0,1},{1,0},{2,3},{3,2},{4,5},{5,4},{6,7},{7,6},{8,9},{9,8},{10,11... | collective-permute-start | bytes 393224 | tf_op jit(solution)/shard_map/ppermute | solution.py:196
  12.7 1.1 %copy-start.3 = (bf16[1024,128]{1,0:T(8,128)(2,1)S(1)}, bf16[1024,128]{1,0:T(8,128)(2,1)}, u32[]{:S(2)}) copy-start(bf16[1024,128]{1,0:T(8,128)(2,1)} %refs_8_.1) | copy-start | bytes 786436
  12.7 1.1 %copy-start.4 = (bf16[1024,128]{1,0:T(8,128)(2,1)S(1)}, bf16[1024,128]{1,0:T(8,128)(2,1)}, u32[]{:S(2)}) copy-start(bf16[1024,128]{1,0:T(8,128)(2,1)} %refs_9_.1) | copy-start | bytes 786436
  14.6 3.8 %collective-permute-start.6 = (bf16[256,512]{1,0:T(8,128)(2,1)S(1)}, bf16[256,512]{1,0:T(8,128)(2,1)S(1)}, u32[]{:S(2)}, u32[]{:S(2)}) collective-permute-start(bf16[256,512]{1,0:T(8,128)(2,1)S(1)} %constant_dynamic-slice_fusion), channel_id=1, source_target_pairs={{0,1},{1,0},{2,3},{3,2},{4,5},{5,4},{6,7},{7,6},{8,9},{9,8},{10,11... | collective-permute-start | bytes 786440 | tf_op jit(solution)/shard_map/ppermute | solution.py:196
  14.8 6.2 %collective-permute-start.7 = (bf16[136,512]{1,0:T(8,128)(2,1)S(1)}, bf16[136,512]{1,0:T(8,128)(2,1)S(1)}, u32[]{:S(2)}, u32[]{:S(2)}) collective-permute-start(bf16[136,512]{1,0:T(8,128)(2,1)S(1)} %get-tuple-element.24), channel_id=1, source_target_pairs={{0,8},{8,0},{16,24},{24,16},{1,9},{9,1},{17,25},{25,17},{2,10},{10... | collective-permute-start | bytes 417800 | tf_op jit(solution)/shard_map/ppermute | solution.py:203
  16.5 8.6 %collective-permute-start.8 = (bf16[136,512]{1,0:T(8,128)(2,1)S(1)}, bf16[136,512]{1,0:T(8,128)(2,1)S(1)}, u32[]{:S(2)}, u32[]{:S(2)}) collective-permute-start(bf16[136,512]{1,0:T(8,128)(2,1)S(1)} %get-tuple-element.25), channel_id=1, source_target_pairs={{0,16},{8,24},{16,0},{24,8},{1,17},{9,25},{17,1},{25,9},{2,18},{10... | collective-permute-start | bytes 417800 | tf_op jit(solution)/shard_map/ppermute | solution.py:203
  18.0 7.1 %collective-permute-start.9 = (bf16[136,512]{1,0:T(8,128)(2,1)S(1)}, bf16[136,512]{1,0:T(8,128)(2,1)S(1)}, u32[]{:S(2)}, u32[]{:S(2)}) collective-permute-start(bf16[136,512]{1,0:T(8,128)(2,1)S(1)} %get-tuple-element.26), channel_id=1, source_target_pairs={{0,24},{8,16},{16,8},{24,0},{1,25},{9,17},{17,9},{25,1},{2,26},{10... | collective-permute-start | bytes 417800 | tf_op jit(solution)/shard_map/ppermute | solution.py:203
  25.2 8.5 %copy-start.5 = (s32[8]{0:T(128)S(1)}, s32[8]{0:T(128)}, u32[]{:S(2)}) copy-start(s32[8]{0:T(128)} %block_map.1) | copy-start | bytes 100
  25.2 8.5 %copy-start.6 = (s32[4]{0:T(128)S(1)}, s32[4]{0:T(128)}, u32[]{:S(2)}) copy-start(s32[4]{0:T(128)} %lengths.1) | copy-start | bytes 52
  25.2 7.1 %collective-permute-start.10 = (bf16[128,512]{1,0:T(8,128)(2,1)S(1)}, bf16[128,512]{1,0:T(8,128)(2,1)S(1)}, u32[]{:S(2)}, u32[]{:S(2)}) collective-permute-start(bf16[128,512]{1,0:T(8,128)(2,1)S(1)} %get-tuple-element.27.refs_0_), channel_id=1, source_target_pairs={{0,24},{8,16},{16,8},{24,0},{1,25},{9,17},{17,9},{25,1},{2,26},{10... | collective-permute-start | bytes 393224 | tf_op jit(solution)/shard_map/ppermute | solution.py:203
  26.7 6.9 %collective-permute-start.11 = (bf16[128,512]{1,0:T(8,128)(2,1)S(1)}, bf16[128,512]{1,0:T(8,128)(2,1)S(1)}, u32[]{:S(2)}, u32[]{:S(2)}) collective-permute-start(bf16[128,512]{1,0:T(8,128)(2,1)S(1)} %get-tuple-element.27.refs_0_), channel_id=1, source_target_pairs={{0,16},{8,24},{16,0},{24,8},{1,17},{9,25},{17,1},{25,9},{2,18},{10... | collective-permute-start | bytes 393224 | tf_op jit(solution)/shard_map/ppermute | solution.py:203
  27.9 5.7 %collective-permute-start.12 = (bf16[128,512]{1,0:T(8,128)(2,1)S(1)}, bf16[128,512]{1,0:T(8,128)(2,1)S(1)}, u32[]{:S(2)}, u32[]{:S(2)}) collective-permute-start(bf16[128,512]{1,0:T(8,128)(2,1)S(1)} %get-tuple-element.27.refs_0_), channel_id=1, source_target_pairs={{0,8},{8,0},{16,24},{24,16},{1,9},{9,1},{17,25},{25,17},{2,10},{10... | collective-permute-start | bytes 393224 | tf_op jit(solution)/shard_map/ppermute | solution.py:203
  35.7 1.6 %collective-permute-start.13 = (bf16[520,256]{1,0:T(8,128)(2,1)S(1)}, bf16[520,256]{1,0:T(8,128)(2,1)S(1)}, u32[]{:S(2)}, u32[]{:S(2)}) collective-permute-start(bf16[520,256]{1,0:T(8,128)(2,1)S(1)} %attend.1.mine), channel_id=1, source_target_pairs={{0,1},{1,0},{2,3},{3,2},{4,5},{5,4},{6,7},{7,6},{8,9},{9,8},{10,11... | collective-permute-start | bytes 798728 | tf_op jit(solution)/shard_map/ppermute | solution.py:196
  37.7 6.4 %collective-permute-start.14 = (bf16[136,512]{1,0:T(8,128)(2,1)S(1)}, bf16[136,512]{1,0:T(8,128)(2,1)S(1)}, u32[]{:S(2)}, u32[]{:S(2)}) collective-permute-start(bf16[136,512]{1,0:T(8,128)(2,1)S(1)} %get-tuple-element.31), channel_id=1, source_target_pairs={{0,8},{8,0},{16,24},{24,16},{1,9},{9,1},{17,25},{25,17},{2,10},{10... | collective-permute-start | bytes 417800 | tf_op jit(solution)/shard_map/ppermute | solution.py:203
  39.2 8.4 %collective-permute-start.15 = (bf16[136,512]{1,0:T(8,128)(2,1)S(1)}, bf16[136,512]{1,0:T(8,128)(2,1)S(1)}, u32[]{:S(2)}, u32[]{:S(2)}) collective-permute-start(bf16[136,512]{1,0:T(8,128)(2,1)S(1)} %get-tuple-element.32), channel_id=1, source_target_pairs={{0,16},{8,24},{16,0},{24,8},{1,17},{9,25},{17,1},{25,9},{2,18},{10... | collective-permute-start | bytes 417800 | tf_op jit(solution)/shard_map/ppermute | solution.py:203
  39.8 7.8 %collective-permute-start.16 = (bf16[136,512]{1,0:T(8,128)(2,1)S(1)}, bf16[136,512]{1,0:T(8,128)(2,1)S(1)}, u32[]{:S(2)}, u32[]{:S(2)}) collective-permute-start(bf16[136,512]{1,0:T(8,128)(2,1)S(1)} %get-tuple-element.33), channel_id=1, source_target_pairs={{0,24},{8,16},{16,8},{24,0},{1,25},{9,17},{17,9},{25,1},{2,26},{10... | collective-permute-start | bytes 417800 | tf_op jit(solution)/shard_map/ppermute | solution.py:203
  47.7 6.7 %collective-permute-start.17 = (bf16[136,512]{1,0:T(8,128)(2,1)S(1)}, bf16[136,512]{1,0:T(8,128)(2,1)S(1)}, u32[]{:S(2)}, u32[]{:S(2)}) collective-permute-start(bf16[136,512]{1,0:T(8,128)(2,1)S(1)} %get-tuple-element.35), channel_id=1, source_target_pairs={{0,2},{1,3},{2,0},{3,1},{4,6},{5,7},{6,4},{7,5},{8,10},{9,11},{10,... | collective-permute-start | bytes 417800 | tf_op jit(solution)/shard_map/ppermute | solution.py:199
  49.4 12.7 %collective-permute-start.18 = (bf16[136,512]{1,0:T(8,128)(2,1)S(1)}, bf16[136,512]{1,0:T(8,128)(2,1)S(1)}, u32[]{:S(2)}, u32[]{:S(2)}) collective-permute-start(bf16[136,512]{1,0:T(8,128)(2,1)S(1)} %get-tuple-element.36), channel_id=1, source_target_pairs={{0,4},{1,5},{2,6},{3,7},{4,0},{5,1},{6,2},{7,3},{8,12},{9,13},{10,... | collective-permute-start | bytes 417800 | tf_op jit(solution)/shard_map/ppermute | solution.py:199
  52.0 10.2 %collective-permute-start.19 = (bf16[136,512]{1,0:T(8,128)(2,1)S(1)}, bf16[136,512]{1,0:T(8,128)(2,1)S(1)}, u32[]{:S(2)}, u32[]{:S(2)}) collective-permute-start(bf16[136,512]{1,0:T(8,128)(2,1)S(1)} %get-tuple-element.37), channel_id=1, source_target_pairs={{0,6},{1,7},{2,4},{3,5},{4,2},{5,3},{6,0},{7,1},{8,14},{9,15},{10,... | collective-permute-start | bytes 417800 | tf_op jit(solution)/shard_map/ppermute | solution.py:199

commit v11 on v10

--- a/solution.py
+++ b/solution.py
@@ -29,7 +29,7 @@
 
 
 def project_kernel(rows, own, *refs):
-    (mine, theirs), refs = ([refs[2], *refs[:2]], [refs[5], *refs[3:5]]), refs[6:]
+    (mine, theirs), refs = (refs[:3], refs[3:6]), refs[6:]
     (new, *weights), refs = refs[:4], refs[4:]
     held, new_held, *outs, inputs = refs
     count = new.shape[0]
@@ -77,7 +77,7 @@
 
 
 def attend_kernel(block_rows, count, scale, block_map, lengths, *refs):
-    blocks, new, attended = (refs[0], *refs[3:0:-1]), refs[4], refs[5]
+    blocks, new, attended = (refs[0], refs[2], refs[3], refs[1]), refs[4], refs[5]
     rows, features = blocks[0].shape
     head = HEAD_SIZE
     q_width = features - 2 * head
@@ -229,15 +229,10 @@
     own_part, new_part, *parts = call(
         functools.partial(project_kernel, rows),
         "project",
-        (own, *mine[1:], mine[0], *theirs[1:], theirs[0], new_columns, w_query, key_matrix, value_matrix),
+        (own, *mine, *theirs, new_columns, w_query, key_matrix, value_matrix),
         [((rows, features), f32), ((pad, features), bf16)] + [(part, bf16)] * (steps - 1),
         [pltpu.VMEM((-(-all_rows // 16) * 16, depth), bf16)],
     )
-
-    w_sent = lax.dynamic_slice_in_dim(w_out, (1 - k) * width, width, 1)
-    w_sent, _ = lax.optimization_barrier((w_sent, new_part))
-    w_other = to_core(w_sent)
-    new_part, w_other = lax.optimization_barrier((new_part, w_other))
 
     held, new = call(
         add_kernel,
@@ -246,15 +241,20 @@
         [((rows, features), bf16), ((pad, features), bf16)],
     )
 
+    first, second, both = to_partners([held] * (steps - 1))
     (attended,) = call(
         functools.partial(
             attend_kernel, steps * rows // block_map.shape[0], count, 1.0 / math.sqrt(HEAD_SIZE)
         ),
         "attend",
-        (block_map, lengths, held, *to_partners([held] * (steps - 1))[::-1], new),
+        (block_map, lengths, held, both, first, second, new),
         [((all_rows, q_width), bf16)],
         spaces=[smem()] * 2 + [vmem()] * (steps + 1),
     )
+
+    w_sent = lax.dynamic_slice_in_dim(w_out, (1 - k) * width, width, 1)
+    w_sent, _ = lax.optimization_barrier((w_sent, held))
+    w_other = to_core(w_sent)
 
     block = (rows + pad, width)
     outs = call(

time: 63 us -> 63 us (level)
    ppermute x5, waiting for transfers between devices: 2.57 us -> 1.33 us  [to_core(): return lax.ppermute(value, 'tp', [(i, i ^ 1) for i in range(tp)])]
  transfers between devices with their start and end apart: 20 -> 20, of which waited for: 15 -> 12; matrix products, arithmetic and copies ran while one was open for 2% -> 2% of each run, Pallas kernels for 0% -> 0%
where the time goes in v11:
time: 63 us; the launch traced here: 62.9 us
  waiting for transfers between devices  34.9 us (55%)
  starting transfers between devices  20.8 us (33%)
  Pallas kernels  4.1 us (7%)
  local copies, waits for them, and re-layouts  2.23 us (4%)
  between operations  0.83 us (1%)
    ppermute x12, waiting for transfers between devices, to_partners(): lax.ppermute(value, 'ctx', [(i, i ^ mask) for i in range(steps)])  23.4 us
    ppermute x12, starting transfers between devices, to_partners(): lax.ppermute(value, 'ctx', [(i, i ^ mask) for i in range(steps)])  15.2 us
    ppermute x3, waiting for transfers between devices, to_chip(): return lax.ppermute(value, 'tp', [(i, i ^ 2 * step) for i in range(tp)])  10.2 us
    ppermute x3, starting transfers between devices, to_chip(): return lax.ppermute(value, 'tp', [(i, i ^ 2 * step) for i in range(tp)])  4.45 us
    pallas_call x6, Pallas kernels, call(): pl.pallas_call(kernel, out_shape=[jax.ShapeDtypeStruct(shape, kind) for s...  4.1 us
    ppermute x5, waiting for transfers between devices, to_core(): return lax.ppermute(value, 'tp', [(i, i ^ 1) for i in range(tp)])  1.33 us
  transfers between devices with their start and end apart: 20, of which 12 were waited for; matrix products, arithmetic and copies ran while one was open for 2% of the time, Pallas kernels for 0%

profile of v11, /device:TPU:0, one launch (start us, length us, event | category | flops | bytes accessed | tf_op | source)
XLA Modules:
  0.0 62.9 jit_solution(6528081517884554562)
XLA Ops:
  0.7 1.1 %fusion = (bf16[64,1024]{1,0:T(8,128)(2,1)S(1)}, bf16[64,1024]{1,0:T(8,128)(2,1)S(1)}, bf16[64,1024]{1,0:T(8,128)(2,1)S(1)}) fusion(bf16[128,4096]{1,0:T(8,128)(2,1)} %param.8, s32[]{:T(128)S(6)} %select_n.30, s32[]{:T(128)S(6)} %select_n.33, s32[]{:T(128)S(6)} %select_n.31, s32[]{:T(128)S(6)} %select_n.32), kind=kLoop, calls=%fused_computation.3 | loop fusion | bytes 786448 | tf_op jit(solution)/shard_map/dynamic_slice | solution.py:220
  1.8 3.0 %collective-permute-start = (bf16[64,1024]{1,0:T(8,128)(2,1)S(1)}, bf16[64,1024]{1,0:T(8,128)(2,1)S(1)}, u32[]{:S(2)}, u32[]{:S(2)}) collective-permute-start(bf16[64,1024]{1,0:T(8,128)(2,1)S(1)} %get-tuple-element.35), channel_id=1, source_target_pairs={{0,8},{8,0},{16,24},{24,16},{1,9},{9,1},{17,25},{25,17},{2,10},{10... | collective-permute-start | bytes 393224 | tf_op jit(solution)/shard_map/ppermute | solution.py:203
  4.8 1.5 %collective-permute-start.1 = (bf16[64,1024]{1,0:T(8,128)(2,1)S(1)}, bf16[64,1024]{1,0:T(8,128)(2,1)S(1)}, u32[]{:S(2)}, u32[]{:S(2)}) collective-permute-start(bf16[64,1024]{1,0:T(8,128)(2,1)S(1)} %get-tuple-element.36), channel_id=1, source_target_pairs={{0,16},{8,24},{16,0},{24,8},{1,17},{9,25},{17,1},{25,9},{2,18},{10... | collective-permute-start | bytes 393224 | tf_op jit(solution)/shard_map/ppermute | solution.py:203
  6.4 2.4 %collective-permute-done.refs_0_ = bf16[64,1024]{1,0:T(8,128)(2,1)S(1)} collective-permute-done((bf16[64,1024]{1,0:T(8,128)(2,1)S(1)}, bf16[64,1024]{1,0:T(8,128)(2,1)S(1)}, u32[]{:S(2)}, u32[]{:S(2)}) %collective-permute-start) | collective-permute-done | bytes 131104 | tf_op jit(solution)/shard_map/ppermute | solution.py:203
  8.7 3.9 %collective-permute-done.1.refs_1_ = bf16[64,1024]{1,0:T(8,128)(2,1)S(1)} collective-permute-done((bf16[64,1024]{1,0:T(8,128)(2,1)S(1)}, bf16[64,1024]{1,0:T(8,128)(2,1)S(1)}, u32[]{:S(2)}, u32[]{:S(2)}) %collective-permute-start.1) | collective-permute-done | bytes 131104 | tf_op jit(solution)/shard_map/ppermute | solution.py:203
  12.6 0.5 collective-permute-start.5
  13.1 1.0 %constant_dynamic-slice_fusion.2.own = bf16[128,1024]{1,0:T(8,128)(2,1)S(1)} fusion(bf16[128,4096]{1,0:T(8,128)(2,1)} %param.8, s32[]{:T(128)S(6)} %select_n.28), kind=kLoop, calls=%fused_computation.2 | loop fusion | bytes 524292 | tf_op jit(solution)/shard_map/dynamic_slice | solution.py:223
  14.2 0.7 %project.1 = (f32[128,512]{1,0:T(8,128)S(1)}, bf16[8,512]{1,0:T(8,128)(2,1)S(1)}, bf16[136,512]{1,0:T(8,128)(2,1)S(1)}, bf16[136,512]{1,0:T(8,128)(2,1)S(1)}, bf16[136,512]{1,0:T(8,128)(2,1)S(1)}) custom-call(bf16[128,1024]{1,0:T(8,128)(2,1)S(1)} %constant_dynamic-slice_fusion.2.own, bf16[64,1024]{1,0:T(8,128)(2,1)S(1)} %collective-permute-done.refs_0_, ...), custom_call_target="tpu_custom_call" | custom-call | tf_op jit(solution)/shard_map/project/pallas_call | solution.py:208
  15.0 1.0 %collective-permute-start.6 = (bf16[136,512]{1,0:T(8,128)(2,1)S(1)}, bf16[136,512]{1,0:T(8,128)(2,1)S(1)}, u32[]{:S(2)}, u32[]{:S(2)}) collective-permute-start(bf16[136,512]{1,0:T(8,128)(2,1)S(1)} %get-tuple-element.20), channel_id=1, source_target_pairs={{0,8},{8,0},{16,24},{24,16},{1,9},{9,1},{17,25},{25,17},{2,10},{10... | collective-permute-start | bytes 417800 | tf_op jit(solution)/shard_map/ppermute | solution.py:203
  16.0 1.1 %collective-permute-start.7 = (bf16[136,512]{1,0:T(8,128)(2,1)S(1)}, bf16[136,512]{1,0:T(8,128)(2,1)S(1)}, u32[]{:S(2)}, u32[]{:S(2)}) collective-permute-start(bf16[136,512]{1,0:T(8,128)(2,1)S(1)} %get-tuple-element.21), channel_id=1, source_target_pairs={{0,16},{8,24},{16,0},{24,8},{1,17},{9,25},{17,1},{25,9},{2,18},{10... | collective-permute-start | bytes 417800 | tf_op jit(solution)/shard_map/ppermute | solution.py:203
  17.1 1.4 %collective-permute-start.8 = (bf16[136,512]{1,0:T(8,128)(2,1)S(1)}, bf16[136,512]{1,0:T(8,128)(2,1)S(1)}, u32[]{:S(2)}, u32[]{:S(2)}) collective-permute-start(bf16[136,512]{1,0:T(8,128)(2,1)S(1)} %get-tuple-element.22), channel_id=1, source_target_pairs={{0,24},{8,16},{16,8},{24,0},{1,25},{9,17},{17,9},{25,1},{2,26},{10... | collective-permute-start | bytes 417800 | tf_op jit(solution)/shard_map/ppermute | solution.py:203
  18.6 3.0 %collective-permute-done.6.first = bf16[136,512]{1,0:T(8,128)(2,1)S(1)} collective-permute-done((bf16[136,512]{1,0:T(8,128)(2,1)S(1)}, bf16[136,512]{1,0:T(8,128)(2,1)S(1)}, u32[]{:S(2)}, u32[]{:S(2)}) %collective-permute-start.6) | collective-permute-done | bytes 139296 | tf_op jit(solution)/shard_map/ppermute | solution.py:203
  21.6 1.6 %collective-permute-done.7.second = bf16[136,512]{1,0:T(8,128)(2,1)S(1)} collective-permute-done((bf16[136,512]{1,0:T(8,128)(2,1)S(1)}, bf16[136,512]{1,0:T(8,128)(2,1)S(1)}, u32[]{:S(2)}, u32[]{:S(2)}) %collective-permute-start.7) | collective-permute-done | bytes 139296 | tf_op jit(solution)/shard_map/ppermute | solution.py:203
  23.2 1.6 %collective-permute-done.8.both = bf16[136,512]{1,0:T(8,128)(2,1)S(1)} collective-permute-done((bf16[136,512]{1,0:T(8,128)(2,1)S(1)}, bf16[136,512]{1,0:T(8,128)(2,1)S(1)}, u32[]{:S(2)}, u32[]{:S(2)}) %collective-permute-start.8) | collective-permute-done | bytes 139296 | tf_op jit(solution)/shard_map/ppermute | solution.py:203
  24.9 0.9 %collective-permute-start.10 = (bf16[128,512]{1,0:T(8,128)(2,1)S(1)}, bf16[128,512]{1,0:T(8,128)(2,1)S(1)}, u32[]{:S(2)}, u32[]{:S(2)}) collective-permute-start(bf16[128,512]{1,0:T(8,128)(2,1)S(1)} %get-tuple-element.23.refs_0_), channel_id=1, source_target_pairs={{0,8},{8,0},{16,24},{24,16},{1,9},{9,1},{17,25},{25,17},{2,10},{10... | collective-permute-start | bytes 393224 | tf_op jit(solution)/shard_map/ppermute | solution.py:203
  25.8 1.5 %collective-permute-start.11 = (bf16[128,512]{1,0:T(8,128)(2,1)S(1)}, bf16[128,512]{1,0:T(8,128)(2,1)S(1)}, u32[]{:S(2)}, u32[]{:S(2)}) collective-permute-start(bf16[128,512]{1,0:T(8,128)(2,1)S(1)} %get-tuple-element.23.refs_0_), channel_id=1, source_target_pairs={{0,16},{8,24},{16,0},{24,8},{1,17},{9,25},{17,1},{25,9},{2,18},{10... | collective-permute-start | bytes 393224 | tf_op jit(solution)/shard_map/ppermute | solution.py:203
  27.3 1.2 %collective-permute-start.9 = (bf16[128,512]{1,0:T(8,128)(2,1)S(1)}, bf16[128,512]{1,0:T(8,128)(2,1)S(1)}, u32[]{:S(2)}, u32[]{:S(2)}) collective-permute-start(bf16[128,512]{1,0:T(8,128)(2,1)S(1)} %get-tuple-element.23.refs_0_), channel_id=1, source_target_pairs={{0,24},{8,16},{16,8},{24,0},{1,25},{9,17},{17,9},{25,1},{2,26},{10... | collective-permute-start | bytes 393224 | tf_op jit(solution)/shard_map/ppermute | solution.py:203
  28.4 2.8 %collective-permute-done.10.refs_2_ = bf16[128,512]{1,0:T(8,128)(2,1)S(1)} collective-permute-done((bf16[128,512]{1,0:T(8,128)(2,1)S(1)}, bf16[128,512]{1,0:T(8,128)(2,1)S(1)}, u32[]{:S(2)}, u32[]{:S(2)}) %collective-permute-start.10) | collective-permute-done | bytes 131104 | tf_op jit(solution)/shard_map/ppermute | solution.py:203
  31.2 2.1 %collective-permute-done.11.refs_3_ = bf16[128,512]{1,0:T(8,128)(2,1)S(1)} collective-permute-done((bf16[128,512]{1,0:T(8,128)(2,1)S(1)}, bf16[128,512]{1,0:T(8,128)(2,1)S(1)}, u32[]{:S(2)}, u32[]{:S(2)}) %collective-permute-start.11) | collective-permute-done | bytes 131104 | tf_op jit(solution)/shard_map/ppermute | solution.py:203
  33.3 2.0 %attend.1.mine = bf16[520,256]{1,0:T(8,128)(2,1)S(1)} custom-call(s32[8]{0:T(128)S(1)} %copy-done.5, s32[4]{0:T(128)S(1)} %copy-done.6, bf16[128,512]{1,0:T(8,128)(2,1)S(1)} %get-tuple-element.23.refs_0_, bf16[128,512]{1,0:T(8,128)(2,1)S(1)} %collective-permute-done.9.refs_1_, bf16[128,512]{1,0:T(8,128)(2,1)S(1)} %collective-permute-done.10.refs_2_, ...), custom_call_target="tpu_custom_call" | custom-call | tf_op jit(solution)/shard_map/attend/pallas_call | solution.py:208
  35.5 0.5 collective-permute-start.13
  36.0 1.3 %collective-permute-done.13.w_other = bf16[256,512]{1,0:T(8,128)(2,1)S(1)} collective-permute-done((bf16[256,512]{1,0:T(8,128)(2,1)S(1)}, bf16[256,512]{1,0:T(8,128)(2,1)S(1)}, u32[]{:S(2)}, u32[]{:S(2)}) %collective-permute-start.13) | collective-permute-done | bytes 262176 | tf_op jit(solution)/shard_map/ppermute | solution.py:196
  37.8 1.1 %collective-permute-start.14 = (bf16[136,512]{1,0:T(8,128)(2,1)S(1)}, bf16[136,512]{1,0:T(8,128)(2,1)S(1)}, u32[]{:S(2)}, u32[]{:S(2)}) collective-permute-start(bf16[136,512]{1,0:T(8,128)(2,1)S(1)} %get-tuple-element.27), channel_id=1, source_target_pairs={{0,8},{8,0},{16,24},{24,16},{1,9},{9,1},{17,25},{25,17},{2,10},{10... | collective-permute-start | bytes 417800 | tf_op jit(solution)/shard_map/ppermute | solution.py:203
  38.9 1.2 %collective-permute-start.15 = (bf16[136,512]{1,0:T(8,128)(2,1)S(1)}, bf16[136,512]{1,0:T(8,128)(2,1)S(1)}, u32[]{:S(2)}, u32[]{:S(2)}) collective-permute-start(bf16[136,512]{1,0:T(8,128)(2,1)S(1)} %get-tuple-element.28), channel_id=1, source_target_pairs={{0,16},{8,24},{16,0},{24,8},{1,17},{9,25},{17,1},{25,9},{2,18},{10... | collective-permute-start | bytes 417800 | tf_op jit(solution)/shard_map/ppermute | solution.py:203
  40.1 1.3 %collective-permute-start.16 = (bf16[136,512]{1,0:T(8,128)(2,1)S(1)}, bf16[136,512]{1,0:T(8,128)(2,1)S(1)}, u32[]{:S(2)}, u32[]{:S(2)}) collective-permute-start(bf16[136,512]{1,0:T(8,128)(2,1)S(1)} %get-tuple-element.29), channel_id=1, source_target_pairs={{0,24},{8,16},{16,8},{24,0},{1,25},{9,17},{17,9},{25,1},{2,26},{10... | collective-permute-start | bytes 417800 | tf_op jit(solution)/shard_map/ppermute | solution.py:203
  41.3 3.0 %collective-permute-done.14.refs_1_ = bf16[136,512]{1,0:T(8,128)(2,1)S(1)} collective-permute-done((bf16[136,512]{1,0:T(8,128)(2,1)S(1)}, bf16[136,512]{1,0:T(8,128)(2,1)S(1)}, u32[]{:S(2)}, u32[]{:S(2)}) %collective-permute-start.14) | collective-permute-done | bytes 139296 | tf_op jit(solution)/shard_map/ppermute | solution.py:203
  44.4 3.0 %collective-permute-done.15.refs_2_ = bf16[136,512]{1,0:T(8,128)(2,1)S(1)} collective-permute-done((bf16[136,512]{1,0:T(8,128)(2,1)S(1)}, bf16[136,512]{1,0:T(8,128)(2,1)S(1)}, u32[]{:S(2)}, u32[]{:S(2)}) %collective-permute-start.15) | collective-permute-done | bytes 139296 | tf_op jit(solution)/shard_map/ppermute | solution.py:203
  47.5 1.6 %collective-permute-start.17 = (bf16[136,512]{1,0:T(8,128)(2,1)S(1)}, bf16[136,512]{1,0:T(8,128)(2,1)S(1)}, u32[]{:S(2)}, u32[]{:S(2)}) collective-permute-start(bf16[136,512]{1,0:T(8,128)(2,1)S(1)} %get-tuple-element.31), channel_id=1, source_target_pairs={{0,2},{1,3},{2,0},{3,1},{4,6},{5,7},{6,4},{7,5},{8,10},{9,11},{10,... | collective-permute-start | bytes 417800 | tf_op jit(solution)/shard_map/ppermute | solution.py:199
  49.1 2.6 %collective-permute-start.18 = (bf16[136,512]{1,0:T(8,128)(2,1)S(1)}, bf16[136,512]{1,0:T(8,128)(2,1)S(1)}, u32[]{:S(2)}, u32[]{:S(2)}) collective-permute-start(bf16[136,512]{1,0:T(8,128)(2,1)S(1)} %get-tuple-element.32), channel_id=1, source_target_pairs={{0,4},{1,5},{2,6},{3,7},{4,0},{5,1},{6,2},{7,3},{8,12},{9,13},{10,... | collective-permute-start | bytes 417800 | tf_op jit(solution)/shard_map/ppermute | solution.py:199
  51.9 2.3 %collective-permute-done.17.refs_1_ = bf16[136,512]{1,0:T(8,128)(2,1)S(1)} collective-permute-done((bf16[136,512]{1,0:T(8,128)(2,1)S(1)}, bf16[136,512]{1,0:T(8,128)(2,1)S(1)}, u32[]{:S(2)}, u32[]{:S(2)}) %collective-permute-start.17) | collective-permute-done | bytes 139296 | tf_op jit(solution)/shard_map/ppermute | solution.py:199
  54.2 7.9 %collective-permute-done.18.refs_2_ = bf16[136,512]{1,0:T(8,128)(2,1)S(1)} collective-permute-done((bf16[136,512]{1,0:T(8,128)(2,1)S(1)}, bf16[136,512]{1,0:T(8,128)(2,1)S(1)}, u32[]{:S(2)}, u32[]{:S(2)}) %collective-permute-start.18) | collective-permute-done | bytes 139296 | tf_op jit(solution)/shard_map/ppermute | solution.py:199
  62.1 0.7 %finish.1 = (bf16[128,512]{1,0:T(8,128)(2,1)}, bf16[4,512]{1,0:T(4,128)(2,1)}) custom-call(bf16[136,512]{1,0:T(8,128)(2,1)S(1)} %get-tuple-element.30.refs_0_, bf16[136,512]{1,0:T(8,128)(2,1)S(1)} %collective-permute-done.17.refs_1_, bf16[136,512]{1,0:T(8,128)(2,1)S(1)} %collective-permute-done.18.refs_2_, bf16[136,512]{1,0:T(8,128)(2,1)S(1)} %collective-permute-done.19.refs_3_), custom_call_target="tpu_custom_call" | custom-call | tf_op jit(solution)/shard_map/finish/pallas_call | solution.py:208
  (32 shorter events, 1.0 us)
Async XLA Ops:
  0.6 12.5 %copy-start = (bf16[4,4096]{1,0:T(4,128)(2,1)S(1)}, bf16[4,4096]{1,0:T(4,128)(2,1)}, u32[]{:S(2)}) copy-start(bf16[4,4096]{1,0:T(4,128)(2,1)} %param.9) | copy-start | bytes 98308
  0.7 13.5 %copy-start.2 = (bf16[1024,256]{1,0:T(8,128)(2,1)S(1)}, bf16[1024,256]{1,0:T(8,128)(2,1)}, u32[]{:S(2)}) copy-start(bf16[1024,256]{1,0:T(8,128)(2,1)} %refs_7_.1) | copy-start | bytes 1572868
  1.8 6.9 %collective-permute-start = (bf16[64,1024]{1,0:T(8,128)(2,1)S(1)}, bf16[64,1024]{1,0:T(8,128)(2,1)S(1)}, u32[]{:S(2)}, u32[]{:S(2)}) collective-permute-start(bf16[64,1024]{1,0:T(8,128)(2,1)S(1)} %get-tuple-element.35), channel_id=1, source_target_pairs={{0,8},{8,0},{16,24},{24,16},{1,9},{9,1},{17,25},{25,17},{2,10},{10... | collective-permute-start | bytes 393224 | tf_op jit(solution)/shard_map/ppermute | solution.py:203
  4.8 7.8 %collective-permute-start.1 = (bf16[64,1024]{1,0:T(8,128)(2,1)S(1)}, bf16[64,1024]{1,0:T(8,128)(2,1)S(1)}, u32[]{:S(2)}, u32[]{:S(2)}) collective-permute-start(bf16[64,1024]{1,0:T(8,128)(2,1)S(1)} %get-tuple-element.36), channel_id=1, source_target_pairs={{0,16},{8,24},{16,0},{24,8},{1,17},{9,25},{17,1},{25,9},{2,18},{10... | collective-permute-start | bytes 393224 | tf_op jit(solution)/shard_map/ppermute | solution.py:203
  6.3 6.3 %collective-permute-start.2 = (bf16[64,1024]{1,0:T(8,128)(2,1)S(1)}, bf16[64,1024]{1,0:T(8,128)(2,1)S(1)}, u32[]{:S(2)}, u32[]{:S(2)}) collective-permute-start(bf16[64,1024]{1,0:T(8,128)(2,1)S(1)} %get-tuple-element.34), channel_id=1, source_target_pairs={{0,24},{8,16},{16,8},{24,0},{1,25},{9,17},{17,9},{25,1},{2,26},{10... | collective-permute-start | bytes 393224 | tf_op jit(solution)/shard_map/ppermute | solution.py:203
  8.7 5.5 %collective-permute-start.3 = (bf16[64,1024]{1,0:T(8,128)(2,1)S(1)}, bf16[64,1024]{1,0:T(8,128)(2,1)S(1)}, u32[]{:S(2)}, u32[]{:S(2)}) collective-permute-start(bf16[64,1024]{1,0:T(8,128)(2,1)S(1)} %collective-permute-done.refs_0_), channel_id=1, source_target_pairs={{0,1},{1,0},{2,3},{3,2},{4,5},{5,4},{6,7},{7,6},{8,9},{9,8},{10,11... | collective-permute-start | bytes 393224 | tf_op jit(solution)/shard_map/ppermute | solution.py:196
  12.6 1.6 %collective-permute-start.4 = (bf16[64,1024]{1,0:T(8,128)(2,1)S(1)}, bf16[64,1024]{1,0:T(8,128)(2,1)S(1)}, u32[]{:S(2)}, u32[]{:S(2)}) collective-permute-start(bf16[64,1024]{1,0:T(8,128)(2,1)S(1)} %collective-permute-done.1.refs_1_), channel_id=1, source_target_pairs={{0,1},{1,0},{2,3},{3,2},{4,5},{5,4},{6,7},{7,6},{8,9},{9,8},{10,11... | collective-permute-start | bytes 393224 | tf_op jit(solution)/shard_map/ppermute | solution.py:196
  12.6 1.6 %collective-permute-start.5 = (bf16[64,1024]{1,0:T(8,128)(2,1)S(1)}, bf16[64,1024]{1,0:T(8,128)(2,1)S(1)}, u32[]{:S(2)}, u32[]{:S(2)}) collective-permute-start(bf16[64,1024]{1,0:T(8,128)(2,1)S(1)} %collective-permute-done.2.refs_2_), channel_id=1, source_target_pairs={{0,1},{1,0},{2,3},{3,2},{4,5},{5,4},{6,7},{7,6},{8,9},{9,8},{10,11... | collective-permute-start | bytes 393224 | tf_op jit(solution)/shard_map/ppermute | solution.py:196
  13.1 1.1 %copy-start.3 = (bf16[1024,128]{1,0:T(8,128)(2,1)S(1)}, bf16[1024,128]{1,0:T(8,128)(2,1)}, u32[]{:S(2)}) copy-start(bf16[1024,128]{1,0:T(8,128)(2,1)} %refs_8_.1) | copy-start | bytes 786436
  13.1 1.1 %copy-start.4 = (bf16[1024,128]{1,0:T(8,128)(2,1)S(1)}, bf16[1024,128]{1,0:T(8,128)(2,1)}, u32[]{:S(2)}) copy-start(bf16[1024,128]{1,0:T(8,128)(2,1)} %refs_9_.1) | copy-start | bytes 786436
  15.0 6.6 %collective-permute-start.6 = (bf16[136,512]{1,0:T(8,128)(2,1)S(1)}, bf16[136,512]{1,0:T(8,128)(2,1)S(1)}, u32[]{:S(2)}, u32[]{:S(2)}) collective-permute-start(bf16[136,512]{1,0:T(8,128)(2,1)S(1)} %get-tuple-element.20), channel_id=1, source_target_pairs={{0,8},{8,0},{16,24},{24,16},{1,9},{9,1},{17,25},{25,17},{2,10},{10... | collective-permute-start | bytes 417800 | tf_op jit(solution)/shard_map/ppermute | solution.py:203
  16.0 7.2 %collective-permute-start.7 = (bf16[136,512]{1,0:T(8,128)(2,1)S(1)}, bf16[136,512]{1,0:T(8,128)(2,1)S(1)}, u32[]{:S(2)}, u32[]{:S(2)}) collective-permute-start(bf16[136,512]{1,0:T(8,128)(2,1)S(1)} %get-tuple-element.21), channel_id=1, source_target_pairs={{0,16},{8,24},{16,0},{24,8},{1,17},{9,25},{17,1},{25,9},{2,18},{10... | collective-permute-start | bytes 417800 | tf_op jit(solution)/shard_map/ppermute | solution.py:203
  17.1 7.7 %collective-permute-start.8 = (bf16[136,512]{1,0:T(8,128)(2,1)S(1)}, bf16[136,512]{1,0:T(8,128)(2,1)S(1)}, u32[]{:S(2)}, u32[]{:S(2)}) collective-permute-start(bf16[136,512]{1,0:T(8,128)(2,1)S(1)} %get-tuple-element.22), channel_id=1, source_target_pairs={{0,24},{8,16},{16,8},{24,0},{1,25},{9,17},{17,9},{25,1},{2,26},{10... | collective-permute-start | bytes 417800 | tf_op jit(solution)/shard_map/ppermute | solution.py:203
  24.8 8.5 %copy-start.5 = (s32[8]{0:T(128)S(1)}, s32[8]{0:T(128)}, u32[]{:S(2)}) copy-start(s32[8]{0:T(128)} %block_map.1) | copy-start | bytes 100
  24.8 8.5 %copy-start.6 = (s32[4]{0:T(128)S(1)}, s32[4]{0:T(128)}, u32[]{:S(2)}) copy-start(s32[4]{0:T(128)} %lengths.1) | copy-start | bytes 52
  24.9 10.6 %copy-start.1 = (bf16[256,1024]{1,0:T(8,128)(2,1)S(1)}, bf16[256,1024]{1,0:T(8,128)(2,1)}, u32[]{:S(2)}) copy-start(bf16[256,1024]{1,0:T(8,128)(2,1)} %w_own.1) | copy-start | bytes 1572868
  24.9 6.3 %collective-permute-start.10 = (bf16[128,512]{1,0:T(8,128)(2,1)S(1)}, bf16[128,512]{1,0:T(8,128)(2,1)S(1)}, u32[]{:S(2)}, u32[]{:S(2)}) collective-permute-start(bf16[128,512]{1,0:T(8,128)(2,1)S(1)} %get-tuple-element.23.refs_0_), channel_id=1, source_target_pairs={{0,8},{8,0},{16,24},{24,16},{1,9},{9,1},{17,25},{25,17},{2,10},{10... | collective-permute-start | bytes 393224 | tf_op jit(solution)/shard_map/ppermute | solution.py:203
  25.8 7.6 %collective-permute-start.11 = (bf16[128,512]{1,0:T(8,128)(2,1)S(1)}, bf16[128,512]{1,0:T(8,128)(2,1)S(1)}, u32[]{:S(2)}, u32[]{:S(2)}) collective-permute-start(bf16[128,512]{1,0:T(8,128)(2,1)S(1)} %get-tuple-element.23.refs_0_), channel_id=1, source_target_pairs={{0,16},{8,24},{16,0},{24,8},{1,17},{9,25},{17,1},{25,9},{2,18},{10... | collective-permute-start | bytes 393224 | tf_op jit(solution)/shard_map/ppermute | solution.py:203
  27.3 6.1 %collective-permute-start.9 = (bf16[128,512]{1,0:T(8,128)(2,1)S(1)}, bf16[128,512]{1,0:T(8,128)(2,1)S(1)}, u32[]{:S(2)}, u32[]{:S(2)}) collective-permute-start(bf16[128,512]{1,0:T(8,128)(2,1)S(1)} %get-tuple-element.23.refs_0_), channel_id=1, source_target_pairs={{0,24},{8,16},{16,8},{24,0},{1,25},{9,17},{17,9},{25,1},{2,26},{10... | collective-permute-start | bytes 393224 | tf_op jit(solution)/shard_map/ppermute | solution.py:203
  35.4 2.0 %collective-permute-start.12 = (bf16[520,256]{1,0:T(8,128)(2,1)S(1)}, bf16[520,256]{1,0:T(8,128)(2,1)S(1)}, u32[]{:S(2)}, u32[]{:S(2)}) collective-permute-start(bf16[520,256]{1,0:T(8,128)(2,1)S(1)} %attend.1.mine), channel_id=1, source_target_pairs={{0,1},{1,0},{2,3},{3,2},{4,5},{5,4},{6,7},{7,6},{8,9},{9,8},{10,11... | collective-permute-start | bytes 798728 | tf_op jit(solution)/shard_map/ppermute | solution.py:196
  35.5 1.9 %collective-permute-start.13 = (bf16[256,512]{1,0:T(8,128)(2,1)S(1)}, bf16[256,512]{1,0:T(8,128)(2,1)S(1)}, u32[]{:S(2)}, u32[]{:S(2)}) collective-permute-start(bf16[256,512]{1,0:T(8,128)(2,1)S(1)} %constant_dynamic-slice_fusion), channel_id=1, source_target_pairs={{0,1},{1,0},{2,3},{3,2},{4,5},{5,4},{6,7},{7,6},{8,9},{9,8},{10,11... | collective-permute-start | bytes 786440 | tf_op jit(solution)/shard_map/ppermute | solution.py:196
  37.8 6.6 %collective-permute-start.14 = (bf16[136,512]{1,0:T(8,128)(2,1)S(1)}, bf16[136,512]{1,0:T(8,128)(2,1)S(1)}, u32[]{:S(2)}, u32[]{:S(2)}) collective-permute-start(bf16[136,512]{1,0:T(8,128)(2,1)S(1)} %get-tuple-element.27), channel_id=1, source_target_pairs={{0,8},{8,0},{16,24},{24,16},{1,9},{9,1},{17,25},{25,17},{2,10},{10... | collective-permute-start | bytes 417800 | tf_op jit(solution)/shard_map/ppermute | solution.py:203
  38.9 8.5 %collective-permute-start.15 = (bf16[136,512]{1,0:T(8,128)(2,1)S(1)}, bf16[136,512]{1,0:T(8,128)(2,1)S(1)}, u32[]{:S(2)}, u32[]{:S(2)}) collective-permute-start(bf16[136,512]{1,0:T(8,128)(2,1)S(1)} %get-tuple-element.28), channel_id=1, source_target_pairs={{0,16},{8,24},{16,0},{24,8},{1,17},{9,25},{17,1},{25,9},{2,18},{10... | collective-permute-start | bytes 417800 | tf_op jit(solution)/shard_map/ppermute | solution.py:203
  40.1 7.3 %collective-permute-start.16 = (bf16[136,512]{1,0:T(8,128)(2,1)S(1)}, bf16[136,512]{1,0:T(8,128)(2,1)S(1)}, u32[]{:S(2)}, u32[]{:S(2)}) collective-permute-start(bf16[136,512]{1,0:T(8,128)(2,1)S(1)} %get-tuple-element.29), channel_id=1, source_target_pairs={{0,24},{8,16},{16,8},{24,0},{1,25},{9,17},{17,9},{25,1},{2,26},{10... | collective-permute-start | bytes 417800 | tf_op jit(solution)/shard_map/ppermute | solution.py:203
  47.5 6.7 %collective-permute-start.17 = (bf16[136,512]{1,0:T(8,128)(2,1)S(1)}, bf16[136,512]{1,0:T(8,128)(2,1)S(1)}, u32[]{:S(2)}, u32[]{:S(2)}) collective-permute-start(bf16[136,512]{1,0:T(8,128)(2,1)S(1)} %get-tuple-element.31), channel_id=1, source_target_pairs={{0,2},{1,3},{2,0},{3,1},{4,6},{5,7},{6,4},{7,5},{8,10},{9,11},{10,... | collective-permute-start | bytes 417800 | tf_op jit(solution)/shard_map/ppermute | solution.py:199
  49.1 13.0 %collective-permute-start.18 = (bf16[136,512]{1,0:T(8,128)(2,1)S(1)}, bf16[136,512]{1,0:T(8,128)(2,1)S(1)}, u32[]{:S(2)}, u32[]{:S(2)}) collective-permute-start(bf16[136,512]{1,0:T(8,128)(2,1)S(1)} %get-tuple-element.32), channel_id=1, source_target_pairs={{0,4},{1,5},{2,6},{3,7},{4,0},{5,1},{6,2},{7,3},{8,12},{9,13},{10,... | collective-permute-start | bytes 417800 | tf_op jit(solution)/shard_map/ppermute | solution.py:199
  51.7 10.5 %collective-permute-start.19 = (bf16[136,512]{1,0:T(8,128)(2,1)S(1)}, bf16[136,512]{1,0:T(8,128)(2,1)S(1)}, u32[]{:S(2)}, u32[]{:S(2)}) collective-permute-start(bf16[136,512]{1,0:T(8,128)(2,1)S(1)} %get-tuple-element.33), channel_id=1, source_target_pairs={{0,6},{1,7},{2,4},{3,5},{4,2},{5,3},{6,0},{7,1},{8,14},{9,15},{10,... | collective-permute-start | bytes 417800 | tf_op jit(solution)/shard_map/ppermute | solution.py:199

commit v12 on v11

--- a/solution.py
+++ b/solution.py
@@ -29,7 +29,7 @@
 
 
 def project_kernel(rows, own, *refs):
-    (mine, theirs), refs = (refs[:3], refs[3:6]), refs[6:]
+    (mine, theirs), refs = ((refs[2], *refs[:2]), (refs[5], *refs[3:5])), refs[6:]
     (new, *weights), refs = refs[:4], refs[4:]
     held, new_held, *outs, inputs = refs
     count = new.shape[0]
@@ -76,66 +76,83 @@
     return found
 
 
-def attend_kernel(block_rows, count, scale, block_map, lengths, *refs):
-    blocks, new, attended = (refs[0], refs[2], refs[3], refs[1]), refs[4], refs[5]
+def attend_kernel(sent, block_rows, count, scale, block_map, lengths, *refs):
+    blocks, new, refs = (refs[0], *refs[3:0:-1]), refs[4], refs[5:]
+    attended = refs[-1]
     rows, features = blocks[0].shape
     head = HEAD_SIZE
     q_width = features - 2 * head
     pad = new.shape[0]
-    tail = len(blocks) * rows
-    c, _, _ = place()
-
-    def column(number):
+    per_device = rows // block_rows
+    tail = len(blocks) * block_rows
+    c, z, _ = place()
+    half = 1 - z % 2 if sent else z % 2
+
+    def whole(number):
         at = slice(number * head, (number + 1) * head)
-        news = jnp.concatenate([new[:, at], jnp.zeros((head - pad, head), new.dtype)], axis=0)
-        return jnp.concatenate([block[:, at] for block in blocks], axis=0), news
-
-    keys, new_keys = column(q_width // head)
-    values, new_values = column(q_width // head + 1)
+        return jnp.concatenate([block[:, at] for block in blocks], axis=0)
+
+    def with_zeros(number):
+        at = slice(number * head, (number + 1) * head)
+        return jnp.concatenate([new[:, at], jnp.zeros((head - pad, head), new.dtype)], axis=0)
+
+    def queries(number):
+        at = slice(number * head, (number + 1) * head)
+        taken = pl.ds(pl.multiple_of(half * block_rows, block_rows), block_rows)
+        return jnp.concatenate([block[taken, at] for block in blocks], axis=0)
+
+    key_at, value_at = q_width // head, q_width // head + 1
+    keys, values = whole(key_at), whole(value_at)
 
     ends, total = [], 0
     for request in range(count):
         total = total + lengths[request]
         ends.append(total)
 
-    def labels(shape, axis):
+    def labels(shape, axis, held):
         index = lax.broadcasted_iota(jnp.int32, shape, axis)
         position = jnp.zeros(shape, jnp.int32)
-        per_device = rows // block_rows
-        for number in range(len(blocks) * per_device):
-            held = per_device * (c ^ (number // per_device)) + number % per_device
+        for number, block in enumerate(held):
             start = number * block_rows
             inside = (index >= start) & (index < start + block_rows)
-            position = jnp.where(inside, block_map[held] * block_rows + index - start, position)
+            position = jnp.where(inside, block_map[block] * block_rows + index - start, position)
         return position, request_of(position, ends)
 
-    q_position, q_request = labels((tail, 1), 0)
-    k_position, k_request = labels((1, tail), 1)
+    devices = [per_device * (c ^ mask) for mask in range(len(blocks))]
+    q_position, q_request = labels((tail, 1), 0, [first + half for first in devices])
+    held = [first + number for first in devices for number in range(per_device)]
+    k_position, k_request = labels((1, len(blocks) * rows), 1, held)
     allowed = (q_request == k_request) & (k_position <= q_position)
+
+    def scores_of(query, keys, allowed):
+        scores = lax.dot_general(
+            query, keys, (((1,), (1,)), ((), ())), preferred_element_type=jnp.float32
+        )
+        return jnp.where(allowed, scores * scale, FLOOR)
+
+    def mix(weights, values):
+        return jnp.dot(weights.astype(jnp.bfloat16), values, preferred_element_type=jnp.float32)
+
+    for number in range(q_width // head):
+        at = slice(number * head, (number + 1) * head)
+        scores = scores_of(queries(number), keys, allowed)
+        weights = jnp.exp(scores - jnp.max(scores, axis=1, keepdims=True))
+        denom = jnp.sum(weights, axis=1, keepdims=True)
+        attended[:tail, at] = (mix(weights, values) / denom).astype(jnp.bfloat16)
+    if not sent:
+        attended[tail:, :] = refs[0][tail:, :]
+        return
+
     new_rows = 2 * ROW_TILE
     new_request = lax.broadcasted_iota(jnp.int32, (new_rows, 1), 0)
     new_allowed = new_request == k_request
     own_allowed = new_request == lax.broadcasted_iota(jnp.int32, (1, head), 1)
-
-    def scores_of(query, keys, allowed):
-        scores = lax.dot_general(
-            query, keys, (((1,), (1,)), ((), ())), preferred_element_type=jnp.float32
-        )
-        return jnp.where(allowed, scores * scale, FLOOR)
-
-    def mix(weights, values):
-        return jnp.dot(weights.astype(jnp.bfloat16), values, preferred_element_type=jnp.float32)
-
+    new_keys, new_values = with_zeros(key_at), with_zeros(value_at)
     for number in range(q_width // head):
         at = slice(number * head, (number + 1) * head)
-        query, new_query = column(number)
-        scores = scores_of(query, keys, allowed)
-        weights = jnp.exp(scores - jnp.max(scores, axis=1, keepdims=True))
-        denom = jnp.sum(weights, axis=1, keepdims=True)
-        attended[:tail, at] = (mix(weights, values) / denom).astype(jnp.bfloat16)
-        new_query = new_query[:new_rows]
-        scores = scores_of(new_query, keys, new_allowed)
-        own_scores = scores_of(new_query, new_keys, own_allowed)
+        query = with_zeros(number)[:new_rows]
+        scores = scores_of(query, keys, new_allowed)
+        own_scores = scores_of(query, new_keys, own_allowed)
         peak = jnp.maximum(
             jnp.max(scores, axis=1, keepdims=True), jnp.max(own_scores, axis=1, keepdims=True)
         )
@@ -146,12 +163,14 @@
         attended[tail:, at] = mixed[:pad].astype(jnp.bfloat16)
 
 
-def output_kernel(rows, mine, theirs, w_own, w_other, *outs):
+def output_kernel(rows, *refs):
+    heads, (w_own, *weights), outs = refs[:4], refs[4:8], refs[8:]
     _, _, k = place()
-    width = w_other.shape[1]
+    width = outs[0].shape[1]
     w_mine = w_own[:, pl.ds(pl.multiple_of(k * width, width), width)]
-    total = jnp.dot(mine[...], w_mine, preferred_element_type=jnp.float32)
-    total += jnp.dot(theirs[...], w_other[...], preferred_element_type=jnp.float32)
+    total = jnp.dot(heads[0][...], w_mine, preferred_element_type=jnp.float32)
+    for ref, weight in zip(heads[1:], weights):
+        total += jnp.dot(ref[...], weight[...], preferred_element_type=jnp.float32)
     total = total.astype(outs[0].dtype)
     for number, out in enumerate(outs):
         out[:rows, :] = total[number * rows : (number + 1) * rows]
@@ -171,11 +190,15 @@
 
 def finish_kernel(*refs):
     parts, (prefill, decode) = refs[:4], refs[4:]
-    terms = [part[...].astype(jnp.float32) for part in parts]
-    total = ((terms[0] + terms[1]) + (terms[2] + terms[3])).astype(prefill.dtype)
-    rows = prefill.shape[0]
-    prefill[...] = total[:rows]
-    decode[...] = total[rows : rows + decode.shape[0]]
+    _, z, _ = place()
+    rows = prefill.shape[0] // 2
+    for odd in range(2):
+        total = parts[odd][...].astype(jnp.float32) + parts[odd + 2][...].astype(jnp.float32)
+        total = total.astype(prefill.dtype)
+        half = z % 2 if odd == 0 else 1 - z % 2
+        prefill[pl.ds(pl.multiple_of(half * rows, rows), rows), :] = total[:rows]
+        if odd == 0:
+            decode[...] = total[rows : rows + decode.shape[0]]
 
 
 def on_device_small(
@@ -225,14 +248,22 @@
     mine = to_partners(sent)
     theirs = [to_core(value) for value in mine]
 
+    w_mine = lax.dynamic_slice_in_dim(w_out, k * width, width, 1)
+    w_theirs = lax.dynamic_slice_in_dim(w_out, (1 - k) * width, width, 1)
+    w_next = to_chip(w_mine, 1)
+    new_columns, w_next = lax.optimization_barrier((new_columns, w_next))
+
     part = (rows + pad, features)
     own_part, new_part, *parts = call(
         functools.partial(project_kernel, rows),
         "project",
-        (own, *mine, *theirs, new_columns, w_query, key_matrix, value_matrix),
+        (own, *mine[1:], mine[0], *theirs[1:], theirs[0], new_columns, w_query, key_matrix, value_matrix),
         [((rows, features), f32), ((pad, features), bf16)] + [(part, bf16)] * (steps - 1),
         [pltpu.VMEM((-(-all_rows // 16) * 16, depth), bf16)],
     )
+
+    w_later, _ = lax.optimization_barrier((w_theirs, new_part))
+    w_next_other = lax.ppermute(w_later, "tp", [(i, i ^ 3) for i in range(tp)])
 
     held, new = call(
         add_kernel,
@@ -242,30 +273,40 @@
     )
 
     first, second, both = to_partners([held] * (steps - 1))
-    (attended,) = call(
-        functools.partial(
-            attend_kernel, steps * rows // block_map.shape[0], count, 1.0 / math.sqrt(HEAD_SIZE)
-        ),
-        "attend",
-        (block_map, lengths, held, both, first, second, new),
-        [((all_rows, q_width), bf16)],
-        spaces=[smem()] * 2 + [vmem()] * (steps + 1),
-    )
-
-    w_sent = lax.dynamic_slice_in_dim(w_out, (1 - k) * width, width, 1)
-    w_sent, _ = lax.optimization_barrier((w_sent, held))
-    w_other = to_core(w_sent)
-
-    block = (rows + pad, width)
+    new, w_next_other = lax.optimization_barrier((new, w_next_other))
+    block_rows = steps * rows // block_map.shape[0]
+
+    def attend(sent, *extra):
+        (attended,) = call(
+            functools.partial(
+                attend_kernel, sent, block_rows, count, 1.0 / math.sqrt(HEAD_SIZE)
+            ),
+            "attend_sent" if sent else "attend_kept",
+            (block_map, lengths, held, both, second, first, new, *extra),
+            [((steps * block_rows + pad, q_width), bf16)],
+            spaces=[smem()] * 2 + [vmem()] * (steps + 1 + len(extra)),
+        )
+        return attended
+
+    sent = attend(True)
+    got = to_chip(sent, 1)
+    kept = attend(False, sent)
+    w_last, _ = lax.optimization_barrier((w_theirs, held))
+    w_other = to_core(w_last)
+
+    block = (block_rows + pad, width)
     outs = call(
-        functools.partial(output_kernel, rows),
+        functools.partial(output_kernel, block_rows),
         "project_out",
-        (attended, to_core(attended), w_out, w_other),
+        (kept, to_core(kept), got, to_core(got), w_out, w_other, w_next, w_next_other),
         [(block, bf16)] * steps,
     )
 
     slots = call(
-        relay_kernel, "relay", [outs[0]] + to_partners(outs[1:]), [(block, bf16)] * steps
+        relay_kernel,
+        "relay",
+        [outs[0]] + to_partners(outs[1:]),
+        [(block if i % 2 == 0 else (block_rows, width), bf16) for i in range(steps)],
     )
     slots = [slots[0]] + [to_chip(slot, step) for step, slot in enumerate(slots[1:], 1)]
     return tuple(
@@ -458,7 +499,9 @@
 
     def on_device(tokens, *rest):
         one_head = rest[2].shape[1] == HEAD_SIZE
-        small = steps == 4 and tp == 8 and one_head and tokens.shape[0] * steps <= 1024
+        two_blocks = rest[-1].shape[0] == 2 * steps
+        few = tokens.shape[0] * steps <= 1024
+        small = steps == 4 and tp == 8 and one_head and two_blocks and few
         if small:
             return on_device_small(steps, tp, tokens, *rest)
         return on_device_large(tokens, *rest)

time: 63 us -> 61 us (0.968)
  waiting for transfers between devices: 34.9 us -> 27.5 us
  starting transfers between devices: 20.8 us -> 25.1 us
  Pallas kernels: 4.1 us -> 5.28 us
    ppermute x12, waiting for transfers between devices: 23.4 us -> 18.8 us  [to_partners(): lax.ppermute(value, 'ctx', [(i, i ^ mask) for i in range(steps)])]
    ppermute x3 -> x5, starting transfers between devices: 4.45 us -> 8.17 us  [to_chip(): return lax.ppermute(value, 'tp', [(i, i ^ 2 * step) for i in range(tp)])]
    ppermute x3 -> x5, waiting for transfers between devices: 10.2 us -> 7.3 us  [to_chip(): return lax.ppermute(value, 'tp', [(i, i ^ 2 * step) for i in range(tp)])]
    pallas_call x6 -> x7, Pallas kernels: 4.1 us -> 5.28 us  [call(): pl.pallas_call(kernel, out_shape=[jax.ShapeDtypeStruct(shape, kind) for s...]
    ppermute x0 -> x1, starting transfers between devices: none -> 0.63 us  [on_device_small(): w_next_other = lax.ppermute(w_later, 'tp', [(i, i ^ 3) for i in range(tp)])]
    ppermute x5 -> x6, waiting for transfers between devices: 1.33 us -> 1.35 us  [to_core(): return lax.ppermute(value, 'tp', [(i, i ^ 1) for i in range(tp)])]
  transfers between devices with their start and end apart: 20 -> 24, of which waited for: 12 -> 15; matrix products, arithmetic and copies ran while one was open for 2% -> 2% of each run, Pallas kernels for 0% -> 2%
where the time goes in v12:
time: 61 us; the launch traced here: 60.9 us
  waiting for transfers between devices  27.5 us (45%)
  starting transfers between devices  25.1 us (41%)
  Pallas kernels  5.28 us (9%)
  local copies, waits for them, and re-layouts  2.17 us (4%)
  between operations  0.84 us (1%)
    ppermute x12, waiting for transfers between devices, to_partners(): lax.ppermute(value, 'ctx', [(i, i ^ mask) for i in range(steps)])  18.8 us
    ppermute x12, starting transfers between devices, to_partners(): lax.ppermute(value, 'ctx', [(i, i ^ mask) for i in range(steps)])  15.2 us
    ppermute x5, starting transfers between devices, to_chip(): return lax.ppermute(value, 'tp', [(i, i ^ 2 * step) for i in range(tp)])  8.17 us
    ppermute x5, waiting for transfers between devices, to_chip(): return lax.ppermute(value, 'tp', [(i, i ^ 2 * step) for i in range(tp)])  7.3 us
    pallas_call x7, Pallas kernels, call(): pl.pallas_call(kernel, out_shape=[jax.ShapeDtypeStruct(shape, kind) for s...  5.28 us
    ppermute x6, waiting for transfers between devices, to_core(): return lax.ppermute(value, 'tp', [(i, i ^ 1) for i in range(tp)])  1.35 us
  transfers between devices with their start and end apart: 24, of which 15 were waited for; matrix products, arithmetic and copies ran while one was open for 2% of the time, Pallas kernels for 2%

profile of v12, /device:TPU:0, one launch (start us, length us, event | category | flops | bytes accessed | tf_op | source)
XLA Modules:
  0.0 60.9 jit_solution(17213892013932559597)
XLA Ops:
  0.7 1.1 %fusion = (bf16[64,1024]{1,0:T(8,128)(2,1)S(1)}, bf16[64,1024]{1,0:T(8,128)(2,1)S(1)}, bf16[64,1024]{1,0:T(8,128)(2,1)S(1)}) fusion(bf16[128,4096]{1,0:T(8,128)(2,1)} %param.8, s32[]{:T(128)S(6)} %select_n.33, s32[]{:T(128)S(6)} %select_n.36, s32[]{:T(128)S(6)} %select_n.34, s32[]{:T(128)S(6)} %select_n.35), kind=kLoop, calls=%fused_computation.4 | loop fusion | bytes 786448 | tf_op jit(solution)/shard_map/dynamic_slice | solution.py:243
  1.8 3.0 %collective-permute-start.2 = (bf16[64,1024]{1,0:T(8,128)(2,1)S(1)}, bf16[64,1024]{1,0:T(8,128)(2,1)S(1)}, u32[]{:S(2)}, u32[]{:S(2)}) collective-permute-start(bf16[64,1024]{1,0:T(8,128)(2,1)S(1)} %get-tuple-element.44), channel_id=1, source_target_pairs={{0,8},{8,0},{16,24},{24,16},{1,9},{9,1},{17,25},{25,17},{2,10},{10... | collective-permute-start | bytes 393224 | tf_op jit(solution)/shard_map/ppermute | solution.py:226
  4.8 1.5 %collective-permute-start = (bf16[64,1024]{1,0:T(8,128)(2,1)S(1)}, bf16[64,1024]{1,0:T(8,128)(2,1)S(1)}, u32[]{:S(2)}, u32[]{:S(2)}) collective-permute-start(bf16[64,1024]{1,0:T(8,128)(2,1)S(1)} %get-tuple-element.45), channel_id=1, source_target_pairs={{0,16},{8,24},{16,0},{24,8},{1,17},{9,25},{17,1},{25,9},{2,18},{10... | collective-permute-start | bytes 393224 | tf_op jit(solution)/shard_map/ppermute | solution.py:226
  6.4 2.1 %collective-permute-start.6 = (bf16[256,512]{1,0:T(8,128)(2,1)S(1)}, bf16[256,512]{1,0:T(8,128)(2,1)S(1)}, u32[]{:S(2)}, u32[]{:S(2)}) collective-permute-start(bf16[256,512]{1,0:T(8,128)(2,1)S(1)} %get-tuple-element.48), channel_id=1, source_target_pairs={{0,2},{1,3},{2,0},{3,1},{4,6},{5,7},{6,4},{7,5},{8,10},{9,11},{10,... | collective-permute-start | bytes 786440 | tf_op jit(solution)/shard_map/ppermute | solution.py:222
  8.7 3.9 %collective-permute-done.refs_0_ = bf16[64,1024]{1,0:T(8,128)(2,1)S(1)} collective-permute-done((bf16[64,1024]{1,0:T(8,128)(2,1)S(1)}, bf16[64,1024]{1,0:T(8,128)(2,1)S(1)}, u32[]{:S(2)}, u32[]{:S(2)}) %collective-permute-start) | collective-permute-done | bytes 131104 | tf_op jit(solution)/shard_map/ppermute | solution.py:226
  13.1 1.0 %constant_dynamic-slice_fusion.3.own = bf16[128,1024]{1,0:T(8,128)(2,1)S(1)} fusion(bf16[128,4096]{1,0:T(8,128)(2,1)} %param.8, s32[]{:T(128)S(6)} %select_n.31), kind=kLoop, calls=%fused_computation.3 | loop fusion | bytes 524292 | tf_op jit(solution)/shard_map/dynamic_slice | solution.py:246
  14.9 1.6 %collective-permute-start.7 = (bf16[136,512]{1,0:T(8,128)(2,1)S(1)}, bf16[136,512]{1,0:T(8,128)(2,1)S(1)}, u32[]{:S(2)}, u32[]{:S(2)}) collective-permute-start(bf16[136,512]{1,0:T(8,128)(2,1)S(1)} %get-tuple-element.26), channel_id=1, source_target_pairs={{0,8},{8,0},{16,24},{24,16},{1,9},{9,1},{17,25},{25,17},{2,10},{10... | collective-permute-start | bytes 417800 | tf_op jit(solution)/shard_map/ppermute | solution.py:226
  16.5 1.5 %collective-permute-start.8 = (bf16[136,512]{1,0:T(8,128)(2,1)S(1)}, bf16[136,512]{1,0:T(8,128)(2,1)S(1)}, u32[]{:S(2)}, u32[]{:S(2)}) collective-permute-start(bf16[136,512]{1,0:T(8,128)(2,1)S(1)} %get-tuple-element.27), channel_id=1, source_target_pairs={{0,16},{8,24},{16,0},{24,8},{1,17},{9,25},{17,1},{25,9},{2,18},{10... | collective-permute-start | bytes 417800 | tf_op jit(solution)/shard_map/ppermute | solution.py:226
  19.1 2.4 %collective-permute-done.7.first = bf16[136,512]{1,0:T(8,128)(2,1)S(1)} collective-permute-done((bf16[136,512]{1,0:T(8,128)(2,1)S(1)}, bf16[136,512]{1,0:T(8,128)(2,1)S(1)}, u32[]{:S(2)}, u32[]{:S(2)}) %collective-permute-start.7) | collective-permute-done | bytes 139296 | tf_op jit(solution)/shard_map/ppermute | solution.py:226
  21.5 2.1 %collective-permute-done.8.second = bf16[136,512]{1,0:T(8,128)(2,1)S(1)} collective-permute-done((bf16[136,512]{1,0:T(8,128)(2,1)S(1)}, bf16[136,512]{1,0:T(8,128)(2,1)S(1)}, u32[]{:S(2)}, u32[]{:S(2)}) %collective-permute-start.8) | collective-permute-done | bytes 139296 | tf_op jit(solution)/shard_map/ppermute | solution.py:226
  23.6 1.2 %collective-permute-done.9.both = bf16[136,512]{1,0:T(8,128)(2,1)S(1)} collective-permute-done((bf16[136,512]{1,0:T(8,128)(2,1)S(1)}, bf16[136,512]{1,0:T(8,128)(2,1)S(1)}, u32[]{:S(2)}, u32[]{:S(2)}) %collective-permute-start.9) | collective-permute-done | bytes 139296 | tf_op jit(solution)/shard_map/ppermute | solution.py:226
  24.9 0.9 %collective-permute-start.12 = (bf16[128,512]{1,0:T(8,128)(2,1)S(1)}, bf16[128,512]{1,0:T(8,128)(2,1)S(1)}, u32[]{:S(2)}, u32[]{:S(2)}) collective-permute-start(bf16[128,512]{1,0:T(8,128)(2,1)S(1)} %get-tuple-element.29.refs_0_), channel_id=1, source_target_pairs={{0,8},{8,0},{16,24},{24,16},{1,9},{9,1},{17,25},{25,17},{2,10},{10... | collective-permute-start | bytes 393224 | tf_op jit(solution)/shard_map/ppermute | solution.py:226
  25.8 1.5 %collective-permute-start.11 = (bf16[128,512]{1,0:T(8,128)(2,1)S(1)}, bf16[128,512]{1,0:T(8,128)(2,1)S(1)}, u32[]{:S(2)}, u32[]{:S(2)}) collective-permute-start(bf16[128,512]{1,0:T(8,128)(2,1)S(1)} %get-tuple-element.29.refs_0_), channel_id=1, source_target_pairs={{0,16},{8,24},{16,0},{24,8},{1,17},{9,25},{17,1},{25,9},{2,18},{10... | collective-permute-start | bytes 393224 | tf_op jit(solution)/shard_map/ppermute | solution.py:226
  27.3 1.2 %collective-permute-start.10 = (bf16[128,512]{1,0:T(8,128)(2,1)S(1)}, bf16[128,512]{1,0:T(8,128)(2,1)S(1)}, u32[]{:S(2)}, u32[]{:S(2)}) collective-permute-start(bf16[128,512]{1,0:T(8,128)(2,1)S(1)} %get-tuple-element.29.refs_0_), channel_id=1, source_target_pairs={{0,24},{8,16},{16,8},{24,0},{1,25},{9,17},{17,9},{25,1},{2,26},{10... | collective-permute-start | bytes 393224 | tf_op jit(solution)/shard_map/ppermute | solution.py:226
  28.4 2.8 %collective-permute-done.12.refs_3_ = bf16[128,512]{1,0:T(8,128)(2,1)S(1)} collective-permute-done((bf16[128,512]{1,0:T(8,128)(2,1)S(1)}, bf16[128,512]{1,0:T(8,128)(2,1)S(1)}, u32[]{:S(2)}, u32[]{:S(2)}) %collective-permute-start.12) | collective-permute-done | bytes 131104 | tf_op jit(solution)/shard_map/ppermute | solution.py:226
  31.3 0.8 %collective-permute-done.11.refs_2_ = bf16[128,512]{1,0:T(8,128)(2,1)S(1)} collective-permute-done((bf16[128,512]{1,0:T(8,128)(2,1)S(1)}, bf16[128,512]{1,0:T(8,128)(2,1)S(1)}, u32[]{:S(2)}, u32[]{:S(2)}) %collective-permute-start.11) | collective-permute-done | bytes 131104 | tf_op jit(solution)/shard_map/ppermute | solution.py:226
  32.1 1.0 %collective-permute-done.10.refs_1_ = bf16[128,512]{1,0:T(8,128)(2,1)S(1)} collective-permute-done((bf16[128,512]{1,0:T(8,128)(2,1)S(1)}, bf16[128,512]{1,0:T(8,128)(2,1)S(1)}, u32[]{:S(2)}, u32[]{:S(2)}) %collective-permute-start.10) | collective-permute-done | bytes 131104 | tf_op jit(solution)/shard_map/ppermute | solution.py:226
  33.1 1.9 %attend_sent.1.refs_5_ = bf16[264,256]{1,0:T(8,128)(2,1)S(1)} custom-call(s32[8]{0:T(128)S(1)} %copy-done.5, s32[4]{0:T(128)S(1)} %copy-done.6, bf16[128,512]{1,0:T(8,128)(2,1)S(1)} %get-tuple-element.29.refs_0_, bf16[128,512]{1,0:T(8,128)(2,1)S(1)} %collective-permute-done.10.refs_1_, bf16[128,512]{1,0:T(8,128)(2,1)S(1)} %collective-permute-done.11.refs_2_, ...), custom_call_target="tpu_custom_call" | custom-call | tf_op jit(solution)/shard_map/attend_sent/pallas_call | solution.py:231
  35.0 1.6 %collective-permute-start.15 = (bf16[264,256]{1,0:T(8,128)(2,1)S(1)}, bf16[264,256]{1,0:T(8,128)(2,1)S(1)}, u32[]{:S(2)}, u32[]{:S(2)}) collective-permute-start(bf16[264,256]{1,0:T(8,128)(2,1)S(1)} %attend_sent.1.refs_5_), channel_id=1, source_target_pairs={{0,2},{1,3},{2,0},{3,1},{4,6},{5,7},{6,4},{7,5},{8,10},{9,11},{10,... | collective-permute-start | bytes 405512 | tf_op jit(solution)/shard_map/ppermute | solution.py:222
  36.6 1.4 %attend_kept.1.refs_0_ = bf16[264,256]{1,0:T(8,128)(2,1)S(1)} custom-call(s32[8]{0:T(128)S(1)} %copy-done.5, s32[4]{0:T(128)S(1)} %copy-done.6, bf16[128,512]{1,0:T(8,128)(2,1)S(1)} %get-tuple-element.29.refs_0_, bf16[128,512]{1,0:T(8,128)(2,1)S(1)} %collective-permute-done.10.refs_1_, bf16[128,512]{1,0:T(8,128)(2,1)S(1)} %collective-permute-done.11.refs_2_, ...), custom_call_target="tpu_custom_call" | custom-call | tf_op jit(solution)/shard_map/attend_kept/pallas_call | solution.py:231
  38.6 1.5 %collective-permute-done.15.refs_2_ = bf16[264,256]{1,0:T(8,128)(2,1)S(1)} collective-permute-done((bf16[264,256]{1,0:T(8,128)(2,1)S(1)}, bf16[264,256]{1,0:T(8,128)(2,1)S(1)}, u32[]{:S(2)}, u32[]{:S(2)}) %collective-permute-start.15) | collective-permute-done | bytes 135200 | tf_op jit(solution)/shard_map/ppermute | solution.py:222
  40.1 1.3 %collective-permute-done.16.refs_3_ = bf16[264,256]{1,0:T(8,128)(2,1)S(1)} collective-permute-done((bf16[264,256]{1,0:T(8,128)(2,1)S(1)}, bf16[264,256]{1,0:T(8,128)(2,1)S(1)}, u32[]{:S(2)}, u32[]{:S(2)}) %collective-permute-start.16) | collective-permute-done | bytes 135200 | tf_op jit(solution)/shard_map/ppermute | solution.py:219
  41.9 1.2 %collective-permute-start.18 = (bf16[72,512]{1,0:T(8,128)(2,1)S(1)}, bf16[72,512]{1,0:T(8,128)(2,1)S(1)}, u32[]{:S(2)}, u32[]{:S(2)}) collective-permute-start(bf16[72,512]{1,0:T(8,128)(2,1)S(1)} %get-tuple-element.37), channel_id=1, source_target_pairs={{0,8},{8,0},{16,24},{24,16},{1,9},{9,1},{17,25},{25,17},{2,10},{10... | collective-permute-start | bytes 221192 | tf_op jit(solution)/shard_map/ppermute | solution.py:226
  43.1 1.5 %collective-permute-start.19 = (bf16[72,512]{1,0:T(8,128)(2,1)S(1)}, bf16[72,512]{1,0:T(8,128)(2,1)S(1)}, u32[]{:S(2)}, u32[]{:S(2)}) collective-permute-start(bf16[72,512]{1,0:T(8,128)(2,1)S(1)} %get-tuple-element.38), channel_id=1, source_target_pairs={{0,16},{8,24},{16,0},{24,8},{1,17},{9,25},{17,1},{25,9},{2,18},{10... | collective-permute-start | bytes 221192 | tf_op jit(solution)/shard_map/ppermute | solution.py:226
  44.6 0.9 %collective-permute-start.20 = (bf16[72,512]{1,0:T(8,128)(2,1)S(1)}, bf16[72,512]{1,0:T(8,128)(2,1)S(1)}, u32[]{:S(2)}, u32[]{:S(2)}) collective-permute-start(bf16[72,512]{1,0:T(8,128)(2,1)S(1)} %get-tuple-element.39), channel_id=1, source_target_pairs={{0,24},{8,16},{16,8},{24,0},{1,25},{9,17},{17,9},{25,1},{2,26},{10... | collective-permute-start | bytes 221192 | tf_op jit(solution)/shard_map/ppermute | solution.py:226
  45.4 0.9 %collective-permute-done.18.refs_1_ = bf16[72,512]{1,0:T(8,128)(2,1)S(1)} collective-permute-done((bf16[72,512]{1,0:T(8,128)(2,1)S(1)}, bf16[72,512]{1,0:T(8,128)(2,1)S(1)}, u32[]{:S(2)}, u32[]{:S(2)}) %collective-permute-start.18) | collective-permute-done | bytes 73760 | tf_op jit(solution)/shard_map/ppermute | solution.py:226
  46.3 1.2 %collective-permute-done.19.refs_2_ = bf16[72,512]{1,0:T(8,128)(2,1)S(1)} collective-permute-done((bf16[72,512]{1,0:T(8,128)(2,1)S(1)}, bf16[72,512]{1,0:T(8,128)(2,1)S(1)}, u32[]{:S(2)}, u32[]{:S(2)}) %collective-permute-start.19) | collective-permute-done | bytes 73760 | tf_op jit(solution)/shard_map/ppermute | solution.py:226
  47.5 2.3 %collective-permute-done.20.refs_3_ = bf16[72,512]{1,0:T(8,128)(2,1)S(1)} collective-permute-done((bf16[72,512]{1,0:T(8,128)(2,1)S(1)}, bf16[72,512]{1,0:T(8,128)(2,1)S(1)}, u32[]{:S(2)}, u32[]{:S(2)}) %collective-permute-start.20) | collective-permute-done | bytes 73760 | tf_op jit(solution)/shard_map/ppermute | solution.py:226
  49.9 2.6 %collective-permute-start.22 = (bf16[72,512]{1,0:T(8,128)(2,1)S(1)}, bf16[72,512]{1,0:T(8,128)(2,1)S(1)}, u32[]{:S(2)}, u32[]{:S(2)}) collective-permute-start(bf16[72,512]{1,0:T(8,128)(2,1)S(1)} %get-tuple-element.42), channel_id=1, source_target_pairs={{0,4},{1,5},{2,6},{3,7},{4,0},{5,1},{6,2},{7,3},{8,12},{9,13},{10,... | collective-permute-start | bytes 221192 | tf_op jit(solution)/shard_map/ppermute | solution.py:222
  52.5 1.6 %collective-permute-start.21 = (bf16[64,512]{1,0:T(8,128)(2,1)S(1)}, bf16[64,512]{1,0:T(8,128)(2,1)S(1)}, u32[]{:S(2)}, u32[]{:S(2)}) collective-permute-start(bf16[64,512]{1,0:T(8,128)(2,1)S(1)} %get-tuple-element.41), channel_id=1, source_target_pairs={{0,2},{1,3},{2,0},{3,1},{4,6},{5,7},{6,4},{7,5},{8,10},{9,11},{10,... | collective-permute-start | bytes 196616 | tf_op jit(solution)/shard_map/ppermute | solution.py:222
  54.3 3.4 %collective-permute-done.21.refs_1_ = bf16[64,512]{1,0:T(8,128)(2,1)S(1)} collective-permute-done((bf16[64,512]{1,0:T(8,128)(2,1)S(1)}, bf16[64,512]{1,0:T(8,128)(2,1)S(1)}, u32[]{:S(2)}, u32[]{:S(2)}) %collective-permute-start.21) | collective-permute-done | bytes 65568 | tf_op jit(solution)/shard_map/ppermute | solution.py:222
  57.7 2.5 %collective-permute-done.23.refs_3_ = bf16[64,512]{1,0:T(8,128)(2,1)S(1)} collective-permute-done((bf16[64,512]{1,0:T(8,128)(2,1)S(1)}, bf16[64,512]{1,0:T(8,128)(2,1)S(1)}, u32[]{:S(2)}, u32[]{:S(2)}) %collective-permute-start.23) | collective-permute-done | bytes 65568 | tf_op jit(solution)/shard_map/ppermute | solution.py:222
  (41 shorter events, 4.8 us)
Async XLA Ops:
  0.6 12.5 %copy-start = (bf16[4,4096]{1,0:T(4,128)(2,1)S(1)}, bf16[4,4096]{1,0:T(4,128)(2,1)}, u32[]{:S(2)}) copy-start(bf16[4,4096]{1,0:T(4,128)(2,1)} %param.9) | copy-start | bytes 98308
  0.6 5.7 %copy-start.1 = (bf16[256,1024]{1,0:T(8,128)(2,1)S(1)}, bf16[256,1024]{1,0:T(8,128)(2,1)}, u32[]{:S(2)}) copy-start(bf16[256,1024]{1,0:T(8,128)(2,1)} %refs_4_.1) | copy-start | bytes 1572868
  1.8 6.9 %collective-permute-start.2 = (bf16[64,1024]{1,0:T(8,128)(2,1)S(1)}, bf16[64,1024]{1,0:T(8,128)(2,1)S(1)}, u32[]{:S(2)}, u32[]{:S(2)}) collective-permute-start(bf16[64,1024]{1,0:T(8,128)(2,1)S(1)} %get-tuple-element.44), channel_id=1, source_target_pairs={{0,8},{8,0},{16,24},{24,16},{1,9},{9,1},{17,25},{25,17},{2,10},{10... | collective-permute-start | bytes 393224 | tf_op jit(solution)/shard_map/ppermute | solution.py:226
  4.8 7.8 %collective-permute-start = (bf16[64,1024]{1,0:T(8,128)(2,1)S(1)}, bf16[64,1024]{1,0:T(8,128)(2,1)S(1)}, u32[]{:S(2)}, u32[]{:S(2)}) collective-permute-start(bf16[64,1024]{1,0:T(8,128)(2,1)S(1)} %get-tuple-element.45), channel_id=1, source_target_pairs={{0,16},{8,24},{16,0},{24,8},{1,17},{9,25},{17,1},{25,9},{2,18},{10... | collective-permute-start | bytes 393224 | tf_op jit(solution)/shard_map/ppermute | solution.py:226
  6.3 6.3 %collective-permute-start.1 = (bf16[64,1024]{1,0:T(8,128)(2,1)S(1)}, bf16[64,1024]{1,0:T(8,128)(2,1)S(1)}, u32[]{:S(2)}, u32[]{:S(2)}) collective-permute-start(bf16[64,1024]{1,0:T(8,128)(2,1)S(1)} %get-tuple-element.46), channel_id=1, source_target_pairs={{0,24},{8,16},{16,8},{24,0},{1,25},{9,17},{17,9},{25,1},{2,26},{10... | collective-permute-start | bytes 393224 | tf_op jit(solution)/shard_map/ppermute | solution.py:226
  6.4 7.8 %copy-start.3 = (bf16[1024,128]{1,0:T(8,128)(2,1)S(1)}, bf16[1024,128]{1,0:T(8,128)(2,1)}, u32[]{:S(2)}) copy-start(bf16[1024,128]{1,0:T(8,128)(2,1)} %refs_8_.1) | copy-start | bytes 786436
  6.4 7.8 %copy-start.4 = (bf16[1024,128]{1,0:T(8,128)(2,1)S(1)}, bf16[1024,128]{1,0:T(8,128)(2,1)}, u32[]{:S(2)}) copy-start(bf16[1024,128]{1,0:T(8,128)(2,1)} %refs_9_.1) | copy-start | bytes 786436
  6.4 7.8 %copy-start.2 = (bf16[1024,256]{1,0:T(8,128)(2,1)S(1)}, bf16[1024,256]{1,0:T(8,128)(2,1)}, u32[]{:S(2)}) copy-start(bf16[1024,256]{1,0:T(8,128)(2,1)} %refs_7_.1) | copy-start | bytes 1572868
  6.4 7.7 %collective-permute-start.6 = (bf16[256,512]{1,0:T(8,128)(2,1)S(1)}, bf16[256,512]{1,0:T(8,128)(2,1)S(1)}, u32[]{:S(2)}, u32[]{:S(2)}) collective-permute-start(bf16[256,512]{1,0:T(8,128)(2,1)S(1)} %get-tuple-element.48), channel_id=1, source_target_pairs={{0,2},{1,3},{2,0},{3,1},{4,6},{5,7},{6,4},{7,5},{8,10},{9,11},{10,... | collective-permute-start | bytes 786440 | tf_op jit(solution)/shard_map/ppermute | solution.py:222
  8.7 5.4 %collective-permute-start.5 = (bf16[64,1024]{1,0:T(8,128)(2,1)S(1)}, bf16[64,1024]{1,0:T(8,128)(2,1)S(1)}, u32[]{:S(2)}, u32[]{:S(2)}) collective-permute-start(bf16[64,1024]{1,0:T(8,128)(2,1)S(1)} %collective-permute-done.2.refs_2_), channel_id=1, source_target_pairs={{0,1},{1,0},{2,3},{3,2},{4,5},{5,4},{6,7},{7,6},{8,9},{9,8},{10,11... | collective-permute-start | bytes 393224 | tf_op jit(solution)/shard_map/ppermute | solution.py:219
  12.6 1.5 %collective-permute-start.3 = (bf16[64,1024]{1,0:T(8,128)(2,1)S(1)}, bf16[64,1024]{1,0:T(8,128)(2,1)S(1)}, u32[]{:S(2)}, u32[]{:S(2)}) collective-permute-start(bf16[64,1024]{1,0:T(8,128)(2,1)S(1)} %collective-permute-done.refs_0_), channel_id=1, source_target_pairs={{0,1},{1,0},{2,3},{3,2},{4,5},{5,4},{6,7},{7,6},{8,9},{9,8},{10,11... | collective-permute-start | bytes 393224 | tf_op jit(solution)/shard_map/ppermute | solution.py:219
  12.6 1.5 %collective-permute-start.4 = (bf16[64,1024]{1,0:T(8,128)(2,1)S(1)}, bf16[64,1024]{1,0:T(8,128)(2,1)S(1)}, u32[]{:S(2)}, u32[]{:S(2)}) collective-permute-start(bf16[64,1024]{1,0:T(8,128)(2,1)S(1)} %collective-permute-done.1.refs_1_), channel_id=1, source_target_pairs={{0,1},{1,0},{2,3},{3,2},{4,5},{5,4},{6,7},{7,6},{8,9},{9,8},{10,11... | collective-permute-start | bytes 393224 | tf_op jit(solution)/shard_map/ppermute | solution.py:219
  14.9 6.6 %collective-permute-start.7 = (bf16[136,512]{1,0:T(8,128)(2,1)S(1)}, bf16[136,512]{1,0:T(8,128)(2,1)S(1)}, u32[]{:S(2)}, u32[]{:S(2)}) collective-permute-start(bf16[136,512]{1,0:T(8,128)(2,1)S(1)} %get-tuple-element.26), channel_id=1, source_target_pairs={{0,8},{8,0},{16,24},{24,16},{1,9},{9,1},{17,25},{25,17},{2,10},{10... | collective-permute-start | bytes 417800 | tf_op jit(solution)/shard_map/ppermute | solution.py:226
  16.5 7.1 %collective-permute-start.8 = (bf16[136,512]{1,0:T(8,128)(2,1)S(1)}, bf16[136,512]{1,0:T(8,128)(2,1)S(1)}, u32[]{:S(2)}, u32[]{:S(2)}) collective-permute-start(bf16[136,512]{1,0:T(8,128)(2,1)S(1)} %get-tuple-element.27), channel_id=1, source_target_pairs={{0,16},{8,24},{16,0},{24,8},{1,17},{9,25},{17,1},{25,9},{2,18},{10... | collective-permute-start | bytes 417800 | tf_op jit(solution)/shard_map/ppermute | solution.py:226
  18.0 6.8 %collective-permute-start.9 = (bf16[136,512]{1,0:T(8,128)(2,1)S(1)}, bf16[136,512]{1,0:T(8,128)(2,1)S(1)}, u32[]{:S(2)}, u32[]{:S(2)}) collective-permute-start(bf16[136,512]{1,0:T(8,128)(2,1)S(1)} %get-tuple-element.28), channel_id=1, source_target_pairs={{0,24},{8,16},{16,8},{24,0},{1,25},{9,17},{17,9},{25,1},{2,26},{10... | collective-permute-start | bytes 417800 | tf_op jit(solution)/shard_map/ppermute | solution.py:226
  18.5 10.0 %collective-permute-start.13 = (bf16[256,512]{1,0:T(8,128)(2,1)S(1)}, bf16[256,512]{1,0:T(8,128)(2,1)S(1)}, u32[]{:S(2)}, u32[]{:S(2)}) collective-permute-start(bf16[256,512]{1,0:T(8,128)(2,1)S(1)} %get-tuple-element.33), channel_id=1, source_target_pairs={{0,3},{1,2},{2,1},{3,0},{4,7},{5,6},{6,5},{7,4},{8,11},{9,10},{10,... | collective-permute-start | bytes 786440 | tf_op jit(solution)/shard_map/ppermute | solution.py:266
  24.9 8.3 %copy-start.5 = (s32[8]{0:T(128)S(1)}, s32[8]{0:T(128)}, u32[]{:S(2)}) copy-start(s32[8]{0:T(128)} %block_map.3) | copy-start | bytes 100
  24.9 8.3 %copy-start.6 = (s32[4]{0:T(128)S(1)}, s32[4]{0:T(128)}, u32[]{:S(2)}) copy-start(s32[4]{0:T(128)} %lengths.3) | copy-start | bytes 52
  24.9 6.4 %collective-permute-start.12 = (bf16[128,512]{1,0:T(8,128)(2,1)S(1)}, bf16[128,512]{1,0:T(8,128)(2,1)S(1)}, u32[]{:S(2)}, u32[]{:S(2)}) collective-permute-start(bf16[128,512]{1,0:T(8,128)(2,1)S(1)} %get-tuple-element.29.refs_0_), channel_id=1, source_target_pairs={{0,8},{8,0},{16,24},{24,16},{1,9},{9,1},{17,25},{25,17},{2,10},{10... | collective-permute-start | bytes 393224 | tf_op jit(solution)/shard_map/ppermute | solution.py:226
  25.8 6.4 %collective-permute-start.11 = (bf16[128,512]{1,0:T(8,128)(2,1)S(1)}, bf16[128,512]{1,0:T(8,128)(2,1)S(1)}, u32[]{:S(2)}, u32[]{:S(2)}) collective-permute-start(bf16[128,512]{1,0:T(8,128)(2,1)S(1)} %get-tuple-element.29.refs_0_), channel_id=1, source_target_pairs={{0,16},{8,24},{16,0},{24,8},{1,17},{9,25},{17,1},{25,9},{2,18},{10... | collective-permute-start | bytes 393224 | tf_op jit(solution)/shard_map/ppermute | solution.py:226
  27.3 5.9 %collective-permute-start.10 = (bf16[128,512]{1,0:T(8,128)(2,1)S(1)}, bf16[128,512]{1,0:T(8,128)(2,1)S(1)}, u32[]{:S(2)}, u32[]{:S(2)}) collective-permute-start(bf16[128,512]{1,0:T(8,128)(2,1)S(1)} %get-tuple-element.29.refs_0_), channel_id=1, source_target_pairs={{0,24},{8,16},{16,8},{24,0},{1,25},{9,17},{17,9},{25,1},{2,26},{10... | collective-permute-start | bytes 393224 | tf_op jit(solution)/shard_map/ppermute | solution.py:226
  35.0 5.1 %collective-permute-start.15 = (bf16[264,256]{1,0:T(8,128)(2,1)S(1)}, bf16[264,256]{1,0:T(8,128)(2,1)S(1)}, u32[]{:S(2)}, u32[]{:S(2)}) collective-permute-start(bf16[264,256]{1,0:T(8,128)(2,1)S(1)} %attend_sent.1.refs_5_), channel_id=1, source_target_pairs={{0,2},{1,3},{2,0},{3,1},{4,6},{5,7},{6,4},{7,5},{8,10},{9,11},{10,... | collective-permute-start | bytes 405512 | tf_op jit(solution)/shard_map/ppermute | solution.py:222
  36.6 3.4 %collective-permute-start.17 = (bf16[256,512]{1,0:T(8,128)(2,1)S(1)}, bf16[256,512]{1,0:T(8,128)(2,1)S(1)}, u32[]{:S(2)}, u32[]{:S(2)}) collective-permute-start(bf16[256,512]{1,0:T(8,128)(2,1)S(1)} %get-tuple-element.33), channel_id=1, source_target_pairs={{0,1},{1,0},{2,3},{3,2},{4,5},{5,4},{6,7},{7,6},{8,9},{9,8},{10,11... | collective-permute-start | bytes 786440 | tf_op jit(solution)/shard_map/ppermute | solution.py:219
  38.0 2.0 %collective-permute-start.14 = (bf16[264,256]{1,0:T(8,128)(2,1)S(1)}, bf16[264,256]{1,0:T(8,128)(2,1)S(1)}, u32[]{:S(2)}, u32[]{:S(2)}) collective-permute-start(bf16[264,256]{1,0:T(8,128)(2,1)S(1)} %attend_kept.1.refs_0_), channel_id=1, source_target_pairs={{0,1},{1,0},{2,3},{3,2},{4,5},{5,4},{6,7},{7,6},{8,9},{9,8},{10,11... | collective-permute-start | bytes 405512 | tf_op jit(solution)/shard_map/ppermute | solution.py:219
  40.1 1.4 %collective-permute-start.16 = (bf16[264,256]{1,0:T(8,128)(2,1)S(1)}, bf16[264,256]{1,0:T(8,128)(2,1)S(1)}, u32[]{:S(2)}, u32[]{:S(2)}) collective-permute-start(bf16[264,256]{1,0:T(8,128)(2,1)S(1)} %collective-permute-done.15.refs_2_), channel_id=1, source_target_pairs={{0,1},{1,0},{2,3},{3,2},{4,5},{5,4},{6,7},{7,6},{8,9},{9,8},{10,11... | collective-permute-start | bytes 405512 | tf_op jit(solution)/shard_map/ppermute | solution.py:219
  41.9 4.4 %collective-permute-start.18 = (bf16[72,512]{1,0:T(8,128)(2,1)S(1)}, bf16[72,512]{1,0:T(8,128)(2,1)S(1)}, u32[]{:S(2)}, u32[]{:S(2)}) collective-permute-start(bf16[72,512]{1,0:T(8,128)(2,1)S(1)} %get-tuple-element.37), channel_id=1, source_target_pairs={{0,8},{8,0},{16,24},{24,16},{1,9},{9,1},{17,25},{25,17},{2,10},{10... | collective-permute-start | bytes 221192 | tf_op jit(solution)/shard_map/ppermute | solution.py:226
  43.1 4.4 %collective-permute-start.19 = (bf16[72,512]{1,0:T(8,128)(2,1)S(1)}, bf16[72,512]{1,0:T(8,128)(2,1)S(1)}, u32[]{:S(2)}, u32[]{:S(2)}) collective-permute-start(bf16[72,512]{1,0:T(8,128)(2,1)S(1)} %get-tuple-element.38), channel_id=1, source_target_pairs={{0,16},{8,24},{16,0},{24,8},{1,17},{9,25},{17,1},{25,9},{2,18},{10... | collective-permute-start | bytes 221192 | tf_op jit(solution)/shard_map/ppermute | solution.py:226
  44.6 5.3 %collective-permute-start.20 = (bf16[72,512]{1,0:T(8,128)(2,1)S(1)}, bf16[72,512]{1,0:T(8,128)(2,1)S(1)}, u32[]{:S(2)}, u32[]{:S(2)}) collective-permute-start(bf16[72,512]{1,0:T(8,128)(2,1)S(1)} %get-tuple-element.39), channel_id=1, source_target_pairs={{0,24},{8,16},{16,8},{24,0},{1,25},{9,17},{17,9},{25,1},{2,26},{10... | collective-permute-start | bytes 221192 | tf_op jit(solution)/shard_map/ppermute | solution.py:226
  49.9 10.3 %collective-permute-start.22 = (bf16[72,512]{1,0:T(8,128)(2,1)S(1)}, bf16[72,512]{1,0:T(8,128)(2,1)S(1)}, u32[]{:S(2)}, u32[]{:S(2)}) collective-permute-start(bf16[72,512]{1,0:T(8,128)(2,1)S(1)} %get-tuple-element.42), channel_id=1, source_target_pairs={{0,4},{1,5},{2,6},{3,7},{4,0},{5,1},{6,2},{7,3},{8,12},{9,13},{10,... | collective-permute-start | bytes 221192 | tf_op jit(solution)/shard_map/ppermute | solution.py:222
  52.5 5.2 %collective-permute-start.21 = (bf16[64,512]{1,0:T(8,128)(2,1)S(1)}, bf16[64,512]{1,0:T(8,128)(2,1)S(1)}, u32[]{:S(2)}, u32[]{:S(2)}) collective-permute-start(bf16[64,512]{1,0:T(8,128)(2,1)S(1)} %get-tuple-element.41), channel_id=1, source_target_pairs={{0,2},{1,3},{2,0},{3,1},{4,6},{5,7},{6,4},{7,5},{8,10},{9,11},{10,... | collective-permute-start | bytes 196616 | tf_op jit(solution)/shard_map/ppermute | solution.py:222
  54.1 6.1 %collective-permute-start.23 = (bf16[64,512]{1,0:T(8,128)(2,1)S(1)}, bf16[64,512]{1,0:T(8,128)(2,1)S(1)}, u32[]{:S(2)}, u32[]{:S(2)}) collective-permute-start(bf16[64,512]{1,0:T(8,128)(2,1)S(1)} %get-tuple-element.43), channel_id=1, source_target_pairs={{0,6},{1,7},{2,4},{3,5},{4,2},{5,3},{6,0},{7,1},{8,14},{9,15},{10,... | collective-permute-start | bytes 196616 | tf_op jit(solution)/shard_map/ppermute | solution.py:222

commit v13 on v12

--- a/solution.py
+++ b/solution.py
@@ -13,6 +13,7 @@
 LAST = 1 << 30
 ROW_TILE = 8
 VMEM_BYTES = 48 * 1024 * 1024
+TOKENS, SUMS, KEYS, OUTPUTS, HEADS = (1, 2, 0), (0, 1, 2), (2, 1, 0), (0, 1, 2), (2, 1, 0)
 
 
 def vmem():
@@ -21,6 +22,14 @@
 
 def smem():
     return pl.BlockSpec(memory_space=pltpu.SMEM)
+
+
+def in_order(order, values):
+    return [values[i] for i in order]
+
+
+def put_back(order, values):
+    return [values[order.index(i)] for i in range(len(order))]
 
 
 def place():
@@ -29,7 +38,7 @@
 
 
 def project_kernel(rows, own, *refs):
-    (mine, theirs), refs = ((refs[2], *refs[:2]), (refs[5], *refs[3:5])), refs[6:]
+    mine, theirs, refs = put_back(TOKENS, refs[:3]), put_back(TOKENS, refs[3:6]), refs[6:]
     (new, *weights), refs = refs[:4], refs[4:]
     held, new_held, *outs, inputs = refs
     count = new.shape[0]
@@ -57,7 +66,8 @@
         column += weight.shape[1]
 
 
-def add_kernel(own, new_own, first, second, both, held, new):
+def add_kernel(own, new_own, *refs):
+    (first, second, both), (held, new) = put_back(SUMS, refs[:3]), refs[3:]
     rows = held.shape[0]
 
     def total(own, at):
@@ -76,38 +86,15 @@
     return found
 
 
-def attend_kernel(sent, block_rows, count, scale, block_map, lengths, *refs):
-    blocks, new, refs = (refs[0], *refs[3:0:-1]), refs[4], refs[5:]
-    attended = refs[-1]
-    rows, features = blocks[0].shape
-    head = HEAD_SIZE
-    q_width = features - 2 * head
-    pad = new.shape[0]
-    per_device = rows // block_rows
-    tail = len(blocks) * block_rows
-    c, z, _ = place()
-    half = 1 - z % 2 if sent else z % 2
-
-    def whole(number):
-        at = slice(number * head, (number + 1) * head)
-        return jnp.concatenate([block[:, at] for block in blocks], axis=0)
-
-    def with_zeros(number):
-        at = slice(number * head, (number + 1) * head)
-        return jnp.concatenate([new[:, at], jnp.zeros((head - pad, head), new.dtype)], axis=0)
-
-    def queries(number):
-        at = slice(number * head, (number + 1) * head)
-        taken = pl.ds(pl.multiple_of(half * block_rows, block_rows), block_rows)
-        return jnp.concatenate([block[taken, at] for block in blocks], axis=0)
-
-    key_at, value_at = q_width // head, q_width // head + 1
-    keys, values = whole(key_at), whole(value_at)
-
+def mask_kernel(block_rows, block_map, lengths, rows_mask, new_mask):
     ends, total = [], 0
-    for request in range(count):
+    for request in range(lengths.shape[0]):
         total = total + lengths[request]
         ends.append(total)
+    c, _, _ = place()
+    count = block_map.shape[0]
+    per_device = 2
+    devices = [per_device * (c ^ mask) for mask in range(count // per_device)]
 
     def labels(shape, axis, held):
         index = lax.broadcasted_iota(jnp.int32, shape, axis)
@@ -118,49 +105,71 @@
             position = jnp.where(inside, block_map[block] * block_rows + index - start, position)
         return position, request_of(position, ends)
 
-    devices = [per_device * (c ^ mask) for mask in range(len(blocks))]
-    q_position, q_request = labels((tail, 1), 0, [first + half for first in devices])
+    keys = new_mask.shape[1]
+    halves = [first + number for number in range(per_device) for first in devices]
+    q_position, q_request = labels((keys, 1), 0, halves)
     held = [first + number for first in devices for number in range(per_device)]
-    k_position, k_request = labels((1, len(blocks) * rows), 1, held)
+    k_position, k_request = labels((1, keys), 1, held)
     allowed = (q_request == k_request) & (k_position <= q_position)
-
-    def scores_of(query, keys, allowed):
+    rows_mask[...] = jnp.where(allowed, 0.0, FLOOR)
+    request = lax.broadcasted_iota(jnp.int32, (new_mask.shape[0], 1), 0)
+    new_mask[...] = jnp.where(request == k_request, 0.0, FLOOR)
+
+
+def attend_kernel(sent, block_rows, scale, *refs):
+    blocks, (new, rows_mask, new_mask), refs = [refs[0], *put_back(KEYS, refs[1:4])], refs[4:7], refs[7:]
+    attended = refs[-1]
+    features = blocks[0].shape[1]
+    head = HEAD_SIZE
+    q_width = features - 2 * head
+    pad = new.shape[0]
+    tail = len(blocks) * block_rows
+    _, z, _ = place()
+    half = 1 - z % 2 if sent else z % 2
+    mask = rows_mask[pl.ds(pl.multiple_of(half * tail, tail), tail), :]
+    if sent:
+        new_rows = new_mask.shape[0]
+        mask = jnp.concatenate([mask, new_mask[...]], axis=0)
+        zeros = jnp.zeros((new_rows - pad, features), new.dtype)
+        news = jnp.concatenate([new[...], zeros], axis=0)
+
+    def columns(number):
+        return slice(number * head, (number + 1) * head)
+
+    def whole(number):
+        return jnp.concatenate([block[:, columns(number)] for block in blocks], axis=0)
+
+    def queries(number):
+        taken = pl.ds(pl.multiple_of(half * block_rows, block_rows), block_rows)
+        parts = [block[taken, columns(number)] for block in blocks]
+        return jnp.concatenate(parts + ([news[:, columns(number)]] if sent else []), axis=0)
+
+    key_at, value_at = q_width // head, q_width // head + 1
+    keys, values = whole(key_at), whole(value_at)
+    for number in range(q_width // head):
+        at = columns(number)
         scores = lax.dot_general(
-            query, keys, (((1,), (1,)), ((), ())), preferred_element_type=jnp.float32
-        )
-        return jnp.where(allowed, scores * scale, FLOOR)
-
-    def mix(weights, values):
-        return jnp.dot(weights.astype(jnp.bfloat16), values, preferred_element_type=jnp.float32)
-
-    for number in range(q_width // head):
-        at = slice(number * head, (number + 1) * head)
-        scores = scores_of(queries(number), keys, allowed)
-        weights = jnp.exp(scores - jnp.max(scores, axis=1, keepdims=True))
+            queries(number), keys, (((1,), (1,)), ((), ())), preferred_element_type=jnp.float32
+        )
+        scores = scores * scale + mask
+        peak = jnp.max(scores, axis=1, keepdims=True)
+        if sent:
+            own = news[:, at].astype(jnp.float32) * news[:, columns(key_at)].astype(jnp.float32)
+            own = jnp.sum(own, axis=1, keepdims=True) * scale
+            new_peak = jnp.maximum(peak[tail:], own)
+            peak = jnp.concatenate([peak[:tail], new_peak], axis=0)
+        weights = jnp.exp(scores - peak)
         denom = jnp.sum(weights, axis=1, keepdims=True)
-        attended[:tail, at] = (mix(weights, values) / denom).astype(jnp.bfloat16)
+        mixed = jnp.dot(weights.astype(jnp.bfloat16), values, preferred_element_type=jnp.float32)
+        attended[:tail, at] = (mixed[:tail] / denom[:tail]).astype(jnp.bfloat16)
+        if sent:
+            weight = jnp.exp(own - new_peak)
+            rounded = weight.astype(jnp.bfloat16).astype(jnp.float32)
+            new_mixed = mixed[tail:] + rounded * news[:, columns(value_at)].astype(jnp.float32)
+            new_mixed = new_mixed / (denom[tail:] + weight)
+            attended[tail:, at] = new_mixed[:pad].astype(jnp.bfloat16)
     if not sent:
         attended[tail:, :] = refs[0][tail:, :]
-        return
-
-    new_rows = 2 * ROW_TILE
-    new_request = lax.broadcasted_iota(jnp.int32, (new_rows, 1), 0)
-    new_allowed = new_request == k_request
-    own_allowed = new_request == lax.broadcasted_iota(jnp.int32, (1, head), 1)
-    new_keys, new_values = with_zeros(key_at), with_zeros(value_at)
-    for number in range(q_width // head):
-        at = slice(number * head, (number + 1) * head)
-        query = with_zeros(number)[:new_rows]
-        scores = scores_of(query, keys, new_allowed)
-        own_scores = scores_of(query, new_keys, own_allowed)
-        peak = jnp.maximum(
-            jnp.max(scores, axis=1, keepdims=True), jnp.max(own_scores, axis=1, keepdims=True)
-        )
-        weights, own_weights = jnp.exp(scores - peak), jnp.exp(own_scores - peak)
-        denom = jnp.sum(weights, axis=1, keepdims=True)
-        denom += jnp.sum(own_weights, axis=1, keepdims=True)
-        mixed = (mix(weights, values) + mix(own_weights, new_values)) / denom
-        attended[tail:, at] = mixed[:pad].astype(jnp.bfloat16)
 
 
 def output_kernel(rows, *refs):
@@ -178,7 +187,7 @@
 
 
 def relay_kernel(*refs):
-    blocks, outs = refs[:4], refs[4:]
+    blocks, outs = [refs[0], *put_back(OUTPUTS, refs[1:4])], refs[4:]
     c, z, _ = place()
     for slot, out in enumerate(outs):
         for mask, block in enumerate(blocks):
@@ -189,7 +198,7 @@
 
 
 def finish_kernel(*refs):
-    parts, (prefill, decode) = refs[:4], refs[4:]
+    parts, (prefill, decode) = [refs[0], *put_back(HEADS, refs[1:4])], refs[4:]
     _, z, _ = place()
     rows = prefill.shape[0] // 2
     for odd in range(2):
@@ -257,7 +266,15 @@
     own_part, new_part, *parts = call(
         functools.partial(project_kernel, rows),
         "project",
-        (own, *mine[1:], mine[0], *theirs[1:], theirs[0], new_columns, w_query, key_matrix, value_matrix),
+        (
+            own,
+            *in_order(TOKENS, mine),
+            *in_order(TOKENS, theirs),
+            new_columns,
+            w_query,
+            key_matrix,
+            value_matrix,
+        ),
         [((rows, features), f32), ((pad, features), bf16)] + [(part, bf16)] * (steps - 1),
         [pltpu.VMEM((-(-all_rows // 16) * 16, depth), bf16)],
     )
@@ -268,23 +285,29 @@
     held, new = call(
         add_kernel,
         "add_parts",
-        (own_part, new_part, *to_partners(parts)),
+        (own_part, new_part, *in_order(SUMS, to_partners(parts))),
         [((rows, features), bf16), ((pad, features), bf16)],
     )
 
-    first, second, both = to_partners([held] * (steps - 1))
+    gathered = [held, *in_order(KEYS, to_partners([held] * (steps - 1)))]
     new, w_next_other = lax.optimization_barrier((new, w_next_other))
     block_rows = steps * rows // block_map.shape[0]
 
+    keys = steps * rows
+    masks = call(
+        functools.partial(mask_kernel, block_rows),
+        "mask",
+        (block_map, lengths),
+        [((keys, keys), f32), ((2 * ROW_TILE, keys), f32)],
+        spaces=[smem()] * 2,
+    )
+
     def attend(sent, *extra):
         (attended,) = call(
-            functools.partial(
-                attend_kernel, sent, block_rows, count, 1.0 / math.sqrt(HEAD_SIZE)
-            ),
+            functools.partial(attend_kernel, sent, block_rows, 1.0 / math.sqrt(HEAD_SIZE)),
             "attend_sent" if sent else "attend_kept",
-            (block_map, lengths, held, both, second, first, new, *extra),
-            [((steps * block_rows + pad, q_width), bf16)],
-            spaces=[smem()] * 2 + [vmem()] * (steps + 1 + len(extra)),
+            (*gathered, new, *masks, *extra),
+            [((keys // 2 + pad, q_width), bf16)],
         )
         return attended
 
@@ -305,10 +328,11 @@
     slots = call(
         relay_kernel,
         "relay",
-        [outs[0]] + to_partners(outs[1:]),
-        [(block if i % 2 == 0 else (block_rows, width), bf16) for i in range(steps)],
-    )
-    slots = [slots[0]] + [to_chip(slot, step) for step, slot in enumerate(slots[1:], 1)]
+        [outs[0], *in_order(OUTPUTS, to_partners(outs[1:]))],
+        [(block, bf16)] * steps,
+    )
+    arrived = [to_chip(slot, step) for step, slot in enumerate(slots[1:], 1)]
+    slots = [slots[0], *in_order(HEADS, arrived)]
     return tuple(
         call(finish_kernel, "finish", slots, [((rows, width), bf16), ((count, width), bf16)])
     )

time: 61 us -> 58.9 us (0.966)
  waiting for transfers between devices: 27.5 us -> 26 us
  Pallas kernels: 5.28 us -> 4.54 us
    ppermute x12, waiting for transfers between devices: 18.8 us -> 18 us  [to_partners(): lax.ppermute(value, 'ctx', [(i, i ^ mask) for i in range(steps)])]
    pallas_call x7 -> x8, Pallas kernels: 5.28 us -> 4.54 us  [call(): pl.pallas_call(kernel, out_shape=[jax.ShapeDtypeStruct(shape, kind) for s...]
  transfers between devices with their start and end apart: 24 -> 24, of which waited for: 15 -> 15; matrix products, arithmetic and copies ran while one was open for 2% -> 2% of each run, Pallas kernels for 2% -> 3%
where the time goes in v13:
time: 58.9 us; the launch traced here: 58.7 us
  waiting for transfers between devices  26 us (44%)
  starting transfers between devices  25.1 us (43%)
  Pallas kernels  4.54 us (8%)
  local copies, waits for them, and re-layouts  2.17 us (4%)
  between operations  0.86 us (1%)
    ppermute x12, waiting for transfers between devices, to_partners(): lax.ppermute(value, 'ctx', [(i, i ^ mask) for i in range(steps)])  18 us
    ppermute x12, starting transfers between devices, to_partners(): lax.ppermute(value, 'ctx', [(i, i ^ mask) for i in range(steps)])  15.2 us
    ppermute x5, starting transfers between devices, to_chip(): return lax.ppermute(value, 'tp', [(i, i ^ 2 * step) for i in range(tp)])  8.19 us
    ppermute x5, waiting for transfers between devices, to_chip(): return lax.ppermute(value, 'tp', [(i, i ^ 2 * step) for i in range(tp)])  6.7 us
    pallas_call x8, Pallas kernels, call(): pl.pallas_call(kernel, out_shape=[jax.ShapeDtypeStruct(shape, kind) for s...  4.54 us
    ppermute x6, waiting for transfers between devices, to_core(): return lax.ppermute(value, 'tp', [(i, i ^ 1) for i in range(tp)])  1.35 us
  transfers between devices with their start and end apart: 24, of which 15 were waited for; matrix products, arithmetic and copies ran while one was open for 2% of the time, Pallas kernels for 3%

profile of v13, /device:TPU:0, one launch (start us, length us, event | category | flops | bytes accessed | tf_op | source)
XLA Modules:
  0.0 58.7 jit_solution(14862979120215065817)
XLA Ops:
  0.7 1.1 %fusion = (bf16[64,1024]{1,0:T(8,128)(2,1)S(1)}, bf16[64,1024]{1,0:T(8,128)(2,1)S(1)}, bf16[64,1024]{1,0:T(8,128)(2,1)S(1)}) fusion(bf16[128,4096]{1,0:T(8,128)(2,1)} %param.8, s32[]{:T(128)S(6)} %select_n.33, s32[]{:T(128)S(6)} %select_n.36, s32[]{:T(128)S(6)} %select_n.34, s32[]{:T(128)S(6)} %select_n.35), kind=kLoop, calls=%fused_computation.4 | loop fusion | bytes 786448 | tf_op jit(solution)/shard_map/dynamic_slice | solution.py:252
  1.8 3.0 %collective-permute-start.2 = (bf16[64,1024]{1,0:T(8,128)(2,1)S(1)}, bf16[64,1024]{1,0:T(8,128)(2,1)S(1)}, u32[]{:S(2)}, u32[]{:S(2)}) collective-permute-start(bf16[64,1024]{1,0:T(8,128)(2,1)S(1)} %get-tuple-element.48), channel_id=1, source_target_pairs={{0,8},{8,0},{16,24},{24,16},{1,9},{9,1},{17,25},{25,17},{2,10},{10... | collective-permute-start | bytes 393224 | tf_op jit(solution)/shard_map/ppermute | solution.py:235
  4.8 1.5 %collective-permute-start = (bf16[64,1024]{1,0:T(8,128)(2,1)S(1)}, bf16[64,1024]{1,0:T(8,128)(2,1)S(1)}, u32[]{:S(2)}, u32[]{:S(2)}) collective-permute-start(bf16[64,1024]{1,0:T(8,128)(2,1)S(1)} %get-tuple-element.49), channel_id=1, source_target_pairs={{0,16},{8,24},{16,0},{24,8},{1,17},{9,25},{17,1},{25,9},{2,18},{10... | collective-permute-start | bytes 393224 | tf_op jit(solution)/shard_map/ppermute | solution.py:235
  6.4 2.1 %collective-permute-start.6 = (bf16[256,512]{1,0:T(8,128)(2,1)S(1)}, bf16[256,512]{1,0:T(8,128)(2,1)S(1)}, u32[]{:S(2)}, u32[]{:S(2)}) collective-permute-start(bf16[256,512]{1,0:T(8,128)(2,1)S(1)} %get-tuple-element.52), channel_id=1, source_target_pairs={{0,2},{1,3},{2,0},{3,1},{4,6},{5,7},{6,4},{7,5},{8,10},{9,11},{10,... | collective-permute-start | bytes 786440 | tf_op jit(solution)/shard_map/ppermute | solution.py:231
  8.7 3.9 %collective-permute-done.refs_0_ = bf16[64,1024]{1,0:T(8,128)(2,1)S(1)} collective-permute-done((bf16[64,1024]{1,0:T(8,128)(2,1)S(1)}, bf16[64,1024]{1,0:T(8,128)(2,1)S(1)}, u32[]{:S(2)}, u32[]{:S(2)}) %collective-permute-start) | collective-permute-done | bytes 131104 | tf_op jit(solution)/shard_map/ppermute | solution.py:235
  13.1 1.0 %constant_dynamic-slice_fusion.3.own = bf16[128,1024]{1,0:T(8,128)(2,1)S(1)} fusion(bf16[128,4096]{1,0:T(8,128)(2,1)} %param.8, s32[]{:T(128)S(6)} %select_n.31), kind=kLoop, calls=%fused_computation.3 | loop fusion | bytes 524292 | tf_op jit(solution)/shard_map/dynamic_slice | solution.py:255
  14.9 1.6 %collective-permute-start.7 = (bf16[136,512]{1,0:T(8,128)(2,1)S(1)}, bf16[136,512]{1,0:T(8,128)(2,1)S(1)}, u32[]{:S(2)}, u32[]{:S(2)}) collective-permute-start(bf16[136,512]{1,0:T(8,128)(2,1)S(1)} %get-tuple-element.28), channel_id=1, source_target_pairs={{0,8},{8,0},{16,24},{24,16},{1,9},{9,1},{17,25},{25,17},{2,10},{10... | collective-permute-start | bytes 417800 | tf_op jit(solution)/shard_map/ppermute | solution.py:235
  16.5 1.5 %collective-permute-start.8 = (bf16[136,512]{1,0:T(8,128)(2,1)S(1)}, bf16[136,512]{1,0:T(8,128)(2,1)S(1)}, u32[]{:S(2)}, u32[]{:S(2)}) collective-permute-start(bf16[136,512]{1,0:T(8,128)(2,1)S(1)} %get-tuple-element.29), channel_id=1, source_target_pairs={{0,16},{8,24},{16,0},{24,8},{1,17},{9,25},{17,1},{25,9},{2,18},{10... | collective-permute-start | bytes 417800 | tf_op jit(solution)/shard_map/ppermute | solution.py:235
  19.1 2.4 %collective-permute-done.7.refs_0_ = bf16[136,512]{1,0:T(8,128)(2,1)S(1)} collective-permute-done((bf16[136,512]{1,0:T(8,128)(2,1)S(1)}, bf16[136,512]{1,0:T(8,128)(2,1)S(1)}, u32[]{:S(2)}, u32[]{:S(2)}) %collective-permute-start.7) | collective-permute-done | bytes 139296 | tf_op jit(solution)/shard_map/ppermute | solution.py:235
  21.5 2.1 %collective-permute-done.8.refs_1_ = bf16[136,512]{1,0:T(8,128)(2,1)S(1)} collective-permute-done((bf16[136,512]{1,0:T(8,128)(2,1)S(1)}, bf16[136,512]{1,0:T(8,128)(2,1)S(1)}, u32[]{:S(2)}, u32[]{:S(2)}) %collective-permute-start.8) | collective-permute-done | bytes 139296 | tf_op jit(solution)/shard_map/ppermute | solution.py:235
  23.6 1.2 %collective-permute-done.9.refs_2_ = bf16[136,512]{1,0:T(8,128)(2,1)S(1)} collective-permute-done((bf16[136,512]{1,0:T(8,128)(2,1)S(1)}, bf16[136,512]{1,0:T(8,128)(2,1)S(1)}, u32[]{:S(2)}, u32[]{:S(2)}) %collective-permute-start.9) | collective-permute-done | bytes 139296 | tf_op jit(solution)/shard_map/ppermute | solution.py:235
  24.9 0.9 %collective-permute-start.12 = (bf16[128,512]{1,0:T(8,128)(2,1)S(1)}, bf16[128,512]{1,0:T(8,128)(2,1)S(1)}, u32[]{:S(2)}, u32[]{:S(2)}) collective-permute-start(bf16[128,512]{1,0:T(8,128)(2,1)S(1)} %get-tuple-element.31.refs_0_), channel_id=1, source_target_pairs={{0,8},{8,0},{16,24},{24,16},{1,9},{9,1},{17,25},{25,17},{2,10},{10... | collective-permute-start | bytes 393224 | tf_op jit(solution)/shard_map/ppermute | solution.py:235
  25.8 1.5 %collective-permute-start.11 = (bf16[128,512]{1,0:T(8,128)(2,1)S(1)}, bf16[128,512]{1,0:T(8,128)(2,1)S(1)}, u32[]{:S(2)}, u32[]{:S(2)}) collective-permute-start(bf16[128,512]{1,0:T(8,128)(2,1)S(1)} %get-tuple-element.31.refs_0_), channel_id=1, source_target_pairs={{0,16},{8,24},{16,0},{24,8},{1,17},{9,25},{17,1},{25,9},{2,18},{10... | collective-permute-start | bytes 393224 | tf_op jit(solution)/shard_map/ppermute | solution.py:235
  27.3 1.2 %collective-permute-start.10 = (bf16[128,512]{1,0:T(8,128)(2,1)S(1)}, bf16[128,512]{1,0:T(8,128)(2,1)S(1)}, u32[]{:S(2)}, u32[]{:S(2)}) collective-permute-start(bf16[128,512]{1,0:T(8,128)(2,1)S(1)} %get-tuple-element.31.refs_0_), channel_id=1, source_target_pairs={{0,24},{8,16},{16,8},{24,0},{1,25},{9,17},{17,9},{25,1},{2,26},{10... | collective-permute-start | bytes 393224 | tf_op jit(solution)/shard_map/ppermute | solution.py:235
  28.4 0.8 %mask.1 = (f32[512,512]{1,0:T(8,128)S(1)}, f32[16,512]{1,0:T(8,128)S(1)}) custom-call(s32[8]{0:T(128)S(1)} %copy-done.5, s32[4]{0:T(128)S(1)} %copy-done.6), custom_call_target="tpu_custom_call" | custom-call | tf_op jit(solution)/shard_map/mask/pallas_call | solution.py:240
  29.3 2.0 %collective-permute-done.12.refs_3_ = bf16[128,512]{1,0:T(8,128)(2,1)S(1)} collective-permute-done((bf16[128,512]{1,0:T(8,128)(2,1)S(1)}, bf16[128,512]{1,0:T(8,128)(2,1)S(1)}, u32[]{:S(2)}, u32[]{:S(2)}) %collective-permute-start.12) | collective-permute-done | bytes 131104 | tf_op jit(solution)/shard_map/ppermute | solution.py:235
  31.3 0.8 %collective-permute-done.11.refs_2_ = bf16[128,512]{1,0:T(8,128)(2,1)S(1)} collective-permute-done((bf16[128,512]{1,0:T(8,128)(2,1)S(1)}, bf16[128,512]{1,0:T(8,128)(2,1)S(1)}, u32[]{:S(2)}, u32[]{:S(2)}) %collective-permute-start.11) | collective-permute-done | bytes 131104 | tf_op jit(solution)/shard_map/ppermute | solution.py:235
  32.1 1.0 %collective-permute-done.10.refs_1_ = bf16[128,512]{1,0:T(8,128)(2,1)S(1)} collective-permute-done((bf16[128,512]{1,0:T(8,128)(2,1)S(1)}, bf16[128,512]{1,0:T(8,128)(2,1)S(1)}, u32[]{:S(2)}, u32[]{:S(2)}) %collective-permute-start.10) | collective-permute-done | bytes 131104 | tf_op jit(solution)/shard_map/ppermute | solution.py:235
  33.1 0.9 %attend_sent.1.refs_7_ = bf16[264,256]{1,0:T(8,128)(2,1)S(1)} custom-call(bf16[128,512]{1,0:T(8,128)(2,1)S(1)} %get-tuple-element.31.refs_0_, bf16[128,512]{1,0:T(8,128)(2,1)S(1)} %collective-permute-done.10.refs_1_, bf16[128,512]{1,0:T(8,128)(2,1)S(1)} %collective-permute-done.11.refs_2_, bf16[128,512]{1,0:T(8,128)(2,1)S(1)} %collective-permute-done.12.refs_3_, ...), custom_call_target="tpu_custom_call" | custom-call | tf_op jit(solution)/shard_map/attend_sent/pallas_call | solution.py:240
  34.1 1.6 %collective-permute-start.15 = (bf16[264,256]{1,0:T(8,128)(2,1)S(1)}, bf16[264,256]{1,0:T(8,128)(2,1)S(1)}, u32[]{:S(2)}, u32[]{:S(2)}) collective-permute-start(bf16[264,256]{1,0:T(8,128)(2,1)S(1)} %attend_sent.1.refs_7_), channel_id=1, source_target_pairs={{0,2},{1,3},{2,0},{3,1},{4,6},{5,7},{6,4},{7,5},{8,10},{9,11},{10,... | collective-permute-start | bytes 405512 | tf_op jit(solution)/shard_map/ppermute | solution.py:231
  37.1 2.1 %collective-permute-done.15.refs_2_ = bf16[264,256]{1,0:T(8,128)(2,1)S(1)} collective-permute-done((bf16[264,256]{1,0:T(8,128)(2,1)S(1)}, bf16[264,256]{1,0:T(8,128)(2,1)S(1)}, u32[]{:S(2)}, u32[]{:S(2)}) %collective-permute-start.15) | collective-permute-done | bytes 135200 | tf_op jit(solution)/shard_map/ppermute | solution.py:231
  39.2 1.3 %collective-permute-done.16.refs_3_ = bf16[264,256]{1,0:T(8,128)(2,1)S(1)} collective-permute-done((bf16[264,256]{1,0:T(8,128)(2,1)S(1)}, bf16[264,256]{1,0:T(8,128)(2,1)S(1)}, u32[]{:S(2)}, u32[]{:S(2)}) %collective-permute-start.16) | collective-permute-done | bytes 135200 | tf_op jit(solution)/shard_map/ppermute | solution.py:228
  41.0 1.2 %collective-permute-start.18 = (bf16[72,512]{1,0:T(8,128)(2,1)S(1)}, bf16[72,512]{1,0:T(8,128)(2,1)S(1)}, u32[]{:S(2)}, u32[]{:S(2)}) collective-permute-start(bf16[72,512]{1,0:T(8,128)(2,1)S(1)} %get-tuple-element.41), channel_id=1, source_target_pairs={{0,8},{8,0},{16,24},{24,16},{1,9},{9,1},{17,25},{25,17},{2,10},{10... | collective-permute-start | bytes 221192 | tf_op jit(solution)/shard_map/ppermute | solution.py:235
  42.2 1.5 %collective-permute-start.19 = (bf16[72,512]{1,0:T(8,128)(2,1)S(1)}, bf16[72,512]{1,0:T(8,128)(2,1)S(1)}, u32[]{:S(2)}, u32[]{:S(2)}) collective-permute-start(bf16[72,512]{1,0:T(8,128)(2,1)S(1)} %get-tuple-element.42), channel_id=1, source_target_pairs={{0,16},{8,24},{16,0},{24,8},{1,17},{9,25},{17,1},{25,9},{2,18},{10... | collective-permute-start | bytes 221192 | tf_op jit(solution)/shard_map/ppermute | solution.py:235
  43.6 0.9 %collective-permute-start.20 = (bf16[72,512]{1,0:T(8,128)(2,1)S(1)}, bf16[72,512]{1,0:T(8,128)(2,1)S(1)}, u32[]{:S(2)}, u32[]{:S(2)}) collective-permute-start(bf16[72,512]{1,0:T(8,128)(2,1)S(1)} %get-tuple-element.43), channel_id=1, source_target_pairs={{0,24},{8,16},{16,8},{24,0},{1,25},{9,17},{17,9},{25,1},{2,26},{10... | collective-permute-start | bytes 221192 | tf_op jit(solution)/shard_map/ppermute | solution.py:235
  44.5 0.9 %collective-permute-done.18.refs_1_ = bf16[72,512]{1,0:T(8,128)(2,1)S(1)} collective-permute-done((bf16[72,512]{1,0:T(8,128)(2,1)S(1)}, bf16[72,512]{1,0:T(8,128)(2,1)S(1)}, u32[]{:S(2)}, u32[]{:S(2)}) %collective-permute-start.18) | collective-permute-done | bytes 73760 | tf_op jit(solution)/shard_map/ppermute | solution.py:235
  45.4 1.2 %collective-permute-done.19.refs_2_ = bf16[72,512]{1,0:T(8,128)(2,1)S(1)} collective-permute-done((bf16[72,512]{1,0:T(8,128)(2,1)S(1)}, bf16[72,512]{1,0:T(8,128)(2,1)S(1)}, u32[]{:S(2)}, u32[]{:S(2)}) %collective-permute-start.19) | collective-permute-done | bytes 73760 | tf_op jit(solution)/shard_map/ppermute | solution.py:235
  46.5 2.4 %collective-permute-done.20.refs_3_ = bf16[72,512]{1,0:T(8,128)(2,1)S(1)} collective-permute-done((bf16[72,512]{1,0:T(8,128)(2,1)S(1)}, bf16[72,512]{1,0:T(8,128)(2,1)S(1)}, u32[]{:S(2)}, u32[]{:S(2)}) %collective-permute-start.20) | collective-permute-done | bytes 73760 | tf_op jit(solution)/shard_map/ppermute | solution.py:235
  49.0 3.7 %collective-permute-start.21 = (bf16[72,512]{1,0:T(8,128)(2,1)S(1)}, bf16[72,512]{1,0:T(8,128)(2,1)S(1)}, u32[]{:S(2)}, u32[]{:S(2)}) collective-permute-start(bf16[72,512]{1,0:T(8,128)(2,1)S(1)} %get-tuple-element.45), channel_id=1, source_target_pairs={{0,6},{1,7},{2,4},{3,5},{4,2},{5,3},{6,0},{7,1},{8,14},{9,15},{10,... | collective-permute-start | bytes 221192 | tf_op jit(solution)/shard_map/ppermute | solution.py:231
  52.6 0.8 %collective-permute-start.23 = (bf16[72,512]{1,0:T(8,128)(2,1)S(1)}, bf16[72,512]{1,0:T(8,128)(2,1)S(1)}, u32[]{:S(2)}, u32[]{:S(2)}) collective-permute-start(bf16[72,512]{1,0:T(8,128)(2,1)S(1)} %get-tuple-element.47), channel_id=1, source_target_pairs={{0,2},{1,3},{2,0},{3,1},{4,6},{5,7},{6,4},{7,5},{8,10},{9,11},{10,... | collective-permute-start | bytes 221192 | tf_op jit(solution)/shard_map/ppermute | solution.py:231
  53.4 1.8 %collective-permute-done.21.refs_1_ = bf16[72,512]{1,0:T(8,128)(2,1)S(1)} collective-permute-done((bf16[72,512]{1,0:T(8,128)(2,1)S(1)}, bf16[72,512]{1,0:T(8,128)(2,1)S(1)}, u32[]{:S(2)}, u32[]{:S(2)}) %collective-permute-start.21) | collective-permute-done | bytes 73760 | tf_op jit(solution)/shard_map/ppermute | solution.py:231
  55.2 2.8 %collective-permute-done.22.refs_2_ = bf16[72,512]{1,0:T(8,128)(2,1)S(1)} collective-permute-done((bf16[72,512]{1,0:T(8,128)(2,1)S(1)}, bf16[72,512]{1,0:T(8,128)(2,1)S(1)}, u32[]{:S(2)}, u32[]{:S(2)}) %collective-permute-start.22) | collective-permute-done | bytes 73760 | tf_op jit(solution)/shard_map/ppermute | solution.py:231
  (42 shorter events, 5.3 us)
Async XLA Ops:
  0.6 12.5 %copy-start = (bf16[4,4096]{1,0:T(4,128)(2,1)S(1)}, bf16[4,4096]{1,0:T(4,128)(2,1)}, u32[]{:S(2)}) copy-start(bf16[4,4096]{1,0:T(4,128)(2,1)} %param.9) | copy-start | bytes 98308
  0.6 5.7 %copy-start.1 = (bf16[256,1024]{1,0:T(8,128)(2,1)S(1)}, bf16[256,1024]{1,0:T(8,128)(2,1)}, u32[]{:S(2)}) copy-start(bf16[256,1024]{1,0:T(8,128)(2,1)} %refs_4_.1) | copy-start | bytes 1572868
  1.8 6.9 %collective-permute-start.2 = (bf16[64,1024]{1,0:T(8,128)(2,1)S(1)}, bf16[64,1024]{1,0:T(8,128)(2,1)S(1)}, u32[]{:S(2)}, u32[]{:S(2)}) collective-permute-start(bf16[64,1024]{1,0:T(8,128)(2,1)S(1)} %get-tuple-element.48), channel_id=1, source_target_pairs={{0,8},{8,0},{16,24},{24,16},{1,9},{9,1},{17,25},{25,17},{2,10},{10... | collective-permute-start | bytes 393224 | tf_op jit(solution)/shard_map/ppermute | solution.py:235
  4.8 7.8 %collective-permute-start = (bf16[64,1024]{1,0:T(8,128)(2,1)S(1)}, bf16[64,1024]{1,0:T(8,128)(2,1)S(1)}, u32[]{:S(2)}, u32[]{:S(2)}) collective-permute-start(bf16[64,1024]{1,0:T(8,128)(2,1)S(1)} %get-tuple-element.49), channel_id=1, source_target_pairs={{0,16},{8,24},{16,0},{24,8},{1,17},{9,25},{17,1},{25,9},{2,18},{10... | collective-permute-start | bytes 393224 | tf_op jit(solution)/shard_map/ppermute | solution.py:235
  6.3 6.3 %collective-permute-start.1 = (bf16[64,1024]{1,0:T(8,128)(2,1)S(1)}, bf16[64,1024]{1,0:T(8,128)(2,1)S(1)}, u32[]{:S(2)}, u32[]{:S(2)}) collective-permute-start(bf16[64,1024]{1,0:T(8,128)(2,1)S(1)} %get-tuple-element.50), channel_id=1, source_target_pairs={{0,24},{8,16},{16,8},{24,0},{1,25},{9,17},{17,9},{25,1},{2,26},{10... | collective-permute-start | bytes 393224 | tf_op jit(solution)/shard_map/ppermute | solution.py:235
  6.4 7.8 %copy-start.3 = (bf16[1024,128]{1,0:T(8,128)(2,1)S(1)}, bf16[1024,128]{1,0:T(8,128)(2,1)}, u32[]{:S(2)}) copy-start(bf16[1024,128]{1,0:T(8,128)(2,1)} %refs_8_.1) | copy-start | bytes 786436
  6.4 7.8 %copy-start.4 = (bf16[1024,128]{1,0:T(8,128)(2,1)S(1)}, bf16[1024,128]{1,0:T(8,128)(2,1)}, u32[]{:S(2)}) copy-start(bf16[1024,128]{1,0:T(8,128)(2,1)} %refs_9_.1) | copy-start | bytes 786436
  6.4 7.8 %copy-start.2 = (bf16[1024,256]{1,0:T(8,128)(2,1)S(1)}, bf16[1024,256]{1,0:T(8,128)(2,1)}, u32[]{:S(2)}) copy-start(bf16[1024,256]{1,0:T(8,128)(2,1)} %refs_7_.1) | copy-start | bytes 1572868
  6.4 7.7 %collective-permute-start.6 = (bf16[256,512]{1,0:T(8,128)(2,1)S(1)}, bf16[256,512]{1,0:T(8,128)(2,1)S(1)}, u32[]{:S(2)}, u32[]{:S(2)}) collective-permute-start(bf16[256,512]{1,0:T(8,128)(2,1)S(1)} %get-tuple-element.52), channel_id=1, source_target_pairs={{0,2},{1,3},{2,0},{3,1},{4,6},{5,7},{6,4},{7,5},{8,10},{9,11},{10,... | collective-permute-start | bytes 786440 | tf_op jit(solution)/shard_map/ppermute | solution.py:231
  8.7 5.4 %collective-permute-start.5 = (bf16[64,1024]{1,0:T(8,128)(2,1)S(1)}, bf16[64,1024]{1,0:T(8,128)(2,1)S(1)}, u32[]{:S(2)}, u32[]{:S(2)}) collective-permute-start(bf16[64,1024]{1,0:T(8,128)(2,1)S(1)} %collective-permute-done.2.refs_2_), channel_id=1, source_target_pairs={{0,1},{1,0},{2,3},{3,2},{4,5},{5,4},{6,7},{7,6},{8,9},{9,8},{10,11... | collective-permute-start | bytes 393224 | tf_op jit(solution)/shard_map/ppermute | solution.py:228
  12.6 1.5 %collective-permute-start.3 = (bf16[64,1024]{1,0:T(8,128)(2,1)S(1)}, bf16[64,1024]{1,0:T(8,128)(2,1)S(1)}, u32[]{:S(2)}, u32[]{:S(2)}) collective-permute-start(bf16[64,1024]{1,0:T(8,128)(2,1)S(1)} %collective-permute-done.refs_0_), channel_id=1, source_target_pairs={{0,1},{1,0},{2,3},{3,2},{4,5},{5,4},{6,7},{7,6},{8,9},{9,8},{10,11... | collective-permute-start | bytes 393224 | tf_op jit(solution)/shard_map/ppermute | solution.py:228
  12.6 1.5 %collective-permute-start.4 = (bf16[64,1024]{1,0:T(8,128)(2,1)S(1)}, bf16[64,1024]{1,0:T(8,128)(2,1)S(1)}, u32[]{:S(2)}, u32[]{:S(2)}) collective-permute-start(bf16[64,1024]{1,0:T(8,128)(2,1)S(1)} %collective-permute-done.1.refs_1_), channel_id=1, source_target_pairs={{0,1},{1,0},{2,3},{3,2},{4,5},{5,4},{6,7},{7,6},{8,9},{9,8},{10,11... | collective-permute-start | bytes 393224 | tf_op jit(solution)/shard_map/ppermute | solution.py:228
  14.9 6.6 %collective-permute-start.7 = (bf16[136,512]{1,0:T(8,128)(2,1)S(1)}, bf16[136,512]{1,0:T(8,128)(2,1)S(1)}, u32[]{:S(2)}, u32[]{:S(2)}) collective-permute-start(bf16[136,512]{1,0:T(8,128)(2,1)S(1)} %get-tuple-element.28), channel_id=1, source_target_pairs={{0,8},{8,0},{16,24},{24,16},{1,9},{9,1},{17,25},{25,17},{2,10},{10... | collective-permute-start | bytes 417800 | tf_op jit(solution)/shard_map/ppermute | solution.py:235
  16.5 7.1 %collective-permute-start.8 = (bf16[136,512]{1,0:T(8,128)(2,1)S(1)}, bf16[136,512]{1,0:T(8,128)(2,1)S(1)}, u32[]{:S(2)}, u32[]{:S(2)}) collective-permute-start(bf16[136,512]{1,0:T(8,128)(2,1)S(1)} %get-tuple-element.29), channel_id=1, source_target_pairs={{0,16},{8,24},{16,0},{24,8},{1,17},{9,25},{17,1},{25,9},{2,18},{10... | collective-permute-start | bytes 417800 | tf_op jit(solution)/shard_map/ppermute | solution.py:235
  18.0 6.8 %collective-permute-start.9 = (bf16[136,512]{1,0:T(8,128)(2,1)S(1)}, bf16[136,512]{1,0:T(8,128)(2,1)S(1)}, u32[]{:S(2)}, u32[]{:S(2)}) collective-permute-start(bf16[136,512]{1,0:T(8,128)(2,1)S(1)} %get-tuple-element.30), channel_id=1, source_target_pairs={{0,24},{8,16},{16,8},{24,0},{1,25},{9,17},{17,9},{25,1},{2,26},{10... | collective-permute-start | bytes 417800 | tf_op jit(solution)/shard_map/ppermute | solution.py:235
  18.5 10.8 %collective-permute-start.13 = (bf16[256,512]{1,0:T(8,128)(2,1)S(1)}, bf16[256,512]{1,0:T(8,128)(2,1)S(1)}, u32[]{:S(2)}, u32[]{:S(2)}) collective-permute-start(bf16[256,512]{1,0:T(8,128)(2,1)S(1)} %get-tuple-element.37), channel_id=1, source_target_pairs={{0,3},{1,2},{2,1},{3,0},{4,7},{5,6},{6,5},{7,4},{8,11},{9,10},{10,... | collective-permute-start | bytes 786440 | tf_op jit(solution)/shard_map/ppermute | solution.py:283
  24.9 3.6 %copy-start.5 = (s32[8]{0:T(128)S(1)}, s32[8]{0:T(128)}, u32[]{:S(2)}) copy-start(s32[8]{0:T(128)} %block_map.1) | copy-start | bytes 100
  24.9 3.6 %copy-start.6 = (s32[4]{0:T(128)S(1)}, s32[4]{0:T(128)}, u32[]{:S(2)}) copy-start(s32[4]{0:T(128)} %lengths.1) | copy-start | bytes 52
  24.9 6.4 %collective-permute-start.12 = (bf16[128,512]{1,0:T(8,128)(2,1)S(1)}, bf16[128,512]{1,0:T(8,128)(2,1)S(1)}, u32[]{:S(2)}, u32[]{:S(2)}) collective-permute-start(bf16[128,512]{1,0:T(8,128)(2,1)S(1)} %get-tuple-element.31.refs_0_), channel_id=1, source_target_pairs={{0,8},{8,0},{16,24},{24,16},{1,9},{9,1},{17,25},{25,17},{2,10},{10... | collective-permute-start | bytes 393224 | tf_op jit(solution)/shard_map/ppermute | solution.py:235
  25.8 6.4 %collective-permute-start.11 = (bf16[128,512]{1,0:T(8,128)(2,1)S(1)}, bf16[128,512]{1,0:T(8,128)(2,1)S(1)}, u32[]{:S(2)}, u32[]{:S(2)}) collective-permute-start(bf16[128,512]{1,0:T(8,128)(2,1)S(1)} %get-tuple-element.31.refs_0_), channel_id=1, source_target_pairs={{0,16},{8,24},{16,0},{24,8},{1,17},{9,25},{17,1},{25,9},{2,18},{10... | collective-permute-start | bytes 393224 | tf_op jit(solution)/shard_map/ppermute | solution.py:235
  27.3 5.9 %collective-permute-start.10 = (bf16[128,512]{1,0:T(8,128)(2,1)S(1)}, bf16[128,512]{1,0:T(8,128)(2,1)S(1)}, u32[]{:S(2)}, u32[]{:S(2)}) collective-permute-start(bf16[128,512]{1,0:T(8,128)(2,1)S(1)} %get-tuple-element.31.refs_0_), channel_id=1, source_target_pairs={{0,24},{8,16},{16,8},{24,0},{1,25},{9,17},{17,9},{25,1},{2,26},{10... | collective-permute-start | bytes 393224 | tf_op jit(solution)/shard_map/ppermute | solution.py:235
  34.1 5.1 %collective-permute-start.15 = (bf16[264,256]{1,0:T(8,128)(2,1)S(1)}, bf16[264,256]{1,0:T(8,128)(2,1)S(1)}, u32[]{:S(2)}, u32[]{:S(2)}) collective-permute-start(bf16[264,256]{1,0:T(8,128)(2,1)S(1)} %attend_sent.1.refs_7_), channel_id=1, source_target_pairs={{0,2},{1,3},{2,0},{3,1},{4,6},{5,7},{6,4},{7,5},{8,10},{9,11},{10,... | collective-permute-start | bytes 405512 | tf_op jit(solution)/shard_map/ppermute | solution.py:231
  35.7 3.4 %collective-permute-start.17 = (bf16[256,512]{1,0:T(8,128)(2,1)S(1)}, bf16[256,512]{1,0:T(8,128)(2,1)S(1)}, u32[]{:S(2)}, u32[]{:S(2)}) collective-permute-start(bf16[256,512]{1,0:T(8,128)(2,1)S(1)} %get-tuple-element.37), channel_id=1, source_target_pairs={{0,1},{1,0},{2,3},{3,2},{4,5},{5,4},{6,7},{7,6},{8,9},{9,8},{10,11... | collective-permute-start | bytes 786440 | tf_op jit(solution)/shard_map/ppermute | solution.py:228
  36.5 2.7 %collective-permute-start.14 = (bf16[264,256]{1,0:T(8,128)(2,1)S(1)}, bf16[264,256]{1,0:T(8,128)(2,1)S(1)}, u32[]{:S(2)}, u32[]{:S(2)}) collective-permute-start(bf16[264,256]{1,0:T(8,128)(2,1)S(1)} %attend_kept.1.refs_0_), channel_id=1, source_target_pairs={{0,1},{1,0},{2,3},{3,2},{4,5},{5,4},{6,7},{7,6},{8,9},{9,8},{10,11... | collective-permute-start | bytes 405512 | tf_op jit(solution)/shard_map/ppermute | solution.py:228
  39.2 1.4 %collective-permute-start.16 = (bf16[264,256]{1,0:T(8,128)(2,1)S(1)}, bf16[264,256]{1,0:T(8,128)(2,1)S(1)}, u32[]{:S(2)}, u32[]{:S(2)}) collective-permute-start(bf16[264,256]{1,0:T(8,128)(2,1)S(1)} %collective-permute-done.15.refs_2_), channel_id=1, source_target_pairs={{0,1},{1,0},{2,3},{3,2},{4,5},{5,4},{6,7},{7,6},{8,9},{9,8},{10,11... | collective-permute-start | bytes 405512 | tf_op jit(solution)/shard_map/ppermute | solution.py:228
  41.0 4.4 %collective-permute-start.18 = (bf16[72,512]{1,0:T(8,128)(2,1)S(1)}, bf16[72,512]{1,0:T(8,128)(2,1)S(1)}, u32[]{:S(2)}, u32[]{:S(2)}) collective-permute-start(bf16[72,512]{1,0:T(8,128)(2,1)S(1)} %get-tuple-element.41), channel_id=1, source_target_pairs={{0,8},{8,0},{16,24},{24,16},{1,9},{9,1},{17,25},{25,17},{2,10},{10... | collective-permute-start | bytes 221192 | tf_op jit(solution)/shard_map/ppermute | solution.py:235
  42.2 4.4 %collective-permute-start.19 = (bf16[72,512]{1,0:T(8,128)(2,1)S(1)}, bf16[72,512]{1,0:T(8,128)(2,1)S(1)}, u32[]{:S(2)}, u32[]{:S(2)}) collective-permute-start(bf16[72,512]{1,0:T(8,128)(2,1)S(1)} %get-tuple-element.42), channel_id=1, source_target_pairs={{0,16},{8,24},{16,0},{24,8},{1,17},{9,25},{17,1},{25,9},{2,18},{10... | collective-permute-start | bytes 221192 | tf_op jit(solution)/shard_map/ppermute | solution.py:235
  43.6 5.3 %collective-permute-start.20 = (bf16[72,512]{1,0:T(8,128)(2,1)S(1)}, bf16[72,512]{1,0:T(8,128)(2,1)S(1)}, u32[]{:S(2)}, u32[]{:S(2)}) collective-permute-start(bf16[72,512]{1,0:T(8,128)(2,1)S(1)} %get-tuple-element.43), channel_id=1, source_target_pairs={{0,24},{8,16},{16,8},{24,0},{1,25},{9,17},{17,9},{25,1},{2,26},{10... | collective-permute-start | bytes 221192 | tf_op jit(solution)/shard_map/ppermute | solution.py:235
  49.0 6.2 %collective-permute-start.21 = (bf16[72,512]{1,0:T(8,128)(2,1)S(1)}, bf16[72,512]{1,0:T(8,128)(2,1)S(1)}, u32[]{:S(2)}, u32[]{:S(2)}) collective-permute-start(bf16[72,512]{1,0:T(8,128)(2,1)S(1)} %get-tuple-element.45), channel_id=1, source_target_pairs={{0,6},{1,7},{2,4},{3,5},{4,2},{5,3},{6,0},{7,1},{8,14},{9,15},{10,... | collective-permute-start | bytes 221192 | tf_op jit(solution)/shard_map/ppermute | solution.py:231
  52.6 5.4 %collective-permute-start.22 = (bf16[72,512]{1,0:T(8,128)(2,1)S(1)}, bf16[72,512]{1,0:T(8,128)(2,1)S(1)}, u32[]{:S(2)}, u32[]{:S(2)}) collective-permute-start(bf16[72,512]{1,0:T(8,128)(2,1)S(1)} %get-tuple-element.46), channel_id=1, source_target_pairs={{0,4},{1,5},{2,6},{3,7},{4,0},{5,1},{6,2},{7,3},{8,12},{9,13},{10,... | collective-permute-start | bytes 221192 | tf_op jit(solution)/shard_map/ppermute | solution.py:231
  52.6 5.4 %collective-permute-start.23 = (bf16[72,512]{1,0:T(8,128)(2,1)S(1)}, bf16[72,512]{1,0:T(8,128)(2,1)S(1)}, u32[]{:S(2)}, u32[]{:S(2)}) collective-permute-start(bf16[72,512]{1,0:T(8,128)(2,1)S(1)} %get-tuple-element.47), channel_id=1, source_target_pairs={{0,2},{1,3},{2,0},{3,1},{4,6},{5,7},{6,4},{7,5},{8,10},{9,11},{10,... | collective-permute-start | bytes 221192 | tf_op jit(solution)/shard_map/ppermute | solution.py:231

commit v14 on v13

--- a/solution.py
+++ b/solution.py
@@ -13,7 +13,7 @@
 LAST = 1 << 30
 ROW_TILE = 8
 VMEM_BYTES = 48 * 1024 * 1024
-TOKENS, SUMS, KEYS, OUTPUTS, HEADS = (1, 2, 0), (0, 1, 2), (2, 1, 0), (0, 1, 2), (2, 1, 0)
+KEYS, OUTPUTS, HEADS = (2, 1, 0), (0, 1, 2), (2, 1, 0)
 
 
 def vmem():
@@ -37,46 +37,62 @@
     return lax.axis_index("ctx"), t // 2, t % 2
 
 
-def project_kernel(rows, own, *refs):
-    mine, theirs, refs = put_back(TOKENS, refs[:3]), put_back(TOKENS, refs[3:6]), refs[6:]
-    (new, *weights), refs = refs[:4], refs[4:]
-    held, new_held, *outs, inputs = refs
+def fill_rows(inputs, number, mine, theirs):
+    _, _, k = place()
+    rows = mine.shape[0]
+    for core, block in ((k, mine), (1 - k, theirs)):
+        first = 2 * rows * number + core * rows
+        inputs[pl.ds(pl.multiple_of(first, rows), rows), :] = block[...]
+
+
+def fill_new(inputs, new):
     count = new.shape[0]
-    pad = new_held.shape[0]
-    tail = 4 * rows
-    _, _, k = place()
-    inputs[:rows, :] = own[...]
-    for number, pair in enumerate(zip(mine, theirs), 1):
-        for core, block in zip((k, 1 - k), pair):
-            first = number * rows + core * block.shape[0]
-            inputs[pl.ds(pl.multiple_of(first, block.shape[0]), block.shape[0]), :] = block[...]
+    tail = inputs.shape[0] - 2 * ROW_TILE
     inputs[tail:, :] = jnp.zeros_like(inputs[tail:, :])
     inputs[tail : tail + count, :] = new[...]
+
+
+def project_both_kernel(mine, theirs, new, wq, wk, wv, out, inputs):
+    fill_rows(inputs, 0, mine, theirs)
+    fill_new(inputs, new)
     x = inputs[...]
     column = 0
-    for weight in (weights[0][...], jnp.concatenate([weights[1][...], weights[2][...]], axis=1)):
+    for weight in (wq[...], jnp.concatenate([wk[...], wv[...]], axis=1)):
+        part = jnp.dot(x, weight, preferred_element_type=jnp.float32)
+        out[:, column : column + weight.shape[1]] = part[: out.shape[0]].astype(out.dtype)
+        column += weight.shape[1]
+
+
+def project_kernel(own, mine1, mine2, theirs1, theirs2, new, wq, wk, wv, *refs):
+    held, first, second, inputs = refs
+    rows = own.shape[0]
+    tail = 3 * rows
+    pad = held.shape[0] - rows
+    inputs[:rows, :] = own[...]
+    fill_rows(inputs, 1, mine1, theirs1)
+    fill_rows(inputs, 2, mine2, theirs2)
+    fill_new(inputs, new)
+    x = inputs[...]
+    column = 0
+    for weight in (wq[...], jnp.concatenate([wk[...], wv[...]], axis=1)):
         part = jnp.dot(x, weight, preferred_element_type=jnp.float32)
         to = slice(column, column + weight.shape[1])
-        held[:, to] = part[:rows]
-        news = part[tail : tail + pad].astype(new_held.dtype)
-        new_held[:, to] = news
-        for step, out in enumerate(outs, 1):
+        for step, out in enumerate((held, first, second)):
             out[:rows, to] = part[step * rows : (step + 1) * rows].astype(out.dtype)
-            out[rows:, to] = news
+            out[rows:, to] = part[tail : tail + pad].astype(out.dtype)
         column += weight.shape[1]
 
 
-def add_kernel(own, new_own, *refs):
-    (first, second, both), (held, new) = put_back(SUMS, refs[:3]), refs[3:]
+def add_kernel(held, part, out):
+    out[...] = held[...] + part[...].astype(jnp.float32)
+
+
+def add_last_kernel(total, first, second, held, new):
     rows = held.shape[0]
-
-    def total(own, at):
-        parts = [own[...].astype(jnp.float32)]
-        parts += [ref[at, :].astype(jnp.float32) for ref in (first, second, both)]
-        return ((parts[0] + parts[1]) + (parts[2] + parts[3])).astype(held.dtype)
-
-    held[...] = total(own, slice(0, rows))
-    new[...] = total(new_own, slice(rows, None))
+    added = first[...].astype(jnp.float32) + second[...].astype(jnp.float32)
+    added = (total[...] + added).astype(held.dtype)
+    held[...] = added[:rows]
+    new[...] = added[rows:]
 
 
 def request_of(position, ends):
@@ -260,32 +276,34 @@
     w_mine = lax.dynamic_slice_in_dim(w_out, k * width, width, 1)
     w_theirs = lax.dynamic_slice_in_dim(w_out, (1 - k) * width, width, 1)
     w_next = to_chip(w_mine, 1)
+
+    part = (rows + pad, features)
+    weights = (w_query, key_matrix, value_matrix)
+    (both,) = call(
+        project_both_kernel,
+        "project_both",
+        (mine[2], theirs[2], new_columns, *weights),
+        [(part, bf16)],
+        [pltpu.VMEM((rows + 2 * ROW_TILE, depth), bf16)],
+    )
     new_columns, w_next = lax.optimization_barrier((new_columns, w_next))
-
-    part = (rows + pad, features)
-    own_part, new_part, *parts = call(
-        functools.partial(project_kernel, rows),
+    own_part, first, second = call(
+        project_kernel,
         "project",
-        (
-            own,
-            *in_order(TOKENS, mine),
-            *in_order(TOKENS, theirs),
-            new_columns,
-            w_query,
-            key_matrix,
-            value_matrix,
-        ),
-        [((rows, features), f32), ((pad, features), bf16)] + [(part, bf16)] * (steps - 1),
-        [pltpu.VMEM((-(-all_rows // 16) * 16, depth), bf16)],
-    )
-
-    w_later, _ = lax.optimization_barrier((w_theirs, new_part))
+        (own, *mine[:2], *theirs[:2], new_columns, *weights),
+        [(part, f32)] + [(part, bf16)] * 2,
+        [pltpu.VMEM((3 * rows + 2 * ROW_TILE, depth), bf16)],
+    )
+
+    w_later, _ = lax.optimization_barrier((w_theirs, both))
     w_next_other = lax.ppermute(w_later, "tp", [(i, i ^ 3) for i in range(tp)])
 
+    first, second, both = to_partners([first, second, both])
+    (total,) = call(add_kernel, "add_both", (own_part, both), [(part, f32)])
     held, new = call(
-        add_kernel,
-        "add_parts",
-        (own_part, new_part, *in_order(SUMS, to_partners(parts))),
+        add_last_kernel,
+        "add_last",
+        (total, first, second),
         [((rows, features), bf16), ((pad, features), bf16)],
     )
 
@@ -329,7 +347,7 @@
         relay_kernel,
         "relay",
         [outs[0], *in_order(OUTPUTS, to_partners(outs[1:]))],
-        [(block, bf16)] * steps,
+        [(block if i % 2 == 0 else (block_rows, width), bf16) for i in range(steps)],
     )
     arrived = [to_chip(slot, step) for step, slot in enumerate(slots[1:], 1)]
     slots = [slots[0], *in_order(HEADS, arrived)]

time: 58.9 us -> 58.4 us (level)
    pallas_call x8 -> x10, Pallas kernels: 4.54 us -> 4.77 us  [call(): pl.pallas_call(kernel, out_shape=[jax.ShapeDtypeStruct(shape, kind) for s...]
  transfers between devices with their start and end apart: 24 -> 24, of which waited for: 15 -> 14; matrix products, arithmetic and copies ran while one was open for 2% -> 2% of each run, Pallas kernels for 3% -> 5%
where the time goes in v14:
time: 58.4 us; the launch traced here: 58.2 us
  waiting for transfers between devices  25.7 us (44%)
  starting transfers between devices  24.7 us (42%)
  Pallas kernels  4.77 us (8%)
  local copies, waits for them, and re-layouts  2.17 us (4%)
  between operations  0.84 us (1%)
    ppermute x12, waiting for transfers between devices, to_partners(): lax.ppermute(value, 'ctx', [(i, i ^ mask) for i in range(steps)])  17.5 us
    ppermute x12, starting transfers between devices, to_partners(): lax.ppermute(value, 'ctx', [(i, i ^ mask) for i in range(steps)])  15.3 us
    ppermute x5, starting transfers between devices, to_chip(): return lax.ppermute(value, 'tp', [(i, i ^ 2 * step) for i in range(tp)])  7.91 us
    ppermute x5, waiting for transfers between devices, to_chip(): return lax.ppermute(value, 'tp', [(i, i ^ 2 * step) for i in range(tp)])  6.84 us
    pallas_call x10, Pallas kernels, call(): pl.pallas_call(kernel, out_shape=[jax.ShapeDtypeStruct(shape, kind) for s...  4.77 us
    ppermute x6, waiting for transfers between devices, to_core(): return lax.ppermute(value, 'tp', [(i, i ^ 1) for i in range(tp)])  1.35 us
  transfers between devices with their start and end apart: 24, of which 14 were waited for; matrix products, arithmetic and copies ran while one was open for 2% of the time, Pallas kernels for 5%

profile of v14, /device:TPU:0, one launch (start us, length us, event | category | flops | bytes accessed | tf_op | source)
XLA Modules:
  0.0 58.2 jit_solution(4905192928765081146)
XLA Ops:
  0.7 1.1 %fusion = (bf16[64,1024]{1,0:T(8,128)(2,1)S(1)}, bf16[64,1024]{1,0:T(8,128)(2,1)S(1)}, bf16[64,1024]{1,0:T(8,128)(2,1)S(1)}) fusion(bf16[128,4096]{1,0:T(8,128)(2,1)} %param.8, s32[]{:T(128)S(6)} %select_n.33, s32[]{:T(128)S(6)} %select_n.37, s32[]{:T(128)S(6)} %select_n.34, s32[]{:T(128)S(6)} %select_n.35), kind=kLoop, calls=%fused_computation.4 | loop fusion | bytes 786448 | tf_op jit(solution)/shard_map/dynamic_slice | solution.py:268
  1.8 4.0 %collective-permute-start.5 = (bf16[64,1024]{1,0:T(8,128)(2,1)S(1)}, bf16[64,1024]{1,0:T(8,128)(2,1)S(1)}, u32[]{:S(2)}, u32[]{:S(2)}) collective-permute-start(bf16[64,1024]{1,0:T(8,128)(2,1)S(1)} %get-tuple-element.44), channel_id=1, source_target_pairs={{0,24},{8,16},{16,8},{24,0},{1,25},{9,17},{17,9},{25,1},{2,26},{10... | collective-permute-start | bytes 393224 | tf_op jit(solution)/shard_map/ppermute | solution.py:251
  6.5 2.0 %collective-permute-start.4 = (bf16[256,512]{1,0:T(8,128)(2,1)S(1)}, bf16[256,512]{1,0:T(8,128)(2,1)S(1)}, u32[]{:S(2)}, u32[]{:S(2)}) collective-permute-start(bf16[256,512]{1,0:T(8,128)(2,1)S(1)} %get-tuple-element.48), channel_id=1, source_target_pairs={{0,2},{1,3},{2,0},{3,1},{4,6},{5,7},{6,4},{7,5},{8,10},{9,11},{10,... | collective-permute-start | bytes 786440 | tf_op jit(solution)/shard_map/ppermute | solution.py:247
  8.5 1.6 %collective-permute-done.5.mine = bf16[64,1024]{1,0:T(8,128)(2,1)S(1)} collective-permute-done((bf16[64,1024]{1,0:T(8,128)(2,1)S(1)}, bf16[64,1024]{1,0:T(8,128)(2,1)S(1)}, u32[]{:S(2)}, u32[]{:S(2)}) %collective-permute-start.5) | collective-permute-done | bytes 131104 | tf_op jit(solution)/shard_map/ppermute | solution.py:251
  10.1 2.2 %collective-permute-done.mine1 = bf16[64,1024]{1,0:T(8,128)(2,1)S(1)} collective-permute-done((bf16[64,1024]{1,0:T(8,128)(2,1)S(1)}, bf16[64,1024]{1,0:T(8,128)(2,1)S(1)}, u32[]{:S(2)}, u32[]{:S(2)}) %collective-permute-start) | collective-permute-done | bytes 131104 | tf_op jit(solution)/shard_map/ppermute | solution.py:251
  12.9 1.0 %constant_dynamic-slice_fusion.3.own = bf16[128,1024]{1,0:T(8,128)(2,1)S(1)} fusion(bf16[128,4096]{1,0:T(8,128)(2,1)} %param.8, s32[]{:T(128)S(6)} %select_n.31), kind=kLoop, calls=%fused_computation.3 | loop fusion | bytes 524292 | tf_op jit(solution)/shard_map/dynamic_slice | solution.py:271
  14.2 1.9 %collective-permute-start.7 = (bf16[136,512]{1,0:T(8,128)(2,1)S(1)}, bf16[136,512]{1,0:T(8,128)(2,1)S(1)}, u32[]{:S(2)}, u32[]{:S(2)}) collective-permute-start(bf16[136,512]{1,0:T(8,128)(2,1)S(1)} %project_both.1), channel_id=1, source_target_pairs={{0,24},{8,16},{16,8},{24,0},{1,25},{9,17},{17,9},{25,1},{2,26},{10... | collective-permute-start | bytes 417800 | tf_op jit(solution)/shard_map/ppermute | solution.py:251
  16.2 0.6 %project.1 = (f32[136,512]{1,0:T(8,128)S(1)}, bf16[136,512]{1,0:T(8,128)(2,1)S(1)}, bf16[136,512]{1,0:T(8,128)(2,1)S(1)}) custom-call(bf16[128,1024]{1,0:T(8,128)(2,1)S(1)} %constant_dynamic-slice_fusion.3.own, bf16[64,1024]{1,0:T(8,128)(2,1)S(1)} %collective-permute-done.mine1, bf16[64,1024]{1,0:T(8,128)(2,1)S(1)} %collective-permute-done.1.mine2, ...), custom_call_target="tpu_custom_call" | custom-call | tf_op jit(solution)/shard_map/project/pallas_call | solution.py:256
  17.4 1.1 %collective-permute-start.9 = (bf16[136,512]{1,0:T(8,128)(2,1)S(1)}, bf16[136,512]{1,0:T(8,128)(2,1)S(1)}, u32[]{:S(2)}, u32[]{:S(2)}) collective-permute-start(bf16[136,512]{1,0:T(8,128)(2,1)S(1)} %get-tuple-element.26), channel_id=1, source_target_pairs={{0,16},{8,24},{16,0},{24,8},{1,17},{9,25},{17,1},{25,9},{2,18},{10... | collective-permute-start | bytes 417800 | tf_op jit(solution)/shard_map/ppermute | solution.py:251
  18.8 2.9 %collective-permute-done.7.part = bf16[136,512]{1,0:T(8,128)(2,1)S(1)} collective-permute-done((bf16[136,512]{1,0:T(8,128)(2,1)S(1)}, bf16[136,512]{1,0:T(8,128)(2,1)S(1)}, u32[]{:S(2)}, u32[]{:S(2)}) %collective-permute-start.7) | collective-permute-done | bytes 139296 | tf_op jit(solution)/shard_map/ppermute | solution.py:251
  21.8 2.0 %collective-permute-done.8.first = bf16[136,512]{1,0:T(8,128)(2,1)S(1)} collective-permute-done((bf16[136,512]{1,0:T(8,128)(2,1)S(1)}, bf16[136,512]{1,0:T(8,128)(2,1)S(1)}, u32[]{:S(2)}, u32[]{:S(2)}) %collective-permute-start.8) | collective-permute-done | bytes 139296 | tf_op jit(solution)/shard_map/ppermute | solution.py:251
  23.9 1.6 %collective-permute-start.12 = (bf16[128,512]{1,0:T(8,128)(2,1)S(1)}, bf16[128,512]{1,0:T(8,128)(2,1)S(1)}, u32[]{:S(2)}, u32[]{:S(2)}) collective-permute-start(bf16[128,512]{1,0:T(8,128)(2,1)S(1)} %get-tuple-element.27.refs_0_), channel_id=1, source_target_pairs={{0,8},{8,0},{16,24},{24,16},{1,9},{9,1},{17,25},{25,17},{2,10},{10... | collective-permute-start | bytes 393224 | tf_op jit(solution)/shard_map/ppermute | solution.py:251
  25.4 1.4 %collective-permute-start.11 = (bf16[128,512]{1,0:T(8,128)(2,1)S(1)}, bf16[128,512]{1,0:T(8,128)(2,1)S(1)}, u32[]{:S(2)}, u32[]{:S(2)}) collective-permute-start(bf16[128,512]{1,0:T(8,128)(2,1)S(1)} %get-tuple-element.27.refs_0_), channel_id=1, source_target_pairs={{0,16},{8,24},{16,0},{24,8},{1,17},{9,25},{17,1},{25,9},{2,18},{10... | collective-permute-start | bytes 393224 | tf_op jit(solution)/shard_map/ppermute | solution.py:251
  26.8 0.6 %collective-permute-start.10 = (bf16[128,512]{1,0:T(8,128)(2,1)S(1)}, bf16[128,512]{1,0:T(8,128)(2,1)S(1)}, u32[]{:S(2)}, u32[]{:S(2)}) collective-permute-start(bf16[128,512]{1,0:T(8,128)(2,1)S(1)} %get-tuple-element.27.refs_0_), channel_id=1, source_target_pairs={{0,24},{8,16},{16,8},{24,0},{1,25},{9,17},{17,9},{25,1},{2,26},{10... | collective-permute-start | bytes 393224 | tf_op jit(solution)/shard_map/ppermute | solution.py:251
  27.5 0.8 %mask.1 = (f32[512,512]{1,0:T(8,128)S(1)}, f32[16,512]{1,0:T(8,128)S(1)}) custom-call(s32[8]{0:T(128)S(1)} %copy-done.5, s32[4]{0:T(128)S(1)} %copy-done.6), custom_call_target="tpu_custom_call" | custom-call | tf_op jit(solution)/shard_map/mask/pallas_call | solution.py:256
  28.3 1.1 %collective-permute-done.12.refs_3_ = bf16[128,512]{1,0:T(8,128)(2,1)S(1)} collective-permute-done((bf16[128,512]{1,0:T(8,128)(2,1)S(1)}, bf16[128,512]{1,0:T(8,128)(2,1)S(1)}, u32[]{:S(2)}, u32[]{:S(2)}) %collective-permute-start.12) | collective-permute-done | bytes 131104 | tf_op jit(solution)/shard_map/ppermute | solution.py:251
  29.4 3.8 %collective-permute-done.11.refs_2_ = bf16[128,512]{1,0:T(8,128)(2,1)S(1)} collective-permute-done((bf16[128,512]{1,0:T(8,128)(2,1)S(1)}, bf16[128,512]{1,0:T(8,128)(2,1)S(1)}, u32[]{:S(2)}, u32[]{:S(2)}) %collective-permute-start.11) | collective-permute-done | bytes 131104 | tf_op jit(solution)/shard_map/ppermute | solution.py:251
  33.2 1.0 %attend_sent.1.refs_7_ = bf16[264,256]{1,0:T(8,128)(2,1)S(1)} custom-call(bf16[128,512]{1,0:T(8,128)(2,1)S(1)} %get-tuple-element.27.refs_0_, bf16[128,512]{1,0:T(8,128)(2,1)S(1)} %collective-permute-done.10.refs_1_, bf16[128,512]{1,0:T(8,128)(2,1)S(1)} %collective-permute-done.11.refs_2_, bf16[128,512]{1,0:T(8,128)(2,1)S(1)} %collective-permute-done.12.refs_3_, ...), custom_call_target="tpu_custom_call" | custom-call | tf_op jit(solution)/shard_map/attend_sent/pallas_call | solution.py:256
  34.2 1.6 %collective-permute-start.15 = (bf16[264,256]{1,0:T(8,128)(2,1)S(1)}, bf16[264,256]{1,0:T(8,128)(2,1)S(1)}, u32[]{:S(2)}, u32[]{:S(2)}) collective-permute-start(bf16[264,256]{1,0:T(8,128)(2,1)S(1)} %attend_sent.1.refs_7_), channel_id=1, source_target_pairs={{0,2},{1,3},{2,0},{3,1},{4,6},{5,7},{6,4},{7,5},{8,10},{9,11},{10,... | collective-permute-start | bytes 405512 | tf_op jit(solution)/shard_map/ppermute | solution.py:247
  35.8 0.8 %attend_kept.1.refs_0_ = bf16[264,256]{1,0:T(8,128)(2,1)S(1)} custom-call(bf16[128,512]{1,0:T(8,128)(2,1)S(1)} %get-tuple-element.27.refs_0_, bf16[128,512]{1,0:T(8,128)(2,1)S(1)} %collective-permute-done.10.refs_1_, bf16[128,512]{1,0:T(8,128)(2,1)S(1)} %collective-permute-done.11.refs_2_, bf16[128,512]{1,0:T(8,128)(2,1)S(1)} %collective-permute-done.12.refs_3_, ...), custom_call_target="tpu_custom_call" | custom-call | tf_op jit(solution)/shard_map/attend_kept/pallas_call | solution.py:256
  37.2 2.1 %collective-permute-done.15.refs_2_ = bf16[264,256]{1,0:T(8,128)(2,1)S(1)} collective-permute-done((bf16[264,256]{1,0:T(8,128)(2,1)S(1)}, bf16[264,256]{1,0:T(8,128)(2,1)S(1)}, u32[]{:S(2)}, u32[]{:S(2)}) %collective-permute-start.15) | collective-permute-done | bytes 135200 | tf_op jit(solution)/shard_map/ppermute | solution.py:247
  39.3 1.3 %collective-permute-done.16.refs_3_ = bf16[264,256]{1,0:T(8,128)(2,1)S(1)} collective-permute-done((bf16[264,256]{1,0:T(8,128)(2,1)S(1)}, bf16[264,256]{1,0:T(8,128)(2,1)S(1)}, u32[]{:S(2)}, u32[]{:S(2)}) %collective-permute-start.16) | collective-permute-done | bytes 135200 | tf_op jit(solution)/shard_map/ppermute | solution.py:244
  41.1 1.3 %collective-permute-start.18 = (bf16[72,512]{1,0:T(8,128)(2,1)S(1)}, bf16[72,512]{1,0:T(8,128)(2,1)S(1)}, u32[]{:S(2)}, u32[]{:S(2)}) collective-permute-start(bf16[72,512]{1,0:T(8,128)(2,1)S(1)} %get-tuple-element.37), channel_id=1, source_target_pairs={{0,8},{8,0},{16,24},{24,16},{1,9},{9,1},{17,25},{25,17},{2,10},{10... | collective-permute-start | bytes 221192 | tf_op jit(solution)/shard_map/ppermute | solution.py:251
  42.4 0.8 %collective-permute-start.19 = (bf16[72,512]{1,0:T(8,128)(2,1)S(1)}, bf16[72,512]{1,0:T(8,128)(2,1)S(1)}, u32[]{:S(2)}, u32[]{:S(2)}) collective-permute-start(bf16[72,512]{1,0:T(8,128)(2,1)S(1)} %get-tuple-element.38), channel_id=1, source_target_pairs={{0,16},{8,24},{16,0},{24,8},{1,17},{9,25},{17,1},{25,9},{2,18},{10... | collective-permute-start | bytes 221192 | tf_op jit(solution)/shard_map/ppermute | solution.py:251
  43.2 1.4 %collective-permute-start.20 = (bf16[72,512]{1,0:T(8,128)(2,1)S(1)}, bf16[72,512]{1,0:T(8,128)(2,1)S(1)}, u32[]{:S(2)}, u32[]{:S(2)}) collective-permute-start(bf16[72,512]{1,0:T(8,128)(2,1)S(1)} %get-tuple-element.39), channel_id=1, source_target_pairs={{0,24},{8,16},{16,8},{24,0},{1,25},{9,17},{17,9},{25,1},{2,26},{10... | collective-permute-start | bytes 221192 | tf_op jit(solution)/shard_map/ppermute | solution.py:251
  44.6 0.9 %collective-permute-done.18.refs_1_ = bf16[72,512]{1,0:T(8,128)(2,1)S(1)} collective-permute-done((bf16[72,512]{1,0:T(8,128)(2,1)S(1)}, bf16[72,512]{1,0:T(8,128)(2,1)S(1)}, u32[]{:S(2)}, u32[]{:S(2)}) %collective-permute-start.18) | collective-permute-done | bytes 73760 | tf_op jit(solution)/shard_map/ppermute | solution.py:251
  45.5 2.1 %collective-permute-done.19.refs_2_ = bf16[72,512]{1,0:T(8,128)(2,1)S(1)} collective-permute-done((bf16[72,512]{1,0:T(8,128)(2,1)S(1)}, bf16[72,512]{1,0:T(8,128)(2,1)S(1)}, u32[]{:S(2)}, u32[]{:S(2)}) %collective-permute-start.19) | collective-permute-done | bytes 73760 | tf_op jit(solution)/shard_map/ppermute | solution.py:251
  47.6 0.9 %collective-permute-done.20.refs_3_ = bf16[72,512]{1,0:T(8,128)(2,1)S(1)} collective-permute-done((bf16[72,512]{1,0:T(8,128)(2,1)S(1)}, bf16[72,512]{1,0:T(8,128)(2,1)S(1)}, u32[]{:S(2)}, u32[]{:S(2)}) %collective-permute-start.20) | collective-permute-done | bytes 73760 | tf_op jit(solution)/shard_map/ppermute | solution.py:251
  48.5 2.6 %collective-permute-start.22 = (bf16[72,512]{1,0:T(8,128)(2,1)S(1)}, bf16[72,512]{1,0:T(8,128)(2,1)S(1)}, u32[]{:S(2)}, u32[]{:S(2)}) collective-permute-start(bf16[72,512]{1,0:T(8,128)(2,1)S(1)} %get-tuple-element.42), channel_id=1, source_target_pairs={{0,4},{1,5},{2,6},{3,7},{4,0},{5,1},{6,2},{7,3},{8,12},{9,13},{10,... | collective-permute-start | bytes 221192 | tf_op jit(solution)/shard_map/ppermute | solution.py:247
  51.2 1.4 %collective-permute-start.21 = (bf16[64,512]{1,0:T(8,128)(2,1)S(1)}, bf16[64,512]{1,0:T(8,128)(2,1)S(1)}, u32[]{:S(2)}, u32[]{:S(2)}) collective-permute-start(bf16[64,512]{1,0:T(8,128)(2,1)S(1)} %get-tuple-element.41), channel_id=1, source_target_pairs={{0,6},{1,7},{2,4},{3,5},{4,2},{5,3},{6,0},{7,1},{8,14},{9,15},{10,... | collective-permute-start | bytes 196616 | tf_op jit(solution)/shard_map/ppermute | solution.py:247
  52.8 4.6 %collective-permute-done.21.refs_1_ = bf16[64,512]{1,0:T(8,128)(2,1)S(1)} collective-permute-done((bf16[64,512]{1,0:T(8,128)(2,1)S(1)}, bf16[64,512]{1,0:T(8,128)(2,1)S(1)}, u32[]{:S(2)}, u32[]{:S(2)}) %collective-permute-start.21) | collective-permute-done | bytes 65568 | tf_op jit(solution)/shard_map/ppermute | solution.py:247
  57.5 0.7 %finish.1 = (bf16[128,512]{1,0:T(8,128)(2,1)}, bf16[4,512]{1,0:T(4,128)(2,1)}) custom-call(bf16[72,512]{1,0:T(8,128)(2,1)S(1)} %get-tuple-element.40.refs_0_, bf16[64,512]{1,0:T(8,128)(2,1)S(1)} %collective-permute-done.21.refs_1_, bf16[72,512]{1,0:T(8,128)(2,1)S(1)} %collective-permute-done.22.refs_2_, bf16[64,512]{1,0:T(8,128)(2,1)S(1)} %collective-permute-done.23.refs_3_), custom_call_target="tpu_custom_call" | custom-call | tf_op jit(solution)/shard_map/finish/pallas_call | solution.py:256
  (44 shorter events, 4.1 us)
Async XLA Ops:
  0.6 12.2 %copy-start = (bf16[4,4096]{1,0:T(4,128)(2,1)S(1)}, bf16[4,4096]{1,0:T(4,128)(2,1)}, u32[]{:S(2)}) copy-start(bf16[4,4096]{1,0:T(4,128)(2,1)} %param.9) | copy-start | bytes 98308
  0.6 5.8 %copy-start.1 = (bf16[256,1024]{1,0:T(8,128)(2,1)S(1)}, bf16[256,1024]{1,0:T(8,128)(2,1)}, u32[]{:S(2)}) copy-start(bf16[256,1024]{1,0:T(8,128)(2,1)} %refs_4_.1) | copy-start | bytes 1572868
  1.8 8.3 %collective-permute-start.5 = (bf16[64,1024]{1,0:T(8,128)(2,1)S(1)}, bf16[64,1024]{1,0:T(8,128)(2,1)S(1)}, u32[]{:S(2)}, u32[]{:S(2)}) collective-permute-start(bf16[64,1024]{1,0:T(8,128)(2,1)S(1)} %get-tuple-element.44), channel_id=1, source_target_pairs={{0,24},{8,16},{16,8},{24,0},{1,25},{9,17},{17,9},{25,1},{2,26},{10... | collective-permute-start | bytes 393224 | tf_op jit(solution)/shard_map/ppermute | solution.py:251
  5.8 6.6 %collective-permute-start = (bf16[64,1024]{1,0:T(8,128)(2,1)S(1)}, bf16[64,1024]{1,0:T(8,128)(2,1)S(1)}, u32[]{:S(2)}, u32[]{:S(2)}) collective-permute-start(bf16[64,1024]{1,0:T(8,128)(2,1)S(1)} %get-tuple-element.45), channel_id=1, source_target_pairs={{0,8},{8,0},{16,24},{24,16},{1,9},{9,1},{17,25},{25,17},{2,10},{10... | collective-permute-start | bytes 393224 | tf_op jit(solution)/shard_map/ppermute | solution.py:251
  6.3 6.0 %collective-permute-start.1 = (bf16[64,1024]{1,0:T(8,128)(2,1)S(1)}, bf16[64,1024]{1,0:T(8,128)(2,1)S(1)}, u32[]{:S(2)}, u32[]{:S(2)}) collective-permute-start(bf16[64,1024]{1,0:T(8,128)(2,1)S(1)} %get-tuple-element.46), channel_id=1, source_target_pairs={{0,16},{8,24},{16,0},{24,8},{1,17},{9,25},{17,1},{25,9},{2,18},{10... | collective-permute-start | bytes 393224 | tf_op jit(solution)/shard_map/ppermute | solution.py:251
  6.4 7.4 %copy-start.3 = (bf16[1024,128]{1,0:T(8,128)(2,1)S(1)}, bf16[1024,128]{1,0:T(8,128)(2,1)}, u32[]{:S(2)}) copy-start(bf16[1024,128]{1,0:T(8,128)(2,1)} %wk.3) | copy-start | bytes 786436
  6.4 7.4 %copy-start.4 = (bf16[1024,128]{1,0:T(8,128)(2,1)S(1)}, bf16[1024,128]{1,0:T(8,128)(2,1)}, u32[]{:S(2)}) copy-start(bf16[1024,128]{1,0:T(8,128)(2,1)} %wv.3) | copy-start | bytes 786436
  6.5 7.4 %copy-start.2 = (bf16[1024,256]{1,0:T(8,128)(2,1)S(1)}, bf16[1024,256]{1,0:T(8,128)(2,1)}, u32[]{:S(2)}) copy-start(bf16[1024,256]{1,0:T(8,128)(2,1)} %wq.3) | copy-start | bytes 1572868
  6.5 9.7 %collective-permute-start.4 = (bf16[256,512]{1,0:T(8,128)(2,1)S(1)}, bf16[256,512]{1,0:T(8,128)(2,1)S(1)}, u32[]{:S(2)}, u32[]{:S(2)}) collective-permute-start(bf16[256,512]{1,0:T(8,128)(2,1)S(1)} %get-tuple-element.48), channel_id=1, source_target_pairs={{0,2},{1,3},{2,0},{3,1},{4,6},{5,7},{6,4},{7,5},{8,10},{9,11},{10,... | collective-permute-start | bytes 786440 | tf_op jit(solution)/shard_map/ppermute | solution.py:247
  10.1 3.7 %collective-permute-start.6 = (bf16[64,1024]{1,0:T(8,128)(2,1)S(1)}, bf16[64,1024]{1,0:T(8,128)(2,1)S(1)}, u32[]{:S(2)}, u32[]{:S(2)}) collective-permute-start(bf16[64,1024]{1,0:T(8,128)(2,1)S(1)} %collective-permute-done.5.mine), channel_id=1, source_target_pairs={{0,1},{1,0},{2,3},{3,2},{4,5},{5,4},{6,7},{7,6},{8,9},{9,8},{10,11... | collective-permute-start | bytes 393224 | tf_op jit(solution)/shard_map/ppermute | solution.py:244
  12.3 3.9 %collective-permute-start.2 = (bf16[64,1024]{1,0:T(8,128)(2,1)S(1)}, bf16[64,1024]{1,0:T(8,128)(2,1)S(1)}, u32[]{:S(2)}, u32[]{:S(2)}) collective-permute-start(bf16[64,1024]{1,0:T(8,128)(2,1)S(1)} %collective-permute-done.mine1), channel_id=1, source_target_pairs={{0,1},{1,0},{2,3},{3,2},{4,5},{5,4},{6,7},{7,6},{8,9},{9,8},{10,11... | collective-permute-start | bytes 393224 | tf_op jit(solution)/shard_map/ppermute | solution.py:244
  12.3 3.8 %collective-permute-start.3 = (bf16[64,1024]{1,0:T(8,128)(2,1)S(1)}, bf16[64,1024]{1,0:T(8,128)(2,1)S(1)}, u32[]{:S(2)}, u32[]{:S(2)}) collective-permute-start(bf16[64,1024]{1,0:T(8,128)(2,1)S(1)} %collective-permute-done.1.mine2), channel_id=1, source_target_pairs={{0,1},{1,0},{2,3},{3,2},{4,5},{5,4},{6,7},{7,6},{8,9},{9,8},{10,11... | collective-permute-start | bytes 393224 | tf_op jit(solution)/shard_map/ppermute | solution.py:244
  14.2 7.5 %collective-permute-start.7 = (bf16[136,512]{1,0:T(8,128)(2,1)S(1)}, bf16[136,512]{1,0:T(8,128)(2,1)S(1)}, u32[]{:S(2)}, u32[]{:S(2)}) collective-permute-start(bf16[136,512]{1,0:T(8,128)(2,1)S(1)} %project_both.1), channel_id=1, source_target_pairs={{0,24},{8,16},{16,8},{24,0},{1,25},{9,17},{17,9},{25,1},{2,26},{10... | collective-permute-start | bytes 417800 | tf_op jit(solution)/shard_map/ppermute | solution.py:251
  16.8 7.0 %collective-permute-start.8 = (bf16[136,512]{1,0:T(8,128)(2,1)S(1)}, bf16[136,512]{1,0:T(8,128)(2,1)S(1)}, u32[]{:S(2)}, u32[]{:S(2)}) collective-permute-start(bf16[136,512]{1,0:T(8,128)(2,1)S(1)} %get-tuple-element.25), channel_id=1, source_target_pairs={{0,8},{8,0},{16,24},{24,16},{1,9},{9,1},{17,25},{25,17},{2,10},{10... | collective-permute-start | bytes 417800 | tf_op jit(solution)/shard_map/ppermute | solution.py:251
  17.4 6.4 %collective-permute-start.9 = (bf16[136,512]{1,0:T(8,128)(2,1)S(1)}, bf16[136,512]{1,0:T(8,128)(2,1)S(1)}, u32[]{:S(2)}, u32[]{:S(2)}) collective-permute-start(bf16[136,512]{1,0:T(8,128)(2,1)S(1)} %get-tuple-element.26), channel_id=1, source_target_pairs={{0,16},{8,24},{16,0},{24,8},{1,17},{9,25},{17,1},{25,9},{2,18},{10... | collective-permute-start | bytes 417800 | tf_op jit(solution)/shard_map/ppermute | solution.py:251
  18.5 9.8 %collective-permute-start.13 = (bf16[256,512]{1,0:T(8,128)(2,1)S(1)}, bf16[256,512]{1,0:T(8,128)(2,1)S(1)}, u32[]{:S(2)}, u32[]{:S(2)}) collective-permute-start(bf16[256,512]{1,0:T(8,128)(2,1)S(1)} %get-tuple-element.33), channel_id=1, source_target_pairs={{0,3},{1,2},{2,1},{3,0},{4,7},{5,6},{6,5},{7,4},{8,11},{9,10},{10,... | collective-permute-start | bytes 786440 | tf_op jit(solution)/shard_map/ppermute | solution.py:299
  23.9 3.6 %copy-start.5 = (s32[8]{0:T(128)S(1)}, s32[8]{0:T(128)}, u32[]{:S(2)}) copy-start(s32[8]{0:T(128)} %block_map.1) | copy-start | bytes 100
  23.9 3.6 %copy-start.6 = (s32[4]{0:T(128)S(1)}, s32[4]{0:T(128)}, u32[]{:S(2)}) copy-start(s32[4]{0:T(128)} %lengths.1) | copy-start | bytes 52
  23.9 5.5 %collective-permute-start.12 = (bf16[128,512]{1,0:T(8,128)(2,1)S(1)}, bf16[128,512]{1,0:T(8,128)(2,1)S(1)}, u32[]{:S(2)}, u32[]{:S(2)}) collective-permute-start(bf16[128,512]{1,0:T(8,128)(2,1)S(1)} %get-tuple-element.27.refs_0_), channel_id=1, source_target_pairs={{0,8},{8,0},{16,24},{24,16},{1,9},{9,1},{17,25},{25,17},{2,10},{10... | collective-permute-start | bytes 393224 | tf_op jit(solution)/shard_map/ppermute | solution.py:251
  25.4 7.8 %collective-permute-start.11 = (bf16[128,512]{1,0:T(8,128)(2,1)S(1)}, bf16[128,512]{1,0:T(8,128)(2,1)S(1)}, u32[]{:S(2)}, u32[]{:S(2)}) collective-permute-start(bf16[128,512]{1,0:T(8,128)(2,1)S(1)} %get-tuple-element.27.refs_0_), channel_id=1, source_target_pairs={{0,16},{8,24},{16,0},{24,8},{1,17},{9,25},{17,1},{25,9},{2,18},{10... | collective-permute-start | bytes 393224 | tf_op jit(solution)/shard_map/ppermute | solution.py:251
  26.8 6.4 %collective-permute-start.10 = (bf16[128,512]{1,0:T(8,128)(2,1)S(1)}, bf16[128,512]{1,0:T(8,128)(2,1)S(1)}, u32[]{:S(2)}, u32[]{:S(2)}) collective-permute-start(bf16[128,512]{1,0:T(8,128)(2,1)S(1)} %get-tuple-element.27.refs_0_), channel_id=1, source_target_pairs={{0,24},{8,16},{16,8},{24,0},{1,25},{9,17},{17,9},{25,1},{2,26},{10... | collective-permute-start | bytes 393224 | tf_op jit(solution)/shard_map/ppermute | solution.py:251
  34.2 5.1 %collective-permute-start.15 = (bf16[264,256]{1,0:T(8,128)(2,1)S(1)}, bf16[264,256]{1,0:T(8,128)(2,1)S(1)}, u32[]{:S(2)}, u32[]{:S(2)}) collective-permute-start(bf16[264,256]{1,0:T(8,128)(2,1)S(1)} %attend_sent.1.refs_7_), channel_id=1, source_target_pairs={{0,2},{1,3},{2,0},{3,1},{4,6},{5,7},{6,4},{7,5},{8,10},{9,11},{10,... | collective-permute-start | bytes 405512 | tf_op jit(solution)/shard_map/ppermute | solution.py:247
  35.8 3.4 %collective-permute-start.17 = (bf16[256,512]{1,0:T(8,128)(2,1)S(1)}, bf16[256,512]{1,0:T(8,128)(2,1)S(1)}, u32[]{:S(2)}, u32[]{:S(2)}) collective-permute-start(bf16[256,512]{1,0:T(8,128)(2,1)S(1)} %get-tuple-element.33), channel_id=1, source_target_pairs={{0,1},{1,0},{2,3},{3,2},{4,5},{5,4},{6,7},{7,6},{8,9},{9,8},{10,11... | collective-permute-start | bytes 786440 | tf_op jit(solution)/shard_map/ppermute | solution.py:244
  36.6 2.7 %collective-permute-start.14 = (bf16[264,256]{1,0:T(8,128)(2,1)S(1)}, bf16[264,256]{1,0:T(8,128)(2,1)S(1)}, u32[]{:S(2)}, u32[]{:S(2)}) collective-permute-start(bf16[264,256]{1,0:T(8,128)(2,1)S(1)} %attend_kept.1.refs_0_), channel_id=1, source_target_pairs={{0,1},{1,0},{2,3},{3,2},{4,5},{5,4},{6,7},{7,6},{8,9},{9,8},{10,11... | collective-permute-start | bytes 405512 | tf_op jit(solution)/shard_map/ppermute | solution.py:244
  39.3 1.4 %collective-permute-start.16 = (bf16[264,256]{1,0:T(8,128)(2,1)S(1)}, bf16[264,256]{1,0:T(8,128)(2,1)S(1)}, u32[]{:S(2)}, u32[]{:S(2)}) collective-permute-start(bf16[264,256]{1,0:T(8,128)(2,1)S(1)} %collective-permute-done.15.refs_2_), channel_id=1, source_target_pairs={{0,1},{1,0},{2,3},{3,2},{4,5},{5,4},{6,7},{7,6},{8,9},{9,8},{10,11... | collective-permute-start | bytes 405512 | tf_op jit(solution)/shard_map/ppermute | solution.py:244
  41.1 4.4 %collective-permute-start.18 = (bf16[72,512]{1,0:T(8,128)(2,1)S(1)}, bf16[72,512]{1,0:T(8,128)(2,1)S(1)}, u32[]{:S(2)}, u32[]{:S(2)}) collective-permute-start(bf16[72,512]{1,0:T(8,128)(2,1)S(1)} %get-tuple-element.37), channel_id=1, source_target_pairs={{0,8},{8,0},{16,24},{24,16},{1,9},{9,1},{17,25},{25,17},{2,10},{10... | collective-permute-start | bytes 221192 | tf_op jit(solution)/shard_map/ppermute | solution.py:251
  42.4 5.1 %collective-permute-start.19 = (bf16[72,512]{1,0:T(8,128)(2,1)S(1)}, bf16[72,512]{1,0:T(8,128)(2,1)S(1)}, u32[]{:S(2)}, u32[]{:S(2)}) collective-permute-start(bf16[72,512]{1,0:T(8,128)(2,1)S(1)} %get-tuple-element.38), channel_id=1, source_target_pairs={{0,16},{8,24},{16,0},{24,8},{1,17},{9,25},{17,1},{25,9},{2,18},{10... | collective-permute-start | bytes 221192 | tf_op jit(solution)/shard_map/ppermute | solution.py:251
  43.2 5.3 %collective-permute-start.20 = (bf16[72,512]{1,0:T(8,128)(2,1)S(1)}, bf16[72,512]{1,0:T(8,128)(2,1)S(1)}, u32[]{:S(2)}, u32[]{:S(2)}) collective-permute-start(bf16[72,512]{1,0:T(8,128)(2,1)S(1)} %get-tuple-element.39), channel_id=1, source_target_pairs={{0,24},{8,16},{16,8},{24,0},{1,25},{9,17},{17,9},{25,1},{2,26},{10... | collective-permute-start | bytes 221192 | tf_op jit(solution)/shard_map/ppermute | solution.py:251
  48.5 9.0 %collective-permute-start.22 = (bf16[72,512]{1,0:T(8,128)(2,1)S(1)}, bf16[72,512]{1,0:T(8,128)(2,1)S(1)}, u32[]{:S(2)}, u32[]{:S(2)}) collective-permute-start(bf16[72,512]{1,0:T(8,128)(2,1)S(1)} %get-tuple-element.42), channel_id=1, source_target_pairs={{0,4},{1,5},{2,6},{3,7},{4,0},{5,1},{6,2},{7,3},{8,12},{9,13},{10,... | collective-permute-start | bytes 221192 | tf_op jit(solution)/shard_map/ppermute | solution.py:247
  51.2 6.2 %collective-permute-start.21 = (bf16[64,512]{1,0:T(8,128)(2,1)S(1)}, bf16[64,512]{1,0:T(8,128)(2,1)S(1)}, u32[]{:S(2)}, u32[]{:S(2)}) collective-permute-start(bf16[64,512]{1,0:T(8,128)(2,1)S(1)} %get-tuple-element.41), channel_id=1, source_target_pairs={{0,6},{1,7},{2,4},{3,5},{4,2},{5,3},{6,0},{7,1},{8,14},{9,15},{10,... | collective-permute-start | bytes 196616 | tf_op jit(solution)/shard_map/ppermute | solution.py:247
  52.6 5.0 %collective-permute-start.23 = (bf16[64,512]{1,0:T(8,128)(2,1)S(1)}, bf16[64,512]{1,0:T(8,128)(2,1)S(1)}, u32[]{:S(2)}, u32[]{:S(2)}) collective-permute-start(bf16[64,512]{1,0:T(8,128)(2,1)S(1)} %get-tuple-element.43), channel_id=1, source_target_pairs={{0,2},{1,3},{2,0},{3,1},{4,6},{5,7},{6,4},{7,5},{8,10},{9,11},{10,... | collective-permute-start | bytes 196616 | tf_op jit(solution)/shard_map/ppermute | solution.py:247

commit v15 on v14

--- a/solution.py
+++ b/solution.py
@@ -13,7 +13,7 @@
 LAST = 1 << 30
 ROW_TILE = 8
 VMEM_BYTES = 48 * 1024 * 1024
-KEYS, OUTPUTS, HEADS = (2, 1, 0), (0, 1, 2), (2, 1, 0)
+KEYS, OUTPUTS, HEADS = (2, 1, 0), (2, 1, 0), (2, 1, 0)
 
 
 def vmem():
@@ -188,18 +188,23 @@
         attended[tail:, :] = refs[0][tail:, :]
 
 
-def output_kernel(rows, *refs):
-    heads, (w_own, *weights), outs = refs[:4], refs[4:8], refs[8:]
+def output_kernel(*refs):
+    heads, (w_own, *weights), total = refs[:3], refs[3:6], refs[6]
     _, _, k = place()
-    width = outs[0].shape[1]
+    width = total.shape[1]
     w_mine = w_own[:, pl.ds(pl.multiple_of(k * width, width), width)]
-    total = jnp.dot(heads[0][...], w_mine, preferred_element_type=jnp.float32)
+    added = jnp.dot(heads[0][...], w_mine, preferred_element_type=jnp.float32)
     for ref, weight in zip(heads[1:], weights):
-        total += jnp.dot(ref[...], weight[...], preferred_element_type=jnp.float32)
-    total = total.astype(outs[0].dtype)
+        added += jnp.dot(ref[...], weight[...], preferred_element_type=jnp.float32)
+    total[...] = added
+
+
+def output_last_kernel(rows, total, heads, weight, *outs):
+    added = total[...] + jnp.dot(heads[...], weight[...], preferred_element_type=jnp.float32)
+    added = added.astype(outs[0].dtype)
     for number, out in enumerate(outs):
-        out[:rows, :] = total[number * rows : (number + 1) * rows]
-        out[rows:, :] = total[len(outs) * rows :]
+        out[:rows, :] = added[number * rows : (number + 1) * rows]
+        out[rows:, :] = added[len(outs) * rows :]
 
 
 def relay_kernel(*refs):
@@ -271,6 +276,7 @@
     own = lax.dynamic_slice_in_dim(tokens, c * depth, depth, 1)
     new_columns = lax.dynamic_slice_in_dim(new_token_states, c * depth, depth, 1)
     mine = to_partners(sent)
+    mine[2], own = lax.optimization_barrier((mine[2], own))
     theirs = [to_core(value) for value in mine]
 
     w_mine = lax.dynamic_slice_in_dim(w_out, k * width, width, 1)
@@ -336,10 +342,16 @@
     w_other = to_core(w_last)
 
     block = (block_rows + pad, width)
+    (total,) = call(
+        output_kernel,
+        "project_out",
+        (kept, to_core(kept), got, w_out, w_other, w_next),
+        [((kept.shape[0], width), f32)],
+    )
     outs = call(
-        functools.partial(output_kernel, block_rows),
-        "project_out",
-        (kept, to_core(kept), got, to_core(got), w_out, w_other, w_next, w_next_other),
+        functools.partial(output_last_kernel, block_rows),
+        "project_last",
+        (total, to_core(got), w_next_other),
         [(block, bf16)] * steps,
     )
 

time: 58.4 us -> 57.5 us (0.985)
  starting transfers between devices: 24.7 us -> 23.1 us
    ppermute x5, starting transfers between devices: 7.91 us -> 6.4 us  [to_chip(): return lax.ppermute(value, 'tp', [(i, i ^ 2 * step) for i in range(tp)])]
    ppermute x5, waiting for transfers between devices: 6.84 us -> 8.31 us  [to_chip(): return lax.ppermute(value, 'tp', [(i, i ^ 2 * step) for i in range(tp)])]
    ppermute x12, waiting for transfers between devices: 17.5 us -> 16.9 us  [to_partners(): lax.ppermute(value, 'ctx', [(i, i ^ mask) for i in range(steps)])]
    pallas_call x10 -> x11, Pallas kernels: 4.77 us -> 4.92 us  [call(): pl.pallas_call(kernel, out_shape=[jax.ShapeDtypeStruct(shape, kind) for s...]
  transfers between devices with their start and end apart: 24 -> 24, of which waited for: 14 -> 13; matrix products, arithmetic and copies ran while one was open for 2% -> 2% of each run, Pallas kernels for 5% -> 5%
where the time goes in v15:
time: 57.5 us; the launch traced here: 57.3 us
  waiting for transfers between devices  26.2 us (46%)
  starting transfers between devices  23.1 us (40%)
  Pallas kernels  4.92 us (9%)
  local copies, waits for them, and re-layouts  2.17 us (4%)
  between operations  0.87 us (2%)
    ppermute x12, waiting for transfers between devices, to_partners(): lax.ppermute(value, 'ctx', [(i, i ^ mask) for i in range(steps)])  16.9 us
    ppermute x12, starting transfers between devices, to_partners(): lax.ppermute(value, 'ctx', [(i, i ^ mask) for i in range(steps)])  15.7 us
    ppermute x5, waiting for transfers between devices, to_chip(): return lax.ppermute(value, 'tp', [(i, i ^ 2 * step) for i in range(tp)])  8.31 us
    ppermute x5, starting transfers between devices, to_chip(): return lax.ppermute(value, 'tp', [(i, i ^ 2 * step) for i in range(tp)])  6.4 us
    pallas_call x11, Pallas kernels, call(): pl.pallas_call(kernel, out_shape=[jax.ShapeDtypeStruct(shape, kind) for s...  4.92 us
  transfers between devices with their start and end apart: 24, of which 13 were waited for; matrix products, arithmetic and copies ran while one was open for 2% of the time, Pallas kernels for 5%

profile of v15, /device:TPU:0, one launch (start us, length us, event | category | flops | bytes accessed | tf_op | source)
XLA Modules:
  0.0 57.3 jit_solution(15556452737470371870)
XLA Ops:
  0.7 1.1 %fusion = (bf16[64,1024]{1,0:T(8,128)(2,1)S(1)}, bf16[64,1024]{1,0:T(8,128)(2,1)S(1)}, bf16[64,1024]{1,0:T(8,128)(2,1)S(1)}) fusion(bf16[128,4096]{1,0:T(8,128)(2,1)} %param.8, s32[]{:T(128)S(6)} %select_n.32, s32[]{:T(128)S(6)} %select_n.36, s32[]{:T(128)S(6)} %select_n.33, s32[]{:T(128)S(6)} %select_n.35), kind=kLoop, calls=%fused_computation.4 | loop fusion | bytes 786448 | tf_op jit(solution)/shard_map/dynamic_slice | solution.py:273
  1.8 4.0 %collective-permute-start = (bf16[64,1024]{1,0:T(8,128)(2,1)S(1)}, bf16[64,1024]{1,0:T(8,128)(2,1)S(1)}, u32[]{:S(2)}, u32[]{:S(2)}) collective-permute-start(bf16[64,1024]{1,0:T(8,128)(2,1)S(1)} %get-tuple-element.49), channel_id=1, source_target_pairs={{0,24},{8,16},{16,8},{24,0},{1,25},{9,17},{17,9},{25,1},{2,26},{10... | collective-permute-start | bytes 393224 | tf_op jit(solution)/shard_map/ppermute | solution.py:256
  5.8 1.6 %collective-permute-start.5 = (bf16[256,512]{1,0:T(8,128)(2,1)S(1)}, bf16[256,512]{1,0:T(8,128)(2,1)S(1)}, u32[]{:S(2)}, u32[]{:S(2)}) collective-permute-start(bf16[256,512]{1,0:T(8,128)(2,1)S(1)} %get-tuple-element.52), channel_id=1, source_target_pairs={{0,2},{1,3},{2,0},{3,1},{4,6},{5,7},{6,4},{7,5},{8,10},{9,11},{10,... | collective-permute-start | bytes 786440 | tf_op jit(solution)/shard_map/ppermute | solution.py:252
  8.0 0.5 collective-permute-start.1
  8.5 1.0 %constant_dynamic-slice_fusion.3.own = bf16[128,1024]{1,0:T(8,128)(2,1)S(1)} fusion(bf16[128,4096]{1,0:T(8,128)(2,1)} %param.8, s32[]{:T(128)S(6)} %select_n.34), kind=kLoop, calls=%fused_computation.3 | loop fusion | bytes 524292 | tf_op jit(solution)/shard_map/dynamic_slice | solution.py:276
  9.6 2.9 %collective-permute-done.2.mine2 = bf16[64,1024]{1,0:T(8,128)(2,1)S(1)} collective-permute-done((bf16[64,1024]{1,0:T(8,128)(2,1)S(1)}, bf16[64,1024]{1,0:T(8,128)(2,1)S(1)}, u32[]{:S(2)}, u32[]{:S(2)}) %collective-permute-start.2) | collective-permute-done | bytes 131104 | tf_op jit(solution)/shard_map/ppermute | solution.py:256
  13.4 2.3 %collective-permute-start.7 = (bf16[136,512]{1,0:T(8,128)(2,1)S(1)}, bf16[136,512]{1,0:T(8,128)(2,1)S(1)}, u32[]{:S(2)}, u32[]{:S(2)}) collective-permute-start(bf16[136,512]{1,0:T(8,128)(2,1)S(1)} %project_both.1), channel_id=1, source_target_pairs={{0,24},{8,16},{16,8},{24,0},{1,25},{9,17},{17,9},{25,1},{2,26},{10... | collective-permute-start | bytes 417800 | tf_op jit(solution)/shard_map/ppermute | solution.py:256
  15.7 0.6 %project.1 = (f32[136,512]{1,0:T(8,128)S(1)}, bf16[136,512]{1,0:T(8,128)(2,1)S(1)}, bf16[136,512]{1,0:T(8,128)(2,1)S(1)}) custom-call(bf16[128,1024]{1,0:T(8,128)(2,1)S(1)} %constant_dynamic-slice_fusion.3.own, bf16[64,1024]{1,0:T(8,128)(2,1)S(1)} %collective-permute-done.1.mine1, bf16[64,1024]{1,0:T(8,128)(2,1)S(1)} %collective-permute-done.2.mine2, ...), custom_call_target="tpu_custom_call" | custom-call | tf_op jit(solution)/shard_map/project/pallas_call | solution.py:261
  16.3 0.8 %collective-permute-start.8 = (bf16[136,512]{1,0:T(8,128)(2,1)S(1)}, bf16[136,512]{1,0:T(8,128)(2,1)S(1)}, u32[]{:S(2)}, u32[]{:S(2)}) collective-permute-start(bf16[136,512]{1,0:T(8,128)(2,1)S(1)} %get-tuple-element.29), channel_id=1, source_target_pairs={{0,8},{8,0},{16,24},{24,16},{1,9},{9,1},{17,25},{25,17},{2,10},{10... | collective-permute-start | bytes 417800 | tf_op jit(solution)/shard_map/ppermute | solution.py:256
  17.9 2.8 %collective-permute-done.7.part = bf16[136,512]{1,0:T(8,128)(2,1)S(1)} collective-permute-done((bf16[136,512]{1,0:T(8,128)(2,1)S(1)}, bf16[136,512]{1,0:T(8,128)(2,1)S(1)}, u32[]{:S(2)}, u32[]{:S(2)}) %collective-permute-start.7) | collective-permute-done | bytes 139296 | tf_op jit(solution)/shard_map/ppermute | solution.py:256
  20.8 2.6 %collective-permute-done.8.first = bf16[136,512]{1,0:T(8,128)(2,1)S(1)} collective-permute-done((bf16[136,512]{1,0:T(8,128)(2,1)S(1)}, bf16[136,512]{1,0:T(8,128)(2,1)S(1)}, u32[]{:S(2)}, u32[]{:S(2)}) %collective-permute-start.8) | collective-permute-done | bytes 139296 | tf_op jit(solution)/shard_map/ppermute | solution.py:256
  23.5 0.9 %collective-permute-start.12 = (bf16[128,512]{1,0:T(8,128)(2,1)S(1)}, bf16[128,512]{1,0:T(8,128)(2,1)S(1)}, u32[]{:S(2)}, u32[]{:S(2)}) collective-permute-start(bf16[128,512]{1,0:T(8,128)(2,1)S(1)} %get-tuple-element.31.refs_0_), channel_id=1, source_target_pairs={{0,8},{8,0},{16,24},{24,16},{1,9},{9,1},{17,25},{25,17},{2,10},{10... | collective-permute-start | bytes 393224 | tf_op jit(solution)/shard_map/ppermute | solution.py:256
  24.4 1.4 %collective-permute-start.11 = (bf16[128,512]{1,0:T(8,128)(2,1)S(1)}, bf16[128,512]{1,0:T(8,128)(2,1)S(1)}, u32[]{:S(2)}, u32[]{:S(2)}) collective-permute-start(bf16[128,512]{1,0:T(8,128)(2,1)S(1)} %get-tuple-element.31.refs_0_), channel_id=1, source_target_pairs={{0,16},{8,24},{16,0},{24,8},{1,17},{9,25},{17,1},{25,9},{2,18},{10... | collective-permute-start | bytes 393224 | tf_op jit(solution)/shard_map/ppermute | solution.py:256
  25.9 1.2 %collective-permute-start.10 = (bf16[128,512]{1,0:T(8,128)(2,1)S(1)}, bf16[128,512]{1,0:T(8,128)(2,1)S(1)}, u32[]{:S(2)}, u32[]{:S(2)}) collective-permute-start(bf16[128,512]{1,0:T(8,128)(2,1)S(1)} %get-tuple-element.31.refs_0_), channel_id=1, source_target_pairs={{0,24},{8,16},{16,8},{24,0},{1,25},{9,17},{17,9},{25,1},{2,26},{10... | collective-permute-start | bytes 393224 | tf_op jit(solution)/shard_map/ppermute | solution.py:256
  27.1 0.8 %mask.1 = (f32[512,512]{1,0:T(8,128)S(1)}, f32[16,512]{1,0:T(8,128)S(1)}) custom-call(s32[8]{0:T(128)S(1)} %copy-done.5, s32[4]{0:T(128)S(1)} %copy-done.6), custom_call_target="tpu_custom_call" | custom-call | tf_op jit(solution)/shard_map/mask/pallas_call | solution.py:261
  27.9 2.1 %collective-permute-done.12.refs_3_ = bf16[128,512]{1,0:T(8,128)(2,1)S(1)} collective-permute-done((bf16[128,512]{1,0:T(8,128)(2,1)S(1)}, bf16[128,512]{1,0:T(8,128)(2,1)S(1)}, u32[]{:S(2)}, u32[]{:S(2)}) %collective-permute-start.12) | collective-permute-done | bytes 131104 | tf_op jit(solution)/shard_map/ppermute | solution.py:256
  30.0 1.2 %collective-permute-done.11.refs_2_ = bf16[128,512]{1,0:T(8,128)(2,1)S(1)} collective-permute-done((bf16[128,512]{1,0:T(8,128)(2,1)S(1)}, bf16[128,512]{1,0:T(8,128)(2,1)S(1)}, u32[]{:S(2)}, u32[]{:S(2)}) %collective-permute-start.11) | collective-permute-done | bytes 131104 | tf_op jit(solution)/shard_map/ppermute | solution.py:256
  31.2 1.6 %collective-permute-done.10.refs_1_ = bf16[128,512]{1,0:T(8,128)(2,1)S(1)} collective-permute-done((bf16[128,512]{1,0:T(8,128)(2,1)S(1)}, bf16[128,512]{1,0:T(8,128)(2,1)S(1)}, u32[]{:S(2)}, u32[]{:S(2)}) %collective-permute-start.10) | collective-permute-done | bytes 131104 | tf_op jit(solution)/shard_map/ppermute | solution.py:256
  32.7 0.9 %attend_sent.1.refs_7_ = bf16[264,256]{1,0:T(8,128)(2,1)S(1)} custom-call(bf16[128,512]{1,0:T(8,128)(2,1)S(1)} %get-tuple-element.31.refs_0_, bf16[128,512]{1,0:T(8,128)(2,1)S(1)} %collective-permute-done.10.refs_1_, bf16[128,512]{1,0:T(8,128)(2,1)S(1)} %collective-permute-done.11.refs_2_, bf16[128,512]{1,0:T(8,128)(2,1)S(1)} %collective-permute-done.12.refs_3_, ...), custom_call_target="tpu_custom_call" | custom-call | tf_op jit(solution)/shard_map/attend_sent/pallas_call | solution.py:261
  33.7 1.1 %collective-permute-start.15 = (bf16[264,256]{1,0:T(8,128)(2,1)S(1)}, bf16[264,256]{1,0:T(8,128)(2,1)S(1)}, u32[]{:S(2)}, u32[]{:S(2)}) collective-permute-start(bf16[264,256]{1,0:T(8,128)(2,1)S(1)} %attend_sent.1.refs_7_), channel_id=1, source_target_pairs={{0,2},{1,3},{2,0},{3,1},{4,6},{5,7},{6,4},{7,5},{8,10},{9,11},{10,... | collective-permute-start | bytes 405512 | tf_op jit(solution)/shard_map/ppermute | solution.py:252
  34.7 0.8 %attend_kept.1.refs_0_ = bf16[264,256]{1,0:T(8,128)(2,1)S(1)} custom-call(bf16[128,512]{1,0:T(8,128)(2,1)S(1)} %get-tuple-element.31.refs_0_, bf16[128,512]{1,0:T(8,128)(2,1)S(1)} %collective-permute-done.10.refs_1_, bf16[128,512]{1,0:T(8,128)(2,1)S(1)} %collective-permute-done.11.refs_2_, bf16[128,512]{1,0:T(8,128)(2,1)S(1)} %collective-permute-done.12.refs_3_, ...), custom_call_target="tpu_custom_call" | custom-call | tf_op jit(solution)/shard_map/attend_kept/pallas_call | solution.py:261
  35.5 0.6 collective-permute-start.14
  36.1 2.7 %collective-permute-done.15.refs_2_ = bf16[264,256]{1,0:T(8,128)(2,1)S(1)} collective-permute-done((bf16[264,256]{1,0:T(8,128)(2,1)S(1)}, bf16[264,256]{1,0:T(8,128)(2,1)S(1)}, u32[]{:S(2)}, u32[]{:S(2)}) %collective-permute-start.15) | collective-permute-done | bytes 135200 | tf_op jit(solution)/shard_map/ppermute | solution.py:252
  39.1 1.0 %collective-permute-done.17.heads = bf16[264,256]{1,0:T(8,128)(2,1)S(1)} collective-permute-done((bf16[264,256]{1,0:T(8,128)(2,1)S(1)}, bf16[264,256]{1,0:T(8,128)(2,1)S(1)}, u32[]{:S(2)}, u32[]{:S(2)}) %collective-permute-start.17) | collective-permute-done | bytes 135200 | tf_op jit(solution)/shard_map/ppermute | solution.py:249
  40.3 1.8 %collective-permute-start.18 = (bf16[72,512]{1,0:T(8,128)(2,1)S(1)}, bf16[72,512]{1,0:T(8,128)(2,1)S(1)}, u32[]{:S(2)}, u32[]{:S(2)}) collective-permute-start(bf16[72,512]{1,0:T(8,128)(2,1)S(1)} %get-tuple-element.41), channel_id=1, source_target_pairs={{0,24},{8,16},{16,8},{24,0},{1,25},{9,17},{17,9},{25,1},{2,26},{10... | collective-permute-start | bytes 221192 | tf_op jit(solution)/shard_map/ppermute | solution.py:256
  42.5 1.3 %collective-permute-start.20 = (bf16[72,512]{1,0:T(8,128)(2,1)S(1)}, bf16[72,512]{1,0:T(8,128)(2,1)S(1)}, u32[]{:S(2)}, u32[]{:S(2)}) collective-permute-start(bf16[72,512]{1,0:T(8,128)(2,1)S(1)} %get-tuple-element.43), channel_id=1, source_target_pairs={{0,8},{8,0},{16,24},{24,16},{1,9},{9,1},{17,25},{25,17},{2,10},{10... | collective-permute-start | bytes 221192 | tf_op jit(solution)/shard_map/ppermute | solution.py:256
  43.9 1.8 %collective-permute-done.18.refs_1_ = bf16[72,512]{1,0:T(8,128)(2,1)S(1)} collective-permute-done((bf16[72,512]{1,0:T(8,128)(2,1)S(1)}, bf16[72,512]{1,0:T(8,128)(2,1)S(1)}, u32[]{:S(2)}, u32[]{:S(2)}) %collective-permute-start.18) | collective-permute-done | bytes 73760 | tf_op jit(solution)/shard_map/ppermute | solution.py:256
  45.7 1.5 %collective-permute-done.19.refs_2_ = bf16[72,512]{1,0:T(8,128)(2,1)S(1)} collective-permute-done((bf16[72,512]{1,0:T(8,128)(2,1)S(1)}, bf16[72,512]{1,0:T(8,128)(2,1)S(1)}, u32[]{:S(2)}, u32[]{:S(2)}) %collective-permute-start.19) | collective-permute-done | bytes 73760 | tf_op jit(solution)/shard_map/ppermute | solution.py:256
  47.3 2.6 %collective-permute-start.22 = (bf16[72,512]{1,0:T(8,128)(2,1)S(1)}, bf16[72,512]{1,0:T(8,128)(2,1)S(1)}, u32[]{:S(2)}, u32[]{:S(2)}) collective-permute-start(bf16[72,512]{1,0:T(8,128)(2,1)S(1)} %get-tuple-element.46), channel_id=1, source_target_pairs={{0,4},{1,5},{2,6},{3,7},{4,0},{5,1},{6,2},{7,3},{8,12},{9,13},{10,... | collective-permute-start | bytes 221192 | tf_op jit(solution)/shard_map/ppermute | solution.py:252
  49.9 0.8 %collective-permute-start.21 = (bf16[64,512]{1,0:T(8,128)(2,1)S(1)}, bf16[64,512]{1,0:T(8,128)(2,1)S(1)}, u32[]{:S(2)}, u32[]{:S(2)}) collective-permute-start(bf16[64,512]{1,0:T(8,128)(2,1)S(1)} %get-tuple-element.45), channel_id=1, source_target_pairs={{0,6},{1,7},{2,4},{3,5},{4,2},{5,3},{6,0},{7,1},{8,14},{9,15},{10,... | collective-permute-start | bytes 196616 | tf_op jit(solution)/shard_map/ppermute | solution.py:252
  51.0 5.3 %collective-permute-done.21.refs_1_ = bf16[64,512]{1,0:T(8,128)(2,1)S(1)} collective-permute-done((bf16[64,512]{1,0:T(8,128)(2,1)S(1)}, bf16[64,512]{1,0:T(8,128)(2,1)S(1)}, u32[]{:S(2)}, u32[]{:S(2)}) %collective-permute-start.21) | collective-permute-done | bytes 65568 | tf_op jit(solution)/shard_map/ppermute | solution.py:252
  56.6 0.7 %finish.1 = (bf16[128,512]{1,0:T(8,128)(2,1)}, bf16[4,512]{1,0:T(4,128)(2,1)}) custom-call(bf16[72,512]{1,0:T(8,128)(2,1)S(1)} %get-tuple-element.44.refs_0_, bf16[64,512]{1,0:T(8,128)(2,1)S(1)} %collective-permute-done.21.refs_1_, bf16[72,512]{1,0:T(8,128)(2,1)S(1)} %collective-permute-done.22.refs_2_, bf16[64,512]{1,0:T(8,128)(2,1)S(1)} %collective-permute-done.23.refs_3_), custom_call_target="tpu_custom_call" | custom-call | tf_op jit(solution)/shard_map/finish/pallas_call | solution.py:261
  (45 shorter events, 4.1 us)
Async XLA Ops:
  0.6 12.3 %copy-start = (bf16[4,4096]{1,0:T(4,128)(2,1)S(1)}, bf16[4,4096]{1,0:T(4,128)(2,1)}, u32[]{:S(2)}) copy-start(bf16[4,4096]{1,0:T(4,128)(2,1)} %param.9) | copy-start | bytes 98308
  0.6 5.1 %copy-start.2 = (bf16[256,1024]{1,0:T(8,128)(2,1)S(1)}, bf16[256,1024]{1,0:T(8,128)(2,1)}, u32[]{:S(2)}) copy-start(bf16[256,1024]{1,0:T(8,128)(2,1)} %refs_3_.1) | copy-start | bytes 1572868
  1.8 7.7 %collective-permute-start = (bf16[64,1024]{1,0:T(8,128)(2,1)S(1)}, bf16[64,1024]{1,0:T(8,128)(2,1)S(1)}, u32[]{:S(2)}, u32[]{:S(2)}) collective-permute-start(bf16[64,1024]{1,0:T(8,128)(2,1)S(1)} %get-tuple-element.49), channel_id=1, source_target_pairs={{0,24},{8,16},{16,8},{24,0},{1,25},{9,17},{17,9},{25,1},{2,26},{10... | collective-permute-start | bytes 393224 | tf_op jit(solution)/shard_map/ppermute | solution.py:256
  5.8 7.2 %copy-start.3 = (bf16[1024,128]{1,0:T(8,128)(2,1)S(1)}, bf16[1024,128]{1,0:T(8,128)(2,1)}, u32[]{:S(2)}) copy-start(bf16[1024,128]{1,0:T(8,128)(2,1)} %wk.3) | copy-start | bytes 786436
  5.8 7.2 %copy-start.4 = (bf16[1024,128]{1,0:T(8,128)(2,1)S(1)}, bf16[1024,128]{1,0:T(8,128)(2,1)}, u32[]{:S(2)}) copy-start(bf16[1024,128]{1,0:T(8,128)(2,1)} %wv.3) | copy-start | bytes 786436
  5.8 7.2 %copy-start.1 = (bf16[1024,256]{1,0:T(8,128)(2,1)S(1)}, bf16[1024,256]{1,0:T(8,128)(2,1)}, u32[]{:S(2)}) copy-start(bf16[1024,256]{1,0:T(8,128)(2,1)} %wq.3) | copy-start | bytes 1572868
  5.8 9.9 %collective-permute-start.5 = (bf16[256,512]{1,0:T(8,128)(2,1)S(1)}, bf16[256,512]{1,0:T(8,128)(2,1)S(1)}, u32[]{:S(2)}, u32[]{:S(2)}) collective-permute-start(bf16[256,512]{1,0:T(8,128)(2,1)S(1)} %get-tuple-element.52), channel_id=1, source_target_pairs={{0,2},{1,3},{2,0},{3,1},{4,6},{5,7},{6,4},{7,5},{8,10},{9,11},{10,... | collective-permute-start | bytes 786440 | tf_op jit(solution)/shard_map/ppermute | solution.py:252
  7.5 5.0 %collective-permute-start.2 = (bf16[64,1024]{1,0:T(8,128)(2,1)S(1)}, bf16[64,1024]{1,0:T(8,128)(2,1)S(1)}, u32[]{:S(2)}, u32[]{:S(2)}) collective-permute-start(bf16[64,1024]{1,0:T(8,128)(2,1)S(1)} %get-tuple-element.48), channel_id=1, source_target_pairs={{0,16},{8,24},{16,0},{24,8},{1,17},{9,25},{17,1},{25,9},{2,18},{10... | collective-permute-start | bytes 393224 | tf_op jit(solution)/shard_map/ppermute | solution.py:256
  8.0 5.0 %collective-permute-start.1 = (bf16[64,1024]{1,0:T(8,128)(2,1)S(1)}, bf16[64,1024]{1,0:T(8,128)(2,1)S(1)}, u32[]{:S(2)}, u32[]{:S(2)}) collective-permute-start(bf16[64,1024]{1,0:T(8,128)(2,1)S(1)} %get-tuple-element.50), channel_id=1, source_target_pairs={{0,8},{8,0},{16,24},{24,16},{1,9},{9,1},{17,25},{25,17},{2,10},{10... | collective-permute-start | bytes 393224 | tf_op jit(solution)/shard_map/ppermute | solution.py:256
  9.5 3.5 %collective-permute-start.6 = (bf16[64,1024]{1,0:T(8,128)(2,1)S(1)}, bf16[64,1024]{1,0:T(8,128)(2,1)S(1)}, u32[]{:S(2)}, u32[]{:S(2)}) collective-permute-start(bf16[64,1024]{1,0:T(8,128)(2,1)S(1)} %collective-permute-done.mine), channel_id=1, source_target_pairs={{0,1},{1,0},{2,3},{3,2},{4,5},{5,4},{6,7},{7,6},{8,9},{9,8},{10,11... | collective-permute-start | bytes 393224 | tf_op jit(solution)/shard_map/ppermute | solution.py:249
  12.4 3.3 %collective-permute-start.4 = (bf16[64,1024]{1,0:T(8,128)(2,1)S(1)}, bf16[64,1024]{1,0:T(8,128)(2,1)S(1)}, u32[]{:S(2)}, u32[]{:S(2)}) collective-permute-start(bf16[64,1024]{1,0:T(8,128)(2,1)S(1)} %collective-permute-done.2.mine2), channel_id=1, source_target_pairs={{0,1},{1,0},{2,3},{3,2},{4,5},{5,4},{6,7},{7,6},{8,9},{9,8},{10,11... | collective-permute-start | bytes 393224 | tf_op jit(solution)/shard_map/ppermute | solution.py:249
  12.9 2.8 %collective-permute-start.3 = (bf16[64,1024]{1,0:T(8,128)(2,1)S(1)}, bf16[64,1024]{1,0:T(8,128)(2,1)S(1)}, u32[]{:S(2)}, u32[]{:S(2)}) collective-permute-start(bf16[64,1024]{1,0:T(8,128)(2,1)S(1)} %collective-permute-done.1.mine1), channel_id=1, source_target_pairs={{0,1},{1,0},{2,3},{3,2},{4,5},{5,4},{6,7},{7,6},{8,9},{9,8},{10,11... | collective-permute-start | bytes 393224 | tf_op jit(solution)/shard_map/ppermute | solution.py:249
  13.4 7.4 %collective-permute-start.7 = (bf16[136,512]{1,0:T(8,128)(2,1)S(1)}, bf16[136,512]{1,0:T(8,128)(2,1)S(1)}, u32[]{:S(2)}, u32[]{:S(2)}) collective-permute-start(bf16[136,512]{1,0:T(8,128)(2,1)S(1)} %project_both.1), channel_id=1, source_target_pairs={{0,24},{8,16},{16,8},{24,0},{1,25},{9,17},{17,9},{25,1},{2,26},{10... | collective-permute-start | bytes 417800 | tf_op jit(solution)/shard_map/ppermute | solution.py:256
  16.3 7.1 %collective-permute-start.8 = (bf16[136,512]{1,0:T(8,128)(2,1)S(1)}, bf16[136,512]{1,0:T(8,128)(2,1)S(1)}, u32[]{:S(2)}, u32[]{:S(2)}) collective-permute-start(bf16[136,512]{1,0:T(8,128)(2,1)S(1)} %get-tuple-element.29), channel_id=1, source_target_pairs={{0,8},{8,0},{16,24},{24,16},{1,9},{9,1},{17,25},{25,17},{2,10},{10... | collective-permute-start | bytes 417800 | tf_op jit(solution)/shard_map/ppermute | solution.py:256
  17.1 6.4 %collective-permute-start.9 = (bf16[136,512]{1,0:T(8,128)(2,1)S(1)}, bf16[136,512]{1,0:T(8,128)(2,1)S(1)}, u32[]{:S(2)}, u32[]{:S(2)}) collective-permute-start(bf16[136,512]{1,0:T(8,128)(2,1)S(1)} %get-tuple-element.30), channel_id=1, source_target_pairs={{0,16},{8,24},{16,0},{24,8},{1,17},{9,25},{17,1},{25,9},{2,18},{10... | collective-permute-start | bytes 417800 | tf_op jit(solution)/shard_map/ppermute | solution.py:256
  17.6 10.3 %collective-permute-start.13 = (bf16[256,512]{1,0:T(8,128)(2,1)S(1)}, bf16[256,512]{1,0:T(8,128)(2,1)S(1)}, u32[]{:S(2)}, u32[]{:S(2)}) collective-permute-start(bf16[256,512]{1,0:T(8,128)(2,1)S(1)} %get-tuple-element.37), channel_id=1, source_target_pairs={{0,3},{1,2},{2,1},{3,0},{4,7},{5,6},{6,5},{7,4},{8,11},{9,10},{10,... | collective-permute-start | bytes 786440 | tf_op jit(solution)/shard_map/ppermute | solution.py:305
  23.5 3.6 %copy-start.5 = (s32[8]{0:T(128)S(1)}, s32[8]{0:T(128)}, u32[]{:S(2)}) copy-start(s32[8]{0:T(128)} %block_map.1) | copy-start | bytes 100
  23.5 3.6 %copy-start.6 = (s32[4]{0:T(128)S(1)}, s32[4]{0:T(128)}, u32[]{:S(2)}) copy-start(s32[4]{0:T(128)} %lengths.1) | copy-start | bytes 52
  23.5 6.5 %collective-permute-start.12 = (bf16[128,512]{1,0:T(8,128)(2,1)S(1)}, bf16[128,512]{1,0:T(8,128)(2,1)S(1)}, u32[]{:S(2)}, u32[]{:S(2)}) collective-permute-start(bf16[128,512]{1,0:T(8,128)(2,1)S(1)} %get-tuple-element.31.refs_0_), channel_id=1, source_target_pairs={{0,8},{8,0},{16,24},{24,16},{1,9},{9,1},{17,25},{25,17},{2,10},{10... | collective-permute-start | bytes 393224 | tf_op jit(solution)/shard_map/ppermute | solution.py:256
  24.4 6.7 %collective-permute-start.11 = (bf16[128,512]{1,0:T(8,128)(2,1)S(1)}, bf16[128,512]{1,0:T(8,128)(2,1)S(1)}, u32[]{:S(2)}, u32[]{:S(2)}) collective-permute-start(bf16[128,512]{1,0:T(8,128)(2,1)S(1)} %get-tuple-element.31.refs_0_), channel_id=1, source_target_pairs={{0,16},{8,24},{16,0},{24,8},{1,17},{9,25},{17,1},{25,9},{2,18},{10... | collective-permute-start | bytes 393224 | tf_op jit(solution)/shard_map/ppermute | solution.py:256
  25.9 6.8 %collective-permute-start.10 = (bf16[128,512]{1,0:T(8,128)(2,1)S(1)}, bf16[128,512]{1,0:T(8,128)(2,1)S(1)}, u32[]{:S(2)}, u32[]{:S(2)}) collective-permute-start(bf16[128,512]{1,0:T(8,128)(2,1)S(1)} %get-tuple-element.31.refs_0_), channel_id=1, source_target_pairs={{0,24},{8,16},{16,8},{24,0},{1,25},{9,17},{17,9},{25,1},{2,26},{10... | collective-permute-start | bytes 393224 | tf_op jit(solution)/shard_map/ppermute | solution.py:256
  33.7 5.1 %collective-permute-start.15 = (bf16[264,256]{1,0:T(8,128)(2,1)S(1)}, bf16[264,256]{1,0:T(8,128)(2,1)S(1)}, u32[]{:S(2)}, u32[]{:S(2)}) collective-permute-start(bf16[264,256]{1,0:T(8,128)(2,1)S(1)} %attend_sent.1.refs_7_), channel_id=1, source_target_pairs={{0,2},{1,3},{2,0},{3,1},{4,6},{5,7},{6,4},{7,5},{8,10},{9,11},{10,... | collective-permute-start | bytes 405512 | tf_op jit(solution)/shard_map/ppermute | solution.py:252
  34.7 4.0 %collective-permute-start.16 = (bf16[256,512]{1,0:T(8,128)(2,1)S(1)}, bf16[256,512]{1,0:T(8,128)(2,1)S(1)}, u32[]{:S(2)}, u32[]{:S(2)}) collective-permute-start(bf16[256,512]{1,0:T(8,128)(2,1)S(1)} %get-tuple-element.37), channel_id=1, source_target_pairs={{0,1},{1,0},{2,3},{3,2},{4,5},{5,4},{6,7},{7,6},{8,9},{9,8},{10,11... | collective-permute-start | bytes 786440 | tf_op jit(solution)/shard_map/ppermute | solution.py:249
  35.5 3.3 %collective-permute-start.14 = (bf16[264,256]{1,0:T(8,128)(2,1)S(1)}, bf16[264,256]{1,0:T(8,128)(2,1)S(1)}, u32[]{:S(2)}, u32[]{:S(2)}) collective-permute-start(bf16[264,256]{1,0:T(8,128)(2,1)S(1)} %attend_kept.1.refs_0_), channel_id=1, source_target_pairs={{0,1},{1,0},{2,3},{3,2},{4,5},{5,4},{6,7},{7,6},{8,9},{9,8},{10,11... | collective-permute-start | bytes 405512 | tf_op jit(solution)/shard_map/ppermute | solution.py:249
  38.7 1.4 %collective-permute-start.17 = (bf16[264,256]{1,0:T(8,128)(2,1)S(1)}, bf16[264,256]{1,0:T(8,128)(2,1)S(1)}, u32[]{:S(2)}, u32[]{:S(2)}) collective-permute-start(bf16[264,256]{1,0:T(8,128)(2,1)S(1)} %collective-permute-done.15.refs_2_), channel_id=1, source_target_pairs={{0,1},{1,0},{2,3},{3,2},{4,5},{5,4},{6,7},{7,6},{8,9},{9,8},{10,11... | collective-permute-start | bytes 405512 | tf_op jit(solution)/shard_map/ppermute | solution.py:249
  40.3 5.4 %collective-permute-start.18 = (bf16[72,512]{1,0:T(8,128)(2,1)S(1)}, bf16[72,512]{1,0:T(8,128)(2,1)S(1)}, u32[]{:S(2)}, u32[]{:S(2)}) collective-permute-start(bf16[72,512]{1,0:T(8,128)(2,1)S(1)} %get-tuple-element.41), channel_id=1, source_target_pairs={{0,24},{8,16},{16,8},{24,0},{1,25},{9,17},{17,9},{25,1},{2,26},{10... | collective-permute-start | bytes 221192 | tf_op jit(solution)/shard_map/ppermute | solution.py:256
  42.1 5.0 %collective-permute-start.19 = (bf16[72,512]{1,0:T(8,128)(2,1)S(1)}, bf16[72,512]{1,0:T(8,128)(2,1)S(1)}, u32[]{:S(2)}, u32[]{:S(2)}) collective-permute-start(bf16[72,512]{1,0:T(8,128)(2,1)S(1)} %get-tuple-element.42), channel_id=1, source_target_pairs={{0,16},{8,24},{16,0},{24,8},{1,17},{9,25},{17,1},{25,9},{2,18},{10... | collective-permute-start | bytes 221192 | tf_op jit(solution)/shard_map/ppermute | solution.py:256
  42.5 4.7 %collective-permute-start.20 = (bf16[72,512]{1,0:T(8,128)(2,1)S(1)}, bf16[72,512]{1,0:T(8,128)(2,1)S(1)}, u32[]{:S(2)}, u32[]{:S(2)}) collective-permute-start(bf16[72,512]{1,0:T(8,128)(2,1)S(1)} %get-tuple-element.43), channel_id=1, source_target_pairs={{0,8},{8,0},{16,24},{24,16},{1,9},{9,1},{17,25},{25,17},{2,10},{10... | collective-permute-start | bytes 221192 | tf_op jit(solution)/shard_map/ppermute | solution.py:256
  47.3 9.3 %collective-permute-start.22 = (bf16[72,512]{1,0:T(8,128)(2,1)S(1)}, bf16[72,512]{1,0:T(8,128)(2,1)S(1)}, u32[]{:S(2)}, u32[]{:S(2)}) collective-permute-start(bf16[72,512]{1,0:T(8,128)(2,1)S(1)} %get-tuple-element.46), channel_id=1, source_target_pairs={{0,4},{1,5},{2,6},{3,7},{4,0},{5,1},{6,2},{7,3},{8,12},{9,13},{10,... | collective-permute-start | bytes 221192 | tf_op jit(solution)/shard_map/ppermute | solution.py:252
  49.9 6.4 %collective-permute-start.21 = (bf16[64,512]{1,0:T(8,128)(2,1)S(1)}, bf16[64,512]{1,0:T(8,128)(2,1)S(1)}, u32[]{:S(2)}, u32[]{:S(2)}) collective-permute-start(bf16[64,512]{1,0:T(8,128)(2,1)S(1)} %get-tuple-element.45), channel_id=1, source_target_pairs={{0,6},{1,7},{2,4},{3,5},{4,2},{5,3},{6,0},{7,1},{8,14},{9,15},{10,... | collective-permute-start | bytes 196616 | tf_op jit(solution)/shard_map/ppermute | solution.py:252
  50.7 5.9 %collective-permute-start.23 = (bf16[64,512]{1,0:T(8,128)(2,1)S(1)}, bf16[64,512]{1,0:T(8,128)(2,1)S(1)}, u32[]{:S(2)}, u32[]{:S(2)}) collective-permute-start(bf16[64,512]{1,0:T(8,128)(2,1)S(1)} %get-tuple-element.47), channel_id=1, source_target_pairs={{0,2},{1,3},{2,0},{3,1},{4,6},{5,7},{6,4},{7,5},{8,10},{9,11},{10,... | collective-permute-start | bytes 196616 | tf_op jit(solution)/shard_map/ppermute | solution.py:252

commit v16 on v15

--- a/solution.py
+++ b/solution.py
@@ -13,7 +13,7 @@
 LAST = 1 << 30
 ROW_TILE = 8
 VMEM_BYTES = 48 * 1024 * 1024
-KEYS, OUTPUTS, HEADS = (2, 1, 0), (2, 1, 0), (2, 1, 0)
+KEYS, OUTPUTS, HEADS = (2, 1, 0), (2, 0, 1), (2, 1, 0)
 
 
 def vmem():

time: 57.5 us -> 57 us (level)
  no operation moved by 1% of the time
where the time goes in v16:
time: 57 us; the launch traced here: 56.8 us
  waiting for transfers between devices  25.7 us (45%)
  starting transfers between devices  23.2 us (41%)
  Pallas kernels  4.9 us (9%)
  local copies, waits for them, and re-layouts  2.17 us (4%)
  between operations  0.87 us (2%)
    ppermute x12, waiting for transfers between devices, to_partners(): lax.ppermute(value, 'ctx', [(i, i ^ mask) for i in range(steps)])  17 us
    ppermute x12, starting transfers between devices, to_partners(): lax.ppermute(value, 'ctx', [(i, i ^ mask) for i in range(steps)])  15.7 us
    ppermute x5, waiting for transfers between devices, to_chip(): return lax.ppermute(value, 'tp', [(i, i ^ 2 * step) for i in range(tp)])  7.74 us
    ppermute x5, starting transfers between devices, to_chip(): return lax.ppermute(value, 'tp', [(i, i ^ 2 * step) for i in range(tp)])  6.46 us
    pallas_call x11, Pallas kernels, call(): pl.pallas_call(kernel, out_shape=[jax.ShapeDtypeStruct(shape, kind) for s...  4.9 us
  transfers between devices with their start and end apart: 24, of which 13 were waited for; matrix products, arithmetic and copies ran while one was open for 2% of the time, Pallas kernels for 5%

profile of v16, /device:TPU:0, one launch (start us, length us, event | category | flops | bytes accessed | tf_op | source)
XLA Modules:
  0.0 56.8 jit_solution(4605787182121918074)
XLA Ops:
  0.7 1.1 %fusion = (bf16[64,1024]{1,0:T(8,128)(2,1)S(1)}, bf16[64,1024]{1,0:T(8,128)(2,1)S(1)}, bf16[64,1024]{1,0:T(8,128)(2,1)S(1)}) fusion(bf16[128,4096]{1,0:T(8,128)(2,1)} %param.8, s32[]{:T(128)S(6)} %select_n.32, s32[]{:T(128)S(6)} %select_n.36, s32[]{:T(128)S(6)} %select_n.33, s32[]{:T(128)S(6)} %select_n.35), kind=kLoop, calls=%fused_computation.4 | loop fusion | bytes 786448 | tf_op jit(solution)/shard_map/dynamic_slice | solution.py:273
  1.8 4.0 %collective-permute-start = (bf16[64,1024]{1,0:T(8,128)(2,1)S(1)}, bf16[64,1024]{1,0:T(8,128)(2,1)S(1)}, u32[]{:S(2)}, u32[]{:S(2)}) collective-permute-start(bf16[64,1024]{1,0:T(8,128)(2,1)S(1)} %get-tuple-element.49), channel_id=1, source_target_pairs={{0,24},{8,16},{16,8},{24,0},{1,25},{9,17},{17,9},{25,1},{2,26},{10... | collective-permute-start | bytes 393224 | tf_op jit(solution)/shard_map/ppermute | solution.py:256
  5.8 1.6 %collective-permute-start.5 = (bf16[256,512]{1,0:T(8,128)(2,1)S(1)}, bf16[256,512]{1,0:T(8,128)(2,1)S(1)}, u32[]{:S(2)}, u32[]{:S(2)}) collective-permute-start(bf16[256,512]{1,0:T(8,128)(2,1)S(1)} %get-tuple-element.52), channel_id=1, source_target_pairs={{0,2},{1,3},{2,0},{3,1},{4,6},{5,7},{6,4},{7,5},{8,10},{9,11},{10,... | collective-permute-start | bytes 786440 | tf_op jit(solution)/shard_map/ppermute | solution.py:252
  8.5 1.0 %constant_dynamic-slice_fusion.3.own = bf16[128,1024]{1,0:T(8,128)(2,1)S(1)} fusion(bf16[128,4096]{1,0:T(8,128)(2,1)} %param.8, s32[]{:T(128)S(6)} %select_n.34), kind=kLoop, calls=%fused_computation.3 | loop fusion | bytes 524292 | tf_op jit(solution)/shard_map/dynamic_slice | solution.py:276
  9.6 2.9 %collective-permute-done.2.mine2 = bf16[64,1024]{1,0:T(8,128)(2,1)S(1)} collective-permute-done((bf16[64,1024]{1,0:T(8,128)(2,1)S(1)}, bf16[64,1024]{1,0:T(8,128)(2,1)S(1)}, u32[]{:S(2)}, u32[]{:S(2)}) %collective-permute-start.2) | collective-permute-done | bytes 131104 | tf_op jit(solution)/shard_map/ppermute | solution.py:256
  13.4 2.3 %collective-permute-start.7 = (bf16[136,512]{1,0:T(8,128)(2,1)S(1)}, bf16[136,512]{1,0:T(8,128)(2,1)S(1)}, u32[]{:S(2)}, u32[]{:S(2)}) collective-permute-start(bf16[136,512]{1,0:T(8,128)(2,1)S(1)} %project_both.1), channel_id=1, source_target_pairs={{0,24},{8,16},{16,8},{24,0},{1,25},{9,17},{17,9},{25,1},{2,26},{10... | collective-permute-start | bytes 417800 | tf_op jit(solution)/shard_map/ppermute | solution.py:256
  15.7 0.6 %project.1 = (f32[136,512]{1,0:T(8,128)S(1)}, bf16[136,512]{1,0:T(8,128)(2,1)S(1)}, bf16[136,512]{1,0:T(8,128)(2,1)S(1)}) custom-call(bf16[128,1024]{1,0:T(8,128)(2,1)S(1)} %constant_dynamic-slice_fusion.3.own, bf16[64,1024]{1,0:T(8,128)(2,1)S(1)} %collective-permute-done.1.mine1, bf16[64,1024]{1,0:T(8,128)(2,1)S(1)} %collective-permute-done.2.mine2, ...), custom_call_target="tpu_custom_call" | custom-call | tf_op jit(solution)/shard_map/project/pallas_call | solution.py:261
  16.3 0.8 %collective-permute-start.8 = (bf16[136,512]{1,0:T(8,128)(2,1)S(1)}, bf16[136,512]{1,0:T(8,128)(2,1)S(1)}, u32[]{:S(2)}, u32[]{:S(2)}) collective-permute-start(bf16[136,512]{1,0:T(8,128)(2,1)S(1)} %get-tuple-element.29), channel_id=1, source_target_pairs={{0,8},{8,0},{16,24},{24,16},{1,9},{9,1},{17,25},{25,17},{2,10},{10... | collective-permute-start | bytes 417800 | tf_op jit(solution)/shard_map/ppermute | solution.py:256
  17.9 2.8 %collective-permute-done.7.part = bf16[136,512]{1,0:T(8,128)(2,1)S(1)} collective-permute-done((bf16[136,512]{1,0:T(8,128)(2,1)S(1)}, bf16[136,512]{1,0:T(8,128)(2,1)S(1)}, u32[]{:S(2)}, u32[]{:S(2)}) %collective-permute-start.7) | collective-permute-done | bytes 139296 | tf_op jit(solution)/shard_map/ppermute | solution.py:256
  20.8 2.6 %collective-permute-done.8.first = bf16[136,512]{1,0:T(8,128)(2,1)S(1)} collective-permute-done((bf16[136,512]{1,0:T(8,128)(2,1)S(1)}, bf16[136,512]{1,0:T(8,128)(2,1)S(1)}, u32[]{:S(2)}, u32[]{:S(2)}) %collective-permute-start.8) | collective-permute-done | bytes 139296 | tf_op jit(solution)/shard_map/ppermute | solution.py:256
  23.5 0.9 %collective-permute-start.12 = (bf16[128,512]{1,0:T(8,128)(2,1)S(1)}, bf16[128,512]{1,0:T(8,128)(2,1)S(1)}, u32[]{:S(2)}, u32[]{:S(2)}) collective-permute-start(bf16[128,512]{1,0:T(8,128)(2,1)S(1)} %get-tuple-element.31.refs_0_), channel_id=1, source_target_pairs={{0,8},{8,0},{16,24},{24,16},{1,9},{9,1},{17,25},{25,17},{2,10},{10... | collective-permute-start | bytes 393224 | tf_op jit(solution)/shard_map/ppermute | solution.py:256
  24.4 1.4 %collective-permute-start.11 = (bf16[128,512]{1,0:T(8,128)(2,1)S(1)}, bf16[128,512]{1,0:T(8,128)(2,1)S(1)}, u32[]{:S(2)}, u32[]{:S(2)}) collective-permute-start(bf16[128,512]{1,0:T(8,128)(2,1)S(1)} %get-tuple-element.31.refs_0_), channel_id=1, source_target_pairs={{0,16},{8,24},{16,0},{24,8},{1,17},{9,25},{17,1},{25,9},{2,18},{10... | collective-permute-start | bytes 393224 | tf_op jit(solution)/shard_map/ppermute | solution.py:256
  25.9 1.2 %collective-permute-start.10 = (bf16[128,512]{1,0:T(8,128)(2,1)S(1)}, bf16[128,512]{1,0:T(8,128)(2,1)S(1)}, u32[]{:S(2)}, u32[]{:S(2)}) collective-permute-start(bf16[128,512]{1,0:T(8,128)(2,1)S(1)} %get-tuple-element.31.refs_0_), channel_id=1, source_target_pairs={{0,24},{8,16},{16,8},{24,0},{1,25},{9,17},{17,9},{25,1},{2,26},{10... | collective-permute-start | bytes 393224 | tf_op jit(solution)/shard_map/ppermute | solution.py:256
  27.1 0.8 %mask.1 = (f32[512,512]{1,0:T(8,128)S(1)}, f32[16,512]{1,0:T(8,128)S(1)}) custom-call(s32[8]{0:T(128)S(1)} %copy-done.5, s32[4]{0:T(128)S(1)} %copy-done.6), custom_call_target="tpu_custom_call" | custom-call | tf_op jit(solution)/shard_map/mask/pallas_call | solution.py:261
  27.9 2.1 %collective-permute-done.12.refs_3_ = bf16[128,512]{1,0:T(8,128)(2,1)S(1)} collective-permute-done((bf16[128,512]{1,0:T(8,128)(2,1)S(1)}, bf16[128,512]{1,0:T(8,128)(2,1)S(1)}, u32[]{:S(2)}, u32[]{:S(2)}) %collective-permute-start.12) | collective-permute-done | bytes 131104 | tf_op jit(solution)/shard_map/ppermute | solution.py:256
  30.0 1.2 %collective-permute-done.11.refs_2_ = bf16[128,512]{1,0:T(8,128)(2,1)S(1)} collective-permute-done((bf16[128,512]{1,0:T(8,128)(2,1)S(1)}, bf16[128,512]{1,0:T(8,128)(2,1)S(1)}, u32[]{:S(2)}, u32[]{:S(2)}) %collective-permute-start.11) | collective-permute-done | bytes 131104 | tf_op jit(solution)/shard_map/ppermute | solution.py:256
  31.2 1.6 %collective-permute-done.10.refs_1_ = bf16[128,512]{1,0:T(8,128)(2,1)S(1)} collective-permute-done((bf16[128,512]{1,0:T(8,128)(2,1)S(1)}, bf16[128,512]{1,0:T(8,128)(2,1)S(1)}, u32[]{:S(2)}, u32[]{:S(2)}) %collective-permute-start.10) | collective-permute-done | bytes 131104 | tf_op jit(solution)/shard_map/ppermute | solution.py:256
  32.7 0.9 %attend_sent.1.refs_7_ = bf16[264,256]{1,0:T(8,128)(2,1)S(1)} custom-call(bf16[128,512]{1,0:T(8,128)(2,1)S(1)} %get-tuple-element.31.refs_0_, bf16[128,512]{1,0:T(8,128)(2,1)S(1)} %collective-permute-done.10.refs_1_, bf16[128,512]{1,0:T(8,128)(2,1)S(1)} %collective-permute-done.11.refs_2_, bf16[128,512]{1,0:T(8,128)(2,1)S(1)} %collective-permute-done.12.refs_3_, ...), custom_call_target="tpu_custom_call" | custom-call | tf_op jit(solution)/shard_map/attend_sent/pallas_call | solution.py:261
  33.7 1.1 %collective-permute-start.15 = (bf16[264,256]{1,0:T(8,128)(2,1)S(1)}, bf16[264,256]{1,0:T(8,128)(2,1)S(1)}, u32[]{:S(2)}, u32[]{:S(2)}) collective-permute-start(bf16[264,256]{1,0:T(8,128)(2,1)S(1)} %attend_sent.1.refs_7_), channel_id=1, source_target_pairs={{0,2},{1,3},{2,0},{3,1},{4,6},{5,7},{6,4},{7,5},{8,10},{9,11},{10,... | collective-permute-start | bytes 405512 | tf_op jit(solution)/shard_map/ppermute | solution.py:252
  34.7 0.8 %attend_kept.1.refs_0_ = bf16[264,256]{1,0:T(8,128)(2,1)S(1)} custom-call(bf16[128,512]{1,0:T(8,128)(2,1)S(1)} %get-tuple-element.31.refs_0_, bf16[128,512]{1,0:T(8,128)(2,1)S(1)} %collective-permute-done.10.refs_1_, bf16[128,512]{1,0:T(8,128)(2,1)S(1)} %collective-permute-done.11.refs_2_, bf16[128,512]{1,0:T(8,128)(2,1)S(1)} %collective-permute-done.12.refs_3_, ...), custom_call_target="tpu_custom_call" | custom-call | tf_op jit(solution)/shard_map/attend_kept/pallas_call | solution.py:261
  35.5 0.6 collective-permute-start.14
  36.1 2.7 %collective-permute-done.15.refs_2_ = bf16[264,256]{1,0:T(8,128)(2,1)S(1)} collective-permute-done((bf16[264,256]{1,0:T(8,128)(2,1)S(1)}, bf16[264,256]{1,0:T(8,128)(2,1)S(1)}, u32[]{:S(2)}, u32[]{:S(2)}) %collective-permute-start.15) | collective-permute-done | bytes 135200 | tf_op jit(solution)/shard_map/ppermute | solution.py:252
  39.1 1.0 %collective-permute-done.17.heads = bf16[264,256]{1,0:T(8,128)(2,1)S(1)} collective-permute-done((bf16[264,256]{1,0:T(8,128)(2,1)S(1)}, bf16[264,256]{1,0:T(8,128)(2,1)S(1)}, u32[]{:S(2)}, u32[]{:S(2)}) %collective-permute-start.17) | collective-permute-done | bytes 135200 | tf_op jit(solution)/shard_map/ppermute | solution.py:249
  40.3 1.8 %collective-permute-start.18 = (bf16[72,512]{1,0:T(8,128)(2,1)S(1)}, bf16[72,512]{1,0:T(8,128)(2,1)S(1)}, u32[]{:S(2)}, u32[]{:S(2)}) collective-permute-start(bf16[72,512]{1,0:T(8,128)(2,1)S(1)} %get-tuple-element.41), channel_id=1, source_target_pairs={{0,24},{8,16},{16,8},{24,0},{1,25},{9,17},{17,9},{25,1},{2,26},{10... | collective-permute-start | bytes 221192 | tf_op jit(solution)/shard_map/ppermute | solution.py:256
  42.1 0.6 %collective-permute-start.19 = (bf16[72,512]{1,0:T(8,128)(2,1)S(1)}, bf16[72,512]{1,0:T(8,128)(2,1)S(1)}, u32[]{:S(2)}, u32[]{:S(2)}) collective-permute-start(bf16[72,512]{1,0:T(8,128)(2,1)S(1)} %get-tuple-element.42), channel_id=1, source_target_pairs={{0,8},{8,0},{16,24},{24,16},{1,9},{9,1},{17,25},{25,17},{2,10},{10... | collective-permute-start | bytes 221192 | tf_op jit(solution)/shard_map/ppermute | solution.py:256
  42.8 1.1 %collective-permute-start.20 = (bf16[72,512]{1,0:T(8,128)(2,1)S(1)}, bf16[72,512]{1,0:T(8,128)(2,1)S(1)}, u32[]{:S(2)}, u32[]{:S(2)}) collective-permute-start(bf16[72,512]{1,0:T(8,128)(2,1)S(1)} %get-tuple-element.43), channel_id=1, source_target_pairs={{0,16},{8,24},{16,0},{24,8},{1,17},{9,25},{17,1},{25,9},{2,18},{10... | collective-permute-start | bytes 221192 | tf_op jit(solution)/shard_map/ppermute | solution.py:256
  43.9 2.5 %collective-permute-done.18.refs_1_ = bf16[72,512]{1,0:T(8,128)(2,1)S(1)} collective-permute-done((bf16[72,512]{1,0:T(8,128)(2,1)S(1)}, bf16[72,512]{1,0:T(8,128)(2,1)S(1)}, u32[]{:S(2)}, u32[]{:S(2)}) %collective-permute-start.18) | collective-permute-done | bytes 73760 | tf_op jit(solution)/shard_map/ppermute | solution.py:256
  46.7 0.6 %collective-permute-done.20.refs_3_ = bf16[72,512]{1,0:T(8,128)(2,1)S(1)} collective-permute-done((bf16[72,512]{1,0:T(8,128)(2,1)S(1)}, bf16[72,512]{1,0:T(8,128)(2,1)S(1)}, u32[]{:S(2)}, u32[]{:S(2)}) %collective-permute-start.20) | collective-permute-done | bytes 73760 | tf_op jit(solution)/shard_map/ppermute | solution.py:256
  47.3 2.6 %collective-permute-start.22 = (bf16[72,512]{1,0:T(8,128)(2,1)S(1)}, bf16[72,512]{1,0:T(8,128)(2,1)S(1)}, u32[]{:S(2)}, u32[]{:S(2)}) collective-permute-start(bf16[72,512]{1,0:T(8,128)(2,1)S(1)} %get-tuple-element.46), channel_id=1, source_target_pairs={{0,4},{1,5},{2,6},{3,7},{4,0},{5,1},{6,2},{7,3},{8,12},{9,13},{10,... | collective-permute-start | bytes 221192 | tf_op jit(solution)/shard_map/ppermute | solution.py:252
  50.0 0.9 %collective-permute-start.21 = (bf16[64,512]{1,0:T(8,128)(2,1)S(1)}, bf16[64,512]{1,0:T(8,128)(2,1)S(1)}, u32[]{:S(2)}, u32[]{:S(2)}) collective-permute-start(bf16[64,512]{1,0:T(8,128)(2,1)S(1)} %get-tuple-element.45), channel_id=1, source_target_pairs={{0,6},{1,7},{2,4},{3,5},{4,2},{5,3},{6,0},{7,1},{8,14},{9,15},{10,... | collective-permute-start | bytes 196616 | tf_op jit(solution)/shard_map/ppermute | solution.py:252
  51.1 5.1 %collective-permute-done.21.refs_1_ = bf16[64,512]{1,0:T(8,128)(2,1)S(1)} collective-permute-done((bf16[64,512]{1,0:T(8,128)(2,1)S(1)}, bf16[64,512]{1,0:T(8,128)(2,1)S(1)}, u32[]{:S(2)}, u32[]{:S(2)}) %collective-permute-start.21) | collective-permute-done | bytes 65568 | tf_op jit(solution)/shard_map/ppermute | solution.py:252
  56.1 0.7 %finish.1 = (bf16[128,512]{1,0:T(8,128)(2,1)}, bf16[4,512]{1,0:T(4,128)(2,1)}) custom-call(bf16[72,512]{1,0:T(8,128)(2,1)S(1)} %get-tuple-element.44.refs_0_, bf16[64,512]{1,0:T(8,128)(2,1)S(1)} %collective-permute-done.21.refs_1_, bf16[72,512]{1,0:T(8,128)(2,1)S(1)} %collective-permute-done.22.refs_2_, bf16[64,512]{1,0:T(8,128)(2,1)S(1)} %collective-permute-done.23.refs_3_), custom_call_target="tpu_custom_call" | custom-call | tf_op jit(solution)/shard_map/finish/pallas_call | solution.py:261
  (45 shorter events, 4.2 us)
Async XLA Ops:
  0.6 12.3 %copy-start = (bf16[4,4096]{1,0:T(4,128)(2,1)S(1)}, bf16[4,4096]{1,0:T(4,128)(2,1)}, u32[]{:S(2)}) copy-start(bf16[4,4096]{1,0:T(4,128)(2,1)} %param.9) | copy-start | bytes 98308
  0.6 5.1 %copy-start.2 = (bf16[256,1024]{1,0:T(8,128)(2,1)S(1)}, bf16[256,1024]{1,0:T(8,128)(2,1)}, u32[]{:S(2)}) copy-start(bf16[256,1024]{1,0:T(8,128)(2,1)} %refs_3_.1) | copy-start | bytes 1572868
  1.8 7.7 %collective-permute-start = (bf16[64,1024]{1,0:T(8,128)(2,1)S(1)}, bf16[64,1024]{1,0:T(8,128)(2,1)S(1)}, u32[]{:S(2)}, u32[]{:S(2)}) collective-permute-start(bf16[64,1024]{1,0:T(8,128)(2,1)S(1)} %get-tuple-element.49), channel_id=1, source_target_pairs={{0,24},{8,16},{16,8},{24,0},{1,25},{9,17},{17,9},{25,1},{2,26},{10... | collective-permute-start | bytes 393224 | tf_op jit(solution)/shard_map/ppermute | solution.py:256
  5.8 7.2 %copy-start.3 = (bf16[1024,128]{1,0:T(8,128)(2,1)S(1)}, bf16[1024,128]{1,0:T(8,128)(2,1)}, u32[]{:S(2)}) copy-start(bf16[1024,128]{1,0:T(8,128)(2,1)} %wk.3) | copy-start | bytes 786436
  5.8 7.2 %copy-start.4 = (bf16[1024,128]{1,0:T(8,128)(2,1)S(1)}, bf16[1024,128]{1,0:T(8,128)(2,1)}, u32[]{:S(2)}) copy-start(bf16[1024,128]{1,0:T(8,128)(2,1)} %wv.3) | copy-start | bytes 786436
  5.8 7.2 %copy-start.1 = (bf16[1024,256]{1,0:T(8,128)(2,1)S(1)}, bf16[1024,256]{1,0:T(8,128)(2,1)}, u32[]{:S(2)}) copy-start(bf16[1024,256]{1,0:T(8,128)(2,1)} %wq.3) | copy-start | bytes 1572868
  5.8 9.9 %collective-permute-start.5 = (bf16[256,512]{1,0:T(8,128)(2,1)S(1)}, bf16[256,512]{1,0:T(8,128)(2,1)S(1)}, u32[]{:S(2)}, u32[]{:S(2)}) collective-permute-start(bf16[256,512]{1,0:T(8,128)(2,1)S(1)} %get-tuple-element.52), channel_id=1, source_target_pairs={{0,2},{1,3},{2,0},{3,1},{4,6},{5,7},{6,4},{7,5},{8,10},{9,11},{10,... | collective-permute-start | bytes 786440 | tf_op jit(solution)/shard_map/ppermute | solution.py:252
  7.5 5.0 %collective-permute-start.2 = (bf16[64,1024]{1,0:T(8,128)(2,1)S(1)}, bf16[64,1024]{1,0:T(8,128)(2,1)S(1)}, u32[]{:S(2)}, u32[]{:S(2)}) collective-permute-start(bf16[64,1024]{1,0:T(8,128)(2,1)S(1)} %get-tuple-element.48), channel_id=1, source_target_pairs={{0,16},{8,24},{16,0},{24,8},{1,17},{9,25},{17,1},{25,9},{2,18},{10... | collective-permute-start | bytes 393224 | tf_op jit(solution)/shard_map/ppermute | solution.py:256
  8.0 5.0 %collective-permute-start.1 = (bf16[64,1024]{1,0:T(8,128)(2,1)S(1)}, bf16[64,1024]{1,0:T(8,128)(2,1)S(1)}, u32[]{:S(2)}, u32[]{:S(2)}) collective-permute-start(bf16[64,1024]{1,0:T(8,128)(2,1)S(1)} %get-tuple-element.50), channel_id=1, source_target_pairs={{0,8},{8,0},{16,24},{24,16},{1,9},{9,1},{17,25},{25,17},{2,10},{10... | collective-permute-start | bytes 393224 | tf_op jit(solution)/shard_map/ppermute | solution.py:256
  9.5 3.5 %collective-permute-start.6 = (bf16[64,1024]{1,0:T(8,128)(2,1)S(1)}, bf16[64,1024]{1,0:T(8,128)(2,1)S(1)}, u32[]{:S(2)}, u32[]{:S(2)}) collective-permute-start(bf16[64,1024]{1,0:T(8,128)(2,1)S(1)} %collective-permute-done.mine), channel_id=1, source_target_pairs={{0,1},{1,0},{2,3},{3,2},{4,5},{5,4},{6,7},{7,6},{8,9},{9,8},{10,11... | collective-permute-start | bytes 393224 | tf_op jit(solution)/shard_map/ppermute | solution.py:249
  12.4 3.3 %collective-permute-start.4 = (bf16[64,1024]{1,0:T(8,128)(2,1)S(1)}, bf16[64,1024]{1,0:T(8,128)(2,1)S(1)}, u32[]{:S(2)}, u32[]{:S(2)}) collective-permute-start(bf16[64,1024]{1,0:T(8,128)(2,1)S(1)} %collective-permute-done.2.mine2), channel_id=1, source_target_pairs={{0,1},{1,0},{2,3},{3,2},{4,5},{5,4},{6,7},{7,6},{8,9},{9,8},{10,11... | collective-permute-start | bytes 393224 | tf_op jit(solution)/shard_map/ppermute | solution.py:249
  12.9 2.8 %collective-permute-start.3 = (bf16[64,1024]{1,0:T(8,128)(2,1)S(1)}, bf16[64,1024]{1,0:T(8,128)(2,1)S(1)}, u32[]{:S(2)}, u32[]{:S(2)}) collective-permute-start(bf16[64,1024]{1,0:T(8,128)(2,1)S(1)} %collective-permute-done.1.mine1), channel_id=1, source_target_pairs={{0,1},{1,0},{2,3},{3,2},{4,5},{5,4},{6,7},{7,6},{8,9},{9,8},{10,11... | collective-permute-start | bytes 393224 | tf_op jit(solution)/shard_map/ppermute | solution.py:249
  13.4 7.4 %collective-permute-start.7 = (bf16[136,512]{1,0:T(8,128)(2,1)S(1)}, bf16[136,512]{1,0:T(8,128)(2,1)S(1)}, u32[]{:S(2)}, u32[]{:S(2)}) collective-permute-start(bf16[136,512]{1,0:T(8,128)(2,1)S(1)} %project_both.1), channel_id=1, source_target_pairs={{0,24},{8,16},{16,8},{24,0},{1,25},{9,17},{17,9},{25,1},{2,26},{10... | collective-permute-start | bytes 417800 | tf_op jit(solution)/shard_map/ppermute | solution.py:256
  16.3 7.1 %collective-permute-start.8 = (bf16[136,512]{1,0:T(8,128)(2,1)S(1)}, bf16[136,512]{1,0:T(8,128)(2,1)S(1)}, u32[]{:S(2)}, u32[]{:S(2)}) collective-permute-start(bf16[136,512]{1,0:T(8,128)(2,1)S(1)} %get-tuple-element.29), channel_id=1, source_target_pairs={{0,8},{8,0},{16,24},{24,16},{1,9},{9,1},{17,25},{25,17},{2,10},{10... | collective-permute-start | bytes 417800 | tf_op jit(solution)/shard_map/ppermute | solution.py:256
  17.1 6.4 %collective-permute-start.9 = (bf16[136,512]{1,0:T(8,128)(2,1)S(1)}, bf16[136,512]{1,0:T(8,128)(2,1)S(1)}, u32[]{:S(2)}, u32[]{:S(2)}) collective-permute-start(bf16[136,512]{1,0:T(8,128)(2,1)S(1)} %get-tuple-element.30), channel_id=1, source_target_pairs={{0,16},{8,24},{16,0},{24,8},{1,17},{9,25},{17,1},{25,9},{2,18},{10... | collective-permute-start | bytes 417800 | tf_op jit(solution)/shard_map/ppermute | solution.py:256
  17.6 10.3 %collective-permute-start.13 = (bf16[256,512]{1,0:T(8,128)(2,1)S(1)}, bf16[256,512]{1,0:T(8,128)(2,1)S(1)}, u32[]{:S(2)}, u32[]{:S(2)}) collective-permute-start(bf16[256,512]{1,0:T(8,128)(2,1)S(1)} %get-tuple-element.37), channel_id=1, source_target_pairs={{0,3},{1,2},{2,1},{3,0},{4,7},{5,6},{6,5},{7,4},{8,11},{9,10},{10,... | collective-permute-start | bytes 786440 | tf_op jit(solution)/shard_map/ppermute | solution.py:305
  23.5 3.6 %copy-start.5 = (s32[8]{0:T(128)S(1)}, s32[8]{0:T(128)}, u32[]{:S(2)}) copy-start(s32[8]{0:T(128)} %block_map.1) | copy-start | bytes 100
  23.5 3.6 %copy-start.6 = (s32[4]{0:T(128)S(1)}, s32[4]{0:T(128)}, u32[]{:S(2)}) copy-start(s32[4]{0:T(128)} %lengths.1) | copy-start | bytes 52
  23.5 6.5 %collective-permute-start.12 = (bf16[128,512]{1,0:T(8,128)(2,1)S(1)}, bf16[128,512]{1,0:T(8,128)(2,1)S(1)}, u32[]{:S(2)}, u32[]{:S(2)}) collective-permute-start(bf16[128,512]{1,0:T(8,128)(2,1)S(1)} %get-tuple-element.31.refs_0_), channel_id=1, source_target_pairs={{0,8},{8,0},{16,24},{24,16},{1,9},{9,1},{17,25},{25,17},{2,10},{10... | collective-permute-start | bytes 393224 | tf_op jit(solution)/shard_map/ppermute | solution.py:256
  24.4 6.7 %collective-permute-start.11 = (bf16[128,512]{1,0:T(8,128)(2,1)S(1)}, bf16[128,512]{1,0:T(8,128)(2,1)S(1)}, u32[]{:S(2)}, u32[]{:S(2)}) collective-permute-start(bf16[128,512]{1,0:T(8,128)(2,1)S(1)} %get-tuple-element.31.refs_0_), channel_id=1, source_target_pairs={{0,16},{8,24},{16,0},{24,8},{1,17},{9,25},{17,1},{25,9},{2,18},{10... | collective-permute-start | bytes 393224 | tf_op jit(solution)/shard_map/ppermute | solution.py:256
  25.9 6.8 %collective-permute-start.10 = (bf16[128,512]{1,0:T(8,128)(2,1)S(1)}, bf16[128,512]{1,0:T(8,128)(2,1)S(1)}, u32[]{:S(2)}, u32[]{:S(2)}) collective-permute-start(bf16[128,512]{1,0:T(8,128)(2,1)S(1)} %get-tuple-element.31.refs_0_), channel_id=1, source_target_pairs={{0,24},{8,16},{16,8},{24,0},{1,25},{9,17},{17,9},{25,1},{2,26},{10... | collective-permute-start | bytes 393224 | tf_op jit(solution)/shard_map/ppermute | solution.py:256
  33.7 5.1 %collective-permute-start.15 = (bf16[264,256]{1,0:T(8,128)(2,1)S(1)}, bf16[264,256]{1,0:T(8,128)(2,1)S(1)}, u32[]{:S(2)}, u32[]{:S(2)}) collective-permute-start(bf16[264,256]{1,0:T(8,128)(2,1)S(1)} %attend_sent.1.refs_7_), channel_id=1, source_target_pairs={{0,2},{1,3},{2,0},{3,1},{4,6},{5,7},{6,4},{7,5},{8,10},{9,11},{10,... | collective-permute-start | bytes 405512 | tf_op jit(solution)/shard_map/ppermute | solution.py:252
  34.7 4.0 %collective-permute-start.16 = (bf16[256,512]{1,0:T(8,128)(2,1)S(1)}, bf16[256,512]{1,0:T(8,128)(2,1)S(1)}, u32[]{:S(2)}, u32[]{:S(2)}) collective-permute-start(bf16[256,512]{1,0:T(8,128)(2,1)S(1)} %get-tuple-element.37), channel_id=1, source_target_pairs={{0,1},{1,0},{2,3},{3,2},{4,5},{5,4},{6,7},{7,6},{8,9},{9,8},{10,11... | collective-permute-start | bytes 786440 | tf_op jit(solution)/shard_map/ppermute | solution.py:249
  35.5 3.3 %collective-permute-start.14 = (bf16[264,256]{1,0:T(8,128)(2,1)S(1)}, bf16[264,256]{1,0:T(8,128)(2,1)S(1)}, u32[]{:S(2)}, u32[]{:S(2)}) collective-permute-start(bf16[264,256]{1,0:T(8,128)(2,1)S(1)} %attend_kept.1.refs_0_), channel_id=1, source_target_pairs={{0,1},{1,0},{2,3},{3,2},{4,5},{5,4},{6,7},{7,6},{8,9},{9,8},{10,11... | collective-permute-start | bytes 405512 | tf_op jit(solution)/shard_map/ppermute | solution.py:249
  38.7 1.4 %collective-permute-start.17 = (bf16[264,256]{1,0:T(8,128)(2,1)S(1)}, bf16[264,256]{1,0:T(8,128)(2,1)S(1)}, u32[]{:S(2)}, u32[]{:S(2)}) collective-permute-start(bf16[264,256]{1,0:T(8,128)(2,1)S(1)} %collective-permute-done.15.refs_2_), channel_id=1, source_target_pairs={{0,1},{1,0},{2,3},{3,2},{4,5},{5,4},{6,7},{7,6},{8,9},{9,8},{10,11... | collective-permute-start | bytes 405512 | tf_op jit(solution)/shard_map/ppermute | solution.py:249
  40.3 6.1 %collective-permute-start.18 = (bf16[72,512]{1,0:T(8,128)(2,1)S(1)}, bf16[72,512]{1,0:T(8,128)(2,1)S(1)}, u32[]{:S(2)}, u32[]{:S(2)}) collective-permute-start(bf16[72,512]{1,0:T(8,128)(2,1)S(1)} %get-tuple-element.41), channel_id=1, source_target_pairs={{0,24},{8,16},{16,8},{24,0},{1,25},{9,17},{17,9},{25,1},{2,26},{10... | collective-permute-start | bytes 221192 | tf_op jit(solution)/shard_map/ppermute | solution.py:256
  42.1 4.5 %collective-permute-start.19 = (bf16[72,512]{1,0:T(8,128)(2,1)S(1)}, bf16[72,512]{1,0:T(8,128)(2,1)S(1)}, u32[]{:S(2)}, u32[]{:S(2)}) collective-permute-start(bf16[72,512]{1,0:T(8,128)(2,1)S(1)} %get-tuple-element.42), channel_id=1, source_target_pairs={{0,8},{8,0},{16,24},{24,16},{1,9},{9,1},{17,25},{25,17},{2,10},{10... | collective-permute-start | bytes 221192 | tf_op jit(solution)/shard_map/ppermute | solution.py:256
  42.8 4.5 %collective-permute-start.20 = (bf16[72,512]{1,0:T(8,128)(2,1)S(1)}, bf16[72,512]{1,0:T(8,128)(2,1)S(1)}, u32[]{:S(2)}, u32[]{:S(2)}) collective-permute-start(bf16[72,512]{1,0:T(8,128)(2,1)S(1)} %get-tuple-element.43), channel_id=1, source_target_pairs={{0,16},{8,24},{16,0},{24,8},{1,17},{9,25},{17,1},{25,9},{2,18},{10... | collective-permute-start | bytes 221192 | tf_op jit(solution)/shard_map/ppermute | solution.py:256
  47.3 8.8 %collective-permute-start.22 = (bf16[72,512]{1,0:T(8,128)(2,1)S(1)}, bf16[72,512]{1,0:T(8,128)(2,1)S(1)}, u32[]{:S(2)}, u32[]{:S(2)}) collective-permute-start(bf16[72,512]{1,0:T(8,128)(2,1)S(1)} %get-tuple-element.46), channel_id=1, source_target_pairs={{0,4},{1,5},{2,6},{3,7},{4,0},{5,1},{6,2},{7,3},{8,12},{9,13},{10,... | collective-permute-start | bytes 221192 | tf_op jit(solution)/shard_map/ppermute | solution.py:252
  50.0 6.2 %collective-permute-start.21 = (bf16[64,512]{1,0:T(8,128)(2,1)S(1)}, bf16[64,512]{1,0:T(8,128)(2,1)S(1)}, u32[]{:S(2)}, u32[]{:S(2)}) collective-permute-start(bf16[64,512]{1,0:T(8,128)(2,1)S(1)} %get-tuple-element.45), channel_id=1, source_target_pairs={{0,6},{1,7},{2,4},{3,5},{4,2},{5,3},{6,0},{7,1},{8,14},{9,15},{10,... | collective-permute-start | bytes 196616 | tf_op jit(solution)/shard_map/ppermute | solution.py:252
  50.8 5.3 %collective-permute-start.23 = (bf16[64,512]{1,0:T(8,128)(2,1)S(1)}, bf16[64,512]{1,0:T(8,128)(2,1)S(1)}, u32[]{:S(2)}, u32[]{:S(2)}) collective-permute-start(bf16[64,512]{1,0:T(8,128)(2,1)S(1)} %get-tuple-element.47), channel_id=1, source_target_pairs={{0,2},{1,3},{2,0},{3,1},{4,6},{5,7},{6,4},{7,5},{8,10},{9,11},{10,... | collective-permute-start | bytes 196616 | tf_op jit(solution)/shard_map/ppermute | solution.py:252

commit v17 on v16

--- a/solution.py
+++ b/solution.py
@@ -12,7 +12,7 @@
 FLOOR = -1e30
 LAST = 1 << 30
 ROW_TILE = 8
-VMEM_BYTES = 48 * 1024 * 1024
+VMEM_BYTES = 24 * 1024 * 1024
 KEYS, OUTPUTS, HEADS = (2, 1, 0), (2, 0, 1), (2, 1, 0)
 
 

time: 57 us -> 57 us (level)
  no operation moved by 1% of the time
where the time goes in v17:
time: 57 us; the launch traced here: 56.8 us
  waiting for transfers between devices  25.7 us (45%)
  starting transfers between devices  23.2 us (41%)
  Pallas kernels  4.9 us (9%)
  local copies, waits for them, and re-layouts  2.17 us (4%)
  between operations  0.87 us (2%)
    ppermute x12, waiting for transfers between devices, to_partners(): lax.ppermute(value, 'ctx', [(i, i ^ mask) for i in range(steps)])  17 us
    ppermute x12, starting transfers between devices, to_partners(): lax.ppermute(value, 'ctx', [(i, i ^ mask) for i in range(steps)])  15.7 us
    ppermute x5, waiting for transfers between devices, to_chip(): return lax.ppermute(value, 'tp', [(i, i ^ 2 * step) for i in range(tp)])  7.74 us
    ppermute x5, starting transfers between devices, to_chip(): return lax.ppermute(value, 'tp', [(i, i ^ 2 * step) for i in range(tp)])  6.46 us
    pallas_call x11, Pallas kernels, call(): pl.pallas_call(kernel, out_shape=[jax.ShapeDtypeStruct(shape, kind) for s...  4.9 us
  transfers between devices with their start and end apart: 24, of which 13 were waited for; matrix products, arithmetic and copies ran while one was open for 2% of the time, Pallas kernels for 5%

profile of v17, /device:TPU:0, one launch (start us, length us, event | category | flops | bytes accessed | tf_op | source)
XLA Modules:
  0.0 56.8 jit_solution(8878101747308029806)
XLA Ops:
  0.7 1.1 %fusion = (bf16[64,1024]{1,0:T(8,128)(2,1)S(1)}, bf16[64,1024]{1,0:T(8,128)(2,1)S(1)}, bf16[64,1024]{1,0:T(8,128)(2,1)S(1)}) fusion(bf16[128,4096]{1,0:T(8,128)(2,1)} %param.8, s32[]{:T(128)S(6)} %select_n.32, s32[]{:T(128)S(6)} %select_n.36, s32[]{:T(128)S(6)} %select_n.33, s32[]{:T(128)S(6)} %select_n.35), kind=kLoop, calls=%fused_computation.4 | loop fusion | bytes 786448 | tf_op jit(solution)/shard_map/dynamic_slice | solution.py:273
  1.8 4.0 %collective-permute-start = (bf16[64,1024]{1,0:T(8,128)(2,1)S(1)}, bf16[64,1024]{1,0:T(8,128)(2,1)S(1)}, u32[]{:S(2)}, u32[]{:S(2)}) collective-permute-start(bf16[64,1024]{1,0:T(8,128)(2,1)S(1)} %get-tuple-element.49), channel_id=1, source_target_pairs={{0,24},{8,16},{16,8},{24,0},{1,25},{9,17},{17,9},{25,1},{2,26},{10... | collective-permute-start | bytes 393224 | tf_op jit(solution)/shard_map/ppermute | solution.py:256
  5.8 1.6 %collective-permute-start.5 = (bf16[256,512]{1,0:T(8,128)(2,1)S(1)}, bf16[256,512]{1,0:T(8,128)(2,1)S(1)}, u32[]{:S(2)}, u32[]{:S(2)}) collective-permute-start(bf16[256,512]{1,0:T(8,128)(2,1)S(1)} %get-tuple-element.52), channel_id=1, source_target_pairs={{0,2},{1,3},{2,0},{3,1},{4,6},{5,7},{6,4},{7,5},{8,10},{9,11},{10,... | collective-permute-start | bytes 786440 | tf_op jit(solution)/shard_map/ppermute | solution.py:252
  8.5 1.0 %constant_dynamic-slice_fusion.3.own = bf16[128,1024]{1,0:T(8,128)(2,1)S(1)} fusion(bf16[128,4096]{1,0:T(8,128)(2,1)} %param.8, s32[]{:T(128)S(6)} %select_n.34), kind=kLoop, calls=%fused_computation.3 | loop fusion | bytes 524292 | tf_op jit(solution)/shard_map/dynamic_slice | solution.py:276
  9.6 2.9 %collective-permute-done.2.mine2 = bf16[64,1024]{1,0:T(8,128)(2,1)S(1)} collective-permute-done((bf16[64,1024]{1,0:T(8,128)(2,1)S(1)}, bf16[64,1024]{1,0:T(8,128)(2,1)S(1)}, u32[]{:S(2)}, u32[]{:S(2)}) %collective-permute-start.2) | collective-permute-done | bytes 131104 | tf_op jit(solution)/shard_map/ppermute | solution.py:256
  13.4 2.3 %collective-permute-start.7 = (bf16[136,512]{1,0:T(8,128)(2,1)S(1)}, bf16[136,512]{1,0:T(8,128)(2,1)S(1)}, u32[]{:S(2)}, u32[]{:S(2)}) collective-permute-start(bf16[136,512]{1,0:T(8,128)(2,1)S(1)} %project_both.1), channel_id=1, source_target_pairs={{0,24},{8,16},{16,8},{24,0},{1,25},{9,17},{17,9},{25,1},{2,26},{10... | collective-permute-start | bytes 417800 | tf_op jit(solution)/shard_map/ppermute | solution.py:256
  15.7 0.6 %project.1 = (f32[136,512]{1,0:T(8,128)S(1)}, bf16[136,512]{1,0:T(8,128)(2,1)S(1)}, bf16[136,512]{1,0:T(8,128)(2,1)S(1)}) custom-call(bf16[128,1024]{1,0:T(8,128)(2,1)S(1)} %constant_dynamic-slice_fusion.3.own, bf16[64,1024]{1,0:T(8,128)(2,1)S(1)} %collective-permute-done.1.mine1, bf16[64,1024]{1,0:T(8,128)(2,1)S(1)} %collective-permute-done.2.mine2, ...), custom_call_target="tpu_custom_call" | custom-call | tf_op jit(solution)/shard_map/project/pallas_call | solution.py:261
  16.3 0.8 %collective-permute-start.8 = (bf16[136,512]{1,0:T(8,128)(2,1)S(1)}, bf16[136,512]{1,0:T(8,128)(2,1)S(1)}, u32[]{:S(2)}, u32[]{:S(2)}) collective-permute-start(bf16[136,512]{1,0:T(8,128)(2,1)S(1)} %get-tuple-element.29), channel_id=1, source_target_pairs={{0,8},{8,0},{16,24},{24,16},{1,9},{9,1},{17,25},{25,17},{2,10},{10... | collective-permute-start | bytes 417800 | tf_op jit(solution)/shard_map/ppermute | solution.py:256
  17.9 2.8 %collective-permute-done.7.part = bf16[136,512]{1,0:T(8,128)(2,1)S(1)} collective-permute-done((bf16[136,512]{1,0:T(8,128)(2,1)S(1)}, bf16[136,512]{1,0:T(8,128)(2,1)S(1)}, u32[]{:S(2)}, u32[]{:S(2)}) %collective-permute-start.7) | collective-permute-done | bytes 139296 | tf_op jit(solution)/shard_map/ppermute | solution.py:256
  20.8 2.6 %collective-permute-done.8.first = bf16[136,512]{1,0:T(8,128)(2,1)S(1)} collective-permute-done((bf16[136,512]{1,0:T(8,128)(2,1)S(1)}, bf16[136,512]{1,0:T(8,128)(2,1)S(1)}, u32[]{:S(2)}, u32[]{:S(2)}) %collective-permute-start.8) | collective-permute-done | bytes 139296 | tf_op jit(solution)/shard_map/ppermute | solution.py:256
  23.5 0.9 %collective-permute-start.12 = (bf16[128,512]{1,0:T(8,128)(2,1)S(1)}, bf16[128,512]{1,0:T(8,128)(2,1)S(1)}, u32[]{:S(2)}, u32[]{:S(2)}) collective-permute-start(bf16[128,512]{1,0:T(8,128)(2,1)S(1)} %get-tuple-element.31.refs_0_), channel_id=1, source_target_pairs={{0,8},{8,0},{16,24},{24,16},{1,9},{9,1},{17,25},{25,17},{2,10},{10... | collective-permute-start | bytes 393224 | tf_op jit(solution)/shard_map/ppermute | solution.py:256
  24.4 1.4 %collective-permute-start.11 = (bf16[128,512]{1,0:T(8,128)(2,1)S(1)}, bf16[128,512]{1,0:T(8,128)(2,1)S(1)}, u32[]{:S(2)}, u32[]{:S(2)}) collective-permute-start(bf16[128,512]{1,0:T(8,128)(2,1)S(1)} %get-tuple-element.31.refs_0_), channel_id=1, source_target_pairs={{0,16},{8,24},{16,0},{24,8},{1,17},{9,25},{17,1},{25,9},{2,18},{10... | collective-permute-start | bytes 393224 | tf_op jit(solution)/shard_map/ppermute | solution.py:256
  25.9 1.2 %collective-permute-start.10 = (bf16[128,512]{1,0:T(8,128)(2,1)S(1)}, bf16[128,512]{1,0:T(8,128)(2,1)S(1)}, u32[]{:S(2)}, u32[]{:S(2)}) collective-permute-start(bf16[128,512]{1,0:T(8,128)(2,1)S(1)} %get-tuple-element.31.refs_0_), channel_id=1, source_target_pairs={{0,24},{8,16},{16,8},{24,0},{1,25},{9,17},{17,9},{25,1},{2,26},{10... | collective-permute-start | bytes 393224 | tf_op jit(solution)/shard_map/ppermute | solution.py:256
  27.1 0.8 %mask.1 = (f32[512,512]{1,0:T(8,128)S(1)}, f32[16,512]{1,0:T(8,128)S(1)}) custom-call(s32[8]{0:T(128)S(1)} %copy-done.5, s32[4]{0:T(128)S(1)} %copy-done.6), custom_call_target="tpu_custom_call" | custom-call | tf_op jit(solution)/shard_map/mask/pallas_call | solution.py:261
  27.9 2.1 %collective-permute-done.12.refs_3_ = bf16[128,512]{1,0:T(8,128)(2,1)S(1)} collective-permute-done((bf16[128,512]{1,0:T(8,128)(2,1)S(1)}, bf16[128,512]{1,0:T(8,128)(2,1)S(1)}, u32[]{:S(2)}, u32[]{:S(2)}) %collective-permute-start.12) | collective-permute-done | bytes 131104 | tf_op jit(solution)/shard_map/ppermute | solution.py:256
  30.0 1.2 %collective-permute-done.11.refs_2_ = bf16[128,512]{1,0:T(8,128)(2,1)S(1)} collective-permute-done((bf16[128,512]{1,0:T(8,128)(2,1)S(1)}, bf16[128,512]{1,0:T(8,128)(2,1)S(1)}, u32[]{:S(2)}, u32[]{:S(2)}) %collective-permute-start.11) | collective-permute-done | bytes 131104 | tf_op jit(solution)/shard_map/ppermute | solution.py:256
  31.2 1.6 %collective-permute-done.10.refs_1_ = bf16[128,512]{1,0:T(8,128)(2,1)S(1)} collective-permute-done((bf16[128,512]{1,0:T(8,128)(2,1)S(1)}, bf16[128,512]{1,0:T(8,128)(2,1)S(1)}, u32[]{:S(2)}, u32[]{:S(2)}) %collective-permute-start.10) | collective-permute-done | bytes 131104 | tf_op jit(solution)/shard_map/ppermute | solution.py:256
  32.7 0.9 %attend_sent.1.refs_7_ = bf16[264,256]{1,0:T(8,128)(2,1)S(1)} custom-call(bf16[128,512]{1,0:T(8,128)(2,1)S(1)} %get-tuple-element.31.refs_0_, bf16[128,512]{1,0:T(8,128)(2,1)S(1)} %collective-permute-done.10.refs_1_, bf16[128,512]{1,0:T(8,128)(2,1)S(1)} %collective-permute-done.11.refs_2_, bf16[128,512]{1,0:T(8,128)(2,1)S(1)} %collective-permute-done.12.refs_3_, ...), custom_call_target="tpu_custom_call" | custom-call | tf_op jit(solution)/shard_map/attend_sent/pallas_call | solution.py:261
  33.7 1.1 %collective-permute-start.15 = (bf16[264,256]{1,0:T(8,128)(2,1)S(1)}, bf16[264,256]{1,0:T(8,128)(2,1)S(1)}, u32[]{:S(2)}, u32[]{:S(2)}) collective-permute-start(bf16[264,256]{1,0:T(8,128)(2,1)S(1)} %attend_sent.1.refs_7_), channel_id=1, source_target_pairs={{0,2},{1,3},{2,0},{3,1},{4,6},{5,7},{6,4},{7,5},{8,10},{9,11},{10,... | collective-permute-start | bytes 405512 | tf_op jit(solution)/shard_map/ppermute | solution.py:252
  34.7 0.8 %attend_kept.1.refs_0_ = bf16[264,256]{1,0:T(8,128)(2,1)S(1)} custom-call(bf16[128,512]{1,0:T(8,128)(2,1)S(1)} %get-tuple-element.31.refs_0_, bf16[128,512]{1,0:T(8,128)(2,1)S(1)} %collective-permute-done.10.refs_1_, bf16[128,512]{1,0:T(8,128)(2,1)S(1)} %collective-permute-done.11.refs_2_, bf16[128,512]{1,0:T(8,128)(2,1)S(1)} %collective-permute-done.12.refs_3_, ...), custom_call_target="tpu_custom_call" | custom-call | tf_op jit(solution)/shard_map/attend_kept/pallas_call | solution.py:261
  35.5 0.6 collective-permute-start.14
  36.1 2.7 %collective-permute-done.15.refs_2_ = bf16[264,256]{1,0:T(8,128)(2,1)S(1)} collective-permute-done((bf16[264,256]{1,0:T(8,128)(2,1)S(1)}, bf16[264,256]{1,0:T(8,128)(2,1)S(1)}, u32[]{:S(2)}, u32[]{:S(2)}) %collective-permute-start.15) | collective-permute-done | bytes 135200 | tf_op jit(solution)/shard_map/ppermute | solution.py:252
  39.1 1.0 %collective-permute-done.17.heads = bf16[264,256]{1,0:T(8,128)(2,1)S(1)} collective-permute-done((bf16[264,256]{1,0:T(8,128)(2,1)S(1)}, bf16[264,256]{1,0:T(8,128)(2,1)S(1)}, u32[]{:S(2)}, u32[]{:S(2)}) %collective-permute-start.17) | collective-permute-done | bytes 135200 | tf_op jit(solution)/shard_map/ppermute | solution.py:249
  40.3 1.8 %collective-permute-start.18 = (bf16[72,512]{1,0:T(8,128)(2,1)S(1)}, bf16[72,512]{1,0:T(8,128)(2,1)S(1)}, u32[]{:S(2)}, u32[]{:S(2)}) collective-permute-start(bf16[72,512]{1,0:T(8,128)(2,1)S(1)} %get-tuple-element.41), channel_id=1, source_target_pairs={{0,24},{8,16},{16,8},{24,0},{1,25},{9,17},{17,9},{25,1},{2,26},{10... | collective-permute-start | bytes 221192 | tf_op jit(solution)/shard_map/ppermute | solution.py:256
  42.1 0.6 %collective-permute-start.19 = (bf16[72,512]{1,0:T(8,128)(2,1)S(1)}, bf16[72,512]{1,0:T(8,128)(2,1)S(1)}, u32[]{:S(2)}, u32[]{:S(2)}) collective-permute-start(bf16[72,512]{1,0:T(8,128)(2,1)S(1)} %get-tuple-element.42), channel_id=1, source_target_pairs={{0,8},{8,0},{16,24},{24,16},{1,9},{9,1},{17,25},{25,17},{2,10},{10... | collective-permute-start | bytes 221192 | tf_op jit(solution)/shard_map/ppermute | solution.py:256
  42.8 1.1 %collective-permute-start.20 = (bf16[72,512]{1,0:T(8,128)(2,1)S(1)}, bf16[72,512]{1,0:T(8,128)(2,1)S(1)}, u32[]{:S(2)}, u32[]{:S(2)}) collective-permute-start(bf16[72,512]{1,0:T(8,128)(2,1)S(1)} %get-tuple-element.43), channel_id=1, source_target_pairs={{0,16},{8,24},{16,0},{24,8},{1,17},{9,25},{17,1},{25,9},{2,18},{10... | collective-permute-start | bytes 221192 | tf_op jit(solution)/shard_map/ppermute | solution.py:256
  43.9 2.5 %collective-permute-done.18.refs_1_ = bf16[72,512]{1,0:T(8,128)(2,1)S(1)} collective-permute-done((bf16[72,512]{1,0:T(8,128)(2,1)S(1)}, bf16[72,512]{1,0:T(8,128)(2,1)S(1)}, u32[]{:S(2)}, u32[]{:S(2)}) %collective-permute-start.18) | collective-permute-done | bytes 73760 | tf_op jit(solution)/shard_map/ppermute | solution.py:256
  46.7 0.6 %collective-permute-done.20.refs_3_ = bf16[72,512]{1,0:T(8,128)(2,1)S(1)} collective-permute-done((bf16[72,512]{1,0:T(8,128)(2,1)S(1)}, bf16[72,512]{1,0:T(8,128)(2,1)S(1)}, u32[]{:S(2)}, u32[]{:S(2)}) %collective-permute-start.20) | collective-permute-done | bytes 73760 | tf_op jit(solution)/shard_map/ppermute | solution.py:256
  47.3 2.6 %collective-permute-start.22 = (bf16[72,512]{1,0:T(8,128)(2,1)S(1)}, bf16[72,512]{1,0:T(8,128)(2,1)S(1)}, u32[]{:S(2)}, u32[]{:S(2)}) collective-permute-start(bf16[72,512]{1,0:T(8,128)(2,1)S(1)} %get-tuple-element.46), channel_id=1, source_target_pairs={{0,4},{1,5},{2,6},{3,7},{4,0},{5,1},{6,2},{7,3},{8,12},{9,13},{10,... | collective-permute-start | bytes 221192 | tf_op jit(solution)/shard_map/ppermute | solution.py:252
  50.0 0.9 %collective-permute-start.21 = (bf16[64,512]{1,0:T(8,128)(2,1)S(1)}, bf16[64,512]{1,0:T(8,128)(2,1)S(1)}, u32[]{:S(2)}, u32[]{:S(2)}) collective-permute-start(bf16[64,512]{1,0:T(8,128)(2,1)S(1)} %get-tuple-element.45), channel_id=1, source_target_pairs={{0,6},{1,7},{2,4},{3,5},{4,2},{5,3},{6,0},{7,1},{8,14},{9,15},{10,... | collective-permute-start | bytes 196616 | tf_op jit(solution)/shard_map/ppermute | solution.py:252
  51.1 5.1 %collective-permute-done.21.refs_1_ = bf16[64,512]{1,0:T(8,128)(2,1)S(1)} collective-permute-done((bf16[64,512]{1,0:T(8,128)(2,1)S(1)}, bf16[64,512]{1,0:T(8,128)(2,1)S(1)}, u32[]{:S(2)}, u32[]{:S(2)}) %collective-permute-start.21) | collective-permute-done | bytes 65568 | tf_op jit(solution)/shard_map/ppermute | solution.py:252
  56.1 0.7 %finish.1 = (bf16[128,512]{1,0:T(8,128)(2,1)}, bf16[4,512]{1,0:T(4,128)(2,1)}) custom-call(bf16[72,512]{1,0:T(8,128)(2,1)S(1)} %get-tuple-element.44.refs_0_, bf16[64,512]{1,0:T(8,128)(2,1)S(1)} %collective-permute-done.21.refs_1_, bf16[72,512]{1,0:T(8,128)(2,1)S(1)} %collective-permute-done.22.refs_2_, bf16[64,512]{1,0:T(8,128)(2,1)S(1)} %collective-permute-done.23.refs_3_), custom_call_target="tpu_custom_call" | custom-call | tf_op jit(solution)/shard_map/finish/pallas_call | solution.py:261
  (45 shorter events, 4.2 us)
Async XLA Ops:
  0.6 12.3 %copy-start = (bf16[4,4096]{1,0:T(4,128)(2,1)S(1)}, bf16[4,4096]{1,0:T(4,128)(2,1)}, u32[]{:S(2)}) copy-start(bf16[4,4096]{1,0:T(4,128)(2,1)} %param.9) | copy-start | bytes 98308
  0.6 5.1 %copy-start.2 = (bf16[256,1024]{1,0:T(8,128)(2,1)S(1)}, bf16[256,1024]{1,0:T(8,128)(2,1)}, u32[]{:S(2)}) copy-start(bf16[256,1024]{1,0:T(8,128)(2,1)} %refs_3_.1) | copy-start | bytes 1572868
  1.8 7.7 %collective-permute-start = (bf16[64,1024]{1,0:T(8,128)(2,1)S(1)}, bf16[64,1024]{1,0:T(8,128)(2,1)S(1)}, u32[]{:S(2)}, u32[]{:S(2)}) collective-permute-start(bf16[64,1024]{1,0:T(8,128)(2,1)S(1)} %get-tuple-element.49), channel_id=1, source_target_pairs={{0,24},{8,16},{16,8},{24,0},{1,25},{9,17},{17,9},{25,1},{2,26},{10... | collective-permute-start | bytes 393224 | tf_op jit(solution)/shard_map/ppermute | solution.py:256
  5.8 7.2 %copy-start.3 = (bf16[1024,128]{1,0:T(8,128)(2,1)S(1)}, bf16[1024,128]{1,0:T(8,128)(2,1)}, u32[]{:S(2)}) copy-start(bf16[1024,128]{1,0:T(8,128)(2,1)} %wk.3) | copy-start | bytes 786436
  5.8 7.2 %copy-start.4 = (bf16[1024,128]{1,0:T(8,128)(2,1)S(1)}, bf16[1024,128]{1,0:T(8,128)(2,1)}, u32[]{:S(2)}) copy-start(bf16[1024,128]{1,0:T(8,128)(2,1)} %wv.3) | copy-start | bytes 786436
  5.8 7.2 %copy-start.1 = (bf16[1024,256]{1,0:T(8,128)(2,1)S(1)}, bf16[1024,256]{1,0:T(8,128)(2,1)}, u32[]{:S(2)}) copy-start(bf16[1024,256]{1,0:T(8,128)(2,1)} %wq.3) | copy-start | bytes 1572868
  5.8 9.9 %collective-permute-start.5 = (bf16[256,512]{1,0:T(8,128)(2,1)S(1)}, bf16[256,512]{1,0:T(8,128)(2,1)S(1)}, u32[]{:S(2)}, u32[]{:S(2)}) collective-permute-start(bf16[256,512]{1,0:T(8,128)(2,1)S(1)} %get-tuple-element.52), channel_id=1, source_target_pairs={{0,2},{1,3},{2,0},{3,1},{4,6},{5,7},{6,4},{7,5},{8,10},{9,11},{10,... | collective-permute-start | bytes 786440 | tf_op jit(solution)/shard_map/ppermute | solution.py:252
  7.5 5.0 %collective-permute-start.2 = (bf16[64,1024]{1,0:T(8,128)(2,1)S(1)}, bf16[64,1024]{1,0:T(8,128)(2,1)S(1)}, u32[]{:S(2)}, u32[]{:S(2)}) collective-permute-start(bf16[64,1024]{1,0:T(8,128)(2,1)S(1)} %get-tuple-element.48), channel_id=1, source_target_pairs={{0,16},{8,24},{16,0},{24,8},{1,17},{9,25},{17,1},{25,9},{2,18},{10... | collective-permute-start | bytes 393224 | tf_op jit(solution)/shard_map/ppermute | solution.py:256
  8.0 5.0 %collective-permute-start.1 = (bf16[64,1024]{1,0:T(8,128)(2,1)S(1)}, bf16[64,1024]{1,0:T(8,128)(2,1)S(1)}, u32[]{:S(2)}, u32[]{:S(2)}) collective-permute-start(bf16[64,1024]{1,0:T(8,128)(2,1)S(1)} %get-tuple-element.50), channel_id=1, source_target_pairs={{0,8},{8,0},{16,24},{24,16},{1,9},{9,1},{17,25},{25,17},{2,10},{10... | collective-permute-start | bytes 393224 | tf_op jit(solution)/shard_map/ppermute | solution.py:256
  9.5 3.5 %collective-permute-start.6 = (bf16[64,1024]{1,0:T(8,128)(2,1)S(1)}, bf16[64,1024]{1,0:T(8,128)(2,1)S(1)}, u32[]{:S(2)}, u32[]{:S(2)}) collective-permute-start(bf16[64,1024]{1,0:T(8,128)(2,1)S(1)} %collective-permute-done.mine), channel_id=1, source_target_pairs={{0,1},{1,0},{2,3},{3,2},{4,5},{5,4},{6,7},{7,6},{8,9},{9,8},{10,11... | collective-permute-start | bytes 393224 | tf_op jit(solution)/shard_map/ppermute | solution.py:249
  12.4 3.3 %collective-permute-start.4 = (bf16[64,1024]{1,0:T(8,128)(2,1)S(1)}, bf16[64,1024]{1,0:T(8,128)(2,1)S(1)}, u32[]{:S(2)}, u32[]{:S(2)}) collective-permute-start(bf16[64,1024]{1,0:T(8,128)(2,1)S(1)} %collective-permute-done.2.mine2), channel_id=1, source_target_pairs={{0,1},{1,0},{2,3},{3,2},{4,5},{5,4},{6,7},{7,6},{8,9},{9,8},{10,11... | collective-permute-start | bytes 393224 | tf_op jit(solution)/shard_map/ppermute | solution.py:249
  12.9 2.8 %collective-permute-start.3 = (bf16[64,1024]{1,0:T(8,128)(2,1)S(1)}, bf16[64,1024]{1,0:T(8,128)(2,1)S(1)}, u32[]{:S(2)}, u32[]{:S(2)}) collective-permute-start(bf16[64,1024]{1,0:T(8,128)(2,1)S(1)} %collective-permute-done.1.mine1), channel_id=1, source_target_pairs={{0,1},{1,0},{2,3},{3,2},{4,5},{5,4},{6,7},{7,6},{8,9},{9,8},{10,11... | collective-permute-start | bytes 393224 | tf_op jit(solution)/shard_map/ppermute | solution.py:249
  13.4 7.4 %collective-permute-start.7 = (bf16[136,512]{1,0:T(8,128)(2,1)S(1)}, bf16[136,512]{1,0:T(8,128)(2,1)S(1)}, u32[]{:S(2)}, u32[]{:S(2)}) collective-permute-start(bf16[136,512]{1,0:T(8,128)(2,1)S(1)} %project_both.1), channel_id=1, source_target_pairs={{0,24},{8,16},{16,8},{24,0},{1,25},{9,17},{17,9},{25,1},{2,26},{10... | collective-permute-start | bytes 417800 | tf_op jit(solution)/shard_map/ppermute | solution.py:256
  16.3 7.1 %collective-permute-start.8 = (bf16[136,512]{1,0:T(8,128)(2,1)S(1)}, bf16[136,512]{1,0:T(8,128)(2,1)S(1)}, u32[]{:S(2)}, u32[]{:S(2)}) collective-permute-start(bf16[136,512]{1,0:T(8,128)(2,1)S(1)} %get-tuple-element.29), channel_id=1, source_target_pairs={{0,8},{8,0},{16,24},{24,16},{1,9},{9,1},{17,25},{25,17},{2,10},{10... | collective-permute-start | bytes 417800 | tf_op jit(solution)/shard_map/ppermute | solution.py:256
  17.1 6.4 %collective-permute-start.9 = (bf16[136,512]{1,0:T(8,128)(2,1)S(1)}, bf16[136,512]{1,0:T(8,128)(2,1)S(1)}, u32[]{:S(2)}, u32[]{:S(2)}) collective-permute-start(bf16[136,512]{1,0:T(8,128)(2,1)S(1)} %get-tuple-element.30), channel_id=1, source_target_pairs={{0,16},{8,24},{16,0},{24,8},{1,17},{9,25},{17,1},{25,9},{2,18},{10... | collective-permute-start | bytes 417800 | tf_op jit(solution)/shard_map/ppermute | solution.py:256
  17.6 10.3 %collective-permute-start.13 = (bf16[256,512]{1,0:T(8,128)(2,1)S(1)}, bf16[256,512]{1,0:T(8,128)(2,1)S(1)}, u32[]{:S(2)}, u32[]{:S(2)}) collective-permute-start(bf16[256,512]{1,0:T(8,128)(2,1)S(1)} %get-tuple-element.37), channel_id=1, source_target_pairs={{0,3},{1,2},{2,1},{3,0},{4,7},{5,6},{6,5},{7,4},{8,11},{9,10},{10,... | collective-permute-start | bytes 786440 | tf_op jit(solution)/shard_map/ppermute | solution.py:305
  23.5 3.6 %copy-start.5 = (s32[8]{0:T(128)S(1)}, s32[8]{0:T(128)}, u32[]{:S(2)}) copy-start(s32[8]{0:T(128)} %block_map.1) | copy-start | bytes 100
  23.5 3.6 %copy-start.6 = (s32[4]{0:T(128)S(1)}, s32[4]{0:T(128)}, u32[]{:S(2)}) copy-start(s32[4]{0:T(128)} %lengths.1) | copy-start | bytes 52
  23.5 6.5 %collective-permute-start.12 = (bf16[128,512]{1,0:T(8,128)(2,1)S(1)}, bf16[128,512]{1,0:T(8,128)(2,1)S(1)}, u32[]{:S(2)}, u32[]{:S(2)}) collective-permute-start(bf16[128,512]{1,0:T(8,128)(2,1)S(1)} %get-tuple-element.31.refs_0_), channel_id=1, source_target_pairs={{0,8},{8,0},{16,24},{24,16},{1,9},{9,1},{17,25},{25,17},{2,10},{10... | collective-permute-start | bytes 393224 | tf_op jit(solution)/shard_map/ppermute | solution.py:256
  24.4 6.7 %collective-permute-start.11 = (bf16[128,512]{1,0:T(8,128)(2,1)S(1)}, bf16[128,512]{1,0:T(8,128)(2,1)S(1)}, u32[]{:S(2)}, u32[]{:S(2)}) collective-permute-start(bf16[128,512]{1,0:T(8,128)(2,1)S(1)} %get-tuple-element.31.refs_0_), channel_id=1, source_target_pairs={{0,16},{8,24},{16,0},{24,8},{1,17},{9,25},{17,1},{25,9},{2,18},{10... | collective-permute-start | bytes 393224 | tf_op jit(solution)/shard_map/ppermute | solution.py:256
  25.9 6.8 %collective-permute-start.10 = (bf16[128,512]{1,0:T(8,128)(2,1)S(1)}, bf16[128,512]{1,0:T(8,128)(2,1)S(1)}, u32[]{:S(2)}, u32[]{:S(2)}) collective-permute-start(bf16[128,512]{1,0:T(8,128)(2,1)S(1)} %get-tuple-element.31.refs_0_), channel_id=1, source_target_pairs={{0,24},{8,16},{16,8},{24,0},{1,25},{9,17},{17,9},{25,1},{2,26},{10... | collective-permute-start | bytes 393224 | tf_op jit(solution)/shard_map/ppermute | solution.py:256
  33.7 5.1 %collective-permute-start.15 = (bf16[264,256]{1,0:T(8,128)(2,1)S(1)}, bf16[264,256]{1,0:T(8,128)(2,1)S(1)}, u32[]{:S(2)}, u32[]{:S(2)}) collective-permute-start(bf16[264,256]{1,0:T(8,128)(2,1)S(1)} %attend_sent.1.refs_7_), channel_id=1, source_target_pairs={{0,2},{1,3},{2,0},{3,1},{4,6},{5,7},{6,4},{7,5},{8,10},{9,11},{10,... | collective-permute-start | bytes 405512 | tf_op jit(solution)/shard_map/ppermute | solution.py:252
  34.7 4.0 %collective-permute-start.16 = (bf16[256,512]{1,0:T(8,128)(2,1)S(1)}, bf16[256,512]{1,0:T(8,128)(2,1)S(1)}, u32[]{:S(2)}, u32[]{:S(2)}) collective-permute-start(bf16[256,512]{1,0:T(8,128)(2,1)S(1)} %get-tuple-element.37), channel_id=1, source_target_pairs={{0,1},{1,0},{2,3},{3,2},{4,5},{5,4},{6,7},{7,6},{8,9},{9,8},{10,11... | collective-permute-start | bytes 786440 | tf_op jit(solution)/shard_map/ppermute | solution.py:249
  35.5 3.3 %collective-permute-start.14 = (bf16[264,256]{1,0:T(8,128)(2,1)S(1)}, bf16[264,256]{1,0:T(8,128)(2,1)S(1)}, u32[]{:S(2)}, u32[]{:S(2)}) collective-permute-start(bf16[264,256]{1,0:T(8,128)(2,1)S(1)} %attend_kept.1.refs_0_), channel_id=1, source_target_pairs={{0,1},{1,0},{2,3},{3,2},{4,5},{5,4},{6,7},{7,6},{8,9},{9,8},{10,11... | collective-permute-start | bytes 405512 | tf_op jit(solution)/shard_map/ppermute | solution.py:249
  38.7 1.4 %collective-permute-start.17 = (bf16[264,256]{1,0:T(8,128)(2,1)S(1)}, bf16[264,256]{1,0:T(8,128)(2,1)S(1)}, u32[]{:S(2)}, u32[]{:S(2)}) collective-permute-start(bf16[264,256]{1,0:T(8,128)(2,1)S(1)} %collective-permute-done.15.refs_2_), channel_id=1, source_target_pairs={{0,1},{1,0},{2,3},{3,2},{4,5},{5,4},{6,7},{7,6},{8,9},{9,8},{10,11... | collective-permute-start | bytes 405512 | tf_op jit(solution)/shard_map/ppermute | solution.py:249
  40.3 6.1 %collective-permute-start.18 = (bf16[72,512]{1,0:T(8,128)(2,1)S(1)}, bf16[72,512]{1,0:T(8,128)(2,1)S(1)}, u32[]{:S(2)}, u32[]{:S(2)}) collective-permute-start(bf16[72,512]{1,0:T(8,128)(2,1)S(1)} %get-tuple-element.41), channel_id=1, source_target_pairs={{0,24},{8,16},{16,8},{24,0},{1,25},{9,17},{17,9},{25,1},{2,26},{10... | collective-permute-start | bytes 221192 | tf_op jit(solution)/shard_map/ppermute | solution.py:256
  42.1 4.5 %collective-permute-start.19 = (bf16[72,512]{1,0:T(8,128)(2,1)S(1)}, bf16[72,512]{1,0:T(8,128)(2,1)S(1)}, u32[]{:S(2)}, u32[]{:S(2)}) collective-permute-start(bf16[72,512]{1,0:T(8,128)(2,1)S(1)} %get-tuple-element.42), channel_id=1, source_target_pairs={{0,8},{8,0},{16,24},{24,16},{1,9},{9,1},{17,25},{25,17},{2,10},{10... | collective-permute-start | bytes 221192 | tf_op jit(solution)/shard_map/ppermute | solution.py:256
  42.8 4.5 %collective-permute-start.20 = (bf16[72,512]{1,0:T(8,128)(2,1)S(1)}, bf16[72,512]{1,0:T(8,128)(2,1)S(1)}, u32[]{:S(2)}, u32[]{:S(2)}) collective-permute-start(bf16[72,512]{1,0:T(8,128)(2,1)S(1)} %get-tuple-element.43), channel_id=1, source_target_pairs={{0,16},{8,24},{16,0},{24,8},{1,17},{9,25},{17,1},{25,9},{2,18},{10... | collective-permute-start | bytes 221192 | tf_op jit(solution)/shard_map/ppermute | solution.py:256
  47.3 8.8 %collective-permute-start.22 = (bf16[72,512]{1,0:T(8,128)(2,1)S(1)}, bf16[72,512]{1,0:T(8,128)(2,1)S(1)}, u32[]{:S(2)}, u32[]{:S(2)}) collective-permute-start(bf16[72,512]{1,0:T(8,128)(2,1)S(1)} %get-tuple-element.46), channel_id=1, source_target_pairs={{0,4},{1,5},{2,6},{3,7},{4,0},{5,1},{6,2},{7,3},{8,12},{9,13},{10,... | collective-permute-start | bytes 221192 | tf_op jit(solution)/shard_map/ppermute | solution.py:252
  50.0 6.2 %collective-permute-start.21 = (bf16[64,512]{1,0:T(8,128)(2,1)S(1)}, bf16[64,512]{1,0:T(8,128)(2,1)S(1)}, u32[]{:S(2)}, u32[]{:S(2)}) collective-permute-start(bf16[64,512]{1,0:T(8,128)(2,1)S(1)} %get-tuple-element.45), channel_id=1, source_target_pairs={{0,6},{1,7},{2,4},{3,5},{4,2},{5,3},{6,0},{7,1},{8,14},{9,15},{10,... | collective-permute-start | bytes 196616 | tf_op jit(solution)/shard_map/ppermute | solution.py:252
  50.8 5.3 %collective-permute-start.23 = (bf16[64,512]{1,0:T(8,128)(2,1)S(1)}, bf16[64,512]{1,0:T(8,128)(2,1)S(1)}, u32[]{:S(2)}, u32[]{:S(2)}) collective-permute-start(bf16[64,512]{1,0:T(8,128)(2,1)S(1)} %get-tuple-element.47), channel_id=1, source_target_pairs={{0,2},{1,3},{2,0},{3,1},{4,6},{5,7},{6,4},{7,5},{8,10},{9,11},{10,... | collective-permute-start | bytes 196616 | tf_op jit(solution)/shard_map/ppermute | solution.py:252

commit v18 on v17

--- a/solution.py
+++ b/solution.py
@@ -338,7 +338,7 @@
     sent = attend(True)
     got = to_chip(sent, 1)
     kept = attend(False, sent)
-    w_last, _ = lax.optimization_barrier((w_theirs, held))
+    w_last, _ = lax.optimization_barrier((w_theirs, kept))
     w_other = to_core(w_last)
 
     block = (block_rows + pad, width)

time: 57 us -> 57 us (level)
  no operation moved by 1% of the time
where the time goes in v18:
time: 57 us; the launch traced here: 56.8 us
  waiting for transfers between devices  25.7 us (45%)
  starting transfers between devices  23.2 us (41%)
  Pallas kernels  4.9 us (9%)
  local copies, waits for them, and re-layouts  2.17 us (4%)
  between operations  0.87 us (2%)
    ppermute x12, waiting for transfers between devices, to_partners(): lax.ppermute(value, 'ctx', [(i, i ^ mask) for i in range(steps)])  17 us
    ppermute x12, starting transfers between devices, to_partners(): lax.ppermute(value, 'ctx', [(i, i ^ mask) for i in range(steps)])  15.7 us
    ppermute x5, waiting for transfers between devices, to_chip(): return lax.ppermute(value, 'tp', [(i, i ^ 2 * step) for i in range(tp)])  7.74 us
    ppermute x5, starting transfers between devices, to_chip(): return lax.ppermute(value, 'tp', [(i, i ^ 2 * step) for i in range(tp)])  6.46 us
    pallas_call x11, Pallas kernels, call(): pl.pallas_call(kernel, out_shape=[jax.ShapeDtypeStruct(shape, kind) for s...  4.9 us
  transfers between devices with their start and end apart: 24, of which 13 were waited for; matrix products, arithmetic and copies ran while one was open for 2% of the time, Pallas kernels for 5%

profile of v18, /device:TPU:0, one launch (start us, length us, event | category | flops | bytes accessed | tf_op | source)
XLA Modules:
  0.0 56.8 jit_solution(10791106974267965863)
XLA Ops:
  0.7 1.1 %fusion = (bf16[64,1024]{1,0:T(8,128)(2,1)S(1)}, bf16[64,1024]{1,0:T(8,128)(2,1)S(1)}, bf16[64,1024]{1,0:T(8,128)(2,1)S(1)}) fusion(bf16[128,4096]{1,0:T(8,128)(2,1)} %param.8, s32[]{:T(128)S(6)} %select_n.32, s32[]{:T(128)S(6)} %select_n.36, s32[]{:T(128)S(6)} %select_n.33, s32[]{:T(128)S(6)} %select_n.35), kind=kLoop, calls=%fused_computation.4 | loop fusion | bytes 786448 | tf_op jit(solution)/shard_map/dynamic_slice | solution.py:273
  1.8 4.0 %collective-permute-start = (bf16[64,1024]{1,0:T(8,128)(2,1)S(1)}, bf16[64,1024]{1,0:T(8,128)(2,1)S(1)}, u32[]{:S(2)}, u32[]{:S(2)}) collective-permute-start(bf16[64,1024]{1,0:T(8,128)(2,1)S(1)} %get-tuple-element.49), channel_id=1, source_target_pairs={{0,24},{8,16},{16,8},{24,0},{1,25},{9,17},{17,9},{25,1},{2,26},{10... | collective-permute-start | bytes 393224 | tf_op jit(solution)/shard_map/ppermute | solution.py:256
  5.8 1.6 %collective-permute-start.5 = (bf16[256,512]{1,0:T(8,128)(2,1)S(1)}, bf16[256,512]{1,0:T(8,128)(2,1)S(1)}, u32[]{:S(2)}, u32[]{:S(2)}) collective-permute-start(bf16[256,512]{1,0:T(8,128)(2,1)S(1)} %get-tuple-element.52), channel_id=1, source_target_pairs={{0,2},{1,3},{2,0},{3,1},{4,6},{5,7},{6,4},{7,5},{8,10},{9,11},{10,... | collective-permute-start | bytes 786440 | tf_op jit(solution)/shard_map/ppermute | solution.py:252
  8.0 0.5 collective-permute-start.1
  8.5 1.0 %constant_dynamic-slice_fusion.3.own = bf16[128,1024]{1,0:T(8,128)(2,1)S(1)} fusion(bf16[128,4096]{1,0:T(8,128)(2,1)} %param.8, s32[]{:T(128)S(6)} %select_n.34), kind=kLoop, calls=%fused_computation.3 | loop fusion | bytes 524292 | tf_op jit(solution)/shard_map/dynamic_slice | solution.py:276
  9.6 2.9 %collective-permute-done.2.mine2 = bf16[64,1024]{1,0:T(8,128)(2,1)S(1)} collective-permute-done((bf16[64,1024]{1,0:T(8,128)(2,1)S(1)}, bf16[64,1024]{1,0:T(8,128)(2,1)S(1)}, u32[]{:S(2)}, u32[]{:S(2)}) %collective-permute-start.2) | collective-permute-done | bytes 131104 | tf_op jit(solution)/shard_map/ppermute | solution.py:256
  13.4 2.3 %collective-permute-start.7 = (bf16[136,512]{1,0:T(8,128)(2,1)S(1)}, bf16[136,512]{1,0:T(8,128)(2,1)S(1)}, u32[]{:S(2)}, u32[]{:S(2)}) collective-permute-start(bf16[136,512]{1,0:T(8,128)(2,1)S(1)} %project_both.1), channel_id=1, source_target_pairs={{0,24},{8,16},{16,8},{24,0},{1,25},{9,17},{17,9},{25,1},{2,26},{10... | collective-permute-start | bytes 417800 | tf_op jit(solution)/shard_map/ppermute | solution.py:256
  15.7 0.6 %project.1 = (f32[136,512]{1,0:T(8,128)S(1)}, bf16[136,512]{1,0:T(8,128)(2,1)S(1)}, bf16[136,512]{1,0:T(8,128)(2,1)S(1)}) custom-call(bf16[128,1024]{1,0:T(8,128)(2,1)S(1)} %constant_dynamic-slice_fusion.3.own, bf16[64,1024]{1,0:T(8,128)(2,1)S(1)} %collective-permute-done.1.mine1, bf16[64,1024]{1,0:T(8,128)(2,1)S(1)} %collective-permute-done.2.mine2, ...), custom_call_target="tpu_custom_call" | custom-call | tf_op jit(solution)/shard_map/project/pallas_call | solution.py:261
  16.3 0.8 %collective-permute-start.8 = (bf16[136,512]{1,0:T(8,128)(2,1)S(1)}, bf16[136,512]{1,0:T(8,128)(2,1)S(1)}, u32[]{:S(2)}, u32[]{:S(2)}) collective-permute-start(bf16[136,512]{1,0:T(8,128)(2,1)S(1)} %get-tuple-element.29), channel_id=1, source_target_pairs={{0,8},{8,0},{16,24},{24,16},{1,9},{9,1},{17,25},{25,17},{2,10},{10... | collective-permute-start | bytes 417800 | tf_op jit(solution)/shard_map/ppermute | solution.py:256
  17.9 2.8 %collective-permute-done.7.part = bf16[136,512]{1,0:T(8,128)(2,1)S(1)} collective-permute-done((bf16[136,512]{1,0:T(8,128)(2,1)S(1)}, bf16[136,512]{1,0:T(8,128)(2,1)S(1)}, u32[]{:S(2)}, u32[]{:S(2)}) %collective-permute-start.7) | collective-permute-done | bytes 139296 | tf_op jit(solution)/shard_map/ppermute | solution.py:256
  20.8 2.6 %collective-permute-done.8.first = bf16[136,512]{1,0:T(8,128)(2,1)S(1)} collective-permute-done((bf16[136,512]{1,0:T(8,128)(2,1)S(1)}, bf16[136,512]{1,0:T(8,128)(2,1)S(1)}, u32[]{:S(2)}, u32[]{:S(2)}) %collective-permute-start.8) | collective-permute-done | bytes 139296 | tf_op jit(solution)/shard_map/ppermute | solution.py:256
  23.5 0.9 %collective-permute-start.12 = (bf16[128,512]{1,0:T(8,128)(2,1)S(1)}, bf16[128,512]{1,0:T(8,128)(2,1)S(1)}, u32[]{:S(2)}, u32[]{:S(2)}) collective-permute-start(bf16[128,512]{1,0:T(8,128)(2,1)S(1)} %get-tuple-element.31.refs_0_), channel_id=1, source_target_pairs={{0,8},{8,0},{16,24},{24,16},{1,9},{9,1},{17,25},{25,17},{2,10},{10... | collective-permute-start | bytes 393224 | tf_op jit(solution)/shard_map/ppermute | solution.py:256
  24.4 1.4 %collective-permute-start.11 = (bf16[128,512]{1,0:T(8,128)(2,1)S(1)}, bf16[128,512]{1,0:T(8,128)(2,1)S(1)}, u32[]{:S(2)}, u32[]{:S(2)}) collective-permute-start(bf16[128,512]{1,0:T(8,128)(2,1)S(1)} %get-tuple-element.31.refs_0_), channel_id=1, source_target_pairs={{0,16},{8,24},{16,0},{24,8},{1,17},{9,25},{17,1},{25,9},{2,18},{10... | collective-permute-start | bytes 393224 | tf_op jit(solution)/shard_map/ppermute | solution.py:256
  25.9 1.2 %collective-permute-start.10 = (bf16[128,512]{1,0:T(8,128)(2,1)S(1)}, bf16[128,512]{1,0:T(8,128)(2,1)S(1)}, u32[]{:S(2)}, u32[]{:S(2)}) collective-permute-start(bf16[128,512]{1,0:T(8,128)(2,1)S(1)} %get-tuple-element.31.refs_0_), channel_id=1, source_target_pairs={{0,24},{8,16},{16,8},{24,0},{1,25},{9,17},{17,9},{25,1},{2,26},{10... | collective-permute-start | bytes 393224 | tf_op jit(solution)/shard_map/ppermute | solution.py:256
  27.1 0.8 %mask.1 = (f32[512,512]{1,0:T(8,128)S(1)}, f32[16,512]{1,0:T(8,128)S(1)}) custom-call(s32[8]{0:T(128)S(1)} %copy-done.5, s32[4]{0:T(128)S(1)} %copy-done.6), custom_call_target="tpu_custom_call" | custom-call | tf_op jit(solution)/shard_map/mask/pallas_call | solution.py:261
  27.9 2.1 %collective-permute-done.12.refs_3_ = bf16[128,512]{1,0:T(8,128)(2,1)S(1)} collective-permute-done((bf16[128,512]{1,0:T(8,128)(2,1)S(1)}, bf16[128,512]{1,0:T(8,128)(2,1)S(1)}, u32[]{:S(2)}, u32[]{:S(2)}) %collective-permute-start.12) | collective-permute-done | bytes 131104 | tf_op jit(solution)/shard_map/ppermute | solution.py:256
  30.0 1.2 %collective-permute-done.11.refs_2_ = bf16[128,512]{1,0:T(8,128)(2,1)S(1)} collective-permute-done((bf16[128,512]{1,0:T(8,128)(2,1)S(1)}, bf16[128,512]{1,0:T(8,128)(2,1)S(1)}, u32[]{:S(2)}, u32[]{:S(2)}) %collective-permute-start.11) | collective-permute-done | bytes 131104 | tf_op jit(solution)/shard_map/ppermute | solution.py:256
  31.2 1.6 %collective-permute-done.10.refs_1_ = bf16[128,512]{1,0:T(8,128)(2,1)S(1)} collective-permute-done((bf16[128,512]{1,0:T(8,128)(2,1)S(1)}, bf16[128,512]{1,0:T(8,128)(2,1)S(1)}, u32[]{:S(2)}, u32[]{:S(2)}) %collective-permute-start.10) | collective-permute-done | bytes 131104 | tf_op jit(solution)/shard_map/ppermute | solution.py:256
  32.7 0.9 %attend_sent.1.refs_7_ = bf16[264,256]{1,0:T(8,128)(2,1)S(1)} custom-call(bf16[128,512]{1,0:T(8,128)(2,1)S(1)} %get-tuple-element.31.refs_0_, bf16[128,512]{1,0:T(8,128)(2,1)S(1)} %collective-permute-done.10.refs_1_, bf16[128,512]{1,0:T(8,128)(2,1)S(1)} %collective-permute-done.11.refs_2_, bf16[128,512]{1,0:T(8,128)(2,1)S(1)} %collective-permute-done.12.refs_3_, ...), custom_call_target="tpu_custom_call" | custom-call | tf_op jit(solution)/shard_map/attend_sent/pallas_call | solution.py:261
  33.7 1.1 %collective-permute-start.15 = (bf16[264,256]{1,0:T(8,128)(2,1)S(1)}, bf16[264,256]{1,0:T(8,128)(2,1)S(1)}, u32[]{:S(2)}, u32[]{:S(2)}) collective-permute-start(bf16[264,256]{1,0:T(8,128)(2,1)S(1)} %attend_sent.1.refs_7_), channel_id=1, source_target_pairs={{0,2},{1,3},{2,0},{3,1},{4,6},{5,7},{6,4},{7,5},{8,10},{9,11},{10,... | collective-permute-start | bytes 405512 | tf_op jit(solution)/shard_map/ppermute | solution.py:252
  34.7 0.8 %attend_kept.1.refs_0_ = bf16[264,256]{1,0:T(8,128)(2,1)S(1)} custom-call(bf16[128,512]{1,0:T(8,128)(2,1)S(1)} %get-tuple-element.31.refs_0_, bf16[128,512]{1,0:T(8,128)(2,1)S(1)} %collective-permute-done.10.refs_1_, bf16[128,512]{1,0:T(8,128)(2,1)S(1)} %collective-permute-done.11.refs_2_, bf16[128,512]{1,0:T(8,128)(2,1)S(1)} %collective-permute-done.12.refs_3_, ...), custom_call_target="tpu_custom_call" | custom-call | tf_op jit(solution)/shard_map/attend_kept/pallas_call | solution.py:261
  36.1 2.7 %collective-permute-done.15.refs_2_ = bf16[264,256]{1,0:T(8,128)(2,1)S(1)} collective-permute-done((bf16[264,256]{1,0:T(8,128)(2,1)S(1)}, bf16[264,256]{1,0:T(8,128)(2,1)S(1)}, u32[]{:S(2)}, u32[]{:S(2)}) %collective-permute-start.15) | collective-permute-done | bytes 135200 | tf_op jit(solution)/shard_map/ppermute | solution.py:252
  39.1 1.0 %collective-permute-done.17.heads = bf16[264,256]{1,0:T(8,128)(2,1)S(1)} collective-permute-done((bf16[264,256]{1,0:T(8,128)(2,1)S(1)}, bf16[264,256]{1,0:T(8,128)(2,1)S(1)}, u32[]{:S(2)}, u32[]{:S(2)}) %collective-permute-start.17) | collective-permute-done | bytes 135200 | tf_op jit(solution)/shard_map/ppermute | solution.py:249
  40.3 1.8 %collective-permute-start.18 = (bf16[72,512]{1,0:T(8,128)(2,1)S(1)}, bf16[72,512]{1,0:T(8,128)(2,1)S(1)}, u32[]{:S(2)}, u32[]{:S(2)}) collective-permute-start(bf16[72,512]{1,0:T(8,128)(2,1)S(1)} %get-tuple-element.41), channel_id=1, source_target_pairs={{0,24},{8,16},{16,8},{24,0},{1,25},{9,17},{17,9},{25,1},{2,26},{10... | collective-permute-start | bytes 221192 | tf_op jit(solution)/shard_map/ppermute | solution.py:256
  42.1 0.6 %collective-permute-start.19 = (bf16[72,512]{1,0:T(8,128)(2,1)S(1)}, bf16[72,512]{1,0:T(8,128)(2,1)S(1)}, u32[]{:S(2)}, u32[]{:S(2)}) collective-permute-start(bf16[72,512]{1,0:T(8,128)(2,1)S(1)} %get-tuple-element.42), channel_id=1, source_target_pairs={{0,8},{8,0},{16,24},{24,16},{1,9},{9,1},{17,25},{25,17},{2,10},{10... | collective-permute-start | bytes 221192 | tf_op jit(solution)/shard_map/ppermute | solution.py:256
  42.8 1.1 %collective-permute-start.20 = (bf16[72,512]{1,0:T(8,128)(2,1)S(1)}, bf16[72,512]{1,0:T(8,128)(2,1)S(1)}, u32[]{:S(2)}, u32[]{:S(2)}) collective-permute-start(bf16[72,512]{1,0:T(8,128)(2,1)S(1)} %get-tuple-element.43), channel_id=1, source_target_pairs={{0,16},{8,24},{16,0},{24,8},{1,17},{9,25},{17,1},{25,9},{2,18},{10... | collective-permute-start | bytes 221192 | tf_op jit(solution)/shard_map/ppermute | solution.py:256
  43.9 2.5 %collective-permute-done.18.refs_1_ = bf16[72,512]{1,0:T(8,128)(2,1)S(1)} collective-permute-done((bf16[72,512]{1,0:T(8,128)(2,1)S(1)}, bf16[72,512]{1,0:T(8,128)(2,1)S(1)}, u32[]{:S(2)}, u32[]{:S(2)}) %collective-permute-start.18) | collective-permute-done | bytes 73760 | tf_op jit(solution)/shard_map/ppermute | solution.py:256
  46.7 0.6 %collective-permute-done.20.refs_3_ = bf16[72,512]{1,0:T(8,128)(2,1)S(1)} collective-permute-done((bf16[72,512]{1,0:T(8,128)(2,1)S(1)}, bf16[72,512]{1,0:T(8,128)(2,1)S(1)}, u32[]{:S(2)}, u32[]{:S(2)}) %collective-permute-start.20) | collective-permute-done | bytes 73760 | tf_op jit(solution)/shard_map/ppermute | solution.py:256
  47.3 2.6 %collective-permute-start.22 = (bf16[72,512]{1,0:T(8,128)(2,1)S(1)}, bf16[72,512]{1,0:T(8,128)(2,1)S(1)}, u32[]{:S(2)}, u32[]{:S(2)}) collective-permute-start(bf16[72,512]{1,0:T(8,128)(2,1)S(1)} %get-tuple-element.46), channel_id=1, source_target_pairs={{0,4},{1,5},{2,6},{3,7},{4,0},{5,1},{6,2},{7,3},{8,12},{9,13},{10,... | collective-permute-start | bytes 221192 | tf_op jit(solution)/shard_map/ppermute | solution.py:252
  50.0 0.9 %collective-permute-start.21 = (bf16[64,512]{1,0:T(8,128)(2,1)S(1)}, bf16[64,512]{1,0:T(8,128)(2,1)S(1)}, u32[]{:S(2)}, u32[]{:S(2)}) collective-permute-start(bf16[64,512]{1,0:T(8,128)(2,1)S(1)} %get-tuple-element.45), channel_id=1, source_target_pairs={{0,6},{1,7},{2,4},{3,5},{4,2},{5,3},{6,0},{7,1},{8,14},{9,15},{10,... | collective-permute-start | bytes 196616 | tf_op jit(solution)/shard_map/ppermute | solution.py:252
  51.1 5.1 %collective-permute-done.21.refs_1_ = bf16[64,512]{1,0:T(8,128)(2,1)S(1)} collective-permute-done((bf16[64,512]{1,0:T(8,128)(2,1)S(1)}, bf16[64,512]{1,0:T(8,128)(2,1)S(1)}, u32[]{:S(2)}, u32[]{:S(2)}) %collective-permute-start.21) | collective-permute-done | bytes 65568 | tf_op jit(solution)/shard_map/ppermute | solution.py:252
  56.1 0.7 %finish.1 = (bf16[128,512]{1,0:T(8,128)(2,1)}, bf16[4,512]{1,0:T(4,128)(2,1)}) custom-call(bf16[72,512]{1,0:T(8,128)(2,1)S(1)} %get-tuple-element.44.refs_0_, bf16[64,512]{1,0:T(8,128)(2,1)S(1)} %collective-permute-done.21.refs_1_, bf16[72,512]{1,0:T(8,128)(2,1)S(1)} %collective-permute-done.22.refs_2_, bf16[64,512]{1,0:T(8,128)(2,1)S(1)} %collective-permute-done.23.refs_3_), custom_call_target="tpu_custom_call" | custom-call | tf_op jit(solution)/shard_map/finish/pallas_call | solution.py:261
  (45 shorter events, 4.2 us)
Async XLA Ops:
  0.6 12.3 %copy-start = (bf16[4,4096]{1,0:T(4,128)(2,1)S(1)}, bf16[4,4096]{1,0:T(4,128)(2,1)}, u32[]{:S(2)}) copy-start(bf16[4,4096]{1,0:T(4,128)(2,1)} %param.9) | copy-start | bytes 98308
  0.6 5.1 %copy-start.2 = (bf16[256,1024]{1,0:T(8,128)(2,1)S(1)}, bf16[256,1024]{1,0:T(8,128)(2,1)}, u32[]{:S(2)}) copy-start(bf16[256,1024]{1,0:T(8,128)(2,1)} %refs_3_.1) | copy-start | bytes 1572868
  1.8 7.7 %collective-permute-start = (bf16[64,1024]{1,0:T(8,128)(2,1)S(1)}, bf16[64,1024]{1,0:T(8,128)(2,1)S(1)}, u32[]{:S(2)}, u32[]{:S(2)}) collective-permute-start(bf16[64,1024]{1,0:T(8,128)(2,1)S(1)} %get-tuple-element.49), channel_id=1, source_target_pairs={{0,24},{8,16},{16,8},{24,0},{1,25},{9,17},{17,9},{25,1},{2,26},{10... | collective-permute-start | bytes 393224 | tf_op jit(solution)/shard_map/ppermute | solution.py:256
  5.8 7.2 %copy-start.3 = (bf16[1024,128]{1,0:T(8,128)(2,1)S(1)}, bf16[1024,128]{1,0:T(8,128)(2,1)}, u32[]{:S(2)}) copy-start(bf16[1024,128]{1,0:T(8,128)(2,1)} %wk.3) | copy-start | bytes 786436
  5.8 7.2 %copy-start.4 = (bf16[1024,128]{1,0:T(8,128)(2,1)S(1)}, bf16[1024,128]{1,0:T(8,128)(2,1)}, u32[]{:S(2)}) copy-start(bf16[1024,128]{1,0:T(8,128)(2,1)} %wv.3) | copy-start | bytes 786436
  5.8 7.2 %copy-start.1 = (bf16[1024,256]{1,0:T(8,128)(2,1)S(1)}, bf16[1024,256]{1,0:T(8,128)(2,1)}, u32[]{:S(2)}) copy-start(bf16[1024,256]{1,0:T(8,128)(2,1)} %wq.3) | copy-start | bytes 1572868
  5.8 9.9 %collective-permute-start.5 = (bf16[256,512]{1,0:T(8,128)(2,1)S(1)}, bf16[256,512]{1,0:T(8,128)(2,1)S(1)}, u32[]{:S(2)}, u32[]{:S(2)}) collective-permute-start(bf16[256,512]{1,0:T(8,128)(2,1)S(1)} %get-tuple-element.52), channel_id=1, source_target_pairs={{0,2},{1,3},{2,0},{3,1},{4,6},{5,7},{6,4},{7,5},{8,10},{9,11},{10,... | collective-permute-start | bytes 786440 | tf_op jit(solution)/shard_map/ppermute | solution.py:252
  7.5 5.0 %collective-permute-start.2 = (bf16[64,1024]{1,0:T(8,128)(2,1)S(1)}, bf16[64,1024]{1,0:T(8,128)(2,1)S(1)}, u32[]{:S(2)}, u32[]{:S(2)}) collective-permute-start(bf16[64,1024]{1,0:T(8,128)(2,1)S(1)} %get-tuple-element.48), channel_id=1, source_target_pairs={{0,16},{8,24},{16,0},{24,8},{1,17},{9,25},{17,1},{25,9},{2,18},{10... | collective-permute-start | bytes 393224 | tf_op jit(solution)/shard_map/ppermute | solution.py:256
  8.0 5.0 %collective-permute-start.1 = (bf16[64,1024]{1,0:T(8,128)(2,1)S(1)}, bf16[64,1024]{1,0:T(8,128)(2,1)S(1)}, u32[]{:S(2)}, u32[]{:S(2)}) collective-permute-start(bf16[64,1024]{1,0:T(8,128)(2,1)S(1)} %get-tuple-element.50), channel_id=1, source_target_pairs={{0,8},{8,0},{16,24},{24,16},{1,9},{9,1},{17,25},{25,17},{2,10},{10... | collective-permute-start | bytes 393224 | tf_op jit(solution)/shard_map/ppermute | solution.py:256
  9.5 3.5 %collective-permute-start.6 = (bf16[64,1024]{1,0:T(8,128)(2,1)S(1)}, bf16[64,1024]{1,0:T(8,128)(2,1)S(1)}, u32[]{:S(2)}, u32[]{:S(2)}) collective-permute-start(bf16[64,1024]{1,0:T(8,128)(2,1)S(1)} %collective-permute-done.mine), channel_id=1, source_target_pairs={{0,1},{1,0},{2,3},{3,2},{4,5},{5,4},{6,7},{7,6},{8,9},{9,8},{10,11... | collective-permute-start | bytes 393224 | tf_op jit(solution)/shard_map/ppermute | solution.py:249
  12.4 3.3 %collective-permute-start.4 = (bf16[64,1024]{1,0:T(8,128)(2,1)S(1)}, bf16[64,1024]{1,0:T(8,128)(2,1)S(1)}, u32[]{:S(2)}, u32[]{:S(2)}) collective-permute-start(bf16[64,1024]{1,0:T(8,128)(2,1)S(1)} %collective-permute-done.2.mine2), channel_id=1, source_target_pairs={{0,1},{1,0},{2,3},{3,2},{4,5},{5,4},{6,7},{7,6},{8,9},{9,8},{10,11... | collective-permute-start | bytes 393224 | tf_op jit(solution)/shard_map/ppermute | solution.py:249
  12.9 2.8 %collective-permute-start.3 = (bf16[64,1024]{1,0:T(8,128)(2,1)S(1)}, bf16[64,1024]{1,0:T(8,128)(2,1)S(1)}, u32[]{:S(2)}, u32[]{:S(2)}) collective-permute-start(bf16[64,1024]{1,0:T(8,128)(2,1)S(1)} %collective-permute-done.1.mine1), channel_id=1, source_target_pairs={{0,1},{1,0},{2,3},{3,2},{4,5},{5,4},{6,7},{7,6},{8,9},{9,8},{10,11... | collective-permute-start | bytes 393224 | tf_op jit(solution)/shard_map/ppermute | solution.py:249
  13.4 7.4 %collective-permute-start.7 = (bf16[136,512]{1,0:T(8,128)(2,1)S(1)}, bf16[136,512]{1,0:T(8,128)(2,1)S(1)}, u32[]{:S(2)}, u32[]{:S(2)}) collective-permute-start(bf16[136,512]{1,0:T(8,128)(2,1)S(1)} %project_both.1), channel_id=1, source_target_pairs={{0,24},{8,16},{16,8},{24,0},{1,25},{9,17},{17,9},{25,1},{2,26},{10... | collective-permute-start | bytes 417800 | tf_op jit(solution)/shard_map/ppermute | solution.py:256
  16.3 7.1 %collective-permute-start.8 = (bf16[136,512]{1,0:T(8,128)(2,1)S(1)}, bf16[136,512]{1,0:T(8,128)(2,1)S(1)}, u32[]{:S(2)}, u32[]{:S(2)}) collective-permute-start(bf16[136,512]{1,0:T(8,128)(2,1)S(1)} %get-tuple-element.29), channel_id=1, source_target_pairs={{0,8},{8,0},{16,24},{24,16},{1,9},{9,1},{17,25},{25,17},{2,10},{10... | collective-permute-start | bytes 417800 | tf_op jit(solution)/shard_map/ppermute | solution.py:256
  17.1 6.4 %collective-permute-start.9 = (bf16[136,512]{1,0:T(8,128)(2,1)S(1)}, bf16[136,512]{1,0:T(8,128)(2,1)S(1)}, u32[]{:S(2)}, u32[]{:S(2)}) collective-permute-start(bf16[136,512]{1,0:T(8,128)(2,1)S(1)} %get-tuple-element.30), channel_id=1, source_target_pairs={{0,16},{8,24},{16,0},{24,8},{1,17},{9,25},{17,1},{25,9},{2,18},{10... | collective-permute-start | bytes 417800 | tf_op jit(solution)/shard_map/ppermute | solution.py:256
  17.6 10.3 %collective-permute-start.13 = (bf16[256,512]{1,0:T(8,128)(2,1)S(1)}, bf16[256,512]{1,0:T(8,128)(2,1)S(1)}, u32[]{:S(2)}, u32[]{:S(2)}) collective-permute-start(bf16[256,512]{1,0:T(8,128)(2,1)S(1)} %get-tuple-element.37), channel_id=1, source_target_pairs={{0,3},{1,2},{2,1},{3,0},{4,7},{5,6},{6,5},{7,4},{8,11},{9,10},{10,... | collective-permute-start | bytes 786440 | tf_op jit(solution)/shard_map/ppermute | solution.py:305
  23.5 3.6 %copy-start.5 = (s32[8]{0:T(128)S(1)}, s32[8]{0:T(128)}, u32[]{:S(2)}) copy-start(s32[8]{0:T(128)} %block_map.1) | copy-start | bytes 100
  23.5 3.6 %copy-start.6 = (s32[4]{0:T(128)S(1)}, s32[4]{0:T(128)}, u32[]{:S(2)}) copy-start(s32[4]{0:T(128)} %lengths.1) | copy-start | bytes 52
  23.5 6.5 %collective-permute-start.12 = (bf16[128,512]{1,0:T(8,128)(2,1)S(1)}, bf16[128,512]{1,0:T(8,128)(2,1)S(1)}, u32[]{:S(2)}, u32[]{:S(2)}) collective-permute-start(bf16[128,512]{1,0:T(8,128)(2,1)S(1)} %get-tuple-element.31.refs_0_), channel_id=1, source_target_pairs={{0,8},{8,0},{16,24},{24,16},{1,9},{9,1},{17,25},{25,17},{2,10},{10... | collective-permute-start | bytes 393224 | tf_op jit(solution)/shard_map/ppermute | solution.py:256
  24.4 6.7 %collective-permute-start.11 = (bf16[128,512]{1,0:T(8,128)(2,1)S(1)}, bf16[128,512]{1,0:T(8,128)(2,1)S(1)}, u32[]{:S(2)}, u32[]{:S(2)}) collective-permute-start(bf16[128,512]{1,0:T(8,128)(2,1)S(1)} %get-tuple-element.31.refs_0_), channel_id=1, source_target_pairs={{0,16},{8,24},{16,0},{24,8},{1,17},{9,25},{17,1},{25,9},{2,18},{10... | collective-permute-start | bytes 393224 | tf_op jit(solution)/shard_map/ppermute | solution.py:256
  25.9 6.8 %collective-permute-start.10 = (bf16[128,512]{1,0:T(8,128)(2,1)S(1)}, bf16[128,512]{1,0:T(8,128)(2,1)S(1)}, u32[]{:S(2)}, u32[]{:S(2)}) collective-permute-start(bf16[128,512]{1,0:T(8,128)(2,1)S(1)} %get-tuple-element.31.refs_0_), channel_id=1, source_target_pairs={{0,24},{8,16},{16,8},{24,0},{1,25},{9,17},{17,9},{25,1},{2,26},{10... | collective-permute-start | bytes 393224 | tf_op jit(solution)/shard_map/ppermute | solution.py:256
  33.7 5.1 %collective-permute-start.15 = (bf16[264,256]{1,0:T(8,128)(2,1)S(1)}, bf16[264,256]{1,0:T(8,128)(2,1)S(1)}, u32[]{:S(2)}, u32[]{:S(2)}) collective-permute-start(bf16[264,256]{1,0:T(8,128)(2,1)S(1)} %attend_sent.1.refs_7_), channel_id=1, source_target_pairs={{0,2},{1,3},{2,0},{3,1},{4,6},{5,7},{6,4},{7,5},{8,10},{9,11},{10,... | collective-permute-start | bytes 405512 | tf_op jit(solution)/shard_map/ppermute | solution.py:252
  35.5 3.3 %collective-permute-start.16 = (bf16[256,512]{1,0:T(8,128)(2,1)S(1)}, bf16[256,512]{1,0:T(8,128)(2,1)S(1)}, u32[]{:S(2)}, u32[]{:S(2)}) collective-permute-start(bf16[256,512]{1,0:T(8,128)(2,1)S(1)} %get-tuple-element.37), channel_id=1, source_target_pairs={{0,1},{1,0},{2,3},{3,2},{4,5},{5,4},{6,7},{7,6},{8,9},{9,8},{10,11... | collective-permute-start | bytes 786440 | tf_op jit(solution)/shard_map/ppermute | solution.py:249
  35.6 3.2 %collective-permute-start.14 = (bf16[264,256]{1,0:T(8,128)(2,1)S(1)}, bf16[264,256]{1,0:T(8,128)(2,1)S(1)}, u32[]{:S(2)}, u32[]{:S(2)}) collective-permute-start(bf16[264,256]{1,0:T(8,128)(2,1)S(1)} %attend_kept.1.refs_0_), channel_id=1, source_target_pairs={{0,1},{1,0},{2,3},{3,2},{4,5},{5,4},{6,7},{7,6},{8,9},{9,8},{10,11... | collective-permute-start | bytes 405512 | tf_op jit(solution)/shard_map/ppermute | solution.py:249
  38.7 1.4 %collective-permute-start.17 = (bf16[264,256]{1,0:T(8,128)(2,1)S(1)}, bf16[264,256]{1,0:T(8,128)(2,1)S(1)}, u32[]{:S(2)}, u32[]{:S(2)}) collective-permute-start(bf16[264,256]{1,0:T(8,128)(2,1)S(1)} %collective-permute-done.15.refs_2_), channel_id=1, source_target_pairs={{0,1},{1,0},{2,3},{3,2},{4,5},{5,4},{6,7},{7,6},{8,9},{9,8},{10,11... | collective-permute-start | bytes 405512 | tf_op jit(solution)/shard_map/ppermute | solution.py:249
  40.3 6.1 %collective-permute-start.18 = (bf16[72,512]{1,0:T(8,128)(2,1)S(1)}, bf16[72,512]{1,0:T(8,128)(2,1)S(1)}, u32[]{:S(2)}, u32[]{:S(2)}) collective-permute-start(bf16[72,512]{1,0:T(8,128)(2,1)S(1)} %get-tuple-element.41), channel_id=1, source_target_pairs={{0,24},{8,16},{16,8},{24,0},{1,25},{9,17},{17,9},{25,1},{2,26},{10... | collective-permute-start | bytes 221192 | tf_op jit(solution)/shard_map/ppermute | solution.py:256
  42.1 4.5 %collective-permute-start.19 = (bf16[72,512]{1,0:T(8,128)(2,1)S(1)}, bf16[72,512]{1,0:T(8,128)(2,1)S(1)}, u32[]{:S(2)}, u32[]{:S(2)}) collective-permute-start(bf16[72,512]{1,0:T(8,128)(2,1)S(1)} %get-tuple-element.42), channel_id=1, source_target_pairs={{0,8},{8,0},{16,24},{24,16},{1,9},{9,1},{17,25},{25,17},{2,10},{10... | collective-permute-start | bytes 221192 | tf_op jit(solution)/shard_map/ppermute | solution.py:256
  42.8 4.5 %collective-permute-start.20 = (bf16[72,512]{1,0:T(8,128)(2,1)S(1)}, bf16[72,512]{1,0:T(8,128)(2,1)S(1)}, u32[]{:S(2)}, u32[]{:S(2)}) collective-permute-start(bf16[72,512]{1,0:T(8,128)(2,1)S(1)} %get-tuple-element.43), channel_id=1, source_target_pairs={{0,16},{8,24},{16,0},{24,8},{1,17},{9,25},{17,1},{25,9},{2,18},{10... | collective-permute-start | bytes 221192 | tf_op jit(solution)/shard_map/ppermute | solution.py:256
  47.3 8.8 %collective-permute-start.22 = (bf16[72,512]{1,0:T(8,128)(2,1)S(1)}, bf16[72,512]{1,0:T(8,128)(2,1)S(1)}, u32[]{:S(2)}, u32[]{:S(2)}) collective-permute-start(bf16[72,512]{1,0:T(8,128)(2,1)S(1)} %get-tuple-element.46), channel_id=1, source_target_pairs={{0,4},{1,5},{2,6},{3,7},{4,0},{5,1},{6,2},{7,3},{8,12},{9,13},{10,... | collective-permute-start | bytes 221192 | tf_op jit(solution)/shard_map/ppermute | solution.py:252
  50.0 6.2 %collective-permute-start.21 = (bf16[64,512]{1,0:T(8,128)(2,1)S(1)}, bf16[64,512]{1,0:T(8,128)(2,1)S(1)}, u32[]{:S(2)}, u32[]{:S(2)}) collective-permute-start(bf16[64,512]{1,0:T(8,128)(2,1)S(1)} %get-tuple-element.45), channel_id=1, source_target_pairs={{0,6},{1,7},{2,4},{3,5},{4,2},{5,3},{6,0},{7,1},{8,14},{9,15},{10,... | collective-permute-start | bytes 196616 | tf_op jit(solution)/shard_map/ppermute | solution.py:252
  50.8 5.3 %collective-permute-start.23 = (bf16[64,512]{1,0:T(8,128)(2,1)S(1)}, bf16[64,512]{1,0:T(8,128)(2,1)S(1)}, u32[]{:S(2)}, u32[]{:S(2)}) collective-permute-start(bf16[64,512]{1,0:T(8,128)(2,1)S(1)} %get-tuple-element.47), channel_id=1, source_target_pairs={{0,2},{1,3},{2,0},{3,1},{4,6},{5,7},{6,4},{7,5},{8,10},{9,11},{10,... | collective-permute-start | bytes 196616 | tf_op jit(solution)/shard_map/ppermute | solution.py:252

commit v19 on v18

--- a/solution.py
+++ b/solution.py
@@ -13,7 +13,7 @@
 LAST = 1 << 30
 ROW_TILE = 8
 VMEM_BYTES = 24 * 1024 * 1024
-KEYS, OUTPUTS, HEADS = (2, 1, 0), (2, 0, 1), (2, 1, 0)
+KEYS, OUTPUTS, HEADS = (2, 1, 0), (2, 0, 1), (1, 2, 0)
 
 
 def vmem():

time: 57 us -> 57 us (level)
  no operation moved by 1% of the time
where the time goes in v19:
time: 57 us; the launch traced here: 56.8 us
  waiting for transfers between devices  25.7 us (45%)
  starting transfers between devices  23.2 us (41%)
  Pallas kernels  4.9 us (9%)
  local copies, waits for them, and re-layouts  2.17 us (4%)
  between operations  0.87 us (2%)
    ppermute x12, waiting for transfers between devices, to_partners(): lax.ppermute(value, 'ctx', [(i, i ^ mask) for i in range(steps)])  17 us
    ppermute x12, starting transfers between devices, to_partners(): lax.ppermute(value, 'ctx', [(i, i ^ mask) for i in range(steps)])  15.7 us
    ppermute x5, waiting for transfers between devices, to_chip(): return lax.ppermute(value, 'tp', [(i, i ^ 2 * step) for i in range(tp)])  7.74 us
    ppermute x5, starting transfers between devices, to_chip(): return lax.ppermute(value, 'tp', [(i, i ^ 2 * step) for i in range(tp)])  6.46 us
    pallas_call x11, Pallas kernels, call(): pl.pallas_call(kernel, out_shape=[jax.ShapeDtypeStruct(shape, kind) for s...  4.9 us
  transfers between devices with their start and end apart: 24, of which 13 were waited for; matrix products, arithmetic and copies ran while one was open for 2% of the time, Pallas kernels for 5%

profile of v19, /device:TPU:0, one launch (start us, length us, event | category | flops | bytes accessed | tf_op | source)
XLA Modules:
  0.0 56.8 jit_solution(3105202546067635646)
XLA Ops:
  0.7 1.1 %fusion = (bf16[64,1024]{1,0:T(8,128)(2,1)S(1)}, bf16[64,1024]{1,0:T(8,128)(2,1)S(1)}, bf16[64,1024]{1,0:T(8,128)(2,1)S(1)}) fusion(bf16[128,4096]{1,0:T(8,128)(2,1)} %param.8, s32[]{:T(128)S(6)} %select_n.32, s32[]{:T(128)S(6)} %select_n.36, s32[]{:T(128)S(6)} %select_n.33, s32[]{:T(128)S(6)} %select_n.35), kind=kLoop, calls=%fused_computation.4 | loop fusion | bytes 786448 | tf_op jit(solution)/shard_map/dynamic_slice | solution.py:273
  1.8 4.0 %collective-permute-start = (bf16[64,1024]{1,0:T(8,128)(2,1)S(1)}, bf16[64,1024]{1,0:T(8,128)(2,1)S(1)}, u32[]{:S(2)}, u32[]{:S(2)}) collective-permute-start(bf16[64,1024]{1,0:T(8,128)(2,1)S(1)} %get-tuple-element.49), channel_id=1, source_target_pairs={{0,24},{8,16},{16,8},{24,0},{1,25},{9,17},{17,9},{25,1},{2,26},{10... | collective-permute-start | bytes 393224 | tf_op jit(solution)/shard_map/ppermute | solution.py:256
  5.8 1.6 %collective-permute-start.5 = (bf16[256,512]{1,0:T(8,128)(2,1)S(1)}, bf16[256,512]{1,0:T(8,128)(2,1)S(1)}, u32[]{:S(2)}, u32[]{:S(2)}) collective-permute-start(bf16[256,512]{1,0:T(8,128)(2,1)S(1)} %get-tuple-element.52), channel_id=1, source_target_pairs={{0,2},{1,3},{2,0},{3,1},{4,6},{5,7},{6,4},{7,5},{8,10},{9,11},{10,... | collective-permute-start | bytes 786440 | tf_op jit(solution)/shard_map/ppermute | solution.py:252
  8.0 0.5 collective-permute-start.1
  8.5 1.0 %constant_dynamic-slice_fusion.3.own = bf16[128,1024]{1,0:T(8,128)(2,1)S(1)} fusion(bf16[128,4096]{1,0:T(8,128)(2,1)} %param.8, s32[]{:T(128)S(6)} %select_n.34), kind=kLoop, calls=%fused_computation.3 | loop fusion | bytes 524292 | tf_op jit(solution)/shard_map/dynamic_slice | solution.py:276
  9.6 2.9 %collective-permute-done.2.mine2 = bf16[64,1024]{1,0:T(8,128)(2,1)S(1)} collective-permute-done((bf16[64,1024]{1,0:T(8,128)(2,1)S(1)}, bf16[64,1024]{1,0:T(8,128)(2,1)S(1)}, u32[]{:S(2)}, u32[]{:S(2)}) %collective-permute-start.2) | collective-permute-done | bytes 131104 | tf_op jit(solution)/shard_map/ppermute | solution.py:256
  13.4 2.3 %collective-permute-start.7 = (bf16[136,512]{1,0:T(8,128)(2,1)S(1)}, bf16[136,512]{1,0:T(8,128)(2,1)S(1)}, u32[]{:S(2)}, u32[]{:S(2)}) collective-permute-start(bf16[136,512]{1,0:T(8,128)(2,1)S(1)} %project_both.1), channel_id=1, source_target_pairs={{0,24},{8,16},{16,8},{24,0},{1,25},{9,17},{17,9},{25,1},{2,26},{10... | collective-permute-start | bytes 417800 | tf_op jit(solution)/shard_map/ppermute | solution.py:256
  15.7 0.6 %project.1 = (f32[136,512]{1,0:T(8,128)S(1)}, bf16[136,512]{1,0:T(8,128)(2,1)S(1)}, bf16[136,512]{1,0:T(8,128)(2,1)S(1)}) custom-call(bf16[128,1024]{1,0:T(8,128)(2,1)S(1)} %constant_dynamic-slice_fusion.3.own, bf16[64,1024]{1,0:T(8,128)(2,1)S(1)} %collective-permute-done.1.mine1, bf16[64,1024]{1,0:T(8,128)(2,1)S(1)} %collective-permute-done.2.mine2, ...), custom_call_target="tpu_custom_call" | custom-call | tf_op jit(solution)/shard_map/project/pallas_call | solution.py:261
  16.3 0.8 %collective-permute-start.8 = (bf16[136,512]{1,0:T(8,128)(2,1)S(1)}, bf16[136,512]{1,0:T(8,128)(2,1)S(1)}, u32[]{:S(2)}, u32[]{:S(2)}) collective-permute-start(bf16[136,512]{1,0:T(8,128)(2,1)S(1)} %get-tuple-element.29), channel_id=1, source_target_pairs={{0,8},{8,0},{16,24},{24,16},{1,9},{9,1},{17,25},{25,17},{2,10},{10... | collective-permute-start | bytes 417800 | tf_op jit(solution)/shard_map/ppermute | solution.py:256
  17.9 2.8 %collective-permute-done.7.part = bf16[136,512]{1,0:T(8,128)(2,1)S(1)} collective-permute-done((bf16[136,512]{1,0:T(8,128)(2,1)S(1)}, bf16[136,512]{1,0:T(8,128)(2,1)S(1)}, u32[]{:S(2)}, u32[]{:S(2)}) %collective-permute-start.7) | collective-permute-done | bytes 139296 | tf_op jit(solution)/shard_map/ppermute | solution.py:256
  20.8 2.6 %collective-permute-done.8.first = bf16[136,512]{1,0:T(8,128)(2,1)S(1)} collective-permute-done((bf16[136,512]{1,0:T(8,128)(2,1)S(1)}, bf16[136,512]{1,0:T(8,128)(2,1)S(1)}, u32[]{:S(2)}, u32[]{:S(2)}) %collective-permute-start.8) | collective-permute-done | bytes 139296 | tf_op jit(solution)/shard_map/ppermute | solution.py:256
  23.5 0.9 %collective-permute-start.12 = (bf16[128,512]{1,0:T(8,128)(2,1)S(1)}, bf16[128,512]{1,0:T(8,128)(2,1)S(1)}, u32[]{:S(2)}, u32[]{:S(2)}) collective-permute-start(bf16[128,512]{1,0:T(8,128)(2,1)S(1)} %get-tuple-element.31.refs_0_), channel_id=1, source_target_pairs={{0,8},{8,0},{16,24},{24,16},{1,9},{9,1},{17,25},{25,17},{2,10},{10... | collective-permute-start | bytes 393224 | tf_op jit(solution)/shard_map/ppermute | solution.py:256
  24.4 1.4 %collective-permute-start.11 = (bf16[128,512]{1,0:T(8,128)(2,1)S(1)}, bf16[128,512]{1,0:T(8,128)(2,1)S(1)}, u32[]{:S(2)}, u32[]{:S(2)}) collective-permute-start(bf16[128,512]{1,0:T(8,128)(2,1)S(1)} %get-tuple-element.31.refs_0_), channel_id=1, source_target_pairs={{0,16},{8,24},{16,0},{24,8},{1,17},{9,25},{17,1},{25,9},{2,18},{10... | collective-permute-start | bytes 393224 | tf_op jit(solution)/shard_map/ppermute | solution.py:256
  25.9 1.2 %collective-permute-start.10 = (bf16[128,512]{1,0:T(8,128)(2,1)S(1)}, bf16[128,512]{1,0:T(8,128)(2,1)S(1)}, u32[]{:S(2)}, u32[]{:S(2)}) collective-permute-start(bf16[128,512]{1,0:T(8,128)(2,1)S(1)} %get-tuple-element.31.refs_0_), channel_id=1, source_target_pairs={{0,24},{8,16},{16,8},{24,0},{1,25},{9,17},{17,9},{25,1},{2,26},{10... | collective-permute-start | bytes 393224 | tf_op jit(solution)/shard_map/ppermute | solution.py:256
  27.1 0.8 %mask.1 = (f32[512,512]{1,0:T(8,128)S(1)}, f32[16,512]{1,0:T(8,128)S(1)}) custom-call(s32[8]{0:T(128)S(1)} %copy-done.5, s32[4]{0:T(128)S(1)} %copy-done.6), custom_call_target="tpu_custom_call" | custom-call | tf_op jit(solution)/shard_map/mask/pallas_call | solution.py:261
  27.9 2.1 %collective-permute-done.12.refs_3_ = bf16[128,512]{1,0:T(8,128)(2,1)S(1)} collective-permute-done((bf16[128,512]{1,0:T(8,128)(2,1)S(1)}, bf16[128,512]{1,0:T(8,128)(2,1)S(1)}, u32[]{:S(2)}, u32[]{:S(2)}) %collective-permute-start.12) | collective-permute-done | bytes 131104 | tf_op jit(solution)/shard_map/ppermute | solution.py:256
  30.0 1.2 %collective-permute-done.11.refs_2_ = bf16[128,512]{1,0:T(8,128)(2,1)S(1)} collective-permute-done((bf16[128,512]{1,0:T(8,128)(2,1)S(1)}, bf16[128,512]{1,0:T(8,128)(2,1)S(1)}, u32[]{:S(2)}, u32[]{:S(2)}) %collective-permute-start.11) | collective-permute-done | bytes 131104 | tf_op jit(solution)/shard_map/ppermute | solution.py:256
  31.2 1.6 %collective-permute-done.10.refs_1_ = bf16[128,512]{1,0:T(8,128)(2,1)S(1)} collective-permute-done((bf16[128,512]{1,0:T(8,128)(2,1)S(1)}, bf16[128,512]{1,0:T(8,128)(2,1)S(1)}, u32[]{:S(2)}, u32[]{:S(2)}) %collective-permute-start.10) | collective-permute-done | bytes 131104 | tf_op jit(solution)/shard_map/ppermute | solution.py:256
  32.7 0.9 %attend_sent.1.refs_7_ = bf16[264,256]{1,0:T(8,128)(2,1)S(1)} custom-call(bf16[128,512]{1,0:T(8,128)(2,1)S(1)} %get-tuple-element.31.refs_0_, bf16[128,512]{1,0:T(8,128)(2,1)S(1)} %collective-permute-done.10.refs_1_, bf16[128,512]{1,0:T(8,128)(2,1)S(1)} %collective-permute-done.11.refs_2_, bf16[128,512]{1,0:T(8,128)(2,1)S(1)} %collective-permute-done.12.refs_3_, ...), custom_call_target="tpu_custom_call" | custom-call | tf_op jit(solution)/shard_map/attend_sent/pallas_call | solution.py:261
  33.7 1.1 %collective-permute-start.15 = (bf16[264,256]{1,0:T(8,128)(2,1)S(1)}, bf16[264,256]{1,0:T(8,128)(2,1)S(1)}, u32[]{:S(2)}, u32[]{:S(2)}) collective-permute-start(bf16[264,256]{1,0:T(8,128)(2,1)S(1)} %attend_sent.1.refs_7_), channel_id=1, source_target_pairs={{0,2},{1,3},{2,0},{3,1},{4,6},{5,7},{6,4},{7,5},{8,10},{9,11},{10,... | collective-permute-start | bytes 405512 | tf_op jit(solution)/shard_map/ppermute | solution.py:252
  34.7 0.8 %attend_kept.1.refs_0_ = bf16[264,256]{1,0:T(8,128)(2,1)S(1)} custom-call(bf16[128,512]{1,0:T(8,128)(2,1)S(1)} %get-tuple-element.31.refs_0_, bf16[128,512]{1,0:T(8,128)(2,1)S(1)} %collective-permute-done.10.refs_1_, bf16[128,512]{1,0:T(8,128)(2,1)S(1)} %collective-permute-done.11.refs_2_, bf16[128,512]{1,0:T(8,128)(2,1)S(1)} %collective-permute-done.12.refs_3_, ...), custom_call_target="tpu_custom_call" | custom-call | tf_op jit(solution)/shard_map/attend_kept/pallas_call | solution.py:261
  36.1 2.7 %collective-permute-done.15.refs_2_ = bf16[264,256]{1,0:T(8,128)(2,1)S(1)} collective-permute-done((bf16[264,256]{1,0:T(8,128)(2,1)S(1)}, bf16[264,256]{1,0:T(8,128)(2,1)S(1)}, u32[]{:S(2)}, u32[]{:S(2)}) %collective-permute-start.15) | collective-permute-done | bytes 135200 | tf_op jit(solution)/shard_map/ppermute | solution.py:252
  39.1 1.0 %collective-permute-done.17.heads = bf16[264,256]{1,0:T(8,128)(2,1)S(1)} collective-permute-done((bf16[264,256]{1,0:T(8,128)(2,1)S(1)}, bf16[264,256]{1,0:T(8,128)(2,1)S(1)}, u32[]{:S(2)}, u32[]{:S(2)}) %collective-permute-start.17) | collective-permute-done | bytes 135200 | tf_op jit(solution)/shard_map/ppermute | solution.py:249
  40.3 1.8 %collective-permute-start.18 = (bf16[72,512]{1,0:T(8,128)(2,1)S(1)}, bf16[72,512]{1,0:T(8,128)(2,1)S(1)}, u32[]{:S(2)}, u32[]{:S(2)}) collective-permute-start(bf16[72,512]{1,0:T(8,128)(2,1)S(1)} %get-tuple-element.41), channel_id=1, source_target_pairs={{0,24},{8,16},{16,8},{24,0},{1,25},{9,17},{17,9},{25,1},{2,26},{10... | collective-permute-start | bytes 221192 | tf_op jit(solution)/shard_map/ppermute | solution.py:256
  42.1 0.6 %collective-permute-start.19 = (bf16[72,512]{1,0:T(8,128)(2,1)S(1)}, bf16[72,512]{1,0:T(8,128)(2,1)S(1)}, u32[]{:S(2)}, u32[]{:S(2)}) collective-permute-start(bf16[72,512]{1,0:T(8,128)(2,1)S(1)} %get-tuple-element.42), channel_id=1, source_target_pairs={{0,8},{8,0},{16,24},{24,16},{1,9},{9,1},{17,25},{25,17},{2,10},{10... | collective-permute-start | bytes 221192 | tf_op jit(solution)/shard_map/ppermute | solution.py:256
  42.8 1.1 %collective-permute-start.20 = (bf16[72,512]{1,0:T(8,128)(2,1)S(1)}, bf16[72,512]{1,0:T(8,128)(2,1)S(1)}, u32[]{:S(2)}, u32[]{:S(2)}) collective-permute-start(bf16[72,512]{1,0:T(8,128)(2,1)S(1)} %get-tuple-element.43), channel_id=1, source_target_pairs={{0,16},{8,24},{16,0},{24,8},{1,17},{9,25},{17,1},{25,9},{2,18},{10... | collective-permute-start | bytes 221192 | tf_op jit(solution)/shard_map/ppermute | solution.py:256
  43.9 2.5 %collective-permute-done.18.refs_1_ = bf16[72,512]{1,0:T(8,128)(2,1)S(1)} collective-permute-done((bf16[72,512]{1,0:T(8,128)(2,1)S(1)}, bf16[72,512]{1,0:T(8,128)(2,1)S(1)}, u32[]{:S(2)}, u32[]{:S(2)}) %collective-permute-start.18) | collective-permute-done | bytes 73760 | tf_op jit(solution)/shard_map/ppermute | solution.py:256
  46.7 0.6 %collective-permute-done.20.refs_3_ = bf16[72,512]{1,0:T(8,128)(2,1)S(1)} collective-permute-done((bf16[72,512]{1,0:T(8,128)(2,1)S(1)}, bf16[72,512]{1,0:T(8,128)(2,1)S(1)}, u32[]{:S(2)}, u32[]{:S(2)}) %collective-permute-start.20) | collective-permute-done | bytes 73760 | tf_op jit(solution)/shard_map/ppermute | solution.py:256
  47.3 2.6 %collective-permute-start.21 = (bf16[72,512]{1,0:T(8,128)(2,1)S(1)}, bf16[72,512]{1,0:T(8,128)(2,1)S(1)}, u32[]{:S(2)}, u32[]{:S(2)}) collective-permute-start(bf16[72,512]{1,0:T(8,128)(2,1)S(1)} %get-tuple-element.45), channel_id=1, source_target_pairs={{0,4},{1,5},{2,6},{3,7},{4,0},{5,1},{6,2},{7,3},{8,12},{9,13},{10,... | collective-permute-start | bytes 221192 | tf_op jit(solution)/shard_map/ppermute | solution.py:252
  50.0 0.9 %collective-permute-start.22 = (bf16[64,512]{1,0:T(8,128)(2,1)S(1)}, bf16[64,512]{1,0:T(8,128)(2,1)S(1)}, u32[]{:S(2)}, u32[]{:S(2)}) collective-permute-start(bf16[64,512]{1,0:T(8,128)(2,1)S(1)} %get-tuple-element.46), channel_id=1, source_target_pairs={{0,6},{1,7},{2,4},{3,5},{4,2},{5,3},{6,0},{7,1},{8,14},{9,15},{10,... | collective-permute-start | bytes 196616 | tf_op jit(solution)/shard_map/ppermute | solution.py:252
  51.1 5.1 %collective-permute-done.22.refs_2_ = bf16[64,512]{1,0:T(8,128)(2,1)S(1)} collective-permute-done((bf16[64,512]{1,0:T(8,128)(2,1)S(1)}, bf16[64,512]{1,0:T(8,128)(2,1)S(1)}, u32[]{:S(2)}, u32[]{:S(2)}) %collective-permute-start.22) | collective-permute-done | bytes 65568 | tf_op jit(solution)/shard_map/ppermute | solution.py:252
  56.1 0.7 %finish.1 = (bf16[128,512]{1,0:T(8,128)(2,1)}, bf16[4,512]{1,0:T(4,128)(2,1)}) custom-call(bf16[72,512]{1,0:T(8,128)(2,1)S(1)} %get-tuple-element.44.refs_0_, bf16[72,512]{1,0:T(8,128)(2,1)S(1)} %collective-permute-done.21.refs_1_, bf16[64,512]{1,0:T(8,128)(2,1)S(1)} %collective-permute-done.22.refs_2_, bf16[64,512]{1,0:T(8,128)(2,1)S(1)} %collective-permute-done.23.refs_3_), custom_call_target="tpu_custom_call" | custom-call | tf_op jit(solution)/shard_map/finish/pallas_call | solution.py:261
  (45 shorter events, 4.2 us)
Async XLA Ops:
  0.6 12.3 %copy-start = (bf16[4,4096]{1,0:T(4,128)(2,1)S(1)}, bf16[4,4096]{1,0:T(4,128)(2,1)}, u32[]{:S(2)}) copy-start(bf16[4,4096]{1,0:T(4,128)(2,1)} %param.9) | copy-start | bytes 98308
  0.6 5.1 %copy-start.2 = (bf16[256,1024]{1,0:T(8,128)(2,1)S(1)}, bf16[256,1024]{1,0:T(8,128)(2,1)}, u32[]{:S(2)}) copy-start(bf16[256,1024]{1,0:T(8,128)(2,1)} %refs_3_.1) | copy-start | bytes 1572868
  1.8 7.7 %collective-permute-start = (bf16[64,1024]{1,0:T(8,128)(2,1)S(1)}, bf16[64,1024]{1,0:T(8,128)(2,1)S(1)}, u32[]{:S(2)}, u32[]{:S(2)}) collective-permute-start(bf16[64,1024]{1,0:T(8,128)(2,1)S(1)} %get-tuple-element.49), channel_id=1, source_target_pairs={{0,24},{8,16},{16,8},{24,0},{1,25},{9,17},{17,9},{25,1},{2,26},{10... | collective-permute-start | bytes 393224 | tf_op jit(solution)/shard_map/ppermute | solution.py:256
  5.8 7.2 %copy-start.3 = (bf16[1024,128]{1,0:T(8,128)(2,1)S(1)}, bf16[1024,128]{1,0:T(8,128)(2,1)}, u32[]{:S(2)}) copy-start(bf16[1024,128]{1,0:T(8,128)(2,1)} %wk.3) | copy-start | bytes 786436
  5.8 7.2 %copy-start.4 = (bf16[1024,128]{1,0:T(8,128)(2,1)S(1)}, bf16[1024,128]{1,0:T(8,128)(2,1)}, u32[]{:S(2)}) copy-start(bf16[1024,128]{1,0:T(8,128)(2,1)} %wv.3) | copy-start | bytes 786436
  5.8 7.2 %copy-start.1 = (bf16[1024,256]{1,0:T(8,128)(2,1)S(1)}, bf16[1024,256]{1,0:T(8,128)(2,1)}, u32[]{:S(2)}) copy-start(bf16[1024,256]{1,0:T(8,128)(2,1)} %wq.3) | copy-start | bytes 1572868
  5.8 9.9 %collective-permute-start.5 = (bf16[256,512]{1,0:T(8,128)(2,1)S(1)}, bf16[256,512]{1,0:T(8,128)(2,1)S(1)}, u32[]{:S(2)}, u32[]{:S(2)}) collective-permute-start(bf16[256,512]{1,0:T(8,128)(2,1)S(1)} %get-tuple-element.52), channel_id=1, source_target_pairs={{0,2},{1,3},{2,0},{3,1},{4,6},{5,7},{6,4},{7,5},{8,10},{9,11},{10,... | collective-permute-start | bytes 786440 | tf_op jit(solution)/shard_map/ppermute | solution.py:252
  7.5 5.0 %collective-permute-start.2 = (bf16[64,1024]{1,0:T(8,128)(2,1)S(1)}, bf16[64,1024]{1,0:T(8,128)(2,1)S(1)}, u32[]{:S(2)}, u32[]{:S(2)}) collective-permute-start(bf16[64,1024]{1,0:T(8,128)(2,1)S(1)} %get-tuple-element.48), channel_id=1, source_target_pairs={{0,16},{8,24},{16,0},{24,8},{1,17},{9,25},{17,1},{25,9},{2,18},{10... | collective-permute-start | bytes 393224 | tf_op jit(solution)/shard_map/ppermute | solution.py:256
  8.0 5.0 %collective-permute-start.1 = (bf16[64,1024]{1,0:T(8,128)(2,1)S(1)}, bf16[64,1024]{1,0:T(8,128)(2,1)S(1)}, u32[]{:S(2)}, u32[]{:S(2)}) collective-permute-start(bf16[64,1024]{1,0:T(8,128)(2,1)S(1)} %get-tuple-element.50), channel_id=1, source_target_pairs={{0,8},{8,0},{16,24},{24,16},{1,9},{9,1},{17,25},{25,17},{2,10},{10... | collective-permute-start | bytes 393224 | tf_op jit(solution)/shard_map/ppermute | solution.py:256
  9.5 3.5 %collective-permute-start.6 = (bf16[64,1024]{1,0:T(8,128)(2,1)S(1)}, bf16[64,1024]{1,0:T(8,128)(2,1)S(1)}, u32[]{:S(2)}, u32[]{:S(2)}) collective-permute-start(bf16[64,1024]{1,0:T(8,128)(2,1)S(1)} %collective-permute-done.mine), channel_id=1, source_target_pairs={{0,1},{1,0},{2,3},{3,2},{4,5},{5,4},{6,7},{7,6},{8,9},{9,8},{10,11... | collective-permute-start | bytes 393224 | tf_op jit(solution)/shard_map/ppermute | solution.py:249
  12.4 3.3 %collective-permute-start.4 = (bf16[64,1024]{1,0:T(8,128)(2,1)S(1)}, bf16[64,1024]{1,0:T(8,128)(2,1)S(1)}, u32[]{:S(2)}, u32[]{:S(2)}) collective-permute-start(bf16[64,1024]{1,0:T(8,128)(2,1)S(1)} %collective-permute-done.2.mine2), channel_id=1, source_target_pairs={{0,1},{1,0},{2,3},{3,2},{4,5},{5,4},{6,7},{7,6},{8,9},{9,8},{10,11... | collective-permute-start | bytes 393224 | tf_op jit(solution)/shard_map/ppermute | solution.py:249
  12.9 2.8 %collective-permute-start.3 = (bf16[64,1024]{1,0:T(8,128)(2,1)S(1)}, bf16[64,1024]{1,0:T(8,128)(2,1)S(1)}, u32[]{:S(2)}, u32[]{:S(2)}) collective-permute-start(bf16[64,1024]{1,0:T(8,128)(2,1)S(1)} %collective-permute-done.1.mine1), channel_id=1, source_target_pairs={{0,1},{1,0},{2,3},{3,2},{4,5},{5,4},{6,7},{7,6},{8,9},{9,8},{10,11... | collective-permute-start | bytes 393224 | tf_op jit(solution)/shard_map/ppermute | solution.py:249
  13.4 7.4 %collective-permute-start.7 = (bf16[136,512]{1,0:T(8,128)(2,1)S(1)}, bf16[136,512]{1,0:T(8,128)(2,1)S(1)}, u32[]{:S(2)}, u32[]{:S(2)}) collective-permute-start(bf16[136,512]{1,0:T(8,128)(2,1)S(1)} %project_both.1), channel_id=1, source_target_pairs={{0,24},{8,16},{16,8},{24,0},{1,25},{9,17},{17,9},{25,1},{2,26},{10... | collective-permute-start | bytes 417800 | tf_op jit(solution)/shard_map/ppermute | solution.py:256
  16.3 7.1 %collective-permute-start.8 = (bf16[136,512]{1,0:T(8,128)(2,1)S(1)}, bf16[136,512]{1,0:T(8,128)(2,1)S(1)}, u32[]{:S(2)}, u32[]{:S(2)}) collective-permute-start(bf16[136,512]{1,0:T(8,128)(2,1)S(1)} %get-tuple-element.29), channel_id=1, source_target_pairs={{0,8},{8,0},{16,24},{24,16},{1,9},{9,1},{17,25},{25,17},{2,10},{10... | collective-permute-start | bytes 417800 | tf_op jit(solution)/shard_map/ppermute | solution.py:256
  17.1 6.4 %collective-permute-start.9 = (bf16[136,512]{1,0:T(8,128)(2,1)S(1)}, bf16[136,512]{1,0:T(8,128)(2,1)S(1)}, u32[]{:S(2)}, u32[]{:S(2)}) collective-permute-start(bf16[136,512]{1,0:T(8,128)(2,1)S(1)} %get-tuple-element.30), channel_id=1, source_target_pairs={{0,16},{8,24},{16,0},{24,8},{1,17},{9,25},{17,1},{25,9},{2,18},{10... | collective-permute-start | bytes 417800 | tf_op jit(solution)/shard_map/ppermute | solution.py:256
  17.6 10.3 %collective-permute-start.13 = (bf16[256,512]{1,0:T(8,128)(2,1)S(1)}, bf16[256,512]{1,0:T(8,128)(2,1)S(1)}, u32[]{:S(2)}, u32[]{:S(2)}) collective-permute-start(bf16[256,512]{1,0:T(8,128)(2,1)S(1)} %get-tuple-element.37), channel_id=1, source_target_pairs={{0,3},{1,2},{2,1},{3,0},{4,7},{5,6},{6,5},{7,4},{8,11},{9,10},{10,... | collective-permute-start | bytes 786440 | tf_op jit(solution)/shard_map/ppermute | solution.py:305
  23.5 3.6 %copy-start.5 = (s32[8]{0:T(128)S(1)}, s32[8]{0:T(128)}, u32[]{:S(2)}) copy-start(s32[8]{0:T(128)} %block_map.1) | copy-start | bytes 100
  23.5 3.6 %copy-start.6 = (s32[4]{0:T(128)S(1)}, s32[4]{0:T(128)}, u32[]{:S(2)}) copy-start(s32[4]{0:T(128)} %lengths.1) | copy-start | bytes 52
  23.5 6.5 %collective-permute-start.12 = (bf16[128,512]{1,0:T(8,128)(2,1)S(1)}, bf16[128,512]{1,0:T(8,128)(2,1)S(1)}, u32[]{:S(2)}, u32[]{:S(2)}) collective-permute-start(bf16[128,512]{1,0:T(8,128)(2,1)S(1)} %get-tuple-element.31.refs_0_), channel_id=1, source_target_pairs={{0,8},{8,0},{16,24},{24,16},{1,9},{9,1},{17,25},{25,17},{2,10},{10... | collective-permute-start | bytes 393224 | tf_op jit(solution)/shard_map/ppermute | solution.py:256
  24.4 6.7 %collective-permute-start.11 = (bf16[128,512]{1,0:T(8,128)(2,1)S(1)}, bf16[128,512]{1,0:T(8,128)(2,1)S(1)}, u32[]{:S(2)}, u32[]{:S(2)}) collective-permute-start(bf16[128,512]{1,0:T(8,128)(2,1)S(1)} %get-tuple-element.31.refs_0_), channel_id=1, source_target_pairs={{0,16},{8,24},{16,0},{24,8},{1,17},{9,25},{17,1},{25,9},{2,18},{10... | collective-permute-start | bytes 393224 | tf_op jit(solution)/shard_map/ppermute | solution.py:256
  25.9 6.8 %collective-permute-start.10 = (bf16[128,512]{1,0:T(8,128)(2,1)S(1)}, bf16[128,512]{1,0:T(8,128)(2,1)S(1)}, u32[]{:S(2)}, u32[]{:S(2)}) collective-permute-start(bf16[128,512]{1,0:T(8,128)(2,1)S(1)} %get-tuple-element.31.refs_0_), channel_id=1, source_target_pairs={{0,24},{8,16},{16,8},{24,0},{1,25},{9,17},{17,9},{25,1},{2,26},{10... | collective-permute-start | bytes 393224 | tf_op jit(solution)/shard_map/ppermute | solution.py:256
  33.7 5.1 %collective-permute-start.15 = (bf16[264,256]{1,0:T(8,128)(2,1)S(1)}, bf16[264,256]{1,0:T(8,128)(2,1)S(1)}, u32[]{:S(2)}, u32[]{:S(2)}) collective-permute-start(bf16[264,256]{1,0:T(8,128)(2,1)S(1)} %attend_sent.1.refs_7_), channel_id=1, source_target_pairs={{0,2},{1,3},{2,0},{3,1},{4,6},{5,7},{6,4},{7,5},{8,10},{9,11},{10,... | collective-permute-start | bytes 405512 | tf_op jit(solution)/shard_map/ppermute | solution.py:252
  35.5 3.3 %collective-permute-start.16 = (bf16[256,512]{1,0:T(8,128)(2,1)S(1)}, bf16[256,512]{1,0:T(8,128)(2,1)S(1)}, u32[]{:S(2)}, u32[]{:S(2)}) collective-permute-start(bf16[256,512]{1,0:T(8,128)(2,1)S(1)} %get-tuple-element.37), channel_id=1, source_target_pairs={{0,1},{1,0},{2,3},{3,2},{4,5},{5,4},{6,7},{7,6},{8,9},{9,8},{10,11... | collective-permute-start | bytes 786440 | tf_op jit(solution)/shard_map/ppermute | solution.py:249
  35.6 3.2 %collective-permute-start.14 = (bf16[264,256]{1,0:T(8,128)(2,1)S(1)}, bf16[264,256]{1,0:T(8,128)(2,1)S(1)}, u32[]{:S(2)}, u32[]{:S(2)}) collective-permute-start(bf16[264,256]{1,0:T(8,128)(2,1)S(1)} %attend_kept.1.refs_0_), channel_id=1, source_target_pairs={{0,1},{1,0},{2,3},{3,2},{4,5},{5,4},{6,7},{7,6},{8,9},{9,8},{10,11... | collective-permute-start | bytes 405512 | tf_op jit(solution)/shard_map/ppermute | solution.py:249
  38.7 1.4 %collective-permute-start.17 = (bf16[264,256]{1,0:T(8,128)(2,1)S(1)}, bf16[264,256]{1,0:T(8,128)(2,1)S(1)}, u32[]{:S(2)}, u32[]{:S(2)}) collective-permute-start(bf16[264,256]{1,0:T(8,128)(2,1)S(1)} %collective-permute-done.15.refs_2_), channel_id=1, source_target_pairs={{0,1},{1,0},{2,3},{3,2},{4,5},{5,4},{6,7},{7,6},{8,9},{9,8},{10,11... | collective-permute-start | bytes 405512 | tf_op jit(solution)/shard_map/ppermute | solution.py:249
  40.3 6.1 %collective-permute-start.18 = (bf16[72,512]{1,0:T(8,128)(2,1)S(1)}, bf16[72,512]{1,0:T(8,128)(2,1)S(1)}, u32[]{:S(2)}, u32[]{:S(2)}) collective-permute-start(bf16[72,512]{1,0:T(8,128)(2,1)S(1)} %get-tuple-element.41), channel_id=1, source_target_pairs={{0,24},{8,16},{16,8},{24,0},{1,25},{9,17},{17,9},{25,1},{2,26},{10... | collective-permute-start | bytes 221192 | tf_op jit(solution)/shard_map/ppermute | solution.py:256
  42.1 4.5 %collective-permute-start.19 = (bf16[72,512]{1,0:T(8,128)(2,1)S(1)}, bf16[72,512]{1,0:T(8,128)(2,1)S(1)}, u32[]{:S(2)}, u32[]{:S(2)}) collective-permute-start(bf16[72,512]{1,0:T(8,128)(2,1)S(1)} %get-tuple-element.42), channel_id=1, source_target_pairs={{0,8},{8,0},{16,24},{24,16},{1,9},{9,1},{17,25},{25,17},{2,10},{10... | collective-permute-start | bytes 221192 | tf_op jit(solution)/shard_map/ppermute | solution.py:256
  42.8 4.5 %collective-permute-start.20 = (bf16[72,512]{1,0:T(8,128)(2,1)S(1)}, bf16[72,512]{1,0:T(8,128)(2,1)S(1)}, u32[]{:S(2)}, u32[]{:S(2)}) collective-permute-start(bf16[72,512]{1,0:T(8,128)(2,1)S(1)} %get-tuple-element.43), channel_id=1, source_target_pairs={{0,16},{8,24},{16,0},{24,8},{1,17},{9,25},{17,1},{25,9},{2,18},{10... | collective-permute-start | bytes 221192 | tf_op jit(solution)/shard_map/ppermute | solution.py:256
  47.3 8.8 %collective-permute-start.21 = (bf16[72,512]{1,0:T(8,128)(2,1)S(1)}, bf16[72,512]{1,0:T(8,128)(2,1)S(1)}, u32[]{:S(2)}, u32[]{:S(2)}) collective-permute-start(bf16[72,512]{1,0:T(8,128)(2,1)S(1)} %get-tuple-element.45), channel_id=1, source_target_pairs={{0,4},{1,5},{2,6},{3,7},{4,0},{5,1},{6,2},{7,3},{8,12},{9,13},{10,... | collective-permute-start | bytes 221192 | tf_op jit(solution)/shard_map/ppermute | solution.py:252
  50.0 6.2 %collective-permute-start.22 = (bf16[64,512]{1,0:T(8,128)(2,1)S(1)}, bf16[64,512]{1,0:T(8,128)(2,1)S(1)}, u32[]{:S(2)}, u32[]{:S(2)}) collective-permute-start(bf16[64,512]{1,0:T(8,128)(2,1)S(1)} %get-tuple-element.46), channel_id=1, source_target_pairs={{0,6},{1,7},{2,4},{3,5},{4,2},{5,3},{6,0},{7,1},{8,14},{9,15},{10,... | collective-permute-start | bytes 196616 | tf_op jit(solution)/shard_map/ppermute | solution.py:252
  50.8 5.3 %collective-permute-start.23 = (bf16[64,512]{1,0:T(8,128)(2,1)S(1)}, bf16[64,512]{1,0:T(8,128)(2,1)S(1)}, u32[]{:S(2)}, u32[]{:S(2)}) collective-permute-start(bf16[64,512]{1,0:T(8,128)(2,1)S(1)} %get-tuple-element.47), channel_id=1, source_target_pairs={{0,2},{1,3},{2,0},{3,1},{4,6},{5,7},{6,4},{7,5},{8,10},{9,11},{10,... | collective-permute-start | bytes 196616 | tf_op jit(solution)/shard_map/ppermute | solution.py:252
